TPU v7x, 32 devices: a whole 2x2x4 slice. The times are simulated.
32 devices in a mesh: dp: 2 (over y), row: 4 (over x, core), col: 4 (over z).
Axes of the slice: x: 2, y: 2, z: 4, core: 2. Of those that a mesh axis runs over, the one named last changes fastest.
Arguments:
- first_homolog_features: bfloat16 [64, 6144], P(('dp', 'col'), 'row'), parts along dimension 0, may hold values from -18 to 18
- second_homolog_features: bfloat16 [64, 6144], P(('dp', 'row'), 'col'), parts along dimension 0, may hold values from -18 to 18
- final_projection_matrix: bfloat16 [1024, 128], replicated, may hold values from -0.1875 to 0.1875
- output_bias: float32 [128], replicated, may hold values from -3 to 3
- cotangent: bfloat16 [384, 192, 128], P(('dp', 'row'), 'col'), parts along dimension 0, may hold values from -6 to 6
Outputs:
- pair_map: bfloat16 [384, 192, 128], P(('dp', 'row'), 'col'), parts along dimension 0
- first_homolog_cotangent: float32 [64, 6144], P(('dp', 'col'), 'row'), parts along dimension 0
- right_grad: float32 [64, 6144], P(('dp', 'row'), 'col'), parts along dimension 0
- projection_cotangent: float32 [2048, 128], P('dp'), parts along dimension 0
- bias_grad: float32 [256], P('dp'), parts along dimension 0
There are 2 independent parts, one for each index of `dp`. A program takes and returns all parts, laid end to end along the dimension named above; an argument that names none is the same for every part. Nothing has to cross between parts.
All inputs are finite; a program needn't handle non-finite values.
Results may differ from a plain program's by a relative error of at most 0.0048.
Values may be sent and summed in bfloat16 or wider, within the bound.
No kernel may reach another device: no remote copies, remote signals or barrier semaphores. Data moves between devices by JAX's collectives and lax.ppermute only.
A program may use at most 128 MiB of HBM per device.

v0:
```python
import jax
import jax.numpy as jnp
from jax import lax
from jax.sharding import PartitionSpec as P

PROJECTED_DEPTH = 32
PAIR_FEATURES = 128


def local(
    first_homolog_features, second_homolog_features, final_projection_matrix, output_bias, cotangent
):
    sequence_count = second_homolog_features.shape[0] * lax.axis_size("row")
    patch_positions = cotangent.shape[0]
    res_total = patch_positions * lax.axis_size("row")
    projection_cuboid = final_projection_matrix.reshape(
        PROJECTED_DEPTH, PROJECTED_DEPTH, PAIR_FEATURES
    )
    right_complete = lax.all_gather(second_homolog_features, "row", axis=0, tiled=True)
    contract = (((0,), (0,)), ((), ()))
    left_complete = lax.all_gather(first_homolog_features, "col", axis=0, tiled=True)
    summed = lax.dot_general(
        left_complete, right_complete, contract, preferred_element_type=jnp.float32
    )
    kronecker_array = (summed / sequence_count).astype(jnp.bfloat16)
    kronecker_pieces = kronecker_array.reshape(
        patch_positions, PROJECTED_DEPTH, patch_positions, PROJECTED_DEPTH
    )
    pair_block = (
        jnp.einsum(
            "icje,cef->ijf", kronecker_pieces, projection_cuboid, preferred_element_type=jnp.float32
        )
        + output_bias
    )
    pair_map = pair_block.astype(jnp.bfloat16)
    outer_grad = jnp.einsum(
        "ijf,cef->icje", cotangent, projection_cuboid, preferred_element_type=jnp.float32
    ).astype(jnp.bfloat16)
    kronecker_cotangent = outer_grad.reshape(
        patch_positions * PROJECTED_DEPTH, patch_positions * PROJECTED_DEPTH
    )
    row_block = right_complete
    first_homolog_cotangent = lax.psum_scatter(
        lax.dot_general(
            row_block,
            kronecker_cotangent,
            (((1,), (1,)), ((), ())),
            preferred_element_type=jnp.float32,
        )
        / sequence_count,
        "col",
        scatter_dimension=0,
        tiled=True,
    )
    row_block = left_complete
    right_grad = lax.psum_scatter(
        jnp.dot(row_block, kronecker_cotangent, preferred_element_type=jnp.float32)
        / sequence_count,
        "row",
        scatter_dimension=0,
        tiled=True,
    )
    weight_cuboid = jnp.einsum(
        "icje,ijf->cef", kronecker_pieces, cotangent, preferred_element_type=jnp.float32
    )
    weight_local = weight_cuboid.reshape(PROJECTED_DEPTH * PROJECTED_DEPTH, PAIR_FEATURES)
    bias_local = jnp.sum(cotangent.astype(jnp.float32), axis=(0, 1))
    weight_summed, bias_summed = lax.psum((weight_local, bias_local), ("row", "col"))
    return (
        pair_map,
        first_homolog_cotangent,
        right_grad,
        weight_summed / res_total,
        bias_summed / res_total,
    )


def solution(mesh):
    return jax.shard_map(
        local,
        mesh=mesh,
        in_specs=(
            P(("dp", "col"), "row"),
            P(("dp", "row"), "col"),
            P(),
            P(),
            P(("dp", "row"), "col", None),
        ),
        out_specs=(
            P(("dp", "row"), "col", None),
            P(("dp", "col"), "row"),
            P(("dp", "row"), "col"),
            P("dp", None),
            P("dp"),
        ),
        check_vma=False,
    )
```

profile of v0, /device:TPU:0, one launch (start us, length us, event | category | flops | bytes accessed | tf_op | source)
XLA Modules:
  0.0 220.0 jit_solution(12408668370533262803)
XLA Ops:
  8.0 0.0 copy-start
  8.0 0.0 all-reduce.2.cloned.1.call-start
  8.1 15.4 %all_gather.6 = bf16[32,1536]{1,0:T(8,128)(2,1)S(1)} all-gather(bf16[8,1536]{1,0:T(8,128)(2,1)} %param.5), channel_id=1, replica_groups=mesh['dp'=2,'row'=4,'col'=4] {'col'}, dimensions={0}, use_global_device_ids=true | all-gather | bytes 122880 | tf_op jit(solution)/shard_map/all_gather | solution.py:21
  23.4 5.5 %all_gather.7 = bf16[32,1536]{1,0:T(8,128)(2,1)S(1)} all-gather(bf16[8,1536]{1,0:T(8,128)(2,1)} %param.6), channel_id=1, replica_groups=mesh['dp'=2,'row'=4,'col'=4] {'row'}, dimensions={0}, use_global_device_ids=true | all-gather | bytes 122880 | tf_op jit(solution)/shard_map/all_gather | solution.py:19
  29.0 3.6 %fusion = bf16[1536,1536]{1,0:T(8,128)(2,1)} fusion(bf16[32,1536]{1,0:T(8,128)(2,1)S(1)} %all_gather.6, bf16[32,1536]{1,0:T(8,128)(2,1)S(1)} %all_gather.7), kind=kOutput, calls=%fused_computation.2 | convolution fusion | flops 155713536 | bytes 4915200 | tf_op jit(solution)/shard_map/dot_general | solution.py:22
  32.5 21.1 %reshape.22 = bf16[48,32,48,32]{3,2,1,0:T(8,128)(2,1)} reshape(bf16[1536,1536]{1,0:T(8,128)(2,1)} %fusion) | data formatting | bytes 9437184 | tf_op jit(solution)/shard_map/reshape | solution.py:26
  53.7 19.9 %copy.14 = bf16[32,32,48,48]{1,0,3,2:T(8,128)(2,1)} copy(bf16[32,32,48,48]{1,3,0,2:T(8,128)(2,1)} %bitcast.43) | data formatting | bytes 9437184 | tf_op jit(solution)/shard_map/icje,ijf->cef/dot_general | solution.py:63
  73.6 0.0 copy-start.1
  73.6 26.0 %dot_general.28 = bf16[1024,48,48]{0,2,1:T(8,128)(2,1)} reshape(bf16[32,32,48,48]{1,0,3,2:T(8,128)(2,1)} %copy.14) | data formatting | bytes 9437184 | tf_op jit(solution)/shard_map/icje,ijf->cef/dot_general | solution.py:63
  99.7 0.0 copy-done.1
  99.7 4.5 %convolution_bitcast_fusion.1 = f32[1024,128]{1,0:T(8,128)} fusion(bf16[1024,48,48]{0,2,1:T(8,128)(2,1)} %dot_general.28, bf16[48,48,128]{2,1,0:T(8,128)(2,1)S(1)} %copy-done.1), kind=kOutput, calls=%fused_computation.10 | convolution fusion | flops 603979776 | bytes 5832704 | tf_op jit(solution)/shard_map/icje,ijf->cef/dot_general | solution.py:63
  104.2 0.0 all-reduce.2.cloned.1.call-update
  104.2 0.0 reduce-scatter.3.cloned.1.call-start
  104.3 0.0 copy-done
  104.3 6.4 %convert_bitcast_fusion = bf16[48,32,48,32]{2,3,0,1:T(8,128)(2,1)} fusion(bf16[32,32,128,1]{2,1,3,0:T(8,128)(2,1)S(1)} %bitcast.42, bf16[48,48,128]{2,1,0:T(8,128)(2,1)S(1)} %copy-done.1), kind=kOutput, calls=%fused_computation | convolution fusion | flops 606339072 | bytes 5570560 | tf_op jit(solution)/shard_map/ijf,cef->icje/dot_general | solution.py:36
  110.7 20.5 %copy.13 = bf16[48,32,48,32]{3,2,1,0:T(8,128)(2,1)} copy(bf16[48,32,48,32]{2,3,0,1:T(8,128)(2,1)} %convert_bitcast_fusion) | data formatting | bytes 9437184 | tf_op jit(solution)/shard_map/convert_element_type | solution.py:38
  131.2 24.7 %reshape.24 = bf16[1536,1536]{1,0:T(8,128)(2,1)} reshape(bf16[48,32,48,32]{3,2,1,0:T(8,128)(2,1)} %copy.13) | data formatting | bytes 9437184 | tf_op jit(solution)/shard_map/reshape | solution.py:39
  155.9 0.0 copy-start.2
  155.9 4.5 %fusion.1 = f32[32,1536]{1,0:T(8,128)} fusion(bf16[1536,1536]{1,0:T(8,128)(2,1)} %reshape.24, bf16[32,1536]{1,0:T(8,128)(2,1)S(1)} %all_gather.7), kind=kOutput, calls=%fused_computation.5 | convolution fusion | flops 151044096 | bytes 5013504 | tf_op jit(solution)/shard_map/dot_general | solution.py:44
  160.4 0.0 reduce-scatter.3.cloned.1.call-update
  160.4 0.0 reduce-scatter.5.cloned.1.call-start
  160.5 3.9 %fusion.2 = f32[32,1536]{1,0:T(8,128)} fusion(bf16[32,1536]{1,0:T(8,128)(2,1)S(1)} %all_gather.6, bf16[1536,1536]{1,0:T(8,128)(2,1)} %reshape.24), kind=kOutput, calls=%fused_computation.6 | convolution fusion | flops 151044096 | bytes 5013504 | tf_op jit(solution)/shard_map/dot_general | solution.py:57
  164.4 0.0 reduce-scatter.5.cloned.1.call-update
  164.4 0.3 convert_reduce_fusion
  164.8 34.4 %psum.15 = f32[128]{0:T(128)S(1)} all-reduce(f32[128]{0:T(128)S(1)} %convert_reduce_fusion), channel_id=1, replica_groups=mesh['dp'=2,'row'=4,'col'=4] {'row','col'}, use_global_device_ids=true, to_apply=%region_4.0 | all-reduce | flops 128 | bytes 1024 | tf_op jit(solution)/shard_map/psum | solution.py:68
  199.2 0.0 copy-done.2
  199.2 11.0 %fusion.4 = bf16[48,48,128]{2,1,0:T(8,128)(2,1)} fusion(bf16[48,32,48,32]{3,2,1,0:T(8,128)(2,1)} %reshape.22, bf16[32,32,128,1]{2,1,0,3:T(8,128)(2,1)S(1)} %bitcast.41, f32[128]{0:T(128)S(1)} %copy-done.2), kind=kOutput, calls=%fused_computation.9 | convolution fusion | flops 604569600 | bytes 5571072 | tf_op jit(solution)/shard_map/icje,cef->ijf/dot_general | solution.py:30
  210.2 0.5 broadcast_multiply_fusion.1
  210.7 0.0 all-reduce.2.cloned.1.call-done
  210.7 1.9 broadcast_multiply_fusion
  212.6 0.0 reduce-scatter.3.cloned.1.call-done
  212.6 0.0 reduce-scatter.5.cloned.1.call-done
Async XLA Ops:
  8.0 96.3 %copy-start = (bf16[1024,128]{1,0:T(8,128)(2,1)S(1)}, bf16[1024,128]{1,0:T(8,128)(2,1)}, u32[]{:S(2)}) copy-start(bf16[1024,128]{1,0:T(8,128)(2,1)} %param.7) | copy-start | bytes 786436
  8.0 202.7 %all-reduce.2.cloned.1.call-start = ((), (), s32[]{:S(2)}) async-start(), calls=%async_computation.4 | async-start | bytes 1048576 | tf_op jit(solution)/shard_map/psum | solution.py:68
  73.6 26.0 %copy-start.1 = (bf16[48,48,128]{2,1,0:T(8,128)(2,1)S(1)}, bf16[48,48,128]{2,1,0:T(8,128)(2,1)}, u32[]{:S(2)}) copy-start(bf16[48,48,128]{2,1,0:T(8,128)(2,1)} %param.9) | copy-start | bytes 1769476
  104.2 108.3 %reduce-scatter.3.cloned.1.call-start = ((), (), s32[]{:S(2)}) async-start(), calls=%async_computation.2 | async-start | bytes 245760 | tf_op jit(solution)/shard_map/reduce_scatter | solution.py:43
  155.9 43.3 %copy-start.2 = (f32[128]{0:T(128)S(1)}, f32[128]{0:T(128)}, u32[]{:S(2)}) copy-start(f32[128]{0:T(128)} %param.8) | copy-start | bytes 1540
  160.4 52.1 %reduce-scatter.5.cloned.1.call-start = ((), (), s32[]{:S(2)}) async-start(), calls=%async_computation.3 | async-start | bytes 245760 | tf_op jit(solution)/shard_map/reduce_scatter | solution.py:56
Sparse Core Ops, SparseCore 0:
  104.3 91.1 all-reduce.1
Sparse Core Ops, SparseCore 1:
  160.5 20.6 reduce-scatter.2
  184.2 17.9 reduce-scatter.4
where the time goes:
time: 223 us; the launch traced here: 220 us
  local copies, waits for them, and re-layouts  112 us (50%)
  blocking collectives  55.3 us (25%)
  matrix products  33.9 us (15%)
  between operations  15.5 us (7%)
  other arithmetic  2.71 us (1%)
    dot_general x2, local copies, waits for them, and re-layouts, local(): jnp.einsum('icje,ijf->cef', kronecker_pieces, cotangent, preferred_elemen...  46 us
    psum x1, blocking collectives, local(): lax.psum((weight_local, bias_local), ('row', 'col'))  34.4 us
    reshape x1, local copies, waits for them, and re-layouts, local(): outer_grad.reshape(patch_positions * PROJECTED_DEPTH, patch_positions * P...  24.7 us
    reshape x1, local copies, waits for them, and re-layouts, local(): kronecker_array.reshape(patch_positions, PROJECTED_DEPTH, patch_positions...  21.1 us
    convert_element_type x1, local copies, waits for them, and re-layouts, local(): outer_grad = jnp.einsum('ijf,cef->icje', cotangent, projection_cuboid, pr...  20.5 us
    all_gather x1, blocking collectives, local(): lax.all_gather(first_homolog_features, 'col', axis=0, tiled=True)  15.4 us
    dot_general x1, matrix products, local(): jnp.einsum('icje,cef->ijf', kronecker_pieces, projection_cuboid, preferre...  11 us
    dot_general x1, matrix products, local(): jnp.einsum('ijf,cef->icje', cotangent, projection_cuboid, preferred_eleme...  6.37 us
  transfers between devices with their start and end apart: 3, of which 0 were waited for; matrix products, arithmetic and copies ran while one was open for 34% of the time, Pallas kernels for 0%

commit v1 on v0

v1 whole, which is shorter than its diff:
```python
import functools

import jax
import jax.numpy as jnp
from jax import lax
from jax.experimental import pallas as pl
from jax.experimental.pallas import tpu as pltpu
from jax.sharding import PartitionSpec as P

PROJECTED_DEPTH = 32
PAIR_FEATURES = 128
GROUP = 8
STEPS = 4
BIAS_ROWS = 16
LANES = 128
F32 = jnp.float32
BF16 = jnp.bfloat16
VMEM_BYTES = 60 * 1024 * 1024

ROWS_BY_ROWS = (((1,), (1,)), ((), ()))
COLS_BY_COLS = (((0,), (0,)), ((), ()))


def params():
    return pltpu.CompilerParams(vmem_limit_bytes=VMEM_BYTES)


def whole(shape):
    return pl.BlockSpec(shape, lambda t: (0,) * len(shape))


def dot(x, y, dims=(((1,), (0,)), ((), ()))):
    return lax.dot_general(x, y, dims, preferred_element_type=F32)


def prepare_kernel(i_n, j_n, w_ref, g_ref, y_ref, y2_ref, wt_ref, bias_ref, g32, gt, w32, we):
    depth = PROJECTED_DEPTH
    t = pl.program_id(0)

    @pl.when(t == 0)
    def _():
        g32[...] = g_ref[...].astype(F32)
        total = jnp.sum(g32[...], axis=0, keepdims=True)
        high = total.astype(BF16).astype(F32)
        row = lax.broadcasted_iota(jnp.int32, (BIAS_ROWS, PAIR_FEATURES), 0)
        bias_ref[...] = jnp.where(
            row == 0, high, jnp.where(row == 1, total - high, 0.0)
        ).astype(BF16)
        for j in range(j_n):
            gt[j * i_n : (j + 1) * i_n, :] = g32[pl.ds(j, i_n, stride=j_n), :].astype(BF16)
        w32[...] = w_ref[...].astype(F32)
        for e in range(depth):
            block = w32[pl.ds(e, depth, stride=depth), :]
            we[e * depth : (e + 1) * depth, :] = block.astype(BF16)
        wt_ref[...] = we[...].astype(F32).T.astype(BF16)

    size = y_ref.shape[0]
    rows = pl.ds(pl.multiple_of(t * size, size), size)
    y_ref[...] = dot(we[rows, :], g_ref[...], ROWS_BY_ROWS).astype(BF16)
    y2_ref[...] = dot(w_ref[rows, :], gt[...], ROWS_BY_ROWS).astype(BF16)


def prepare(w, g, i_n, j_n):
    pairs = i_n * j_n
    channels = w.shape[0]
    size = channels // STEPS
    return pl.pallas_call(
        functools.partial(prepare_kernel, i_n, j_n),
        grid=(STEPS,),
        in_specs=[whole(w.shape), whole(g.shape)],
        out_specs=[
            pl.BlockSpec((size, pairs), lambda t: (t, 0)),
            pl.BlockSpec((size, pairs), lambda t: (t, 0)),
            whole((PAIR_FEATURES, channels)),
            whole((BIAS_ROWS, PAIR_FEATURES)),
        ],
        out_shape=[
            jax.ShapeDtypeStruct((channels, pairs), BF16),
            jax.ShapeDtypeStruct((channels, pairs), BF16),
            jax.ShapeDtypeStruct((PAIR_FEATURES, channels), BF16),
            jax.ShapeDtypeStruct((BIAS_ROWS, PAIR_FEATURES), BF16),
        ],
        scratch_shapes=[
            pltpu.VMEM(g.shape, F32),
            pltpu.VMEM(g.shape, BF16),
            pltpu.VMEM(w.shape, F32),
            pltpu.VMEM(w.shape, BF16),
        ],
        compiler_params=params(),
        cost_estimate=pl.CostEstimate(
            flops=4 * pairs * channels * PAIR_FEATURES,
            bytes_accessed=4 * pairs * channels,
            transcendentals=0,
        ),
    )(w, g)


def join(pieces, axis, held):
    count = len(pieces)
    depth = pieces[0].shape[0]
    me = lax.axis_index(axis)
    for p, piece in enumerate(pieces):
        start = pl.multiple_of(lax.rem(me - p + count, count) * depth, depth)
        held[pl.ds(start, depth), :] = piece[...].astype(F32)


def repeat_matrix(sequences):
    shape = (sequences, GROUP * sequences)
    lane = lax.broadcasted_iota(jnp.int32, shape, 1)
    row = lax.broadcasted_iota(jnp.int32, shape, 0)
    return (lax.rem(lane, sequences) == row).astype(BF16)


def spread(held, wide):
    both = dot(held[...].T.astype(BF16), repeat_matrix(held.shape[0]))
    for l in range(wide.shape[0]):
        wide[l] = both[:, l * LANES : (l + 1) * LANES]


def tiles_of(sequences, tile):
    lane = lax.broadcasted_iota(jnp.int32, (1, LANES), 1) + tile * LANES
    return [
        (m, lax.div(lane, sequences) == m)
        for m in range(GROUP)
        if m * sequences < (tile + 1) * LANES and (m + 1) * sequences > tile * LANES
    ]


def fill_diagonal(wide, diagonal, slot, channel, positions, sequences):
    for l in range(wide.shape[0]):
        block = wide[l, pl.ds(channel, positions, stride=PROJECTED_DEPTH), :]
        for m, mask in tiles_of(sequences, l):
            diagonal[slot, m * positions : (m + 1) * positions, l * LANES : (l + 1) * LANES] = (
                jnp.where(mask, block, 0.0).astype(BF16)
            )


def outer_kernel(i_n, j_n, row_n, col_n, *refs):
    depth = PROJECTED_DEPTH
    a_pieces, refs = refs[:col_n], refs[col_n:]
    b_pieces, refs = refs[:row_n], refs[row_n:]
    (g_ref, bias_ref), refs = refs[:2], refs[2:]
    x_ref, refs = refs[0], refs[1:]
    messages, refs = refs[:row_n], refs[row_n:]
    a_held, b_held, wide, left, diagonal, total, ordered = refs
    sequences = a_held.shape[0]
    groups = i_n // GROUP
    per_step = depth // STEPS
    span = GROUP * j_n
    t = pl.program_id(0)

    @pl.when(t == 0)
    def _():
        join(a_pieces, "col", a_held)
        join(b_pieces, "row", b_held)
        spread(a_held, wide)
        for l in range(wide.shape[0]):
            members = tiles_of(sequences, l)
            for k in range(groups):
                block = jnp.zeros((depth, LANES), F32)
                for m, mask in members:
                    start = (k * GROUP + m) * depth
                    block = jnp.where(mask, wide[l, start : start + depth, :], block)
                left[k * depth : (k + 1) * depth, l * LANES : (l + 1) * LANES] = block.astype(BF16)
        spread(b_held, wide)
        diagonal[...] = jnp.zeros(diagonal.shape, BF16)

    for e in range(per_step):
        fill_diagonal(wide, diagonal, e, t * per_step + e, j_n, sequences)
    for e in range(0, per_step, 2):
        right = diagonal[e : e + 2].reshape(2 * span, diagonal.shape[2])
        product = dot(left[...], right, ROWS_BY_ROWS).astype(BF16)
        for n in range(2):
            for k in range(groups):
                x_ref[(e + n) * depth : (e + n + 1) * depth, k * span : (k + 1) * span] = product[
                    k * depth : (k + 1) * depth, n * span : (n + 1) * span
                ]
    size = x_ref.shape[0]
    total[pl.ds(pl.multiple_of(t * size, size), size), :] = dot(x_ref[...], g_ref[...])

    @pl.when(t == STEPS - 1)
    def _():
        for c in range(depth):
            ordered[c * depth : (c + 1) * depth, :] = total[pl.ds(c, depth, stride=depth), :]
        share = ordered.shape[0] // row_n
        me = lax.axis_index("row")
        for p, message in enumerate(messages):
            start = pl.multiple_of(lax.rem(me + p, row_n) * share, share)
            message[0:share, :] = ordered[pl.ds(start, share), :].astype(message.dtype)
            message[share:, :] = bias_ref[...].astype(message.dtype)


def outer(a_pieces, b_pieces, g, bias_rows, i_n, j_n, sequences):
    row_n, col_n = len(b_pieces), len(a_pieces)
    depth = PROJECTED_DEPTH
    channels = depth * depth
    pairs = i_n * j_n
    share = channels // row_n
    tiles = GROUP * sequences // LANES
    operands = [*a_pieces, *b_pieces, g, bias_rows]
    results = pl.pallas_call(
        functools.partial(outer_kernel, i_n, j_n, row_n, col_n),
        grid=(STEPS,),
        in_specs=[whole(x.shape) for x in operands],
        out_specs=[pl.BlockSpec((channels // STEPS, pairs), lambda t: (t, 0))]
        + [whole((share + BIAS_ROWS, PAIR_FEATURES))] * row_n,
        out_shape=[jax.ShapeDtypeStruct((channels, pairs), BF16)]
        + [
            jax.ShapeDtypeStruct((share + BIAS_ROWS, PAIR_FEATURES), F32 if p == 0 else BF16)
            for p in range(row_n)
        ],
        scratch_shapes=[
            pltpu.VMEM((sequences, i_n * depth), F32),
            pltpu.VMEM((sequences, j_n * depth), F32),
            pltpu.VMEM((tiles, i_n * depth, LANES), F32),
            pltpu.VMEM((i_n // GROUP * depth, GROUP * sequences), BF16),
            pltpu.VMEM((depth // STEPS, GROUP * j_n, GROUP * sequences), BF16),
            pltpu.VMEM((channels, PAIR_FEATURES), F32),
            pltpu.VMEM((channels, PAIR_FEATURES), F32),
        ],
        compiler_params=params(),
        cost_estimate=pl.CostEstimate(
            flops=4 * pairs * channels * PAIR_FEATURES,
            bytes_accessed=2 * pairs * channels,
            transcendentals=0,
        ),
    )(*operands)
    return results[0], results[1:]


def gradient_kernel(i_n, j_n, row_n, col_n, *refs):
    depth = PROJECTED_DEPTH
    a_pieces, refs = refs[:col_n], refs[col_n:]
    b_pieces, refs = refs[:row_n], refs[row_n:]
    (y_ref, y2_ref), refs = refs[:2], refs[2:]
    left_out, refs = refs[:col_n], refs[col_n:]
    right_out, refs = refs[:row_n], refs[row_n:]
    a_held, b_held, a_wide, b_wide, a_diagonal, b_diagonal, left, right, grown = refs
    sequences = a_held.shape[0]
    per_step = depth // STEPS
    t = pl.program_id(0)

    @pl.when(t == 0)
    def _():
        join(a_pieces, "col", a_held)
        join(b_pieces, "row", b_held)
        spread(a_held, a_wide)
        spread(b_held, b_wide)
        for ref in (a_diagonal, b_diagonal):
            ref[...] = jnp.zeros(ref.shape, BF16)
        for ref in (left, right):
            ref[...] = jnp.zeros(ref.shape, F32)

    def accumulate(source, wide, diagonal, result, positions, others):
        span = GROUP * positions
        for n in range(per_step):
            fill_diagonal(wide, diagonal, n, t * per_step + n, positions, sequences)
        for n in range(0, per_step, 2):
            rows = [
                jnp.concatenate(
                    [
                        source[m * depth : (m + 1) * depth, k * span : (k + 1) * span]
                        for m in (n, n + 1)
                    ],
                    axis=1,
                )
                for k in range(others // GROUP)
            ]
            result[...] += dot(
                jnp.concatenate(rows, axis=0),
                diagonal[n : n + 2].reshape(2 * span, diagonal.shape[2]),
            )

    accumulate(y_ref, b_wide, b_diagonal, left, j_n, i_n)
    accumulate(y2_ref, a_wide, a_diagonal, right, i_n, j_n)

    def deliver(result, held, outs, axis, positions):
        scaled = (result[...] * (1.0 / sequences)).astype(BF16)
        for l in range(scaled.shape[1] // LANES):
            members = dict(tiles_of(sequences, l))
            for k in range(positions // GROUP):
                block = scaled[k * depth : (k + 1) * depth, l * LANES : (l + 1) * LANES]
                for m in range(GROUP):
                    start = (k * GROUP + m) * depth
                    grown[start : start + depth, l * LANES : (l + 1) * LANES] = (
                        jnp.where(members[m], block.astype(F32), 0.0).astype(BF16)
                        if m in members
                        else jnp.zeros((depth, LANES), BF16)
                    )
        held[...] = dot(repeat_matrix(sequences), grown[...], ROWS_BY_ROWS)
        count = len(outs)
        share = sequences // count
        me = lax.axis_index(axis)
        for p, out in enumerate(outs):
            start = pl.multiple_of(lax.rem(me + p, count) * share, share)
            out[...] = held[pl.ds(start, share), :].astype(out.dtype)

    @pl.when(t == STEPS - 1)
    def _():
        deliver(left, a_held, left_out, "col", i_n)
        deliver(right, b_held, right_out, "row", j_n)


def gradients(a_pieces, b_pieces, y, y2, i_n, j_n, sequences):
    row_n, col_n = len(b_pieces), len(a_pieces)
    depth = PROJECTED_DEPTH
    channels, pairs = y.shape
    tiles = GROUP * sequences // LANES
    size = channels // STEPS
    pieces = [*a_pieces, *b_pieces]
    block = pl.BlockSpec((size, pairs), lambda t: (t, 0))

    def part(p, axis_n, positions):
        return jax.ShapeDtypeStruct((sequences // axis_n, positions * depth), F32 if p == 0 else BF16)

    shapes = [part(p, col_n, i_n) for p in range(col_n)] + [part(p, row_n, j_n) for p in range(row_n)]
    results = pl.pallas_call(
        functools.partial(gradient_kernel, i_n, j_n, row_n, col_n),
        grid=(STEPS,),
        in_specs=[whole(x.shape) for x in pieces] + [block, block],
        out_specs=[whole(x.shape) for x in shapes],
        out_shape=shapes,
        scratch_shapes=[
            pltpu.VMEM((sequences, i_n * depth), F32),
            pltpu.VMEM((sequences, j_n * depth), F32),
            pltpu.VMEM((tiles, i_n * depth, LANES), F32),
            pltpu.VMEM((tiles, j_n * depth, LANES), F32),
            pltpu.VMEM((depth // STEPS, GROUP * i_n, GROUP * sequences), BF16),
            pltpu.VMEM((depth // STEPS, GROUP * j_n, GROUP * sequences), BF16),
            pltpu.VMEM((i_n // GROUP * depth, GROUP * sequences), F32),
            pltpu.VMEM((j_n // GROUP * depth, GROUP * sequences), F32),
            pltpu.VMEM((i_n * depth, GROUP * sequences), BF16),
        ],
        compiler_params=params(),
        cost_estimate=pl.CostEstimate(
            flops=4 * pairs * channels * PAIR_FEATURES,
            bytes_accessed=4 * pairs * channels,
            transcendentals=0,
        ),
    )(*pieces, y, y2)
    return results[:col_n], results[col_n:]


def pair_kernel(sequences, x_ref, wt_ref, bias_ref, out_ref):
    product = dot(wt_ref[...], x_ref[...])
    out_ref[...] = (product.T * (1.0 / sequences) + bias_ref[...]).astype(BF16)


def pair(x, wt, output_bias, sequences):
    channels, pairs = x.shape
    count = 3
    size = pairs // count
    return pl.pallas_call(
        functools.partial(pair_kernel, sequences),
        grid=(count,),
        in_specs=[
            pl.BlockSpec((channels, size), lambda t: (0, t)),
            whole(wt.shape),
            whole((1, PAIR_FEATURES)),
        ],
        out_specs=pl.BlockSpec((size, PAIR_FEATURES), lambda t: (t, 0)),
        out_shape=jax.ShapeDtypeStruct((pairs, PAIR_FEATURES), BF16),
        compiler_params=params(),
        cost_estimate=pl.CostEstimate(
            flops=4 * pairs * channels * PAIR_FEATURES,
            bytes_accessed=2 * pairs * channels,
            transcendentals=0,
        ),
    )(x, wt, output_bias.reshape(1, PAIR_FEATURES))


def column_sum_kernel(res_total, *refs):
    pieces, (piece_out, bias_out, held) = refs[:-3], refs[-3:]
    count = len(pieces)
    me = lax.axis_index("col")
    for p, piece in enumerate(pieces):
        held[lax.rem(me - p + count, count)] = piece[...]
    total = held[0].astype(F32)
    for n in range(1, count):
        total += held[n].astype(F32)
    share = piece_out.shape[0]
    piece_out[...] = total[0:share].astype(BF16)
    bias_out[...] = (total[share : share + 1] + total[share + 1 : share + 2]) * (1.0 / res_total)


def column_sum(pieces, res_total):
    rows = pieces[0].shape[0]
    return pl.pallas_call(
        functools.partial(column_sum_kernel, res_total),
        out_shape=[
            jax.ShapeDtypeStruct((rows - BIAS_ROWS, PAIR_FEATURES), BF16),
            jax.ShapeDtypeStruct((1, PAIR_FEATURES), F32),
        ],
        scratch_shapes=[pltpu.VMEM((len(pieces), rows, PAIR_FEATURES), BF16)],
        compiler_params=params(),
    )(*pieces)


def place_kernel(scale, *refs):
    pieces, out_ref = refs[:-1], refs[-1]
    count = len(pieces)
    me = lax.axis_index("row")
    for p, piece in enumerate(pieces):
        share = piece.shape[0]
        start = pl.multiple_of(lax.rem(me - p + count, count) * share, share)
        out_ref[pl.ds(start, share), :] = piece[...].astype(F32) * scale


def place(pieces, scale):
    rows = pieces[0].shape[0] * len(pieces)
    return pl.pallas_call(
        functools.partial(place_kernel, scale),
        out_shape=jax.ShapeDtypeStruct((rows, PAIR_FEATURES), F32),
        compiler_params=params(),
    )(*pieces)


def shift(x, axis, distance):
    count = lax.axis_size(axis)
    return lax.ppermute(x, axis, [(n, (n + distance) % count) for n in range(count)])


def broadcast(x, axis):
    return [x] + [shift(x, axis, d) for d in range(1, lax.axis_size(axis))]


def exchange(parts, axis):
    return [parts[0]] + [shift(parts[d], axis, d) for d in range(1, len(parts))]


def total_of(parts):
    total = parts[0].astype(F32)
    for part in parts[1:]:
        total = total + part.astype(F32)
    return total


def local(
    first_homolog_features, second_homolog_features, final_projection_matrix, output_bias, cotangent
):
    i_n, j_n, _ = cotangent.shape
    sequences = second_homolog_features.shape[0] * lax.axis_size("row")
    res_total = i_n * lax.axis_size("row")
    g = cotangent.reshape(i_n * j_n, PAIR_FEATURES)
    a_pieces = broadcast(first_homolog_features, "col")
    b_pieces = broadcast(second_homolog_features, "row")
    y, y2, wt, bias_rows = prepare(final_projection_matrix, g, i_n, j_n)

    x, messages = outer(a_pieces, b_pieces, g, bias_rows, i_n, j_n, sequences)
    row_parts = exchange(messages, "row")

    left_parts, right_parts = gradients(a_pieces, b_pieces, y, y2, i_n, j_n, sequences)
    left_grad = total_of(exchange(left_parts, "col"))
    right_grad = total_of(exchange(right_parts, "row"))

    share = total_of(row_parts).astype(BF16)
    share, bias_grad = column_sum(broadcast(share, "col"), res_total)
    pair_map = pair(x, wt, output_bias, sequences)
    projection = place(broadcast(share, "row"), 1.0 / (sequences * res_total))
    return (
        pair_map.reshape(i_n, j_n, PAIR_FEATURES),
        left_grad,
        right_grad,
        projection,
        bias_grad.reshape(PAIR_FEATURES),
    )


def solution(mesh):
    return jax.shard_map(
        local,
        mesh=mesh,
        in_specs=(
            P(("dp", "col"), "row"),
            P(("dp", "row"), "col"),
            P(),
            P(),
            P(("dp", "row"), "col", None),
        ),
        out_specs=(
            P(("dp", "row"), "col", None),
            P(("dp", "col"), "row"),
            P(("dp", "row"), "col"),
            P("dp", None),
            P("dp"),
        ),
        check_vma=False,
    )
```

time: 223 us -> 69.6 us (0.31); the launches traced: 220 us -> 69.2 us
  local copies, waits for them, and re-layouts: 112 us -> 2.8 us
  blocking collectives: 55.3 us -> 0 us
  matrix products: 33.9 us -> 0 us
  Pallas kernels: 0 us -> 33.6 us
  starting transfers between devices: 0.13 us -> 21.2 us
  between operations: 15.5 us -> 0.81 us
  waiting for transfers between devices: 0.05 us -> 9.46 us
    dot_general x2 -> x0, local copies, waits for them, and re-layouts: 46 us -> none  [local(): jnp.einsum('icje,ijf->cef', kronecker_pieces, cotangent, preferred_elemen...]
    reshape x2 -> x0, local copies, waits for them, and re-layouts: 45.9 us -> none  [the longest x1 24.7 us: local(): outer_grad.reshape(patch_positions * PROJECTED_DEPTH, patch_positions * P...]
    psum x1 -> x0, blocking collectives: 34.4 us -> none  [local(): lax.psum((weight_local, bias_local), ('row', 'col'))]
    dot_general x6 -> x0, matrix products: 33.9 us -> none  [the longest x1 11 us: local(): jnp.einsum('icje,cef->ijf', kronecker_pieces, projection_cuboid, preferre...]
    pallas_call x0 -> x6, Pallas kernels: none -> 33.6 us  [the longest x1 10.4 us: gradients(): pl.pallas_call(functools.partial(gradient_kernel, i_n, j_n, row_n, col_n)...]
    ppermute x0 -> x21, starting transfers between devices: none -> 21.2 us  [shift(): lax.ppermute(x, axis, [(n, (n + distance) % count) for n in range(count)])]
    all_gather x2 -> x0, blocking collectives: 20.9 us -> none  [the longest x1 15.4 us: local(): lax.all_gather(first_homolog_features, 'col', axis=0, tiled=True)]
    convert_element_type x1 -> x0, local copies, waits for them, and re-layouts: 20.5 us -> none  [local(): outer_grad = jnp.einsum('ijf,cef->icje', cotangent, projection_cuboid, pr...]
  transfers between devices with their start and end apart: 3 -> 21, of which waited for: 0 -> 4; matrix products, arithmetic and copies ran while one was open for 34% -> 2% of each run, Pallas kernels for 0% -> 34%
where the time goes in v1:
time: 69.6 us; the launch traced here: 69.2 us
  Pallas kernels  33.6 us (48%)
  starting transfers between devices  21.2 us (30%)
  waiting for transfers between devices  9.46 us (14%)
  local copies, waits for them, and re-layouts  2.8 us (4%)
  other arithmetic  1.32 us (2%)
  between operations  0.81 us (1%)
    ppermute x21, starting transfers between devices, shift(): lax.ppermute(x, axis, [(n, (n + distance) % count) for n in range(count)])  21.2 us
    pallas_call x1, Pallas kernels, gradients(): pl.pallas_call(functools.partial(gradient_kernel, i_n, j_n, row_n, col_n)...  10.4 us
    ppermute x21, waiting for transfers between devices, shift(): lax.ppermute(x, axis, [(n, (n + distance) % count) for n in range(count)])  9.46 us
    pallas_call x1, Pallas kernels, outer(): pl.pallas_call(functools.partial(outer_kernel, i_n, j_n, row_n, col_n), g...  8.25 us
    pallas_call x1, Pallas kernels, prepare(): pl.pallas_call(functools.partial(prepare_kernel, i_n, j_n), grid=(STEPS,)...  6.88 us
    pallas_call x1, Pallas kernels, pair(): pl.pallas_call(functools.partial(pair_kernel, sequences), grid=(count,),...  4.61 us
    unnamed x36, local copies, waits for them, and re-layouts  2.8 us
    pallas_call x1, Pallas kernels, place(): pl.pallas_call(functools.partial(place_kernel, scale), out_shape=jax.Shap...  1.77 us
  transfers between devices with their start and end apart: 21, of which 4 were waited for; matrix products, arithmetic and copies ran while one was open for 2% of the time, Pallas kernels for 34%

profile of v1, /device:TPU:0, one launch (start us, length us, event | category | flops | bytes accessed | tf_op | source)
XLA Modules:
  0.0 69.2 jit_solution(4059734513139496696)
XLA Ops:
  0.6 5.1 %collective-permute-start.2 = (bf16[8,1536]{1,0:T(8,128)(2,1)}, bf16[8,1536]{1,0:T(8,128)(2,1)S(1)}, u32[]{:S(2)}, u32[]{:S(2)}) collective-permute-start(bf16[8,1536]{1,0:T(8,128)(2,1)} %refs_0_.3), channel_id=1, source_target_pairs={{0,3},{1,0},{2,1},{3,2},{4,7},{5,4},{6,5},{7,6},{8,11},{9,8},{10,9... | collective-permute-start | bytes 73736 | tf_op jit(solution)/shard_map/ppermute | solution.py:420
  5.7 1.0 %collective-permute-start = (bf16[8,1536]{1,0:T(8,128)(2,1)}, bf16[8,1536]{1,0:T(8,128)(2,1)S(1)}, u32[]{:S(2)}, u32[]{:S(2)}) collective-permute-start(bf16[8,1536]{1,0:T(8,128)(2,1)} %refs_0_.3), channel_id=1, source_target_pairs={{0,1},{1,2},{2,3},{3,0},{4,5},{5,6},{6,7},{7,4},{8,9},{9,10},{10,1... | collective-permute-start | bytes 73736 | tf_op jit(solution)/shard_map/ppermute | solution.py:420
  6.8 1.4 %collective-permute-start.4 = (bf16[8,1536]{1,0:T(8,128)(2,1)}, bf16[8,1536]{1,0:T(8,128)(2,1)S(1)}, u32[]{:S(2)}, u32[]{:S(2)}) collective-permute-start(bf16[8,1536]{1,0:T(8,128)(2,1)} %refs_4_.3), channel_id=1, source_target_pairs={{0,8},{4,12},{8,0},{12,4},{1,9},{5,13},{9,1},{13,5},{2,10},{6,14},... | collective-permute-start | bytes 73736 | tf_op jit(solution)/shard_map/ppermute | solution.py:420
  8.2 0.2 collective-permute-start.3
  8.5 6.9 %shard_map.92 = (bf16[1024,2304]{1,0:T(8,128)(2,1)}, bf16[1024,2304]{1,0:T(8,128)(2,1)}, bf16[128,1024]{1,0:T(8,128)(2,1)}, bf16[16,128]{1,0:T(8,128)(2,1)}) custom-call(bf16[1024,128]{1,0:T(8,128)(2,1)} %w_ref.1, bf16[2304,128]{1,0:T(8,128)(2,1)} %bitcast.6), custom_call_target="tpu_custom_call" | custom-call | flops 1207959552 | bytes 9437184 | tf_op jit(solution)/shard_map/pallas_call | solution.py:67
  15.5 0.5 copy-done.11
  16.1 8.2 %shard_map.93 = (bf16[1024,2304]{1,0:T(8,128)(2,1)}, f32[272,128]{1,0:T(8,128)}, bf16[272,128]{1,0:T(8,128)(2,1)}, bf16[272,128]{1,0:T(8,128)(2,1)}, bf16[272,128]{1,0:T(8,128)(2,1)}) custom-call(bf16[8,1536]{1,0:T(8,128)(2,1)} %refs_0_.3, bf16[8,1536]{1,0:T(8,128)(2,1)} %copy-done.12, bf16[8,1536]{1,0:T(8,128)(2,1)} %copy-done.11, ...), custom_call_target="tpu_custom_call" | custom-call | flops 1207959552 | bytes 4718592 | tf_op jit(solution)/shard_map/pallas_call | solution.py:201
  24.3 0.6 collective-permute-start.12
  24.9 1.3 %collective-permute-start.13 = (bf16[272,128]{1,0:T(8,128)(2,1)}, bf16[272,128]{1,0:T(8,128)(2,1)S(1)}, u32[]{:S(2)}, u32[]{:S(2)}) collective-permute-start(bf16[272,128]{1,0:T(8,128)(2,1)} %get-tuple-element.39), channel_id=1, source_target_pairs={{0,8},{4,12},{8,0},{12,4},{1,9},{5,13},{9,1},{13,5},{2,10},{6,14},... | collective-permute-start | bytes 208904 | tf_op jit(solution)/shard_map/ppermute | solution.py:420
  26.4 10.4 %shard_map.95 = (f32[8,1536]{1,0:T(8,128)}, bf16[8,1536]{1,0:T(8,128)(2,1)}, bf16[8,1536]{1,0:T(8,128)(2,1)}, bf16[8,1536]{1,0:T(8,128)(2,1)}, f32[8,1536]{1,0:T...) custom-call(bf16[8,1536]{1,0:T(8,128)(2,1)} %refs_0_.3, ...), custom_call_target="tpu_custom_call" | custom-call | flops 1207959552 | bytes 9437184 | tf_op jit(solution)/shard_map/pallas_call | solution.py:317
  36.8 2.5 %collective-permute-start.6 = (bf16[8,1536]{1,0:T(8,128)(2,1)}, bf16[8,1536]{1,0:T(8,128)(2,1)S(1)}, u32[]{:S(2)}, u32[]{:S(2)}) collective-permute-start(bf16[8,1536]{1,0:T(8,128)(2,1)} %get-tuple-element.30), channel_id=1, source_target_pairs={{0,1},{1,2},{2,3},{3,0},{4,5},{5,6},{6,7},{7,4},{8,9},{9,10},{10,1... | collective-permute-start | bytes 73736 | tf_op jit(solution)/shard_map/ppermute | solution.py:420
  39.3 2.2 %collective-permute-start.7 = (bf16[8,1536]{1,0:T(8,128)(2,1)}, bf16[8,1536]{1,0:T(8,128)(2,1)S(1)}, u32[]{:S(2)}, u32[]{:S(2)}) collective-permute-start(bf16[8,1536]{1,0:T(8,128)(2,1)} %get-tuple-element.31), channel_id=1, source_target_pairs={{0,2},{1,3},{2,0},{3,1},{4,6},{5,7},{6,4},{7,5},{8,10},{9,11},{10,... | collective-permute-start | bytes 73736 | tf_op jit(solution)/shard_map/ppermute | solution.py:420
  41.5 0.4 collective-permute-start.8
  42.0 1.9 %collective-permute-start.17 = (bf16[272,128]{1,0:T(8,128)(2,1)S(1)}, bf16[272,128]{1,0:T(8,128)(2,1)S(1)}, u32[]{:S(2)}, u32[]{:S(2)}) collective-permute-start(bf16[272,128]{1,0:T(8,128)(2,1)S(1)} %add_convert_fusion.refs_0_), channel_id=1, source_target_pairs={{0,3},{1,0},{2,1},{3,2},{4,7},{5,4},{6,5},{7,6},{8,11},{9,8},{10,9... | collective-permute-start | bytes 208904 | tf_op jit(solution)/shard_map/ppermute | solution.py:420
  43.9 4.6 %shard_map.94 = bf16[2304,128]{1,0:T(8,128)(2,1)} custom-call(bf16[1024,2304]{1,0:T(8,128)(2,1)} %get-tuple-element.25.x_ref, bf16[128,1024]{1,0:T(8,128)(2,1)} %get-tuple-element.26.wt_ref, f32[1,128]{1,0:T(1,128)} %bitcast.5), custom_call_target="tpu_custom_call" | custom-call | flops 1207959552 | bytes 4718592 | tf_op jit(solution)/shard_map/pallas_call | solution.py:353
  48.5 1.5 %collective-permute-start.10 = (bf16[8,1536]{1,0:T(8,128)(2,1)S(1)}, bf16[8,1536]{1,0:T(8,128)(2,1)S(1)}, u32[]{:S(2)}, u32[]{:S(2)}) collective-permute-start(bf16[8,1536]{1,0:T(8,128)(2,1)S(1)} %copy-done.17), channel_id=1, source_target_pairs={{0,8},{4,12},{8,0},{12,4},{1,9},{5,13},{9,1},{13,5},{2,10},{6,14},... | collective-permute-start | bytes 73736 | tf_op jit(solution)/shard_map/ppermute | solution.py:420
  50.0 1.2 %collective-permute-start.11 = (bf16[8,1536]{1,0:T(8,128)(2,1)S(1)}, bf16[8,1536]{1,0:T(8,128)(2,1)S(1)}, u32[]{:S(2)}, u32[]{:S(2)}) collective-permute-start(bf16[8,1536]{1,0:T(8,128)(2,1)S(1)} %copy-done.16), channel_id=1, source_target_pairs={{0,12},{4,0},{8,4},{12,8},{1,13},{5,1},{9,5},{13,9},{2,14},{6,2},{... | collective-permute-start | bytes 73736 | tf_op jit(solution)/shard_map/ppermute | solution.py:420
  51.2 0.4 collective-permute-start.16
  51.6 0.6 collective-permute-start.15
  52.2 0.6 convert_add_fusion.1
  52.8 5.3 %collective-permute-done.16.refs_2_ = bf16[272,128]{1,0:T(8,128)(2,1)S(1)} collective-permute-done((bf16[272,128]{1,0:T(8,128)(2,1)S(1)}, bf16[272,128]{1,0:T(8,128)(2,1)S(1)}, u32[]{:S(2)}, u32[]{:S(2)}) %collective-permute-start.16) | collective-permute-done | bytes 69664 | tf_op jit(solution)/shard_map/ppermute | solution.py:420
  58.2 0.6 copy-done.3
  58.8 0.6 copy-done.4
  59.4 1.7 %shard_map.96 = (bf16[256,128]{1,0:T(8,128)(2,1)}, f32[1,128]{1,0:T(1,128)}) custom-call(bf16[272,128]{1,0:T(8,128)(2,1)} %copy-done, bf16[272,128]{1,0:T(8,128)(2,1)} %copy-done.4, bf16[272,128]{1,0:T(8,128)(2,1)} %copy-done.3, bf16[272,128]{1,0:T(8,128)(2,1)} %copy-done.2), custom_call_target="tpu_custom_call" | custom-call | tf_op jit(solution)/shard_map/pallas_call | solution.py:388
  61.1 0.4 collective-permute-start.19
  61.8 0.6 convert_add_fusion
  62.4 1.5 %collective-permute-done.20.refs_3_ = bf16[256,128]{1,0:T(8,128)(2,1)S(1)} collective-permute-done((bf16[256,128]{1,0:T(8,128)(2,1)}, bf16[256,128]{1,0:T(8,128)(2,1)S(1)}, u32[]{:S(2)}, u32[]{:S(2)}) %collective-permute-start.20) | collective-permute-done | bytes 65568 | tf_op jit(solution)/shard_map/ppermute | solution.py:420
  63.9 2.3 %collective-permute-done.19.refs_2_ = bf16[256,128]{1,0:T(8,128)(2,1)S(1)} collective-permute-done((bf16[256,128]{1,0:T(8,128)(2,1)}, bf16[256,128]{1,0:T(8,128)(2,1)S(1)}, u32[]{:S(2)}, u32[]{:S(2)}) %collective-permute-start.19) | collective-permute-done | bytes 65568 | tf_op jit(solution)/shard_map/ppermute | solution.py:420
  66.2 0.3 collective-permute-done.18.refs_1_
  66.5 0.3 copy-done.6
  66.8 0.6 copy-done.7
  67.4 1.8 %shard_map.97 = f32[1024,128]{1,0:T(8,128)} custom-call(bf16[256,128]{1,0:T(8,128)(2,1)} %get-tuple-element.41.refs_0_, bf16[256,128]{1,0:T(8,128)(2,1)} %copy-done.7, bf16[256,128]{1,0:T(8,128)(2,1)} %copy-done.6, bf16[256,128]{1,0:T(8,128)(2,1)} %copy-done.5), custom_call_target="tpu_custom_call" | custom-call | tf_op jit(solution)/shard_map/pallas_call | solution.py:411
  (55 shorter events, 0.7 us)
Async XLA Ops:
  0.6 7.6 %collective-permute-start.2 = (bf16[8,1536]{1,0:T(8,128)(2,1)}, bf16[8,1536]{1,0:T(8,128)(2,1)S(1)}, u32[]{:S(2)}, u32[]{:S(2)}) collective-permute-start(bf16[8,1536]{1,0:T(8,128)(2,1)} %refs_0_.3), channel_id=1, source_target_pairs={{0,3},{1,0},{2,1},{3,2},{4,7},{5,4},{6,5},{7,6},{8,11},{9,8},{10,9... | collective-permute-start | bytes 73736 | tf_op jit(solution)/shard_map/ppermute | solution.py:420
  5.7 9.6 %collective-permute-start.1 = (bf16[8,1536]{1,0:T(8,128)(2,1)}, bf16[8,1536]{1,0:T(8,128)(2,1)S(1)}, u32[]{:S(2)}, u32[]{:S(2)}) collective-permute-start(bf16[8,1536]{1,0:T(8,128)(2,1)} %refs_0_.3), channel_id=1, source_target_pairs={{0,2},{1,3},{2,0},{3,1},{4,6},{5,7},{6,4},{7,5},{8,10},{9,11},{10,... | collective-permute-start | bytes 73736 | tf_op jit(solution)/shard_map/ppermute | solution.py:420
  5.7 9.6 %collective-permute-start = (bf16[8,1536]{1,0:T(8,128)(2,1)}, bf16[8,1536]{1,0:T(8,128)(2,1)S(1)}, u32[]{:S(2)}, u32[]{:S(2)}) collective-permute-start(bf16[8,1536]{1,0:T(8,128)(2,1)} %refs_0_.3), channel_id=1, source_target_pairs={{0,1},{1,2},{2,3},{3,0},{4,5},{5,6},{6,7},{7,4},{8,9},{9,10},{10,1... | collective-permute-start | bytes 73736 | tf_op jit(solution)/shard_map/ppermute | solution.py:420
  6.7 8.6 %collective-permute-start.5 = (bf16[8,1536]{1,0:T(8,128)(2,1)}, bf16[8,1536]{1,0:T(8,128)(2,1)S(1)}, u32[]{:S(2)}, u32[]{:S(2)}) collective-permute-start(bf16[8,1536]{1,0:T(8,128)(2,1)} %refs_4_.3), channel_id=1, source_target_pairs={{0,12},{4,0},{8,4},{12,8},{1,13},{5,1},{9,5},{13,9},{2,14},{6,2},{... | collective-permute-start | bytes 73736 | tf_op jit(solution)/shard_map/ppermute | solution.py:420
  6.8 8.6 %collective-permute-start.4 = (bf16[8,1536]{1,0:T(8,128)(2,1)}, bf16[8,1536]{1,0:T(8,128)(2,1)S(1)}, u32[]{:S(2)}, u32[]{:S(2)}) collective-permute-start(bf16[8,1536]{1,0:T(8,128)(2,1)} %refs_4_.3), channel_id=1, source_target_pairs={{0,8},{4,12},{8,0},{12,4},{1,9},{5,13},{9,1},{13,5},{2,10},{6,14},... | collective-permute-start | bytes 73736 | tf_op jit(solution)/shard_map/ppermute | solution.py:420
  8.2 7.2 %copy-start.10 = (bf16[8,1536]{1,0:T(8,128)(2,1)}, bf16[8,1536]{1,0:T(8,128)(2,1)S(1)}, u32[]{:S(2)}) copy-start(bf16[8,1536]{1,0:T(8,128)(2,1)S(1)} %collective-permute-done.2.refs_3_) | copy-start | bytes 73732
  8.2 7.2 %collective-permute-start.3 = (bf16[8,1536]{1,0:T(8,128)(2,1)}, bf16[8,1536]{1,0:T(8,128)(2,1)S(1)}, u32[]{:S(2)}, u32[]{:S(2)}) collective-permute-start(bf16[8,1536]{1,0:T(8,128)(2,1)} %refs_4_.3), channel_id=1, source_target_pairs={{0,4},{4,8},{8,12},{12,0},{1,5},{5,9},{9,13},{13,1},{2,6},{6,10},{... | collective-permute-start | bytes 73736 | tf_op jit(solution)/shard_map/ppermute | solution.py:420
  24.3 17.2 %collective-permute-start.12 = (bf16[272,128]{1,0:T(8,128)(2,1)}, bf16[272,128]{1,0:T(8,128)(2,1)S(1)}, u32[]{:S(2)}, u32[]{:S(2)}) collective-permute-start(bf16[272,128]{1,0:T(8,128)(2,1)} %get-tuple-element.38), channel_id=1, source_target_pairs={{0,4},{4,8},{8,12},{12,0},{1,5},{5,9},{9,13},{13,1},{2,6},{6,10},{... | collective-permute-start | bytes 208904 | tf_op jit(solution)/shard_map/ppermute | solution.py:420
  24.9 17.0 %collective-permute-start.13 = (bf16[272,128]{1,0:T(8,128)(2,1)}, bf16[272,128]{1,0:T(8,128)(2,1)S(1)}, u32[]{:S(2)}, u32[]{:S(2)}) collective-permute-start(bf16[272,128]{1,0:T(8,128)(2,1)} %get-tuple-element.39), channel_id=1, source_target_pairs={{0,8},{4,12},{8,0},{12,4},{1,9},{5,13},{9,1},{13,5},{2,10},{6,14},... | collective-permute-start | bytes 208904 | tf_op jit(solution)/shard_map/ppermute | solution.py:420
  26.3 15.7 %collective-permute-start.14 = (bf16[272,128]{1,0:T(8,128)(2,1)}, bf16[272,128]{1,0:T(8,128)(2,1)S(1)}, u32[]{:S(2)}, u32[]{:S(2)}) collective-permute-start(bf16[272,128]{1,0:T(8,128)(2,1)} %get-tuple-element.40), channel_id=1, source_target_pairs={{0,12},{4,0},{8,4},{12,8},{1,13},{5,1},{9,5},{13,9},{2,14},{6,2},{... | collective-permute-start | bytes 208904 | tf_op jit(solution)/shard_map/ppermute | solution.py:420
  26.4 15.6 %copy-start.1 = (f32[272,128]{1,0:T(8,128)S(1)}, f32[272,128]{1,0:T(8,128)}, u32[]{:S(2)}) copy-start(f32[272,128]{1,0:T(8,128)} %get-tuple-element.37) | copy-start | bytes 417796
  36.8 11.7 %copy-start.17 = (bf16[8,1536]{1,0:T(8,128)(2,1)S(1)}, bf16[8,1536]{1,0:T(8,128)(2,1)}, u32[]{:S(2)}) copy-start(bf16[8,1536]{1,0:T(8,128)(2,1)} %get-tuple-element.35) | copy-start | bytes 73732
  36.8 13.2 %copy-start.16 = (bf16[8,1536]{1,0:T(8,128)(2,1)S(1)}, bf16[8,1536]{1,0:T(8,128)(2,1)}, u32[]{:S(2)}) copy-start(bf16[8,1536]{1,0:T(8,128)(2,1)} %get-tuple-element.36) | copy-start | bytes 73732
  36.8 15.4 %copy-start.9 = (f32[8,1536]{1,0:T(8,128)S(1)}, f32[8,1536]{1,0:T(8,128)}, u32[]{:S(2)}) copy-start(f32[8,1536]{1,0:T(8,128)} %get-tuple-element.29) | copy-start | bytes 147460
  36.8 24.9 %copy-start.8 = (f32[8,1536]{1,0:T(8,128)S(1)}, f32[8,1536]{1,0:T(8,128)}, u32[]{:S(2)}) copy-start(f32[8,1536]{1,0:T(8,128)} %get-tuple-element.33) | copy-start | bytes 147460
  36.8 11.6 %collective-permute-start.6 = (bf16[8,1536]{1,0:T(8,128)(2,1)}, bf16[8,1536]{1,0:T(8,128)(2,1)S(1)}, u32[]{:S(2)}, u32[]{:S(2)}) collective-permute-start(bf16[8,1536]{1,0:T(8,128)(2,1)} %get-tuple-element.30), channel_id=1, source_target_pairs={{0,1},{1,2},{2,3},{3,0},{4,5},{5,6},{6,7},{7,4},{8,9},{9,10},{10,1... | collective-permute-start | bytes 73736 | tf_op jit(solution)/shard_map/ppermute | solution.py:420
  39.3 10.7 %collective-permute-start.7 = (bf16[8,1536]{1,0:T(8,128)(2,1)}, bf16[8,1536]{1,0:T(8,128)(2,1)S(1)}, u32[]{:S(2)}, u32[]{:S(2)}) collective-permute-start(bf16[8,1536]{1,0:T(8,128)(2,1)} %get-tuple-element.31), channel_id=1, source_target_pairs={{0,2},{1,3},{2,0},{3,1},{4,6},{5,7},{6,4},{7,5},{8,10},{9,11},{10,... | collective-permute-start | bytes 73736 | tf_op jit(solution)/shard_map/ppermute | solution.py:420
  41.5 9.6 %collective-permute-start.8 = (bf16[8,1536]{1,0:T(8,128)(2,1)}, bf16[8,1536]{1,0:T(8,128)(2,1)S(1)}, u32[]{:S(2)}, u32[]{:S(2)}) collective-permute-start(bf16[8,1536]{1,0:T(8,128)(2,1)} %get-tuple-element.32), channel_id=1, source_target_pairs={{0,3},{1,0},{2,1},{3,2},{4,7},{5,4},{6,5},{7,6},{8,11},{9,8},{10,9... | collective-permute-start | bytes 73736 | tf_op jit(solution)/shard_map/ppermute | solution.py:420
  41.9 19.6 %collective-permute-start.9 = (bf16[8,1536]{1,0:T(8,128)(2,1)}, bf16[8,1536]{1,0:T(8,128)(2,1)S(1)}, u32[]{:S(2)}, u32[]{:S(2)}) collective-permute-start(bf16[8,1536]{1,0:T(8,128)(2,1)} %get-tuple-element.34), channel_id=1, source_target_pairs={{0,4},{4,8},{8,12},{12,0},{1,5},{5,9},{9,13},{13,1},{2,6},{6,10},{... | collective-permute-start | bytes 73736 | tf_op jit(solution)/shard_map/ppermute | solution.py:420
  42.0 16.2 %copy-start = (bf16[272,128]{1,0:T(8,128)(2,1)}, bf16[272,128]{1,0:T(8,128)(2,1)S(1)}, u32[]{:S(2)}) copy-start(bf16[272,128]{1,0:T(8,128)(2,1)S(1)} %add_convert_fusion.refs_0_) | copy-start | bytes 208900
  42.0 9.6 %collective-permute-start.17 = (bf16[272,128]{1,0:T(8,128)(2,1)S(1)}, bf16[272,128]{1,0:T(8,128)(2,1)S(1)}, u32[]{:S(2)}, u32[]{:S(2)}) collective-permute-start(bf16[272,128]{1,0:T(8,128)(2,1)S(1)} %add_convert_fusion.refs_0_), channel_id=1, source_target_pairs={{0,3},{1,0},{2,1},{3,2},{4,7},{5,4},{6,5},{7,6},{8,11},{9,8},{10,9... | collective-permute-start | bytes 208904 | tf_op jit(solution)/shard_map/ppermute | solution.py:420
  48.5 13.3 %collective-permute-start.10 = (bf16[8,1536]{1,0:T(8,128)(2,1)S(1)}, bf16[8,1536]{1,0:T(8,128)(2,1)S(1)}, u32[]{:S(2)}, u32[]{:S(2)}) collective-permute-start(bf16[8,1536]{1,0:T(8,128)(2,1)S(1)} %copy-done.17), channel_id=1, source_target_pairs={{0,8},{4,12},{8,0},{12,4},{1,9},{5,13},{9,1},{13,5},{2,10},{6,14},... | collective-permute-start | bytes 73736 | tf_op jit(solution)/shard_map/ppermute | solution.py:420
  50.0 11.7 %collective-permute-start.11 = (bf16[8,1536]{1,0:T(8,128)(2,1)S(1)}, bf16[8,1536]{1,0:T(8,128)(2,1)S(1)}, u32[]{:S(2)}, u32[]{:S(2)}) collective-permute-start(bf16[8,1536]{1,0:T(8,128)(2,1)S(1)} %copy-done.16), channel_id=1, source_target_pairs={{0,12},{4,0},{8,4},{12,8},{1,13},{5,1},{9,5},{13,9},{2,14},{6,2},{... | collective-permute-start | bytes 73736 | tf_op jit(solution)/shard_map/ppermute | solution.py:420
  51.2 7.0 %collective-permute-start.16 = (bf16[272,128]{1,0:T(8,128)(2,1)S(1)}, bf16[272,128]{1,0:T(8,128)(2,1)S(1)}, u32[]{:S(2)}, u32[]{:S(2)}) collective-permute-start(bf16[272,128]{1,0:T(8,128)(2,1)S(1)} %add_convert_fusion.refs_0_), channel_id=1, source_target_pairs={{0,2},{1,3},{2,0},{3,1},{4,6},{5,7},{6,4},{7,5},{8,10},{9,11},{10,... | collective-permute-start | bytes 208904 | tf_op jit(solution)/shard_map/ppermute | solution.py:420
  51.6 6.5 %copy-start.2 = (bf16[272,128]{1,0:T(8,128)(2,1)}, bf16[272,128]{1,0:T(8,128)(2,1)S(1)}, u32[]{:S(2)}) copy-start(bf16[272,128]{1,0:T(8,128)(2,1)S(1)} %collective-permute-done.17.refs_3_) | copy-start | bytes 208900
  51.6 6.5 %collective-permute-start.15 = (bf16[272,128]{1,0:T(8,128)(2,1)S(1)}, bf16[272,128]{1,0:T(8,128)(2,1)S(1)}, u32[]{:S(2)}, u32[]{:S(2)}) collective-permute-start(bf16[272,128]{1,0:T(8,128)(2,1)S(1)} %add_convert_fusion.refs_0_), channel_id=1, source_target_pairs={{0,1},{1,2},{2,3},{3,0},{4,5},{5,6},{6,7},{7,4},{8,9},{9,10},{10,1... | collective-permute-start | bytes 208904 | tf_op jit(solution)/shard_map/ppermute | solution.py:420
  58.1 0.6 copy-start.3
  58.8 0.6 copy-start.4
  61.1 2.8 %collective-permute-start.20 = (bf16[256,128]{1,0:T(8,128)(2,1)}, bf16[256,128]{1,0:T(8,128)(2,1)S(1)}, u32[]{:S(2)}, u32[]{:S(2)}) collective-permute-start(bf16[256,128]{1,0:T(8,128)(2,1)} %get-tuple-element.41.refs_0_), channel_id=1, source_target_pairs={{0,12},{4,0},{8,4},{12,8},{1,13},{5,1},{9,5},{13,9},{2,14},{6,2},{... | collective-permute-start | bytes 196616 | tf_op jit(solution)/shard_map/ppermute | solution.py:420
  61.1 5.1 %collective-permute-start.19 = (bf16[256,128]{1,0:T(8,128)(2,1)}, bf16[256,128]{1,0:T(8,128)(2,1)S(1)}, u32[]{:S(2)}, u32[]{:S(2)}) collective-permute-start(bf16[256,128]{1,0:T(8,128)(2,1)} %get-tuple-element.41.refs_0_), channel_id=1, source_target_pairs={{0,8},{4,12},{8,0},{12,4},{1,9},{5,13},{9,1},{13,5},{2,10},{6,14},... | collective-permute-start | bytes 196616 | tf_op jit(solution)/shard_map/ppermute | solution.py:420
  61.5 5.0 %collective-permute-start.18 = (bf16[256,128]{1,0:T(8,128)(2,1)}, bf16[256,128]{1,0:T(8,128)(2,1)S(1)}, u32[]{:S(2)}, u32[]{:S(2)}) collective-permute-start(bf16[256,128]{1,0:T(8,128)(2,1)} %get-tuple-element.41.refs_0_), channel_id=1, source_target_pairs={{0,4},{4,8},{8,12},{12,0},{1,5},{5,9},{9,13},{13,1},{2,6},{6,10},{... | collective-permute-start | bytes 196616 | tf_op jit(solution)/shard_map/ppermute | solution.py:420
  63.8 2.7 %copy-start.5 = (bf16[256,128]{1,0:T(8,128)(2,1)}, bf16[256,128]{1,0:T(8,128)(2,1)S(1)}, u32[]{:S(2)}) copy-start(bf16[256,128]{1,0:T(8,128)(2,1)S(1)} %collective-permute-done.20.refs_3_) | copy-start | bytes 196612
  (7 other events, 4.3 us)

commit v2 on v1

--- a/solution.py
+++ b/solution.py
@@ -15,14 +15,14 @@
 LANES = 128
 F32 = jnp.float32
 BF16 = jnp.bfloat16
-VMEM_BYTES = 60 * 1024 * 1024
+MIB = 1024 * 1024
 
 ROWS_BY_ROWS = (((1,), (1,)), ((), ()))
 COLS_BY_COLS = (((0,), (0,)), ((), ()))
 
 
-def params():
-    return pltpu.CompilerParams(vmem_limit_bytes=VMEM_BYTES)
+def params(sequences=0):
+    return pltpu.CompilerParams(vmem_limit_bytes=min(10 + 10 * sequences // 32, 50) * MIB + 2 * MIB)
 
 
 def whole(shape):
@@ -86,7 +86,7 @@
             pltpu.VMEM(w.shape, F32),
             pltpu.VMEM(w.shape, BF16),
         ],
-        compiler_params=params(),
+        compiler_params=params(32),
         cost_estimate=pl.CostEstimate(
             flops=4 * pairs * channels * PAIR_FEATURES,
             bytes_accessed=4 * pairs * channels,
@@ -218,7 +218,7 @@
             pltpu.VMEM((channels, PAIR_FEATURES), F32),
             pltpu.VMEM((channels, PAIR_FEATURES), F32),
         ],
-        compiler_params=params(),
+        compiler_params=params(sequences),
         cost_estimate=pl.CostEstimate(
             flops=4 * pairs * channels * PAIR_FEATURES,
             bytes_accessed=2 * pairs * channels,
@@ -331,7 +331,7 @@
             pltpu.VMEM((j_n // GROUP * depth, GROUP * sequences), F32),
             pltpu.VMEM((i_n * depth, GROUP * sequences), BF16),
         ],
-        compiler_params=params(),
+        compiler_params=params(sequences),
         cost_estimate=pl.CostEstimate(
             flops=4 * pairs * channels * PAIR_FEATURES,
             bytes_accessed=4 * pairs * channels,

time: 69.6 us -> 59.4 us (0.85)
  Pallas kernels: 33.6 us -> 21.9 us
  local copies, waits for them, and re-layouts: 2.8 us -> 4.55 us
    pallas_call x1, Pallas kernels: 6.88 us -> 4.12 us  [prepare(): pl.pallas_call(functools.partial(prepare_kernel, i_n, j_n), grid=(STEPS,)...]
    pallas_call x1, Pallas kernels: 10.4 us -> 7.93 us  [gradients(): pl.pallas_call(functools.partial(gradient_kernel, i_n, j_n, row_n, col_n)...]
    pallas_call x1, Pallas kernels: 8.25 us -> 5.82 us  [outer(): pl.pallas_call(functools.partial(outer_kernel, i_n, j_n, row_n, col_n), g...]
    pallas_call x1, Pallas kernels: 4.61 us -> 2.56 us  [pair(): pl.pallas_call(functools.partial(pair_kernel, sequences), grid=(count,),...]
    unnamed x36 -> x12, local copies, waits for them, and re-layouts: 2.8 us -> 4.55 us
    pallas_call x1, Pallas kernels: 1.69 us -> 0.59 us  [column_sum(): pl.pallas_call(functools.partial(column_sum_kernel, res_total), out_shape...]
    pallas_call x1, Pallas kernels: 1.77 us -> 0.84 us  [place(): pl.pallas_call(functools.partial(place_kernel, scale), out_shape=jax.Shap...]
  transfers between devices with their start and end apart: 21 -> 21, of which waited for: 4 -> 4; matrix products, arithmetic and copies ran while one was open for 2% -> 2% of each run, Pallas kernels for 34% -> 26%
where the time goes in v2:
time: 59.4 us; the launch traced here: 59.1 us
  Pallas kernels  21.9 us (37%)
  starting transfers between devices  21.8 us (37%)
  waiting for transfers between devices  8.83 us (15%)
  local copies, waits for them, and re-layouts  4.55 us (8%)
  other arithmetic  1.32 us (2%)
  between operations  0.73 us (1%)
    ppermute x21, starting transfers between devices, shift(): lax.ppermute(x, axis, [(n, (n + distance) % count) for n in range(count)])  21.8 us
    ppermute x21, waiting for transfers between devices, shift(): lax.ppermute(x, axis, [(n, (n + distance) % count) for n in range(count)])  8.83 us
    pallas_call x1, Pallas kernels, gradients(): pl.pallas_call(functools.partial(gradient_kernel, i_n, j_n, row_n, col_n)...  7.93 us
    pallas_call x1, Pallas kernels, outer(): pl.pallas_call(functools.partial(outer_kernel, i_n, j_n, row_n, col_n), g...  5.82 us
    unnamed x12, local copies, waits for them, and re-layouts  4.55 us
    pallas_call x1, Pallas kernels, prepare(): pl.pallas_call(functools.partial(prepare_kernel, i_n, j_n), grid=(STEPS,)...  4.12 us
    pallas_call x1, Pallas kernels, pair(): pl.pallas_call(functools.partial(pair_kernel, sequences), grid=(count,),...  2.56 us
    add x2, other arithmetic, total_of(): total = total + part.astype(F32)  1.27 us
  transfers between devices with their start and end apart: 21, of which 4 were waited for; matrix products, arithmetic and copies ran while one was open for 2% of the time, Pallas kernels for 26%

profile of v2, /device:TPU:0, one launch (start us, length us, event | category | flops | bytes accessed | tf_op | source)
XLA Modules:
  0.0 59.1 jit_solution(11949479938993459828)
XLA Ops:
  0.6 5.1 %collective-permute-start.2 = (bf16[8,1536]{1,0:T(8,128)(2,1)}, bf16[8,1536]{1,0:T(8,128)(2,1)S(1)}, u32[]{:S(2)}, u32[]{:S(2)}) collective-permute-start(bf16[8,1536]{1,0:T(8,128)(2,1)} %refs_0_.3), channel_id=1, source_target_pairs={{0,3},{1,0},{2,1},{3,2},{4,7},{5,4},{6,5},{7,6},{8,11},{9,8},{10,9... | collective-permute-start | bytes 73736 | tf_op jit(solution)/shard_map/ppermute | solution.py:420
  5.7 1.0 %collective-permute-start = (bf16[8,1536]{1,0:T(8,128)(2,1)}, bf16[8,1536]{1,0:T(8,128)(2,1)S(1)}, u32[]{:S(2)}, u32[]{:S(2)}) collective-permute-start(bf16[8,1536]{1,0:T(8,128)(2,1)} %refs_0_.3), channel_id=1, source_target_pairs={{0,1},{1,2},{2,3},{3,0},{4,5},{5,6},{6,7},{7,4},{8,9},{9,10},{10,1... | collective-permute-start | bytes 73736 | tf_op jit(solution)/shard_map/ppermute | solution.py:420
  6.8 1.4 %collective-permute-start.4 = (bf16[8,1536]{1,0:T(8,128)(2,1)}, bf16[8,1536]{1,0:T(8,128)(2,1)S(1)}, u32[]{:S(2)}, u32[]{:S(2)}) collective-permute-start(bf16[8,1536]{1,0:T(8,128)(2,1)} %refs_4_.3), channel_id=1, source_target_pairs={{0,8},{4,12},{8,0},{12,4},{1,9},{5,13},{9,1},{13,5},{2,10},{6,14},... | collective-permute-start | bytes 73736 | tf_op jit(solution)/shard_map/ppermute | solution.py:420
  8.2 0.2 collective-permute-start.3
  8.5 1.1 %copy-done.3 = bf16[48,48,128]{2,1,0:T(8,128)(2,1)S(1)} copy-done((bf16[48,48,128]{2,1,0:T(8,128)(2,1)S(1)}, bf16[48,48,128]{2,1,0:T(8,128)(2,1)}, u32[]{:S(2)}) %copy-start.3) | copy-done | bytes 589848
  9.5 0.9 %copy-done.5 = bf16[1024,128]{1,0:T(8,128)(2,1)S(1)} copy-done((bf16[1024,128]{1,0:T(8,128)(2,1)S(1)}, bf16[1024,128]{1,0:T(8,128)(2,1)}, u32[]{:S(2)}) %copy-start.5) | copy-done | bytes 262168
  10.5 4.1 %shard_map.92 = (bf16[1024,2304]{1,0:T(8,128)(2,1)S(1)}, bf16[1024,2304]{1,0:T(8,128)(2,1)S(1)}, bf16[128,1024]{1,0:T(8,128)(2,1)S(1)}, bf16[16,128]{1,0:T(8,128)(2,1)S(1)}) custom-call(bf16[1024,128]{1,0:T(8,128)(2,1)S(1)} %copy-done.5, bf16[2304,128]{1,0:T(8,128)(2,1)S(1)} %bitcast.5), custom_call_target="tpu_custom_call" | custom-call | flops 1207959552 | bytes 9437184 | tf_op jit(solution)/shard_map/pallas_call | solution.py:67
  14.7 0.7 %copy-done = bf16[8,1536]{1,0:T(8,128)(2,1)S(1)} copy-done((bf16[8,1536]{1,0:T(8,128)(2,1)S(1)}, bf16[8,1536]{1,0:T(8,128)(2,1)}, u32[]{:S(2)}) %copy-start) | copy-done | bytes 24600
  15.4 0.7 %copy-done.1 = bf16[8,1536]{1,0:T(8,128)(2,1)S(1)} copy-done((bf16[8,1536]{1,0:T(8,128)(2,1)S(1)}, bf16[8,1536]{1,0:T(8,128)(2,1)}, u32[]{:S(2)}) %copy-start.1) | copy-done | bytes 24600
  16.1 1.1 %copy-done.4 = bf16[48,48,128]{2,1,0:T(8,128)(2,1)S(1)} copy-done((bf16[48,48,128]{2,1,0:T(8,128)(2,1)S(1)}, bf16[48,48,128]{2,1,0:T(8,128)(2,1)}, u32[]{:S(2)}) %copy-start.4) | copy-done | bytes 589848
  17.2 5.8 %shard_map.93 = (bf16[1024,2304]{1,0:T(8,128)(2,1)S(1)}, f32[272,128]{1,0:T(8,128)S(1)}, bf16[272,128]{1,0:T(8,128)(2,1)S(1)}, bf16[272,128]{1,0:T(8,128)(2,1)S(1)}, bf16[272,128]{1,0:T(8,128)(2,1)S(1)}) custom-call(bf16[8,1536]{1,0:T(8,128)(2,1)S(1)} %copy-done, bf16[8,1536]{1,0:T(8,128)(2,1)S(1)} %collective-permute-done.refs_1_, ...), custom_call_target="tpu_custom_call" | custom-call | flops 1207959552 | bytes 4718592 | tf_op jit(solution)/shard_map/pallas_call | solution.py:201
  23.0 0.7 %collective-permute-start.12 = (bf16[272,128]{1,0:T(8,128)(2,1)S(1)}, bf16[272,128]{1,0:T(8,128)(2,1)S(1)}, u32[]{:S(2)}, u32[]{:S(2)}) collective-permute-start(bf16[272,128]{1,0:T(8,128)(2,1)S(1)} %get-tuple-element.38), channel_id=1, source_target_pairs={{0,4},{4,8},{8,12},{12,0},{1,5},{5,9},{9,13},{13,1},{2,6},{6,10},{... | collective-permute-start | bytes 208904 | tf_op jit(solution)/shard_map/ppermute | solution.py:420
  23.7 1.3 %collective-permute-start.13 = (bf16[272,128]{1,0:T(8,128)(2,1)S(1)}, bf16[272,128]{1,0:T(8,128)(2,1)S(1)}, u32[]{:S(2)}, u32[]{:S(2)}) collective-permute-start(bf16[272,128]{1,0:T(8,128)(2,1)S(1)} %get-tuple-element.39), channel_id=1, source_target_pairs={{0,8},{4,12},{8,0},{12,4},{1,9},{5,13},{9,1},{13,5},{2,10},{6,14},... | collective-permute-start | bytes 208904 | tf_op jit(solution)/shard_map/ppermute | solution.py:420
  25.1 7.9 %shard_map.95 = (f32[8,1536]{1,0:T(8,128)S(1)}, bf16[8,1536]{1,0:T(8,128)(2,1)S(1)}, bf16[8,1536]{1,0:T(8,128)(2,1)S(1)}, bf16[8,1536]{1,0:T(8,128)(2,1)S(1)}, f...) custom-call(bf16[8,1536]{1,0:T(8,128)(2,1)S(1)} %copy-done, ...), custom_call_target="tpu_custom_call" | custom-call | flops 1207959552 | bytes 9437184 | tf_op jit(solution)/shard_map/pallas_call | solution.py:317
  33.1 2.5 %collective-permute-start.6 = (bf16[8,1536]{1,0:T(8,128)(2,1)S(1)}, bf16[8,1536]{1,0:T(8,128)(2,1)S(1)}, u32[]{:S(2)}, u32[]{:S(2)}) collective-permute-start(bf16[8,1536]{1,0:T(8,128)(2,1)S(1)} %get-tuple-element.30), channel_id=1, source_target_pairs={{0,1},{1,2},{2,3},{3,0},{4,5},{5,6},{6,7},{7,4},{8,9},{9,10},{10,1... | collective-permute-start | bytes 73736 | tf_op jit(solution)/shard_map/ppermute | solution.py:420
  35.6 2.2 %collective-permute-start.7 = (bf16[8,1536]{1,0:T(8,128)(2,1)S(1)}, bf16[8,1536]{1,0:T(8,128)(2,1)S(1)}, u32[]{:S(2)}, u32[]{:S(2)}) collective-permute-start(bf16[8,1536]{1,0:T(8,128)(2,1)S(1)} %get-tuple-element.31), channel_id=1, source_target_pairs={{0,2},{1,3},{2,0},{3,1},{4,6},{5,7},{6,4},{7,5},{8,10},{9,11},{10,... | collective-permute-start | bytes 73736 | tf_op jit(solution)/shard_map/ppermute | solution.py:420
  37.8 0.3 collective-permute-start.8
  38.2 1.9 %collective-permute-start.17 = (bf16[272,128]{1,0:T(8,128)(2,1)S(1)}, bf16[272,128]{1,0:T(8,128)(2,1)S(1)}, u32[]{:S(2)}, u32[]{:S(2)}) collective-permute-start(bf16[272,128]{1,0:T(8,128)(2,1)S(1)} %add_convert_fusion.refs_0_), channel_id=1, source_target_pairs={{0,3},{1,0},{2,1},{3,2},{4,7},{5,4},{6,5},{7,6},{8,11},{9,8},{10,9... | collective-permute-start | bytes 208904 | tf_op jit(solution)/shard_map/ppermute | solution.py:420
  40.1 2.6 %shard_map.94 = bf16[2304,128]{1,0:T(8,128)(2,1)} custom-call(bf16[1024,2304]{1,0:T(8,128)(2,1)S(1)} %get-tuple-element.25.x_ref, bf16[128,1024]{1,0:T(8,128)(2,1)S(1)} %get-tuple-element.26.wt_ref, f32[1,128]{1,0:T(1,128)S(1)} %bitcast.4), custom_call_target="tpu_custom_call" | custom-call | flops 1207959552 | bytes 4718592 | tf_op jit(solution)/shard_map/pallas_call | solution.py:353
  42.6 1.5 %collective-permute-start.10 = (bf16[8,1536]{1,0:T(8,128)(2,1)S(1)}, bf16[8,1536]{1,0:T(8,128)(2,1)S(1)}, u32[]{:S(2)}, u32[]{:S(2)}) collective-permute-start(bf16[8,1536]{1,0:T(8,128)(2,1)S(1)} %get-tuple-element.35), channel_id=1, source_target_pairs={{0,8},{4,12},{8,0},{12,4},{1,9},{5,13},{9,1},{13,5},{2,10},{6,14},... | collective-permute-start | bytes 73736 | tf_op jit(solution)/shard_map/ppermute | solution.py:420
  44.1 1.2 %collective-permute-start.11 = (bf16[8,1536]{1,0:T(8,128)(2,1)S(1)}, bf16[8,1536]{1,0:T(8,128)(2,1)S(1)}, u32[]{:S(2)}, u32[]{:S(2)}) collective-permute-start(bf16[8,1536]{1,0:T(8,128)(2,1)S(1)} %get-tuple-element.36), channel_id=1, source_target_pairs={{0,12},{4,0},{8,4},{12,8},{1,13},{5,1},{9,5},{13,9},{2,14},{6,2},{... | collective-permute-start | bytes 73736 | tf_op jit(solution)/shard_map/ppermute | solution.py:420
  45.3 0.4 collective-permute-start.16
  45.8 0.6 collective-permute-start.15
  46.3 0.6 %convert_add_fusion.1 = f32[8,1536]{1,0:T(8,128)} fusion(bf16[8,1536]{1,0:T(8,128)(2,1)S(1)} %collective-permute-done.8, bf16[8,1536]{1,0:T(8,128)(2,1)S(1)} %collective-permute-done.7, f32[8,1536]{1,0:T(8,128)S(1)} %get-tuple-element.29, bf16[8,1536]{1,0:T(8,128)(2,1)S(1)} %collective-permute-done.6), kind=kLoop, calls=%fused_computation.2 | loop fusion | flops 73728 | bytes 172032 | tf_op jit(solution)/shard_map/add | solution.py:434
  47.0 5.3 %collective-permute-done.16.refs_2_ = bf16[272,128]{1,0:T(8,128)(2,1)S(1)} collective-permute-done((bf16[272,128]{1,0:T(8,128)(2,1)S(1)}, bf16[272,128]{1,0:T(8,128)(2,1)S(1)}, u32[]{:S(2)}, u32[]{:S(2)}) %collective-permute-start.16) | collective-permute-done | bytes 69664 | tf_op jit(solution)/shard_map/ppermute | solution.py:420
  52.3 0.6 shard_map.96
  52.9 1.0 %collective-permute-start.19 = (bf16[256,128]{1,0:T(8,128)(2,1)S(1)}, bf16[256,128]{1,0:T(8,128)(2,1)S(1)}, u32[]{:S(2)}, u32[]{:S(2)}) collective-permute-start(bf16[256,128]{1,0:T(8,128)(2,1)S(1)} %get-tuple-element.41.refs_0_), channel_id=1, source_target_pairs={{0,8},{4,12},{8,0},{12,4},{1,9},{5,13},{9,1},{13,5},{2,10},{6,14},... | collective-permute-start | bytes 196616 | tf_op jit(solution)/shard_map/ppermute | solution.py:420
  53.9 0.2 collective-permute-start.18
  54.1 0.6 %convert_add_fusion = f32[8,1536]{1,0:T(8,128)} fusion(bf16[8,1536]{1,0:T(8,128)(2,1)S(1)} %collective-permute-done.11, bf16[8,1536]{1,0:T(8,128)(2,1)S(1)} %collective-permute-done.10, f32[8,1536]{1,0:T(8,128)S(1)} %get-tuple-element.33, bf16[8,1536]{1,0:T(8,128)(2,1)S(1)} %collective-permute-done.9), kind=kLoop, calls=%fused_computation.1 | loop fusion | flops 73728 | bytes 172032 | tf_op jit(solution)/shard_map/add | solution.py:434
  54.9 3.0 %collective-permute-done.19.refs_2_ = bf16[256,128]{1,0:T(8,128)(2,1)S(1)} collective-permute-done((bf16[256,128]{1,0:T(8,128)(2,1)S(1)}, bf16[256,128]{1,0:T(8,128)(2,1)S(1)}, u32[]{:S(2)}, u32[]{:S(2)}) %collective-permute-start.19) | collective-permute-done | bytes 65568 | tf_op jit(solution)/shard_map/ppermute | solution.py:420
  57.8 0.4 collective-permute-done.18.refs_1_
  58.2 0.8 %shard_map.97 = f32[1024,128]{1,0:T(8,128)} custom-call(bf16[256,128]{1,0:T(8,128)(2,1)S(1)} %get-tuple-element.41.refs_0_, bf16[256,128]{1,0:T(8,128)(2,1)S(1)} %collective-permute-done.18.refs_1_, bf16[256,128]{1,0:T(8,128)(2,1)S(1)} %collective-permute-done.19.refs_2_, bf16[256,128]{1,0:T(8,128)(2,1)S(1)} %collective-permute-done.20.refs_3_), custom_call_target="tpu_custom_call" | custom-call | tf_op jit(solution)/shard_map/pallas_call | solution.py:411
  (31 shorter events, 0.5 us)
Async XLA Ops:
  0.6 7.6 %collective-permute-start.2 = (bf16[8,1536]{1,0:T(8,128)(2,1)}, bf16[8,1536]{1,0:T(8,128)(2,1)S(1)}, u32[]{:S(2)}, u32[]{:S(2)}) collective-permute-start(bf16[8,1536]{1,0:T(8,128)(2,1)} %refs_0_.3), channel_id=1, source_target_pairs={{0,3},{1,0},{2,1},{3,2},{4,7},{5,4},{6,5},{7,6},{8,11},{9,8},{10,9... | collective-permute-start | bytes 73736 | tf_op jit(solution)/shard_map/ppermute | solution.py:420
  5.7 8.9 %collective-permute-start.1 = (bf16[8,1536]{1,0:T(8,128)(2,1)}, bf16[8,1536]{1,0:T(8,128)(2,1)S(1)}, u32[]{:S(2)}, u32[]{:S(2)}) collective-permute-start(bf16[8,1536]{1,0:T(8,128)(2,1)} %refs_0_.3), channel_id=1, source_target_pairs={{0,2},{1,3},{2,0},{3,1},{4,6},{5,7},{6,4},{7,5},{8,10},{9,11},{10,... | collective-permute-start | bytes 73736 | tf_op jit(solution)/shard_map/ppermute | solution.py:420
  5.7 8.9 %collective-permute-start = (bf16[8,1536]{1,0:T(8,128)(2,1)}, bf16[8,1536]{1,0:T(8,128)(2,1)S(1)}, u32[]{:S(2)}, u32[]{:S(2)}) collective-permute-start(bf16[8,1536]{1,0:T(8,128)(2,1)} %refs_0_.3), channel_id=1, source_target_pairs={{0,1},{1,2},{2,3},{3,0},{4,5},{5,6},{6,7},{7,4},{8,9},{9,10},{10,1... | collective-permute-start | bytes 73736 | tf_op jit(solution)/shard_map/ppermute | solution.py:420
  6.7 7.9 %collective-permute-start.5 = (bf16[8,1536]{1,0:T(8,128)(2,1)}, bf16[8,1536]{1,0:T(8,128)(2,1)S(1)}, u32[]{:S(2)}, u32[]{:S(2)}) collective-permute-start(bf16[8,1536]{1,0:T(8,128)(2,1)} %refs_4_.3), channel_id=1, source_target_pairs={{0,12},{4,0},{8,4},{12,8},{1,13},{5,1},{9,5},{13,9},{2,14},{6,2},{... | collective-permute-start | bytes 73736 | tf_op jit(solution)/shard_map/ppermute | solution.py:420
  6.8 7.8 %collective-permute-start.4 = (bf16[8,1536]{1,0:T(8,128)(2,1)}, bf16[8,1536]{1,0:T(8,128)(2,1)S(1)}, u32[]{:S(2)}, u32[]{:S(2)}) collective-permute-start(bf16[8,1536]{1,0:T(8,128)(2,1)} %refs_4_.3), channel_id=1, source_target_pairs={{0,8},{4,12},{8,0},{12,4},{1,9},{5,13},{9,1},{13,5},{2,10},{6,14},... | collective-permute-start | bytes 73736 | tf_op jit(solution)/shard_map/ppermute | solution.py:420
  8.2 6.4 %collective-permute-start.3 = (bf16[8,1536]{1,0:T(8,128)(2,1)}, bf16[8,1536]{1,0:T(8,128)(2,1)S(1)}, u32[]{:S(2)}, u32[]{:S(2)}) collective-permute-start(bf16[8,1536]{1,0:T(8,128)(2,1)} %refs_4_.3), channel_id=1, source_target_pairs={{0,4},{4,8},{8,12},{12,0},{1,5},{5,9},{9,13},{13,1},{2,6},{6,10},{... | collective-permute-start | bytes 73736 | tf_op jit(solution)/shard_map/ppermute | solution.py:420
  8.5 1.1 %copy-start.3 = (bf16[48,48,128]{2,1,0:T(8,128)(2,1)S(1)}, bf16[48,48,128]{2,1,0:T(8,128)(2,1)}, u32[]{:S(2)}) copy-start(bf16[48,48,128]{2,1,0:T(8,128)(2,1)} %param.9) | copy-start | bytes 1769476
  9.5 0.9 %copy-start.5 = (bf16[1024,128]{1,0:T(8,128)(2,1)S(1)}, bf16[1024,128]{1,0:T(8,128)(2,1)}, u32[]{:S(2)}) copy-start(bf16[1024,128]{1,0:T(8,128)(2,1)} %w_ref.1) | copy-start | bytes 786436
  14.7 0.7 %copy-start = (bf16[8,1536]{1,0:T(8,128)(2,1)S(1)}, bf16[8,1536]{1,0:T(8,128)(2,1)}, u32[]{:S(2)}) copy-start(bf16[8,1536]{1,0:T(8,128)(2,1)} %refs_0_.3) | copy-start | bytes 73732
  15.4 0.7 %copy-start.1 = (bf16[8,1536]{1,0:T(8,128)(2,1)S(1)}, bf16[8,1536]{1,0:T(8,128)(2,1)}, u32[]{:S(2)}) copy-start(bf16[8,1536]{1,0:T(8,128)(2,1)} %refs_4_.3) | copy-start | bytes 73732
  16.1 1.1 %copy-start.4 = (bf16[48,48,128]{2,1,0:T(8,128)(2,1)S(1)}, bf16[48,48,128]{2,1,0:T(8,128)(2,1)}, u32[]{:S(2)}) copy-start(bf16[48,48,128]{2,1,0:T(8,128)(2,1)} %param.9) | copy-start | bytes 1769476
  23.0 14.8 %collective-permute-start.12 = (bf16[272,128]{1,0:T(8,128)(2,1)S(1)}, bf16[272,128]{1,0:T(8,128)(2,1)S(1)}, u32[]{:S(2)}, u32[]{:S(2)}) collective-permute-start(bf16[272,128]{1,0:T(8,128)(2,1)S(1)} %get-tuple-element.38), channel_id=1, source_target_pairs={{0,4},{4,8},{8,12},{12,0},{1,5},{5,9},{9,13},{13,1},{2,6},{6,10},{... | collective-permute-start | bytes 208904 | tf_op jit(solution)/shard_map/ppermute | solution.py:420
  23.7 14.5 %collective-permute-start.13 = (bf16[272,128]{1,0:T(8,128)(2,1)S(1)}, bf16[272,128]{1,0:T(8,128)(2,1)S(1)}, u32[]{:S(2)}, u32[]{:S(2)}) collective-permute-start(bf16[272,128]{1,0:T(8,128)(2,1)S(1)} %get-tuple-element.39), channel_id=1, source_target_pairs={{0,8},{4,12},{8,0},{12,4},{1,9},{5,13},{9,1},{13,5},{2,10},{6,14},... | collective-permute-start | bytes 208904 | tf_op jit(solution)/shard_map/ppermute | solution.py:420
  25.0 13.1 %collective-permute-start.14 = (bf16[272,128]{1,0:T(8,128)(2,1)S(1)}, bf16[272,128]{1,0:T(8,128)(2,1)S(1)}, u32[]{:S(2)}, u32[]{:S(2)}) collective-permute-start(bf16[272,128]{1,0:T(8,128)(2,1)S(1)} %get-tuple-element.40), channel_id=1, source_target_pairs={{0,12},{4,0},{8,4},{12,8},{1,13},{5,1},{9,5},{13,9},{2,14},{6,2},{... | collective-permute-start | bytes 208904 | tf_op jit(solution)/shard_map/ppermute | solution.py:420
  25.1 15.0 %copy-start.2 = (f32[128]{0:T(128)S(1)}, f32[128]{0:T(128)}, u32[]{:S(2)}) copy-start(f32[128]{0:T(128)} %param.8) | copy-start | bytes 1540
  33.1 9.6 %collective-permute-start.6 = (bf16[8,1536]{1,0:T(8,128)(2,1)S(1)}, bf16[8,1536]{1,0:T(8,128)(2,1)S(1)}, u32[]{:S(2)}, u32[]{:S(2)}) collective-permute-start(bf16[8,1536]{1,0:T(8,128)(2,1)S(1)} %get-tuple-element.30), channel_id=1, source_target_pairs={{0,1},{1,2},{2,3},{3,0},{4,5},{5,6},{6,7},{7,4},{8,9},{9,10},{10,1... | collective-permute-start | bytes 73736 | tf_op jit(solution)/shard_map/ppermute | solution.py:420
  35.6 8.6 %collective-permute-start.7 = (bf16[8,1536]{1,0:T(8,128)(2,1)S(1)}, bf16[8,1536]{1,0:T(8,128)(2,1)S(1)}, u32[]{:S(2)}, u32[]{:S(2)}) collective-permute-start(bf16[8,1536]{1,0:T(8,128)(2,1)S(1)} %get-tuple-element.31), channel_id=1, source_target_pairs={{0,2},{1,3},{2,0},{3,1},{4,6},{5,7},{6,4},{7,5},{8,10},{9,11},{10,... | collective-permute-start | bytes 73736 | tf_op jit(solution)/shard_map/ppermute | solution.py:420
  37.8 7.5 %collective-permute-start.8 = (bf16[8,1536]{1,0:T(8,128)(2,1)S(1)}, bf16[8,1536]{1,0:T(8,128)(2,1)S(1)}, u32[]{:S(2)}, u32[]{:S(2)}) collective-permute-start(bf16[8,1536]{1,0:T(8,128)(2,1)S(1)} %get-tuple-element.32), channel_id=1, source_target_pairs={{0,3},{1,0},{2,1},{3,2},{4,7},{5,4},{6,5},{7,6},{8,11},{9,8},{10,9... | collective-permute-start | bytes 73736 | tf_op jit(solution)/shard_map/ppermute | solution.py:420
  38.1 15.7 %collective-permute-start.9 = (bf16[8,1536]{1,0:T(8,128)(2,1)S(1)}, bf16[8,1536]{1,0:T(8,128)(2,1)S(1)}, u32[]{:S(2)}, u32[]{:S(2)}) collective-permute-start(bf16[8,1536]{1,0:T(8,128)(2,1)S(1)} %get-tuple-element.34), channel_id=1, source_target_pairs={{0,4},{4,8},{8,12},{12,0},{1,5},{5,9},{9,13},{13,1},{2,6},{6,10},{... | collective-permute-start | bytes 73736 | tf_op jit(solution)/shard_map/ppermute | solution.py:420
  38.2 7.6 %collective-permute-start.17 = (bf16[272,128]{1,0:T(8,128)(2,1)S(1)}, bf16[272,128]{1,0:T(8,128)(2,1)S(1)}, u32[]{:S(2)}, u32[]{:S(2)}) collective-permute-start(bf16[272,128]{1,0:T(8,128)(2,1)S(1)} %add_convert_fusion.refs_0_), channel_id=1, source_target_pairs={{0,3},{1,0},{2,1},{3,2},{4,7},{5,4},{6,5},{7,6},{8,11},{9,8},{10,9... | collective-permute-start | bytes 208904 | tf_op jit(solution)/shard_map/ppermute | solution.py:420
  42.6 11.5 %collective-permute-start.10 = (bf16[8,1536]{1,0:T(8,128)(2,1)S(1)}, bf16[8,1536]{1,0:T(8,128)(2,1)S(1)}, u32[]{:S(2)}, u32[]{:S(2)}) collective-permute-start(bf16[8,1536]{1,0:T(8,128)(2,1)S(1)} %get-tuple-element.35), channel_id=1, source_target_pairs={{0,8},{4,12},{8,0},{12,4},{1,9},{5,13},{9,1},{13,5},{2,10},{6,14},... | collective-permute-start | bytes 73736 | tf_op jit(solution)/shard_map/ppermute | solution.py:420
  44.1 10.0 %collective-permute-start.11 = (bf16[8,1536]{1,0:T(8,128)(2,1)S(1)}, bf16[8,1536]{1,0:T(8,128)(2,1)S(1)}, u32[]{:S(2)}, u32[]{:S(2)}) collective-permute-start(bf16[8,1536]{1,0:T(8,128)(2,1)S(1)} %get-tuple-element.36), channel_id=1, source_target_pairs={{0,12},{4,0},{8,4},{12,8},{1,13},{5,1},{9,5},{13,9},{2,14},{6,2},{... | collective-permute-start | bytes 73736 | tf_op jit(solution)/shard_map/ppermute | solution.py:420
  45.3 7.0 %collective-permute-start.16 = (bf16[272,128]{1,0:T(8,128)(2,1)S(1)}, bf16[272,128]{1,0:T(8,128)(2,1)S(1)}, u32[]{:S(2)}, u32[]{:S(2)}) collective-permute-start(bf16[272,128]{1,0:T(8,128)(2,1)S(1)} %add_convert_fusion.refs_0_), channel_id=1, source_target_pairs={{0,2},{1,3},{2,0},{3,1},{4,6},{5,7},{6,4},{7,5},{8,10},{9,11},{10,... | collective-permute-start | bytes 208904 | tf_op jit(solution)/shard_map/ppermute | solution.py:420
  45.8 6.5 %collective-permute-start.15 = (bf16[272,128]{1,0:T(8,128)(2,1)S(1)}, bf16[272,128]{1,0:T(8,128)(2,1)S(1)}, u32[]{:S(2)}, u32[]{:S(2)}) collective-permute-start(bf16[272,128]{1,0:T(8,128)(2,1)S(1)} %add_convert_fusion.refs_0_), channel_id=1, source_target_pairs={{0,1},{1,2},{2,3},{3,0},{4,5},{5,6},{6,7},{7,4},{8,9},{9,10},{10,1... | collective-permute-start | bytes 208904 | tf_op jit(solution)/shard_map/ppermute | solution.py:420
  52.9 2.0 %collective-permute-start.20 = (bf16[256,128]{1,0:T(8,128)(2,1)S(1)}, bf16[256,128]{1,0:T(8,128)(2,1)S(1)}, u32[]{:S(2)}, u32[]{:S(2)}) collective-permute-start(bf16[256,128]{1,0:T(8,128)(2,1)S(1)} %get-tuple-element.41.refs_0_), channel_id=1, source_target_pairs={{0,12},{4,0},{8,4},{12,8},{1,13},{5,1},{9,5},{13,9},{2,14},{6,2},{... | collective-permute-start | bytes 196616 | tf_op jit(solution)/shard_map/ppermute | solution.py:420
  52.9 5.0 %collective-permute-start.19 = (bf16[256,128]{1,0:T(8,128)(2,1)S(1)}, bf16[256,128]{1,0:T(8,128)(2,1)S(1)}, u32[]{:S(2)}, u32[]{:S(2)}) collective-permute-start(bf16[256,128]{1,0:T(8,128)(2,1)S(1)} %get-tuple-element.41.refs_0_), channel_id=1, source_target_pairs={{0,8},{4,12},{8,0},{12,4},{1,9},{5,13},{9,1},{13,5},{2,10},{6,14},... | collective-permute-start | bytes 196616 | tf_op jit(solution)/shard_map/ppermute | solution.py:420
  53.9 4.3 %collective-permute-start.18 = (bf16[256,128]{1,0:T(8,128)(2,1)S(1)}, bf16[256,128]{1,0:T(8,128)(2,1)S(1)}, u32[]{:S(2)}, u32[]{:S(2)}) collective-permute-start(bf16[256,128]{1,0:T(8,128)(2,1)S(1)} %get-tuple-element.41.refs_0_), channel_id=1, source_target_pairs={{0,4},{4,8},{8,12},{12,0},{1,5},{5,9},{9,13},{13,1},{2,6},{6,10},{... | collective-permute-start | bytes 196616 | tf_op jit(solution)/shard_map/ppermute | solution.py:420

commit v3 on v0

v3 whole, which is shorter than its diff:
```python
import functools

import jax
import jax.numpy as jnp
from jax import lax
from jax.experimental import pallas as pl
from jax.experimental.pallas import tpu as pltpu
from jax.sharding import PartitionSpec as P

PROJECTED_DEPTH = 32
PAIR_FEATURES = 128
GROUP = 8
STEPS = 4
BIAS_ROWS = 16
LANES = 128
F32 = jnp.float32
BF16 = jnp.bfloat16
MIB = 1024 * 1024

ROWS_BY_ROWS = (((1,), (1,)), ((), ()))
COLS_BY_COLS = (((0,), (0,)), ((), ()))


def params(sequences=0):
    return pltpu.CompilerParams(vmem_limit_bytes=min(10 + 10 * sequences // 32, 50) * MIB + 2 * MIB)


def whole(shape):
    return pl.BlockSpec(shape, lambda t: (0,) * len(shape))


def dot(x, y, dims=(((1,), (0,)), ((), ()))):
    return lax.dot_general(x, y, dims, preferred_element_type=F32)


def prepare_kernel(
    i_n, j_n, a_hbm, b_hbm, w_hbm, g_hbm, y_ref, y2_ref, wt_ref, bias_ref, a_ref, b_ref, g_ref,
    w_ref, g32, gt, w32, we, sems,
):
    depth = PROJECTED_DEPTH
    copies = [
        pltpu.make_async_copy(source, target, sems.at[n])
        for n, (source, target) in enumerate(
            [(w_hbm, w_ref), (g_hbm, g_ref), (a_hbm, a_ref), (b_hbm, b_ref)]
        )
    ]
    for copy in copies:
        copy.start()
    copies[0].wait()
    w32[...] = w_ref[...].astype(F32)
    for e in range(depth):
        block = w32[pl.ds(e, depth, stride=depth), :]
        we[e * depth : (e + 1) * depth, :] = block.astype(BF16)
    wt_ref[...] = we[...].astype(F32).T.astype(BF16)
    copies[1].wait()
    g32[...] = g_ref[...].astype(F32)
    total = jnp.sum(g32[...], axis=0, keepdims=True)
    high = total.astype(BF16).astype(F32)
    row = lax.broadcasted_iota(jnp.int32, (BIAS_ROWS, PAIR_FEATURES), 0)
    bias_ref[...] = jnp.where(row == 0, high, jnp.where(row == 1, total - high, 0.0)).astype(BF16)
    for j in range(j_n):
        gt[j * i_n : (j + 1) * i_n, :] = g32[pl.ds(j, i_n, stride=j_n), :].astype(BF16)

    size = y_ref.shape[0] // STEPS

    @pl.loop(0, STEPS)
    def _(t):
        rows = pl.ds(pl.multiple_of(t * size, size), size)
        y_ref[rows, :] = dot(we[rows, :], g_ref[...], ROWS_BY_ROWS).astype(BF16)
        y2_ref[rows, :] = dot(w_ref[rows, :], gt[...], ROWS_BY_ROWS).astype(BF16)

    copies[2].wait()
    copies[3].wait()


def in_vmem():
    return pl.BlockSpec(memory_space=pltpu.VMEM)


def prepare(a, b, w, g, i_n, j_n):
    pairs = i_n * j_n
    channels = w.shape[0]
    shapes = [
        jax.ShapeDtypeStruct((channels, pairs), BF16),
        jax.ShapeDtypeStruct((channels, pairs), BF16),
        jax.ShapeDtypeStruct((PAIR_FEATURES, channels), BF16),
        jax.ShapeDtypeStruct((BIAS_ROWS, PAIR_FEATURES), BF16),
        jax.ShapeDtypeStruct(a.shape, BF16),
        jax.ShapeDtypeStruct(b.shape, BF16),
        jax.ShapeDtypeStruct(g.shape, BF16),
    ]
    return pl.pallas_call(
        functools.partial(prepare_kernel, i_n, j_n),
        in_specs=[pl.BlockSpec(memory_space=pltpu.HBM)] * 4,
        out_specs=[in_vmem()] * len(shapes),
        out_shape=shapes,
        scratch_shapes=[
            pltpu.VMEM(w.shape, BF16),
            pltpu.VMEM(g.shape, F32),
            pltpu.VMEM(g.shape, BF16),
            pltpu.VMEM(w.shape, F32),
            pltpu.VMEM(w.shape, BF16),
            pltpu.SemaphoreType.DMA((4,)),
        ],
        compiler_params=params(32),
        cost_estimate=pl.CostEstimate(
            flops=4 * pairs * channels * PAIR_FEATURES,
            bytes_accessed=4 * pairs * channels,
            transcendentals=0,
        ),
    )(a, b, w, g)


def join(pieces, axis, held):
    count = len(pieces)
    depth = pieces[0].shape[0]
    me = lax.axis_index(axis)
    for p, piece in enumerate(pieces):
        start = pl.multiple_of(lax.rem(me - p + count, count) * depth, depth)
        held[pl.ds(start, depth), :] = piece[...].astype(F32)


def repeat_matrix(sequences):
    shape = (sequences, GROUP * sequences)
    lane = lax.broadcasted_iota(jnp.int32, shape, 1)
    row = lax.broadcasted_iota(jnp.int32, shape, 0)
    return (lax.rem(lane, sequences) == row).astype(BF16)


def spread(held, wide):
    both = dot(held[...].T.astype(BF16), repeat_matrix(held.shape[0]))
    for l in range(wide.shape[0]):
        wide[l] = both[:, l * LANES : (l + 1) * LANES]


def tiles_of(sequences, tile):
    lane = lax.broadcasted_iota(jnp.int32, (1, LANES), 1) + tile * LANES
    return [
        (m, lax.div(lane, sequences) == m)
        for m in range(GROUP)
        if m * sequences < (tile + 1) * LANES and (m + 1) * sequences > tile * LANES
    ]


def fill_diagonal(wide, diagonal, slot, channel, positions, sequences):
    for l in range(wide.shape[0]):
        block = wide[l, pl.ds(channel, positions, stride=PROJECTED_DEPTH), :]
        for m, mask in tiles_of(sequences, l):
            diagonal[slot, m * positions : (m + 1) * positions, l * LANES : (l + 1) * LANES] = (
                jnp.where(mask, block, 0.0).astype(BF16)
            )


def outer_kernel(i_n, j_n, row_n, col_n, *refs):
    depth = PROJECTED_DEPTH
    a_pieces, refs = refs[:col_n], refs[col_n:]
    b_pieces, refs = refs[:row_n], refs[row_n:]
    g_ref, bias_ref, x_ref, message = refs[:4]
    a_held, b_held, wide, left, diagonal, total, ordered = refs[4:]
    sequences = a_held.shape[0]
    groups = i_n // GROUP
    per_step = depth // STEPS
    span = GROUP * j_n

    join(a_pieces, "col", a_held)
    join(b_pieces, "row", b_held)
    spread(a_held, wide)
    for l in range(wide.shape[0]):
        members = tiles_of(sequences, l)
        for k in range(groups):
            block = jnp.zeros((depth, LANES), F32)
            for m, mask in members:
                start = (k * GROUP + m) * depth
                block = jnp.where(mask, wide[l, start : start + depth, :], block)
            left[k * depth : (k + 1) * depth, l * LANES : (l + 1) * LANES] = block.astype(BF16)
    spread(b_held, wide)
    diagonal[...] = jnp.zeros(diagonal.shape, BF16)

    @pl.loop(0, STEPS)
    def _(t):
        for e in range(per_step):
            fill_diagonal(wide, diagonal, e, t * per_step + e, j_n, sequences)
        size = per_step * depth
        first = pl.multiple_of(t * size, size)
        for e in range(0, per_step, 2):
            right = diagonal[e : e + 2].reshape(2 * span, diagonal.shape[2])
            product = dot(left[...], right, ROWS_BY_ROWS).astype(BF16)
            for n in range(2):
                for k in range(groups):
                    x_ref[pl.ds(first + (e + n) * depth, depth), k * span : (k + 1) * span] = product[
                        k * depth : (k + 1) * depth, n * span : (n + 1) * span
                    ]
        total[pl.ds(first, size), :] = dot(x_ref[pl.ds(first, size), :], g_ref[...])

    for c in range(depth):
        ordered[c * depth : (c + 1) * depth, :] = total[pl.ds(c, depth, stride=depth), :]
    share = ordered.shape[0] // row_n
    for p in range(row_n):
        message[p, 0:share, :] = ordered[p * share : (p + 1) * share, :].astype(BF16)
        message[p, share:, :] = bias_ref[...]


def outer(a_pieces, b_pieces, g, bias_rows, i_n, j_n, sequences):
    row_n, col_n = len(b_pieces), len(a_pieces)
    depth = PROJECTED_DEPTH
    channels = depth * depth
    pairs = i_n * j_n
    share = channels // row_n
    tiles = GROUP * sequences // LANES
    operands = [*a_pieces, *b_pieces, g, bias_rows]
    return pl.pallas_call(
        functools.partial(outer_kernel, i_n, j_n, row_n, col_n),
        in_specs=[in_vmem()] * len(operands),
        out_specs=[in_vmem()] * 2,
        out_shape=[
            jax.ShapeDtypeStruct((channels, pairs), BF16),
            jax.ShapeDtypeStruct((row_n, share + BIAS_ROWS, PAIR_FEATURES), BF16),
        ],
        scratch_shapes=[
            pltpu.VMEM((sequences, i_n * depth), F32),
            pltpu.VMEM((sequences, j_n * depth), F32),
            pltpu.VMEM((tiles, i_n * depth, LANES), F32),
            pltpu.VMEM((i_n // GROUP * depth, GROUP * sequences), BF16),
            pltpu.VMEM((depth // STEPS, GROUP * j_n, GROUP * sequences), BF16),
            pltpu.VMEM((channels, PAIR_FEATURES), F32),
            pltpu.VMEM((channels, PAIR_FEATURES), F32),
        ],
        compiler_params=params(sequences),
        cost_estimate=pl.CostEstimate(
            flops=4 * pairs * channels * PAIR_FEATURES,
            bytes_accessed=2 * pairs * channels,
            transcendentals=0,
        ),
    )(*operands)


def gradient_kernel(axis, count, positions, others, *refs):
    depth = PROJECTED_DEPTH
    pieces, source, out = refs[:count], refs[count], refs[count + 1]
    held, wide, diagonal, result, grown, grad = refs[count + 2 :]
    sequences = held.shape[0]
    per_step = depth // STEPS
    span = GROUP * others

    join(pieces, axis, held)
    spread(held, wide)
    diagonal[...] = jnp.zeros(diagonal.shape, BF16)
    result[...] = jnp.zeros(result.shape, F32)

    @pl.loop(0, STEPS)
    def _(t):
        for n in range(per_step):
            fill_diagonal(wide, diagonal, n, t * per_step + n, others, sequences)
        first = pl.multiple_of(t * per_step * depth, per_step * depth)
        for n in range(0, per_step, 2):
            rows = [
                jnp.concatenate(
                    [
                        source[pl.ds(first + m * depth, depth), k * span : (k + 1) * span]
                        for m in (n, n + 1)
                    ],
                    axis=1,
                )
                for k in range(positions // GROUP)
            ]
            result[...] += dot(
                jnp.concatenate(rows, axis=0),
                diagonal[n : n + 2].reshape(2 * span, diagonal.shape[2]),
            )

    scaled = (result[...] * (1.0 / sequences)).astype(BF16)
    for l in range(scaled.shape[1] // LANES):
        members = dict(tiles_of(sequences, l))
        for k in range(positions // GROUP):
            block = scaled[k * depth : (k + 1) * depth, l * LANES : (l + 1) * LANES]
            for m in range(GROUP):
                start = (k * GROUP + m) * depth
                grown[start : start + depth, l * LANES : (l + 1) * LANES] = (
                    jnp.where(members[m], block.astype(F32), 0.0).astype(BF16)
                    if m in members
                    else jnp.zeros((depth, LANES), BF16)
                )
    grad[...] = dot(repeat_matrix(sequences), grown[...], ROWS_BY_ROWS)
    share = sequences // out.shape[0]
    for p in range(out.shape[0]):
        mine = grad[p * share : (p + 1) * share, :]
        out[p] = jnp.concatenate(
            [mine[:, l * LANES : (l + 1) * LANES] for l in range(mine.shape[1] // LANES)], axis=0
        ).astype(BF16)


def gradient(pieces, axis, source, parts, positions, others, sequences):
    depth = PROJECTED_DEPTH
    channels, pairs = source.shape
    tiles = GROUP * sequences // LANES
    rows = sequences // parts * positions * depth // LANES
    return pl.pallas_call(
        functools.partial(gradient_kernel, axis, len(pieces), positions, others),
        in_specs=[in_vmem()] * (len(pieces) + 1),
        out_specs=in_vmem(),
        out_shape=jax.ShapeDtypeStruct((parts, rows, LANES), BF16),
        scratch_shapes=[
            pltpu.VMEM((sequences, others * depth), F32),
            pltpu.VMEM((tiles, others * depth, LANES), F32),
            pltpu.VMEM((depth // STEPS, GROUP * others, GROUP * sequences), BF16),
            pltpu.VMEM((positions // GROUP * depth, GROUP * sequences), F32),
            pltpu.VMEM((positions * depth, GROUP * sequences), BF16),
            pltpu.VMEM((sequences, positions * depth), F32),
        ],
        compiler_params=params(sequences),
        cost_estimate=pl.CostEstimate(
            flops=2 * pairs * channels * PAIR_FEATURES,
            bytes_accessed=2 * pairs * channels,
            transcendentals=0,
        ),
    )(*pieces, source)


def pair_kernel(sequences, x_ref, wt_ref, bias_ref, out_ref):
    product = dot(wt_ref[...], x_ref[...])
    out_ref[...] = (product.T * (1.0 / sequences) + bias_ref[...]).astype(BF16)


def pair(x, wt, output_bias, sequences):
    channels, pairs = x.shape
    count = 3
    size = pairs // count
    return pl.pallas_call(
        functools.partial(pair_kernel, sequences),
        grid=(count,),
        in_specs=[
            pl.BlockSpec((channels, size), lambda t: (0, t)),
            whole(wt.shape),
            whole((1, PAIR_FEATURES)),
        ],
        out_specs=pl.BlockSpec((size, PAIR_FEATURES), lambda t: (t, 0)),
        out_shape=jax.ShapeDtypeStruct((pairs, PAIR_FEATURES), BF16),
        compiler_params=params(),
        cost_estimate=pl.CostEstimate(
            flops=4 * pairs * channels * PAIR_FEATURES,
            bytes_accessed=2 * pairs * channels,
            transcendentals=0,
        ),
    )(x, wt, output_bias.reshape(1, PAIR_FEATURES))


def sum_parts(ref, start, stop):
    total = ref[0, start:stop, :].astype(F32)
    for n in range(1, ref.shape[0]):
        total += ref[n, start:stop, :].astype(F32)
    return total


def unfold(total, share, out):
    for l in range(out.shape[1] // LANES):
        out[:, l * LANES : (l + 1) * LANES] = total[l * share : (l + 1) * share, :]


def row_sum_kernel(parts, grads, message):
    rows = parts.shape[1]
    total = sum_parts(parts, 0, rows).astype(BF16)
    for p in range(message.shape[0]):
        message[p, 0:rows, :] = total
        message[p, rows:, :] = grads[p]


def row_sum(parts, grads):
    shape = (grads.shape[0], parts.shape[1] + grads.shape[1], LANES)
    return pl.pallas_call(
        row_sum_kernel,
        in_specs=[in_vmem()] * 2,
        out_specs=in_vmem(),
        out_shape=jax.ShapeDtypeStruct(shape, BF16),
        compiler_params=params(),
    )(parts, grads)


def column_sum_kernel(res_total, parts, grads, message, left_out, bias_out):
    share = message.shape[1] - grads.shape[1]
    total = sum_parts(parts, 0, share + BIAS_ROWS)
    piece = total[0:share].astype(BF16)
    for p in range(message.shape[0]):
        message[p, 0:share, :] = piece
        message[p, share:, :] = grads[p]
    bias_out[...] = (total[share : share + 1] + total[share + 1 : share + 2]) * (1.0 / res_total)
    unfold(sum_parts(parts, share + BIAS_ROWS, parts.shape[1]), left_out.shape[0], left_out)


def column_sum(parts, grads, share, left_shape, res_total):
    return pl.pallas_call(
        functools.partial(column_sum_kernel, res_total),
        in_specs=[in_vmem()] * 2,
        out_specs=[in_vmem()] * 3,
        out_shape=[
            jax.ShapeDtypeStruct((grads.shape[0], share + grads.shape[1], LANES), BF16),
            jax.ShapeDtypeStruct(left_shape, F32),
            jax.ShapeDtypeStruct((1, PAIR_FEATURES), F32),
        ],
        compiler_params=params(),
    )(parts, grads)


def finish_kernel(scale, parts, projection, right_out):
    count = parts.shape[0]
    share = projection.shape[0] // count
    for p in range(count):
        projection[p * share : (p + 1) * share, :] = parts[p, 0:share, :].astype(F32) * scale
    unfold(sum_parts(parts, share, parts.shape[1]), right_out.shape[0], right_out)


def finish(parts, channels, right_shape, scale):
    return pl.pallas_call(
        functools.partial(finish_kernel, scale),
        in_specs=[in_vmem()],
        out_specs=[in_vmem()] * 2,
        out_shape=[
            jax.ShapeDtypeStruct((channels, PAIR_FEATURES), F32),
            jax.ShapeDtypeStruct(right_shape, F32),
        ],
        compiler_params=params(),
    )(parts)


def shift(x, axis, distance):
    count = lax.axis_size(axis)
    return lax.ppermute(x, axis, [(n, (n + distance) % count) for n in range(count)])


def gather(x, axis):
    return [shift(x, axis, d) for d in range(1, lax.axis_size(axis))]


def exchange(parts, axis):
    return lax.all_to_all(parts, axis, 0, 0, tiled=True)


def local(
    first_homolog_features, second_homolog_features, final_projection_matrix, output_bias, cotangent
):
    i_n, j_n, _ = cotangent.shape
    row_n, col_n = lax.axis_size("row"), lax.axis_size("col")
    sequences = second_homolog_features.shape[0] * row_n
    channels = final_projection_matrix.shape[0]
    res_total = i_n * row_n
    a_pieces = gather(first_homolog_features, "col")
    b_pieces = gather(second_homolog_features, "row")
    y, y2, wt, bias_rows, a_own, b_own, g = prepare(
        first_homolog_features,
        second_homolog_features,
        final_projection_matrix,
        cotangent.reshape(i_n * j_n, PAIR_FEATURES),
        i_n,
        j_n,
    )
    a_pieces = [a_own] + a_pieces
    b_pieces = [b_own] + b_pieces

    x, message = outer(a_pieces, b_pieces, g, bias_rows, i_n, j_n, sequences)
    parts = exchange(message, "row")
    left_grads = gradient(b_pieces, "row", y, col_n, i_n, j_n, sequences)
    parts = exchange(row_sum(parts, left_grads), "col")
    right_grads = gradient(a_pieces, "col", y2, row_n, j_n, i_n, sequences)
    message, left_grad, bias_grad = column_sum(
        parts, right_grads, channels // row_n, first_homolog_features.shape, res_total
    )
    parts = exchange(message, "row")
    pair_map = pair(x, wt, output_bias, sequences)
    projection, right_grad = finish(
        parts, channels, second_homolog_features.shape, 1.0 / (sequences * res_total)
    )
    return (
        pair_map.reshape(i_n, j_n, PAIR_FEATURES),
        left_grad,
        right_grad,
        projection,
        bias_grad.reshape(PAIR_FEATURES),
    )


def solution(mesh):
    return jax.shard_map(
        local,
        mesh=mesh,
        in_specs=(
            P(("dp", "col"), "row"),
            P(("dp", "row"), "col"),
            P(),
            P(),
            P(("dp", "row"), "col", None),
        ),
        out_specs=(
            P(("dp", "row"), "col", None),
            P(("dp", "col"), "row"),
            P(("dp", "row"), "col"),
            P("dp", None),
            P("dp"),
        ),
        check_vma=False,
    )
```

time: 223 us -> 70.4 us (0.32); the launches traced: 220 us -> 69.8 us
  local copies, waits for them, and re-layouts: 112 us -> 17 us
  blocking collectives: 55.3 us -> 0 us
  matrix products: 33.9 us -> 0 us
  Pallas kernels: 0 us -> 24.1 us
  starting transfers between devices: 0.13 us -> 19.7 us
  between operations: 15.5 us -> 0.78 us
  waiting for transfers between devices: 0.05 us -> 8.16 us
  other arithmetic: 2.71 us -> 0 us
    dot_general x2 -> x0, local copies, waits for them, and re-layouts: 46 us -> none  [local(): jnp.einsum('icje,ijf->cef', kronecker_pieces, cotangent, preferred_elemen...]
    reshape x2 -> x0, local copies, waits for them, and re-layouts: 45.9 us -> none  [the longest x1 24.7 us: local(): outer_grad.reshape(patch_positions * PROJECTED_DEPTH, patch_positions * P...]
    psum x1 -> x0, blocking collectives: 34.4 us -> none  [local(): lax.psum((weight_local, bias_local), ('row', 'col'))]
    dot_general x6 -> x0, matrix products: 33.9 us -> none  [the longest x1 11 us: local(): jnp.einsum('icje,cef->ijf', kronecker_pieces, projection_cuboid, preferre...]
    pallas_call x0 -> x8, Pallas kernels: none -> 24.1 us  [the longest x2 7.75 us: gradient(): pl.pallas_call(functools.partial(gradient_kernel, axis, len(pieces), posi...]
    all_gather x2 -> x0, blocking collectives: 20.9 us -> none  [the longest x1 15.4 us: local(): lax.all_gather(first_homolog_features, 'col', axis=0, tiled=True)]
    convert_element_type x1 -> x0, local copies, waits for them, and re-layouts: 20.5 us -> none  [local(): outer_grad = jnp.einsum('ijf,cef->icje', cotangent, projection_cuboid, pr...]
    unnamed x6 -> x22, local copies, waits for them, and re-layouts: 0.02 us -> 17 us
  transfers between devices with their start and end apart: 3 -> 9, of which waited for: 0 -> 2; matrix products, arithmetic and copies ran while one was open for 34% -> 0% of each run, Pallas kernels for 0% -> 21%
where the time goes in v3:
time: 70.4 us; the launch traced here: 69.8 us
  Pallas kernels  24.1 us (34%)
  starting transfers between devices  19.7 us (28%)
  local copies, waits for them, and re-layouts  17 us (24%)
  waiting for transfers between devices  8.16 us (12%)
  between operations  0.78 us (1%)
    unnamed x22, local copies, waits for them, and re-layouts  17 us
    all_to_all x3, starting transfers between devices, exchange(): return lax.all_to_all(parts, axis, 0, 0, tiled=True)  10.4 us
    ppermute x6, starting transfers between devices, shift(): lax.ppermute(x, axis, [(n, (n + distance) % count) for n in range(count)])  9.35 us
    all_to_all x3, waiting for transfers between devices, exchange(): return lax.all_to_all(parts, axis, 0, 0, tiled=True)  8.14 us
    pallas_call x2, Pallas kernels, gradient(): pl.pallas_call(functools.partial(gradient_kernel, axis, len(pieces), posi...  7.75 us
    pallas_call x1, Pallas kernels, outer(): pl.pallas_call(functools.partial(outer_kernel, i_n, j_n, row_n, col_n), i...  6.97 us
    pallas_call x1, Pallas kernels, prepare(): pl.pallas_call(functools.partial(prepare_kernel, i_n, j_n), in_specs=[pl....  4.43 us
    pallas_call x1, Pallas kernels, pair(): pl.pallas_call(functools.partial(pair_kernel, sequences), grid=(count,),...  2.54 us
  transfers between devices with their start and end apart: 9, of which 2 were waited for; matrix products, arithmetic and copies ran while one was open for 0% of the time, Pallas kernels for 21%

profile of v3, /device:TPU:0, one launch (start us, length us, event | category | flops | bytes accessed | tf_op | source)
XLA Modules:
  0.0 69.8 jit_solution(15654560534941643619)
XLA Ops:
  0.6 3.1 %collective-permute-start = (bf16[8,1536]{1,0:T(8,128)(2,1)}, bf16[8,1536]{1,0:T(8,128)(2,1)S(1)}, u32[]{:S(2)}, u32[]{:S(2)}) collective-permute-start(bf16[8,1536]{1,0:T(8,128)(2,1)} %a_hbm.1), channel_id=1, source_target_pairs={{0,1},{1,2},{2,3},{3,0},{4,5},{5,6},{6,7},{7,4},{8,9},{9,10},{10,1... | collective-permute-start | bytes 73736 | tf_op jit(solution)/shard_map/ppermute | solution.py:426
  3.7 2.1 %collective-permute-start.2 = (bf16[8,1536]{1,0:T(8,128)(2,1)}, bf16[8,1536]{1,0:T(8,128)(2,1)S(1)}, u32[]{:S(2)}, u32[]{:S(2)}) collective-permute-start(bf16[8,1536]{1,0:T(8,128)(2,1)} %a_hbm.1), channel_id=1, source_target_pairs={{0,3},{1,0},{2,1},{3,2},{4,7},{5,4},{6,5},{7,6},{8,11},{9,8},{10,9... | collective-permute-start | bytes 73736 | tf_op jit(solution)/shard_map/ppermute | solution.py:426
  5.8 0.9 %collective-permute-start.1 = (bf16[8,1536]{1,0:T(8,128)(2,1)}, bf16[8,1536]{1,0:T(8,128)(2,1)S(1)}, u32[]{:S(2)}, u32[]{:S(2)}) collective-permute-start(bf16[8,1536]{1,0:T(8,128)(2,1)} %a_hbm.1), channel_id=1, source_target_pairs={{0,2},{1,3},{2,0},{3,1},{4,6},{5,7},{6,4},{7,5},{8,10},{9,11},{10,... | collective-permute-start | bytes 73736 | tf_op jit(solution)/shard_map/ppermute | solution.py:426
  6.8 1.7 %collective-permute-start.5 = (bf16[8,1536]{1,0:T(8,128)(2,1)}, bf16[8,1536]{1,0:T(8,128)(2,1)S(1)}, u32[]{:S(2)}, u32[]{:S(2)}) collective-permute-start(bf16[8,1536]{1,0:T(8,128)(2,1)} %b_hbm.1), channel_id=1, source_target_pairs={{0,12},{4,0},{8,4},{12,8},{1,13},{5,1},{9,5},{13,9},{2,14},{6,2},{... | collective-permute-start | bytes 73736 | tf_op jit(solution)/shard_map/ppermute | solution.py:426
  8.5 1.5 %collective-permute-start.4 = (bf16[8,1536]{1,0:T(8,128)(2,1)}, bf16[8,1536]{1,0:T(8,128)(2,1)S(1)}, u32[]{:S(2)}, u32[]{:S(2)}) collective-permute-start(bf16[8,1536]{1,0:T(8,128)(2,1)} %b_hbm.1), channel_id=1, source_target_pairs={{0,8},{4,12},{8,0},{12,4},{1,9},{5,13},{9,1},{13,5},{2,10},{6,14},... | collective-permute-start | bytes 73736 | tf_op jit(solution)/shard_map/ppermute | solution.py:426
  10.0 1.1 %copy-done.7 = bf16[48,48,128]{2,1,0:T(8,128)(2,1)S(1)} copy-done((bf16[48,48,128]{2,1,0:T(8,128)(2,1)S(1)}, bf16[48,48,128]{2,1,0:T(8,128)(2,1)}, u32[]{:S(2)}) %copy-start.7) | copy-done | bytes 589848
  11.1 0.9 %copy-done.8 = bf16[1024,128]{1,0:T(8,128)(2,1)S(1)} copy-done((bf16[1024,128]{1,0:T(8,128)(2,1)S(1)}, bf16[1024,128]{1,0:T(8,128)(2,1)}, u32[]{:S(2)}) %copy-start.8) | copy-done | bytes 262168
  12.0 0.7 %copy-done.9 = bf16[8,1536]{1,0:T(8,128)(2,1)S(1)} copy-done((bf16[8,1536]{1,0:T(8,128)(2,1)S(1)}, bf16[8,1536]{1,0:T(8,128)(2,1)}, u32[]{:S(2)}) %copy-start.9) | copy-done | bytes 24600
  12.7 0.7 %copy-done.10 = bf16[8,1536]{1,0:T(8,128)(2,1)S(1)} copy-done((bf16[8,1536]{1,0:T(8,128)(2,1)S(1)}, bf16[8,1536]{1,0:T(8,128)(2,1)}, u32[]{:S(2)}) %copy-start.10) | copy-done | bytes 24600
  13.5 4.4 %shard_map.92 = (bf16[1024,2304]{1,0:T(8,128)(2,1)S(1)}, bf16[1024,2304]{1,0:T(8,128)(2,1)S(1)}, bf16[128,1024]{1,0:T(8,128)(2,1)S(1)}, bf16[16,128]{1,0:T(8,128...) custom-call(bf16[8,1536]{1,0:T(8,128)(2,1)S(1)} %copy-done.9, ...), custom_call_target="tpu_custom_call" | custom-call | flops 1207959552 | bytes 9437184 | tf_op jit(solution)/shard_map/pallas_call | solution.py:92
  17.9 2.1 %copy-done.2 = bf16[1024,2304]{1,0:T(8,128)(2,1)} copy-done((bf16[1024,2304]{1,0:T(8,128)(2,1)}, bf16[1024,2304]{1,0:T(8,128)(2,1)S(1)}, u32[]{:S(2)}) %copy-start.2) | copy-done | bytes 4718616
  20.1 2.2 %copy-done.4 = bf16[1024,2304]{1,0:T(8,128)(2,1)} copy-done((bf16[1024,2304]{1,0:T(8,128)(2,1)}, bf16[1024,2304]{1,0:T(8,128)(2,1)S(1)}, u32[]{:S(2)}) %copy-start.4) | copy-done | bytes 4718616
  22.3 0.0 collective-permute-done.2.refs_3_
  22.3 0.0 collective-permute-done.1.refs_2_
  22.3 0.0 collective-permute-done.3.refs_5_.refs_1_
  22.3 7.0 %shard_map.93 = (bf16[1024,2304]{1,0:T(8,128)(2,1)S(1)}, bf16[4,272,128]{2,1,0:T(8,128)(2,1)}) custom-call(bf16[8,1536]{1,0:T(8,128)(2,1)S(1)} %get-tuple-element.19.refs_0_, bf16[8,1536]{1,0:T(8,128)(2,1)S(1)} %collective-permute-done.refs_1_, bf16[8,1536]{1,0:T(8,128)(2,1)S(1)} %collective-permute-done.1.refs_2_, ...), custom_call_target="tpu_custom_call" | custom-call | flops 1207959552 | bytes 4718592 | tf_op jit(solution)/shard_map/pallas_call | solution.py:211
  29.3 2.2 %copy-done = bf16[1024,2304]{1,0:T(8,128)(2,1)} copy-done((bf16[1024,2304]{1,0:T(8,128)(2,1)}, bf16[1024,2304]{1,0:T(8,128)(2,1)S(1)}, u32[]{:S(2)}) %copy-start) | copy-done | bytes 4718616
  31.5 3.5 %all-to-all-start = ((bf16[4,272,128]{2,1,0:T(8,128)(2,1)}), bf16[4,272,128]{2,1,0:T(8,128)(2,1)S(1)}, u32[]{:S(2)}, u32[]{:S(2)}) async-start(bf16[4,272,128]{2,1,0:T(8,128)(2,1)} %get-tuple-element.25), calls=%async_computation | async-start | bytes 557056 | tf_op jit(solution)/shard_map/all_to_all | solution.py:434
  34.9 2.3 %copy-done.5 = bf16[1024,2304]{1,0:T(8,128)(2,1)S(1)} copy-done((bf16[1024,2304]{1,0:T(8,128)(2,1)S(1)}, bf16[1024,2304]{1,0:T(8,128)(2,1)}, u32[]{:S(2)}) %copy-start.5) | copy-done | bytes 4718616
  37.3 3.9 %shard_map.95.grads = bf16[4,96,128]{2,1,0:T(8,128)(2,1)S(1)} custom-call(bf16[8,1536]{1,0:T(8,128)(2,1)S(1)} %get-tuple-element.20.refs_4_.refs_0_, bf16[8,1536]{1,0:T(8,128)(2,1)S(1)} %collective-permute-done.3.refs_5_.refs_1_, bf16[8,1536]{1,0:T(8,128)(2,1)S(1)} %collective-permute-done.4.refs_6_.refs_2_, ...), custom_call_target="tpu_custom_call" | custom-call | flops 603979776 | bytes 4718592 | tf_op jit(solution)/shard_map/pallas_call | solution.py:297
  41.2 0.0 copy-start.6
  41.2 0.8 %shard_map.96 = bf16[4,368,128]{2,1,0:T(8,128)(2,1)} custom-call(bf16[4,272,128]{2,1,0:T(8,128)(2,1)S(1)} %all-to-all-done.parts, bf16[4,96,128]{2,1,0:T(8,128)(2,1)S(1)} %shard_map.95.grads), custom_call_target="tpu_custom_call" | custom-call | tf_op jit(solution)/shard_map/pallas_call | solution.py:369
  42.0 3.5 %all-to-all-start.1 = ((bf16[4,368,128]{2,1,0:T(8,128)(2,1)}), bf16[4,368,128]{2,1,0:T(8,128)(2,1)S(1)}, u32[]{:S(2)}, u32[]{:S(2)}) async-start(bf16[4,368,128]{2,1,0:T(8,128)(2,1)} %shard_map.96), calls=%async_computation.1 | async-start | bytes 753664 | tf_op jit(solution)/shard_map/all_to_all | solution.py:434
  45.4 2.3 %copy-done.3 = bf16[1024,2304]{1,0:T(8,128)(2,1)S(1)} copy-done((bf16[1024,2304]{1,0:T(8,128)(2,1)S(1)}, bf16[1024,2304]{1,0:T(8,128)(2,1)}, u32[]{:S(2)}) %copy-start.3) | copy-done | bytes 4718616
  47.8 3.9 %shard_map.97.grads = bf16[4,96,128]{2,1,0:T(8,128)(2,1)S(1)} custom-call(bf16[8,1536]{1,0:T(8,128)(2,1)S(1)} %get-tuple-element.19.refs_0_, bf16[8,1536]{1,0:T(8,128)(2,1)S(1)} %collective-permute-done.refs_1_, bf16[8,1536]{1,0:T(8,128)(2,1)S(1)} %collective-permute-done.1.refs_2_, bf16[8,1536]{1,0:T(8,128)(2,1)S(1)} %collective-permute-done.2.refs_3_, ...), custom_call_target="tpu_custom_call" | custom-call | flops 603979776 | bytes 4718592 | tf_op jit(solution)/shard_map/pallas_call | solution.py:297
  51.7 6.0 %all-to-all-done.1.parts = bf16[4,368,128]{2,1,0:T(8,128)(2,1)S(1)} async-done(((bf16[4,368,128]{2,1,0:T(8,128)(2,1)}), bf16[4,368,128]{2,1,0:T(8,128)(2,1)S(1)}, u32[]{:S(2)}, u32[]{:S(2)}) %all-to-all-start.1) | async-done | bytes 376864 | tf_op jit(solution)/shard_map/all_to_all | solution.py:434
  57.6 0.8 %shard_map.98 = (bf16[4,352,128]{2,1,0:T(8,128)(2,1)}, f32[8,1536]{1,0:T(8,128)}, f32[1,128]{1,0:T(1,128)}) custom-call(bf16[4,368,128]{2,1,0:T(8,128)(2,1)S(1)} %all-to-all-done.1.parts, bf16[4,96,128]{2,1,0:T(8,128)(2,1)S(1)} %shard_map.97.grads), custom_call_target="tpu_custom_call" | custom-call | tf_op jit(solution)/shard_map/pallas_call | solution.py:390
  58.4 3.5 %all-to-all-start.2 = ((bf16[4,352,128]{2,1,0:T(8,128)(2,1)}), bf16[4,352,128]{2,1,0:T(8,128)(2,1)S(1)}, u32[]{:S(2)}, u32[]{:S(2)}) async-start(bf16[4,352,128]{2,1,0:T(8,128)(2,1)} %get-tuple-element.29), calls=%async_computation.2 | async-start | bytes 720896 | tf_op jit(solution)/shard_map/all_to_all | solution.py:434
  61.9 2.3 %copy-done.1 = bf16[1024,2304]{1,0:T(8,128)(2,1)S(1)} copy-done((bf16[1024,2304]{1,0:T(8,128)(2,1)S(1)}, bf16[1024,2304]{1,0:T(8,128)(2,1)}, u32[]{:S(2)}) %copy-start.1) | copy-done | bytes 4718616
  64.2 2.5 %shard_map.94 = bf16[2304,128]{1,0:T(8,128)(2,1)} custom-call(bf16[1024,2304]{1,0:T(8,128)(2,1)S(1)} %copy-done.1, bf16[128,1024]{1,0:T(8,128)(2,1)S(1)} %get-tuple-element.24.wt_ref, f32[1,128]{1,0:T(1,128)S(1)} %bitcast.4), custom_call_target="tpu_custom_call" | custom-call | flops 1207959552 | bytes 4718592 | tf_op jit(solution)/shard_map/pallas_call | solution.py:328
  66.8 2.2 %all-to-all-done.2.parts = bf16[4,352,128]{2,1,0:T(8,128)(2,1)S(1)} async-done(((bf16[4,352,128]{2,1,0:T(8,128)(2,1)}), bf16[4,352,128]{2,1,0:T(8,128)(2,1)S(1)}, u32[]{:S(2)}, u32[]{:S(2)}) %all-to-all-start.2) | async-done | bytes 360480 | tf_op jit(solution)/shard_map/all_to_all | solution.py:434
  68.9 0.8 %shard_map.99 = (f32[1024,128]{1,0:T(8,128)}, f32[8,1536]{1,0:T(8,128)}) custom-call(bf16[4,352,128]{2,1,0:T(8,128)(2,1)S(1)} %all-to-all-done.2.parts), custom_call_target="tpu_custom_call" | custom-call | tf_op jit(solution)/shard_map/pallas_call | solution.py:412
  (16 shorter events, 0.0 us)
Async XLA Ops:
  0.6 7.9 %collective-permute-start = (bf16[8,1536]{1,0:T(8,128)(2,1)}, bf16[8,1536]{1,0:T(8,128)(2,1)S(1)}, u32[]{:S(2)}, u32[]{:S(2)}) collective-permute-start(bf16[8,1536]{1,0:T(8,128)(2,1)} %a_hbm.1), channel_id=1, source_target_pairs={{0,1},{1,2},{2,3},{3,0},{4,5},{5,6},{6,7},{7,4},{8,9},{9,10},{10,1... | collective-permute-start | bytes 73736 | tf_op jit(solution)/shard_map/ppermute | solution.py:426
  3.7 18.6 %collective-permute-start.2 = (bf16[8,1536]{1,0:T(8,128)(2,1)}, bf16[8,1536]{1,0:T(8,128)(2,1)S(1)}, u32[]{:S(2)}, u32[]{:S(2)}) collective-permute-start(bf16[8,1536]{1,0:T(8,128)(2,1)} %a_hbm.1), channel_id=1, source_target_pairs={{0,3},{1,0},{2,1},{3,2},{4,7},{5,4},{6,5},{7,6},{8,11},{9,8},{10,9... | collective-permute-start | bytes 73736 | tf_op jit(solution)/shard_map/ppermute | solution.py:426
  5.8 16.5 %collective-permute-start.1 = (bf16[8,1536]{1,0:T(8,128)(2,1)}, bf16[8,1536]{1,0:T(8,128)(2,1)S(1)}, u32[]{:S(2)}, u32[]{:S(2)}) collective-permute-start(bf16[8,1536]{1,0:T(8,128)(2,1)} %a_hbm.1), channel_id=1, source_target_pairs={{0,2},{1,3},{2,0},{3,1},{4,6},{5,7},{6,4},{7,5},{8,10},{9,11},{10,... | collective-permute-start | bytes 73736 | tf_op jit(solution)/shard_map/ppermute | solution.py:426
  6.7 15.5 %collective-permute-start.3 = (bf16[8,1536]{1,0:T(8,128)(2,1)}, bf16[8,1536]{1,0:T(8,128)(2,1)S(1)}, u32[]{:S(2)}, u32[]{:S(2)}) collective-permute-start(bf16[8,1536]{1,0:T(8,128)(2,1)} %b_hbm.1), channel_id=1, source_target_pairs={{0,4},{4,8},{8,12},{12,0},{1,5},{5,9},{9,13},{13,1},{2,6},{6,10},{... | collective-permute-start | bytes 73736 | tf_op jit(solution)/shard_map/ppermute | solution.py:426
  6.8 15.5 %collective-permute-start.5 = (bf16[8,1536]{1,0:T(8,128)(2,1)}, bf16[8,1536]{1,0:T(8,128)(2,1)S(1)}, u32[]{:S(2)}, u32[]{:S(2)}) collective-permute-start(bf16[8,1536]{1,0:T(8,128)(2,1)} %b_hbm.1), channel_id=1, source_target_pairs={{0,12},{4,0},{8,4},{12,8},{1,13},{5,1},{9,5},{13,9},{2,14},{6,2},{... | collective-permute-start | bytes 73736 | tf_op jit(solution)/shard_map/ppermute | solution.py:426
  8.5 13.8 %collective-permute-start.4 = (bf16[8,1536]{1,0:T(8,128)(2,1)}, bf16[8,1536]{1,0:T(8,128)(2,1)S(1)}, u32[]{:S(2)}, u32[]{:S(2)}) collective-permute-start(bf16[8,1536]{1,0:T(8,128)(2,1)} %b_hbm.1), channel_id=1, source_target_pairs={{0,8},{4,12},{8,0},{12,4},{1,9},{5,13},{9,1},{13,5},{2,10},{6,14},... | collective-permute-start | bytes 73736 | tf_op jit(solution)/shard_map/ppermute | solution.py:426
  10.0 1.1 %copy-start.7 = (bf16[48,48,128]{2,1,0:T(8,128)(2,1)S(1)}, bf16[48,48,128]{2,1,0:T(8,128)(2,1)}, u32[]{:S(2)}) copy-start(bf16[48,48,128]{2,1,0:T(8,128)(2,1)} %param.9) | copy-start | bytes 1769476
  11.1 0.9 %copy-start.8 = (bf16[1024,128]{1,0:T(8,128)(2,1)S(1)}, bf16[1024,128]{1,0:T(8,128)(2,1)}, u32[]{:S(2)}) copy-start(bf16[1024,128]{1,0:T(8,128)(2,1)} %w_hbm.1) | copy-start | bytes 786436
  12.0 0.7 %copy-start.9 = (bf16[8,1536]{1,0:T(8,128)(2,1)S(1)}, bf16[8,1536]{1,0:T(8,128)(2,1)}, u32[]{:S(2)}) copy-start(bf16[8,1536]{1,0:T(8,128)(2,1)} %a_hbm.1) | copy-start | bytes 73732
  12.7 0.7 %copy-start.10 = (bf16[8,1536]{1,0:T(8,128)(2,1)S(1)}, bf16[8,1536]{1,0:T(8,128)(2,1)}, u32[]{:S(2)}) copy-start(bf16[8,1536]{1,0:T(8,128)(2,1)} %b_hbm.1) | copy-start | bytes 73732
  17.9 2.1 %copy-start.2 = (bf16[1024,2304]{1,0:T(8,128)(2,1)}, bf16[1024,2304]{1,0:T(8,128)(2,1)S(1)}, u32[]{:S(2)}) copy-start(bf16[1024,2304]{1,0:T(8,128)(2,1)S(1)} %get-tuple-element.27.refs_4_) | copy-start | bytes 14155780
  20.1 2.2 %copy-start.4 = (bf16[1024,2304]{1,0:T(8,128)(2,1)}, bf16[1024,2304]{1,0:T(8,128)(2,1)S(1)}, u32[]{:S(2)}) copy-start(bf16[1024,2304]{1,0:T(8,128)(2,1)S(1)} %get-tuple-element.26.refs_4_) | copy-start | bytes 14155780
  29.3 2.2 %copy-start = (bf16[1024,2304]{1,0:T(8,128)(2,1)}, bf16[1024,2304]{1,0:T(8,128)(2,1)S(1)}, u32[]{:S(2)}) copy-start(bf16[1024,2304]{1,0:T(8,128)(2,1)S(1)} %get-tuple-element.23.x_ref) | copy-start | bytes 14155780
  31.5 9.7 %all-to-all-start = ((bf16[4,272,128]{2,1,0:T(8,128)(2,1)}), bf16[4,272,128]{2,1,0:T(8,128)(2,1)S(1)}, u32[]{:S(2)}, u32[]{:S(2)}) async-start(bf16[4,272,128]{2,1,0:T(8,128)(2,1)} %get-tuple-element.25), calls=%async_computation | async-start | bytes 557056 | tf_op jit(solution)/shard_map/all_to_all | solution.py:434
  34.9 2.3 %copy-start.5 = (bf16[1024,2304]{1,0:T(8,128)(2,1)S(1)}, bf16[1024,2304]{1,0:T(8,128)(2,1)}, u32[]{:S(2)}) copy-start(bf16[1024,2304]{1,0:T(8,128)(2,1)} %copy-done.4) | copy-start | bytes 14155780
  41.2 20.7 %copy-start.6 = (f32[128]{0:T(128)S(1)}, f32[128]{0:T(128)}, u32[]{:S(2)}) copy-start(f32[128]{0:T(128)} %param.8) | copy-start | bytes 1540
  42.0 15.7 %all-to-all-start.1 = ((bf16[4,368,128]{2,1,0:T(8,128)(2,1)}), bf16[4,368,128]{2,1,0:T(8,128)(2,1)S(1)}, u32[]{:S(2)}, u32[]{:S(2)}) async-start(bf16[4,368,128]{2,1,0:T(8,128)(2,1)} %shard_map.96), calls=%async_computation.1 | async-start | bytes 753664 | tf_op jit(solution)/shard_map/all_to_all | solution.py:434
  45.4 2.3 %copy-start.3 = (bf16[1024,2304]{1,0:T(8,128)(2,1)S(1)}, bf16[1024,2304]{1,0:T(8,128)(2,1)}, u32[]{:S(2)}) copy-start(bf16[1024,2304]{1,0:T(8,128)(2,1)} %copy-done.2) | copy-start | bytes 14155780
  58.4 10.5 %all-to-all-start.2 = ((bf16[4,352,128]{2,1,0:T(8,128)(2,1)}), bf16[4,352,128]{2,1,0:T(8,128)(2,1)S(1)}, u32[]{:S(2)}, u32[]{:S(2)}) async-start(bf16[4,352,128]{2,1,0:T(8,128)(2,1)} %get-tuple-element.29), calls=%async_computation.2 | async-start | bytes 720896 | tf_op jit(solution)/shard_map/all_to_all | solution.py:434
  61.9 2.3 %copy-start.1 = (bf16[1024,2304]{1,0:T(8,128)(2,1)S(1)}, bf16[1024,2304]{1,0:T(8,128)(2,1)}, u32[]{:S(2)}) copy-start(bf16[1024,2304]{1,0:T(8,128)(2,1)} %copy-done) | copy-start | bytes 14155780

commit v4 on v3

--- a/solution.py
+++ b/solution.py
@@ -108,7 +108,7 @@
             bytes_accessed=4 * pairs * channels,
             transcendentals=0,
         ),
-    )(a, b, w, g)
+    )(*[pltpu.with_memory_space_constraint(x, pltpu.HBM) for x in (a, b, w, g)])
 
 
 def join(pieces, axis, held):
@@ -151,12 +151,19 @@
             )
 
 
+def parts_shapes(count, rows):
+    return [jax.ShapeDtypeStruct((rows, LANES), F32)] + [
+        jax.ShapeDtypeStruct((rows, LANES), BF16)
+    ] * (count - 1)
+
+
 def outer_kernel(i_n, j_n, row_n, col_n, *refs):
     depth = PROJECTED_DEPTH
     a_pieces, refs = refs[:col_n], refs[col_n:]
     b_pieces, refs = refs[:row_n], refs[row_n:]
-    g_ref, bias_ref, x_ref, message = refs[:4]
-    a_held, b_held, wide, left, diagonal, total, ordered = refs[4:]
+    (g_ref, bias_ref, x_ref), refs = refs[:3], refs[3:]
+    messages, refs = refs[:row_n], refs[row_n:]
+    a_held, b_held, wide, left, diagonal, total, ordered = refs
     sequences = a_held.shape[0]
     groups = i_n // GROUP
     per_step = depth // STEPS
@@ -181,23 +188,26 @@
         for e in range(per_step):
             fill_diagonal(wide, diagonal, e, t * per_step + e, j_n, sequences)
         size = per_step * depth
-        first = pl.multiple_of(t * size, size)
+        rows = pl.ds(pl.multiple_of(t * size, size), size)
+        x_part = x_ref.at[rows]
         for e in range(0, per_step, 2):
             right = diagonal[e : e + 2].reshape(2 * span, diagonal.shape[2])
             product = dot(left[...], right, ROWS_BY_ROWS).astype(BF16)
             for n in range(2):
                 for k in range(groups):
-                    x_ref[pl.ds(first + (e + n) * depth, depth), k * span : (k + 1) * span] = product[
+                    x_part[(e + n) * depth : (e + n + 1) * depth, k * span : (k + 1) * span] = product[
                         k * depth : (k + 1) * depth, n * span : (n + 1) * span
                     ]
-        total[pl.ds(first, size), :] = dot(x_ref[pl.ds(first, size), :], g_ref[...])
+        total[rows, :] = dot(x_part[...], g_ref[...])
 
     for c in range(depth):
         ordered[c * depth : (c + 1) * depth, :] = total[pl.ds(c, depth, stride=depth), :]
     share = ordered.shape[0] // row_n
-    for p in range(row_n):
-        message[p, 0:share, :] = ordered[p * share : (p + 1) * share, :].astype(BF16)
-        message[p, share:, :] = bias_ref[...]
+    me = lax.axis_index("row")
+    for p, message in enumerate(messages):
+        start = pl.multiple_of(lax.rem(me + p, row_n) * share, share)
+        message[0:share, :] = ordered[pl.ds(start, share), :].astype(message.dtype)
+        message[share:, :] = bias_ref[...].astype(message.dtype)
 
 
 def outer(a_pieces, b_pieces, g, bias_rows, i_n, j_n, sequences):
@@ -208,14 +218,13 @@
     share = channels // row_n
     tiles = GROUP * sequences // LANES
     operands = [*a_pieces, *b_pieces, g, bias_rows]
-    return pl.pallas_call(
+    shapes = [jax.ShapeDtypeStruct((channels, pairs), BF16)]
+    shapes += parts_shapes(row_n, share + BIAS_ROWS)
+    results = pl.pallas_call(
         functools.partial(outer_kernel, i_n, j_n, row_n, col_n),
         in_specs=[in_vmem()] * len(operands),
-        out_specs=[in_vmem()] * 2,
-        out_shape=[
-            jax.ShapeDtypeStruct((channels, pairs), BF16),
-            jax.ShapeDtypeStruct((row_n, share + BIAS_ROWS, PAIR_FEATURES), BF16),
-        ],
+        out_specs=[in_vmem()] * len(shapes),
+        out_shape=shapes,
         scratch_shapes=[
             pltpu.VMEM((sequences, i_n * depth), F32),
             pltpu.VMEM((sequences, j_n * depth), F32),
@@ -232,12 +241,14 @@
             transcendentals=0,
         ),
     )(*operands)
-
-
-def gradient_kernel(axis, count, positions, others, *refs):
+    return results[0], results[1:]
+
+
+def gradient_kernel(axis, out_axis, count, parts, positions, others, *refs):
     depth = PROJECTED_DEPTH
-    pieces, source, out = refs[:count], refs[count], refs[count + 1]
-    held, wide, diagonal, result, grown, grad = refs[count + 2 :]
+    pieces, source, refs = refs[:count], refs[count], refs[count + 1 :]
+    outs, refs = refs[:parts], refs[parts:]
+    held, wide, diagonal, result, grown, grad = refs
     sequences = held.shape[0]
     per_step = depth // STEPS
     span = GROUP * others
@@ -251,12 +262,13 @@
     def _(t):
         for n in range(per_step):
             fill_diagonal(wide, diagonal, n, t * per_step + n, others, sequences)
-        first = pl.multiple_of(t * per_step * depth, per_step * depth)
+        size = per_step * depth
+        part = source.at[pl.ds(pl.multiple_of(t * size, size), size)]
         for n in range(0, per_step, 2):
             rows = [
                 jnp.concatenate(
                     [
-                        source[pl.ds(first + m * depth, depth), k * span : (k + 1) * span]
+                        part[m * depth : (m + 1) * depth, k * span : (k + 1) * span]
                         for m in (n, n + 1)
                     ],
                     axis=1,
@@ -281,24 +293,27 @@
                     else jnp.zeros((depth, LANES), BF16)
                 )
     grad[...] = dot(repeat_matrix(sequences), grown[...], ROWS_BY_ROWS)
-    share = sequences // out.shape[0]
-    for p in range(out.shape[0]):
-        mine = grad[p * share : (p + 1) * share, :]
-        out[p] = jnp.concatenate(
+    share = sequences // parts
+    me = lax.axis_index(out_axis)
+    for p, out in enumerate(outs):
+        mine = grad[pl.ds(pl.multiple_of(lax.rem(me + p, parts) * share, share), share), :]
+        out[...] = jnp.concatenate(
             [mine[:, l * LANES : (l + 1) * LANES] for l in range(mine.shape[1] // LANES)], axis=0
-        ).astype(BF16)
-
-
-def gradient(pieces, axis, source, parts, positions, others, sequences):
+        ).astype(out.dtype)
+
+
+def gradient(pieces, axis, out_axis, source, parts, positions, others, sequences):
     depth = PROJECTED_DEPTH
     channels, pairs = source.shape
     tiles = GROUP * sequences // LANES
     rows = sequences // parts * positions * depth // LANES
     return pl.pallas_call(
-        functools.partial(gradient_kernel, axis, len(pieces), positions, others),
+        functools.partial(
+            gradient_kernel, axis, out_axis, len(pieces), parts, positions, others
+        ),
         in_specs=[in_vmem()] * (len(pieces) + 1),
-        out_specs=in_vmem(),
-        out_shape=jax.ShapeDtypeStruct((parts, rows, LANES), BF16),
+        out_specs=[in_vmem()] * parts,
+        out_shape=parts_shapes(parts, rows),
         scratch_shapes=[
             pltpu.VMEM((sequences, others * depth), F32),
             pltpu.VMEM((tiles, others * depth, LANES), F32),
@@ -344,81 +359,105 @@
     )(x, wt, output_bias.reshape(1, PAIR_FEATURES))
 
 
-def sum_parts(ref, start, stop):
-    total = ref[0, start:stop, :].astype(F32)
-    for n in range(1, ref.shape[0]):
-        total += ref[n, start:stop, :].astype(F32)
-    return total
-
-
 def unfold(total, share, out):
     for l in range(out.shape[1] // LANES):
         out[:, l * LANES : (l + 1) * LANES] = total[l * share : (l + 1) * share, :]
 
 
-def row_sum_kernel(parts, grads, message):
-    rows = parts.shape[1]
-    total = sum_parts(parts, 0, rows).astype(BF16)
-    for p in range(message.shape[0]):
-        message[p, 0:rows, :] = total
-        message[p, rows:, :] = grads[p]
+def row_sum_kernel(row_n, *refs):
+    parts, refs = refs[:row_n], refs[row_n:]
+    grads, messages = refs[: len(refs) // 2], refs[len(refs) // 2 :]
+    rows = parts[0].shape[0]
+    total = parts[0][...]
+    for part in parts[1:]:
+        total += part[...].astype(F32)
+    total = total.astype(BF16)
+    for message, grad in zip(messages, grads, strict=True):
+        message[0:rows, :] = total
+        message[rows:, :] = grad[...]
 
 
 def row_sum(parts, grads):
-    shape = (grads.shape[0], parts.shape[1] + grads.shape[1], LANES)
+    shape = (parts[0].shape[0] + grads[0].shape[0], LANES)
     return pl.pallas_call(
-        row_sum_kernel,
-        in_specs=[in_vmem()] * 2,
-        out_specs=in_vmem(),
-        out_shape=jax.ShapeDtypeStruct(shape, BF16),
+        functools.partial(row_sum_kernel, len(parts)),
+        in_specs=[in_vmem()] * (len(parts) + len(grads)),
+        out_specs=[in_vmem()] * len(grads),
+        out_shape=[jax.ShapeDtypeStruct(shape, BF16)] * len(grads),
         compiler_params=params(),
-    )(parts, grads)
-
-
-def column_sum_kernel(res_total, parts, grads, message, left_out, bias_out):
-    share = message.shape[1] - grads.shape[1]
-    total = sum_parts(parts, 0, share + BIAS_ROWS)
+    )(*parts, *grads)
+
+
+def column_sum_kernel(res_total, col_n, *refs):
+    parts, grad, refs = refs[: col_n - 1], refs[col_n - 1], refs[col_n:]
+    own, refs = refs[0], refs[1:]
+    grads, refs = refs[: (len(refs) - 4) // 2], refs[(len(refs) - 4) // 2 :]
+    messages, (piece_out, left_out, bias_out, held) = refs[:-4], refs[-4:]
+    share = piece_out.shape[0]
+    rows = share + BIAS_ROWS
+    me = lax.axis_index("col")
+    for p, part in enumerate((own, *parts)):
+        held[lax.rem(me - p + col_n, col_n)] = part[0:rows, :]
+    total = held[0].astype(F32)
+    for n in range(1, col_n):
+        total += held[n].astype(F32)
     piece = total[0:share].astype(BF16)
-    for p in range(message.shape[0]):
-        message[p, 0:share, :] = piece
-        message[p, share:, :] = grads[p]
+    piece_out[...] = piece
+    for message, other in zip(messages, grads, strict=True):
+        message[0:share, :] = piece
+        message[share:, :] = other[...]
     bias_out[...] = (total[share : share + 1] + total[share + 1 : share + 2]) * (1.0 / res_total)
-    unfold(sum_parts(parts, share + BIAS_ROWS, parts.shape[1]), left_out.shape[0], left_out)
-
-
-def column_sum(parts, grads, share, left_shape, res_total):
-    return pl.pallas_call(
-        functools.partial(column_sum_kernel, res_total),
-        in_specs=[in_vmem()] * 2,
-        out_specs=[in_vmem()] * 3,
-        out_shape=[
-            jax.ShapeDtypeStruct((grads.shape[0], share + grads.shape[1], LANES), BF16),
-            jax.ShapeDtypeStruct(left_shape, F32),
-            jax.ShapeDtypeStruct((1, PAIR_FEATURES), F32),
-        ],
+    left = grad[...]
+    for part in parts:
+        left += part[rows:, :].astype(F32)
+    unfold(left, left_out.shape[0], left_out)
+
+
+def column_sum(parts, left_own, own, grads, share, left_shape, res_total):
+    rows = share + grads[0].shape[0]
+    operands = [*parts, left_own, own, *grads]
+    shapes = [jax.ShapeDtypeStruct((rows, LANES), BF16)] * len(grads) + [
+        jax.ShapeDtypeStruct((share, LANES), BF16),
+        jax.ShapeDtypeStruct(left_shape, F32),
+        jax.ShapeDtypeStruct((1, PAIR_FEATURES), F32),
+    ]
+    *messages, piece, left, bias = pl.pallas_call(
+        functools.partial(column_sum_kernel, res_total, len(parts) + 1),
+        in_specs=[in_vmem()] * len(operands),
+        out_specs=[in_vmem()] * len(shapes),
+        out_shape=shapes,
+        scratch_shapes=[pltpu.VMEM((len(parts) + 1, share + BIAS_ROWS, LANES), BF16)],
         compiler_params=params(),
-    )(parts, grads)
-
-
-def finish_kernel(scale, parts, projection, right_out):
-    count = parts.shape[0]
-    share = projection.shape[0] // count
-    for p in range(count):
-        projection[p * share : (p + 1) * share, :] = parts[p, 0:share, :].astype(F32) * scale
-    unfold(sum_parts(parts, share, parts.shape[1]), right_out.shape[0], right_out)
-
-
-def finish(parts, channels, right_shape, scale):
+    )(*operands)
+    return messages, piece, left, bias
+
+
+def finish_kernel(scale, *refs):
+    parts, (piece, grad, projection, right_out) = refs[:-4], refs[-4:]
+    row_n = len(parts) + 1
+    share = piece.shape[0]
+    me = lax.axis_index("row")
+    right = grad[...]
+    for p, part in enumerate((piece, *parts)):
+        start = pl.multiple_of(lax.rem(me - p + row_n, row_n) * share, share)
+        projection[pl.ds(start, share), :] = part[0:share, :].astype(F32) * scale
+        if p > 0:
+            right += part[share:, :].astype(F32)
+    unfold(right, right_out.shape[0], right_out)
+
+
+def finish(parts, piece, right_own, right_shape, scale):
+    operands = [*parts, piece, right_own]
     return pl.pallas_call(
         functools.partial(finish_kernel, scale),
-        in_specs=[in_vmem()],
+        in_specs=[in_vmem()] * len(operands),
         out_specs=[in_vmem()] * 2,
         out_shape=[
-            jax.ShapeDtypeStruct((channels, PAIR_FEATURES), F32),
+            jax.ShapeDtypeStruct((piece.shape[0] * (len(parts) + 1), PAIR_FEATURES), F32),
             jax.ShapeDtypeStruct(right_shape, F32),
         ],
         compiler_params=params(),
-    )(parts)
+    )(*operands)
 
 
 def shift(x, axis, distance):
@@ -431,7 +470,7 @@
 
 
 def exchange(parts, axis):
-    return lax.all_to_all(parts, axis, 0, 0, tiled=True)
+    return [shift(part, axis, d) for d, part in enumerate(parts, 1)]
 
 
 def local(
@@ -455,18 +494,29 @@
     a_pieces = [a_own] + a_pieces
     b_pieces = [b_own] + b_pieces
 
-    x, message = outer(a_pieces, b_pieces, g, bias_rows, i_n, j_n, sequences)
-    parts = exchange(message, "row")
-    left_grads = gradient(b_pieces, "row", y, col_n, i_n, j_n, sequences)
-    parts = exchange(row_sum(parts, left_grads), "col")
-    right_grads = gradient(a_pieces, "col", y2, row_n, j_n, i_n, sequences)
-    message, left_grad, bias_grad = column_sum(
-        parts, right_grads, channels // row_n, first_homolog_features.shape, res_total
+    x, (row_own, *messages) = outer(a_pieces, b_pieces, g, bias_rows, i_n, j_n, sequences)
+    row_parts = [row_own] + exchange(messages, "row")
+    left_own, *left_grads = gradient(b_pieces, "row", "col", y, col_n, i_n, j_n, sequences)
+    messages = row_sum(row_parts, left_grads)
+    col_parts = exchange(messages, "col")
+    right_own, *right_grads = gradient(a_pieces, "col", "row", y2, row_n, j_n, i_n, sequences)
+    messages, piece, left_grad, bias_grad = column_sum(
+        col_parts,
+        left_own,
+        messages[0],
+        right_grads,
+        channels // row_n,
+        first_homolog_features.shape,
+        res_total,
     )
-    parts = exchange(message, "row")
+    row_parts = exchange(messages, "row")
     pair_map = pair(x, wt, output_bias, sequences)
     projection, right_grad = finish(
-        parts, channels, second_homolog_features.shape, 1.0 / (sequences * res_total)
+        row_parts,
+        piece,
+        right_own,
+        second_homolog_features.shape,
+        1.0 / (sequences * res_total),
     )
     return (
         pair_map.reshape(i_n, j_n, PAIR_FEATURES),

time: 70.4 us -> 45.6 us (0.65)
  local copies, waits for them, and re-layouts: 17 us -> 0.01 us
  waiting for transfers between devices: 8.16 us -> 2.95 us
  starting transfers between devices: 19.7 us -> 18.3 us
  Pallas kernels: 24.1 us -> 23 us
    unnamed x22 -> x2, local copies, waits for them, and re-layouts: 17 us -> 0.01 us
    all_to_all x3 -> x0, starting transfers between devices: 10.4 us -> none  [exchange(): return lax.all_to_all(parts, axis, 0, 0, tiled=True)]
    ppermute x6 -> x15, starting transfers between devices: 9.35 us -> 18.3 us  [shift(): lax.ppermute(x, axis, [(n, (n + distance) % count) for n in range(count)])]
    all_to_all x3 -> x0, waiting for transfers between devices: 8.14 us -> none  [exchange(): return lax.all_to_all(parts, axis, 0, 0, tiled=True)]
    ppermute x6 -> x15, waiting for transfers between devices: 0.02 us -> 2.95 us  [shift(): lax.ppermute(x, axis, [(n, (n + distance) % count) for n in range(count)])]
    pallas_call x1, Pallas kernels: 6.97 us -> 5.77 us  [outer(): pl.pallas_call(functools.partial(outer_kernel, i_n, j_n, row_n, col_n), i...]
    pallas_call x1, Pallas kernels: 4.43 us -> 5.19 us  [prepare(): pl.pallas_call(functools.partial(prepare_kernel, i_n, j_n), in_specs=[pl....]
    pallas_call x4, Pallas kernels: 9.31 us -> 8.6 us  [the longest x2 7.83 us: gradient(): pl.pallas_call(functools.partial(gradient_kernel, axis, out_axis, len(pie...]
  transfers between devices with their start and end apart: 9 -> 15, of which waited for: 2 -> 4; matrix products, arithmetic and copies ran while one was open for 0% -> 0% of each run, Pallas kernels for 21% -> 35%
where the time goes in v4:
time: 45.6 us; the launch traced here: 45 us
  Pallas kernels  23 us (50%)
  starting transfers between devices  18.3 us (40%)
  waiting for transfers between devices  2.95 us (6%)
  between operations  0.75 us (2%)
    ppermute x15, starting transfers between devices, shift(): lax.ppermute(x, axis, [(n, (n + distance) % count) for n in range(count)])  18.3 us
    pallas_call x2, Pallas kernels, gradient(): pl.pallas_call(functools.partial(gradient_kernel, axis, out_axis, len(pie...  7.83 us
    pallas_call x1, Pallas kernels, outer(): pl.pallas_call(functools.partial(outer_kernel, i_n, j_n, row_n, col_n), i...  5.77 us
    pallas_call x1, Pallas kernels, prepare(): pl.pallas_call(functools.partial(prepare_kernel, i_n, j_n), in_specs=[pl....  5.19 us
    ppermute x15, waiting for transfers between devices, shift(): lax.ppermute(x, axis, [(n, (n + distance) % count) for n in range(count)])  2.95 us
    pallas_call x1, Pallas kernels, pair(): pl.pallas_call(functools.partial(pair_kernel, sequences), grid=(count,),...  2.56 us
  transfers between devices with their start and end apart: 15, of which 4 were waited for; matrix products, arithmetic and copies ran while one was open for 0% of the time, Pallas kernels for 35%

profile of v4, /device:TPU:0, one launch (start us, length us, event | category | flops | bytes accessed | tf_op | source)
XLA Modules:
  0.0 45.0 jit_solution(9202316140464639939)
XLA Ops:
  0.6 3.1 %collective-permute-start = (bf16[8,1536]{1,0:T(8,128)(2,1)}, bf16[8,1536]{1,0:T(8,128)(2,1)S(1)}, u32[]{:S(2)}, u32[]{:S(2)}) collective-permute-start(bf16[8,1536]{1,0:T(8,128)(2,1)} %a_hbm.1), channel_id=1, source_target_pairs={{0,1},{1,2},{2,3},{3,0},{4,5},{5,6},{6,7},{7,4},{8,9},{9,10},{10,1... | collective-permute-start | bytes 73736 | tf_op jit(solution)/shard_map/ppermute | solution.py:465
  3.7 2.1 %collective-permute-start.2 = (bf16[8,1536]{1,0:T(8,128)(2,1)}, bf16[8,1536]{1,0:T(8,128)(2,1)S(1)}, u32[]{:S(2)}, u32[]{:S(2)}) collective-permute-start(bf16[8,1536]{1,0:T(8,128)(2,1)} %a_hbm.1), channel_id=1, source_target_pairs={{0,3},{1,0},{2,1},{3,2},{4,7},{5,4},{6,5},{7,6},{8,11},{9,8},{10,9... | collective-permute-start | bytes 73736 | tf_op jit(solution)/shard_map/ppermute | solution.py:465
  5.8 0.9 %collective-permute-start.1 = (bf16[8,1536]{1,0:T(8,128)(2,1)}, bf16[8,1536]{1,0:T(8,128)(2,1)S(1)}, u32[]{:S(2)}, u32[]{:S(2)}) collective-permute-start(bf16[8,1536]{1,0:T(8,128)(2,1)} %a_hbm.1), channel_id=1, source_target_pairs={{0,2},{1,3},{2,0},{3,1},{4,6},{5,7},{6,4},{7,5},{8,10},{9,11},{10,... | collective-permute-start | bytes 73736 | tf_op jit(solution)/shard_map/ppermute | solution.py:465
  6.7 0.0 collective-permute-start.3
  6.8 1.7 %collective-permute-start.5 = (bf16[8,1536]{1,0:T(8,128)(2,1)}, bf16[8,1536]{1,0:T(8,128)(2,1)S(1)}, u32[]{:S(2)}, u32[]{:S(2)}) collective-permute-start(bf16[8,1536]{1,0:T(8,128)(2,1)} %b_hbm.1), channel_id=1, source_target_pairs={{0,12},{4,0},{8,4},{12,8},{1,13},{5,1},{9,5},{13,9},{2,14},{6,2},{... | collective-permute-start | bytes 73736 | tf_op jit(solution)/shard_map/ppermute | solution.py:465
  8.5 0.0 collective-permute-done.refs_1_
  8.5 1.5 %collective-permute-start.4 = (bf16[8,1536]{1,0:T(8,128)(2,1)}, bf16[8,1536]{1,0:T(8,128)(2,1)S(1)}, u32[]{:S(2)}, u32[]{:S(2)}) collective-permute-start(bf16[8,1536]{1,0:T(8,128)(2,1)} %b_hbm.1), channel_id=1, source_target_pairs={{0,8},{4,12},{8,0},{12,4},{1,9},{5,13},{9,1},{13,5},{2,10},{6,14},... | collective-permute-start | bytes 73736 | tf_op jit(solution)/shard_map/ppermute | solution.py:465
  10.0 5.2 %shard_map.92 = (bf16[1024,2304]{1,0:T(8,128)(2,1)S(1)}, bf16[1024,2304]{1,0:T(8,128)(2,1)S(1)}, bf16[128,1024]{1,0:T(8,128)(2,1)S(1)}, bf16[16,128]{1,0:T(8,128...) custom-call(bf16[8,1536]{1,0:T(8,128)(2,1)} %a_hbm.1, ...), custom_call_target="tpu_custom_call" | custom-call | flops 1207959552 | bytes 9437184 | tf_op jit(solution)/shard_map/pallas_call | solution.py:92
  15.2 0.0 collective-permute-done.2.refs_3_
  15.2 0.0 collective-permute-done.1.refs_2_
  15.2 0.0 collective-permute-done.3.refs_5_.refs_1_
  15.2 5.8 %shard_map.93 = (bf16[1024,2304]{1,0:T(8,128)(2,1)S(1)}, f32[272,128]{1,0:T(8,128)S(1)}, bf16[272,128]{1,0:T(8,128)(2,1)S(1)}, bf16[272,128]{1,0:T(8,128)(2,1)S(1)}, bf16[272,128]{1,0:T(8,128)(2,1)S(1)}) custom-call(bf16[8,1536]{1,0:T(8,128)(2,1)S(1)} %get-tuple-element.36.refs_0_, bf16[8,1536]{1,0:T(8,128)(2,1)S(1)} %collective-permute-done.refs_1_, ...), custom_call_target="tpu_custom_call" | custom-call | flops 1207959552 | bytes 4718592 | tf_op jit(solution)/shard_map/pallas_call | solution.py:223
  21.0 0.1 collective-permute-start.6
  21.1 0.6 %collective-permute-start.7 = (bf16[272,128]{1,0:T(8,128)(2,1)S(1)}, bf16[272,128]{1,0:T(8,128)(2,1)S(1)}, u32[]{:S(2)}, u32[]{:S(2)}) collective-permute-start(bf16[272,128]{1,0:T(8,128)(2,1)S(1)} %get-tuple-element.44), channel_id=1, source_target_pairs={{0,8},{4,12},{8,0},{12,4},{1,9},{5,13},{9,1},{13,5},{2,10},{6,14},... | collective-permute-start | bytes 208904 | tf_op jit(solution)/shard_map/ppermute | solution.py:465
  21.7 1.4 %collective-permute-start.8 = (bf16[272,128]{1,0:T(8,128)(2,1)S(1)}, bf16[272,128]{1,0:T(8,128)(2,1)S(1)}, u32[]{:S(2)}, u32[]{:S(2)}) collective-permute-start(bf16[272,128]{1,0:T(8,128)(2,1)S(1)} %get-tuple-element.45), channel_id=1, source_target_pairs={{0,12},{4,0},{8,4},{12,8},{1,13},{5,1},{9,5},{13,9},{2,14},{6,2},{... | collective-permute-start | bytes 208904 | tf_op jit(solution)/shard_map/ppermute | solution.py:465
  23.1 3.9 %shard_map.95 = (f32[96,128]{1,0:T(8,128)S(1)}, bf16[96,128]{1,0:T(8,128)(2,1)S(1)}, bf16[96,128]{1,0:T(8,128)(2,1)S(1)}, bf16[96,128]{1,0:T(8,128)(2,1)S(1)}) custom-call(bf16[8,1536]{1,0:T(8,128)(2,1)S(1)} %get-tuple-element.37.refs_4_.refs_0_, bf16[8,1536]{1,0:T(8,128)(2,1)S(1)} %collective-permute-done.3.refs_5_.refs_1_, ...), custom_call_target="tpu_custom_call" | custom-call | flops 603979776 | bytes 4718592 | tf_op jit(solution)/shard_map/pallas_call | solution.py:310
  27.0 0.0 collective-permute-done.8.refs_3_
  27.1 2.1 %collective-permute-start.10 = (bf16[368,128]{1,0:T(8,128)(2,1)S(1)}, bf16[368,128]{1,0:T(8,128)(2,1)S(1)}, u32[]{:S(2)}, u32[]{:S(2)}) collective-permute-start(bf16[368,128]{1,0:T(8,128)(2,1)S(1)} %get-tuple-element.51), channel_id=1, source_target_pairs={{0,2},{1,3},{2,0},{3,1},{4,6},{5,7},{6,4},{7,5},{8,10},{9,11},{10,... | collective-permute-start | bytes 282632 | tf_op jit(solution)/shard_map/ppermute | solution.py:465
  29.1 1.9 %collective-permute-start.11 = (bf16[368,128]{1,0:T(8,128)(2,1)S(1)}, bf16[368,128]{1,0:T(8,128)(2,1)S(1)}, u32[]{:S(2)}, u32[]{:S(2)}) collective-permute-start(bf16[368,128]{1,0:T(8,128)(2,1)S(1)} %get-tuple-element.52), channel_id=1, source_target_pairs={{0,3},{1,0},{2,1},{3,2},{4,7},{5,4},{6,5},{7,6},{8,11},{9,8},{10,9... | collective-permute-start | bytes 282632 | tf_op jit(solution)/shard_map/ppermute | solution.py:465
  31.1 0.1 collective-permute-start.9
  31.2 3.9 %shard_map.97 = (f32[96,128]{1,0:T(8,128)S(1)}, bf16[96,128]{1,0:T(8,128)(2,1)S(1)}, bf16[96,128]{1,0:T(8,128)(2,1)S(1)}, bf16[96,128]{1,0:T(8,128)(2,1)S(1)}) custom-call(bf16[8,1536]{1,0:T(8,128)(2,1)S(1)} %get-tuple-element.36.refs_0_, bf16[8,1536]{1,0:T(8,128)(2,1)S(1)} %collective-permute-done.refs_1_, ...), custom_call_target="tpu_custom_call" | custom-call | flops 603979776 | bytes 4718592 | tf_op jit(solution)/shard_map/pallas_call | solution.py:310
  35.1 1.1 %collective-permute-done.10.refs_1_ = bf16[368,128]{1,0:T(8,128)(2,1)S(1)} collective-permute-done((bf16[368,128]{1,0:T(8,128)(2,1)S(1)}, bf16[368,128]{1,0:T(8,128)(2,1)S(1)}, u32[]{:S(2)}, u32[]{:S(2)}) %collective-permute-start.10) | collective-permute-done | bytes 94240 | tf_op jit(solution)/shard_map/ppermute | solution.py:465
  36.2 1.4 %collective-permute-done.9.refs_0_ = bf16[368,128]{1,0:T(8,128)(2,1)S(1)} collective-permute-done((bf16[368,128]{1,0:T(8,128)(2,1)S(1)}, bf16[368,128]{1,0:T(8,128)(2,1)S(1)}, u32[]{:S(2)}, u32[]{:S(2)}) %collective-permute-start.9) | collective-permute-done | bytes 94240 | tf_op jit(solution)/shard_map/ppermute | solution.py:465
  37.7 0.7 %shard_map.98 = (bf16[352,128]{1,0:T(8,128)(2,1)S(1)}, bf16[352,128]{1,0:T(8,128)(2,1)S(1)}, bf16[352,128]{1,0:T(8,128)(2,1)S(1)}, bf16[256,128]{1,0:T(8,128)(2,...) custom-call(bf16[368,128]{1,0:T(8,128)(2,1)S(1)} %collective-permute-done.9.refs_0_, ...), custom_call_target="tpu_custom_call" | custom-call | tf_op jit(solution)/shard_map/pallas_call | solution.py:424
  38.4 0.0 collective-permute-start.12
  38.4 1.4 %collective-permute-start.13 = (bf16[352,128]{1,0:T(8,128)(2,1)S(1)}, bf16[352,128]{1,0:T(8,128)(2,1)S(1)}, u32[]{:S(2)}, u32[]{:S(2)}) collective-permute-start(bf16[352,128]{1,0:T(8,128)(2,1)S(1)} %get-tuple-element.60), channel_id=1, source_target_pairs={{0,8},{4,12},{8,0},{12,4},{1,9},{5,13},{9,1},{13,5},{2,10},{6,14},... | collective-permute-start | bytes 270344 | tf_op jit(solution)/shard_map/ppermute | solution.py:465
  39.8 1.4 %collective-permute-start.14 = (bf16[352,128]{1,0:T(8,128)(2,1)S(1)}, bf16[352,128]{1,0:T(8,128)(2,1)S(1)}, u32[]{:S(2)}, u32[]{:S(2)}) collective-permute-start(bf16[352,128]{1,0:T(8,128)(2,1)S(1)} %get-tuple-element.61), channel_id=1, source_target_pairs={{0,12},{4,0},{8,4},{12,8},{1,13},{5,1},{9,5},{13,9},{2,14},{6,2},{... | collective-permute-start | bytes 270344 | tf_op jit(solution)/shard_map/ppermute | solution.py:465
  41.2 2.6 %shard_map.94 = bf16[2304,128]{1,0:T(8,128)(2,1)} custom-call(bf16[1024,2304]{1,0:T(8,128)(2,1)S(1)} %get-tuple-element.40.x_ref, bf16[128,1024]{1,0:T(8,128)(2,1)S(1)} %get-tuple-element.41.wt_ref, f32[1,128]{1,0:T(1,128)S(1)} %bitcast.4), custom_call_target="tpu_custom_call" | custom-call | flops 1207959552 | bytes 4718592 | tf_op jit(solution)/shard_map/pallas_call | solution.py:343
  43.8 0.0 collective-permute-done.12.refs_0_
  43.8 0.1 collective-permute-done.13.refs_1_
  43.9 0.3 collective-permute-done.14.refs_2_
  44.1 0.8 %shard_map.99 = (f32[1024,128]{1,0:T(8,128)}, f32[8,1536]{1,0:T(8,128)}) custom-call(bf16[352,128]{1,0:T(8,128)(2,1)S(1)} %collective-permute-done.12.refs_0_, bf16[352,128]{1,0:T(8,128)(2,1)S(1)} %collective-permute-done.13.refs_1_, bf16[352,128]{1,0:T(8,128)(2,1)S(1)} %collective-permute-done.14.refs_2_, bf16[256,128]{1,0:T(8,128)(2,1)S(1)} %get-tuple-element.62.refs_3_, ...), custom_call_target="tpu_custom_call" | custom-call | tf_op jit(solution)/shard_map/pallas_call | solution.py:451
  (8 shorter events, 0.1 us)
Async XLA Ops:
  0.6 7.9 %collective-permute-start = (bf16[8,1536]{1,0:T(8,128)(2,1)}, bf16[8,1536]{1,0:T(8,128)(2,1)S(1)}, u32[]{:S(2)}, u32[]{:S(2)}) collective-permute-start(bf16[8,1536]{1,0:T(8,128)(2,1)} %a_hbm.1), channel_id=1, source_target_pairs={{0,1},{1,2},{2,3},{3,0},{4,5},{5,6},{6,7},{7,4},{8,9},{9,10},{10,1... | collective-permute-start | bytes 73736 | tf_op jit(solution)/shard_map/ppermute | solution.py:465
  3.7 11.5 %collective-permute-start.2 = (bf16[8,1536]{1,0:T(8,128)(2,1)}, bf16[8,1536]{1,0:T(8,128)(2,1)S(1)}, u32[]{:S(2)}, u32[]{:S(2)}) collective-permute-start(bf16[8,1536]{1,0:T(8,128)(2,1)} %a_hbm.1), channel_id=1, source_target_pairs={{0,3},{1,0},{2,1},{3,2},{4,7},{5,4},{6,5},{7,6},{8,11},{9,8},{10,9... | collective-permute-start | bytes 73736 | tf_op jit(solution)/shard_map/ppermute | solution.py:465
  5.8 9.4 %collective-permute-start.1 = (bf16[8,1536]{1,0:T(8,128)(2,1)}, bf16[8,1536]{1,0:T(8,128)(2,1)S(1)}, u32[]{:S(2)}, u32[]{:S(2)}) collective-permute-start(bf16[8,1536]{1,0:T(8,128)(2,1)} %a_hbm.1), channel_id=1, source_target_pairs={{0,2},{1,3},{2,0},{3,1},{4,6},{5,7},{6,4},{7,5},{8,10},{9,11},{10,... | collective-permute-start | bytes 73736 | tf_op jit(solution)/shard_map/ppermute | solution.py:465
  6.7 8.5 %collective-permute-start.3 = (bf16[8,1536]{1,0:T(8,128)(2,1)}, bf16[8,1536]{1,0:T(8,128)(2,1)S(1)}, u32[]{:S(2)}, u32[]{:S(2)}) collective-permute-start(bf16[8,1536]{1,0:T(8,128)(2,1)} %b_hbm.1), channel_id=1, source_target_pairs={{0,4},{4,8},{8,12},{12,0},{1,5},{5,9},{9,13},{13,1},{2,6},{6,10},{... | collective-permute-start | bytes 73736 | tf_op jit(solution)/shard_map/ppermute | solution.py:465
  6.8 8.5 %collective-permute-start.5 = (bf16[8,1536]{1,0:T(8,128)(2,1)}, bf16[8,1536]{1,0:T(8,128)(2,1)S(1)}, u32[]{:S(2)}, u32[]{:S(2)}) collective-permute-start(bf16[8,1536]{1,0:T(8,128)(2,1)} %b_hbm.1), channel_id=1, source_target_pairs={{0,12},{4,0},{8,4},{12,8},{1,13},{5,1},{9,5},{13,9},{2,14},{6,2},{... | collective-permute-start | bytes 73736 | tf_op jit(solution)/shard_map/ppermute | solution.py:465
  8.5 6.7 %collective-permute-start.4 = (bf16[8,1536]{1,0:T(8,128)(2,1)}, bf16[8,1536]{1,0:T(8,128)(2,1)S(1)}, u32[]{:S(2)}, u32[]{:S(2)}) collective-permute-start(bf16[8,1536]{1,0:T(8,128)(2,1)} %b_hbm.1), channel_id=1, source_target_pairs={{0,8},{4,12},{8,0},{12,4},{1,9},{5,13},{9,1},{13,5},{2,10},{6,14},... | collective-permute-start | bytes 73736 | tf_op jit(solution)/shard_map/ppermute | solution.py:465
  21.0 6.0 %collective-permute-start.6 = (bf16[272,128]{1,0:T(8,128)(2,1)S(1)}, bf16[272,128]{1,0:T(8,128)(2,1)S(1)}, u32[]{:S(2)}, u32[]{:S(2)}) collective-permute-start(bf16[272,128]{1,0:T(8,128)(2,1)S(1)} %get-tuple-element.43), channel_id=1, source_target_pairs={{0,4},{4,8},{8,12},{12,0},{1,5},{5,9},{9,13},{13,1},{2,6},{6,10},{... | collective-permute-start | bytes 208904 | tf_op jit(solution)/shard_map/ppermute | solution.py:465
  21.1 5.9 %collective-permute-start.7 = (bf16[272,128]{1,0:T(8,128)(2,1)S(1)}, bf16[272,128]{1,0:T(8,128)(2,1)S(1)}, u32[]{:S(2)}, u32[]{:S(2)}) collective-permute-start(bf16[272,128]{1,0:T(8,128)(2,1)S(1)} %get-tuple-element.44), channel_id=1, source_target_pairs={{0,8},{4,12},{8,0},{12,4},{1,9},{5,13},{9,1},{13,5},{2,10},{6,14},... | collective-permute-start | bytes 208904 | tf_op jit(solution)/shard_map/ppermute | solution.py:465
  21.7 5.3 %collective-permute-start.8 = (bf16[272,128]{1,0:T(8,128)(2,1)S(1)}, bf16[272,128]{1,0:T(8,128)(2,1)S(1)}, u32[]{:S(2)}, u32[]{:S(2)}) collective-permute-start(bf16[272,128]{1,0:T(8,128)(2,1)S(1)} %get-tuple-element.45), channel_id=1, source_target_pairs={{0,12},{4,0},{8,4},{12,8},{1,13},{5,1},{9,5},{13,9},{2,14},{6,2},{... | collective-permute-start | bytes 208904 | tf_op jit(solution)/shard_map/ppermute | solution.py:465
  23.1 18.2 %copy-start = (f32[128]{0:T(128)S(1)}, f32[128]{0:T(128)}, u32[]{:S(2)}) copy-start(f32[128]{0:T(128)} %param.8) | copy-start | bytes 1540
  27.1 9.2 %collective-permute-start.10 = (bf16[368,128]{1,0:T(8,128)(2,1)S(1)}, bf16[368,128]{1,0:T(8,128)(2,1)S(1)}, u32[]{:S(2)}, u32[]{:S(2)}) collective-permute-start(bf16[368,128]{1,0:T(8,128)(2,1)S(1)} %get-tuple-element.51), channel_id=1, source_target_pairs={{0,2},{1,3},{2,0},{3,1},{4,6},{5,7},{6,4},{7,5},{8,10},{9,11},{10,... | collective-permute-start | bytes 282632 | tf_op jit(solution)/shard_map/ppermute | solution.py:465
  29.1 7.1 %collective-permute-start.11 = (bf16[368,128]{1,0:T(8,128)(2,1)S(1)}, bf16[368,128]{1,0:T(8,128)(2,1)S(1)}, u32[]{:S(2)}, u32[]{:S(2)}) collective-permute-start(bf16[368,128]{1,0:T(8,128)(2,1)S(1)} %get-tuple-element.52), channel_id=1, source_target_pairs={{0,3},{1,0},{2,1},{3,2},{4,7},{5,4},{6,5},{7,6},{8,11},{9,8},{10,9... | collective-permute-start | bytes 282632 | tf_op jit(solution)/shard_map/ppermute | solution.py:465
  31.1 6.6 %collective-permute-start.9 = (bf16[368,128]{1,0:T(8,128)(2,1)S(1)}, bf16[368,128]{1,0:T(8,128)(2,1)S(1)}, u32[]{:S(2)}, u32[]{:S(2)}) collective-permute-start(bf16[368,128]{1,0:T(8,128)(2,1)S(1)} %get-tuple-element.50.refs_4_), channel_id=1, source_target_pairs={{0,1},{1,2},{2,3},{3,0},{4,5},{5,6},{6,7},{7,4},{8,9},{9,10},{10,1... | collective-permute-start | bytes 282632 | tf_op jit(solution)/shard_map/ppermute | solution.py:465
  38.4 5.4 %collective-permute-start.12 = (bf16[352,128]{1,0:T(8,128)(2,1)S(1)}, bf16[352,128]{1,0:T(8,128)(2,1)S(1)}, u32[]{:S(2)}, u32[]{:S(2)}) collective-permute-start(bf16[352,128]{1,0:T(8,128)(2,1)S(1)} %get-tuple-element.59), channel_id=1, source_target_pairs={{0,4},{4,8},{8,12},{12,0},{1,5},{5,9},{9,13},{13,1},{2,6},{6,10},{... | collective-permute-start | bytes 270344 | tf_op jit(solution)/shard_map/ppermute | solution.py:465
  38.4 5.5 %collective-permute-start.13 = (bf16[352,128]{1,0:T(8,128)(2,1)S(1)}, bf16[352,128]{1,0:T(8,128)(2,1)S(1)}, u32[]{:S(2)}, u32[]{:S(2)}) collective-permute-start(bf16[352,128]{1,0:T(8,128)(2,1)S(1)} %get-tuple-element.60), channel_id=1, source_target_pairs={{0,8},{4,12},{8,0},{12,4},{1,9},{5,13},{9,1},{13,5},{2,10},{6,14},... | collective-permute-start | bytes 270344 | tf_op jit(solution)/shard_map/ppermute | solution.py:465
  39.8 4.3 %collective-permute-start.14 = (bf16[352,128]{1,0:T(8,128)(2,1)S(1)}, bf16[352,128]{1,0:T(8,128)(2,1)S(1)}, u32[]{:S(2)}, u32[]{:S(2)}) collective-permute-start(bf16[352,128]{1,0:T(8,128)(2,1)S(1)} %get-tuple-element.61), channel_id=1, source_target_pairs={{0,12},{4,0},{8,4},{12,8},{1,13},{5,1},{9,5},{13,9},{2,14},{6,2},{... | collective-permute-start | bytes 270344 | tf_op jit(solution)/shard_map/ppermute | solution.py:465

commit v5 on v4

--- a/solution.py
+++ b/solution.py
@@ -33,10 +33,7 @@
     return lax.dot_general(x, y, dims, preferred_element_type=F32)
 
 
-def prepare_kernel(
-    i_n, j_n, a_hbm, b_hbm, w_hbm, g_hbm, y_ref, y2_ref, wt_ref, bias_ref, a_ref, b_ref, g_ref,
-    w_ref, g32, gt, w32, we, sems,
-):
+def load_kernel(a_hbm, b_hbm, w_hbm, g_hbm, we_ref, wt_ref, a_ref, b_ref, w_ref, g_ref, w32, sems):
     depth = PROJECTED_DEPTH
     copies = [
         pltpu.make_async_copy(source, target, sems.at[n])
@@ -50,74 +47,111 @@
     w32[...] = w_ref[...].astype(F32)
     for e in range(depth):
         block = w32[pl.ds(e, depth, stride=depth), :]
-        we[e * depth : (e + 1) * depth, :] = block.astype(BF16)
-    wt_ref[...] = we[...].astype(F32).T.astype(BF16)
-    copies[1].wait()
+        we_ref[e * depth : (e + 1) * depth, :] = block.astype(BF16)
+    wt_ref[...] = we_ref[...].astype(F32).T.astype(BF16)
+    for copy in copies[1:]:
+        copy.wait()
+
+
+def in_vmem():
+    return pl.BlockSpec(memory_space=pltpu.VMEM)
+
+
+def load(a, b, w, g):
+    shapes = [
+        jax.ShapeDtypeStruct(w.shape, BF16),
+        jax.ShapeDtypeStruct(w.shape[::-1], BF16),
+        *[jax.ShapeDtypeStruct(x.shape, BF16) for x in (a, b, w, g)],
+    ]
+    return pl.pallas_call(
+        load_kernel,
+        in_specs=[pl.BlockSpec(memory_space=pltpu.HBM)] * 4,
+        out_specs=[in_vmem()] * len(shapes),
+        out_shape=shapes,
+        scratch_shapes=[pltpu.VMEM(w.shape, F32), pltpu.SemaphoreType.DMA((4,))],
+        compiler_params=params(),
+        cost_estimate=pl.CostEstimate(
+            flops=1000 * w.size, bytes_accessed=16 * w.size, transcendentals=0
+        ),
+    )(*[pltpu.with_memory_space_constraint(x, pltpu.HBM) for x in (a, b, w, g)])
+
+
+def stack_kernel(*refs):
+    half = len(refs) * 2 // 3
+    for n, out in enumerate(refs[half:]):
+        first, second = refs[2 * n], refs[2 * n + 1]
+        rows = first.shape[0]
+        both = jnp.concatenate([first[...].astype(F32), second[...].astype(F32)], axis=0)
+        out[...] = both.astype(BF16)
+
+
+def stack(*pairs):
+    shapes = [
+        jax.ShapeDtypeStruct((2 * first.shape[0], first.shape[1]), BF16) for first, _ in pairs
+    ]
+    operands = [x for pair in pairs for x in pair]
+    return pl.pallas_call(
+        stack_kernel,
+        in_specs=[in_vmem()] * len(operands),
+        out_specs=[in_vmem()] * len(shapes),
+        out_shape=shapes,
+        compiler_params=params(),
+    )(*operands)
+
+
+def prepare_kernel(i_n, j_n, we_ref, g_ref, y_ref, gt_ref, bias_ref, g32):
     g32[...] = g_ref[...].astype(F32)
     total = jnp.sum(g32[...], axis=0, keepdims=True)
     high = total.astype(BF16).astype(F32)
     row = lax.broadcasted_iota(jnp.int32, (BIAS_ROWS, PAIR_FEATURES), 0)
     bias_ref[...] = jnp.where(row == 0, high, jnp.where(row == 1, total - high, 0.0)).astype(BF16)
-    for j in range(j_n):
-        gt[j * i_n : (j + 1) * i_n, :] = g32[pl.ds(j, i_n, stride=j_n), :].astype(BF16)
-
     size = y_ref.shape[0] // STEPS
 
     @pl.loop(0, STEPS)
     def _(t):
         rows = pl.ds(pl.multiple_of(t * size, size), size)
-        y_ref[rows, :] = dot(we[rows, :], g_ref[...], ROWS_BY_ROWS).astype(BF16)
-        y2_ref[rows, :] = dot(w_ref[rows, :], gt[...], ROWS_BY_ROWS).astype(BF16)
-
-    copies[2].wait()
-    copies[3].wait()
-
-
-def in_vmem():
-    return pl.BlockSpec(memory_space=pltpu.VMEM)
-
-
-def prepare(a, b, w, g, i_n, j_n):
+        y_ref[rows, :] = dot(we_ref[rows, :], g_ref[...], ROWS_BY_ROWS).astype(BF16)
+
+
+    for j in range(j_n):
+        gt_ref[j * i_n : (j + 1) * i_n, :] = g32[pl.ds(j, i_n, stride=j_n), :].astype(BF16)
+
+
+def prepare(we, g, i_n, j_n):
     pairs = i_n * j_n
-    channels = w.shape[0]
+    channels = we.shape[0]
     shapes = [
         jax.ShapeDtypeStruct((channels, pairs), BF16),
-        jax.ShapeDtypeStruct((channels, pairs), BF16),
-        jax.ShapeDtypeStruct((PAIR_FEATURES, channels), BF16),
+        jax.ShapeDtypeStruct(g.shape, BF16),
         jax.ShapeDtypeStruct((BIAS_ROWS, PAIR_FEATURES), BF16),
-        jax.ShapeDtypeStruct(a.shape, BF16),
-        jax.ShapeDtypeStruct(b.shape, BF16),
-        jax.ShapeDtypeStruct(g.shape, BF16),
     ]
     return pl.pallas_call(
         functools.partial(prepare_kernel, i_n, j_n),
-        in_specs=[pl.BlockSpec(memory_space=pltpu.HBM)] * 4,
+        in_specs=[in_vmem()] * 2,
         out_specs=[in_vmem()] * len(shapes),
         out_shape=shapes,
-        scratch_shapes=[
-            pltpu.VMEM(w.shape, BF16),
-            pltpu.VMEM(g.shape, F32),
-            pltpu.VMEM(g.shape, BF16),
-            pltpu.VMEM(w.shape, F32),
-            pltpu.VMEM(w.shape, BF16),
-            pltpu.SemaphoreType.DMA((4,)),
-        ],
-        compiler_params=params(32),
+        scratch_shapes=[pltpu.VMEM(g.shape, F32)],
+        compiler_params=params(16),
         cost_estimate=pl.CostEstimate(
-            flops=4 * pairs * channels * PAIR_FEATURES,
+            flops=2 * pairs * channels * PAIR_FEATURES,
             bytes_accessed=4 * pairs * channels,
             transcendentals=0,
         ),
-    )(*[pltpu.with_memory_space_constraint(x, pltpu.HBM) for x in (a, b, w, g)])
+    )(we, g)
 
 
 def join(pieces, axis, held):
     count = len(pieces)
-    depth = pieces[0].shape[0]
+    depth = pieces[0].shape[0] // 2
     me = lax.axis_index(axis)
+    odd = lax.rem(me, 2)
+    home = lax.div(me, 2)
     for p, piece in enumerate(pieces):
-        start = pl.multiple_of(lax.rem(me - p + count, count) * depth, depth)
-        held[pl.ds(start, depth), :] = piece[...].astype(F32)
+        start = lax.rem(home - p + count, count) * 2 * depth
+        both = piece[...].astype(F32)
+        for n in range(2):
+            place = start + (1 - odd if n else odd) * depth
+            held[pl.ds(pl.multiple_of(place, depth), depth), :] = both[n * depth : (n + 1) * depth]
 
 
 def repeat_matrix(sequences):
@@ -144,10 +178,10 @@
 
 def fill_diagonal(wide, diagonal, slot, channel, positions, sequences):
     for l in range(wide.shape[0]):
-        block = wide[l, pl.ds(channel, positions, stride=PROJECTED_DEPTH), :]
+        block = wide[l, pl.ds(channel, positions, stride=PROJECTED_DEPTH), :].astype(BF16)
         for m, mask in tiles_of(sequences, l):
             diagonal[slot, m * positions : (m + 1) * positions, l * LANES : (l + 1) * LANES] = (
-                jnp.where(mask, block, 0.0).astype(BF16)
+                block * mask.astype(F32).astype(BF16)
             )
 
 
@@ -159,11 +193,11 @@
 
 def outer_kernel(i_n, j_n, row_n, col_n, *refs):
     depth = PROJECTED_DEPTH
-    a_pieces, refs = refs[:col_n], refs[col_n:]
-    b_pieces, refs = refs[:row_n], refs[row_n:]
-    (g_ref, bias_ref, x_ref), refs = refs[:3], refs[3:]
+    a_pieces, refs = refs[: col_n // 2], refs[col_n // 2 :]
+    b_pieces, refs = refs[: row_n // 2], refs[row_n // 2 :]
+    (g_ref, bias_ref, x_ref, a_wide, b_wide), refs = refs[:5], refs[5:]
     messages, refs = refs[:row_n], refs[row_n:]
-    a_held, b_held, wide, left, diagonal, total, ordered = refs
+    a_held, b_held, left, diagonal, total, ordered = refs
     sequences = a_held.shape[0]
     groups = i_n // GROUP
     per_step = depth // STEPS
@@ -171,22 +205,22 @@
 
     join(a_pieces, "col", a_held)
     join(b_pieces, "row", b_held)
-    spread(a_held, wide)
-    for l in range(wide.shape[0]):
+    spread(a_held, a_wide)
+    for l in range(a_wide.shape[0]):
         members = tiles_of(sequences, l)
         for k in range(groups):
             block = jnp.zeros((depth, LANES), F32)
             for m, mask in members:
                 start = (k * GROUP + m) * depth
-                block = jnp.where(mask, wide[l, start : start + depth, :], block)
+                block = jnp.where(mask, a_wide[l, start : start + depth, :], block)
             left[k * depth : (k + 1) * depth, l * LANES : (l + 1) * LANES] = block.astype(BF16)
-    spread(b_held, wide)
+    spread(b_held, b_wide)
     diagonal[...] = jnp.zeros(diagonal.shape, BF16)
 
     @pl.loop(0, STEPS)
     def _(t):
         for e in range(per_step):
-            fill_diagonal(wide, diagonal, e, t * per_step + e, j_n, sequences)
+            fill_diagonal(b_wide, diagonal, e, t * per_step + e, j_n, sequences)
         size = per_step * depth
         rows = pl.ds(pl.multiple_of(t * size, size), size)
         x_part = x_ref.at[rows]
@@ -211,7 +245,7 @@
 
 
 def outer(a_pieces, b_pieces, g, bias_rows, i_n, j_n, sequences):
-    row_n, col_n = len(b_pieces), len(a_pieces)
+    row_n, col_n = 2 * len(b_pieces), 2 * len(a_pieces)
     depth = PROJECTED_DEPTH
     channels = depth * depth
     pairs = i_n * j_n
@@ -219,6 +253,7 @@
     tiles = GROUP * sequences // LANES
     operands = [*a_pieces, *b_pieces, g, bias_rows]
     shapes = [jax.ShapeDtypeStruct((channels, pairs), BF16)]
+    shapes += [jax.ShapeDtypeStruct((tiles, n * depth, LANES), F32) for n in (i_n, j_n)]
     shapes += parts_shapes(row_n, share + BIAS_ROWS)
     results = pl.pallas_call(
         functools.partial(outer_kernel, i_n, j_n, row_n, col_n),
@@ -228,7 +263,6 @@
         scratch_shapes=[
             pltpu.VMEM((sequences, i_n * depth), F32),
             pltpu.VMEM((sequences, j_n * depth), F32),
-            pltpu.VMEM((tiles, i_n * depth, LANES), F32),
             pltpu.VMEM((i_n // GROUP * depth, GROUP * sequences), BF16),
             pltpu.VMEM((depth // STEPS, GROUP * j_n, GROUP * sequences), BF16),
             pltpu.VMEM((channels, PAIR_FEATURES), F32),
@@ -241,20 +275,18 @@
             transcendentals=0,
         ),
     )(*operands)
-    return results[0], results[1:]
-
-
-def gradient_kernel(axis, out_axis, count, parts, positions, others, *refs):
+    return *results[:3], results[3:]
+
+
+def gradient_kernel(axis, positions, others, sequences, *refs):
     depth = PROJECTED_DEPTH
-    pieces, source, refs = refs[:count], refs[count], refs[count + 1 :]
-    outs, refs = refs[:parts], refs[parts:]
-    held, wide, diagonal, result, grown, grad = refs
-    sequences = held.shape[0]
+    wide, refs = refs[0], refs[1:]
+    parts = lax.axis_size(axis)
+    diagonal, result, grown, grad = refs[-4:]
+    sources, outs = refs[: -4 - parts], refs[-4 - parts : -4]
     per_step = depth // STEPS
     span = GROUP * others
 
-    join(pieces, axis, held)
-    spread(held, wide)
     diagonal[...] = jnp.zeros(diagonal.shape, BF16)
     result[...] = jnp.zeros(result.shape, F32)
 
@@ -263,9 +295,13 @@
         for n in range(per_step):
             fill_diagonal(wide, diagonal, n, t * per_step + n, others, sequences)
         size = per_step * depth
-        part = source.at[pl.ds(pl.multiple_of(t * size, size), size)]
+        rows = pl.ds(pl.multiple_of(t * size, size), size)
+        if len(sources) == 1:
+            part = sources[0].at[rows]
+        else:
+            part = dot(sources[0][rows, :], sources[1][...], ROWS_BY_ROWS).astype(BF16)
         for n in range(0, per_step, 2):
-            rows = [
+            blocks = [
                 jnp.concatenate(
                     [
                         part[m * depth : (m + 1) * depth, k * span : (k + 1) * span]
@@ -276,7 +312,7 @@
                 for k in range(positions // GROUP)
             ]
             result[...] += dot(
-                jnp.concatenate(rows, axis=0),
+                jnp.concatenate(blocks, axis=0),
                 diagonal[n : n + 2].reshape(2 * span, diagonal.shape[2]),
             )
 
@@ -288,13 +324,13 @@
             for m in range(GROUP):
                 start = (k * GROUP + m) * depth
                 grown[start : start + depth, l * LANES : (l + 1) * LANES] = (
-                    jnp.where(members[m], block.astype(F32), 0.0).astype(BF16)
+                    block * members[m].astype(F32).astype(BF16)
                     if m in members
                     else jnp.zeros((depth, LANES), BF16)
                 )
     grad[...] = dot(repeat_matrix(sequences), grown[...], ROWS_BY_ROWS)
     share = sequences // parts
-    me = lax.axis_index(out_axis)
+    me = lax.axis_index(axis)
     for p, out in enumerate(outs):
         mine = grad[pl.ds(pl.multiple_of(lax.rem(me + p, parts) * share, share), share), :]
         out[...] = jnp.concatenate(
@@ -302,21 +338,17 @@
         ).astype(out.dtype)
 
 
-def gradient(pieces, axis, out_axis, source, parts, positions, others, sequences):
+def gradient(wide, sources, axis, positions, others, sequences):
     depth = PROJECTED_DEPTH
-    channels, pairs = source.shape
-    tiles = GROUP * sequences // LANES
+    channels, pairs = depth * depth, positions * others
+    parts = lax.axis_size(axis)
     rows = sequences // parts * positions * depth // LANES
     return pl.pallas_call(
-        functools.partial(
-            gradient_kernel, axis, out_axis, len(pieces), parts, positions, others
-        ),
-        in_specs=[in_vmem()] * (len(pieces) + 1),
+        functools.partial(gradient_kernel, axis, positions, others, sequences),
+        in_specs=[in_vmem()] * (len(sources) + 1),
         out_specs=[in_vmem()] * parts,
         out_shape=parts_shapes(parts, rows),
         scratch_shapes=[
-            pltpu.VMEM((sequences, others * depth), F32),
-            pltpu.VMEM((tiles, others * depth, LANES), F32),
             pltpu.VMEM((depth // STEPS, GROUP * others, GROUP * sequences), BF16),
             pltpu.VMEM((positions // GROUP * depth, GROUP * sequences), F32),
             pltpu.VMEM((positions * depth, GROUP * sequences), BF16),
@@ -324,11 +356,11 @@
         ],
         compiler_params=params(sequences),
         cost_estimate=pl.CostEstimate(
-            flops=2 * pairs * channels * PAIR_FEATURES,
+            flops=2 * len(sources) * pairs * channels * PAIR_FEATURES,
             bytes_accessed=2 * pairs * channels,
             transcendentals=0,
         ),
-    )(*pieces, source)
+    )(wide, *sources)
 
 
 def pair_kernel(sequences, x_ref, wt_ref, bias_ref, out_ref):
@@ -465,8 +497,12 @@
     return lax.ppermute(x, axis, [(n, (n + distance) % count) for n in range(count)])
 
 
-def gather(x, axis):
-    return [shift(x, axis, d) for d in range(1, lax.axis_size(axis))]
+def neighbour(x, axis):
+    return lax.ppermute(x, axis, [(n, n ^ 1) for n in range(lax.axis_size(axis))])
+
+
+def shift_pairs(x, axis):
+    return [x] + [shift(x, axis, d) for d in range(2, lax.axis_size(axis), 2)]
 
 
 def exchange(parts, axis):
@@ -477,29 +513,31 @@
     first_homolog_features, second_homolog_features, final_projection_matrix, output_bias, cotangent
 ):
     i_n, j_n, _ = cotangent.shape
-    row_n, col_n = lax.axis_size("row"), lax.axis_size("col")
+    row_n = lax.axis_size("row")
     sequences = second_homolog_features.shape[0] * row_n
     channels = final_projection_matrix.shape[0]
     res_total = i_n * row_n
-    a_pieces = gather(first_homolog_features, "col")
-    b_pieces = gather(second_homolog_features, "row")
-    y, y2, wt, bias_rows, a_own, b_own, g = prepare(
+    a_near = neighbour(first_homolog_features, "col")
+    b_near = neighbour(second_homolog_features, "row")
+    we, wt, a, b, w, g = load(
         first_homolog_features,
         second_homolog_features,
         final_projection_matrix,
         cotangent.reshape(i_n * j_n, PAIR_FEATURES),
-        i_n,
-        j_n,
     )
-    a_pieces = [a_own] + a_pieces
-    b_pieces = [b_own] + b_pieces
-
-    x, (row_own, *messages) = outer(a_pieces, b_pieces, g, bias_rows, i_n, j_n, sequences)
+    a_pair, b_pair = stack((a, a_near), (b, b_near))
+    a_pieces = shift_pairs(a_pair, "col")
+    b_pieces = shift_pairs(b_pair, "row")
+    y, gt, bias_rows = prepare(we, g, i_n, j_n)
+
+    x, a_wide, b_wide, (row_own, *messages) = outer(
+        a_pieces, b_pieces, g, bias_rows, i_n, j_n, sequences
+    )
     row_parts = [row_own] + exchange(messages, "row")
-    left_own, *left_grads = gradient(b_pieces, "row", "col", y, col_n, i_n, j_n, sequences)
+    left_own, *left_grads = gradient(b_wide, [y], "col", i_n, j_n, sequences)
     messages = row_sum(row_parts, left_grads)
     col_parts = exchange(messages, "col")
-    right_own, *right_grads = gradient(a_pieces, "col", "row", y2, row_n, j_n, i_n, sequences)
+    right_own, *right_grads = gradient(a_wide, [w, gt], "row", j_n, i_n, sequences)
     messages, piece, left_grad, bias_grad = column_sum(
         col_parts,
         left_own,

time: 45.6 us -> 43.8 us (0.961)
  the two profiles are of different devices: /device:TPU:0 before, /device:TPU:1 now
where the time goes in v5:
time: 43.8 us; the launch traced here: 43.6 us
  Pallas kernels  23.7 us (54%)
  starting transfers between devices  16.7 us (38%)
  waiting for transfers between devices  2.49 us (6%)
  between operations  0.76 us (2%)
    ppermute x11, starting transfers between devices, shift(): lax.ppermute(x, axis, [(n, (n + distance) % count) for n in range(count)])  13.5 us
    pallas_call x2, Pallas kernels, gradient(): pl.pallas_call(functools.partial(gradient_kernel, axis, positions, others...  9.75 us
    pallas_call x1, Pallas kernels, outer(): pl.pallas_call(functools.partial(outer_kernel, i_n, j_n, row_n, col_n), i...  5.81 us
    ppermute x2, starting transfers between devices, neighbour(): lax.ppermute(x, axis, [(n, n ^ 1) for n in range(lax.axis_size(axis))])  3.15 us
    pallas_call x1, Pallas kernels, prepare(): pl.pallas_call(functools.partial(prepare_kernel, i_n, j_n), in_specs=[in_...  2.61 us
    pallas_call x1, Pallas kernels, pair(): pl.pallas_call(functools.partial(pair_kernel, sequences), grid=(count,),...  2.56 us
    ppermute x11, waiting for transfers between devices, shift(): lax.ppermute(x, axis, [(n, (n + distance) % count) for n in range(count)])  2.48 us
    pallas_call x1, Pallas kernels, load(): pl.pallas_call(load_kernel, in_specs=[pl.BlockSpec(memory_space=pltpu.HBM...  1.39 us
  transfers between devices with their start and end apart: 13, of which 3 were waited for; matrix products, arithmetic and copies ran while one was open for 0% of the time, Pallas kernels for 37%

profile of v5, /device:TPU:1, one launch (start us, length us, event | category | flops | bytes accessed | tf_op | source)
XLA Modules:
  0.0 43.6 jit_solution(4403994466190773463)
XLA Ops:
  0.6 2.2 %collective-permute-start = (bf16[8,1536]{1,0:T(8,128)(2,1)}, bf16[8,1536]{1,0:T(8,128)(2,1)S(1)}, u32[]{:S(2)}, u32[]{:S(2)}) collective-permute-start(bf16[8,1536]{1,0:T(8,128)(2,1)} %a_hbm.1), channel_id=1, source_target_pairs={{0,1},{1,0},{2,3},{3,2},{4,5},{5,4},{6,7},{7,6},{8,9},{9,8},{10,11... | collective-permute-start | bytes 73736 | tf_op jit(solution)/shard_map/ppermute | solution.py:501
  2.8 1.0 %collective-permute-start.1 = (bf16[8,1536]{1,0:T(8,128)(2,1)}, bf16[8,1536]{1,0:T(8,128)(2,1)S(1)}, u32[]{:S(2)}, u32[]{:S(2)}) collective-permute-start(bf16[8,1536]{1,0:T(8,128)(2,1)} %b_hbm.1), channel_id=1, source_target_pairs={{0,4},{4,0},{8,12},{12,8},{1,5},{5,1},{9,13},{13,9},{2,6},{6,2},{1... | collective-permute-start | bytes 73736 | tf_op jit(solution)/shard_map/ppermute | solution.py:501
  3.8 1.4 %shard_map.92 = (bf16[1024,128]{1,0:T(8,128)(2,1)S(1)}, bf16[128,1024]{1,0:T(8,128)(2,1)S(1)}, bf16[8,1536]{1,0:T(8,128)(2,1)S(1)}, bf16[8,1536]{1,0:T(8,128)(2,...) custom-call(bf16[8,1536]{1,0:T(8,128)(2,1)} %a_hbm.1, bf16[8,1536]{1,0:T(8,128)(2,1)} %b_hbm.1, ...), custom_call_target="tpu_custom_call" | custom-call | flops 131072000 | bytes 2097152 | tf_op jit(solution)/shard_map/pallas_call | solution.py:66
  5.2 0.0 collective-permute-done.refs_1_
  5.2 0.0 collective-permute-done.1.refs_3_
  5.2 2.4 %collective-permute-start.2 = (bf16[16,1536]{1,0:T(8,128)(2,1)S(1)}, bf16[16,1536]{1,0:T(8,128)(2,1)S(1)}, u32[]{:S(2)}, u32[]{:S(2)}) collective-permute-start(bf16[16,1536]{1,0:T(8,128)(2,1)S(1)} %get-tuple-element.44.refs_0_), channel_id=1, source_target_pairs={{0,2},{1,3},{2,0},{3,1},{4,6},{5,7},{6,4},{7,5},{8,10},{9,11},{10,... | collective-permute-start | bytes 147464 | tf_op jit(solution)/shard_map/ppermute | solution.py:497
  7.6 1.2 %collective-permute-start.3 = (bf16[16,1536]{1,0:T(8,128)(2,1)S(1)}, bf16[16,1536]{1,0:T(8,128)(2,1)S(1)}, u32[]{:S(2)}, u32[]{:S(2)}) collective-permute-start(bf16[16,1536]{1,0:T(8,128)(2,1)S(1)} %get-tuple-element.45.refs_2_), channel_id=1, source_target_pairs={{0,8},{4,12},{8,0},{12,4},{1,9},{5,13},{9,1},{13,5},{2,10},{6,14},... | collective-permute-start | bytes 147464 | tf_op jit(solution)/shard_map/ppermute | solution.py:497
  8.8 2.6 %shard_map.94 = (bf16[1024,2304]{1,0:T(8,128)(2,1)S(1)}, bf16[2304,128]{1,0:T(8,128)(2,1)S(1)}, bf16[16,128]{1,0:T(8,128)(2,1)S(1)}) custom-call(bf16[1024,128]{1,0:T(8,128)(2,1)S(1)} %get-tuple-element.47.we_ref, bf16[2304,128]{1,0:T(8,128)(2,1)S(1)} %get-tuple-element.46.g_ref.refs_4_), custom_call_target="tpu_custom_call" | custom-call | flops 603979776 | bytes 9437184 | tf_op jit(solution)/shard_map/pallas_call | solution.py:128
  11.4 0.0 collective-permute-done.2.refs_1_
  11.4 0.0 collective-permute-done.3.refs_3_
  11.4 5.8 %shard_map.95 = (bf16[1024,2304]{1,0:T(8,128)(2,1)S(1)}, f32[2,1536,128]{2,1,0:T(8,128)S(1)}, f32[2,1536,128]{2,1,0:T(8,128)S(1)}, f32[272,128]{1,0:T(8,128)S(1)...) custom-call(bf16[16,1536]{1,0:T(8,128)(2,1)S(1)} %get-tuple-element.44.refs_0_, ...), custom_call_target="tpu_custom_call" | custom-call | flops 1207959552 | bytes 4718592 | tf_op jit(solution)/shard_map/pallas_call | solution.py:258
  17.2 2.7 %collective-permute-start.4 = (bf16[272,128]{1,0:T(8,128)(2,1)S(1)}, bf16[272,128]{1,0:T(8,128)(2,1)S(1)}, u32[]{:S(2)}, u32[]{:S(2)}) collective-permute-start(bf16[272,128]{1,0:T(8,128)(2,1)S(1)} %get-tuple-element.52), channel_id=1, source_target_pairs={{0,4},{4,8},{8,12},{12,0},{1,5},{5,9},{9,13},{13,1},{2,6},{6,10},{... | collective-permute-start | bytes 208904 | tf_op jit(solution)/shard_map/ppermute | solution.py:497
  19.9 0.3 collective-permute-start.5
  20.2 0.2 collective-permute-start.6
  20.4 3.5 %shard_map.97 = (f32[96,128]{1,0:T(8,128)S(1)}, bf16[96,128]{1,0:T(8,128)(2,1)S(1)}, bf16[96,128]{1,0:T(8,128)(2,1)S(1)}, bf16[96,128]{1,0:T(8,128)(2,1)S(1)}) custom-call(f32[2,1536,128]{2,1,0:T(8,128)S(1)} %get-tuple-element.55.refs_0_, bf16[1024,2304]{1,0:T(8,128)(2,1)S(1)} %get-tuple-element.56.refs_1_), custom_call_target="tpu_custom_call" | custom-call | flops 603979776 | bytes 4718592 | tf_op jit(solution)/shard_map/pallas_call | solution.py:346
  23.9 0.0 collective-permute-done.4.refs_1_
  24.0 0.0 collective-permute-done.5.refs_2_
  24.0 0.2 collective-permute-done.6.refs_3_
  24.2 0.7 %collective-permute-start.8 = (bf16[368,128]{1,0:T(8,128)(2,1)S(1)}, bf16[368,128]{1,0:T(8,128)(2,1)S(1)}, u32[]{:S(2)}, u32[]{:S(2)}) collective-permute-start(bf16[368,128]{1,0:T(8,128)(2,1)S(1)} %get-tuple-element.61), channel_id=1, source_target_pairs={{0,2},{1,3},{2,0},{3,1},{4,6},{5,7},{6,4},{7,5},{8,10},{9,11},{10,... | collective-permute-start | bytes 282632 | tf_op jit(solution)/shard_map/ppermute | solution.py:497
  24.9 2.7 %collective-permute-start.9 = (bf16[368,128]{1,0:T(8,128)(2,1)S(1)}, bf16[368,128]{1,0:T(8,128)(2,1)S(1)}, u32[]{:S(2)}, u32[]{:S(2)}) collective-permute-start(bf16[368,128]{1,0:T(8,128)(2,1)S(1)} %get-tuple-element.62), channel_id=1, source_target_pairs={{0,3},{1,0},{2,1},{3,2},{4,7},{5,4},{6,5},{7,6},{8,11},{9,8},{10,9... | collective-permute-start | bytes 282632 | tf_op jit(solution)/shard_map/ppermute | solution.py:497
  27.7 0.0 collective-permute-start.7
  27.7 6.2 %shard_map.99 = (f32[96,128]{1,0:T(8,128)S(1)}, bf16[96,128]{1,0:T(8,128)(2,1)S(1)}, bf16[96,128]{1,0:T(8,128)(2,1)S(1)}, bf16[96,128]{1,0:T(8,128)(2,1)S(1)}) custom-call(f32[2,1536,128]{2,1,0:T(8,128)S(1)} %get-tuple-element.64.refs_0_, bf16[1024,128]{1,0:T(8,128)(2,1)S(1)} %get-tuple-element.65.refs_1_, bf16[2304,128]{1,0:T(8,128)(2,1)S(1)} %get-tuple-element.66.refs_2_), custom_call_target="tpu_custom_call" | custom-call | flops 1207959552 | bytes 4718592 | tf_op jit(solution)/shard_map/pallas_call | solution.py:346
  33.9 0.0 collective-permute-done.7.refs_0_
  33.9 0.7 %shard_map.100 = (bf16[352,128]{1,0:T(8,128)(2,1)S(1)}, bf16[352,128]{1,0:T(8,128)(2,1)S(1)}, bf16[352,128]{1,0:T(8,128)(2,1)S(1)}, bf16[256,128]{1,0:T(8,128)(2...) custom-call(bf16[368,128]{1,0:T(8,128)(2,1)S(1)} %collective-permute-done.7.refs_0_, ...), custom_call_target="tpu_custom_call" | custom-call | tf_op jit(solution)/shard_map/pallas_call | solution.py:456
  34.6 2.6 %collective-permute-start.10 = (bf16[352,128]{1,0:T(8,128)(2,1)S(1)}, bf16[352,128]{1,0:T(8,128)(2,1)S(1)}, u32[]{:S(2)}, u32[]{:S(2)}) collective-permute-start(bf16[352,128]{1,0:T(8,128)(2,1)S(1)} %get-tuple-element.71), channel_id=1, source_target_pairs={{0,4},{4,8},{8,12},{12,0},{1,5},{5,9},{9,13},{13,1},{2,6},{6,10},{... | collective-permute-start | bytes 270344 | tf_op jit(solution)/shard_map/ppermute | solution.py:497
  37.3 0.7 %collective-permute-start.11 = (bf16[352,128]{1,0:T(8,128)(2,1)S(1)}, bf16[352,128]{1,0:T(8,128)(2,1)S(1)}, u32[]{:S(2)}, u32[]{:S(2)}) collective-permute-start(bf16[352,128]{1,0:T(8,128)(2,1)S(1)} %get-tuple-element.72), channel_id=1, source_target_pairs={{0,8},{4,12},{8,0},{12,4},{1,9},{5,13},{9,1},{13,5},{2,10},{6,14},... | collective-permute-start | bytes 270344 | tf_op jit(solution)/shard_map/ppermute | solution.py:497
  38.0 0.0 collective-permute-start.12
  38.0 2.6 %shard_map.96 = bf16[2304,128]{1,0:T(8,128)(2,1)} custom-call(bf16[1024,2304]{1,0:T(8,128)(2,1)S(1)} %get-tuple-element.49.x_ref, bf16[128,1024]{1,0:T(8,128)(2,1)S(1)} %get-tuple-element.50.wt_ref, f32[1,128]{1,0:T(1,128)S(1)} %bitcast.4), custom_call_target="tpu_custom_call" | custom-call | flops 1207959552 | bytes 4718592 | tf_op jit(solution)/shard_map/pallas_call | solution.py:375
  40.5 0.0 collective-permute-done.10.refs_0_
  40.5 1.7 %collective-permute-done.11.refs_1_ = bf16[352,128]{1,0:T(8,128)(2,1)S(1)} collective-permute-done((bf16[352,128]{1,0:T(8,128)(2,1)S(1)}, bf16[352,128]{1,0:T(8,128)(2,1)S(1)}, u32[]{:S(2)}, u32[]{:S(2)}) %collective-permute-start.11) | collective-permute-done | bytes 90144 | tf_op jit(solution)/shard_map/ppermute | solution.py:497
  42.2 0.6 %collective-permute-done.12.refs_2_ = bf16[352,128]{1,0:T(8,128)(2,1)S(1)} collective-permute-done((bf16[352,128]{1,0:T(8,128)(2,1)S(1)}, bf16[352,128]{1,0:T(8,128)(2,1)S(1)}, u32[]{:S(2)}, u32[]{:S(2)}) %collective-permute-start.12) | collective-permute-done | bytes 90144 | tf_op jit(solution)/shard_map/ppermute | solution.py:497
  42.8 0.8 %shard_map.101 = (f32[1024,128]{1,0:T(8,128)}, f32[8,1536]{1,0:T(8,128)}) custom-call(bf16[352,128]{1,0:T(8,128)(2,1)S(1)} %collective-permute-done.10.refs_0_, bf16[352,128]{1,0:T(8,128)(2,1)S(1)} %collective-permute-done.11.refs_1_, bf16[352,128]{1,0:T(8,128)(2,1)S(1)} %collective-permute-done.12.refs_2_, bf16[256,128]{1,0:T(8,128)(2,1)S(1)} %get-tuple-element.74.refs_3_, ...), custom_call_target="tpu_custom_call" | custom-call | tf_op jit(solution)/shard_map/pallas_call | solution.py:483
  (6 shorter events, 0.1 us)
Async XLA Ops:
  0.6 4.5 %collective-permute-start = (bf16[8,1536]{1,0:T(8,128)(2,1)}, bf16[8,1536]{1,0:T(8,128)(2,1)S(1)}, u32[]{:S(2)}, u32[]{:S(2)}) collective-permute-start(bf16[8,1536]{1,0:T(8,128)(2,1)} %a_hbm.1), channel_id=1, source_target_pairs={{0,1},{1,0},{2,3},{3,2},{4,5},{5,4},{6,7},{7,6},{8,9},{9,8},{10,11... | collective-permute-start | bytes 73736 | tf_op jit(solution)/shard_map/ppermute | solution.py:501
  2.8 2.4 %collective-permute-start.1 = (bf16[8,1536]{1,0:T(8,128)(2,1)}, bf16[8,1536]{1,0:T(8,128)(2,1)S(1)}, u32[]{:S(2)}, u32[]{:S(2)}) collective-permute-start(bf16[8,1536]{1,0:T(8,128)(2,1)} %b_hbm.1), channel_id=1, source_target_pairs={{0,4},{4,0},{8,12},{12,8},{1,5},{5,1},{9,13},{13,9},{2,6},{6,2},{1... | collective-permute-start | bytes 73736 | tf_op jit(solution)/shard_map/ppermute | solution.py:501
  5.2 6.2 %collective-permute-start.2 = (bf16[16,1536]{1,0:T(8,128)(2,1)S(1)}, bf16[16,1536]{1,0:T(8,128)(2,1)S(1)}, u32[]{:S(2)}, u32[]{:S(2)}) collective-permute-start(bf16[16,1536]{1,0:T(8,128)(2,1)S(1)} %get-tuple-element.44.refs_0_), channel_id=1, source_target_pairs={{0,2},{1,3},{2,0},{3,1},{4,6},{5,7},{6,4},{7,5},{8,10},{9,11},{10,... | collective-permute-start | bytes 147464 | tf_op jit(solution)/shard_map/ppermute | solution.py:497
  7.6 3.8 %collective-permute-start.3 = (bf16[16,1536]{1,0:T(8,128)(2,1)S(1)}, bf16[16,1536]{1,0:T(8,128)(2,1)S(1)}, u32[]{:S(2)}, u32[]{:S(2)}) collective-permute-start(bf16[16,1536]{1,0:T(8,128)(2,1)S(1)} %get-tuple-element.45.refs_2_), channel_id=1, source_target_pairs={{0,8},{4,12},{8,0},{12,4},{1,9},{5,13},{9,1},{13,5},{2,10},{6,14},... | collective-permute-start | bytes 147464 | tf_op jit(solution)/shard_map/ppermute | solution.py:497
  17.2 6.7 %collective-permute-start.4 = (bf16[272,128]{1,0:T(8,128)(2,1)S(1)}, bf16[272,128]{1,0:T(8,128)(2,1)S(1)}, u32[]{:S(2)}, u32[]{:S(2)}) collective-permute-start(bf16[272,128]{1,0:T(8,128)(2,1)S(1)} %get-tuple-element.52), channel_id=1, source_target_pairs={{0,4},{4,8},{8,12},{12,0},{1,5},{5,9},{9,13},{13,1},{2,6},{6,10},{... | collective-permute-start | bytes 208904 | tf_op jit(solution)/shard_map/ppermute | solution.py:497
  19.9 4.0 %collective-permute-start.5 = (bf16[272,128]{1,0:T(8,128)(2,1)S(1)}, bf16[272,128]{1,0:T(8,128)(2,1)S(1)}, u32[]{:S(2)}, u32[]{:S(2)}) collective-permute-start(bf16[272,128]{1,0:T(8,128)(2,1)S(1)} %get-tuple-element.53), channel_id=1, source_target_pairs={{0,8},{4,12},{8,0},{12,4},{1,9},{5,13},{9,1},{13,5},{2,10},{6,14},... | collective-permute-start | bytes 208904 | tf_op jit(solution)/shard_map/ppermute | solution.py:497
  20.2 3.9 %collective-permute-start.6 = (bf16[272,128]{1,0:T(8,128)(2,1)S(1)}, bf16[272,128]{1,0:T(8,128)(2,1)S(1)}, u32[]{:S(2)}, u32[]{:S(2)}) collective-permute-start(bf16[272,128]{1,0:T(8,128)(2,1)S(1)} %get-tuple-element.54), channel_id=1, source_target_pairs={{0,12},{4,0},{8,4},{12,8},{1,13},{5,1},{9,5},{13,9},{2,14},{6,2},{... | collective-permute-start | bytes 208904 | tf_op jit(solution)/shard_map/ppermute | solution.py:497
  20.4 17.6 %copy-start = (f32[128]{0:T(128)S(1)}, f32[128]{0:T(128)}, u32[]{:S(2)}) copy-start(f32[128]{0:T(128)} %param.8) | copy-start | bytes 1540
  24.2 9.7 %collective-permute-start.8 = (bf16[368,128]{1,0:T(8,128)(2,1)S(1)}, bf16[368,128]{1,0:T(8,128)(2,1)S(1)}, u32[]{:S(2)}, u32[]{:S(2)}) collective-permute-start(bf16[368,128]{1,0:T(8,128)(2,1)S(1)} %get-tuple-element.61), channel_id=1, source_target_pairs={{0,2},{1,3},{2,0},{3,1},{4,6},{5,7},{6,4},{7,5},{8,10},{9,11},{10,... | collective-permute-start | bytes 282632 | tf_op jit(solution)/shard_map/ppermute | solution.py:497
  24.9 9.0 %collective-permute-start.9 = (bf16[368,128]{1,0:T(8,128)(2,1)S(1)}, bf16[368,128]{1,0:T(8,128)(2,1)S(1)}, u32[]{:S(2)}, u32[]{:S(2)}) collective-permute-start(bf16[368,128]{1,0:T(8,128)(2,1)S(1)} %get-tuple-element.62), channel_id=1, source_target_pairs={{0,3},{1,0},{2,1},{3,2},{4,7},{5,4},{6,5},{7,6},{8,11},{9,8},{10,9... | collective-permute-start | bytes 282632 | tf_op jit(solution)/shard_map/ppermute | solution.py:497
  27.7 6.3 %collective-permute-start.7 = (bf16[368,128]{1,0:T(8,128)(2,1)S(1)}, bf16[368,128]{1,0:T(8,128)(2,1)S(1)}, u32[]{:S(2)}, u32[]{:S(2)}) collective-permute-start(bf16[368,128]{1,0:T(8,128)(2,1)S(1)} %get-tuple-element.60.refs_4_), channel_id=1, source_target_pairs={{0,1},{1,2},{2,3},{3,0},{4,5},{5,6},{6,7},{7,4},{8,9},{9,10},{10,1... | collective-permute-start | bytes 282632 | tf_op jit(solution)/shard_map/ppermute | solution.py:497
  34.6 5.9 %collective-permute-start.10 = (bf16[352,128]{1,0:T(8,128)(2,1)S(1)}, bf16[352,128]{1,0:T(8,128)(2,1)S(1)}, u32[]{:S(2)}, u32[]{:S(2)}) collective-permute-start(bf16[352,128]{1,0:T(8,128)(2,1)S(1)} %get-tuple-element.71), channel_id=1, source_target_pairs={{0,4},{4,8},{8,12},{12,0},{1,5},{5,9},{9,13},{13,1},{2,6},{6,10},{... | collective-permute-start | bytes 270344 | tf_op jit(solution)/shard_map/ppermute | solution.py:497
  37.3 4.9 %collective-permute-start.11 = (bf16[352,128]{1,0:T(8,128)(2,1)S(1)}, bf16[352,128]{1,0:T(8,128)(2,1)S(1)}, u32[]{:S(2)}, u32[]{:S(2)}) collective-permute-start(bf16[352,128]{1,0:T(8,128)(2,1)S(1)} %get-tuple-element.72), channel_id=1, source_target_pairs={{0,8},{4,12},{8,0},{12,4},{1,9},{5,13},{9,1},{13,5},{2,10},{6,14},... | collective-permute-start | bytes 270344 | tf_op jit(solution)/shard_map/ppermute | solution.py:497
  38.0 4.8 %collective-permute-start.12 = (bf16[352,128]{1,0:T(8,128)(2,1)S(1)}, bf16[352,128]{1,0:T(8,128)(2,1)S(1)}, u32[]{:S(2)}, u32[]{:S(2)}) collective-permute-start(bf16[352,128]{1,0:T(8,128)(2,1)S(1)} %get-tuple-element.73), channel_id=1, source_target_pairs={{0,12},{4,0},{8,4},{12,8},{1,13},{5,1},{9,5},{13,9},{2,14},{6,2},{... | collective-permute-start | bytes 270344 | tf_op jit(solution)/shard_map/ppermute | solution.py:497

commit v6 on v5

--- a/solution.py
+++ b/solution.py
@@ -11,6 +11,7 @@
 PAIR_FEATURES = 128
 GROUP = 8
 STEPS = 4
+CHUNKS = 2
 BIAS_ROWS = 16
 LANES = 128
 F32 = jnp.float32
@@ -200,7 +201,7 @@
     a_held, b_held, left, diagonal, total, ordered = refs
     sequences = a_held.shape[0]
     groups = i_n // GROUP
-    per_step = depth // STEPS
+    per_step = depth // CHUNKS
     span = GROUP * j_n
 
     join(a_pieces, "col", a_held)
@@ -217,7 +218,7 @@
     spread(b_held, b_wide)
     diagonal[...] = jnp.zeros(diagonal.shape, BF16)
 
-    @pl.loop(0, STEPS)
+    @pl.loop(0, CHUNKS)
     def _(t):
         for e in range(per_step):
             fill_diagonal(b_wide, diagonal, e, t * per_step + e, j_n, sequences)
@@ -264,7 +265,7 @@
             pltpu.VMEM((sequences, i_n * depth), F32),
             pltpu.VMEM((sequences, j_n * depth), F32),
             pltpu.VMEM((i_n // GROUP * depth, GROUP * sequences), BF16),
-            pltpu.VMEM((depth // STEPS, GROUP * j_n, GROUP * sequences), BF16),
+            pltpu.VMEM((depth // CHUNKS, GROUP * j_n, GROUP * sequences), BF16),
             pltpu.VMEM((channels, PAIR_FEATURES), F32),
             pltpu.VMEM((channels, PAIR_FEATURES), F32),
         ],
@@ -282,15 +283,15 @@
     depth = PROJECTED_DEPTH
     wide, refs = refs[0], refs[1:]
     parts = lax.axis_size(axis)
-    diagonal, result, grown, grad = refs[-4:]
-    sources, outs = refs[: -4 - parts], refs[-4 - parts : -4]
-    per_step = depth // STEPS
+    diagonal, result, grown, grad, product = refs[-5:]
+    sources, outs = refs[: -5 - parts], refs[-5 - parts : -5]
+    per_step = depth // CHUNKS
     span = GROUP * others
 
     diagonal[...] = jnp.zeros(diagonal.shape, BF16)
     result[...] = jnp.zeros(result.shape, F32)
 
-    @pl.loop(0, STEPS)
+    @pl.loop(0, CHUNKS)
     def _(t):
         for n in range(per_step):
             fill_diagonal(wide, diagonal, n, t * per_step + n, others, sequences)
@@ -299,7 +300,10 @@
         if len(sources) == 1:
             part = sources[0].at[rows]
         else:
-            part = dot(sources[0][rows, :], sources[1][...], ROWS_BY_ROWS).astype(BF16)
+            part = product
+            for n in range(0, size, size // 2):
+                block = sources[0][pl.ds(pl.multiple_of(t * size + n, size // 2), size // 2), :]
+                part[n : n + size // 2, :] = dot(block, sources[1][...], ROWS_BY_ROWS).astype(BF16)
         for n in range(0, per_step, 2):
             blocks = [
                 jnp.concatenate(
@@ -349,10 +353,11 @@
         out_specs=[in_vmem()] * parts,
         out_shape=parts_shapes(parts, rows),
         scratch_shapes=[
-            pltpu.VMEM((depth // STEPS, GROUP * others, GROUP * sequences), BF16),
+            pltpu.VMEM((depth // CHUNKS, GROUP * others, GROUP * sequences), BF16),
             pltpu.VMEM((positions // GROUP * depth, GROUP * sequences), F32),
             pltpu.VMEM((positions * depth, GROUP * sequences), BF16),
             pltpu.VMEM((sequences, positions * depth), F32),
+            pltpu.VMEM((channels // CHUNKS if len(sources) > 1 else 16, pairs), BF16),
         ],
         compiler_params=params(sequences),
         cost_estimate=pl.CostEstimate(

time: 43.8 us -> 43.1 us (0.984)
  the two profiles are of different devices: /device:TPU:1 before, /device:TPU:0 now
where the time goes in v6:
time: 43.1 us; the launch traced here: 42.4 us
  Pallas kernels  21.5 us (50%)
  starting transfers between devices  17.5 us (41%)
  waiting for transfers between devices  2.69 us (6%)
  between operations  0.74 us (2%)
    ppermute x11, starting transfers between devices, shift(): lax.ppermute(x, axis, [(n, (n + distance) % count) for n in range(count)])  14.4 us
    pallas_call x2, Pallas kernels, gradient(): pl.pallas_call(functools.partial(gradient_kernel, axis, positions, others...  7.99 us
    pallas_call x1, Pallas kernels, outer(): pl.pallas_call(functools.partial(outer_kernel, i_n, j_n, row_n, col_n), i...  5.36 us
    ppermute x2, starting transfers between devices, neighbour(): lax.ppermute(x, axis, [(n, n ^ 1) for n in range(lax.axis_size(axis))])  3.09 us
    pallas_call x1, Pallas kernels, prepare(): pl.pallas_call(functools.partial(prepare_kernel, i_n, j_n), in_specs=[in_...  2.61 us
    pallas_call x1, Pallas kernels, pair(): pl.pallas_call(functools.partial(pair_kernel, sequences), grid=(count,),...  2.56 us
    ppermute x11, waiting for transfers between devices, shift(): lax.ppermute(x, axis, [(n, (n + distance) % count) for n in range(count)])  2.07 us
    pallas_call x1, Pallas kernels, load(): pl.pallas_call(load_kernel, in_specs=[pl.BlockSpec(memory_space=pltpu.HBM...  1.39 us
  transfers between devices with their start and end apart: 13, of which 5 were waited for; matrix products, arithmetic and copies ran while one was open for 0% of the time, Pallas kernels for 34%

profile of v6, /device:TPU:0, one launch (start us, length us, event | category | flops | bytes accessed | tf_op | source)
XLA Modules:
  0.0 42.4 jit_solution(11461165535278589836)
XLA Ops:
  0.6 3.1 %collective-permute-start = (bf16[8,1536]{1,0:T(8,128)(2,1)}, bf16[8,1536]{1,0:T(8,128)(2,1)S(1)}, u32[]{:S(2)}, u32[]{:S(2)}) collective-permute-start(bf16[8,1536]{1,0:T(8,128)(2,1)} %a_hbm.1), channel_id=1, source_target_pairs={{0,1},{1,0},{2,3},{3,2},{4,5},{5,4},{6,7},{7,6},{8,9},{9,8},{10,11... | collective-permute-start | bytes 73736 | tf_op jit(solution)/shard_map/ppermute | solution.py:506
  3.7 0.0 collective-permute-start.1
  3.7 1.4 %shard_map.92 = (bf16[1024,128]{1,0:T(8,128)(2,1)S(1)}, bf16[128,1024]{1,0:T(8,128)(2,1)S(1)}, bf16[8,1536]{1,0:T(8,128)(2,1)S(1)}, bf16[8,1536]{1,0:T(8,128)(2,...) custom-call(bf16[8,1536]{1,0:T(8,128)(2,1)} %a_hbm.1, bf16[8,1536]{1,0:T(8,128)(2,1)} %b_hbm.1, ...), custom_call_target="tpu_custom_call" | custom-call | flops 131072000 | bytes 2097152 | tf_op jit(solution)/shard_map/pallas_call | solution.py:67
  5.1 0.6 %collective-permute-done.refs_1_ = bf16[8,1536]{1,0:T(8,128)(2,1)S(1)} collective-permute-done((bf16[8,1536]{1,0:T(8,128)(2,1)}, bf16[8,1536]{1,0:T(8,128)(2,1)S(1)}, u32[]{:S(2)}, u32[]{:S(2)}) %collective-permute-start) | collective-permute-done | bytes 24608 | tf_op jit(solution)/shard_map/ppermute | solution.py:506
  5.7 0.0 collective-permute-done.1.refs_3_
  5.8 3.1 %collective-permute-start.2 = (bf16[16,1536]{1,0:T(8,128)(2,1)S(1)}, bf16[16,1536]{1,0:T(8,128)(2,1)S(1)}, u32[]{:S(2)}, u32[]{:S(2)}) collective-permute-start(bf16[16,1536]{1,0:T(8,128)(2,1)S(1)} %get-tuple-element.44.refs_0_), channel_id=1, source_target_pairs={{0,2},{1,3},{2,0},{3,1},{4,6},{5,7},{6,4},{7,5},{8,10},{9,11},{10,... | collective-permute-start | bytes 147464 | tf_op jit(solution)/shard_map/ppermute | solution.py:502
  8.9 1.5 %collective-permute-start.3 = (bf16[16,1536]{1,0:T(8,128)(2,1)S(1)}, bf16[16,1536]{1,0:T(8,128)(2,1)S(1)}, u32[]{:S(2)}, u32[]{:S(2)}) collective-permute-start(bf16[16,1536]{1,0:T(8,128)(2,1)S(1)} %get-tuple-element.45.refs_2_), channel_id=1, source_target_pairs={{0,8},{4,12},{8,0},{12,4},{1,9},{5,13},{9,1},{13,5},{2,10},{6,14},... | collective-permute-start | bytes 147464 | tf_op jit(solution)/shard_map/ppermute | solution.py:502
  10.3 2.6 %shard_map.94 = (bf16[1024,2304]{1,0:T(8,128)(2,1)S(1)}, bf16[2304,128]{1,0:T(8,128)(2,1)S(1)}, bf16[16,128]{1,0:T(8,128)(2,1)S(1)}) custom-call(bf16[1024,128]{1,0:T(8,128)(2,1)S(1)} %get-tuple-element.47.we_ref, bf16[2304,128]{1,0:T(8,128)(2,1)S(1)} %get-tuple-element.46.g_ref.refs_4_), custom_call_target="tpu_custom_call" | custom-call | flops 603979776 | bytes 9437184 | tf_op jit(solution)/shard_map/pallas_call | solution.py:129
  13.0 0.0 collective-permute-done.2.refs_1_
  13.0 0.0 collective-permute-done.3.refs_3_
  13.0 5.4 %shard_map.95 = (bf16[1024,2304]{1,0:T(8,128)(2,1)S(1)}, f32[2,1536,128]{2,1,0:T(8,128)S(1)}, f32[2,1536,128]{2,1,0:T(8,128)S(1)}, f32[272,128]{1,0:T(8,128)S(1)...) custom-call(bf16[16,1536]{1,0:T(8,128)(2,1)S(1)} %get-tuple-element.44.refs_0_, ...), custom_call_target="tpu_custom_call" | custom-call | flops 1207959552 | bytes 4718592 | tf_op jit(solution)/shard_map/pallas_call | solution.py:259
  18.3 0.1 collective-permute-start.4
  18.4 1.5 %collective-permute-start.5 = (bf16[272,128]{1,0:T(8,128)(2,1)S(1)}, bf16[272,128]{1,0:T(8,128)(2,1)S(1)}, u32[]{:S(2)}, u32[]{:S(2)}) collective-permute-start(bf16[272,128]{1,0:T(8,128)(2,1)S(1)} %get-tuple-element.53), channel_id=1, source_target_pairs={{0,8},{4,12},{8,0},{12,4},{1,9},{5,13},{9,1},{13,5},{2,10},{6,14},... | collective-permute-start | bytes 208904 | tf_op jit(solution)/shard_map/ppermute | solution.py:502
  19.9 1.4 %collective-permute-start.6 = (bf16[272,128]{1,0:T(8,128)(2,1)S(1)}, bf16[272,128]{1,0:T(8,128)(2,1)S(1)}, u32[]{:S(2)}, u32[]{:S(2)}) collective-permute-start(bf16[272,128]{1,0:T(8,128)(2,1)S(1)} %get-tuple-element.54), channel_id=1, source_target_pairs={{0,12},{4,0},{8,4},{12,8},{1,13},{5,1},{9,5},{13,9},{2,14},{6,2},{... | collective-permute-start | bytes 208904 | tf_op jit(solution)/shard_map/ppermute | solution.py:502
  21.3 3.3 %shard_map.97 = (f32[96,128]{1,0:T(8,128)S(1)}, bf16[96,128]{1,0:T(8,128)(2,1)S(1)}, bf16[96,128]{1,0:T(8,128)(2,1)S(1)}, bf16[96,128]{1,0:T(8,128)(2,1)S(1)}) custom-call(f32[2,1536,128]{2,1,0:T(8,128)S(1)} %get-tuple-element.55.refs_0_, bf16[1024,2304]{1,0:T(8,128)(2,1)S(1)} %get-tuple-element.56.refs_1_), custom_call_target="tpu_custom_call" | custom-call | flops 603979776 | bytes 4718592 | tf_op jit(solution)/shard_map/pallas_call | solution.py:350
  24.6 0.0 collective-permute-done.4.refs_1_
  24.6 0.0 collective-permute-done.5.refs_2_
  24.7 1.0 %collective-permute-start.8 = (bf16[368,128]{1,0:T(8,128)(2,1)S(1)}, bf16[368,128]{1,0:T(8,128)(2,1)S(1)}, u32[]{:S(2)}, u32[]{:S(2)}) collective-permute-start(bf16[368,128]{1,0:T(8,128)(2,1)S(1)} %get-tuple-element.61), channel_id=1, source_target_pairs={{0,2},{1,3},{2,0},{3,1},{4,6},{5,7},{6,4},{7,5},{8,10},{9,11},{10,... | collective-permute-start | bytes 282632 | tf_op jit(solution)/shard_map/ppermute | solution.py:502
  25.7 3.0 %collective-permute-start.9 = (bf16[368,128]{1,0:T(8,128)(2,1)S(1)}, bf16[368,128]{1,0:T(8,128)(2,1)S(1)}, u32[]{:S(2)}, u32[]{:S(2)}) collective-permute-start(bf16[368,128]{1,0:T(8,128)(2,1)S(1)} %get-tuple-element.62), channel_id=1, source_target_pairs={{0,3},{1,0},{2,1},{3,2},{4,7},{5,4},{6,5},{7,6},{8,11},{9,8},{10,9... | collective-permute-start | bytes 282632 | tf_op jit(solution)/shard_map/ppermute | solution.py:502
  28.7 0.0 collective-permute-start.7
  28.7 4.7 %shard_map.99 = (f32[96,128]{1,0:T(8,128)S(1)}, bf16[96,128]{1,0:T(8,128)(2,1)S(1)}, bf16[96,128]{1,0:T(8,128)(2,1)S(1)}, bf16[96,128]{1,0:T(8,128)(2,1)S(1)}) custom-call(f32[2,1536,128]{2,1,0:T(8,128)S(1)} %get-tuple-element.64.refs_0_, bf16[1024,128]{1,0:T(8,128)(2,1)S(1)} %get-tuple-element.65.refs_1_, bf16[2304,128]{1,0:T(8,128)(2,1)S(1)} %get-tuple-element.66.refs_2_), custom_call_target="tpu_custom_call" | custom-call | flops 1207959552 | bytes 4718592 | tf_op jit(solution)/shard_map/pallas_call | solution.py:350
  33.4 0.5 %collective-permute-done.8.refs_1_ = bf16[368,128]{1,0:T(8,128)(2,1)S(1)} collective-permute-done((bf16[368,128]{1,0:T(8,128)(2,1)S(1)}, bf16[368,128]{1,0:T(8,128)(2,1)S(1)}, u32[]{:S(2)}, u32[]{:S(2)}) %collective-permute-start.8) | collective-permute-done | bytes 94240 | tf_op jit(solution)/shard_map/ppermute | solution.py:502
  33.9 0.0 collective-permute-done.9.refs_2_
  33.9 1.2 %collective-permute-done.7.refs_0_ = bf16[368,128]{1,0:T(8,128)(2,1)S(1)} collective-permute-done((bf16[368,128]{1,0:T(8,128)(2,1)S(1)}, bf16[368,128]{1,0:T(8,128)(2,1)S(1)}, u32[]{:S(2)}, u32[]{:S(2)}) %collective-permute-start.7) | collective-permute-done | bytes 94240 | tf_op jit(solution)/shard_map/ppermute | solution.py:502
  35.1 0.7 %shard_map.100 = (bf16[352,128]{1,0:T(8,128)(2,1)S(1)}, bf16[352,128]{1,0:T(8,128)(2,1)S(1)}, bf16[352,128]{1,0:T(8,128)(2,1)S(1)}, bf16[256,128]{1,0:T(8,128)(2...) custom-call(bf16[368,128]{1,0:T(8,128)(2,1)S(1)} %collective-permute-done.7.refs_0_, ...), custom_call_target="tpu_custom_call" | custom-call | tf_op jit(solution)/shard_map/pallas_call | solution.py:461
  35.9 1.4 %collective-permute-start.11 = (bf16[352,128]{1,0:T(8,128)(2,1)S(1)}, bf16[352,128]{1,0:T(8,128)(2,1)S(1)}, u32[]{:S(2)}, u32[]{:S(2)}) collective-permute-start(bf16[352,128]{1,0:T(8,128)(2,1)S(1)} %get-tuple-element.72), channel_id=1, source_target_pairs={{0,8},{4,12},{8,0},{12,4},{1,9},{5,13},{9,1},{13,5},{2,10},{6,14},... | collective-permute-start | bytes 270344 | tf_op jit(solution)/shard_map/ppermute | solution.py:502
  37.2 1.4 %collective-permute-start.12 = (bf16[352,128]{1,0:T(8,128)(2,1)S(1)}, bf16[352,128]{1,0:T(8,128)(2,1)S(1)}, u32[]{:S(2)}, u32[]{:S(2)}) collective-permute-start(bf16[352,128]{1,0:T(8,128)(2,1)S(1)} %get-tuple-element.73), channel_id=1, source_target_pairs={{0,12},{4,0},{8,4},{12,8},{1,13},{5,1},{9,5},{13,9},{2,14},{6,2},{... | collective-permute-start | bytes 270344 | tf_op jit(solution)/shard_map/ppermute | solution.py:502
  38.7 2.6 %shard_map.96 = bf16[2304,128]{1,0:T(8,128)(2,1)} custom-call(bf16[1024,2304]{1,0:T(8,128)(2,1)S(1)} %get-tuple-element.49.x_ref, bf16[128,1024]{1,0:T(8,128)(2,1)S(1)} %get-tuple-element.50.wt_ref, f32[1,128]{1,0:T(1,128)S(1)} %bitcast.4), custom_call_target="tpu_custom_call" | custom-call | flops 1207959552 | bytes 4718592 | tf_op jit(solution)/shard_map/pallas_call | solution.py:380
  41.2 0.0 collective-permute-done.10.refs_0_
  41.2 0.1 collective-permute-done.11.refs_1_
  41.3 0.3 collective-permute-done.12.refs_2_
  41.6 0.8 %shard_map.101 = (f32[1024,128]{1,0:T(8,128)}, f32[8,1536]{1,0:T(8,128)}) custom-call(bf16[352,128]{1,0:T(8,128)(2,1)S(1)} %collective-permute-done.10.refs_0_, bf16[352,128]{1,0:T(8,128)(2,1)S(1)} %collective-permute-done.11.refs_1_, bf16[352,128]{1,0:T(8,128)(2,1)S(1)} %collective-permute-done.12.refs_2_, bf16[256,128]{1,0:T(8,128)(2,1)S(1)} %get-tuple-element.74.refs_3_, ...), custom_call_target="tpu_custom_call" | custom-call | tf_op jit(solution)/shard_map/pallas_call | solution.py:488
  (6 shorter events, 0.1 us)
Async XLA Ops:
  0.6 5.1 %collective-permute-start = (bf16[8,1536]{1,0:T(8,128)(2,1)}, bf16[8,1536]{1,0:T(8,128)(2,1)S(1)}, u32[]{:S(2)}, u32[]{:S(2)}) collective-permute-start(bf16[8,1536]{1,0:T(8,128)(2,1)} %a_hbm.1), channel_id=1, source_target_pairs={{0,1},{1,0},{2,3},{3,2},{4,5},{5,4},{6,7},{7,6},{8,9},{9,8},{10,11... | collective-permute-start | bytes 73736 | tf_op jit(solution)/shard_map/ppermute | solution.py:506
  3.7 2.0 %collective-permute-start.1 = (bf16[8,1536]{1,0:T(8,128)(2,1)}, bf16[8,1536]{1,0:T(8,128)(2,1)S(1)}, u32[]{:S(2)}, u32[]{:S(2)}) collective-permute-start(bf16[8,1536]{1,0:T(8,128)(2,1)} %b_hbm.1), channel_id=1, source_target_pairs={{0,4},{4,0},{8,12},{12,8},{1,5},{5,1},{9,13},{13,9},{2,6},{6,2},{1... | collective-permute-start | bytes 73736 | tf_op jit(solution)/shard_map/ppermute | solution.py:506
  5.8 7.2 %collective-permute-start.2 = (bf16[16,1536]{1,0:T(8,128)(2,1)S(1)}, bf16[16,1536]{1,0:T(8,128)(2,1)S(1)}, u32[]{:S(2)}, u32[]{:S(2)}) collective-permute-start(bf16[16,1536]{1,0:T(8,128)(2,1)S(1)} %get-tuple-element.44.refs_0_), channel_id=1, source_target_pairs={{0,2},{1,3},{2,0},{3,1},{4,6},{5,7},{6,4},{7,5},{8,10},{9,11},{10,... | collective-permute-start | bytes 147464 | tf_op jit(solution)/shard_map/ppermute | solution.py:502
  8.9 4.1 %collective-permute-start.3 = (bf16[16,1536]{1,0:T(8,128)(2,1)S(1)}, bf16[16,1536]{1,0:T(8,128)(2,1)S(1)}, u32[]{:S(2)}, u32[]{:S(2)}) collective-permute-start(bf16[16,1536]{1,0:T(8,128)(2,1)S(1)} %get-tuple-element.45.refs_2_), channel_id=1, source_target_pairs={{0,8},{4,12},{8,0},{12,4},{1,9},{5,13},{9,1},{13,5},{2,10},{6,14},... | collective-permute-start | bytes 147464 | tf_op jit(solution)/shard_map/ppermute | solution.py:502
  18.3 6.3 %collective-permute-start.4 = (bf16[272,128]{1,0:T(8,128)(2,1)S(1)}, bf16[272,128]{1,0:T(8,128)(2,1)S(1)}, u32[]{:S(2)}, u32[]{:S(2)}) collective-permute-start(bf16[272,128]{1,0:T(8,128)(2,1)S(1)} %get-tuple-element.52), channel_id=1, source_target_pairs={{0,4},{4,8},{8,12},{12,0},{1,5},{5,9},{9,13},{13,1},{2,6},{6,10},{... | collective-permute-start | bytes 208904 | tf_op jit(solution)/shard_map/ppermute | solution.py:502
  18.4 6.2 %collective-permute-start.5 = (bf16[272,128]{1,0:T(8,128)(2,1)S(1)}, bf16[272,128]{1,0:T(8,128)(2,1)S(1)}, u32[]{:S(2)}, u32[]{:S(2)}) collective-permute-start(bf16[272,128]{1,0:T(8,128)(2,1)S(1)} %get-tuple-element.53), channel_id=1, source_target_pairs={{0,8},{4,12},{8,0},{12,4},{1,9},{5,13},{9,1},{13,5},{2,10},{6,14},... | collective-permute-start | bytes 208904 | tf_op jit(solution)/shard_map/ppermute | solution.py:502
  19.9 4.7 %collective-permute-start.6 = (bf16[272,128]{1,0:T(8,128)(2,1)S(1)}, bf16[272,128]{1,0:T(8,128)(2,1)S(1)}, u32[]{:S(2)}, u32[]{:S(2)}) collective-permute-start(bf16[272,128]{1,0:T(8,128)(2,1)S(1)} %get-tuple-element.54), channel_id=1, source_target_pairs={{0,12},{4,0},{8,4},{12,8},{1,13},{5,1},{9,5},{13,9},{2,14},{6,2},{... | collective-permute-start | bytes 208904 | tf_op jit(solution)/shard_map/ppermute | solution.py:502
  21.3 17.4 %copy-start = (f32[128]{0:T(128)S(1)}, f32[128]{0:T(128)}, u32[]{:S(2)}) copy-start(f32[128]{0:T(128)} %param.8) | copy-start | bytes 1540
  24.7 9.2 %collective-permute-start.8 = (bf16[368,128]{1,0:T(8,128)(2,1)S(1)}, bf16[368,128]{1,0:T(8,128)(2,1)S(1)}, u32[]{:S(2)}, u32[]{:S(2)}) collective-permute-start(bf16[368,128]{1,0:T(8,128)(2,1)S(1)} %get-tuple-element.61), channel_id=1, source_target_pairs={{0,2},{1,3},{2,0},{3,1},{4,6},{5,7},{6,4},{7,5},{8,10},{9,11},{10,... | collective-permute-start | bytes 282632 | tf_op jit(solution)/shard_map/ppermute | solution.py:502
  25.7 8.2 %collective-permute-start.9 = (bf16[368,128]{1,0:T(8,128)(2,1)S(1)}, bf16[368,128]{1,0:T(8,128)(2,1)S(1)}, u32[]{:S(2)}, u32[]{:S(2)}) collective-permute-start(bf16[368,128]{1,0:T(8,128)(2,1)S(1)} %get-tuple-element.62), channel_id=1, source_target_pairs={{0,3},{1,0},{2,1},{3,2},{4,7},{5,4},{6,5},{7,6},{8,11},{9,8},{10,9... | collective-permute-start | bytes 282632 | tf_op jit(solution)/shard_map/ppermute | solution.py:502
  28.7 6.4 %collective-permute-start.7 = (bf16[368,128]{1,0:T(8,128)(2,1)S(1)}, bf16[368,128]{1,0:T(8,128)(2,1)S(1)}, u32[]{:S(2)}, u32[]{:S(2)}) collective-permute-start(bf16[368,128]{1,0:T(8,128)(2,1)S(1)} %get-tuple-element.60.refs_4_), channel_id=1, source_target_pairs={{0,1},{1,2},{2,3},{3,0},{4,5},{5,6},{6,7},{7,4},{8,9},{9,10},{10,1... | collective-permute-start | bytes 282632 | tf_op jit(solution)/shard_map/ppermute | solution.py:502
  35.8 5.4 %collective-permute-start.10 = (bf16[352,128]{1,0:T(8,128)(2,1)S(1)}, bf16[352,128]{1,0:T(8,128)(2,1)S(1)}, u32[]{:S(2)}, u32[]{:S(2)}) collective-permute-start(bf16[352,128]{1,0:T(8,128)(2,1)S(1)} %get-tuple-element.71), channel_id=1, source_target_pairs={{0,4},{4,8},{8,12},{12,0},{1,5},{5,9},{9,13},{13,1},{2,6},{6,10},{... | collective-permute-start | bytes 270344 | tf_op jit(solution)/shard_map/ppermute | solution.py:502
  35.9 5.5 %collective-permute-start.11 = (bf16[352,128]{1,0:T(8,128)(2,1)S(1)}, bf16[352,128]{1,0:T(8,128)(2,1)S(1)}, u32[]{:S(2)}, u32[]{:S(2)}) collective-permute-start(bf16[352,128]{1,0:T(8,128)(2,1)S(1)} %get-tuple-element.72), channel_id=1, source_target_pairs={{0,8},{4,12},{8,0},{12,4},{1,9},{5,13},{9,1},{13,5},{2,10},{6,14},... | collective-permute-start | bytes 270344 | tf_op jit(solution)/shard_map/ppermute | solution.py:502
  37.2 4.3 %collective-permute-start.12 = (bf16[352,128]{1,0:T(8,128)(2,1)S(1)}, bf16[352,128]{1,0:T(8,128)(2,1)S(1)}, u32[]{:S(2)}, u32[]{:S(2)}) collective-permute-start(bf16[352,128]{1,0:T(8,128)(2,1)S(1)} %get-tuple-element.73), channel_id=1, source_target_pairs={{0,12},{4,0},{8,4},{12,8},{1,13},{5,1},{9,5},{13,9},{2,14},{6,2},{... | collective-permute-start | bytes 270344 | tf_op jit(solution)/shard_map/ppermute | solution.py:502

commit v7 on v6

--- a/solution.py
+++ b/solution.py
@@ -198,7 +198,7 @@
     b_pieces, refs = refs[: row_n // 2], refs[row_n // 2 :]
     (g_ref, bias_ref, x_ref, a_wide, b_wide), refs = refs[:5], refs[5:]
     messages, refs = refs[:row_n], refs[row_n:]
-    a_held, b_held, left, diagonal, total, ordered = refs
+    a_held, b_held, left, diagonal, total = refs
     sequences = a_held.shape[0]
     groups = i_n // GROUP
     per_step = depth // CHUNKS
@@ -235,13 +235,13 @@
                     ]
         total[rows, :] = dot(x_part[...], g_ref[...])
 
-    for c in range(depth):
-        ordered[c * depth : (c + 1) * depth, :] = total[pl.ds(c, depth, stride=depth), :]
-    share = ordered.shape[0] // row_n
+    share = total.shape[0] // row_n
     me = lax.axis_index("row")
     for p, message in enumerate(messages):
-        start = pl.multiple_of(lax.rem(me + p, row_n) * share, share)
-        message[0:share, :] = ordered[pl.ds(start, share), :].astype(message.dtype)
+        start = lax.rem(me + p, row_n) * (share // depth)
+        for n in range(share // depth):
+            block = total[pl.ds(start + n, depth, stride=depth), :]
+            message[n * depth : (n + 1) * depth, :] = block.astype(message.dtype)
         message[share:, :] = bias_ref[...].astype(message.dtype)
 
 
@@ -267,7 +267,6 @@
             pltpu.VMEM((i_n // GROUP * depth, GROUP * sequences), BF16),
             pltpu.VMEM((depth // CHUNKS, GROUP * j_n, GROUP * sequences), BF16),
             pltpu.VMEM((channels, PAIR_FEATURES), F32),
-            pltpu.VMEM((channels, PAIR_FEATURES), F32),
         ],
         compiler_params=params(sequences),
         cost_estimate=pl.CostEstimate(
@@ -279,12 +278,25 @@
     return *results[:3], results[3:]
 
 
-def gradient_kernel(axis, positions, others, sequences, *refs):
+def in_order(count):
+    return lambda me: ([me], [[lax.rem(me + d, count)] for d in range(1, count)])
+
+
+def in_pairs(count):
+    def plan(me):
+        near = me + 1 - 2 * lax.rem(me, 2)
+        steps = range(0, count, 2)
+        return [lax.rem(me + d, count) for d in steps], [[lax.rem(near + d, count) for d in steps]]
+
+    return plan
+
+
+def gradient_kernel(axis, plan, kept, positions, others, sequences, *refs):
     depth = PROJECTED_DEPTH
-    wide, refs = refs[0], refs[1:]
+    wide, source, _ = refs[:3]
+    outs = refs[3:-4]
+    diagonal, result, grown, grad = refs[-4:]
     parts = lax.axis_size(axis)
-    diagonal, result, grown, grad, product = refs[-5:]
-    sources, outs = refs[: -5 - parts], refs[-5 - parts : -5]
     per_step = depth // CHUNKS
     span = GROUP * others
 
@@ -297,13 +309,7 @@
             fill_diagonal(wide, diagonal, n, t * per_step + n, others, sequences)
         size = per_step * depth
         rows = pl.ds(pl.multiple_of(t * size, size), size)
-        if len(sources) == 1:
-            part = sources[0].at[rows]
-        else:
-            part = product
-            for n in range(0, size, size // 2):
-                block = sources[0][pl.ds(pl.multiple_of(t * size + n, size // 2), size // 2), :]
-                part[n : n + size // 2, :] = dot(block, sources[1][...], ROWS_BY_ROWS).astype(BF16)
+        part = source.at[rows]
         for n in range(0, per_step, 2):
             blocks = [
                 jnp.concatenate(
@@ -334,38 +340,74 @@
                 )
     grad[...] = dot(repeat_matrix(sequences), grown[...], ROWS_BY_ROWS)
     share = sequences // parts
-    me = lax.axis_index(axis)
-    for p, out in enumerate(outs):
-        mine = grad[pl.ds(pl.multiple_of(lax.rem(me + p, parts) * share, share), share), :]
-        out[...] = jnp.concatenate(
+
+    def rows_of(p):
+        mine = grad[pl.ds(pl.multiple_of(p * share, share), share), :]
+        return jnp.concatenate(
             [mine[:, l * LANES : (l + 1) * LANES] for l in range(mine.shape[1] // LANES)], axis=0
-        ).astype(out.dtype)
-
-
-def gradient(wide, sources, axis, positions, others, sequences):
+        )
+
+    stay, go = plan(lax.axis_index(axis))
+    for p, out in zip(stay, outs[:kept], strict=True):
+        out[...] = rows_of(p)
+    for group, out in zip(go, outs[kept:], strict=True):
+        size = out.shape[0] // len(group)
+        for n, p in enumerate(group):
+            out[n * size : (n + 1) * size, :] = rows_of(p).astype(BF16)
+
+
+def gradient(wide, source, after, axis, plan, kept, groups, positions, others, sequences):
     depth = PROJECTED_DEPTH
     channels, pairs = depth * depth, positions * others
     parts = lax.axis_size(axis)
     rows = sequences // parts * positions * depth // LANES
-    return pl.pallas_call(
-        functools.partial(gradient_kernel, axis, positions, others, sequences),
-        in_specs=[in_vmem()] * (len(sources) + 1),
-        out_specs=[in_vmem()] * parts,
-        out_shape=parts_shapes(parts, rows),
+    group = (parts - kept) // groups
+    shapes = [jax.ShapeDtypeStruct((rows, LANES), F32)] * kept
+    shapes += [jax.ShapeDtypeStruct((group * rows, LANES), BF16)] * groups
+    results = pl.pallas_call(
+        functools.partial(gradient_kernel, axis, plan, kept, positions, others, sequences),
+        in_specs=[in_vmem(), in_vmem(), pl.BlockSpec(memory_space=pl.ANY)],
+        out_specs=[in_vmem()] * len(shapes),
+        out_shape=shapes,
         scratch_shapes=[
             pltpu.VMEM((depth // CHUNKS, GROUP * others, GROUP * sequences), BF16),
             pltpu.VMEM((positions // GROUP * depth, GROUP * sequences), F32),
             pltpu.VMEM((positions * depth, GROUP * sequences), BF16),
             pltpu.VMEM((sequences, positions * depth), F32),
-            pltpu.VMEM((channels // CHUNKS if len(sources) > 1 else 16, pairs), BF16),
         ],
         compiler_params=params(sequences),
         cost_estimate=pl.CostEstimate(
-            flops=2 * len(sources) * pairs * channels * PAIR_FEATURES,
+            flops=2 * pairs * channels * PAIR_FEATURES,
             bytes_accessed=2 * pairs * channels,
             transcendentals=0,
         ),
-    )(wide, *sources)
+    )(wide, source, after)
+    return results[:kept], results[kept:]
+
+
+def product_kernel(left_ref, right_ref, _, out_ref):
+    size = out_ref.shape[0] // STEPS
+
+    @pl.loop(0, STEPS)
+    def _(t):
+        rows = pl.ds(pl.multiple_of(t * size, size), size)
+        out_ref[rows, :] = dot(left_ref[rows, :], right_ref[...], ROWS_BY_ROWS).astype(BF16)
+
+
+def product(left, right, after):
+    shape = (left.shape[0], right.shape[0])
+    return pl.pallas_call(
+        product_kernel,
+        in_specs=[in_vmem(), in_vmem(), pl.BlockSpec(memory_space=pl.ANY)],
+        out_specs=in_vmem(),
+        out_shape=jax.ShapeDtypeStruct(shape, BF16),
+        compiler_params=params(16),
+        cost_estimate=pl.CostEstimate(
+            flops=2 * shape[0] * shape[1] * left.shape[1],
+            bytes_accessed=4 * shape[0] * shape[1],
+            transcendentals=0,
+        ),
+    )(left, right, after)
 
 
 def pair_kernel(sequences, x_ref, wt_ref, bias_ref, out_ref):
@@ -401,42 +443,67 @@
         out[:, l * LANES : (l + 1) * LANES] = total[l * share : (l + 1) * share, :]
 
 
-def row_sum_kernel(row_n, *refs):
-    parts, refs = refs[:row_n], refs[row_n:]
-    grads, messages = refs[: len(refs) // 2], refs[len(refs) // 2 :]
+def row_sum_kernel(*refs):
+    parts, grad, message = refs[:-2], refs[-2], refs[-1]
     rows = parts[0].shape[0]
     total = parts[0][...]
     for part in parts[1:]:
         total += part[...].astype(F32)
-    total = total.astype(BF16)
-    for message, grad in zip(messages, grads, strict=True):
-        message[0:rows, :] = total
-        message[rows:, :] = grad[...]
-
-
-def row_sum(parts, grads):
-    shape = (parts[0].shape[0] + grads[0].shape[0], LANES)
+    message[0:rows, :] = total.astype(BF16)
+    message[rows:, :] = grad[...]
+
+
+def row_sum(parts, grad):
+    shape = (parts[0].shape[0] + grad.shape[0], LANES)
     return pl.pallas_call(
-        functools.partial(row_sum_kernel, len(parts)),
-        in_specs=[in_vmem()] * (len(parts) + len(grads)),
-        out_specs=[in_vmem()] * len(grads),
-        out_shape=[jax.ShapeDtypeStruct(shape, BF16)] * len(grads),
+        row_sum_kernel,
+        in_specs=[in_vmem()] * (len(parts) + 1),
+        out_specs=in_vmem(),
+        out_shape=jax.ShapeDtypeStruct(shape, BF16),
         compiler_params=params(),
-    )(*parts, *grads)
-
-
-def column_sum_kernel(res_total, col_n, *refs):
-    parts, grad, refs = refs[: col_n - 1], refs[col_n - 1], refs[col_n:]
+    )(*parts, grad)
+
+
+def pair_sum_kernel(rows, own, near, _, *refs):
+    count = len(refs) // 2
+    grads, left_out, messages = refs[:count], refs[count], refs[count + 1 :]
+    total = (own[0:rows, :].astype(F32) + near[0:rows, :].astype(F32)).astype(BF16)
+    size = left_out.shape[0]
+    for n, grad in enumerate(grads):
+        both = grad[...] + near[rows + n * size : rows + (n + 1) * size, :].astype(F32)
+        if n == 0:
+            left_out[...] = both
+        else:
+            messages[n - 1][0:rows, :] = total
+            messages[n - 1][rows:, :] = both.astype(BF16)
+
+
+def pair_sum(own, near, after, grads, rows):
+    size = grads[0].shape[0]
+    shapes = [jax.ShapeDtypeStruct((size, LANES), F32)]
+    shapes += [jax.ShapeDtypeStruct((rows + size, LANES), BF16)] * (len(grads) - 1)
+    left, *messages = pl.pallas_call(
+        functools.partial(pair_sum_kernel, rows),
+        in_specs=[in_vmem()] * 2 + [pl.BlockSpec(memory_space=pl.ANY)] + [in_vmem()] * len(grads),
+        out_specs=[in_vmem()] * len(shapes),
+        out_shape=shapes,
+        compiler_params=params(),
+    )(own, near, after, *grads)
+    return left, messages
+
+
+def column_sum_kernel(res_total, count, *refs):
+    parts, grad, refs = refs[: count - 1], refs[count - 1], refs[count:]
     own, refs = refs[0], refs[1:]
     grads, refs = refs[: (len(refs) - 4) // 2], refs[(len(refs) - 4) // 2 :]
     messages, (piece_out, left_out, bias_out, held) = refs[:-4], refs[-4:]
     share = piece_out.shape[0]
     rows = share + BIAS_ROWS
-    me = lax.axis_index("col")
+    home = lax.div(lax.axis_index("col"), 2)
     for p, part in enumerate((own, *parts)):
-        held[lax.rem(me - p + col_n, col_n)] = part[0:rows, :]
+        held[lax.rem(home - p + count, count)] = part[0:rows, :]
     total = held[0].astype(F32)
-    for n in range(1, col_n):
+    for n in range(1, count):
         total += held[n].astype(F32)
     piece = total[0:share].astype(BF16)
     piece_out[...] = piece
@@ -518,7 +585,7 @@
     first_homolog_features, second_homolog_features, final_projection_matrix, output_bias, cotangent
 ):
     i_n, j_n, _ = cotangent.shape
-    row_n = lax.axis_size("row")
+    row_n, col_n = lax.axis_size("row"), lax.axis_size("col")
     sequences = second_homolog_features.shape[0] * row_n
     channels = final_projection_matrix.shape[0]
     res_total = i_n * row_n
@@ -539,10 +606,17 @@
         a_pieces, b_pieces, g, bias_rows, i_n, j_n, sequences
     )
     row_parts = [row_own] + exchange(messages, "row")
-    left_own, *left_grads = gradient(b_wide, [y], "col", i_n, j_n, sequences)
-    messages = row_sum(row_parts, left_grads)
-    col_parts = exchange(messages, "col")
-    right_own, *right_grads = gradient(a_wide, [w, gt], "row", j_n, i_n, sequences)
+    left_kept, (left_sent,) = gradient(
+        b_wide, y, row_own, "col", in_pairs(col_n), col_n // 2, 1, i_n, j_n, sequences
+    )
+    message = row_sum(row_parts, left_sent)
+    near = neighbour(message, "col")
+    y2 = product(w, gt, message)
+    left_own, messages = pair_sum(message, near, y2, left_kept, row_own.shape[0])
+    col_parts = [shift(part, "col", 2 * d) for d, part in enumerate(messages, 1)]
+    (right_own,), right_grads = gradient(
+        a_wide, y2, messages[0], "row", in_order(row_n), 1, row_n - 1, j_n, i_n, sequences
+    )
     messages, piece, left_grad, bias_grad = column_sum(
         col_parts,
         left_own,

time: 43.1 us -> 44 us (1.021); the launches traced: 42.4 us -> 43.9 us
  waiting for transfers between devices: 2.69 us -> 3.57 us
    ppermute x2 -> x3, starting transfers between devices: 3.09 us -> 4.73 us  [neighbour(): lax.ppermute(x, axis, [(n, n ^ 1) for n in range(lax.axis_size(axis))])]
    ppermute x11 -> x9, starting transfers between devices: 14.4 us -> 12.9 us  [shift(): lax.ppermute(x, axis, [(n, (n + distance) % count) for n in range(count)])]
    ppermute x2 -> x3, waiting for transfers between devices: 0.62 us -> 1.99 us  [neighbour(): lax.ppermute(x, axis, [(n, n ^ 1) for n in range(lax.axis_size(axis))])]
    pallas_call x3 -> x5, Pallas kernels: 8.04 us -> 8.53 us  [the longest x2 6.58 us: gradient(): pl.pallas_call(functools.partial(gradient_kernel, axis, plan, kept, posit...]
    ppermute x11 -> x9, waiting for transfers between devices: 2.07 us -> 1.58 us  [shift(): lax.ppermute(x, axis, [(n, (n + distance) % count) for n in range(count)])]
  transfers between devices with their start and end apart: 13 -> 12, of which waited for: 5 -> 4; matrix products, arithmetic and copies ran while one was open for 0% -> 0% of each run, Pallas kernels for 34% -> 34%
where the time goes in v7:
time: 44 us; the launch traced here: 43.9 us
  Pallas kernels  21.9 us (50%)
  starting transfers between devices  17.6 us (40%)
  waiting for transfers between devices  3.57 us (8%)
  between operations  0.75 us (2%)
    ppermute x9, starting transfers between devices, shift(): lax.ppermute(x, axis, [(n, (n + distance) % count) for n in range(count)])  12.9 us
    pallas_call x2, Pallas kernels, gradient(): pl.pallas_call(functools.partial(gradient_kernel, axis, plan, kept, posit...  6.58 us
    pallas_call x1, Pallas kernels, outer(): pl.pallas_call(functools.partial(outer_kernel, i_n, j_n, row_n, col_n), i...  5.33 us
    ppermute x3, starting transfers between devices, neighbour(): lax.ppermute(x, axis, [(n, n ^ 1) for n in range(lax.axis_size(axis))])  4.73 us
    pallas_call x1, Pallas kernels, prepare(): pl.pallas_call(functools.partial(prepare_kernel, i_n, j_n), in_specs=[in_...  2.65 us
    pallas_call x1, Pallas kernels, pair(): pl.pallas_call(functools.partial(pair_kernel, sequences), grid=(count,),...  2.56 us
    ppermute x3, waiting for transfers between devices, neighbour(): lax.ppermute(x, axis, [(n, n ^ 1) for n in range(lax.axis_size(axis))])  1.99 us
    pallas_call x1, Pallas kernels, product(): pl.pallas_call(product_kernel, in_specs=[in_vmem(), in_vmem(), pl.BlockSp...  1.88 us
  transfers between devices with their start and end apart: 12, of which 4 were waited for; matrix products, arithmetic and copies ran while one was open for 0% of the time, Pallas kernels for 34%

profile of v7, /device:TPU:0, one launch (start us, length us, event | category | flops | bytes accessed | tf_op | source)
XLA Modules:
  0.0 43.9 jit_solution(10144609378307750855)
XLA Ops:
  0.6 3.1 %collective-permute-start = (bf16[8,1536]{1,0:T(8,128)(2,1)}, bf16[8,1536]{1,0:T(8,128)(2,1)S(1)}, u32[]{:S(2)}, u32[]{:S(2)}) collective-permute-start(bf16[8,1536]{1,0:T(8,128)(2,1)} %a_hbm.1), channel_id=1, source_target_pairs={{0,1},{1,0},{2,3},{3,2},{4,5},{5,4},{6,7},{7,6},{8,9},{9,8},{10,11... | collective-permute-start | bytes 73736 | tf_op jit(solution)/shard_map/ppermute | solution.py:573
  3.7 0.0 collective-permute-start.1
  3.7 1.4 %shard_map.92 = (bf16[1024,128]{1,0:T(8,128)(2,1)S(1)}, bf16[128,1024]{1,0:T(8,128)(2,1)S(1)}, bf16[8,1536]{1,0:T(8,128)(2,1)S(1)}, bf16[8,1536]{1,0:T(8,128)(2,...) custom-call(bf16[8,1536]{1,0:T(8,128)(2,1)} %a_hbm.1, bf16[8,1536]{1,0:T(8,128)(2,1)} %b_hbm.1, ...), custom_call_target="tpu_custom_call" | custom-call | flops 131072000 | bytes 2097152 | tf_op jit(solution)/shard_map/pallas_call | solution.py:67
  5.1 0.6 %collective-permute-done.refs_1_ = bf16[8,1536]{1,0:T(8,128)(2,1)S(1)} collective-permute-done((bf16[8,1536]{1,0:T(8,128)(2,1)}, bf16[8,1536]{1,0:T(8,128)(2,1)S(1)}, u32[]{:S(2)}, u32[]{:S(2)}) %collective-permute-start) | collective-permute-done | bytes 24608 | tf_op jit(solution)/shard_map/ppermute | solution.py:573
  5.7 0.0 collective-permute-done.1.refs_3_
  5.8 3.1 %collective-permute-start.2 = (bf16[16,1536]{1,0:T(8,128)(2,1)S(1)}, bf16[16,1536]{1,0:T(8,128)(2,1)S(1)}, u32[]{:S(2)}, u32[]{:S(2)}) collective-permute-start(bf16[16,1536]{1,0:T(8,128)(2,1)S(1)} %get-tuple-element.42.refs_0_), channel_id=1, source_target_pairs={{0,2},{1,3},{2,0},{3,1},{4,6},{5,7},{6,4},{7,5},{8,10},{9,11},{10,... | collective-permute-start | bytes 147464 | tf_op jit(solution)/shard_map/ppermute | solution.py:569
  8.9 1.5 %collective-permute-start.3 = (bf16[16,1536]{1,0:T(8,128)(2,1)S(1)}, bf16[16,1536]{1,0:T(8,128)(2,1)S(1)}, u32[]{:S(2)}, u32[]{:S(2)}) collective-permute-start(bf16[16,1536]{1,0:T(8,128)(2,1)S(1)} %get-tuple-element.43.refs_2_), channel_id=1, source_target_pairs={{0,8},{4,12},{8,0},{12,4},{1,9},{5,13},{9,1},{13,5},{2,10},{6,14},... | collective-permute-start | bytes 147464 | tf_op jit(solution)/shard_map/ppermute | solution.py:569
  10.3 2.6 %shard_map.94 = (bf16[1024,2304]{1,0:T(8,128)(2,1)S(1)}, bf16[2304,128]{1,0:T(8,128)(2,1)S(1)}, bf16[16,128]{1,0:T(8,128)(2,1)S(1)}) custom-call(bf16[1024,128]{1,0:T(8,128)(2,1)S(1)} %get-tuple-element.45.we_ref, bf16[2304,128]{1,0:T(8,128)(2,1)S(1)} %get-tuple-element.44.g_ref.refs_4_), custom_call_target="tpu_custom_call" | custom-call | flops 603979776 | bytes 9437184 | tf_op jit(solution)/shard_map/pallas_call | solution.py:129
  13.0 0.0 collective-permute-done.2.refs_1_
  13.0 0.0 collective-permute-done.3.refs_3_
  13.0 5.3 %shard_map.95 = (bf16[1024,2304]{1,0:T(8,128)(2,1)S(1)}, f32[2,1536,128]{2,1,0:T(8,128)S(1)}, f32[2,1536,128]{2,1,0:T(8,128)S(1)}, f32[272,128]{1,0:T(8,128)S(1)...) custom-call(bf16[16,1536]{1,0:T(8,128)(2,1)S(1)} %get-tuple-element.42.refs_0_, ...), custom_call_target="tpu_custom_call" | custom-call | flops 1207959552 | bytes 4718592 | tf_op jit(solution)/shard_map/pallas_call | solution.py:259
  18.4 0.1 collective-permute-start.4
  18.4 1.5 %collective-permute-start.5 = (bf16[272,128]{1,0:T(8,128)(2,1)S(1)}, bf16[272,128]{1,0:T(8,128)(2,1)S(1)}, u32[]{:S(2)}, u32[]{:S(2)}) collective-permute-start(bf16[272,128]{1,0:T(8,128)(2,1)S(1)} %get-tuple-element.51), channel_id=1, source_target_pairs={{0,8},{4,12},{8,0},{12,4},{1,9},{5,13},{9,1},{13,5},{2,10},{6,14},... | collective-permute-start | bytes 208904 | tf_op jit(solution)/shard_map/ppermute | solution.py:569
  19.9 1.4 %collective-permute-start.6 = (bf16[272,128]{1,0:T(8,128)(2,1)S(1)}, bf16[272,128]{1,0:T(8,128)(2,1)S(1)}, u32[]{:S(2)}, u32[]{:S(2)}) collective-permute-start(bf16[272,128]{1,0:T(8,128)(2,1)S(1)} %get-tuple-element.52), channel_id=1, source_target_pairs={{0,12},{4,0},{8,4},{12,8},{1,13},{5,1},{9,5},{13,9},{2,14},{6,2},{... | collective-permute-start | bytes 208904 | tf_op jit(solution)/shard_map/ppermute | solution.py:569
  21.3 3.3 %shard_map.97 = (f32[96,128]{1,0:T(8,128)S(1)}, f32[96,128]{1,0:T(8,128)S(1)}, bf16[192,128]{1,0:T(8,128)(2,1)S(1)}) custom-call(f32[2,1536,128]{2,1,0:T(8,128)S(1)} %get-tuple-element.53.refs_0_, bf16[1024,2304]{1,0:T(8,128)(2,1)S(1)} %get-tuple-element.54.refs_1_, f32[272,128]{1,0:T(8,128)S(1)} %get-tuple-element.49.refs_2_.refs_0_), custom_call_target="tpu_custom_call" | custom-call | flops 603979776 | bytes 4718592 | tf_op jit(solution)/shard_map/pallas_call | solution.py:367
  24.6 0.0 collective-permute-done.4.refs_1_
  24.6 0.0 collective-permute-done.5.refs_2_
  24.6 0.0 collective-permute-done.6.refs_3_
  24.7 1.6 %collective-permute-start.7 = (bf16[464,128]{1,0:T(8,128)(2,1)S(1)}, bf16[464,128]{1,0:T(8,128)(2,1)S(1)}, u32[]{:S(2)}, u32[]{:S(2)}) collective-permute-start(bf16[464,128]{1,0:T(8,128)(2,1)S(1)} %shard_map.98._.own), channel_id=1, source_target_pairs={{0,1},{1,0},{2,3},{3,2},{4,5},{5,4},{6,7},{7,6},{8,9},{9,8},{10,11... | collective-permute-start | bytes 356360 | tf_op jit(solution)/shard_map/ppermute | solution.py:573
  26.3 1.9 %shard_map.99._.refs_1_ = bf16[1024,2304]{1,0:T(8,128)(2,1)S(1)} custom-call(bf16[1024,128]{1,0:T(8,128)(2,1)S(1)} %get-tuple-element.56.left_ref, bf16[2304,128]{1,0:T(8,128)(2,1)S(1)} %get-tuple-element.57.right_ref, bf16[464,128]{1,0:T(8,128)(2,1)S(1)} %shard_map.98._.own), custom_call_target="tpu_custom_call" | custom-call | flops 603979776 | bytes 9437184 | tf_op jit(solution)/shard_map/pallas_call | solution.py:399
  28.2 1.4 %collective-permute-done.7.near = bf16[464,128]{1,0:T(8,128)(2,1)S(1)} collective-permute-done((bf16[464,128]{1,0:T(8,128)(2,1)S(1)}, bf16[464,128]{1,0:T(8,128)(2,1)S(1)}, u32[]{:S(2)}, u32[]{:S(2)}) %collective-permute-start.7) | collective-permute-done | bytes 118816 | tf_op jit(solution)/shard_map/ppermute | solution.py:573
  29.6 1.0 %collective-permute-start.8 = (bf16[368,128]{1,0:T(8,128)(2,1)S(1)}, bf16[368,128]{1,0:T(8,128)(2,1)S(1)}, u32[]{:S(2)}, u32[]{:S(2)}) collective-permute-start(bf16[368,128]{1,0:T(8,128)(2,1)S(1)} %get-tuple-element.60.refs_2_), channel_id=1, source_target_pairs={{0,2},{1,3},{2,0},{3,1},{4,6},{5,7},{6,4},{7,5},{8,10},{9,11},{10,... | collective-permute-start | bytes 282632 | tf_op jit(solution)/shard_map/ppermute | solution.py:569
  30.6 3.3 %shard_map.101 = (f32[96,128]{1,0:T(8,128)S(1)}, bf16[96,128]{1,0:T(8,128)(2,1)S(1)}, bf16[96,128]{1,0:T(8,128)(2,1)S(1)}, bf16[96,128]{1,0:T(8,128)(2,1)S(1)}) custom-call(f32[2,1536,128]{2,1,0:T(8,128)S(1)} %get-tuple-element.62.refs_0_, bf16[1024,2304]{1,0:T(8,128)(2,1)S(1)} %shard_map.99._.refs_1_, bf16[368,128]{1,0:T(8,128)(2,1)S(1)} %get-tuple-element.60.refs_2_), custom_call_target="tpu_custom_call" | custom-call | flops 603979776 | bytes 4718592 | tf_op jit(solution)/shard_map/pallas_call | solution.py:367
  33.9 1.2 %collective-permute-done.8.refs_0_ = bf16[368,128]{1,0:T(8,128)(2,1)S(1)} collective-permute-done((bf16[368,128]{1,0:T(8,128)(2,1)S(1)}, bf16[368,128]{1,0:T(8,128)(2,1)S(1)}, u32[]{:S(2)}, u32[]{:S(2)}) %collective-permute-start.8) | collective-permute-done | bytes 94240 | tf_op jit(solution)/shard_map/ppermute | solution.py:569
  35.1 0.6 %shard_map.102 = (bf16[352,128]{1,0:T(8,128)(2,1)S(1)}, bf16[352,128]{1,0:T(8,128)(2,1)S(1)}, bf16[352,128]{1,0:T(8,128)(2,1)S(1)}, bf16[256,128]{1,0:T(8,128)(2...) custom-call(bf16[368,128]{1,0:T(8,128)(2,1)S(1)} %collective-permute-done.8.refs_0_, ...), custom_call_target="tpu_custom_call" | custom-call | tf_op jit(solution)/shard_map/pallas_call | solution.py:528
  35.8 0.0 collective-permute-start.9
  35.8 2.9 %collective-permute-start.10 = (bf16[352,128]{1,0:T(8,128)(2,1)S(1)}, bf16[352,128]{1,0:T(8,128)(2,1)S(1)}, u32[]{:S(2)}, u32[]{:S(2)}) collective-permute-start(bf16[352,128]{1,0:T(8,128)(2,1)S(1)} %get-tuple-element.68), channel_id=1, source_target_pairs={{0,8},{4,12},{8,0},{12,4},{1,9},{5,13},{9,1},{13,5},{2,10},{6,14},... | collective-permute-start | bytes 270344 | tf_op jit(solution)/shard_map/ppermute | solution.py:569
  38.7 1.4 %collective-permute-start.11 = (bf16[352,128]{1,0:T(8,128)(2,1)S(1)}, bf16[352,128]{1,0:T(8,128)(2,1)S(1)}, u32[]{:S(2)}, u32[]{:S(2)}) collective-permute-start(bf16[352,128]{1,0:T(8,128)(2,1)S(1)} %get-tuple-element.69), channel_id=1, source_target_pairs={{0,12},{4,0},{8,4},{12,8},{1,13},{5,1},{9,5},{13,9},{2,14},{6,2},{... | collective-permute-start | bytes 270344 | tf_op jit(solution)/shard_map/ppermute | solution.py:569
  40.1 2.6 %shard_map.96 = bf16[2304,128]{1,0:T(8,128)(2,1)} custom-call(bf16[1024,2304]{1,0:T(8,128)(2,1)S(1)} %get-tuple-element.47.x_ref, bf16[128,1024]{1,0:T(8,128)(2,1)S(1)} %get-tuple-element.48.wt_ref, f32[1,128]{1,0:T(1,128)S(1)} %bitcast.4), custom_call_target="tpu_custom_call" | custom-call | flops 1207959552 | bytes 4718592 | tf_op jit(solution)/shard_map/pallas_call | solution.py:422
  42.7 0.0 collective-permute-done.10.refs_1_
  42.7 0.3 collective-permute-done.11.refs_2_
  43.0 0.8 %shard_map.103 = (f32[1024,128]{1,0:T(8,128)}, f32[8,1536]{1,0:T(8,128)}) custom-call(bf16[352,128]{1,0:T(8,128)(2,1)S(1)} %collective-permute-done.9.refs_0_, bf16[352,128]{1,0:T(8,128)(2,1)S(1)} %collective-permute-done.10.refs_1_, bf16[352,128]{1,0:T(8,128)(2,1)S(1)} %collective-permute-done.11.refs_2_, bf16[256,128]{1,0:T(8,128)(2,1)S(1)} %get-tuple-element.70.refs_3_, ...), custom_call_target="tpu_custom_call" | custom-call | tf_op jit(solution)/shard_map/pallas_call | solution.py:555
  (6 shorter events, 0.1 us)
Async XLA Ops:
  0.6 5.1 %collective-permute-start = (bf16[8,1536]{1,0:T(8,128)(2,1)}, bf16[8,1536]{1,0:T(8,128)(2,1)S(1)}, u32[]{:S(2)}, u32[]{:S(2)}) collective-permute-start(bf16[8,1536]{1,0:T(8,128)(2,1)} %a_hbm.1), channel_id=1, source_target_pairs={{0,1},{1,0},{2,3},{3,2},{4,5},{5,4},{6,7},{7,6},{8,9},{9,8},{10,11... | collective-permute-start | bytes 73736 | tf_op jit(solution)/shard_map/ppermute | solution.py:573
  3.7 2.0 %collective-permute-start.1 = (bf16[8,1536]{1,0:T(8,128)(2,1)}, bf16[8,1536]{1,0:T(8,128)(2,1)S(1)}, u32[]{:S(2)}, u32[]{:S(2)}) collective-permute-start(bf16[8,1536]{1,0:T(8,128)(2,1)} %b_hbm.1), channel_id=1, source_target_pairs={{0,4},{4,0},{8,12},{12,8},{1,5},{5,1},{9,13},{13,9},{2,6},{6,2},{1... | collective-permute-start | bytes 73736 | tf_op jit(solution)/shard_map/ppermute | solution.py:573
  5.8 7.2 %collective-permute-start.2 = (bf16[16,1536]{1,0:T(8,128)(2,1)S(1)}, bf16[16,1536]{1,0:T(8,128)(2,1)S(1)}, u32[]{:S(2)}, u32[]{:S(2)}) collective-permute-start(bf16[16,1536]{1,0:T(8,128)(2,1)S(1)} %get-tuple-element.42.refs_0_), channel_id=1, source_target_pairs={{0,2},{1,3},{2,0},{3,1},{4,6},{5,7},{6,4},{7,5},{8,10},{9,11},{10,... | collective-permute-start | bytes 147464 | tf_op jit(solution)/shard_map/ppermute | solution.py:569
  8.9 4.2 %collective-permute-start.3 = (bf16[16,1536]{1,0:T(8,128)(2,1)S(1)}, bf16[16,1536]{1,0:T(8,128)(2,1)S(1)}, u32[]{:S(2)}, u32[]{:S(2)}) collective-permute-start(bf16[16,1536]{1,0:T(8,128)(2,1)S(1)} %get-tuple-element.43.refs_2_), channel_id=1, source_target_pairs={{0,8},{4,12},{8,0},{12,4},{1,9},{5,13},{9,1},{13,5},{2,10},{6,14},... | collective-permute-start | bytes 147464 | tf_op jit(solution)/shard_map/ppermute | solution.py:569
  18.4 6.2 %collective-permute-start.4 = (bf16[272,128]{1,0:T(8,128)(2,1)S(1)}, bf16[272,128]{1,0:T(8,128)(2,1)S(1)}, u32[]{:S(2)}, u32[]{:S(2)}) collective-permute-start(bf16[272,128]{1,0:T(8,128)(2,1)S(1)} %get-tuple-element.50), channel_id=1, source_target_pairs={{0,4},{4,8},{8,12},{12,0},{1,5},{5,9},{9,13},{13,1},{2,6},{6,10},{... | collective-permute-start | bytes 208904 | tf_op jit(solution)/shard_map/ppermute | solution.py:569
  18.4 6.2 %collective-permute-start.5 = (bf16[272,128]{1,0:T(8,128)(2,1)S(1)}, bf16[272,128]{1,0:T(8,128)(2,1)S(1)}, u32[]{:S(2)}, u32[]{:S(2)}) collective-permute-start(bf16[272,128]{1,0:T(8,128)(2,1)S(1)} %get-tuple-element.51), channel_id=1, source_target_pairs={{0,8},{4,12},{8,0},{12,4},{1,9},{5,13},{9,1},{13,5},{2,10},{6,14},... | collective-permute-start | bytes 208904 | tf_op jit(solution)/shard_map/ppermute | solution.py:569
  19.9 4.7 %collective-permute-start.6 = (bf16[272,128]{1,0:T(8,128)(2,1)S(1)}, bf16[272,128]{1,0:T(8,128)(2,1)S(1)}, u32[]{:S(2)}, u32[]{:S(2)}) collective-permute-start(bf16[272,128]{1,0:T(8,128)(2,1)S(1)} %get-tuple-element.52), channel_id=1, source_target_pairs={{0,12},{4,0},{8,4},{12,8},{1,13},{5,1},{9,5},{13,9},{2,14},{6,2},{... | collective-permute-start | bytes 208904 | tf_op jit(solution)/shard_map/ppermute | solution.py:569
  24.7 4.9 %collective-permute-start.7 = (bf16[464,128]{1,0:T(8,128)(2,1)S(1)}, bf16[464,128]{1,0:T(8,128)(2,1)S(1)}, u32[]{:S(2)}, u32[]{:S(2)}) collective-permute-start(bf16[464,128]{1,0:T(8,128)(2,1)S(1)} %shard_map.98._.own), channel_id=1, source_target_pairs={{0,1},{1,0},{2,3},{3,2},{4,5},{5,4},{6,7},{7,6},{8,9},{9,8},{10,11... | collective-permute-start | bytes 356360 | tf_op jit(solution)/shard_map/ppermute | solution.py:573
  29.6 10.6 %copy-start = (f32[128]{0:T(128)S(1)}, f32[128]{0:T(128)}, u32[]{:S(2)}) copy-start(f32[128]{0:T(128)} %param.8) | copy-start | bytes 1540
  29.6 5.5 %collective-permute-start.8 = (bf16[368,128]{1,0:T(8,128)(2,1)S(1)}, bf16[368,128]{1,0:T(8,128)(2,1)S(1)}, u32[]{:S(2)}, u32[]{:S(2)}) collective-permute-start(bf16[368,128]{1,0:T(8,128)(2,1)S(1)} %get-tuple-element.60.refs_2_), channel_id=1, source_target_pairs={{0,2},{1,3},{2,0},{3,1},{4,6},{5,7},{6,4},{7,5},{8,10},{9,11},{10,... | collective-permute-start | bytes 282632 | tf_op jit(solution)/shard_map/ppermute | solution.py:569
  35.8 6.9 %collective-permute-start.9 = (bf16[352,128]{1,0:T(8,128)(2,1)S(1)}, bf16[352,128]{1,0:T(8,128)(2,1)S(1)}, u32[]{:S(2)}, u32[]{:S(2)}) collective-permute-start(bf16[352,128]{1,0:T(8,128)(2,1)S(1)} %get-tuple-element.67), channel_id=1, source_target_pairs={{0,4},{4,8},{8,12},{12,0},{1,5},{5,9},{9,13},{13,1},{2,6},{6,10},{... | collective-permute-start | bytes 270344 | tf_op jit(solution)/shard_map/ppermute | solution.py:569
  35.8 6.9 %collective-permute-start.10 = (bf16[352,128]{1,0:T(8,128)(2,1)S(1)}, bf16[352,128]{1,0:T(8,128)(2,1)S(1)}, u32[]{:S(2)}, u32[]{:S(2)}) collective-permute-start(bf16[352,128]{1,0:T(8,128)(2,1)S(1)} %get-tuple-element.68), channel_id=1, source_target_pairs={{0,8},{4,12},{8,0},{12,4},{1,9},{5,13},{9,1},{13,5},{2,10},{6,14},... | collective-permute-start | bytes 270344 | tf_op jit(solution)/shard_map/ppermute | solution.py:569
  38.7 4.3 %collective-permute-start.11 = (bf16[352,128]{1,0:T(8,128)(2,1)S(1)}, bf16[352,128]{1,0:T(8,128)(2,1)S(1)}, u32[]{:S(2)}, u32[]{:S(2)}) collective-permute-start(bf16[352,128]{1,0:T(8,128)(2,1)S(1)} %get-tuple-element.69), channel_id=1, source_target_pairs={{0,12},{4,0},{8,4},{12,8},{1,13},{5,1},{9,5},{13,9},{2,14},{6,2},{... | collective-permute-start | bytes 270344 | tf_op jit(solution)/shard_map/ppermute | solution.py:569

commit v8 on v7

--- a/solution.py
+++ b/solution.py
@@ -10,7 +10,7 @@
 PROJECTED_DEPTH = 32
 PAIR_FEATURES = 128
 GROUP = 8
-STEPS = 4
+MULTIPLY_ROWS = 384
 CHUNKS = 2
 BIAS_ROWS = 16
 LANES = 128
@@ -100,19 +100,27 @@
     )(*operands)
 
 
+def split(total):
+    high = total.astype(BF16).astype(F32)
+    row = lax.broadcasted_iota(jnp.int32, (BIAS_ROWS, PAIR_FEATURES), 0)
+    return jnp.where(row == 0, high, jnp.where(row == 1, total - high, 0.0)).astype(BF16)
+
+
+def joined(block):
+    block = block.astype(F32)
+    return block[0:1] + block[1:2]
+
+
+def multiply(left_ref, right_ref, out_ref):
+    for n in range(0, right_ref.shape[0], MULTIPLY_ROWS):
+        rows = slice(n, n + MULTIPLY_ROWS)
+        out_ref[:, rows] = dot(left_ref[...], right_ref[rows, :], ROWS_BY_ROWS).astype(BF16)
+
+
 def prepare_kernel(i_n, j_n, we_ref, g_ref, y_ref, gt_ref, bias_ref, g32):
     g32[...] = g_ref[...].astype(F32)
-    total = jnp.sum(g32[...], axis=0, keepdims=True)
-    high = total.astype(BF16).astype(F32)
-    row = lax.broadcasted_iota(jnp.int32, (BIAS_ROWS, PAIR_FEATURES), 0)
-    bias_ref[...] = jnp.where(row == 0, high, jnp.where(row == 1, total - high, 0.0)).astype(BF16)
-    size = y_ref.shape[0] // STEPS
-
-    @pl.loop(0, STEPS)
-    def _(t):
-        rows = pl.ds(pl.multiple_of(t * size, size), size)
-        y_ref[rows, :] = dot(we_ref[rows, :], g_ref[...], ROWS_BY_ROWS).astype(BF16)
-
+    bias_ref[...] = split(jnp.sum(g32[...], axis=0, keepdims=True))
+    multiply(we_ref, g_ref, y_ref)
 
     for j in range(j_n):
         gt_ref[j * i_n : (j + 1) * i_n, :] = g32[pl.ds(j, i_n, stride=j_n), :].astype(BF16)
@@ -177,6 +185,16 @@
     ]
 
 
+def clear_off_diagonal(diagonal, positions, sequences):
+    for l in range(diagonal.shape[2] // LANES):
+        members = dict(tiles_of(sequences, l))
+        for m in range(GROUP):
+            if m not in members:
+                rows = slice(m * positions, (m + 1) * positions)
+                shape = (diagonal.shape[0], positions, LANES)
+                diagonal[:, rows, l * LANES : (l + 1) * LANES] = jnp.zeros(shape, BF16)
+
+
 def fill_diagonal(wide, diagonal, slot, channel, positions, sequences):
     for l in range(wide.shape[0]):
         block = wide[l, pl.ds(channel, positions, stride=PROJECTED_DEPTH), :].astype(BF16)
@@ -186,19 +204,35 @@
             )
 
 
-def parts_shapes(count, rows):
-    return [jax.ShapeDtypeStruct((rows, LANES), F32)] + [
-        jax.ShapeDtypeStruct((rows, LANES), BF16)
-    ] * (count - 1)
+def near_of(me):
+    return me + 1 - 2 * lax.rem(me, 2)
+
+
+def by_pairs(count):
+    def plan(me):
+        groups = [
+            [lax.rem(me + d, count), lax.rem(near_of(me) + d, count)] for d in range(0, count, 2)
+        ]
+        return groups[0], groups[1:]
+
+    return plan
+
+
+def in_pairs(count):
+    def plan(me):
+        steps = range(0, count, 2)
+        near = near_of(me)
+        return [lax.rem(me + d, count) for d in steps], [[lax.rem(near + d, count) for d in steps]]
+
+    return plan
 
 
 def outer_kernel(i_n, j_n, row_n, col_n, *refs):
     depth = PROJECTED_DEPTH
     a_pieces, refs = refs[: col_n // 2], refs[col_n // 2 :]
     b_pieces, refs = refs[: row_n // 2], refs[row_n // 2 :]
-    (g_ref, bias_ref, x_ref, a_wide, b_wide), refs = refs[:5], refs[5:]
-    messages, refs = refs[:row_n], refs[row_n:]
-    a_held, b_held, left, diagonal, total = refs
+    g_ref, bias_ref, x_ref, a_wide, b_wide, kept, message = refs[:7]
+    a_held, b_held, left, diagonal, total = refs[7:]
     sequences = a_held.shape[0]
     groups = i_n // GROUP
     per_step = depth // CHUNKS
@@ -216,7 +250,7 @@
                 block = jnp.where(mask, a_wide[l, start : start + depth, :], block)
             left[k * depth : (k + 1) * depth, l * LANES : (l + 1) * LANES] = block.astype(BF16)
     spread(b_held, b_wide)
-    diagonal[...] = jnp.zeros(diagonal.shape, BF16)
+    clear_off_diagonal(diagonal, j_n, sequences)
 
     @pl.loop(0, CHUNKS)
     def _(t):
@@ -237,12 +271,14 @@
 
     share = total.shape[0] // row_n
     me = lax.axis_index("row")
-    for p, message in enumerate(messages):
-        start = lax.rem(me + p, row_n) * (share // depth)
-        for n in range(share // depth):
-            block = total[pl.ds(start + n, depth, stride=depth), :]
-            message[n * depth : (n + 1) * depth, :] = block.astype(message.dtype)
-        message[share:, :] = bias_ref[...].astype(message.dtype)
+    stay, (go,) = in_pairs(row_n)(me)
+    for out, parts in ((kept, stay), (message, go)):
+        for p, part in enumerate(parts):
+            for n in range(share // depth):
+                block = total[pl.ds(part * (share // depth) + n, depth, stride=depth), :]
+                first = p * share + n * depth
+                out[first : first + depth, :] = block.astype(out.dtype)
+    message[len(go) * share :, :] = bias_ref[...]
 
 
 def outer(a_pieces, b_pieces, g, bias_rows, i_n, j_n, sequences):
@@ -250,13 +286,15 @@
     depth = PROJECTED_DEPTH
     channels = depth * depth
     pairs = i_n * j_n
-    share = channels // row_n
     tiles = GROUP * sequences // LANES
     operands = [*a_pieces, *b_pieces, g, bias_rows]
     shapes = [jax.ShapeDtypeStruct((channels, pairs), BF16)]
     shapes += [jax.ShapeDtypeStruct((tiles, n * depth, LANES), F32) for n in (i_n, j_n)]
-    shapes += parts_shapes(row_n, share + BIAS_ROWS)
-    results = pl.pallas_call(
+    shapes += [
+        jax.ShapeDtypeStruct((channels // 2, LANES), F32),
+        jax.ShapeDtypeStruct((channels // 2 + BIAS_ROWS, LANES), BF16),
+    ]
+    return pl.pallas_call(
         functools.partial(outer_kernel, i_n, j_n, row_n, col_n),
         in_specs=[in_vmem()] * len(operands),
         out_specs=[in_vmem()] * len(shapes),
@@ -275,35 +313,25 @@
             transcendentals=0,
         ),
     )(*operands)
-    return *results[:3], results[3:]
-
-
-def in_order(count):
-    return lambda me: ([me], [[lax.rem(me + d, count)] for d in range(1, count)])
-
-
-def in_pairs(count):
-    def plan(me):
-        near = me + 1 - 2 * lax.rem(me, 2)
-        steps = range(0, count, 2)
-        return [lax.rem(me + d, count) for d in steps], [[lax.rem(near + d, count) for d in steps]]
-
-    return plan
-
-
-def gradient_kernel(axis, plan, kept, positions, others, sequences, *refs):
+
+
+def gradient_kernel(axis, plan, kept, positions, others, sequences, chunks, *refs):
     depth = PROJECTED_DEPTH
     wide, source, _ = refs[:3]
-    outs = refs[3:-4]
-    diagonal, result, grown, grad = refs[-4:]
+    first, last = chunks[0] == 0, chunks[-1] == CHUNKS - 1
+    before, refs = (None, refs[3:]) if first else (refs[3], refs[4:])
+    if last:
+        outs, (diagonal, result, grown, grad) = refs[:-4], refs[-4:]
+    else:
+        result, diagonal = refs
     parts = lax.axis_size(axis)
     per_step = depth // CHUNKS
     span = GROUP * others
 
-    diagonal[...] = jnp.zeros(diagonal.shape, BF16)
-    result[...] = jnp.zeros(result.shape, F32)
-
-    @pl.loop(0, CHUNKS)
+    clear_off_diagonal(diagonal, others, sequences)
+    result[...] = jnp.zeros(result.shape, F32) if first else before[...]
+
+    @pl.loop(chunks[0], chunks[-1] + 1)
     def _(t):
         for n in range(per_step):
             fill_diagonal(wide, diagonal, n, t * per_step + n, others, sequences)
@@ -326,6 +354,8 @@
                 diagonal[n : n + 2].reshape(2 * span, diagonal.shape[2]),
             )
 
+    if not last:
+        return
     scaled = (result[...] * (1.0 / sequences)).astype(BF16)
     for l in range(scaled.shape[1] // LANES):
         members = dict(tiles_of(sequences, l))
@@ -356,42 +386,67 @@
             out[n * size : (n + 1) * size, :] = rows_of(p).astype(BF16)
 
 
-def gradient(wide, source, after, axis, plan, kept, groups, positions, others, sequences):
+def gradient_call(kernel, operands, after, shapes, scratch, others, sequences, flops):
+    specs = [in_vmem()] * len(operands)
+    specs.insert(2, pl.BlockSpec(memory_space=pl.ANY))
+    diagonal = pltpu.VMEM((PROJECTED_DEPTH // CHUNKS, GROUP * others, GROUP * sequences), BF16)
+    return pl.pallas_call(
+        kernel,
+        in_specs=specs,
+        out_specs=[in_vmem()] * len(shapes),
+        out_shape=shapes,
+        scratch_shapes=[diagonal, *scratch],
+        compiler_params=params(sequences),
+        cost_estimate=pl.CostEstimate(
+            flops=flops, bytes_accessed=2 * operands[1].size, transcendentals=0
+        ),
+    )(*operands[:2], after, *operands[2:])
+
+
+def gradient_start(wide, source, after, axis, positions, others, sequences):
+    shape = (positions // GROUP * PROJECTED_DEPTH, GROUP * sequences)
+    chunks = range(CHUNKS // 2)
+    (before,) = gradient_call(
+        functools.partial(gradient_kernel, axis, None, 0, positions, others, sequences, chunks),
+        [wide, source],
+        after,
+        [jax.ShapeDtypeStruct(shape, F32)],
+        [],
+        others,
+        sequences,
+        source.size * PAIR_FEATURES,
+    )
+    return before
+
+
+def gradient(wide, source, after, axis, plan, kept, groups, positions, others, sequences, before=None):
     depth = PROJECTED_DEPTH
-    channels, pairs = depth * depth, positions * others
     parts = lax.axis_size(axis)
     rows = sequences // parts * positions * depth // LANES
-    group = (parts - kept) // groups
     shapes = [jax.ShapeDtypeStruct((rows, LANES), F32)] * kept
-    shapes += [jax.ShapeDtypeStruct((group * rows, LANES), BF16)] * groups
-    results = pl.pallas_call(
-        functools.partial(gradient_kernel, axis, plan, kept, positions, others, sequences),
-        in_specs=[in_vmem(), in_vmem(), pl.BlockSpec(memory_space=pl.ANY)],
-        out_specs=[in_vmem()] * len(shapes),
-        out_shape=shapes,
-        scratch_shapes=[
-            pltpu.VMEM((depth // CHUNKS, GROUP * others, GROUP * sequences), BF16),
+    if groups > 0:
+        group = (parts - kept) // groups
+        shapes += [jax.ShapeDtypeStruct((group * rows, LANES), BF16)] * groups
+    chunks = range(0 if before is None else CHUNKS // 2, CHUNKS)
+    results = gradient_call(
+        functools.partial(gradient_kernel, axis, plan, kept, positions, others, sequences, chunks),
+        [wide, source] + ([] if before is None else [before]),
+        after,
+        shapes,
+        [
             pltpu.VMEM((positions // GROUP * depth, GROUP * sequences), F32),
             pltpu.VMEM((positions * depth, GROUP * sequences), BF16),
             pltpu.VMEM((sequences, positions * depth), F32),
         ],
-        compiler_params=params(sequences),
-        cost_estimate=pl.CostEstimate(
-            flops=2 * pairs * channels * PAIR_FEATURES,
-            bytes_accessed=2 * pairs * channels,
-            transcendentals=0,
-        ),
-    )(wide, source, after)
+        others,
+        sequences,
+        2 * source.size * PAIR_FEATURES,
+    )
     return results[:kept], results[kept:]
 
 
 def product_kernel(left_ref, right_ref, _, out_ref):
-    size = out_ref.shape[0] // STEPS
-
-    @pl.loop(0, STEPS)
-    def _(t):
-        rows = pl.ds(pl.multiple_of(t * size, size), size)
-        out_ref[rows, :] = dot(left_ref[rows, :], right_ref[...], ROWS_BY_ROWS).astype(BF16)
+    multiply(left_ref, right_ref, out_ref)
 
 
 def product(left, right, after):
@@ -410,7 +465,8 @@
     )(left, right, after)
 
 
-def pair_kernel(sequences, x_ref, wt_ref, bias_ref, out_ref):
+def pair_kernel(sequences, x_ref, wt_ref, bias_ref, out_ref, done_ref):
+    done_ref[...] = jnp.zeros(done_ref.shape, F32)
     product = dot(wt_ref[...], x_ref[...])
     out_ref[...] = (product.T * (1.0 / sequences) + bias_ref[...]).astype(BF16)
 
@@ -427,8 +483,11 @@
             whole(wt.shape),
             whole((1, PAIR_FEATURES)),
         ],
-        out_specs=pl.BlockSpec((size, PAIR_FEATURES), lambda t: (t, 0)),
-        out_shape=jax.ShapeDtypeStruct((pairs, PAIR_FEATURES), BF16),
+        out_specs=[pl.BlockSpec((size, PAIR_FEATURES), lambda t: (t, 0)), whole((8, LANES))],
+        out_shape=[
+            jax.ShapeDtypeStruct((pairs, PAIR_FEATURES), BF16),
+            jax.ShapeDtypeStruct((8, LANES), F32),
+        ],
         compiler_params=params(),
         cost_estimate=pl.CostEstimate(
             flops=4 * pairs * channels * PAIR_FEATURES,
@@ -443,125 +502,160 @@
         out[:, l * LANES : (l + 1) * LANES] = total[l * share : (l + 1) * share, :]
 
 
-def row_sum_kernel(*refs):
-    parts, grad, message = refs[:-2], refs[-2], refs[-1]
-    rows = parts[0].shape[0]
-    total = parts[0][...]
-    for part in parts[1:]:
-        total += part[...].astype(F32)
-    message[0:rows, :] = total.astype(BF16)
-    message[rows:, :] = grad[...]
-
-
-def row_sum(parts, grad):
-    shape = (parts[0].shape[0] + grad.shape[0], LANES)
+def call(kernel, operands, shapes, after=()):
+    specs = [in_vmem()] * len(operands) + [pl.BlockSpec(memory_space=pl.ANY)] * len(after)
     return pl.pallas_call(
-        row_sum_kernel,
-        in_specs=[in_vmem()] * (len(parts) + 1),
-        out_specs=in_vmem(),
-        out_shape=jax.ShapeDtypeStruct(shape, BF16),
+        kernel,
+        in_specs=specs,
+        out_specs=[in_vmem()] * len(shapes),
+        out_shape=[jax.ShapeDtypeStruct(shape, kind) for shape, kind in shapes],
         compiler_params=params(),
-    )(*parts, grad)
-
-
-def pair_sum_kernel(rows, own, near, _, *refs):
-    count = len(refs) // 2
-    grads, left_out, messages = refs[:count], refs[count], refs[count + 1 :]
-    total = (own[0:rows, :].astype(F32) + near[0:rows, :].astype(F32)).astype(BF16)
-    size = left_out.shape[0]
-    for n, grad in enumerate(grads):
-        both = grad[...] + near[rows + n * size : rows + (n + 1) * size, :].astype(F32)
-        if n == 0:
-            left_out[...] = both
-        else:
-            messages[n - 1][0:rows, :] = total
-            messages[n - 1][rows:, :] = both.astype(BF16)
-
-
-def pair_sum(own, near, after, grads, rows):
+    )(*operands, *after)
+
+
+def row_pair_sum(kept, bias, near, after, share):
+    count = kept.shape[0] // share
+
+    def kernel(kept, bias, near, _, own, bias_out, *messages):
+        total = split(joined(bias[...]) + joined(near[count * share :, :]))
+        bias_out[...] = total
+        for p in range(count):
+            rows = slice(p * share, (p + 1) * share)
+            both = kept[rows, :] + near[rows, :].astype(F32)
+            if p == 0:
+                own[...] = both
+            else:
+                messages[p - 1][0:share, :] = both.astype(BF16)
+                messages[p - 1][share:, :] = total
+
+    shapes = [((share, LANES), F32), (bias.shape, BF16)]
+    shapes += [((share + BIAS_ROWS, LANES), BF16)] * (count - 1)
+    own, bias, *messages = call(kernel, [kept, bias, near], shapes, [after])
+    return own, bias, messages
+
+
+def row_sum(own, bias, parts, grad):
+    share = own.shape[0]
+
+    def kernel(own, bias, *refs):
+        parts, grad, message = refs[:-2], refs[-2], refs[-1]
+        total, bias_total = own[...], joined(bias[...])
+        for part in parts:
+            total += part[0:share, :].astype(F32)
+            bias_total += joined(part[share:, :])
+        message[0:share, :] = total.astype(BF16)
+        message[share : share + BIAS_ROWS, :] = split(bias_total)
+        message[share + BIAS_ROWS :, :] = grad[...]
+
+    shape = (share + BIAS_ROWS + grad.shape[0], LANES)
+    (message,) = call(kernel, [own, bias, *parts, grad], [(shape, BF16)])
+    return message
+
+
+def column_pair_sum(own, near, grads, after, share):
+    rows = share + BIAS_ROWS
     size = grads[0].shape[0]
-    shapes = [jax.ShapeDtypeStruct((size, LANES), F32)]
-    shapes += [jax.ShapeDtypeStruct((rows + size, LANES), BF16)] * (len(grads) - 1)
-    left, *messages = pl.pallas_call(
-        functools.partial(pair_sum_kernel, rows),
-        in_specs=[in_vmem()] * 2 + [pl.BlockSpec(memory_space=pl.ANY)] + [in_vmem()] * len(grads),
-        out_specs=[in_vmem()] * len(shapes),
-        out_shape=shapes,
-        compiler_params=params(),
-    )(own, near, after, *grads)
+
+    def kernel(own, near, *refs):
+        grads, left_out, messages = refs[: len(grad_list)], refs[len(grad_list) + 1], refs[len(grad_list) + 2 :]
+        total = (own[0:share, :].astype(F32) + near[0:share, :].astype(F32)).astype(BF16)
+        bias = split(joined(own[share:rows, :]) + joined(near[share:rows, :]))
+        for n, grad in enumerate(grads):
+            both = grad[...] + near[rows + n * size : rows + (n + 1) * size, :].astype(F32)
+            if n == 0:
+                left_out[...] = both
+            else:
+                messages[n - 1][0:share, :] = total
+                messages[n - 1][share:rows, :] = bias
+                messages[n - 1][rows:, :] = both.astype(BF16)
+
+    grad_list = list(grads)
+    shapes = [((size, LANES), F32)] + [((rows + size, LANES), BF16)] * (len(grad_list) - 1)
+    left, *messages = call(kernel, [own, near, *grad_list], shapes, [after])
     return left, messages
 
 
-def column_sum_kernel(res_total, count, *refs):
-    parts, grad, refs = refs[: count - 1], refs[count - 1], refs[count:]
-    own, refs = refs[0], refs[1:]
-    grads, refs = refs[: (len(refs) - 4) // 2], refs[(len(refs) - 4) // 2 :]
-    messages, (piece_out, left_out, bias_out, held) = refs[:-4], refs[-4:]
-    share = piece_out.shape[0]
+def column_sum(parts, left_own, own, grads, share, left_shape, res_total):
     rows = share + BIAS_ROWS
-    home = lax.div(lax.axis_index("col"), 2)
-    for p, part in enumerate((own, *parts)):
-        held[lax.rem(home - p + count, count)] = part[0:rows, :]
-    total = held[0].astype(F32)
-    for n in range(1, count):
-        total += held[n].astype(F32)
-    piece = total[0:share].astype(BF16)
-    piece_out[...] = piece
-    for message, other in zip(messages, grads, strict=True):
-        message[0:share, :] = piece
-        message[share:, :] = other[...]
-    bias_out[...] = (total[share : share + 1] + total[share + 1 : share + 2]) * (1.0 / res_total)
-    left = grad[...]
-    for part in parts:
-        left += part[rows:, :].astype(F32)
-    unfold(left, left_out.shape[0], left_out)
-
-
-def column_sum(parts, left_own, own, grads, share, left_shape, res_total):
-    rows = share + grads[0].shape[0]
-    operands = [*parts, left_own, own, *grads]
-    shapes = [jax.ShapeDtypeStruct((rows, LANES), BF16)] * len(grads) + [
+    count = len(parts) + 1
+
+    def kernel(*refs):
+        parts, grad, own, refs = refs[: count - 1], refs[count - 1], refs[count], refs[count + 1 :]
+        grads, refs = refs[: len(grad_list)], refs[len(grad_list) :]
+        messages, (piece_out, left_out, bias_out, held) = refs[:-4], refs[-4:]
+        home = lax.div(lax.axis_index("col"), 2)
+        for p, part in enumerate((own, *parts)):
+            held[lax.rem(home - p + count, count)] = part[0:rows, :]
+        total, bias = held[0, 0:share, :].astype(F32), joined(held[0, share:, :])
+        for n in range(1, count):
+            total += held[n, 0:share, :].astype(F32)
+            bias += joined(held[n, share:, :])
+        piece = total.astype(BF16)
+        piece_out[...] = piece
+        for message, other in zip(messages, grads, strict=True):
+            message[0:share, :] = piece
+            message[share:, :] = other[...]
+        bias_out[...] = bias * (1.0 / res_total)
+        left = grad[...]
+        for part in parts:
+            left += part[rows:, :].astype(F32)
+        unfold(left, left_out.shape[0], left_out)
+
+    grad_list = list(grads)
+    operands = [*parts, left_own, own, *grad_list]
+    shapes = [
+        jax.ShapeDtypeStruct((share + grad.shape[0], LANES), BF16) for grad in grad_list
+    ] + [
         jax.ShapeDtypeStruct((share, LANES), BF16),
         jax.ShapeDtypeStruct(left_shape, F32),
         jax.ShapeDtypeStruct((1, PAIR_FEATURES), F32),
     ]
     *messages, piece, left, bias = pl.pallas_call(
-        functools.partial(column_sum_kernel, res_total, len(parts) + 1),
+        kernel,
         in_specs=[in_vmem()] * len(operands),
         out_specs=[in_vmem()] * len(shapes),
         out_shape=shapes,
-        scratch_shapes=[pltpu.VMEM((len(parts) + 1, share + BIAS_ROWS, LANES), BF16)],
+        scratch_shapes=[pltpu.VMEM((count, rows, LANES), BF16)],
         compiler_params=params(),
     )(*operands)
     return messages, piece, left, bias
 
 
-def finish_kernel(scale, *refs):
-    parts, (piece, grad, projection, right_out) = refs[:-4], refs[-4:]
-    row_n = len(parts) + 1
-    share = piece.shape[0]
-    me = lax.axis_index("row")
-    right = grad[...]
-    for p, part in enumerate((piece, *parts)):
-        start = pl.multiple_of(lax.rem(me - p + row_n, row_n) * share, share)
-        projection[pl.ds(start, share), :] = part[0:share, :].astype(F32) * scale
-        if p > 0:
-            right += part[share:, :].astype(F32)
-    unfold(right, right_out.shape[0], right_out)
-
-
-def finish(parts, piece, right_own, right_shape, scale):
-    operands = [*parts, piece, right_own]
-    return pl.pallas_call(
-        functools.partial(finish_kernel, scale),
-        in_specs=[in_vmem()] * len(operands),
-        out_specs=[in_vmem()] * 2,
-        out_shape=[
-            jax.ShapeDtypeStruct((piece.shape[0] * (len(parts) + 1), PAIR_FEATURES), F32),
-            jax.ShapeDtypeStruct(right_shape, F32),
-        ],
-        compiler_params=params(),
-    )(*operands)
+def finish_pairs(piece, grads, parts, after):
+    share, size = piece.shape[0], grads[0].shape[0]
+    count = len(parts) + 1
+
+    def kernel(piece, own, other, *refs):
+        parts, (message, right_out) = refs[: count - 1], refs[-2:]
+        message[0:share, :] = piece[...]
+        mine, theirs = own[...], other[...]
+        for p, part in enumerate(parts, 1):
+            message[p * share : (p + 1) * share, :] = part[0:share, :]
+            mine += part[share : share + size, :].astype(F32)
+            theirs += part[share + size :, :].astype(F32)
+        message[count * share :, :] = theirs.astype(BF16)
+        right_out[...] = mine
+
+    shapes = [((count * share + size, LANES), BF16), ((size, LANES), F32)]
+    return call(kernel, [piece, *grads, *parts], shapes, [after])
+
+
+def finish(own, near, right_own, right_shape, share, scale):
+    count = lax.axis_size("row") // 2
+
+    def kernel(own, near, right_own, projection, right_out):
+        me = lax.axis_index("row")
+        home, odd = lax.div(me, 2), lax.rem(me, 2)
+        for ref, parity in ((own, odd), (near, 1 - odd)):
+            for p in range(count):
+                place = 2 * lax.rem(home - p + count, count) + parity
+                rows = pl.ds(pl.multiple_of(place * share, share), share)
+                projection[rows, :] = ref[p * share : (p + 1) * share, :].astype(F32) * scale
+        right = right_own[...] + near[count * share :, :].astype(F32)
+        unfold(right, right_out.shape[0], right_out)
+
+    shapes = [((2 * count * share, PAIR_FEATURES), F32), (right_shape, F32)]
+    return call(kernel, [own, near, right_own], shapes)
 
 
 def shift(x, axis, distance):
@@ -577,8 +671,8 @@
     return [x] + [shift(x, axis, d) for d in range(2, lax.axis_size(axis), 2)]
 
 
-def exchange(parts, axis):
-    return [shift(part, axis, d) for d, part in enumerate(parts, 1)]
+def send_pairs(parts, axis):
+    return [shift(part, axis, 2 * p) for p, part in enumerate(parts, 1)]
 
 
 def local(
@@ -602,37 +696,41 @@
     b_pieces = shift_pairs(b_pair, "row")
     y, gt, bias_rows = prepare(we, g, i_n, j_n)
 
-    x, a_wide, b_wide, (row_own, *messages) = outer(
+    x, a_wide, b_wide, kept, message = outer(
         a_pieces, b_pieces, g, bias_rows, i_n, j_n, sequences
     )
-    row_parts = [row_own] + exchange(messages, "row")
+    share = channels // row_n
+
+    near = neighbour(message, "row")
+    before = gradient_start(b_wide, y, message, "col", i_n, j_n, sequences)
+    own, bias, messages = row_pair_sum(kept, bias_rows, near, before, share)
+    parts = send_pairs(messages, "row")
     left_kept, (left_sent,) = gradient(
-        b_wide, y, row_own, "col", in_pairs(col_n), col_n // 2, 1, i_n, j_n, sequences
-    )
-    message = row_sum(row_parts, left_sent)
+        b_wide, y, bias, "col", in_pairs(col_n), col_n // 2, 1, i_n, j_n, sequences, before
+    )
+
+    message = row_sum(own, bias, parts, left_sent)
     near = neighbour(message, "col")
     y2 = product(w, gt, message)
-    left_own, messages = pair_sum(message, near, y2, left_kept, row_own.shape[0])
-    col_parts = [shift(part, "col", 2 * d) for d, part in enumerate(messages, 1)]
-    (right_own,), right_grads = gradient(
-        a_wide, y2, messages[0], "row", in_order(row_n), 1, row_n - 1, j_n, i_n, sequences
-    )
+    left_own, messages = column_pair_sum(message, near, left_kept, y2, share)
+    parts = send_pairs(messages, "col")
+    right_kept, right_sent = gradient(
+        a_wide, y2, left_own, "row", by_pairs(row_n), 2, row_n // 2 - 1, j_n, i_n, sequences
+    )
+
     messages, piece, left_grad, bias_grad = column_sum(
-        col_parts,
-        left_own,
-        messages[0],
-        right_grads,
-        channels // row_n,
-        first_homolog_features.shape,
-        res_total,
-    )
-    row_parts = exchange(messages, "row")
-    pair_map = pair(x, wt, output_bias, sequences)
+        parts, left_own, messages[0], right_sent, share, first_homolog_features.shape, res_total
+    )
+    parts = send_pairs(messages, "row")
+    pair_map, pair_done = pair(x, wt, output_bias, sequences)
+    message, right_own = finish_pairs(piece, right_kept, parts, pair_done)
+    near = neighbour(message, "row")
     projection, right_grad = finish(
-        row_parts,
-        piece,
+        message,
+        near,
         right_own,
         second_homolog_features.shape,
+        share,
         1.0 / (sequences * res_total),
     )
     return (

time: 44 us -> 43.2 us (0.982)
  starting transfers between devices: 17.6 us -> 13.7 us
  waiting for transfers between devices: 3.57 us -> 7.46 us
  Pallas kernels: 21.9 us -> 21.2 us
    ppermute x9 -> x5, starting transfers between devices: 12.9 us -> 8.83 us  [shift(): lax.ppermute(x, axis, [(n, (n + distance) % count) for n in range(count)])]
    ppermute x9 -> x5, waiting for transfers between devices: 1.58 us -> 3.58 us  [shift(): lax.ppermute(x, axis, [(n, (n + distance) % count) for n in range(count)])]
    ppermute x3 -> x5, waiting for transfers between devices: 1.99 us -> 3.88 us  [neighbour(): lax.ppermute(x, axis, [(n, n ^ 1) for n in range(lax.axis_size(axis))])]
    pallas_call x1, Pallas kernels: 2.65 us -> 1.75 us  [prepare(): pl.pallas_call(functools.partial(prepare_kernel, i_n, j_n), in_specs=[in_...]
    pallas_call x1, Pallas kernels: 1.88 us -> 1.38 us  [product(): pl.pallas_call(product_kernel, in_specs=[in_vmem(), in_vmem(), pl.BlockSp...]
    pallas_call x6 -> x9, Pallas kernels: 8.14 us -> 8.58 us  [the longest x3 6.98 us: gradient_call(): pl.pallas_call(kernel, in_specs=specs, out_specs=[in_vmem()] * len(shapes...]
    ppermute x3 -> x5, starting transfers between devices: 4.73 us -> 4.88 us  [neighbour(): lax.ppermute(x, axis, [(n, n ^ 1) for n in range(lax.axis_size(axis))])]
  transfers between devices with their start and end apart: 12 -> 10, of which waited for: 4 -> 7; matrix products, arithmetic and copies ran while one was open for 0% -> 0% of each run, Pallas kernels for 34% -> 33%
where the time goes in v8:
time: 43.2 us; the launch traced here: 43.1 us
  Pallas kernels  21.2 us (49%)
  starting transfers between devices  13.7 us (32%)
  waiting for transfers between devices  7.46 us (17%)
  between operations  0.73 us (2%)
    ppermute x5, starting transfers between devices, shift(): lax.ppermute(x, axis, [(n, (n + distance) % count) for n in range(count)])  8.83 us
    pallas_call x3, Pallas kernels, gradient_call(): pl.pallas_call(kernel, in_specs=specs, out_specs=[in_vmem()] * len(shapes...  6.98 us
    pallas_call x1, Pallas kernels, outer(): pl.pallas_call(functools.partial(outer_kernel, i_n, j_n, row_n, col_n), i...  5.49 us
    ppermute x5, starting transfers between devices, neighbour(): lax.ppermute(x, axis, [(n, n ^ 1) for n in range(lax.axis_size(axis))])  4.88 us
    ppermute x5, waiting for transfers between devices, neighbour(): lax.ppermute(x, axis, [(n, n ^ 1) for n in range(lax.axis_size(axis))])  3.88 us
    ppermute x5, waiting for transfers between devices, shift(): lax.ppermute(x, axis, [(n, (n + distance) % count) for n in range(count)])  3.58 us
    pallas_call x1, Pallas kernels, pair(): pl.pallas_call(functools.partial(pair_kernel, sequences), grid=(count,),...  2.55 us
    pallas_call x1, Pallas kernels, prepare(): pl.pallas_call(functools.partial(prepare_kernel, i_n, j_n), in_specs=[in_...  1.75 us
  transfers between devices with their start and end apart: 10, of which 7 were waited for; matrix products, arithmetic and copies ran while one was open for 0% of the time, Pallas kernels for 33%

profile of v8, /device:TPU:0, one launch (start us, length us, event | category | flops | bytes accessed | tf_op | source)
XLA Modules:
  0.0 43.1 jit_solution(7834571715100797832)
XLA Ops:
  0.6 3.1 %collective-permute-start = (bf16[8,1536]{1,0:T(8,128)(2,1)}, bf16[8,1536]{1,0:T(8,128)(2,1)S(1)}, u32[]{:S(2)}, u32[]{:S(2)}) collective-permute-start(bf16[8,1536]{1,0:T(8,128)(2,1)} %a_hbm.1), channel_id=1, source_target_pairs={{0,1},{1,0},{2,3},{3,2},{4,5},{5,4},{6,7},{7,6},{8,9},{9,8},{10,11... | collective-permute-start | bytes 73736 | tf_op jit(solution)/shard_map/ppermute | solution.py:667
  3.7 0.0 collective-permute-start.1
  3.7 1.4 %shard_map.92 = (bf16[1024,128]{1,0:T(8,128)(2,1)S(1)}, bf16[128,1024]{1,0:T(8,128)(2,1)S(1)}, bf16[8,1536]{1,0:T(8,128)(2,1)S(1)}, bf16[8,1536]{1,0:T(8,128)(2,...) custom-call(bf16[8,1536]{1,0:T(8,128)(2,1)} %a_hbm.1, bf16[8,1536]{1,0:T(8,128)(2,1)} %b_hbm.1, ...), custom_call_target="tpu_custom_call" | custom-call | flops 131072000 | bytes 2097152 | tf_op jit(solution)/shard_map/pallas_call | solution.py:67
  5.1 0.6 %collective-permute-done.refs_1_ = bf16[8,1536]{1,0:T(8,128)(2,1)S(1)} collective-permute-done((bf16[8,1536]{1,0:T(8,128)(2,1)}, bf16[8,1536]{1,0:T(8,128)(2,1)S(1)}, u32[]{:S(2)}, u32[]{:S(2)}) %collective-permute-start) | collective-permute-done | bytes 24608 | tf_op jit(solution)/shard_map/ppermute | solution.py:667
  5.7 0.0 collective-permute-done.1.refs_3_
  5.8 3.1 %collective-permute-start.2 = (bf16[16,1536]{1,0:T(8,128)(2,1)S(1)}, bf16[16,1536]{1,0:T(8,128)(2,1)S(1)}, u32[]{:S(2)}, u32[]{:S(2)}) collective-permute-start(bf16[16,1536]{1,0:T(8,128)(2,1)S(1)} %get-tuple-element.44.refs_0_), channel_id=1, source_target_pairs={{0,2},{1,3},{2,0},{3,1},{4,6},{5,7},{6,4},{7,5},{8,10},{9,11},{10,... | collective-permute-start | bytes 147464 | tf_op jit(solution)/shard_map/ppermute | solution.py:663
  8.9 1.5 %collective-permute-start.3 = (bf16[16,1536]{1,0:T(8,128)(2,1)S(1)}, bf16[16,1536]{1,0:T(8,128)(2,1)S(1)}, u32[]{:S(2)}, u32[]{:S(2)}) collective-permute-start(bf16[16,1536]{1,0:T(8,128)(2,1)S(1)} %get-tuple-element.45.refs_2_), channel_id=1, source_target_pairs={{0,8},{4,12},{8,0},{12,4},{1,9},{5,13},{9,1},{13,5},{2,10},{6,14},... | collective-permute-start | bytes 147464 | tf_op jit(solution)/shard_map/ppermute | solution.py:663
  10.3 1.8 %shard_map.94 = (bf16[1024,2304]{1,0:T(8,128)(2,1)S(1)}, bf16[2304,128]{1,0:T(8,128)(2,1)S(1)}, bf16[16,128]{1,0:T(8,128)(2,1)S(1)}) custom-call(bf16[1024,128]{1,0:T(8,128)(2,1)S(1)} %get-tuple-element.47.we_ref, bf16[2304,128]{1,0:T(8,128)(2,1)S(1)} %get-tuple-element.46.g_ref.refs_4_), custom_call_target="tpu_custom_call" | custom-call | flops 603979776 | bytes 9437184 | tf_op jit(solution)/shard_map/pallas_call | solution.py:137
  12.1 0.0 collective-permute-done.2.refs_1_
  12.1 0.8 %collective-permute-done.3.refs_3_ = bf16[16,1536]{1,0:T(8,128)(2,1)S(1)} collective-permute-done((bf16[16,1536]{1,0:T(8,128)(2,1)S(1)}, bf16[16,1536]{1,0:T(8,128)(2,1)S(1)}, u32[]{:S(2)}, u32[]{:S(2)}) %collective-permute-start.3) | collective-permute-done | bytes 49184 | tf_op jit(solution)/shard_map/ppermute | solution.py:663
  12.9 5.5 %shard_map.95 = (bf16[1024,2304]{1,0:T(8,128)(2,1)S(1)}, f32[2,1536,128]{2,1,0:T(8,128)S(1)}, f32[2,1536,128]{2,1,0:T(8,128)S(1)}, f32[512,128]{1,0:T(8,128)S(1)}, bf16[528,128]{1,0:T(8,128)(2,1)S(1)}) custom-call(bf16[16,1536]{1,0:T(8,128)(2,1)S(1)} %get-tuple-element.44.refs_0_, bf16[16,1536]{1,0:T(8,128)(2,1)S(1)} %collective-permute-done.2.refs_1_, ...), custom_call_target="tpu_custom_call" | custom-call | flops 1207959552 | bytes 4718592 | tf_op jit(solution)/shard_map/pallas_call | solution.py:297
  18.4 0.1 collective-permute-start.4
  18.5 1.6 %shard_map.97._.refs_3_ = f32[192,256]{1,0:T(8,128)S(1)} custom-call(f32[2,1536,128]{2,1,0:T(8,128)S(1)} %get-tuple-element.54.refs_0_, bf16[1024,2304]{1,0:T(8,128)(2,1)S(1)} %get-tuple-element.55.refs_1_, bf16[528,128]{1,0:T(8,128)(2,1)S(1)} %get-tuple-element.53.refs_2_), custom_call_target="tpu_custom_call" | custom-call | flops 301989888 | bytes 4718592 | tf_op jit(solution)/shard_map/pallas_call | solution.py:393
  20.1 0.0 collective-permute-done.4.near
  20.1 1.6 %collective-permute-start.5 = (bf16[272,128]{1,0:T(8,128)(2,1)S(1)}, bf16[272,128]{1,0:T(8,128)(2,1)S(1)}, u32[]{:S(2)}, u32[]{:S(2)}) collective-permute-start(bf16[272,128]{1,0:T(8,128)(2,1)S(1)} %get-tuple-element.58), channel_id=1, source_target_pairs={{0,8},{4,12},{8,0},{12,4},{1,9},{5,13},{9,1},{13,5},{2,10},{6,14},... | collective-permute-start | bytes 208904 | tf_op jit(solution)/shard_map/ppermute | solution.py:663
  21.7 2.2 %shard_map.99 = (f32[96,128]{1,0:T(8,128)S(1)}, f32[96,128]{1,0:T(8,128)S(1)}, bf16[192,128]{1,0:T(8,128)(2,1)S(1)}) custom-call(f32[2,1536,128]{2,1,0:T(8,128)S(1)} %get-tuple-element.54.refs_0_, bf16[1024,2304]{1,0:T(8,128)(2,1)S(1)} %get-tuple-element.55.refs_1_, bf16[16,128]{1,0:T(8,128)(2,1)S(1)} %get-tuple-element.57.refs_2_.bias, ...), custom_call_target="tpu_custom_call" | custom-call | flops 603979776 | bytes 4718592 | tf_op jit(solution)/shard_map/pallas_call | solution.py:393
  23.8 0.9 %collective-permute-done.5.refs_0_ = bf16[272,128]{1,0:T(8,128)(2,1)S(1)} collective-permute-done((bf16[272,128]{1,0:T(8,128)(2,1)S(1)}, bf16[272,128]{1,0:T(8,128)(2,1)S(1)}, u32[]{:S(2)}, u32[]{:S(2)}) %collective-permute-start.5) | collective-permute-done | bytes 69664 | tf_op jit(solution)/shard_map/ppermute | solution.py:663
  24.8 1.6 %collective-permute-start.6 = (bf16[464,128]{1,0:T(8,128)(2,1)S(1)}, bf16[464,128]{1,0:T(8,128)(2,1)S(1)}, u32[]{:S(2)}, u32[]{:S(2)}) collective-permute-start(bf16[464,128]{1,0:T(8,128)(2,1)S(1)} %shard_map.100._.own), channel_id=1, source_target_pairs={{0,1},{1,0},{2,3},{3,2},{4,5},{5,4},{6,7},{7,6},{8,9},{9,8},{10,11... | collective-permute-start | bytes 356360 | tf_op jit(solution)/shard_map/ppermute | solution.py:667
  26.4 1.4 %shard_map.101.refs_2_.refs_1_ = bf16[1024,2304]{1,0:T(8,128)(2,1)S(1)} custom-call(bf16[1024,128]{1,0:T(8,128)(2,1)S(1)} %get-tuple-element.62.left_ref, bf16[2304,128]{1,0:T(8,128)(2,1)S(1)} %get-tuple-element.63.right_ref, bf16[464,128]{1,0:T(8,128)(2,1)S(1)} %shard_map.100._.own), custom_call_target="tpu_custom_call" | custom-call | flops 603979776 | bytes 9437184 | tf_op jit(solution)/shard_map/pallas_call | solution.py:454
  27.8 1.9 %collective-permute-done.6.near = bf16[464,128]{1,0:T(8,128)(2,1)S(1)} collective-permute-done((bf16[464,128]{1,0:T(8,128)(2,1)S(1)}, bf16[464,128]{1,0:T(8,128)(2,1)S(1)}, u32[]{:S(2)}, u32[]{:S(2)}) %collective-permute-start.6) | collective-permute-done | bytes 118816 | tf_op jit(solution)/shard_map/ppermute | solution.py:667
  29.7 0.0 copy-start
  29.8 1.2 %collective-permute-start.7 = (bf16[368,128]{1,0:T(8,128)(2,1)S(1)}, bf16[368,128]{1,0:T(8,128)(2,1)S(1)}, u32[]{:S(2)}, u32[]{:S(2)}) collective-permute-start(bf16[368,128]{1,0:T(8,128)(2,1)S(1)} %get-tuple-element.64.refs_2_), channel_id=1, source_target_pairs={{0,2},{1,3},{2,0},{3,1},{4,6},{5,7},{6,4},{7,5},{8,10},{9,11},{10,... | collective-permute-start | bytes 282632 | tf_op jit(solution)/shard_map/ppermute | solution.py:663
  31.0 3.3 %shard_map.103 = (f32[96,128]{1,0:T(8,128)S(1)}, f32[96,128]{1,0:T(8,128)S(1)}, bf16[192,128]{1,0:T(8,128)(2,1)S(1)}) custom-call(f32[2,1536,128]{2,1,0:T(8,128)S(1)} %get-tuple-element.66.refs_0_, bf16[1024,2304]{1,0:T(8,128)(2,1)S(1)} %shard_map.101.refs_2_.refs_1_, f32[96,128]{1,0:T(8,128)S(1)} %get-tuple-element.65.refs_2_.refs_1_), custom_call_target="tpu_custom_call" | custom-call | flops 603979776 | bytes 4718592 | tf_op jit(solution)/shard_map/pallas_call | solution.py:393
  34.3 1.1 %collective-permute-done.7.refs_0_ = bf16[368,128]{1,0:T(8,128)(2,1)S(1)} collective-permute-done((bf16[368,128]{1,0:T(8,128)(2,1)S(1)}, bf16[368,128]{1,0:T(8,128)(2,1)S(1)}, u32[]{:S(2)}, u32[]{:S(2)}) %collective-permute-start.7) | collective-permute-done | bytes 94240 | tf_op jit(solution)/shard_map/ppermute | solution.py:663
  35.3 0.6 %shard_map.104 = (bf16[448,128]{1,0:T(8,128)(2,1)S(1)}, bf16[256,128]{1,0:T(8,128)(2,1)S(1)}, f32[8,1536]{1,0:T(8,128)}, f32[1,128]{1,0:T(1,128)}) custom-call(bf16[368,128]{1,0:T(8,128)(2,1)S(1)} %collective-permute-done.7.refs_0_, f32[96,128]{1,0:T(8,128)S(1)} %get-tuple-element.65.refs_2_.refs_1_, bf16[368,128]{1,0:T(8,128)(2,1)S(1)} %get-tuple-element.64.refs_2_, ...), custom_call_target="tpu_custom_call" | custom-call | tf_op jit(solution)/shard_map/pallas_call | solution.py:613
  35.9 1.5 %collective-permute-start.8 = (bf16[448,128]{1,0:T(8,128)(2,1)S(1)}, bf16[448,128]{1,0:T(8,128)(2,1)S(1)}, u32[]{:S(2)}, u32[]{:S(2)}) collective-permute-start(bf16[448,128]{1,0:T(8,128)(2,1)S(1)} %get-tuple-element.72), channel_id=1, source_target_pairs={{0,8},{4,12},{8,0},{12,4},{1,9},{5,13},{9,1},{13,5},{2,10},{6,14},... | collective-permute-start | bytes 344072 | tf_op jit(solution)/shard_map/ppermute | solution.py:663
  37.4 0.0 copy-done
  37.4 2.5 %shard_map.96 = (bf16[2304,128]{1,0:T(8,128)(2,1)}, f32[8,128]{1,0:T(8,128)S(1)}) custom-call(bf16[1024,2304]{1,0:T(8,128)(2,1)S(1)} %get-tuple-element.49.x_ref, bf16[128,1024]{1,0:T(8,128)(2,1)S(1)} %get-tuple-element.50.wt_ref, f32[1,128]{1,0:T(1,128)S(1)} %bitcast.4), custom_call_target="tpu_custom_call" | custom-call | flops 1207959552 | bytes 4718592 | tf_op jit(solution)/shard_map/pallas_call | solution.py:478
  40.0 0.8 %collective-permute-done.8.refs_0_ = bf16[448,128]{1,0:T(8,128)(2,1)S(1)} collective-permute-done((bf16[448,128]{1,0:T(8,128)(2,1)S(1)}, bf16[448,128]{1,0:T(8,128)(2,1)S(1)}, u32[]{:S(2)}, u32[]{:S(2)}) %collective-permute-start.8) | collective-permute-done | bytes 114720 | tf_op jit(solution)/shard_map/ppermute | solution.py:663
  40.8 0.1 collective-permute-start.9
  40.8 1.4 %collective-permute-done.9.near = bf16[608,128]{1,0:T(8,128)(2,1)S(1)} collective-permute-done((bf16[608,128]{1,0:T(8,128)(2,1)S(1)}, bf16[608,128]{1,0:T(8,128)(2,1)S(1)}, u32[]{:S(2)}, u32[]{:S(2)}) %collective-permute-start.9) | collective-permute-done | bytes 155680 | tf_op jit(solution)/shard_map/ppermute | solution.py:667
  42.2 0.9 %shard_map.106 = (f32[1024,128]{1,0:T(8,128)}, f32[8,1536]{1,0:T(8,128)}) custom-call(bf16[608,128]{1,0:T(8,128)(2,1)S(1)} %get-tuple-element.74.own, bf16[608,128]{1,0:T(8,128)(2,1)S(1)} %collective-permute-done.9.near, f32[96,128]{1,0:T(8,128)S(1)} %get-tuple-element.75.right_own), custom_call_target="tpu_custom_call" | custom-call | tf_op jit(solution)/shard_map/pallas_call | solution.py:507
  (5 shorter events, 0.1 us)
Async XLA Ops:
  0.6 5.1 %collective-permute-start = (bf16[8,1536]{1,0:T(8,128)(2,1)}, bf16[8,1536]{1,0:T(8,128)(2,1)S(1)}, u32[]{:S(2)}, u32[]{:S(2)}) collective-permute-start(bf16[8,1536]{1,0:T(8,128)(2,1)} %a_hbm.1), channel_id=1, source_target_pairs={{0,1},{1,0},{2,3},{3,2},{4,5},{5,4},{6,7},{7,6},{8,9},{9,8},{10,11... | collective-permute-start | bytes 73736 | tf_op jit(solution)/shard_map/ppermute | solution.py:667
  3.7 2.0 %collective-permute-start.1 = (bf16[8,1536]{1,0:T(8,128)(2,1)}, bf16[8,1536]{1,0:T(8,128)(2,1)S(1)}, u32[]{:S(2)}, u32[]{:S(2)}) collective-permute-start(bf16[8,1536]{1,0:T(8,128)(2,1)} %b_hbm.1), channel_id=1, source_target_pairs={{0,4},{4,0},{8,12},{12,8},{1,5},{5,1},{9,13},{13,9},{2,6},{6,2},{1... | collective-permute-start | bytes 73736 | tf_op jit(solution)/shard_map/ppermute | solution.py:667
  5.8 6.4 %collective-permute-start.2 = (bf16[16,1536]{1,0:T(8,128)(2,1)S(1)}, bf16[16,1536]{1,0:T(8,128)(2,1)S(1)}, u32[]{:S(2)}, u32[]{:S(2)}) collective-permute-start(bf16[16,1536]{1,0:T(8,128)(2,1)S(1)} %get-tuple-element.44.refs_0_), channel_id=1, source_target_pairs={{0,2},{1,3},{2,0},{3,1},{4,6},{5,7},{6,4},{7,5},{8,10},{9,11},{10,... | collective-permute-start | bytes 147464 | tf_op jit(solution)/shard_map/ppermute | solution.py:663
  8.9 4.1 %collective-permute-start.3 = (bf16[16,1536]{1,0:T(8,128)(2,1)S(1)}, bf16[16,1536]{1,0:T(8,128)(2,1)S(1)}, u32[]{:S(2)}, u32[]{:S(2)}) collective-permute-start(bf16[16,1536]{1,0:T(8,128)(2,1)S(1)} %get-tuple-element.45.refs_2_), channel_id=1, source_target_pairs={{0,8},{4,12},{8,0},{12,4},{1,9},{5,13},{9,1},{13,5},{2,10},{6,14},... | collective-permute-start | bytes 147464 | tf_op jit(solution)/shard_map/ppermute | solution.py:663
  18.4 1.6 %collective-permute-start.4 = (bf16[528,128]{1,0:T(8,128)(2,1)S(1)}, bf16[528,128]{1,0:T(8,128)(2,1)S(1)}, u32[]{:S(2)}, u32[]{:S(2)}) collective-permute-start(bf16[528,128]{1,0:T(8,128)(2,1)S(1)} %get-tuple-element.53.refs_2_), channel_id=1, source_target_pairs={{0,4},{4,0},{8,12},{12,8},{1,5},{5,1},{9,13},{13,9},{2,6},{6,2},{1... | collective-permute-start | bytes 405512 | tf_op jit(solution)/shard_map/ppermute | solution.py:667
  20.1 4.7 %collective-permute-start.5 = (bf16[272,128]{1,0:T(8,128)(2,1)S(1)}, bf16[272,128]{1,0:T(8,128)(2,1)S(1)}, u32[]{:S(2)}, u32[]{:S(2)}) collective-permute-start(bf16[272,128]{1,0:T(8,128)(2,1)S(1)} %get-tuple-element.58), channel_id=1, source_target_pairs={{0,8},{4,12},{8,0},{12,4},{1,9},{5,13},{9,1},{13,5},{2,10},{6,14},... | collective-permute-start | bytes 208904 | tf_op jit(solution)/shard_map/ppermute | solution.py:663
  24.8 4.9 %collective-permute-start.6 = (bf16[464,128]{1,0:T(8,128)(2,1)S(1)}, bf16[464,128]{1,0:T(8,128)(2,1)S(1)}, u32[]{:S(2)}, u32[]{:S(2)}) collective-permute-start(bf16[464,128]{1,0:T(8,128)(2,1)S(1)} %shard_map.100._.own), channel_id=1, source_target_pairs={{0,1},{1,0},{2,3},{3,2},{4,5},{5,4},{6,7},{7,6},{8,9},{9,8},{10,11... | collective-permute-start | bytes 356360 | tf_op jit(solution)/shard_map/ppermute | solution.py:667
  29.7 7.7 %copy-start = (f32[128]{0:T(128)S(1)}, f32[128]{0:T(128)}, u32[]{:S(2)}) copy-start(f32[128]{0:T(128)} %param.8) | copy-start | bytes 1540
  29.8 5.5 %collective-permute-start.7 = (bf16[368,128]{1,0:T(8,128)(2,1)S(1)}, bf16[368,128]{1,0:T(8,128)(2,1)S(1)}, u32[]{:S(2)}, u32[]{:S(2)}) collective-permute-start(bf16[368,128]{1,0:T(8,128)(2,1)S(1)} %get-tuple-element.64.refs_2_), channel_id=1, source_target_pairs={{0,2},{1,3},{2,0},{3,1},{4,6},{5,7},{6,4},{7,5},{8,10},{9,11},{10,... | collective-permute-start | bytes 282632 | tf_op jit(solution)/shard_map/ppermute | solution.py:663
  35.9 4.8 %collective-permute-start.8 = (bf16[448,128]{1,0:T(8,128)(2,1)S(1)}, bf16[448,128]{1,0:T(8,128)(2,1)S(1)}, u32[]{:S(2)}, u32[]{:S(2)}) collective-permute-start(bf16[448,128]{1,0:T(8,128)(2,1)S(1)} %get-tuple-element.72), channel_id=1, source_target_pairs={{0,8},{4,12},{8,0},{12,4},{1,9},{5,13},{9,1},{13,5},{2,10},{6,14},... | collective-permute-start | bytes 344072 | tf_op jit(solution)/shard_map/ppermute | solution.py:663
  40.8 1.4 %collective-permute-start.9 = (bf16[608,128]{1,0:T(8,128)(2,1)S(1)}, bf16[608,128]{1,0:T(8,128)(2,1)S(1)}, u32[]{:S(2)}, u32[]{:S(2)}) collective-permute-start(bf16[608,128]{1,0:T(8,128)(2,1)S(1)} %get-tuple-element.74.own), channel_id=1, source_target_pairs={{0,4},{4,0},{8,12},{12,8},{1,5},{5,1},{9,13},{13,9},{2,6},{6,2},{1... | collective-permute-start | bytes 466952 | tf_op jit(solution)/shard_map/ppermute | solution.py:667

commit v9 on v8

--- a/solution.py
+++ b/solution.py
@@ -185,37 +185,31 @@
     ]
 
 
-def clear_off_diagonal(diagonal, positions, sequences):
-    for l in range(diagonal.shape[2] // LANES):
-        members = dict(tiles_of(sequences, l))
-        for m in range(GROUP):
-            if m not in members:
-                rows = slice(m * positions, (m + 1) * positions)
-                shape = (diagonal.shape[0], positions, LANES)
-                diagonal[:, rows, l * LANES : (l + 1) * LANES] = jnp.zeros(shape, BF16)
-
-
-def fill_diagonal(wide, diagonal, slot, channel, positions, sequences):
+def diagonal_of(wide, channel, positions, sequences):
+    columns = []
     for l in range(wide.shape[0]):
         block = wide[l, pl.ds(channel, positions, stride=PROJECTED_DEPTH), :].astype(BF16)
-        for m, mask in tiles_of(sequences, l):
-            diagonal[slot, m * positions : (m + 1) * positions, l * LANES : (l + 1) * LANES] = (
-                block * mask.astype(F32).astype(BF16)
+        members = dict(tiles_of(sequences, l))
+        columns.append(
+            jnp.concatenate(
+                [
+                    block * members[m].astype(F32).astype(BF16)
+                    if m in members
+                    else jnp.zeros(block.shape, BF16)
+                    for m in range(GROUP)
+                ],
+                axis=0,
             )
+        )
+    return jnp.concatenate(columns, axis=1)
 
 
 def near_of(me):
     return me + 1 - 2 * lax.rem(me, 2)
 
 
-def by_pairs(count):
-    def plan(me):
-        groups = [
-            [lax.rem(me + d, count), lax.rem(near_of(me) + d, count)] for d in range(0, count, 2)
-        ]
-        return groups[0], groups[1:]
-
-    return plan
+def in_order(count):
+    return lambda me: ([me], [[lax.rem(me + d, count)] for d in range(1, count)])
 
 
 def in_pairs(count):
@@ -231,8 +225,8 @@
     depth = PROJECTED_DEPTH
     a_pieces, refs = refs[: col_n // 2], refs[col_n // 2 :]
     b_pieces, refs = refs[: row_n // 2], refs[row_n // 2 :]
-    g_ref, bias_ref, x_ref, a_wide, b_wide, kept, message = refs[:7]
-    a_held, b_held, left, diagonal, total = refs[7:]
+    g_ref, bias_ref, x_ref, a_held, b_wide = refs[:5]
+    messages, (b_held, left, total) = refs[5 : 5 + row_n], refs[5 + row_n :]
     sequences = a_held.shape[0]
     groups = i_n // GROUP
     per_step = depth // CHUNKS
@@ -240,28 +234,28 @@
 
     join(a_pieces, "col", a_held)
     join(b_pieces, "row", b_held)
-    spread(a_held, a_wide)
-    for l in range(a_wide.shape[0]):
-        members = tiles_of(sequences, l)
-        for k in range(groups):
-            block = jnp.zeros((depth, LANES), F32)
-            for m, mask in members:
-                start = (k * GROUP + m) * depth
-                block = jnp.where(mask, a_wide[l, start : start + depth, :], block)
-            left[k * depth : (k + 1) * depth, l * LANES : (l + 1) * LANES] = block.astype(BF16)
     spread(b_held, b_wide)
-    clear_off_diagonal(diagonal, j_n, sequences)
+    turned = a_held[...].T.astype(BF16)
+    shape = (sequences, GROUP * sequences)
+    shifted = lax.broadcasted_iota(jnp.int32, shape, 1) - lax.broadcasted_iota(jnp.int32, shape, 0)
+    value = jnp.zeros(left.shape, F32)
+    for m in range(GROUP):
+        rows = [
+            turned[(k * GROUP + m) * depth : (k * GROUP + m + 1) * depth, :] for k in range(groups)
+        ]
+        value += dot(jnp.concatenate(rows, axis=0), (shifted == m * sequences).astype(BF16))
+    left[...] = value.astype(BF16)
 
     @pl.loop(0, CHUNKS)
     def _(t):
-        for e in range(per_step):
-            fill_diagonal(b_wide, diagonal, e, t * per_step + e, j_n, sequences)
         size = per_step * depth
         rows = pl.ds(pl.multiple_of(t * size, size), size)
         x_part = x_ref.at[rows]
         for e in range(0, per_step, 2):
-            right = diagonal[e : e + 2].reshape(2 * span, diagonal.shape[2])
-            product = dot(left[...], right, ROWS_BY_ROWS).astype(BF16)
+            right = [diagonal_of(b_wide, t * per_step + e + n, j_n, sequences) for n in range(2)]
+            product = dot(
+                left[...], jnp.concatenate(right, axis=0), ROWS_BY_ROWS
+            ).astype(BF16)
             for n in range(2):
                 for k in range(groups):
                     x_part[(e + n) * depth : (e + n + 1) * depth, k * span : (k + 1) * span] = product[
@@ -271,14 +265,12 @@
 
     share = total.shape[0] // row_n
     me = lax.axis_index("row")
-    stay, (go,) = in_pairs(row_n)(me)
-    for out, parts in ((kept, stay), (message, go)):
-        for p, part in enumerate(parts):
-            for n in range(share // depth):
-                block = total[pl.ds(part * (share // depth) + n, depth, stride=depth), :]
-                first = p * share + n * depth
-                out[first : first + depth, :] = block.astype(out.dtype)
-    message[len(go) * share :, :] = bias_ref[...]
+    stay, go = in_order(row_n)(me)
+    for message, (part,) in zip(messages, [stay, *go], strict=True):
+        for n in range(share // depth):
+            block = total[pl.ds(part * (share // depth) + n, depth, stride=depth), :]
+            message[n * depth : (n + 1) * depth, :] = block.astype(message.dtype)
+        message[share:, :] = bias_ref[...].astype(message.dtype)
 
 
 def outer(a_pieces, b_pieces, g, bias_rows, i_n, j_n, sequences):
@@ -289,21 +281,22 @@
     tiles = GROUP * sequences // LANES
     operands = [*a_pieces, *b_pieces, g, bias_rows]
     shapes = [jax.ShapeDtypeStruct((channels, pairs), BF16)]
-    shapes += [jax.ShapeDtypeStruct((tiles, n * depth, LANES), F32) for n in (i_n, j_n)]
     shapes += [
-        jax.ShapeDtypeStruct((channels // 2, LANES), F32),
-        jax.ShapeDtypeStruct((channels // 2 + BIAS_ROWS, LANES), BF16),
-    ]
-    return pl.pallas_call(
+        jax.ShapeDtypeStruct((sequences, i_n * depth), F32),
+        jax.ShapeDtypeStruct((tiles, j_n * depth, LANES), F32),
+    ]
+    shapes += [
+        jax.ShapeDtypeStruct((channels // row_n + BIAS_ROWS, LANES), BF16 if p else F32)
+        for p in range(row_n)
+    ]
+    results = pl.pallas_call(
         functools.partial(outer_kernel, i_n, j_n, row_n, col_n),
         in_specs=[in_vmem()] * len(operands),
         out_specs=[in_vmem()] * len(shapes),
         out_shape=shapes,
         scratch_shapes=[
-            pltpu.VMEM((sequences, i_n * depth), F32),
             pltpu.VMEM((sequences, j_n * depth), F32),
             pltpu.VMEM((i_n // GROUP * depth, GROUP * sequences), BF16),
-            pltpu.VMEM((depth // CHUNKS, GROUP * j_n, GROUP * sequences), BF16),
             pltpu.VMEM((channels, PAIR_FEATURES), F32),
         ],
         compiler_params=params(sequences),
@@ -313,28 +306,24 @@
             transcendentals=0,
         ),
     )(*operands)
-
-
-def gradient_kernel(axis, plan, kept, positions, others, sequences, chunks, *refs):
+    return *results[:3], results[3:]
+
+
+def gradient_kernel(axis, plan, kept, positions, others, sequences, *refs):
     depth = PROJECTED_DEPTH
-    wide, source, _ = refs[:3]
-    first, last = chunks[0] == 0, chunks[-1] == CHUNKS - 1
-    before, refs = (None, refs[3:]) if first else (refs[3], refs[4:])
-    if last:
-        outs, (diagonal, result, grown, grad) = refs[:-4], refs[-4:]
-    else:
-        result, diagonal = refs
+    wide, source = refs[:2]
+    outs, (result, grown, grad, own_wide) = refs[3:-4], refs[-4:]
+    if len(wide.shape) == 2:
+        spread(wide, own_wide)
+        wide = own_wide
     parts = lax.axis_size(axis)
     per_step = depth // CHUNKS
     span = GROUP * others
 
-    clear_off_diagonal(diagonal, others, sequences)
-    result[...] = jnp.zeros(result.shape, F32) if first else before[...]
-
-    @pl.loop(chunks[0], chunks[-1] + 1)
+    result[...] = jnp.zeros(result.shape, F32)
+
+    @pl.loop(0, CHUNKS)
     def _(t):
-        for n in range(per_step):
-            fill_diagonal(wide, diagonal, n, t * per_step + n, others, sequences)
         size = per_step * depth
         rows = pl.ds(pl.multiple_of(t * size, size), size)
         part = source.at[rows]
@@ -349,13 +338,11 @@
                 )
                 for k in range(positions // GROUP)
             ]
-            result[...] += dot(
-                jnp.concatenate(blocks, axis=0),
-                diagonal[n : n + 2].reshape(2 * span, diagonal.shape[2]),
-            )
-
-    if not last:
-        return
+            right = [
+                diagonal_of(wide, t * per_step + m, others, sequences) for m in (n, n + 1)
+            ]
+            result[...] += dot(jnp.concatenate(blocks, axis=0), jnp.concatenate(right, axis=0))
+
     scaled = (result[...] * (1.0 / sequences)).astype(BF16)
     for l in range(scaled.shape[1] // LANES):
         members = dict(tiles_of(sequences, l))
@@ -386,62 +373,32 @@
             out[n * size : (n + 1) * size, :] = rows_of(p).astype(BF16)
 
 
-def gradient_call(kernel, operands, after, shapes, scratch, others, sequences, flops):
-    specs = [in_vmem()] * len(operands)
-    specs.insert(2, pl.BlockSpec(memory_space=pl.ANY))
-    diagonal = pltpu.VMEM((PROJECTED_DEPTH // CHUNKS, GROUP * others, GROUP * sequences), BF16)
-    return pl.pallas_call(
-        kernel,
-        in_specs=specs,
-        out_specs=[in_vmem()] * len(shapes),
-        out_shape=shapes,
-        scratch_shapes=[diagonal, *scratch],
-        compiler_params=params(sequences),
-        cost_estimate=pl.CostEstimate(
-            flops=flops, bytes_accessed=2 * operands[1].size, transcendentals=0
-        ),
-    )(*operands[:2], after, *operands[2:])
-
-
-def gradient_start(wide, source, after, axis, positions, others, sequences):
-    shape = (positions // GROUP * PROJECTED_DEPTH, GROUP * sequences)
-    chunks = range(CHUNKS // 2)
-    (before,) = gradient_call(
-        functools.partial(gradient_kernel, axis, None, 0, positions, others, sequences, chunks),
-        [wide, source],
-        after,
-        [jax.ShapeDtypeStruct(shape, F32)],
-        [],
-        others,
-        sequences,
-        source.size * PAIR_FEATURES,
-    )
-    return before
-
-
-def gradient(wide, source, after, axis, plan, kept, groups, positions, others, sequences, before=None):
+def gradient(wide, source, after, axis, plan, kept, groups, positions, others, sequences):
     depth = PROJECTED_DEPTH
     parts = lax.axis_size(axis)
     rows = sequences // parts * positions * depth // LANES
     shapes = [jax.ShapeDtypeStruct((rows, LANES), F32)] * kept
-    if groups > 0:
-        group = (parts - kept) // groups
-        shapes += [jax.ShapeDtypeStruct((group * rows, LANES), BF16)] * groups
-    chunks = range(0 if before is None else CHUNKS // 2, CHUNKS)
-    results = gradient_call(
-        functools.partial(gradient_kernel, axis, plan, kept, positions, others, sequences, chunks),
-        [wide, source] + ([] if before is None else [before]),
-        after,
-        shapes,
-        [
+    group = (parts - kept) // groups
+    shapes += [jax.ShapeDtypeStruct((group * rows, LANES), BF16)] * groups
+    tiles = GROUP * sequences // LANES if wide.ndim == 2 else 1
+    results = pl.pallas_call(
+        functools.partial(gradient_kernel, axis, plan, kept, positions, others, sequences),
+        in_specs=[in_vmem(), in_vmem(), pl.BlockSpec(memory_space=pl.ANY)],
+        out_specs=[in_vmem()] * len(shapes),
+        out_shape=shapes,
+        scratch_shapes=[
             pltpu.VMEM((positions // GROUP * depth, GROUP * sequences), F32),
             pltpu.VMEM((positions * depth, GROUP * sequences), BF16),
             pltpu.VMEM((sequences, positions * depth), F32),
+            pltpu.VMEM((tiles, others * depth if wide.ndim == 2 else 8, LANES), F32),
         ],
-        others,
-        sequences,
-        2 * source.size * PAIR_FEATURES,
-    )
+        compiler_params=params(sequences),
+        cost_estimate=pl.CostEstimate(
+            flops=2 * source.size * PAIR_FEATURES,
+            bytes_accessed=2 * source.size,
+            transcendentals=0,
+        ),
+    )(wide, source, after)
     return results[:kept], results[kept:]
 
 
@@ -465,8 +422,7 @@
     )(left, right, after)
 
 
-def pair_kernel(sequences, x_ref, wt_ref, bias_ref, out_ref, done_ref):
-    done_ref[...] = jnp.zeros(done_ref.shape, F32)
+def pair_kernel(sequences, x_ref, wt_ref, bias_ref, out_ref):
     product = dot(wt_ref[...], x_ref[...])
     out_ref[...] = (product.T * (1.0 / sequences) + bias_ref[...]).astype(BF16)
 
@@ -483,11 +439,8 @@
             whole(wt.shape),
             whole((1, PAIR_FEATURES)),
         ],
-        out_specs=[pl.BlockSpec((size, PAIR_FEATURES), lambda t: (t, 0)), whole((8, LANES))],
-        out_shape=[
-            jax.ShapeDtypeStruct((pairs, PAIR_FEATURES), BF16),
-            jax.ShapeDtypeStruct((8, LANES), F32),
-        ],
+        out_specs=pl.BlockSpec((size, PAIR_FEATURES), lambda t: (t, 0)),
+        out_shape=jax.ShapeDtypeStruct((pairs, PAIR_FEATURES), BF16),
         compiler_params=params(),
         cost_estimate=pl.CostEstimate(
             flops=4 * pairs * channels * PAIR_FEATURES,
@@ -502,53 +455,39 @@
         out[:, l * LANES : (l + 1) * LANES] = total[l * share : (l + 1) * share, :]
 
 
-def call(kernel, operands, shapes, after=()):
+def call(kernel, operands, shapes, after=(), scratch=()):
     specs = [in_vmem()] * len(operands) + [pl.BlockSpec(memory_space=pl.ANY)] * len(after)
     return pl.pallas_call(
         kernel,
         in_specs=specs,
         out_specs=[in_vmem()] * len(shapes),
         out_shape=[jax.ShapeDtypeStruct(shape, kind) for shape, kind in shapes],
+        scratch_shapes=scratch,
         compiler_params=params(),
     )(*operands, *after)
 
 
-def row_pair_sum(kept, bias, near, after, share):
-    count = kept.shape[0] // share
-
-    def kernel(kept, bias, near, _, own, bias_out, *messages):
-        total = split(joined(bias[...]) + joined(near[count * share :, :]))
-        bias_out[...] = total
-        for p in range(count):
-            rows = slice(p * share, (p + 1) * share)
-            both = kept[rows, :] + near[rows, :].astype(F32)
-            if p == 0:
-                own[...] = both
-            else:
-                messages[p - 1][0:share, :] = both.astype(BF16)
-                messages[p - 1][share:, :] = total
-
-    shapes = [((share, LANES), F32), (bias.shape, BF16)]
-    shapes += [((share + BIAS_ROWS, LANES), BF16)] * (count - 1)
-    own, bias, *messages = call(kernel, [kept, bias, near], shapes, [after])
-    return own, bias, messages
-
-
-def row_sum(own, bias, parts, grad):
-    share = own.shape[0]
-
-    def kernel(own, bias, *refs):
-        parts, grad, message = refs[:-2], refs[-2], refs[-1]
-        total, bias_total = own[...], joined(bias[...])
-        for part in parts:
-            total += part[0:share, :].astype(F32)
-            bias_total += joined(part[share:, :])
+def row_sum(parts, grad, share):
+    count = len(parts)
+
+    def kernel(*refs):
+        parts, (grad, message, held) = refs[:count], refs[count:]
+        me = lax.axis_index("row")
+        total = parts[0][0:share, :]
+        for p, part in enumerate(parts):
+            held[lax.rem(me - p + count, count)] = part[share:, :].astype(F32)
+            if p > 0:
+                total += part[0:share, :].astype(F32)
+        bias = joined(held[0])
+        for n in range(1, count):
+            bias += joined(held[n])
         message[0:share, :] = total.astype(BF16)
-        message[share : share + BIAS_ROWS, :] = split(bias_total)
+        message[share : share + BIAS_ROWS, :] = split(bias)
         message[share + BIAS_ROWS :, :] = grad[...]
 
     shape = (share + BIAS_ROWS + grad.shape[0], LANES)
-    (message,) = call(kernel, [own, bias, *parts, grad], [(shape, BF16)])
+    scratch = [pltpu.VMEM((count, BIAS_ROWS, LANES), F32)]
+    (message,) = call(kernel, [*parts, grad], [(shape, BF16)], scratch=scratch)
     return message
 
 
@@ -575,14 +514,14 @@
     return left, messages
 
 
-def column_sum(parts, left_own, own, grads, share, left_shape, res_total):
+def column_sum(parts, left_own, own, grads, share):
     rows = share + BIAS_ROWS
     count = len(parts) + 1
+    sent = len(grads)
 
     def kernel(*refs):
-        parts, grad, own, refs = refs[: count - 1], refs[count - 1], refs[count], refs[count + 1 :]
-        grads, refs = refs[: len(grad_list)], refs[len(grad_list) :]
-        messages, (piece_out, left_out, bias_out, held) = refs[:-4], refs[-4:]
+        parts, (grad, own), refs = refs[: count - 1], refs[count - 1 : count + 1], refs[count + 1 :]
+        grads, messages, (piece_out, left_out, bias_out, held) = refs[:sent], refs[sent:-4], refs[-4:]
         home = lax.div(lax.axis_index("col"), 2)
         for p, part in enumerate((own, *parts)):
             held[lax.rem(home - p + count, count)] = part[0:rows, :]
@@ -595,67 +534,46 @@
         for message, other in zip(messages, grads, strict=True):
             message[0:share, :] = piece
             message[share:, :] = other[...]
-        bias_out[...] = bias * (1.0 / res_total)
+        bias_out[...] = jnp.broadcast_to(bias, bias_out.shape)
         left = grad[...]
         for part in parts:
             left += part[rows:, :].astype(F32)
-        unfold(left, left_out.shape[0], left_out)
-
-    grad_list = list(grads)
-    operands = [*parts, left_own, own, *grad_list]
+        left_out[...] = left
+
+    shapes = [((share + grad.shape[0], LANES), BF16) for grad in grads]
+    shapes += [((share, LANES), BF16), (left_own.shape, F32), ((8, LANES), F32)]
+    scratch = [pltpu.VMEM((count, rows, LANES), BF16)]
+    *messages, piece, left, bias = call(
+        kernel, [*parts, left_own, own, *grads], shapes, scratch=scratch
+    )
+    return messages, piece, left, bias
+
+
+def finish(parts, piece, left, right_own, bias, left_shape, right_shape, scale, bias_scale):
+    count = len(parts) + 1
+    share = piece.shape[0]
+
+    def kernel(*refs):
+        parts, refs = refs[: count - 1], refs[count - 1 :]
+        piece, left, right_own, bias, projection, left_out, right_out, bias_out = refs
+        me = lax.axis_index("row")
+        right = right_own[...]
+        for p, part in enumerate((piece, *parts)):
+            rows = pl.ds(pl.multiple_of(lax.rem(me - p + count, count) * share, share), share)
+            projection[rows, :] = part[0:share, :].astype(F32) * scale
+            if p > 0:
+                right += part[share:, :].astype(F32)
+        unfold(left[...], left_out.shape[0], left_out)
+        unfold(right, right_out.shape[0], right_out)
+        bias_out[...] = bias[0:1, :] * bias_scale
+
     shapes = [
-        jax.ShapeDtypeStruct((share + grad.shape[0], LANES), BF16) for grad in grad_list
-    ] + [
-        jax.ShapeDtypeStruct((share, LANES), BF16),
-        jax.ShapeDtypeStruct(left_shape, F32),
-        jax.ShapeDtypeStruct((1, PAIR_FEATURES), F32),
-    ]
-    *messages, piece, left, bias = pl.pallas_call(
-        kernel,
-        in_specs=[in_vmem()] * len(operands),
-        out_specs=[in_vmem()] * len(shapes),
-        out_shape=shapes,
-        scratch_shapes=[pltpu.VMEM((count, rows, LANES), BF16)],
-        compiler_params=params(),
-    )(*operands)
-    return messages, piece, left, bias
-
-
-def finish_pairs(piece, grads, parts, after):
-    share, size = piece.shape[0], grads[0].shape[0]
-    count = len(parts) + 1
-
-    def kernel(piece, own, other, *refs):
-        parts, (message, right_out) = refs[: count - 1], refs[-2:]
-        message[0:share, :] = piece[...]
-        mine, theirs = own[...], other[...]
-        for p, part in enumerate(parts, 1):
-            message[p * share : (p + 1) * share, :] = part[0:share, :]
-            mine += part[share : share + size, :].astype(F32)
-            theirs += part[share + size :, :].astype(F32)
-        message[count * share :, :] = theirs.astype(BF16)
-        right_out[...] = mine
-
-    shapes = [((count * share + size, LANES), BF16), ((size, LANES), F32)]
-    return call(kernel, [piece, *grads, *parts], shapes, [after])
-
-
-def finish(own, near, right_own, right_shape, share, scale):
-    count = lax.axis_size("row") // 2
-
-    def kernel(own, near, right_own, projection, right_out):
-        me = lax.axis_index("row")
-        home, odd = lax.div(me, 2), lax.rem(me, 2)
-        for ref, parity in ((own, odd), (near, 1 - odd)):
-            for p in range(count):
-                place = 2 * lax.rem(home - p + count, count) + parity
-                rows = pl.ds(pl.multiple_of(place * share, share), share)
-                projection[rows, :] = ref[p * share : (p + 1) * share, :].astype(F32) * scale
-        right = right_own[...] + near[count * share :, :].astype(F32)
-        unfold(right, right_out.shape[0], right_out)
-
-    shapes = [((2 * count * share, PAIR_FEATURES), F32), (right_shape, F32)]
-    return call(kernel, [own, near, right_own], shapes)
+        ((count * share, PAIR_FEATURES), F32),
+        (left_shape, F32),
+        (right_shape, F32),
+        ((1, PAIR_FEATURES), F32),
+    ]
+    return call(kernel, [*parts, piece, left, right_own, bias], shapes)
 
 
 def shift(x, axis, distance):
@@ -669,6 +587,10 @@
 
 def shift_pairs(x, axis):
     return [x] + [shift(x, axis, d) for d in range(2, lax.axis_size(axis), 2)]
+
+
+def send(parts, axis):
+    return [shift(part, axis, d) for d, part in enumerate(parts, 1)]
 
 
 def send_pairs(parts, axis):
@@ -696,42 +618,38 @@
     b_pieces = shift_pairs(b_pair, "row")
     y, gt, bias_rows = prepare(we, g, i_n, j_n)
 
-    x, a_wide, b_wide, kept, message = outer(
+    x, a_held, b_wide, (own, *messages) = outer(
         a_pieces, b_pieces, g, bias_rows, i_n, j_n, sequences
     )
     share = channels // row_n
 
-    near = neighbour(message, "row")
-    before = gradient_start(b_wide, y, message, "col", i_n, j_n, sequences)
-    own, bias, messages = row_pair_sum(kept, bias_rows, near, before, share)
-    parts = send_pairs(messages, "row")
+    parts = [own] + send(messages, "row")
     left_kept, (left_sent,) = gradient(
-        b_wide, y, bias, "col", in_pairs(col_n), col_n // 2, 1, i_n, j_n, sequences, before
-    )
-
-    message = row_sum(own, bias, parts, left_sent)
+        b_wide, y, own, "col", in_pairs(col_n), col_n // 2, 1, i_n, j_n, sequences
+    )
+
+    message = row_sum(parts, left_sent, share)
     near = neighbour(message, "col")
     y2 = product(w, gt, message)
     left_own, messages = column_pair_sum(message, near, left_kept, y2, share)
     parts = send_pairs(messages, "col")
-    right_kept, right_sent = gradient(
-        a_wide, y2, left_own, "row", by_pairs(row_n), 2, row_n // 2 - 1, j_n, i_n, sequences
-    )
-
-    messages, piece, left_grad, bias_grad = column_sum(
-        parts, left_own, messages[0], right_sent, share, first_homolog_features.shape, res_total
-    )
-    parts = send_pairs(messages, "row")
-    pair_map, pair_done = pair(x, wt, output_bias, sequences)
-    message, right_own = finish_pairs(piece, right_kept, parts, pair_done)
-    near = neighbour(message, "row")
-    projection, right_grad = finish(
-        message,
-        near,
+    (right_own,), right_sent = gradient(
+        a_held, y2, left_own, "row", in_order(row_n), 1, row_n - 1, j_n, i_n, sequences
+    )
+
+    messages, piece, left_own, bias = column_sum(parts, left_own, messages[0], right_sent, share)
+    parts = send(messages, "row")
+    pair_map = pair(x, wt, output_bias, sequences)
+    projection, left_grad, right_grad, bias_grad = finish(
+        parts,
+        piece,
+        left_own,
         right_own,
+        bias,
+        first_homolog_features.shape,
         second_homolog_features.shape,
-        share,
         1.0 / (sequences * res_total),
+        1.0 / res_total,
     )
     return (
         pair_map.reshape(i_n, j_n, PAIR_FEATURES),

time: 43.2 us -> 43.6 us (level)
  Pallas kernels: 21.2 us -> 17.5 us
  starting transfers between devices: 13.7 us -> 16.6 us
  waiting for transfers between devices: 7.46 us -> 8.31 us
    ppermute x5 -> x9, starting transfers between devices: 8.83 us -> 11.9 us  [shift(): lax.ppermute(x, axis, [(n, (n + distance) % count) for n in range(count)])]
    pallas_call x4 -> x2, Pallas kernels: 7.61 us -> 4.65 us  [gradient(): pl.pallas_call(functools.partial(gradient_kernel, axis, plan, kept, posit...]
    ppermute x5 -> x9, waiting for transfers between devices: 3.58 us -> 4.89 us  [shift(): lax.ppermute(x, axis, [(n, (n + distance) % count) for n in range(count)])]
    pallas_call x1, Pallas kernels: 5.49 us -> 4.78 us  [outer(): pl.pallas_call(functools.partial(outer_kernel, i_n, j_n, row_n, col_n), i...]
    ppermute x5 -> x3, waiting for transfers between devices: 3.88 us -> 3.43 us  [neighbour(): lax.ppermute(x, axis, [(n, n ^ 1) for n in range(lax.axis_size(axis))])]
    ppermute x5 -> x3, starting transfers between devices: 4.88 us -> 4.72 us  [neighbour(): lax.ppermute(x, axis, [(n, n ^ 1) for n in range(lax.axis_size(axis))])]
    pallas_call x5 -> x4, Pallas kernels: 0.97 us -> 1.01 us  [call(): pl.pallas_call(kernel, in_specs=specs, out_specs=[in_vmem()] * len(shapes...]
  transfers between devices with their start and end apart: 10 -> 12, of which waited for: 7 -> 5; matrix products, arithmetic and copies ran while one was open for 0% -> 0% of each run, Pallas kernels for 33% -> 27%
where the time goes in v9:
time: 43.6 us; the launch traced here: 43.2 us
  Pallas kernels  17.5 us (40%)
  starting transfers between devices  16.6 us (38%)
  waiting for transfers between devices  8.31 us (19%)
  between operations  0.75 us (2%)
    ppermute x9, starting transfers between devices, shift(): lax.ppermute(x, axis, [(n, (n + distance) % count) for n in range(count)])  11.9 us
    ppermute x9, waiting for transfers between devices, shift(): lax.ppermute(x, axis, [(n, (n + distance) % count) for n in range(count)])  4.89 us
    pallas_call x1, Pallas kernels, outer(): pl.pallas_call(functools.partial(outer_kernel, i_n, j_n, row_n, col_n), i...  4.78 us
    ppermute x3, starting transfers between devices, neighbour(): lax.ppermute(x, axis, [(n, n ^ 1) for n in range(lax.axis_size(axis))])  4.72 us
    pallas_call x2, Pallas kernels, gradient(): pl.pallas_call(functools.partial(gradient_kernel, axis, plan, kept, posit...  4.65 us
    ppermute x3, waiting for transfers between devices, neighbour(): lax.ppermute(x, axis, [(n, n ^ 1) for n in range(lax.axis_size(axis))])  3.43 us
    pallas_call x1, Pallas kernels, pair(): pl.pallas_call(functools.partial(pair_kernel, sequences), grid=(count,),...  2.55 us
    pallas_call x1, Pallas kernels, prepare(): pl.pallas_call(functools.partial(prepare_kernel, i_n, j_n), in_specs=[in_...  1.75 us
  transfers between devices with their start and end apart: 12, of which 5 were waited for; matrix products, arithmetic and copies ran while one was open for 0% of the time, Pallas kernels for 27%

profile of v9, /device:TPU:0, one launch (start us, length us, event | category | flops | bytes accessed | tf_op | source)
XLA Modules:
  0.0 43.2 jit_solution(14201994341482180261)
XLA Ops:
  0.6 3.1 %collective-permute-start = (bf16[8,1536]{1,0:T(8,128)(2,1)}, bf16[8,1536]{1,0:T(8,128)(2,1)S(1)}, u32[]{:S(2)}, u32[]{:S(2)}) collective-permute-start(bf16[8,1536]{1,0:T(8,128)(2,1)} %a_hbm.1), channel_id=1, source_target_pairs={{0,1},{1,0},{2,3},{3,2},{4,5},{5,4},{6,7},{7,6},{8,9},{9,8},{10,11... | collective-permute-start | bytes 73736 | tf_op jit(solution)/shard_map/ppermute | solution.py:585
  3.7 0.0 collective-permute-start.1
  3.7 1.4 %shard_map.92 = (bf16[1024,128]{1,0:T(8,128)(2,1)S(1)}, bf16[128,1024]{1,0:T(8,128)(2,1)S(1)}, bf16[8,1536]{1,0:T(8,128)(2,1)S(1)}, bf16[8,1536]{1,0:T(8,128)(2,...) custom-call(bf16[8,1536]{1,0:T(8,128)(2,1)} %a_hbm.1, bf16[8,1536]{1,0:T(8,128)(2,1)} %b_hbm.1, ...), custom_call_target="tpu_custom_call" | custom-call | flops 131072000 | bytes 2097152 | tf_op jit(solution)/shard_map/pallas_call | solution.py:67
  5.1 0.6 %collective-permute-done.refs_1_ = bf16[8,1536]{1,0:T(8,128)(2,1)S(1)} collective-permute-done((bf16[8,1536]{1,0:T(8,128)(2,1)}, bf16[8,1536]{1,0:T(8,128)(2,1)S(1)}, u32[]{:S(2)}, u32[]{:S(2)}) %collective-permute-start) | collective-permute-done | bytes 24608 | tf_op jit(solution)/shard_map/ppermute | solution.py:585
  5.7 0.0 collective-permute-done.1.refs_3_
  5.8 3.1 %collective-permute-start.2 = (bf16[16,1536]{1,0:T(8,128)(2,1)S(1)}, bf16[16,1536]{1,0:T(8,128)(2,1)S(1)}, u32[]{:S(2)}, u32[]{:S(2)}) collective-permute-start(bf16[16,1536]{1,0:T(8,128)(2,1)S(1)} %get-tuple-element.44.refs_0_), channel_id=1, source_target_pairs={{0,2},{1,3},{2,0},{3,1},{4,6},{5,7},{6,4},{7,5},{8,10},{9,11},{10,... | collective-permute-start | bytes 147464 | tf_op jit(solution)/shard_map/ppermute | solution.py:581
  8.9 1.5 %collective-permute-start.3 = (bf16[16,1536]{1,0:T(8,128)(2,1)S(1)}, bf16[16,1536]{1,0:T(8,128)(2,1)S(1)}, u32[]{:S(2)}, u32[]{:S(2)}) collective-permute-start(bf16[16,1536]{1,0:T(8,128)(2,1)S(1)} %get-tuple-element.45.refs_2_), channel_id=1, source_target_pairs={{0,8},{4,12},{8,0},{12,4},{1,9},{5,13},{9,1},{13,5},{2,10},{6,14},... | collective-permute-start | bytes 147464 | tf_op jit(solution)/shard_map/ppermute | solution.py:581
  10.3 1.7 %shard_map.94 = (bf16[1024,2304]{1,0:T(8,128)(2,1)S(1)}, bf16[2304,128]{1,0:T(8,128)(2,1)S(1)}, bf16[16,128]{1,0:T(8,128)(2,1)S(1)}) custom-call(bf16[1024,128]{1,0:T(8,128)(2,1)S(1)} %get-tuple-element.47.we_ref, bf16[2304,128]{1,0:T(8,128)(2,1)S(1)} %get-tuple-element.46.g_ref.refs_4_), custom_call_target="tpu_custom_call" | custom-call | flops 603979776 | bytes 9437184 | tf_op jit(solution)/shard_map/pallas_call | solution.py:137
  12.1 0.8 %collective-permute-done.3.refs_3_ = bf16[16,1536]{1,0:T(8,128)(2,1)S(1)} collective-permute-done((bf16[16,1536]{1,0:T(8,128)(2,1)S(1)}, bf16[16,1536]{1,0:T(8,128)(2,1)S(1)}, u32[]{:S(2)}, u32[]{:S(2)}) %collective-permute-start.3) | collective-permute-done | bytes 49184 | tf_op jit(solution)/shard_map/ppermute | solution.py:581
  12.9 4.8 %shard_map.95 = (bf16[1024,2304]{1,0:T(8,128)(2,1)S(1)}, f32[32,1536]{1,0:T(8,128)S(1)}, f32[2,1536,128]{2,1,0:T(8,128)S(1)}, f32[272,128]{1,0:T(8,128)S(1)}, bf...) custom-call(bf16[16,1536]{1,0:T(8,128)(2,1)S(1)} %get-tuple-element.44.refs_0_, ...), custom_call_target="tpu_custom_call" | custom-call | flops 1207959552 | bytes 4718592 | tf_op jit(solution)/shard_map/pallas_call | solution.py:292
  17.7 0.1 collective-permute-start.4
  17.8 1.6 %collective-permute-start.5 = (bf16[272,128]{1,0:T(8,128)(2,1)S(1)}, bf16[272,128]{1,0:T(8,128)(2,1)S(1)}, u32[]{:S(2)}, u32[]{:S(2)}) collective-permute-start(bf16[272,128]{1,0:T(8,128)(2,1)S(1)} %get-tuple-element.53), channel_id=1, source_target_pairs={{0,8},{4,12},{8,0},{12,4},{1,9},{5,13},{9,1},{13,5},{2,10},{6,14},... | collective-permute-start | bytes 208904 | tf_op jit(solution)/shard_map/ppermute | solution.py:581
  19.4 1.4 %collective-permute-start.6 = (bf16[272,128]{1,0:T(8,128)(2,1)S(1)}, bf16[272,128]{1,0:T(8,128)(2,1)S(1)}, u32[]{:S(2)}, u32[]{:S(2)}) collective-permute-start(bf16[272,128]{1,0:T(8,128)(2,1)S(1)} %get-tuple-element.54), channel_id=1, source_target_pairs={{0,12},{4,0},{8,4},{12,8},{1,13},{5,1},{9,5},{13,9},{2,14},{6,2},{... | collective-permute-start | bytes 208904 | tf_op jit(solution)/shard_map/ppermute | solution.py:581
  20.8 2.1 %shard_map.97 = (f32[96,128]{1,0:T(8,128)S(1)}, f32[96,128]{1,0:T(8,128)S(1)}, bf16[192,128]{1,0:T(8,128)(2,1)S(1)}) custom-call(f32[2,1536,128]{2,1,0:T(8,128)S(1)} %get-tuple-element.55.refs_0_, bf16[1024,2304]{1,0:T(8,128)(2,1)S(1)} %get-tuple-element.56.refs_1_, f32[272,128]{1,0:T(8,128)S(1)} %get-tuple-element.51.refs_2_.refs_0_), custom_call_target="tpu_custom_call" | custom-call | flops 603979776 | bytes 4718592 | tf_op jit(solution)/shard_map/pallas_call | solution.py:384
  22.9 0.0 collective-permute-done.5.refs_2_
  22.9 0.0 collective-permute-done.6.refs_3_
  22.9 0.1 shard_map.98._.own
  23.0 1.6 %collective-permute-start.7 = (bf16[464,128]{1,0:T(8,128)(2,1)S(1)}, bf16[464,128]{1,0:T(8,128)(2,1)S(1)}, u32[]{:S(2)}, u32[]{:S(2)}) collective-permute-start(bf16[464,128]{1,0:T(8,128)(2,1)S(1)} %shard_map.98._.own), channel_id=1, source_target_pairs={{0,1},{1,0},{2,3},{3,2},{4,5},{5,4},{6,7},{7,6},{8,9},{9,8},{10,11... | collective-permute-start | bytes 356360 | tf_op jit(solution)/shard_map/ppermute | solution.py:585
  24.6 1.4 %shard_map.99.refs_2_.refs_1_ = bf16[1024,2304]{1,0:T(8,128)(2,1)S(1)} custom-call(bf16[1024,128]{1,0:T(8,128)(2,1)S(1)} %get-tuple-element.60.left_ref, bf16[2304,128]{1,0:T(8,128)(2,1)S(1)} %get-tuple-element.61.right_ref, bf16[464,128]{1,0:T(8,128)(2,1)S(1)} %shard_map.98._.own), custom_call_target="tpu_custom_call" | custom-call | flops 603979776 | bytes 9437184 | tf_op jit(solution)/shard_map/pallas_call | solution.py:411
  26.0 2.8 %collective-permute-done.7.near = bf16[464,128]{1,0:T(8,128)(2,1)S(1)} collective-permute-done((bf16[464,128]{1,0:T(8,128)(2,1)S(1)}, bf16[464,128]{1,0:T(8,128)(2,1)S(1)}, u32[]{:S(2)}, u32[]{:S(2)}) %collective-permute-start.7) | collective-permute-done | bytes 118816 | tf_op jit(solution)/shard_map/ppermute | solution.py:585
  28.9 1.2 %collective-permute-start.8 = (bf16[368,128]{1,0:T(8,128)(2,1)S(1)}, bf16[368,128]{1,0:T(8,128)(2,1)S(1)}, u32[]{:S(2)}, u32[]{:S(2)}) collective-permute-start(bf16[368,128]{1,0:T(8,128)(2,1)S(1)} %get-tuple-element.62.refs_2_), channel_id=1, source_target_pairs={{0,2},{1,3},{2,0},{3,1},{4,6},{5,7},{6,4},{7,5},{8,10},{9,11},{10,... | collective-permute-start | bytes 282632 | tf_op jit(solution)/shard_map/ppermute | solution.py:581
  30.1 2.5 %shard_map.101 = (f32[96,128]{1,0:T(8,128)S(1)}, bf16[96,128]{1,0:T(8,128)(2,1)S(1)}, bf16[96,128]{1,0:T(8,128)(2,1)S(1)}, bf16[96,128]{1,0:T(8,128)(2,1)S(1)}) custom-call(f32[32,1536]{1,0:T(8,128)S(1)} %get-tuple-element.64.refs_0_, bf16[1024,2304]{1,0:T(8,128)(2,1)S(1)} %shard_map.99.refs_2_.refs_1_, f32[96,128]{1,0:T(8,128)S(1)} %get-tuple-element.63.refs_2_.refs_1_), custom_call_target="tpu_custom_call" | custom-call | flops 603979776 | bytes 4718592 | tf_op jit(solution)/shard_map/pallas_call | solution.py:384
  32.6 3.7 %collective-permute-done.8.refs_0_ = bf16[368,128]{1,0:T(8,128)(2,1)S(1)} collective-permute-done((bf16[368,128]{1,0:T(8,128)(2,1)S(1)}, bf16[368,128]{1,0:T(8,128)(2,1)S(1)}, u32[]{:S(2)}, u32[]{:S(2)}) %collective-permute-start.8) | collective-permute-done | bytes 94240 | tf_op jit(solution)/shard_map/ppermute | solution.py:581
  36.3 0.1 shard_map.102
  36.4 0.1 collective-permute-start.9
  36.4 1.6 %collective-permute-start.10 = (bf16[352,128]{1,0:T(8,128)(2,1)S(1)}, bf16[352,128]{1,0:T(8,128)(2,1)S(1)}, u32[]{:S(2)}, u32[]{:S(2)}) collective-permute-start(bf16[352,128]{1,0:T(8,128)(2,1)S(1)} %get-tuple-element.69), channel_id=1, source_target_pairs={{0,8},{4,12},{8,0},{12,4},{1,9},{5,13},{9,1},{13,5},{2,10},{6,14},... | collective-permute-start | bytes 270344 | tf_op jit(solution)/shard_map/ppermute | solution.py:581
  38.0 1.4 %collective-permute-start.11 = (bf16[352,128]{1,0:T(8,128)(2,1)S(1)}, bf16[352,128]{1,0:T(8,128)(2,1)S(1)}, u32[]{:S(2)}, u32[]{:S(2)}) collective-permute-start(bf16[352,128]{1,0:T(8,128)(2,1)S(1)} %get-tuple-element.70), channel_id=1, source_target_pairs={{0,12},{4,0},{8,4},{12,8},{1,13},{5,1},{9,5},{13,9},{2,14},{6,2},{... | collective-permute-start | bytes 270344 | tf_op jit(solution)/shard_map/ppermute | solution.py:581
  39.4 2.5 %shard_map.96 = bf16[2304,128]{1,0:T(8,128)(2,1)} custom-call(bf16[1024,2304]{1,0:T(8,128)(2,1)S(1)} %get-tuple-element.49.x_ref, bf16[128,1024]{1,0:T(8,128)(2,1)S(1)} %get-tuple-element.50.wt_ref, f32[1,128]{1,0:T(1,128)S(1)} %bitcast.4), custom_call_target="tpu_custom_call" | custom-call | flops 1207959552 | bytes 4718592 | tf_op jit(solution)/shard_map/pallas_call | solution.py:434
  42.0 0.0 collective-permute-done.9.refs_0_
  42.0 0.0 collective-permute-done.10.refs_1_
  42.0 0.3 collective-permute-done.11.refs_2_
  42.3 0.9 %shard_map.103 = (f32[1024,128]{1,0:T(8,128)}, f32[8,1536]{1,0:T(8,128)}, f32[8,1536]{1,0:T(8,128)}, f32[1,128]{1,0:T(1,128)}) custom-call(bf16[352,128]{1,0:T(8,128)(2,1)S(1)} %collective-permute-done.9.refs_0_, bf16[352,128]{1,0:T(8,128)(2,1)S(1)} %collective-permute-done.10.refs_1_, bf16[352,128]{1,0:T(8,128)(2,1)S(1)} %collective-permute-done.11.refs_2_, ...), custom_call_target="tpu_custom_call" | custom-call | tf_op jit(solution)/shard_map/pallas_call | solution.py:460
  (6 shorter events, 0.0 us)
Async XLA Ops:
  0.6 5.1 %collective-permute-start = (bf16[8,1536]{1,0:T(8,128)(2,1)}, bf16[8,1536]{1,0:T(8,128)(2,1)S(1)}, u32[]{:S(2)}, u32[]{:S(2)}) collective-permute-start(bf16[8,1536]{1,0:T(8,128)(2,1)} %a_hbm.1), channel_id=1, source_target_pairs={{0,1},{1,0},{2,3},{3,2},{4,5},{5,4},{6,7},{7,6},{8,9},{9,8},{10,11... | collective-permute-start | bytes 73736 | tf_op jit(solution)/shard_map/ppermute | solution.py:585
  3.7 2.0 %collective-permute-start.1 = (bf16[8,1536]{1,0:T(8,128)(2,1)}, bf16[8,1536]{1,0:T(8,128)(2,1)S(1)}, u32[]{:S(2)}, u32[]{:S(2)}) collective-permute-start(bf16[8,1536]{1,0:T(8,128)(2,1)} %b_hbm.1), channel_id=1, source_target_pairs={{0,4},{4,0},{8,12},{12,8},{1,5},{5,1},{9,13},{13,9},{2,6},{6,2},{1... | collective-permute-start | bytes 73736 | tf_op jit(solution)/shard_map/ppermute | solution.py:585
  5.8 6.3 %collective-permute-start.2 = (bf16[16,1536]{1,0:T(8,128)(2,1)S(1)}, bf16[16,1536]{1,0:T(8,128)(2,1)S(1)}, u32[]{:S(2)}, u32[]{:S(2)}) collective-permute-start(bf16[16,1536]{1,0:T(8,128)(2,1)S(1)} %get-tuple-element.44.refs_0_), channel_id=1, source_target_pairs={{0,2},{1,3},{2,0},{3,1},{4,6},{5,7},{6,4},{7,5},{8,10},{9,11},{10,... | collective-permute-start | bytes 147464 | tf_op jit(solution)/shard_map/ppermute | solution.py:581
  8.9 4.1 %collective-permute-start.3 = (bf16[16,1536]{1,0:T(8,128)(2,1)S(1)}, bf16[16,1536]{1,0:T(8,128)(2,1)S(1)}, u32[]{:S(2)}, u32[]{:S(2)}) collective-permute-start(bf16[16,1536]{1,0:T(8,128)(2,1)S(1)} %get-tuple-element.45.refs_2_), channel_id=1, source_target_pairs={{0,8},{4,12},{8,0},{12,4},{1,9},{5,13},{9,1},{13,5},{2,10},{6,14},... | collective-permute-start | bytes 147464 | tf_op jit(solution)/shard_map/ppermute | solution.py:581
  17.7 5.2 %collective-permute-start.4 = (bf16[272,128]{1,0:T(8,128)(2,1)S(1)}, bf16[272,128]{1,0:T(8,128)(2,1)S(1)}, u32[]{:S(2)}, u32[]{:S(2)}) collective-permute-start(bf16[272,128]{1,0:T(8,128)(2,1)S(1)} %get-tuple-element.52), channel_id=1, source_target_pairs={{0,4},{4,8},{8,12},{12,0},{1,5},{5,9},{9,13},{13,1},{2,6},{6,10},{... | collective-permute-start | bytes 208904 | tf_op jit(solution)/shard_map/ppermute | solution.py:581
  17.8 5.1 %collective-permute-start.5 = (bf16[272,128]{1,0:T(8,128)(2,1)S(1)}, bf16[272,128]{1,0:T(8,128)(2,1)S(1)}, u32[]{:S(2)}, u32[]{:S(2)}) collective-permute-start(bf16[272,128]{1,0:T(8,128)(2,1)S(1)} %get-tuple-element.53), channel_id=1, source_target_pairs={{0,8},{4,12},{8,0},{12,4},{1,9},{5,13},{9,1},{13,5},{2,10},{6,14},... | collective-permute-start | bytes 208904 | tf_op jit(solution)/shard_map/ppermute | solution.py:581
  19.4 3.6 %collective-permute-start.6 = (bf16[272,128]{1,0:T(8,128)(2,1)S(1)}, bf16[272,128]{1,0:T(8,128)(2,1)S(1)}, u32[]{:S(2)}, u32[]{:S(2)}) collective-permute-start(bf16[272,128]{1,0:T(8,128)(2,1)S(1)} %get-tuple-element.54), channel_id=1, source_target_pairs={{0,12},{4,0},{8,4},{12,8},{1,13},{5,1},{9,5},{13,9},{2,14},{6,2},{... | collective-permute-start | bytes 208904 | tf_op jit(solution)/shard_map/ppermute | solution.py:581
  23.0 5.8 %collective-permute-start.7 = (bf16[464,128]{1,0:T(8,128)(2,1)S(1)}, bf16[464,128]{1,0:T(8,128)(2,1)S(1)}, u32[]{:S(2)}, u32[]{:S(2)}) collective-permute-start(bf16[464,128]{1,0:T(8,128)(2,1)S(1)} %shard_map.98._.own), channel_id=1, source_target_pairs={{0,1},{1,0},{2,3},{3,2},{4,5},{5,4},{6,7},{7,6},{8,9},{9,8},{10,11... | collective-permute-start | bytes 356360 | tf_op jit(solution)/shard_map/ppermute | solution.py:585
  28.8 10.6 %copy-start = (f32[128]{0:T(128)S(1)}, f32[128]{0:T(128)}, u32[]{:S(2)}) copy-start(f32[128]{0:T(128)} %param.8) | copy-start | bytes 1540
  28.9 7.4 %collective-permute-start.8 = (bf16[368,128]{1,0:T(8,128)(2,1)S(1)}, bf16[368,128]{1,0:T(8,128)(2,1)S(1)}, u32[]{:S(2)}, u32[]{:S(2)}) collective-permute-start(bf16[368,128]{1,0:T(8,128)(2,1)S(1)} %get-tuple-element.62.refs_2_), channel_id=1, source_target_pairs={{0,2},{1,3},{2,0},{3,1},{4,6},{5,7},{6,4},{7,5},{8,10},{9,11},{10,... | collective-permute-start | bytes 282632 | tf_op jit(solution)/shard_map/ppermute | solution.py:581
  36.4 5.6 %collective-permute-start.9 = (bf16[352,128]{1,0:T(8,128)(2,1)S(1)}, bf16[352,128]{1,0:T(8,128)(2,1)S(1)}, u32[]{:S(2)}, u32[]{:S(2)}) collective-permute-start(bf16[352,128]{1,0:T(8,128)(2,1)S(1)} %get-tuple-element.68), channel_id=1, source_target_pairs={{0,4},{4,8},{8,12},{12,0},{1,5},{5,9},{9,13},{13,1},{2,6},{6,10},{... | collective-permute-start | bytes 270344 | tf_op jit(solution)/shard_map/ppermute | solution.py:581
  36.4 5.5 %collective-permute-start.10 = (bf16[352,128]{1,0:T(8,128)(2,1)S(1)}, bf16[352,128]{1,0:T(8,128)(2,1)S(1)}, u32[]{:S(2)}, u32[]{:S(2)}) collective-permute-start(bf16[352,128]{1,0:T(8,128)(2,1)S(1)} %get-tuple-element.69), channel_id=1, source_target_pairs={{0,8},{4,12},{8,0},{12,4},{1,9},{5,13},{9,1},{13,5},{2,10},{6,14},... | collective-permute-start | bytes 270344 | tf_op jit(solution)/shard_map/ppermute | solution.py:581
  38.0 4.3 %collective-permute-start.11 = (bf16[352,128]{1,0:T(8,128)(2,1)S(1)}, bf16[352,128]{1,0:T(8,128)(2,1)S(1)}, u32[]{:S(2)}, u32[]{:S(2)}) collective-permute-start(bf16[352,128]{1,0:T(8,128)(2,1)S(1)} %get-tuple-element.70), channel_id=1, source_target_pairs={{0,12},{4,0},{8,4},{12,8},{1,13},{5,1},{9,5},{13,9},{2,14},{6,2},{... | collective-permute-start | bytes 270344 | tf_op jit(solution)/shard_map/ppermute | solution.py:581

commit v10 on v9

--- a/solution.py
+++ b/solution.py
@@ -77,27 +77,16 @@
     )(*[pltpu.with_memory_space_constraint(x, pltpu.HBM) for x in (a, b, w, g)])
 
 
-def stack_kernel(*refs):
-    half = len(refs) * 2 // 3
-    for n, out in enumerate(refs[half:]):
-        first, second = refs[2 * n], refs[2 * n + 1]
-        rows = first.shape[0]
-        both = jnp.concatenate([first[...].astype(F32), second[...].astype(F32)], axis=0)
-        out[...] = both.astype(BF16)
-
-
-def stack(*pairs):
-    shapes = [
-        jax.ShapeDtypeStruct((2 * first.shape[0], first.shape[1]), BF16) for first, _ in pairs
-    ]
-    operands = [x for pair in pairs for x in pair]
-    return pl.pallas_call(
-        stack_kernel,
-        in_specs=[in_vmem()] * len(operands),
-        out_specs=[in_vmem()] * len(shapes),
-        out_shape=shapes,
-        compiler_params=params(),
-    )(*operands)
+def stack(*groups):
+    def kernel(*refs):
+        refs, outs = refs[: -len(groups)], refs[-len(groups) :]
+        for group, out in zip(groups, outs, strict=True):
+            blocks = [ref[...].astype(F32) for ref in refs[: len(group)]]
+            refs = refs[len(group) :]
+            out[...] = jnp.concatenate(blocks, axis=0).astype(BF16)
+
+    shapes = [((len(group) * group[0].shape[0], group[0].shape[1]), BF16) for group in groups]
+    return call(kernel, [x for group in groups for x in group], shapes)
 
 
 def split(total):
@@ -150,17 +139,15 @@
 
 
 def join(pieces, axis, held):
-    count = len(pieces)
-    depth = pieces[0].shape[0] // 2
+    half = lax.axis_size(axis) // 2
+    depth = pieces[0].shape[0] // half
     me = lax.axis_index(axis)
-    odd = lax.rem(me, 2)
-    home = lax.div(me, 2)
-    for p, piece in enumerate(pieces):
-        start = lax.rem(home - p + count, count) * 2 * depth
-        both = piece[...].astype(F32)
-        for n in range(2):
-            place = start + (1 - odd if n else odd) * depth
-            held[pl.ds(pl.multiple_of(place, depth), depth), :] = both[n * depth : (n + 1) * depth]
+    odd, home = lax.rem(me, 2), lax.div(me, 2)
+    for piece, parity in zip(pieces, (odd, 1 - odd), strict=True):
+        block = piece[...].astype(F32)
+        for p in range(half):
+            place = (2 * lax.rem(home - p + half, half) + parity) * depth
+            held[pl.ds(pl.multiple_of(place, depth), depth), :] = block[p * depth : (p + 1) * depth]
 
 
 def repeat_matrix(sequences):
@@ -208,23 +195,10 @@
     return me + 1 - 2 * lax.rem(me, 2)
 
 
-def in_order(count):
-    return lambda me: ([me], [[lax.rem(me + d, count)] for d in range(1, count)])
-
-
-def in_pairs(count):
-    def plan(me):
-        steps = range(0, count, 2)
-        near = near_of(me)
-        return [lax.rem(me + d, count) for d in steps], [[lax.rem(near + d, count) for d in steps]]
-
-    return plan
-
-
-def outer_kernel(i_n, j_n, row_n, col_n, *refs):
+def outer_kernel(i_n, j_n, *refs):
     depth = PROJECTED_DEPTH
-    a_pieces, refs = refs[: col_n // 2], refs[col_n // 2 :]
-    b_pieces, refs = refs[: row_n // 2], refs[row_n // 2 :]
+    row_n = lax.axis_size("row")
+    a_pieces, b_pieces, refs = refs[:2], refs[2:4], refs[4:]
     g_ref, bias_ref, x_ref, a_held, b_wide = refs[:5]
     messages, (b_held, left, total) = refs[5 : 5 + row_n], refs[5 + row_n :]
     sequences = a_held.shape[0]
@@ -265,8 +239,8 @@
 
     share = total.shape[0] // row_n
     me = lax.axis_index("row")
-    stay, go = in_order(row_n)(me)
-    for message, (part,) in zip(messages, [stay, *go], strict=True):
+    for p, message in enumerate(messages):
+        part = lax.rem(me + p, row_n)
         for n in range(share // depth):
             block = total[pl.ds(part * (share // depth) + n, depth, stride=depth), :]
             message[n * depth : (n + 1) * depth, :] = block.astype(message.dtype)
@@ -274,7 +248,7 @@
 
 
 def outer(a_pieces, b_pieces, g, bias_rows, i_n, j_n, sequences):
-    row_n, col_n = 2 * len(b_pieces), 2 * len(a_pieces)
+    row_n = lax.axis_size("row")
     depth = PROJECTED_DEPTH
     channels = depth * depth
     pairs = i_n * j_n
@@ -290,7 +264,7 @@
         for p in range(row_n)
     ]
     results = pl.pallas_call(
-        functools.partial(outer_kernel, i_n, j_n, row_n, col_n),
+        functools.partial(outer_kernel, i_n, j_n),
         in_specs=[in_vmem()] * len(operands),
         out_specs=[in_vmem()] * len(shapes),
         out_shape=shapes,
@@ -309,7 +283,7 @@
     return *results[:3], results[3:]
 
 
-def gradient_kernel(axis, plan, kept, positions, others, sequences, *refs):
+def gradient_kernel(axis, positions, others, sequences, *refs):
     depth = PROJECTED_DEPTH
     wide, source = refs[:2]
     outs, (result, grown, grad, own_wide) = refs[3:-4], refs[-4:]
@@ -364,25 +338,24 @@
             [mine[:, l * LANES : (l + 1) * LANES] for l in range(mine.shape[1] // LANES)], axis=0
         )
 
-    stay, go = plan(lax.axis_index(axis))
-    for p, out in zip(stay, outs[:kept], strict=True):
-        out[...] = rows_of(p)
-    for group, out in zip(go, outs[kept:], strict=True):
-        size = out.shape[0] // len(group)
-        for n, p in enumerate(group):
-            out[n * size : (n + 1) * size, :] = rows_of(p).astype(BF16)
-
-
-def gradient(wide, source, after, axis, plan, kept, groups, positions, others, sequences):
+    me = lax.axis_index(axis)
+    near = me + 1 - 2 * lax.rem(me, 2)
+    *kept, message = outs
+    size = kept[0].shape[0]
+    for p, out in enumerate(kept):
+        out[...] = rows_of(lax.rem(me + 2 * p, parts))
+        message[p * size : (p + 1) * size, :] = rows_of(lax.rem(near + 2 * p, parts)).astype(BF16)
+
+
+def gradient(wide, source, after, axis, positions, others, sequences):
     depth = PROJECTED_DEPTH
     parts = lax.axis_size(axis)
     rows = sequences // parts * positions * depth // LANES
-    shapes = [jax.ShapeDtypeStruct((rows, LANES), F32)] * kept
-    group = (parts - kept) // groups
-    shapes += [jax.ShapeDtypeStruct((group * rows, LANES), BF16)] * groups
+    shapes = [jax.ShapeDtypeStruct((rows, LANES), F32)] * (parts // 2)
+    shapes += [jax.ShapeDtypeStruct((parts // 2 * rows, LANES), BF16)]
     tiles = GROUP * sequences // LANES if wide.ndim == 2 else 1
-    results = pl.pallas_call(
-        functools.partial(gradient_kernel, axis, plan, kept, positions, others, sequences),
+    *kept, message = pl.pallas_call(
+        functools.partial(gradient_kernel, axis, positions, others, sequences),
         in_specs=[in_vmem(), in_vmem(), pl.BlockSpec(memory_space=pl.ANY)],
         out_specs=[in_vmem()] * len(shapes),
         out_shape=shapes,
@@ -399,7 +372,7 @@
             transcendentals=0,
         ),
     )(wide, source, after)
-    return results[:kept], results[kept:]
+    return kept, message
 
 
 def product_kernel(left_ref, right_ref, _, out_ref):
@@ -422,12 +395,13 @@
     )(left, right, after)
 
 
-def pair_kernel(sequences, x_ref, wt_ref, bias_ref, out_ref):
+def pair_kernel(sequences, x_ref, wt_ref, bias_ref, _, out_ref, done_ref):
+    done_ref[...] = jnp.zeros(done_ref.shape, F32)
     product = dot(wt_ref[...], x_ref[...])
     out_ref[...] = (product.T * (1.0 / sequences) + bias_ref[...]).astype(BF16)
 
 
-def pair(x, wt, output_bias, sequences):
+def pair(x, wt, output_bias, after, sequences):
     channels, pairs = x.shape
     count = 3
     size = pairs // count
@@ -438,16 +412,20 @@
             pl.BlockSpec((channels, size), lambda t: (0, t)),
             whole(wt.shape),
             whole((1, PAIR_FEATURES)),
+            pl.BlockSpec(memory_space=pl.ANY),
         ],
-        out_specs=pl.BlockSpec((size, PAIR_FEATURES), lambda t: (t, 0)),
-        out_shape=jax.ShapeDtypeStruct((pairs, PAIR_FEATURES), BF16),
+        out_specs=[pl.BlockSpec((size, PAIR_FEATURES), lambda t: (t, 0)), whole((8, LANES))],
+        out_shape=[
+            jax.ShapeDtypeStruct((pairs, PAIR_FEATURES), BF16),
+            jax.ShapeDtypeStruct((8, LANES), F32),
+        ],
         compiler_params=params(),
         cost_estimate=pl.CostEstimate(
             flops=4 * pairs * channels * PAIR_FEATURES,
             bytes_accessed=2 * pairs * channels,
             transcendentals=0,
         ),
-    )(x, wt, output_bias.reshape(1, PAIR_FEATURES))
+    )(x, wt, output_bias.reshape(1, PAIR_FEATURES), after)
 
 
 def unfold(total, share, out):
@@ -467,11 +445,11 @@
     )(*operands, *after)
 
 
-def row_sum(parts, grad, share):
+def row_sum(parts, after, share):
     count = len(parts)
 
     def kernel(*refs):
-        parts, (grad, message, held) = refs[:count], refs[count:]
+        parts, (_, message, held) = refs[:count], refs[count:]
         me = lax.axis_index("row")
         total = parts[0][0:share, :]
         for p, part in enumerate(parts):
@@ -482,89 +460,91 @@
         for n in range(1, count):
             bias += joined(held[n])
         message[0:share, :] = total.astype(BF16)
-        message[share : share + BIAS_ROWS, :] = split(bias)
-        message[share + BIAS_ROWS :, :] = grad[...]
-
-    shape = (share + BIAS_ROWS + grad.shape[0], LANES)
+        message[share:, :] = split(bias)
+
     scratch = [pltpu.VMEM((count, BIAS_ROWS, LANES), F32)]
-    (message,) = call(kernel, [*parts, grad], [(shape, BF16)], scratch=scratch)
+    (message,) = call(kernel, parts, [((share + BIAS_ROWS, LANES), BF16)], [after], scratch)
     return message
 
 
-def column_pair_sum(own, near, grads, after, share):
+def add_near(kept, near, own, messages):
+    size = own.shape[0]
+    for p, part in enumerate(kept):
+        both = part[...] + near[p * size : (p + 1) * size, :].astype(F32)
+        if p == 0:
+            own[...] = both
+        else:
+            messages[p - 1][...] = both.astype(BF16)
+
+
+def column_pair_sum(own, near, kept, grad_near, passed, share):
+    count = len(kept)
+
+    def kernel(own, near, grad_near, passed, *refs):
+        kept, (message, passed_on, grad_own), messages = (
+            refs[:count],
+            refs[count : count + 3],
+            refs[count + 3 :],
+        )
+        passed_on[...] = passed[...]
+        total = own[0:share, :].astype(F32) + near[0:share, :].astype(F32)
+        message[0:share, :] = total.astype(BF16)
+        message[share:, :] = split(joined(own[share:, :]) + joined(near[share:, :]))
+        add_near(kept, grad_near, grad_own, messages)
+
+    size = kept[0].shape
+    shapes = [(own.shape, BF16), (passed.shape, BF16), (size, F32)] + [(size, BF16)] * (count - 1)
+    message, passed, grad_own, *messages = call(
+        kernel, [own, near, grad_near, passed, *kept], shapes
+    )
+    return message, passed, grad_own, messages
+
+
+def column_sum(parts, kept, grad_near, after, share):
     rows = share + BIAS_ROWS
-    size = grads[0].shape[0]
-
-    def kernel(own, near, *refs):
-        grads, left_out, messages = refs[: len(grad_list)], refs[len(grad_list) + 1], refs[len(grad_list) + 2 :]
-        total = (own[0:share, :].astype(F32) + near[0:share, :].astype(F32)).astype(BF16)
-        bias = split(joined(own[share:rows, :]) + joined(near[share:rows, :]))
-        for n, grad in enumerate(grads):
-            both = grad[...] + near[rows + n * size : rows + (n + 1) * size, :].astype(F32)
-            if n == 0:
-                left_out[...] = both
-            else:
-                messages[n - 1][0:share, :] = total
-                messages[n - 1][share:rows, :] = bias
-                messages[n - 1][rows:, :] = both.astype(BF16)
-
-    grad_list = list(grads)
-    shapes = [((size, LANES), F32)] + [((rows + size, LANES), BF16)] * (len(grad_list) - 1)
-    left, *messages = call(kernel, [own, near, *grad_list], shapes, [after])
-    return left, messages
-
-
-def column_sum(parts, left_own, own, grads, share):
-    rows = share + BIAS_ROWS
-    count = len(parts) + 1
-    sent = len(grads)
-
-    def kernel(*refs):
-        parts, (grad, own), refs = refs[: count - 1], refs[count - 1 : count + 1], refs[count + 1 :]
-        grads, messages, (piece_out, left_out, bias_out, held) = refs[:sent], refs[sent:-4], refs[-4:]
+    count = len(parts)
+    kept_n = len(kept)
+
+    def kernel(grad_near, *refs):
+        parts, kept = refs[:count], refs[count : count + kept_n]
+        refs = refs[count + kept_n + len(after) :]
+        piece_out, bias_out, grad_own, *messages, held = refs
         home = lax.div(lax.axis_index("col"), 2)
-        for p, part in enumerate((own, *parts)):
-            held[lax.rem(home - p + count, count)] = part[0:rows, :]
+        for p, part in enumerate(parts):
+            held[lax.rem(home - p + count, count)] = part[...]
         total, bias = held[0, 0:share, :].astype(F32), joined(held[0, share:, :])
         for n in range(1, count):
             total += held[n, 0:share, :].astype(F32)
             bias += joined(held[n, share:, :])
-        piece = total.astype(BF16)
-        piece_out[...] = piece
-        for message, other in zip(messages, grads, strict=True):
-            message[0:share, :] = piece
-            message[share:, :] = other[...]
+        piece_out[...] = total.astype(BF16)
         bias_out[...] = jnp.broadcast_to(bias, bias_out.shape)
-        left = grad[...]
-        for part in parts:
-            left += part[rows:, :].astype(F32)
-        left_out[...] = left
-
-    shapes = [((share + grad.shape[0], LANES), BF16) for grad in grads]
-    shapes += [((share, LANES), BF16), (left_own.shape, F32), ((8, LANES), F32)]
+        add_near(kept, grad_near, grad_own, messages)
+
+    size = kept[0].shape
+    shapes = [((share, LANES), BF16), ((8, LANES), F32), (size, F32)] + [(size, BF16)] * (kept_n - 1)
     scratch = [pltpu.VMEM((count, rows, LANES), BF16)]
-    *messages, piece, left, bias = call(
-        kernel, [*parts, left_own, own, *grads], shapes, scratch=scratch
-    )
-    return messages, piece, left, bias
-
-
-def finish(parts, piece, left, right_own, bias, left_shape, right_shape, scale, bias_scale):
-    count = len(parts) + 1
-    share = piece.shape[0]
+    piece, bias, grad_own, *messages = call(
+        kernel, [grad_near, *parts, *kept], shapes, after, scratch
+    )
+    return piece, bias, grad_own, messages
+
+
+def finish(pieces, left, right, bias, left_shape, right_shape, scale, bias_scale):
+    count, left_n = len(pieces), len(left)
+    share = pieces[0].shape[0]
 
     def kernel(*refs):
-        parts, refs = refs[: count - 1], refs[count - 1 :]
-        piece, left, right_own, bias, projection, left_out, right_out, bias_out = refs
+        pieces, left, right = refs[:count], refs[count : count + left_n], refs[count + left_n : -5]
+        bias, projection, left_out, right_out, bias_out = refs[-5:]
         me = lax.axis_index("row")
-        right = right_own[...]
-        for p, part in enumerate((piece, *parts)):
+        for p, piece in enumerate(pieces):
             rows = pl.ds(pl.multiple_of(lax.rem(me - p + count, count) * share, share), share)
-            projection[rows, :] = part[0:share, :].astype(F32) * scale
-            if p > 0:
-                right += part[share:, :].astype(F32)
-        unfold(left[...], left_out.shape[0], left_out)
-        unfold(right, right_out.shape[0], right_out)
+            projection[rows, :] = piece[...].astype(F32) * scale
+        for terms, out in ((left, left_out), (right, right_out)):
+            total = terms[0][...]
+            for term in terms[1:]:
+                total += term[...].astype(F32)
+            unfold(total, out.shape[0], out)
         bias_out[...] = bias[0:1, :] * bias_scale
 
     shapes = [
@@ -573,7 +553,7 @@
         (right_shape, F32),
         ((1, PAIR_FEATURES), F32),
     ]
-    return call(kernel, [*parts, piece, left, right_own, bias], shapes)
+    return call(kernel, [*pieces, *left, *right, bias], shapes)
 
 
 def shift(x, axis, distance):
@@ -585,12 +565,12 @@
     return lax.ppermute(x, axis, [(n, n ^ 1) for n in range(lax.axis_size(axis))])
 
 
-def shift_pairs(x, axis):
-    return [x] + [shift(x, axis, d) for d in range(2, lax.axis_size(axis), 2)]
-
-
 def send(parts, axis):
     return [shift(part, axis, d) for d, part in enumerate(parts, 1)]
+
+
+def spread_pairs(x, axis):
+    return send_pairs([x] * (lax.axis_size(axis) // 2 - 1), axis)
 
 
 def send_pairs(parts, axis):
@@ -601,21 +581,21 @@
     first_homolog_features, second_homolog_features, final_projection_matrix, output_bias, cotangent
 ):
     i_n, j_n, _ = cotangent.shape
-    row_n, col_n = lax.axis_size("row"), lax.axis_size("col")
+    row_n = lax.axis_size("row")
     sequences = second_homolog_features.shape[0] * row_n
     channels = final_projection_matrix.shape[0]
     res_total = i_n * row_n
-    a_near = neighbour(first_homolog_features, "col")
-    b_near = neighbour(second_homolog_features, "row")
+    a_far = spread_pairs(first_homolog_features, "col")
+    b_far = spread_pairs(second_homolog_features, "row")
     we, wt, a, b, w, g = load(
         first_homolog_features,
         second_homolog_features,
         final_projection_matrix,
         cotangent.reshape(i_n * j_n, PAIR_FEATURES),
     )
-    a_pair, b_pair = stack((a, a_near), (b, b_near))
-    a_pieces = shift_pairs(a_pair, "col")
-    b_pieces = shift_pairs(b_pair, "row")
+    a, b = stack([a, *a_far], [b, *b_far])
+    a_pieces = [a, neighbour(a, "col")]
+    b_pieces = [b, neighbour(b, "row")]
     y, gt, bias_rows = prepare(we, g, i_n, j_n)
 
     x, a_held, b_wide, (own, *messages) = outer(
@@ -624,27 +604,31 @@
     share = channels // row_n
 
     parts = [own] + send(messages, "row")
-    left_kept, (left_sent,) = gradient(
-        b_wide, y, own, "col", in_pairs(col_n), col_n // 2, 1, i_n, j_n, sequences
-    )
-
-    message = row_sum(parts, left_sent, share)
+    y2 = product(w, gt, own)
+    right_kept, message = gradient(a_held, y2, own, "row", j_n, i_n, sequences)
+    right_near = neighbour(message, "row")
+
+    message = row_sum(parts, message, share)
     near = neighbour(message, "col")
-    y2 = product(w, gt, message)
-    left_own, messages = column_pair_sum(message, near, left_kept, y2, share)
-    parts = send_pairs(messages, "col")
-    (right_own,), right_sent = gradient(
-        a_held, y2, left_own, "row", in_order(row_n), 1, row_n - 1, j_n, i_n, sequences
-    )
-
-    messages, piece, left_own, bias = column_sum(parts, left_own, messages[0], right_sent, share)
-    parts = send(messages, "row")
-    pair_map = pair(x, wt, output_bias, sequences)
+    left_kept, left_message = gradient(b_wide, y, message, "col", i_n, j_n, sequences)
+    message, left_message, right_own, right_messages = column_pair_sum(
+        message, near, right_kept, right_near, left_message, share
+    )
+
+    parts = [message] + spread_pairs(message, "col")
+    left_near = neighbour(left_message, "col")
+    right = [right_own] + send_pairs(right_messages, "row")
+    pair_map, pair_done = pair(x, wt, output_bias, message, sequences)
+    piece, bias, left_own, left_messages = column_sum(
+        parts, left_kept, left_near, [pair_done, *right[1:]], share
+    )
+
+    pieces = [piece] + send([piece] * (row_n - 1), "row")
+    left = [left_own] + send_pairs(left_messages, "col")
     projection, left_grad, right_grad, bias_grad = finish(
-        parts,
-        piece,
-        left_own,
-        right_own,
+        pieces,
+        left,
+        right,
         bias,
         first_homolog_features.shape,
         second_homolog_features.shape,

time: 43.6 us -> 44.8 us (1.028)
  starting transfers between devices: 16.6 us -> 17.3 us
  waiting for transfers between devices: 8.31 us -> 8.99 us
    ppermute x9 -> x11, waiting for transfers between devices: 4.89 us -> 7.67 us  [shift(): lax.ppermute(x, axis, [(n, (n + distance) % count) for n in range(count)])]
    ppermute x3 -> x5, waiting for transfers between devices: 3.43 us -> 1.32 us  [neighbour(): lax.ppermute(x, axis, [(n, n ^ 1) for n in range(lax.axis_size(axis))])]
    ppermute x9 -> x11, starting transfers between devices: 11.9 us -> 12.5 us  [shift(): lax.ppermute(x, axis, [(n, (n + distance) % count) for n in range(count)])]
    ppermute x3 -> x5, starting transfers between devices: 4.72 us -> 4.87 us  [neighbour(): lax.ppermute(x, axis, [(n, n ^ 1) for n in range(lax.axis_size(axis))])]
    pallas_call x4 -> x3, Pallas kernels: 9.43 us -> 9.44 us  [the longest x1 4.8 us: outer(): pl.pallas_call(functools.partial(outer_kernel, i_n, j_n), in_specs=[in_vm...]
    pallas_call x4 -> x5, Pallas kernels: 1.01 us -> 1 us  [call(): pl.pallas_call(kernel, in_specs=specs, out_specs=[in_vmem()] * len(shapes...]
  transfers between devices with their start and end apart: 12 -> 16, of which waited for: 5 -> 5; matrix products, arithmetic and copies ran while one was open for 0% -> 0% of each run, Pallas kernels for 27% -> 26%
where the time goes in v10:
time: 44.8 us; the launch traced here: 44.6 us
  Pallas kernels  17.5 us (39%)
  starting transfers between devices  17.3 us (39%)
  waiting for transfers between devices  8.99 us (20%)
  between operations  0.77 us (2%)
    ppermute x11, starting transfers between devices, shift(): lax.ppermute(x, axis, [(n, (n + distance) % count) for n in range(count)])  12.5 us
    ppermute x11, waiting for transfers between devices, shift(): lax.ppermute(x, axis, [(n, (n + distance) % count) for n in range(count)])  7.67 us
    ppermute x5, starting transfers between devices, neighbour(): lax.ppermute(x, axis, [(n, n ^ 1) for n in range(lax.axis_size(axis))])  4.87 us
    pallas_call x1, Pallas kernels, outer(): pl.pallas_call(functools.partial(outer_kernel, i_n, j_n), in_specs=[in_vm...  4.8 us
    pallas_call x2, Pallas kernels, gradient(): pl.pallas_call(functools.partial(gradient_kernel, axis, positions, others...  4.65 us
    pallas_call x1, Pallas kernels, pair(): pl.pallas_call(functools.partial(pair_kernel, sequences), grid=(count,),...  2.55 us
    pallas_call x1, Pallas kernels, prepare(): pl.pallas_call(functools.partial(prepare_kernel, i_n, j_n), in_specs=[in_...  1.75 us
    pallas_call x1, Pallas kernels, load(): pl.pallas_call(load_kernel, in_specs=[pl.BlockSpec(memory_space=pltpu.HBM...  1.39 us
  transfers between devices with their start and end apart: 16, of which 5 were waited for; matrix products, arithmetic and copies ran while one was open for 0% of the time, Pallas kernels for 26%

profile of v10, /device:TPU:0, one launch (start us, length us, event | category | flops | bytes accessed | tf_op | source)
XLA Modules:
  0.0 44.6 jit_solution(1164935646971388902)
XLA Ops:
  0.6 4.1 %collective-permute-start = (bf16[8,1536]{1,0:T(8,128)(2,1)}, bf16[8,1536]{1,0:T(8,128)(2,1)S(1)}, u32[]{:S(2)}, u32[]{:S(2)}) collective-permute-start(bf16[8,1536]{1,0:T(8,128)(2,1)} %a_hbm.1), channel_id=1, source_target_pairs={{0,2},{1,3},{2,0},{3,1},{4,6},{5,7},{6,4},{7,5},{8,10},{9,11},{10,... | collective-permute-start | bytes 73736 | tf_op jit(solution)/shard_map/ppermute | solution.py:561
  4.7 1.5 %collective-permute-start.1 = (bf16[8,1536]{1,0:T(8,128)(2,1)}, bf16[8,1536]{1,0:T(8,128)(2,1)S(1)}, u32[]{:S(2)}, u32[]{:S(2)}) collective-permute-start(bf16[8,1536]{1,0:T(8,128)(2,1)} %b_hbm.1), channel_id=1, source_target_pairs={{0,8},{4,12},{8,0},{12,4},{1,9},{5,13},{9,1},{13,5},{2,10},{6,14},... | collective-permute-start | bytes 73736 | tf_op jit(solution)/shard_map/ppermute | solution.py:561
  6.2 1.4 %shard_map.92 = (bf16[1024,128]{1,0:T(8,128)(2,1)S(1)}, bf16[128,1024]{1,0:T(8,128)(2,1)S(1)}, bf16[8,1536]{1,0:T(8,128)(2,1)S(1)}, bf16[8,1536]{1,0:T(8,128)(2,...) custom-call(bf16[8,1536]{1,0:T(8,128)(2,1)} %a_hbm.1, bf16[8,1536]{1,0:T(8,128)(2,1)} %b_hbm.1, ...), custom_call_target="tpu_custom_call" | custom-call | flops 131072000 | bytes 2097152 | tf_op jit(solution)/shard_map/pallas_call | solution.py:67
  7.6 1.1 %collective-permute-done.1.refs_3_ = bf16[8,1536]{1,0:T(8,128)(2,1)S(1)} collective-permute-done((bf16[8,1536]{1,0:T(8,128)(2,1)}, bf16[8,1536]{1,0:T(8,128)(2,1)S(1)}, u32[]{:S(2)}, u32[]{:S(2)}) %collective-permute-start.1) | collective-permute-done | bytes 24608 | tf_op jit(solution)/shard_map/ppermute | solution.py:561
  8.8 1.6 %collective-permute-start.2 = (bf16[16,1536]{1,0:T(8,128)(2,1)S(1)}, bf16[16,1536]{1,0:T(8,128)(2,1)S(1)}, u32[]{:S(2)}, u32[]{:S(2)}) collective-permute-start(bf16[16,1536]{1,0:T(8,128)(2,1)S(1)} %get-tuple-element.45.refs_0_), channel_id=1, source_target_pairs={{0,1},{1,0},{2,3},{3,2},{4,5},{5,4},{6,7},{7,6},{8,9},{9,8},{10,11... | collective-permute-start | bytes 147464 | tf_op jit(solution)/shard_map/ppermute | solution.py:565
  10.4 0.0 collective-permute-start.3
  10.4 1.8 %shard_map.94 = (bf16[1024,2304]{1,0:T(8,128)(2,1)S(1)}, bf16[2304,128]{1,0:T(8,128)(2,1)S(1)}, bf16[16,128]{1,0:T(8,128)(2,1)S(1)}) custom-call(bf16[1024,128]{1,0:T(8,128)(2,1)S(1)} %get-tuple-element.48.we_ref, bf16[2304,128]{1,0:T(8,128)(2,1)S(1)} %get-tuple-element.47.g_ref.refs_4_), custom_call_target="tpu_custom_call" | custom-call | flops 603979776 | bytes 9437184 | tf_op jit(solution)/shard_map/pallas_call | solution.py:126
  12.2 0.7 %collective-permute-done.2.refs_1_ = bf16[16,1536]{1,0:T(8,128)(2,1)S(1)} collective-permute-done((bf16[16,1536]{1,0:T(8,128)(2,1)S(1)}, bf16[16,1536]{1,0:T(8,128)(2,1)S(1)}, u32[]{:S(2)}, u32[]{:S(2)}) %collective-permute-start.2) | collective-permute-done | bytes 49184 | tf_op jit(solution)/shard_map/ppermute | solution.py:565
  12.9 0.0 collective-permute-done.3.refs_3_
  12.9 4.8 %shard_map.95 = (bf16[1024,2304]{1,0:T(8,128)(2,1)S(1)}, f32[32,1536]{1,0:T(8,128)S(1)}, f32[2,1536,128]{2,1,0:T(8,128)S(1)}, f32[272,128]{1,0:T(8,128)S(1)}, bf...) custom-call(bf16[16,1536]{1,0:T(8,128)(2,1)S(1)} %get-tuple-element.45.refs_0_, ...), custom_call_target="tpu_custom_call" | custom-call | flops 1207959552 | bytes 4718592 | tf_op jit(solution)/shard_map/pallas_call | solution.py:266
  17.7 0.1 collective-permute-start.4
  17.8 1.5 %collective-permute-start.5 = (bf16[272,128]{1,0:T(8,128)(2,1)S(1)}, bf16[272,128]{1,0:T(8,128)(2,1)S(1)}, u32[]{:S(2)}, u32[]{:S(2)}) collective-permute-start(bf16[272,128]{1,0:T(8,128)(2,1)S(1)} %get-tuple-element.54), channel_id=1, source_target_pairs={{0,8},{4,12},{8,0},{12,4},{1,9},{5,13},{9,1},{13,5},{2,10},{6,14},... | collective-permute-start | bytes 208904 | tf_op jit(solution)/shard_map/ppermute | solution.py:561
  19.4 1.4 %collective-permute-start.6 = (bf16[272,128]{1,0:T(8,128)(2,1)S(1)}, bf16[272,128]{1,0:T(8,128)(2,1)S(1)}, u32[]{:S(2)}, u32[]{:S(2)}) collective-permute-start(bf16[272,128]{1,0:T(8,128)(2,1)S(1)} %get-tuple-element.55), channel_id=1, source_target_pairs={{0,12},{4,0},{8,4},{12,8},{1,13},{5,1},{9,5},{13,9},{2,14},{6,2},{... | collective-permute-start | bytes 208904 | tf_op jit(solution)/shard_map/ppermute | solution.py:561
  20.7 1.4 %shard_map.96.refs_1_ = bf16[1024,2304]{1,0:T(8,128)(2,1)S(1)} custom-call(bf16[1024,128]{1,0:T(8,128)(2,1)S(1)} %get-tuple-element.57.left_ref, bf16[2304,128]{1,0:T(8,128)(2,1)S(1)} %get-tuple-element.58.right_ref, f32[272,128]{1,0:T(8,128)S(1)} %get-tuple-element.52._.refs_2_.refs_0_), custom_call_target="tpu_custom_call" | custom-call | flops 603979776 | bytes 9437184 | tf_op jit(solution)/shard_map/pallas_call | solution.py:384
  22.1 2.5 %shard_map.97 = (f32[96,128]{1,0:T(8,128)S(1)}, f32[96,128]{1,0:T(8,128)S(1)}, bf16[192,128]{1,0:T(8,128)(2,1)S(1)}) custom-call(f32[32,1536]{1,0:T(8,128)S(1)} %get-tuple-element.56.refs_0_, bf16[1024,2304]{1,0:T(8,128)(2,1)S(1)} %shard_map.96.refs_1_, f32[272,128]{1,0:T(8,128)S(1)} %get-tuple-element.52._.refs_2_.refs_0_), custom_call_target="tpu_custom_call" | custom-call | flops 603979776 | bytes 4718592 | tf_op jit(solution)/shard_map/pallas_call | solution.py:357
  24.6 0.0 copy-start
  24.7 0.0 collective-permute-done.4.refs_1_
  24.7 0.0 collective-permute-done.5.refs_2_
  24.7 1.6 %collective-permute-start.7 = (bf16[272,128]{1,0:T(8,128)(2,1)S(1)}, bf16[272,128]{1,0:T(8,128)(2,1)S(1)}, u32[]{:S(2)}, u32[]{:S(2)}) collective-permute-start(bf16[272,128]{1,0:T(8,128)(2,1)S(1)} %shard_map.98.refs_2_.own), channel_id=1, source_target_pairs={{0,1},{1,0},{2,3},{3,2},{4,5},{5,4},{6,7},{7,6},{8,9},{9,8},{10,11... | collective-permute-start | bytes 208904 | tf_op jit(solution)/shard_map/ppermute | solution.py:565
  26.4 2.1 %shard_map.99 = (f32[96,128]{1,0:T(8,128)S(1)}, f32[96,128]{1,0:T(8,128)S(1)}, bf16[192,128]{1,0:T(8,128)(2,1)S(1)}) custom-call(f32[2,1536,128]{2,1,0:T(8,128)S(1)} %get-tuple-element.60.refs_0_, bf16[1024,2304]{1,0:T(8,128)(2,1)S(1)} %get-tuple-element.61.refs_1_, bf16[272,128]{1,0:T(8,128)(2,1)S(1)} %shard_map.98.refs_2_.own), custom_call_target="tpu_custom_call" | custom-call | flops 603979776 | bytes 4718592 | tf_op jit(solution)/shard_map/pallas_call | solution.py:357
  28.6 0.6 %collective-permute-done.7.near = bf16[272,128]{1,0:T(8,128)(2,1)S(1)} collective-permute-done((bf16[272,128]{1,0:T(8,128)(2,1)S(1)}, bf16[272,128]{1,0:T(8,128)(2,1)S(1)}, u32[]{:S(2)}, u32[]{:S(2)}) %collective-permute-start.7) | collective-permute-done | bytes 69664 | tf_op jit(solution)/shard_map/ppermute | solution.py:565
  29.2 0.6 %collective-permute-start.11 = (bf16[96,128]{1,0:T(8,128)(2,1)S(1)}, bf16[96,128]{1,0:T(8,128)(2,1)S(1)}, u32[]{:S(2)}, u32[]{:S(2)}) collective-permute-start(bf16[96,128]{1,0:T(8,128)(2,1)S(1)} %get-tuple-element.71), channel_id=1, source_target_pairs={{0,8},{4,12},{8,0},{12,4},{1,9},{5,13},{9,1},{13,5},{2,10},{6,14},... | collective-permute-start | bytes 73736 | tf_op jit(solution)/shard_map/ppermute | solution.py:561
  29.8 1.6 %collective-permute-start.9 = (bf16[192,128]{1,0:T(8,128)(2,1)S(1)}, bf16[192,128]{1,0:T(8,128)(2,1)S(1)}, u32[]{:S(2)}, u32[]{:S(2)}) collective-permute-start(bf16[192,128]{1,0:T(8,128)(2,1)S(1)} %get-tuple-element.67), channel_id=1, source_target_pairs={{0,1},{1,0},{2,3},{3,2},{4,5},{5,4},{6,7},{7,6},{8,9},{9,8},{10,11... | collective-permute-start | bytes 147464 | tf_op jit(solution)/shard_map/ppermute | solution.py:565
  31.3 1.1 %collective-permute-start.10 = (bf16[272,128]{1,0:T(8,128)(2,1)S(1)}, bf16[272,128]{1,0:T(8,128)(2,1)S(1)}, u32[]{:S(2)}, u32[]{:S(2)}) collective-permute-start(bf16[272,128]{1,0:T(8,128)(2,1)S(1)} %get-tuple-element.65._.refs_0_), channel_id=1, source_target_pairs={{0,2},{1,3},{2,0},{3,1},{4,6},{5,7},{6,4},{7,5},{8,10},{9,11},{10,... | collective-permute-start | bytes 208904 | tf_op jit(solution)/shard_map/ppermute | solution.py:561
  32.4 2.5 %shard_map.101 = (bf16[2304,128]{1,0:T(8,128)(2,1)}, f32[8,128]{1,0:T(8,128)S(1)}) custom-call(bf16[1024,2304]{1,0:T(8,128)(2,1)S(1)} %get-tuple-element.50.x_ref, bf16[128,1024]{1,0:T(8,128)(2,1)S(1)} %get-tuple-element.51.wt_ref, f32[1,128]{1,0:T(1,128)S(1)} %bitcast.4, bf16[272,128]{1,0:T(8,128)(2,1)S(1)} %get-tuple-element.65._.refs_0_), custom_call_target="tpu_custom_call" | custom-call | flops 1207959552 | bytes 4718592 | tf_op jit(solution)/shard_map/pallas_call | solution.py:408
  35.0 2.2 %collective-permute-done.10.refs_1_ = bf16[272,128]{1,0:T(8,128)(2,1)S(1)} collective-permute-done((bf16[272,128]{1,0:T(8,128)(2,1)S(1)}, bf16[272,128]{1,0:T(8,128)(2,1)S(1)}, u32[]{:S(2)}, u32[]{:S(2)}) %collective-permute-start.10) | collective-permute-done | bytes 69664 | tf_op jit(solution)/shard_map/ppermute | solution.py:561
  37.2 0.1 collective-permute-start.14
  37.3 1.6 %collective-permute-start.13 = (bf16[256,128]{1,0:T(8,128)(2,1)S(1)}, bf16[256,128]{1,0:T(8,128)(2,1)S(1)}, u32[]{:S(2)}, u32[]{:S(2)}) collective-permute-start(bf16[256,128]{1,0:T(8,128)(2,1)S(1)} %get-tuple-element.72.refs_0_), channel_id=1, source_target_pairs={{0,8},{4,12},{8,0},{12,4},{1,9},{5,13},{9,1},{13,5},{2,10},{6,14},... | collective-permute-start | bytes 196616 | tf_op jit(solution)/shard_map/ppermute | solution.py:561
  38.8 0.2 collective-permute-start.12
  39.0 0.4 collective-permute-start.15
  39.4 4.3 %collective-permute-done.15.refs_5_ = bf16[96,128]{1,0:T(8,128)(2,1)S(1)} collective-permute-done((bf16[96,128]{1,0:T(8,128)(2,1)S(1)}, bf16[96,128]{1,0:T(8,128)(2,1)S(1)}, u32[]{:S(2)}, u32[]{:S(2)}) %collective-permute-start.15) | collective-permute-done | bytes 24608 | tf_op jit(solution)/shard_map/ppermute | solution.py:561
  43.8 0.9 %shard_map.103 = (f32[1024,128]{1,0:T(8,128)}, f32[8,1536]{1,0:T(8,128)}, f32[8,1536]{1,0:T(8,128)}, f32[1,128]{1,0:T(1,128)}) custom-call(bf16[256,128]{1,0:T(8,128)(2,1)S(1)} %get-tuple-element.72.refs_0_, bf16[256,128]{1,0:T(8,128)(2,1)S(1)} %collective-permute-done.12.refs_1_, bf16[256,128]{1,0:T(8,128)(2,1)S(1)} %collective-permute-done.13.refs_2_, ...), custom_call_target="tpu_custom_call" | custom-call | tf_op jit(solution)/shard_map/pallas_call | solution.py:438
  (14 shorter events, 0.2 us)
Async XLA Ops:
  0.6 7.0 %collective-permute-start = (bf16[8,1536]{1,0:T(8,128)(2,1)}, bf16[8,1536]{1,0:T(8,128)(2,1)S(1)}, u32[]{:S(2)}, u32[]{:S(2)}) collective-permute-start(bf16[8,1536]{1,0:T(8,128)(2,1)} %a_hbm.1), channel_id=1, source_target_pairs={{0,2},{1,3},{2,0},{3,1},{4,6},{5,7},{6,4},{7,5},{8,10},{9,11},{10,... | collective-permute-start | bytes 73736 | tf_op jit(solution)/shard_map/ppermute | solution.py:561
  4.7 4.0 %collective-permute-start.1 = (bf16[8,1536]{1,0:T(8,128)(2,1)}, bf16[8,1536]{1,0:T(8,128)(2,1)S(1)}, u32[]{:S(2)}, u32[]{:S(2)}) collective-permute-start(bf16[8,1536]{1,0:T(8,128)(2,1)} %b_hbm.1), channel_id=1, source_target_pairs={{0,8},{4,12},{8,0},{12,4},{1,9},{5,13},{9,1},{13,5},{2,10},{6,14},... | collective-permute-start | bytes 73736 | tf_op jit(solution)/shard_map/ppermute | solution.py:561
  8.8 4.2 %collective-permute-start.2 = (bf16[16,1536]{1,0:T(8,128)(2,1)S(1)}, bf16[16,1536]{1,0:T(8,128)(2,1)S(1)}, u32[]{:S(2)}, u32[]{:S(2)}) collective-permute-start(bf16[16,1536]{1,0:T(8,128)(2,1)S(1)} %get-tuple-element.45.refs_0_), channel_id=1, source_target_pairs={{0,1},{1,0},{2,3},{3,2},{4,5},{5,4},{6,7},{7,6},{8,9},{9,8},{10,11... | collective-permute-start | bytes 147464 | tf_op jit(solution)/shard_map/ppermute | solution.py:565
  10.4 2.5 %collective-permute-start.3 = (bf16[16,1536]{1,0:T(8,128)(2,1)S(1)}, bf16[16,1536]{1,0:T(8,128)(2,1)S(1)}, u32[]{:S(2)}, u32[]{:S(2)}) collective-permute-start(bf16[16,1536]{1,0:T(8,128)(2,1)S(1)} %get-tuple-element.46.refs_2_), channel_id=1, source_target_pairs={{0,4},{4,0},{8,12},{12,8},{1,5},{5,1},{9,13},{13,9},{2,6},{6,2},{1... | collective-permute-start | bytes 147464 | tf_op jit(solution)/shard_map/ppermute | solution.py:565
  17.7 6.9 %collective-permute-start.4 = (bf16[272,128]{1,0:T(8,128)(2,1)S(1)}, bf16[272,128]{1,0:T(8,128)(2,1)S(1)}, u32[]{:S(2)}, u32[]{:S(2)}) collective-permute-start(bf16[272,128]{1,0:T(8,128)(2,1)S(1)} %get-tuple-element.53), channel_id=1, source_target_pairs={{0,4},{4,8},{8,12},{12,0},{1,5},{5,9},{9,13},{13,1},{2,6},{6,10},{... | collective-permute-start | bytes 208904 | tf_op jit(solution)/shard_map/ppermute | solution.py:561
  17.8 6.9 %collective-permute-start.5 = (bf16[272,128]{1,0:T(8,128)(2,1)S(1)}, bf16[272,128]{1,0:T(8,128)(2,1)S(1)}, u32[]{:S(2)}, u32[]{:S(2)}) collective-permute-start(bf16[272,128]{1,0:T(8,128)(2,1)S(1)} %get-tuple-element.54), channel_id=1, source_target_pairs={{0,8},{4,12},{8,0},{12,4},{1,9},{5,13},{9,1},{13,5},{2,10},{6,14},... | collective-permute-start | bytes 208904 | tf_op jit(solution)/shard_map/ppermute | solution.py:561
  19.4 5.3 %collective-permute-start.6 = (bf16[272,128]{1,0:T(8,128)(2,1)S(1)}, bf16[272,128]{1,0:T(8,128)(2,1)S(1)}, u32[]{:S(2)}, u32[]{:S(2)}) collective-permute-start(bf16[272,128]{1,0:T(8,128)(2,1)S(1)} %get-tuple-element.55), channel_id=1, source_target_pairs={{0,12},{4,0},{8,4},{12,8},{1,13},{5,1},{9,5},{13,9},{2,14},{6,2},{... | collective-permute-start | bytes 208904 | tf_op jit(solution)/shard_map/ppermute | solution.py:561
  24.6 7.7 %copy-start = (f32[128]{0:T(128)S(1)}, f32[128]{0:T(128)}, u32[]{:S(2)}) copy-start(f32[128]{0:T(128)} %param.8) | copy-start | bytes 1540
  24.7 4.4 %collective-permute-start.7 = (bf16[272,128]{1,0:T(8,128)(2,1)S(1)}, bf16[272,128]{1,0:T(8,128)(2,1)S(1)}, u32[]{:S(2)}, u32[]{:S(2)}) collective-permute-start(bf16[272,128]{1,0:T(8,128)(2,1)S(1)} %shard_map.98.refs_2_.own), channel_id=1, source_target_pairs={{0,1},{1,0},{2,3},{3,2},{4,5},{5,4},{6,7},{7,6},{8,9},{9,8},{10,11... | collective-permute-start | bytes 208904 | tf_op jit(solution)/shard_map/ppermute | solution.py:565
  26.4 2.2 %collective-permute-start.8 = (bf16[192,128]{1,0:T(8,128)(2,1)S(1)}, bf16[192,128]{1,0:T(8,128)(2,1)S(1)}, u32[]{:S(2)}, u32[]{:S(2)}) collective-permute-start(bf16[192,128]{1,0:T(8,128)(2,1)S(1)} %get-tuple-element.59.refs_4_), channel_id=1, source_target_pairs={{0,4},{4,0},{8,12},{12,8},{1,5},{5,1},{9,13},{13,9},{2,6},{6,2},{1... | collective-permute-start | bytes 147464 | tf_op jit(solution)/shard_map/ppermute | solution.py:565
  29.2 5.8 %collective-permute-start.11 = (bf16[96,128]{1,0:T(8,128)(2,1)S(1)}, bf16[96,128]{1,0:T(8,128)(2,1)S(1)}, u32[]{:S(2)}, u32[]{:S(2)}) collective-permute-start(bf16[96,128]{1,0:T(8,128)(2,1)S(1)} %get-tuple-element.71), channel_id=1, source_target_pairs={{0,8},{4,12},{8,0},{12,4},{1,9},{5,13},{9,1},{13,5},{2,10},{6,14},... | collective-permute-start | bytes 73736 | tf_op jit(solution)/shard_map/ppermute | solution.py:561
  29.8 5.2 %collective-permute-start.9 = (bf16[192,128]{1,0:T(8,128)(2,1)S(1)}, bf16[192,128]{1,0:T(8,128)(2,1)S(1)}, u32[]{:S(2)}, u32[]{:S(2)}) collective-permute-start(bf16[192,128]{1,0:T(8,128)(2,1)S(1)} %get-tuple-element.67), channel_id=1, source_target_pairs={{0,1},{1,0},{2,3},{3,2},{4,5},{5,4},{6,7},{7,6},{8,9},{9,8},{10,11... | collective-permute-start | bytes 147464 | tf_op jit(solution)/shard_map/ppermute | solution.py:565
  31.3 5.8 %collective-permute-start.10 = (bf16[272,128]{1,0:T(8,128)(2,1)S(1)}, bf16[272,128]{1,0:T(8,128)(2,1)S(1)}, u32[]{:S(2)}, u32[]{:S(2)}) collective-permute-start(bf16[272,128]{1,0:T(8,128)(2,1)S(1)} %get-tuple-element.65._.refs_0_), channel_id=1, source_target_pairs={{0,2},{1,3},{2,0},{3,1},{4,6},{5,7},{6,4},{7,5},{8,10},{9,11},{10,... | collective-permute-start | bytes 208904 | tf_op jit(solution)/shard_map/ppermute | solution.py:561
  37.2 6.5 %collective-permute-start.14 = (bf16[256,128]{1,0:T(8,128)(2,1)S(1)}, bf16[256,128]{1,0:T(8,128)(2,1)S(1)}, u32[]{:S(2)}, u32[]{:S(2)}) collective-permute-start(bf16[256,128]{1,0:T(8,128)(2,1)S(1)} %get-tuple-element.72.refs_0_), channel_id=1, source_target_pairs={{0,12},{4,0},{8,4},{12,8},{1,13},{5,1},{9,5},{13,9},{2,14},{6,2},{... | collective-permute-start | bytes 196616 | tf_op jit(solution)/shard_map/ppermute | solution.py:561
  37.3 6.5 %collective-permute-start.13 = (bf16[256,128]{1,0:T(8,128)(2,1)S(1)}, bf16[256,128]{1,0:T(8,128)(2,1)S(1)}, u32[]{:S(2)}, u32[]{:S(2)}) collective-permute-start(bf16[256,128]{1,0:T(8,128)(2,1)S(1)} %get-tuple-element.72.refs_0_), channel_id=1, source_target_pairs={{0,8},{4,12},{8,0},{12,4},{1,9},{5,13},{9,1},{13,5},{2,10},{6,14},... | collective-permute-start | bytes 196616 | tf_op jit(solution)/shard_map/ppermute | solution.py:561
  38.8 4.9 %collective-permute-start.12 = (bf16[256,128]{1,0:T(8,128)(2,1)S(1)}, bf16[256,128]{1,0:T(8,128)(2,1)S(1)}, u32[]{:S(2)}, u32[]{:S(2)}) collective-permute-start(bf16[256,128]{1,0:T(8,128)(2,1)S(1)} %get-tuple-element.72.refs_0_), channel_id=1, source_target_pairs={{0,4},{4,8},{8,12},{12,0},{1,5},{5,9},{9,13},{13,1},{2,6},{6,10},{... | collective-permute-start | bytes 196616 | tf_op jit(solution)/shard_map/ppermute | solution.py:561
  39.0 4.7 %collective-permute-start.15 = (bf16[96,128]{1,0:T(8,128)(2,1)S(1)}, bf16[96,128]{1,0:T(8,128)(2,1)S(1)}, u32[]{:S(2)}, u32[]{:S(2)}) collective-permute-start(bf16[96,128]{1,0:T(8,128)(2,1)S(1)} %get-tuple-element.74), channel_id=1, source_target_pairs={{0,2},{1,3},{2,0},{3,1},{4,6},{5,7},{6,4},{7,5},{8,10},{9,11},{10,... | collective-permute-start | bytes 73736 | tf_op jit(solution)/shard_map/ppermute | solution.py:561

commit v11 on v10

--- a/solution.py
+++ b/solution.py
@@ -193,6 +193,23 @@
 
 def near_of(me):
     return me + 1 - 2 * lax.rem(me, 2)
+
+
+def near_of(me):
+    return me + 1 - 2 * lax.rem(me, 2)
+
+
+def in_order(count):
+    return lambda me: ([me], [[lax.rem(me + d, count)] for d in range(1, count)])
+
+
+def in_pairs(count):
+    def plan(me):
+        steps = range(0, count, 2)
+        near = near_of(me)
+        return [lax.rem(me + d, count) for d in steps], [[lax.rem(near + d, count) for d in steps]]
+
+    return plan
 
 
 def outer_kernel(i_n, j_n, *refs):
@@ -283,7 +300,7 @@
     return *results[:3], results[3:]
 
 
-def gradient_kernel(axis, positions, others, sequences, *refs):
+def gradient_kernel(axis, plan, kept, positions, others, sequences, *refs):
     depth = PROJECTED_DEPTH
     wide, source = refs[:2]
     outs, (result, grown, grad, own_wide) = refs[3:-4], refs[-4:]
@@ -338,24 +355,25 @@
             [mine[:, l * LANES : (l + 1) * LANES] for l in range(mine.shape[1] // LANES)], axis=0
         )
 
-    me = lax.axis_index(axis)
-    near = me + 1 - 2 * lax.rem(me, 2)
-    *kept, message = outs
-    size = kept[0].shape[0]
-    for p, out in enumerate(kept):
-        out[...] = rows_of(lax.rem(me + 2 * p, parts))
-        message[p * size : (p + 1) * size, :] = rows_of(lax.rem(near + 2 * p, parts)).astype(BF16)
-
-
-def gradient(wide, source, after, axis, positions, others, sequences):
+    stay, go = plan(lax.axis_index(axis))
+    for p, out in zip(stay, outs[:kept], strict=True):
+        out[...] = rows_of(p)
+    for group, out in zip(go, outs[kept:], strict=True):
+        size = out.shape[0] // len(group)
+        for n, p in enumerate(group):
+            out[n * size : (n + 1) * size, :] = rows_of(p).astype(BF16)
+
+
+def gradient(wide, source, after, axis, plan, kept, groups, positions, others, sequences):
     depth = PROJECTED_DEPTH
     parts = lax.axis_size(axis)
     rows = sequences // parts * positions * depth // LANES
-    shapes = [jax.ShapeDtypeStruct((rows, LANES), F32)] * (parts // 2)
-    shapes += [jax.ShapeDtypeStruct((parts // 2 * rows, LANES), BF16)]
+    shapes = [jax.ShapeDtypeStruct((rows, LANES), F32)] * kept
+    group = (parts - kept) // groups
+    shapes += [jax.ShapeDtypeStruct((group * rows, LANES), BF16)] * groups
     tiles = GROUP * sequences // LANES if wide.ndim == 2 else 1
-    *kept, message = pl.pallas_call(
-        functools.partial(gradient_kernel, axis, positions, others, sequences),
+    results = pl.pallas_call(
+        functools.partial(gradient_kernel, axis, plan, kept, positions, others, sequences),
         in_specs=[in_vmem(), in_vmem(), pl.BlockSpec(memory_space=pl.ANY)],
         out_specs=[in_vmem()] * len(shapes),
         out_shape=shapes,
@@ -372,7 +390,7 @@
             transcendentals=0,
         ),
     )(wide, source, after)
-    return kept, message
+    return results[:kept], results[kept:]
 
 
 def product_kernel(left_ref, right_ref, _, out_ref):
@@ -395,8 +413,7 @@
     )(left, right, after)
 
 
-def pair_kernel(sequences, x_ref, wt_ref, bias_ref, _, out_ref, done_ref):
-    done_ref[...] = jnp.zeros(done_ref.shape, F32)
+def pair_kernel(sequences, x_ref, wt_ref, bias_ref, _, out_ref):
     product = dot(wt_ref[...], x_ref[...])
     out_ref[...] = (product.T * (1.0 / sequences) + bias_ref[...]).astype(BF16)
 
@@ -414,11 +431,8 @@
             whole((1, PAIR_FEATURES)),
             pl.BlockSpec(memory_space=pl.ANY),
         ],
-        out_specs=[pl.BlockSpec((size, PAIR_FEATURES), lambda t: (t, 0)), whole((8, LANES))],
-        out_shape=[
-            jax.ShapeDtypeStruct((pairs, PAIR_FEATURES), BF16),
-            jax.ShapeDtypeStruct((8, LANES), F32),
-        ],
+        out_specs=pl.BlockSpec((size, PAIR_FEATURES), lambda t: (t, 0)),
+        out_shape=jax.ShapeDtypeStruct((pairs, PAIR_FEATURES), BF16),
         compiler_params=params(),
         cost_estimate=pl.CostEstimate(
             flops=4 * pairs * channels * PAIR_FEATURES,
@@ -467,48 +481,40 @@
     return message
 
 
-def add_near(kept, near, own, messages):
-    size = own.shape[0]
-    for p, part in enumerate(kept):
-        both = part[...] + near[p * size : (p + 1) * size, :].astype(F32)
-        if p == 0:
-            own[...] = both
-        else:
-            messages[p - 1][...] = both.astype(BF16)
-
-
-def column_pair_sum(own, near, kept, grad_near, passed, share):
+def pair_sum(kept, near, after):
+    def kernel(*refs):
+        kept, near, (own, *messages) = refs[:count], refs[count], refs[count + 2 :]
+        size = own.shape[0]
+        for p, part in enumerate(kept):
+            both = part[...] + near[p * size : (p + 1) * size, :].astype(F32)
+            if p == 0:
+                own[...] = both
+            else:
+                messages[p - 1][...] = both.astype(BF16)
+
     count = len(kept)
-
-    def kernel(own, near, grad_near, passed, *refs):
-        kept, (message, passed_on, grad_own), messages = (
-            refs[:count],
-            refs[count : count + 3],
-            refs[count + 3 :],
-        )
-        passed_on[...] = passed[...]
+    shapes = [(kept[0].shape, F32)] + [(kept[0].shape, BF16)] * (count - 1)
+    own, *messages = call(kernel, [*kept, near], shapes, [after])
+    return own, messages
+
+
+def column_pair_sum(own, near, after, share):
+    def kernel(own, near, _, message):
         total = own[0:share, :].astype(F32) + near[0:share, :].astype(F32)
         message[0:share, :] = total.astype(BF16)
         message[share:, :] = split(joined(own[share:, :]) + joined(near[share:, :]))
-        add_near(kept, grad_near, grad_own, messages)
-
-    size = kept[0].shape
-    shapes = [(own.shape, BF16), (passed.shape, BF16), (size, F32)] + [(size, BF16)] * (count - 1)
-    message, passed, grad_own, *messages = call(
-        kernel, [own, near, grad_near, passed, *kept], shapes
-    )
-    return message, passed, grad_own, messages
-
-
-def column_sum(parts, kept, grad_near, after, share):
+
+    (message,) = call(kernel, [own, near], [(own.shape, BF16)], [after])
+    return message
+
+
+def column_sum(parts, grads, share):
     rows = share + BIAS_ROWS
-    count = len(parts)
-    kept_n = len(kept)
-
-    def kernel(grad_near, *refs):
-        parts, kept = refs[:count], refs[count : count + kept_n]
-        refs = refs[count + kept_n + len(after) :]
-        piece_out, bias_out, grad_own, *messages, held = refs
+    count, sent = len(parts), len(grads)
+
+    def kernel(*refs):
+        parts, grads, refs = refs[:count], refs[count : count + sent], refs[count + sent :]
+        messages, (piece_out, bias_out, held) = refs[:sent], refs[sent:]
         home = lax.div(lax.axis_index("col"), 2)
         for p, part in enumerate(parts):
             held[lax.rem(home - p + count, count)] = part[...]
@@ -516,35 +522,39 @@
         for n in range(1, count):
             total += held[n, 0:share, :].astype(F32)
             bias += joined(held[n, share:, :])
-        piece_out[...] = total.astype(BF16)
+        piece = total.astype(BF16)
+        piece_out[...] = piece
+        for message, grad in zip(messages, grads, strict=True):
+            message[0:share, :] = piece
+            message[share:, :] = grad[...]
         bias_out[...] = jnp.broadcast_to(bias, bias_out.shape)
-        add_near(kept, grad_near, grad_own, messages)
-
-    size = kept[0].shape
-    shapes = [((share, LANES), BF16), ((8, LANES), F32), (size, F32)] + [(size, BF16)] * (kept_n - 1)
+
+    shapes = [((share + grad.shape[0], LANES), BF16) for grad in grads]
+    shapes += [((share, LANES), BF16), ((8, LANES), F32)]
     scratch = [pltpu.VMEM((count, rows, LANES), BF16)]
-    piece, bias, grad_own, *messages = call(
-        kernel, [grad_near, *parts, *kept], shapes, after, scratch
-    )
-    return piece, bias, grad_own, messages
-
-
-def finish(pieces, left, right, bias, left_shape, right_shape, scale, bias_scale):
+    *messages, piece, bias = call(kernel, [*parts, *grads], shapes, scratch=scratch)
+    return messages, piece, bias
+
+
+def finish(pieces, left, right_own, bias, left_shape, right_shape, scale, bias_scale):
     count, left_n = len(pieces), len(left)
     share = pieces[0].shape[0]
 
     def kernel(*refs):
-        pieces, left, right = refs[:count], refs[count : count + left_n], refs[count + left_n : -5]
-        bias, projection, left_out, right_out, bias_out = refs[-5:]
+        pieces, left, refs = refs[:count], refs[count : count + left_n], refs[count + left_n :]
+        right_own, bias, projection, left_out, right_out, bias_out = refs
         me = lax.axis_index("row")
+        right_total = right_own[...]
         for p, piece in enumerate(pieces):
             rows = pl.ds(pl.multiple_of(lax.rem(me - p + count, count) * share, share), share)
-            projection[rows, :] = piece[...].astype(F32) * scale
-        for terms, out in ((left, left_out), (right, right_out)):
-            total = terms[0][...]
-            for term in terms[1:]:
-                total += term[...].astype(F32)
-            unfold(total, out.shape[0], out)
+            projection[rows, :] = piece[0:share, :].astype(F32) * scale
+            if p > 0:
+                right_total += piece[share:, :].astype(F32)
+        left_total = left[0][...]
+        for term in left[1:]:
+            left_total += term[...].astype(F32)
+        unfold(left_total, left_out.shape[0], left_out)
+        unfold(right_total, right_out.shape[0], right_out)
         bias_out[...] = bias[0:1, :] * bias_scale
 
     shapes = [
@@ -553,7 +563,7 @@
         (right_shape, F32),
         ((1, PAIR_FEATURES), F32),
     ]
-    return call(kernel, [*pieces, *left, *right, bias], shapes)
+    return call(kernel, [*pieces, *left, right_own, bias], shapes)
 
 
 def shift(x, axis, distance):
@@ -581,7 +591,7 @@
     first_homolog_features, second_homolog_features, final_projection_matrix, output_bias, cotangent
 ):
     i_n, j_n, _ = cotangent.shape
-    row_n = lax.axis_size("row")
+    row_n, col_n = lax.axis_size("row"), lax.axis_size("col")
     sequences = second_homolog_features.shape[0] * row_n
     channels = final_projection_matrix.shape[0]
     res_total = i_n * row_n
@@ -604,31 +614,30 @@
     share = channels // row_n
 
     parts = [own] + send(messages, "row")
-    y2 = product(w, gt, own)
-    right_kept, message = gradient(a_held, y2, own, "row", j_n, i_n, sequences)
-    right_near = neighbour(message, "row")
+    left_kept, (message,) = gradient(
+        b_wide, y, own, "col", in_pairs(col_n), col_n // 2, 1, i_n, j_n, sequences
+    )
+    left_near = neighbour(message, "col")
 
     message = row_sum(parts, message, share)
     near = neighbour(message, "col")
-    left_kept, left_message = gradient(b_wide, y, message, "col", i_n, j_n, sequences)
-    message, left_message, right_own, right_messages = column_pair_sum(
-        message, near, right_kept, right_near, left_message, share
+    left_own, left_messages = pair_sum(left_kept, left_near, message)
+    left = [left_own] + send_pairs(left_messages, "col")
+    y2 = product(w, gt, left_own)
+
+    message = column_pair_sum(message, near, y2, share)
+    parts = [message] + spread_pairs(message, "col")
+    (right_own,), right_sent = gradient(
+        a_held, y2, message, "row", in_order(row_n), 1, row_n - 1, j_n, i_n, sequences
     )
 
-    parts = [message] + spread_pairs(message, "col")
-    left_near = neighbour(left_message, "col")
-    right = [right_own] + send_pairs(right_messages, "row")
-    pair_map, pair_done = pair(x, wt, output_bias, message, sequences)
-    piece, bias, left_own, left_messages = column_sum(
-        parts, left_kept, left_near, [pair_done, *right[1:]], share
-    )
-
-    pieces = [piece] + send([piece] * (row_n - 1), "row")
-    left = [left_own] + send_pairs(left_messages, "col")
+    messages, piece, bias = column_sum(parts, right_sent, share)
+    pieces = [piece] + send(messages, "row")
+    pair_map = pair(x, wt, output_bias, piece, sequences)
     projection, left_grad, right_grad, bias_grad = finish(
         pieces,
         left,
-        right,
+        right_own,
         bias,
         first_homolog_features.shape,
         second_homolog_features.shape,

time: 44.8 us -> 42 us (0.938)
  waiting for transfers between devices: 8.99 us -> 4.69 us
  starting transfers between devices: 17.3 us -> 18.8 us
    ppermute x11 -> x10, waiting for transfers between devices: 7.67 us -> 1.5 us  [shift(): lax.ppermute(x, axis, [(n, (n + distance) % count) for n in range(count)])]
    ppermute x11 -> x10, starting transfers between devices: 12.5 us -> 15 us  [shift(): lax.ppermute(x, axis, [(n, (n + distance) % count) for n in range(count)])]
    ppermute x5 -> x4, waiting for transfers between devices: 1.32 us -> 3.2 us  [neighbour(): lax.ppermute(x, axis, [(n, n ^ 1) for n in range(lax.axis_size(axis))])]
    ppermute x5 -> x4, starting transfers between devices: 4.87 us -> 3.8 us  [neighbour(): lax.ppermute(x, axis, [(n, n ^ 1) for n in range(lax.axis_size(axis))])]
    pallas_call x5 -> x6, Pallas kernels: 1 us -> 1.02 us  [call(): pl.pallas_call(kernel, in_specs=specs, out_specs=[in_vmem()] * len(shapes...]
  transfers between devices with their start and end apart: 16 -> 14, of which waited for: 5 -> 4; matrix products, arithmetic and copies ran while one was open for 0% -> 0% of each run, Pallas kernels for 26% -> 28%
where the time goes in v11:
time: 42 us; the launch traced here: 41.8 us
  starting transfers between devices  18.8 us (45%)
  Pallas kernels  17.5 us (42%)
  waiting for transfers between devices  4.69 us (11%)
  between operations  0.76 us (2%)
    ppermute x10, starting transfers between devices, shift(): lax.ppermute(x, axis, [(n, (n + distance) % count) for n in range(count)])  15 us
    pallas_call x1, Pallas kernels, outer(): pl.pallas_call(functools.partial(outer_kernel, i_n, j_n), in_specs=[in_vm...  4.8 us
    pallas_call x2, Pallas kernels, gradient(): pl.pallas_call(functools.partial(gradient_kernel, axis, plan, kept, posit...  4.65 us
    ppermute x4, starting transfers between devices, neighbour(): lax.ppermute(x, axis, [(n, n ^ 1) for n in range(lax.axis_size(axis))])  3.8 us
    ppermute x4, waiting for transfers between devices, neighbour(): lax.ppermute(x, axis, [(n, n ^ 1) for n in range(lax.axis_size(axis))])  3.2 us
    pallas_call x1, Pallas kernels, pair(): pl.pallas_call(functools.partial(pair_kernel, sequences), grid=(count,),...  2.55 us
    pallas_call x1, Pallas kernels, prepare(): pl.pallas_call(functools.partial(prepare_kernel, i_n, j_n), in_specs=[in_...  1.75 us
    ppermute x10, waiting for transfers between devices, shift(): lax.ppermute(x, axis, [(n, (n + distance) % count) for n in range(count)])  1.5 us
  transfers between devices with their start and end apart: 14, of which 4 were waited for; matrix products, arithmetic and copies ran while one was open for 0% of the time, Pallas kernels for 28%

profile of v11, /device:TPU:0, one launch (start us, length us, event | category | flops | bytes accessed | tf_op | source)
XLA Modules:
  0.0 41.8 jit_solution(14633690644859850770)
XLA Ops:
  0.6 4.1 %collective-permute-start = (bf16[8,1536]{1,0:T(8,128)(2,1)}, bf16[8,1536]{1,0:T(8,128)(2,1)S(1)}, u32[]{:S(2)}, u32[]{:S(2)}) collective-permute-start(bf16[8,1536]{1,0:T(8,128)(2,1)} %a_hbm.1), channel_id=1, source_target_pairs={{0,2},{1,3},{2,0},{3,1},{4,6},{5,7},{6,4},{7,5},{8,10},{9,11},{10,... | collective-permute-start | bytes 73736 | tf_op jit(solution)/shard_map/ppermute | solution.py:571
  4.7 1.5 %collective-permute-start.1 = (bf16[8,1536]{1,0:T(8,128)(2,1)}, bf16[8,1536]{1,0:T(8,128)(2,1)S(1)}, u32[]{:S(2)}, u32[]{:S(2)}) collective-permute-start(bf16[8,1536]{1,0:T(8,128)(2,1)} %b_hbm.1), channel_id=1, source_target_pairs={{0,8},{4,12},{8,0},{12,4},{1,9},{5,13},{9,1},{13,5},{2,10},{6,14},... | collective-permute-start | bytes 73736 | tf_op jit(solution)/shard_map/ppermute | solution.py:571
  6.2 1.4 %shard_map.92 = (bf16[1024,128]{1,0:T(8,128)(2,1)S(1)}, bf16[128,1024]{1,0:T(8,128)(2,1)S(1)}, bf16[8,1536]{1,0:T(8,128)(2,1)S(1)}, bf16[8,1536]{1,0:T(8,128)(2,...) custom-call(bf16[8,1536]{1,0:T(8,128)(2,1)} %a_hbm.1, bf16[8,1536]{1,0:T(8,128)(2,1)} %b_hbm.1, ...), custom_call_target="tpu_custom_call" | custom-call | flops 131072000 | bytes 2097152 | tf_op jit(solution)/shard_map/pallas_call | solution.py:67
  7.6 0.0 collective-permute-done.refs_1_
  7.6 1.1 %collective-permute-done.1.refs_3_ = bf16[8,1536]{1,0:T(8,128)(2,1)S(1)} collective-permute-done((bf16[8,1536]{1,0:T(8,128)(2,1)}, bf16[8,1536]{1,0:T(8,128)(2,1)S(1)}, u32[]{:S(2)}, u32[]{:S(2)}) %collective-permute-start.1) | collective-permute-done | bytes 24608 | tf_op jit(solution)/shard_map/ppermute | solution.py:571
  8.8 1.6 %collective-permute-start.2 = (bf16[16,1536]{1,0:T(8,128)(2,1)S(1)}, bf16[16,1536]{1,0:T(8,128)(2,1)S(1)}, u32[]{:S(2)}, u32[]{:S(2)}) collective-permute-start(bf16[16,1536]{1,0:T(8,128)(2,1)S(1)} %get-tuple-element.43.refs_0_), channel_id=1, source_target_pairs={{0,1},{1,0},{2,3},{3,2},{4,5},{5,4},{6,7},{7,6},{8,9},{9,8},{10,11... | collective-permute-start | bytes 147464 | tf_op jit(solution)/shard_map/ppermute | solution.py:575
  10.4 0.0 collective-permute-start.3
  10.4 1.7 %shard_map.94 = (bf16[1024,2304]{1,0:T(8,128)(2,1)S(1)}, bf16[2304,128]{1,0:T(8,128)(2,1)S(1)}, bf16[16,128]{1,0:T(8,128)(2,1)S(1)}) custom-call(bf16[1024,128]{1,0:T(8,128)(2,1)S(1)} %get-tuple-element.46.we_ref, bf16[2304,128]{1,0:T(8,128)(2,1)S(1)} %get-tuple-element.45.g_ref.refs_4_), custom_call_target="tpu_custom_call" | custom-call | flops 603979776 | bytes 9437184 | tf_op jit(solution)/shard_map/pallas_call | solution.py:126
  12.2 0.8 %collective-permute-done.2.refs_1_ = bf16[16,1536]{1,0:T(8,128)(2,1)S(1)} collective-permute-done((bf16[16,1536]{1,0:T(8,128)(2,1)S(1)}, bf16[16,1536]{1,0:T(8,128)(2,1)S(1)}, u32[]{:S(2)}, u32[]{:S(2)}) %collective-permute-start.2) | collective-permute-done | bytes 49184 | tf_op jit(solution)/shard_map/ppermute | solution.py:575
  12.9 4.8 %shard_map.95 = (bf16[1024,2304]{1,0:T(8,128)(2,1)S(1)}, f32[32,1536]{1,0:T(8,128)S(1)}, f32[2,1536,128]{2,1,0:T(8,128)S(1)}, f32[272,128]{1,0:T(8,128)S(1)}, bf...) custom-call(bf16[16,1536]{1,0:T(8,128)(2,1)S(1)} %get-tuple-element.43.refs_0_, ...), custom_call_target="tpu_custom_call" | custom-call | flops 1207959552 | bytes 4718592 | tf_op jit(solution)/shard_map/pallas_call | solution.py:283
  17.7 0.1 collective-permute-start.4
  17.8 1.6 %collective-permute-start.5 = (bf16[272,128]{1,0:T(8,128)(2,1)S(1)}, bf16[272,128]{1,0:T(8,128)(2,1)S(1)}, u32[]{:S(2)}, u32[]{:S(2)}) collective-permute-start(bf16[272,128]{1,0:T(8,128)(2,1)S(1)} %get-tuple-element.52), channel_id=1, source_target_pairs={{0,8},{4,12},{8,0},{12,4},{1,9},{5,13},{9,1},{13,5},{2,10},{6,14},... | collective-permute-start | bytes 208904 | tf_op jit(solution)/shard_map/ppermute | solution.py:571
  19.4 1.4 %collective-permute-start.6 = (bf16[272,128]{1,0:T(8,128)(2,1)S(1)}, bf16[272,128]{1,0:T(8,128)(2,1)S(1)}, u32[]{:S(2)}, u32[]{:S(2)}) collective-permute-start(bf16[272,128]{1,0:T(8,128)(2,1)S(1)} %get-tuple-element.53), channel_id=1, source_target_pairs={{0,12},{4,0},{8,4},{12,8},{1,13},{5,1},{9,5},{13,9},{2,14},{6,2},{... | collective-permute-start | bytes 208904 | tf_op jit(solution)/shard_map/ppermute | solution.py:571
  20.8 2.1 %shard_map.96 = (f32[96,128]{1,0:T(8,128)S(1)}, f32[96,128]{1,0:T(8,128)S(1)}, bf16[192,128]{1,0:T(8,128)(2,1)S(1)}) custom-call(f32[2,1536,128]{2,1,0:T(8,128)S(1)} %get-tuple-element.54.refs_0_, bf16[1024,2304]{1,0:T(8,128)(2,1)S(1)} %get-tuple-element.55.refs_1_, f32[272,128]{1,0:T(8,128)S(1)} %get-tuple-element.50.refs_2_.refs_0_), custom_call_target="tpu_custom_call" | custom-call | flops 603979776 | bytes 4718592 | tf_op jit(solution)/shard_map/pallas_call | solution.py:375
  22.9 1.6 %collective-permute-start.8 = (bf16[192,128]{1,0:T(8,128)(2,1)S(1)}, bf16[192,128]{1,0:T(8,128)(2,1)S(1)}, u32[]{:S(2)}, u32[]{:S(2)}) collective-permute-start(bf16[192,128]{1,0:T(8,128)(2,1)S(1)} %get-tuple-element.56.refs_4_), channel_id=1, source_target_pairs={{0,1},{1,0},{2,3},{3,2},{4,5},{5,4},{6,7},{7,6},{8,9},{9,8},{10,11... | collective-permute-start | bytes 147464 | tf_op jit(solution)/shard_map/ppermute | solution.py:575
  24.6 0.5 %collective-permute-start.7 = (bf16[272,128]{1,0:T(8,128)(2,1)S(1)}, bf16[272,128]{1,0:T(8,128)(2,1)S(1)}, u32[]{:S(2)}, u32[]{:S(2)}) collective-permute-start(bf16[272,128]{1,0:T(8,128)(2,1)S(1)} %shard_map.97.refs_3_.own), channel_id=1, source_target_pairs={{0,1},{1,0},{2,3},{3,2},{4,5},{5,4},{6,7},{7,6},{8,9},{9,8},{10,11... | collective-permute-start | bytes 208904 | tf_op jit(solution)/shard_map/ppermute | solution.py:575
  25.1 2.4 %collective-permute-done.8.refs_2_ = bf16[192,128]{1,0:T(8,128)(2,1)S(1)} collective-permute-done((bf16[192,128]{1,0:T(8,128)(2,1)S(1)}, bf16[192,128]{1,0:T(8,128)(2,1)S(1)}, u32[]{:S(2)}, u32[]{:S(2)}) %collective-permute-start.8) | collective-permute-done | bytes 49184 | tf_op jit(solution)/shard_map/ppermute | solution.py:575
  27.6 1.4 %shard_map.99._.refs_1_ = bf16[1024,2304]{1,0:T(8,128)(2,1)S(1)} custom-call(bf16[1024,128]{1,0:T(8,128)(2,1)S(1)} %get-tuple-element.57.left_ref, bf16[2304,128]{1,0:T(8,128)(2,1)S(1)} %get-tuple-element.58.right_ref, f32[96,128]{1,0:T(8,128)S(1)} %get-tuple-element.61._.refs_4_), custom_call_target="tpu_custom_call" | custom-call | flops 603979776 | bytes 9437184 | tf_op jit(solution)/shard_map/pallas_call | solution.py:402
  29.0 0.0 copy-start
  29.0 0.0 collective-permute-done.7.near
  29.0 1.1 %collective-permute-start.9 = (bf16[272,128]{1,0:T(8,128)(2,1)S(1)}, bf16[272,128]{1,0:T(8,128)(2,1)S(1)}, u32[]{:S(2)}, u32[]{:S(2)}) collective-permute-start(bf16[272,128]{1,0:T(8,128)(2,1)S(1)} %shard_map.100.refs_2_.refs_0_), channel_id=1, source_target_pairs={{0,2},{1,3},{2,0},{3,1},{4,6},{5,7},{6,4},{7,5},{8,10},{9,11},{10,... | collective-permute-start | bytes 208904 | tf_op jit(solution)/shard_map/ppermute | solution.py:571
  30.1 1.9 %collective-permute-start.13 = (bf16[96,128]{1,0:T(8,128)(2,1)S(1)}, bf16[96,128]{1,0:T(8,128)(2,1)S(1)}, u32[]{:S(2)}, u32[]{:S(2)}) collective-permute-start(bf16[96,128]{1,0:T(8,128)(2,1)S(1)} %get-tuple-element.70), channel_id=1, source_target_pairs={{0,2},{1,3},{2,0},{3,1},{4,6},{5,7},{6,4},{7,5},{8,10},{9,11},{10,... | collective-permute-start | bytes 73736 | tf_op jit(solution)/shard_map/ppermute | solution.py:571
  32.0 2.5 %shard_map.101 = (f32[96,128]{1,0:T(8,128)S(1)}, bf16[96,128]{1,0:T(8,128)(2,1)S(1)}, bf16[96,128]{1,0:T(8,128)(2,1)S(1)}, bf16[96,128]{1,0:T(8,128)(2,1)S(1)}) custom-call(f32[32,1536]{1,0:T(8,128)S(1)} %get-tuple-element.62.refs_0_, bf16[1024,2304]{1,0:T(8,128)(2,1)S(1)} %shard_map.99._.refs_1_, bf16[272,128]{1,0:T(8,128)(2,1)S(1)} %shard_map.100.refs_2_.refs_0_), custom_call_target="tpu_custom_call" | custom-call | flops 603979776 | bytes 4718592 | tf_op jit(solution)/shard_map/pallas_call | solution.py:375
  34.5 0.0 collective-permute-done.9.refs_1_
  34.6 0.1 shard_map.102
  34.6 0.1 collective-permute-start.10
  34.7 2.0 %collective-permute-start.11 = (bf16[352,128]{1,0:T(8,128)(2,1)S(1)}, bf16[352,128]{1,0:T(8,128)(2,1)S(1)}, u32[]{:S(2)}, u32[]{:S(2)}) collective-permute-start(bf16[352,128]{1,0:T(8,128)(2,1)S(1)} %get-tuple-element.68), channel_id=1, source_target_pairs={{0,8},{4,12},{8,0},{12,4},{1,9},{5,13},{9,1},{13,5},{2,10},{6,14},... | collective-permute-start | bytes 270344 | tf_op jit(solution)/shard_map/ppermute | solution.py:571
  36.7 1.4 %collective-permute-start.12 = (bf16[352,128]{1,0:T(8,128)(2,1)S(1)}, bf16[352,128]{1,0:T(8,128)(2,1)S(1)}, u32[]{:S(2)}, u32[]{:S(2)}) collective-permute-start(bf16[352,128]{1,0:T(8,128)(2,1)S(1)} %get-tuple-element.69), channel_id=1, source_target_pairs={{0,12},{4,0},{8,4},{12,8},{1,13},{5,1},{9,5},{13,9},{2,14},{6,2},{... | collective-permute-start | bytes 270344 | tf_op jit(solution)/shard_map/ppermute | solution.py:571
  38.1 2.5 %shard_map.103 = bf16[2304,128]{1,0:T(8,128)(2,1)} custom-call(bf16[1024,2304]{1,0:T(8,128)(2,1)S(1)} %get-tuple-element.48.x_ref, bf16[128,1024]{1,0:T(8,128)(2,1)S(1)} %get-tuple-element.49.wt_ref, f32[1,128]{1,0:T(1,128)S(1)} %bitcast.4, bf16[256,128]{1,0:T(8,128)(2,1)S(1)} %get-tuple-element.66._.refs_0_), custom_call_target="tpu_custom_call" | custom-call | flops 1207959552 | bytes 4718592 | tf_op jit(solution)/shard_map/pallas_call | solution.py:425
  40.6 0.0 collective-permute-done.11.refs_2_
  40.6 0.3 collective-permute-done.12.refs_3_
  41.0 0.9 %shard_map.104 = (f32[1024,128]{1,0:T(8,128)}, f32[8,1536]{1,0:T(8,128)}, f32[8,1536]{1,0:T(8,128)}, f32[1,128]{1,0:T(1,128)}) custom-call(bf16[256,128]{1,0:T(8,128)(2,1)S(1)} %get-tuple-element.66._.refs_0_, bf16[352,128]{1,0:T(8,128)(2,1)S(1)} %collective-permute-done.10.refs_1_, bf16[352,128]{1,0:T(8,128)(2,1)S(1)} %collective-permute-done.11.refs_2_, ...), custom_call_target="tpu_custom_call" | custom-call | tf_op jit(solution)/shard_map/pallas_call | solution.py:452
  (11 shorter events, 0.1 us)
Async XLA Ops:
  0.6 7.0 %collective-permute-start = (bf16[8,1536]{1,0:T(8,128)(2,1)}, bf16[8,1536]{1,0:T(8,128)(2,1)S(1)}, u32[]{:S(2)}, u32[]{:S(2)}) collective-permute-start(bf16[8,1536]{1,0:T(8,128)(2,1)} %a_hbm.1), channel_id=1, source_target_pairs={{0,2},{1,3},{2,0},{3,1},{4,6},{5,7},{6,4},{7,5},{8,10},{9,11},{10,... | collective-permute-start | bytes 73736 | tf_op jit(solution)/shard_map/ppermute | solution.py:571
  4.7 4.0 %collective-permute-start.1 = (bf16[8,1536]{1,0:T(8,128)(2,1)}, bf16[8,1536]{1,0:T(8,128)(2,1)S(1)}, u32[]{:S(2)}, u32[]{:S(2)}) collective-permute-start(bf16[8,1536]{1,0:T(8,128)(2,1)} %b_hbm.1), channel_id=1, source_target_pairs={{0,8},{4,12},{8,0},{12,4},{1,9},{5,13},{9,1},{13,5},{2,10},{6,14},... | collective-permute-start | bytes 73736 | tf_op jit(solution)/shard_map/ppermute | solution.py:571
  8.8 4.2 %collective-permute-start.2 = (bf16[16,1536]{1,0:T(8,128)(2,1)S(1)}, bf16[16,1536]{1,0:T(8,128)(2,1)S(1)}, u32[]{:S(2)}, u32[]{:S(2)}) collective-permute-start(bf16[16,1536]{1,0:T(8,128)(2,1)S(1)} %get-tuple-element.43.refs_0_), channel_id=1, source_target_pairs={{0,1},{1,0},{2,3},{3,2},{4,5},{5,4},{6,7},{7,6},{8,9},{9,8},{10,11... | collective-permute-start | bytes 147464 | tf_op jit(solution)/shard_map/ppermute | solution.py:575
  10.4 2.5 %collective-permute-start.3 = (bf16[16,1536]{1,0:T(8,128)(2,1)S(1)}, bf16[16,1536]{1,0:T(8,128)(2,1)S(1)}, u32[]{:S(2)}, u32[]{:S(2)}) collective-permute-start(bf16[16,1536]{1,0:T(8,128)(2,1)S(1)} %get-tuple-element.44.refs_2_), channel_id=1, source_target_pairs={{0,4},{4,0},{8,12},{12,8},{1,5},{5,1},{9,13},{13,9},{2,6},{6,2},{1... | collective-permute-start | bytes 147464 | tf_op jit(solution)/shard_map/ppermute | solution.py:575
  17.7 6.8 %collective-permute-start.4 = (bf16[272,128]{1,0:T(8,128)(2,1)S(1)}, bf16[272,128]{1,0:T(8,128)(2,1)S(1)}, u32[]{:S(2)}, u32[]{:S(2)}) collective-permute-start(bf16[272,128]{1,0:T(8,128)(2,1)S(1)} %get-tuple-element.51), channel_id=1, source_target_pairs={{0,4},{4,8},{8,12},{12,0},{1,5},{5,9},{9,13},{13,1},{2,6},{6,10},{... | collective-permute-start | bytes 208904 | tf_op jit(solution)/shard_map/ppermute | solution.py:571
  17.8 6.8 %collective-permute-start.5 = (bf16[272,128]{1,0:T(8,128)(2,1)S(1)}, bf16[272,128]{1,0:T(8,128)(2,1)S(1)}, u32[]{:S(2)}, u32[]{:S(2)}) collective-permute-start(bf16[272,128]{1,0:T(8,128)(2,1)S(1)} %get-tuple-element.52), channel_id=1, source_target_pairs={{0,8},{4,12},{8,0},{12,4},{1,9},{5,13},{9,1},{13,5},{2,10},{6,14},... | collective-permute-start | bytes 208904 | tf_op jit(solution)/shard_map/ppermute | solution.py:571
  19.4 5.2 %collective-permute-start.6 = (bf16[272,128]{1,0:T(8,128)(2,1)S(1)}, bf16[272,128]{1,0:T(8,128)(2,1)S(1)}, u32[]{:S(2)}, u32[]{:S(2)}) collective-permute-start(bf16[272,128]{1,0:T(8,128)(2,1)S(1)} %get-tuple-element.53), channel_id=1, source_target_pairs={{0,12},{4,0},{8,4},{12,8},{1,13},{5,1},{9,5},{13,9},{2,14},{6,2},{... | collective-permute-start | bytes 208904 | tf_op jit(solution)/shard_map/ppermute | solution.py:571
  22.9 4.7 %collective-permute-start.8 = (bf16[192,128]{1,0:T(8,128)(2,1)S(1)}, bf16[192,128]{1,0:T(8,128)(2,1)S(1)}, u32[]{:S(2)}, u32[]{:S(2)}) collective-permute-start(bf16[192,128]{1,0:T(8,128)(2,1)S(1)} %get-tuple-element.56.refs_4_), channel_id=1, source_target_pairs={{0,1},{1,0},{2,3},{3,2},{4,5},{5,4},{6,7},{7,6},{8,9},{9,8},{10,11... | collective-permute-start | bytes 147464 | tf_op jit(solution)/shard_map/ppermute | solution.py:575
  24.6 4.4 %collective-permute-start.7 = (bf16[272,128]{1,0:T(8,128)(2,1)S(1)}, bf16[272,128]{1,0:T(8,128)(2,1)S(1)}, u32[]{:S(2)}, u32[]{:S(2)}) collective-permute-start(bf16[272,128]{1,0:T(8,128)(2,1)S(1)} %shard_map.97.refs_3_.own), channel_id=1, source_target_pairs={{0,1},{1,0},{2,3},{3,2},{4,5},{5,4},{6,7},{7,6},{8,9},{9,8},{10,11... | collective-permute-start | bytes 208904 | tf_op jit(solution)/shard_map/ppermute | solution.py:575
  29.0 9.1 %copy-start = (f32[128]{0:T(128)S(1)}, f32[128]{0:T(128)}, u32[]{:S(2)}) copy-start(f32[128]{0:T(128)} %param.8) | copy-start | bytes 1540
  29.0 5.5 %collective-permute-start.9 = (bf16[272,128]{1,0:T(8,128)(2,1)S(1)}, bf16[272,128]{1,0:T(8,128)(2,1)S(1)}, u32[]{:S(2)}, u32[]{:S(2)}) collective-permute-start(bf16[272,128]{1,0:T(8,128)(2,1)S(1)} %shard_map.100.refs_2_.refs_0_), channel_id=1, source_target_pairs={{0,2},{1,3},{2,0},{3,1},{4,6},{5,7},{6,4},{7,5},{8,10},{9,11},{10,... | collective-permute-start | bytes 208904 | tf_op jit(solution)/shard_map/ppermute | solution.py:571
  30.1 10.5 %collective-permute-start.13 = (bf16[96,128]{1,0:T(8,128)(2,1)S(1)}, bf16[96,128]{1,0:T(8,128)(2,1)S(1)}, u32[]{:S(2)}, u32[]{:S(2)}) collective-permute-start(bf16[96,128]{1,0:T(8,128)(2,1)S(1)} %get-tuple-element.70), channel_id=1, source_target_pairs={{0,2},{1,3},{2,0},{3,1},{4,6},{5,7},{6,4},{7,5},{8,10},{9,11},{10,... | collective-permute-start | bytes 73736 | tf_op jit(solution)/shard_map/ppermute | solution.py:571
  34.6 6.0 %collective-permute-start.10 = (bf16[352,128]{1,0:T(8,128)(2,1)S(1)}, bf16[352,128]{1,0:T(8,128)(2,1)S(1)}, u32[]{:S(2)}, u32[]{:S(2)}) collective-permute-start(bf16[352,128]{1,0:T(8,128)(2,1)S(1)} %get-tuple-element.67), channel_id=1, source_target_pairs={{0,4},{4,8},{8,12},{12,0},{1,5},{5,9},{9,13},{13,1},{2,6},{6,10},{... | collective-permute-start | bytes 270344 | tf_op jit(solution)/shard_map/ppermute | solution.py:571
  34.7 6.0 %collective-permute-start.11 = (bf16[352,128]{1,0:T(8,128)(2,1)S(1)}, bf16[352,128]{1,0:T(8,128)(2,1)S(1)}, u32[]{:S(2)}, u32[]{:S(2)}) collective-permute-start(bf16[352,128]{1,0:T(8,128)(2,1)S(1)} %get-tuple-element.68), channel_id=1, source_target_pairs={{0,8},{4,12},{8,0},{12,4},{1,9},{5,13},{9,1},{13,5},{2,10},{6,14},... | collective-permute-start | bytes 270344 | tf_op jit(solution)/shard_map/ppermute | solution.py:571
  36.7 4.3 %collective-permute-start.12 = (bf16[352,128]{1,0:T(8,128)(2,1)S(1)}, bf16[352,128]{1,0:T(8,128)(2,1)S(1)}, u32[]{:S(2)}, u32[]{:S(2)}) collective-permute-start(bf16[352,128]{1,0:T(8,128)(2,1)S(1)} %get-tuple-element.69), channel_id=1, source_target_pairs={{0,12},{4,0},{8,4},{12,8},{1,13},{5,1},{9,5},{13,9},{2,14},{6,2},{... | collective-permute-start | bytes 270344 | tf_op jit(solution)/shard_map/ppermute | solution.py:571

commit v12 on v11

--- a/solution.py
+++ b/solution.py
@@ -11,7 +11,7 @@
 PAIR_FEATURES = 128
 GROUP = 8
 MULTIPLY_ROWS = 384
-CHUNKS = 2
+CHUNKS = 1
 BIAS_ROWS = 16
 LANES = 128
 F32 = jnp.float32
@@ -146,7 +146,7 @@
     for piece, parity in zip(pieces, (odd, 1 - odd), strict=True):
         block = piece[...].astype(F32)
         for p in range(half):
-            place = (2 * lax.rem(home - p + half, half) + parity) * depth
+            place = (2 * lax.bitwise_xor(home, p) + parity) * depth
             held[pl.ds(pl.multiple_of(place, depth), depth), :] = block[p * depth : (p + 1) * depth]
 
 
@@ -170,6 +170,13 @@
         for m in range(GROUP)
         if m * sequences < (tile + 1) * LANES and (m + 1) * sequences > tile * LANES
     ]
+
+
+def chunks(body):
+    if CHUNKS == 1:
+        body(0)
+    else:
+        pl.loop(0, CHUNKS)(body)
 
 
 def diagonal_of(wide, channel, positions, sequences):
@@ -191,23 +198,16 @@
     return jnp.concatenate(columns, axis=1)
 
 
-def near_of(me):
-    return me + 1 - 2 * lax.rem(me, 2)
-
-
-def near_of(me):
-    return me + 1 - 2 * lax.rem(me, 2)
-
-
-def in_order(count):
-    return lambda me: ([me], [[lax.rem(me + d, count)] for d in range(1, count)])
+def alone(count):
+    return lambda me: ([me], [[lax.bitwise_xor(me, d)] for d in range(1, count)])
 
 
 def in_pairs(count):
     def plan(me):
-        steps = range(0, count, 2)
-        near = near_of(me)
-        return [lax.rem(me + d, count) for d in steps], [[lax.rem(near + d, count) for d in steps]]
+        evens = range(0, count, 2)
+        return [lax.bitwise_xor(me, d) for d in evens], [
+            [lax.bitwise_xor(me, d + 1) for d in evens]
+        ]
 
     return plan
 
@@ -237,10 +237,10 @@
         value += dot(jnp.concatenate(rows, axis=0), (shifted == m * sequences).astype(BF16))
     left[...] = value.astype(BF16)
 
-    @pl.loop(0, CHUNKS)
+    @chunks
     def _(t):
         size = per_step * depth
-        rows = pl.ds(pl.multiple_of(t * size, size), size)
+        rows = pl.ds(t * size if CHUNKS == 1 else pl.multiple_of(t * size, size), size)
         x_part = x_ref.at[rows]
         for e in range(0, per_step, 2):
             right = [diagonal_of(b_wide, t * per_step + e + n, j_n, sequences) for n in range(2)]
@@ -257,7 +257,7 @@
     share = total.shape[0] // row_n
     me = lax.axis_index("row")
     for p, message in enumerate(messages):
-        part = lax.rem(me + p, row_n)
+        part = lax.bitwise_xor(me, p)
         for n in range(share // depth):
             block = total[pl.ds(part * (share // depth) + n, depth, stride=depth), :]
             message[n * depth : (n + 1) * depth, :] = block.astype(message.dtype)
@@ -303,20 +303,17 @@
 def gradient_kernel(axis, plan, kept, positions, others, sequences, *refs):
     depth = PROJECTED_DEPTH
     wide, source = refs[:2]
-    outs, (result, grown, grad, own_wide) = refs[3:-4], refs[-4:]
-    if len(wide.shape) == 2:
-        spread(wide, own_wide)
-        wide = own_wide
+    outs, (result, grown, grad) = refs[3:-3], refs[-3:]
     parts = lax.axis_size(axis)
     per_step = depth // CHUNKS
     span = GROUP * others
 
     result[...] = jnp.zeros(result.shape, F32)
 
-    @pl.loop(0, CHUNKS)
+    @chunks
     def _(t):
         size = per_step * depth
-        rows = pl.ds(pl.multiple_of(t * size, size), size)
+        rows = pl.ds(t * size if CHUNKS == 1 else pl.multiple_of(t * size, size), size)
         part = source.at[rows]
         for n in range(0, per_step, 2):
             blocks = [
@@ -371,7 +368,6 @@
     shapes = [jax.ShapeDtypeStruct((rows, LANES), F32)] * kept
     group = (parts - kept) // groups
     shapes += [jax.ShapeDtypeStruct((group * rows, LANES), BF16)] * groups
-    tiles = GROUP * sequences // LANES if wide.ndim == 2 else 1
     results = pl.pallas_call(
         functools.partial(gradient_kernel, axis, plan, kept, positions, others, sequences),
         in_specs=[in_vmem(), in_vmem(), pl.BlockSpec(memory_space=pl.ANY)],
@@ -381,7 +377,6 @@
             pltpu.VMEM((positions // GROUP * depth, GROUP * sequences), F32),
             pltpu.VMEM((positions * depth, GROUP * sequences), BF16),
             pltpu.VMEM((sequences, positions * depth), F32),
-            pltpu.VMEM((tiles, others * depth if wide.ndim == 2 else 8, LANES), F32),
         ],
         compiler_params=params(sequences),
         cost_estimate=pl.CostEstimate(
@@ -393,24 +388,26 @@
     return results[:kept], results[kept:]
 
 
-def product_kernel(left_ref, right_ref, _, out_ref):
+def product_kernel(left_ref, right_ref, held, _, out_ref, wide):
+    spread(held, wide)
     multiply(left_ref, right_ref, out_ref)
 
 
-def product(left, right, after):
+def product(left, right, held, after):
     shape = (left.shape[0], right.shape[0])
+    spread_shape = (GROUP * held.shape[0] // LANES, held.shape[1], LANES)
     return pl.pallas_call(
         product_kernel,
-        in_specs=[in_vmem(), in_vmem(), pl.BlockSpec(memory_space=pl.ANY)],
-        out_specs=in_vmem(),
-        out_shape=jax.ShapeDtypeStruct(shape, BF16),
-        compiler_params=params(16),
+        in_specs=[in_vmem()] * 3 + [pl.BlockSpec(memory_space=pl.ANY)],
+        out_specs=[in_vmem()] * 2,
+        out_shape=[jax.ShapeDtypeStruct(shape, BF16), jax.ShapeDtypeStruct(spread_shape, F32)],
+        compiler_params=params(32),
         cost_estimate=pl.CostEstimate(
             flops=2 * shape[0] * shape[1] * left.shape[1],
             bytes_accessed=4 * shape[0] * shape[1],
             transcendentals=0,
         ),
-    )(left, right, after)
+    )(left, right, held, after)
 
 
 def pair_kernel(sequences, x_ref, wt_ref, bias_ref, _, out_ref):
@@ -459,6 +456,10 @@
     )(*operands, *after)
 
 
+def partners(count):
+    return [0, *range(count - 1, 0, -1)]
+
+
 def row_sum(parts, after, share):
     count = len(parts)
 
@@ -466,8 +467,8 @@
         parts, (_, message, held) = refs[:count], refs[count:]
         me = lax.axis_index("row")
         total = parts[0][0:share, :]
-        for p, part in enumerate(parts):
-            held[lax.rem(me - p + count, count)] = part[share:, :].astype(F32)
+        for p, part in zip(partners(count), parts, strict=True):
+            held[lax.bitwise_xor(me, p)] = part[share:, :].astype(F32)
             if p > 0:
                 total += part[0:share, :].astype(F32)
         bias = joined(held[0])
@@ -517,7 +518,7 @@
         messages, (piece_out, bias_out, held) = refs[:sent], refs[sent:]
         home = lax.div(lax.axis_index("col"), 2)
         for p, part in enumerate(parts):
-            held[lax.rem(home - p + count, count)] = part[...]
+            held[lax.bitwise_xor(home, p)] = part[...]
         total, bias = held[0, 0:share, :].astype(F32), joined(held[0, share:, :])
         for n in range(1, count):
             total += held[n, 0:share, :].astype(F32)
@@ -545,8 +546,8 @@
         right_own, bias, projection, left_out, right_out, bias_out = refs
         me = lax.axis_index("row")
         right_total = right_own[...]
-        for p, piece in enumerate(pieces):
-            rows = pl.ds(pl.multiple_of(lax.rem(me - p + count, count) * share, share), share)
+        for p, piece in zip(partners(count), pieces, strict=True):
+            rows = pl.ds(pl.multiple_of(lax.bitwise_xor(me, p) * share, share), share)
             projection[rows, :] = piece[0:share, :].astype(F32) * scale
             if p > 0:
                 right_total += piece[share:, :].astype(F32)
@@ -566,25 +567,17 @@
     return call(kernel, [*pieces, *left, right_own, bias], shapes)
 
 
-def shift(x, axis, distance):
-    count = lax.axis_size(axis)
-    return lax.ppermute(x, axis, [(n, (n + distance) % count) for n in range(count)])
-
-
-def neighbour(x, axis):
-    return lax.ppermute(x, axis, [(n, n ^ 1) for n in range(lax.axis_size(axis))])
-
-
-def send(parts, axis):
-    return [shift(part, axis, d) for d, part in enumerate(parts, 1)]
-
-
-def spread_pairs(x, axis):
-    return send_pairs([x] * (lax.axis_size(axis) // 2 - 1), axis)
-
-
-def send_pairs(parts, axis):
-    return [shift(part, axis, 2 * p) for p, part in enumerate(parts, 1)]
+def swap(x, axis, p):
+    return lax.ppermute(x, axis, [(n, n ^ p) for n in range(lax.axis_size(axis))])
+
+
+def swap_each(parts, axis, step=1):
+    count = len(parts)
+    return [swap(parts[n - 1], axis, n * step) for n in range(count, 0, -1)][::-1]
+
+
+def from_evens(x, axis):
+    return swap_each([x] * (lax.axis_size(axis) // 2 - 1), axis, 2)
 
 
 def local(
@@ -595,8 +588,8 @@
     sequences = second_homolog_features.shape[0] * row_n
     channels = final_projection_matrix.shape[0]
     res_total = i_n * row_n
-    a_far = spread_pairs(first_homolog_features, "col")
-    b_far = spread_pairs(second_homolog_features, "row")
+    a_far = from_evens(first_homolog_features, "col")
+    b_far = from_evens(second_homolog_features, "row")
     we, wt, a, b, w, g = load(
         first_homolog_features,
         second_homolog_features,
@@ -604,8 +597,8 @@
         cotangent.reshape(i_n * j_n, PAIR_FEATURES),
     )
     a, b = stack([a, *a_far], [b, *b_far])
-    a_pieces = [a, neighbour(a, "col")]
-    b_pieces = [b, neighbour(b, "row")]
+    a_pieces = [a, swap(a, "col", 1)]
+    b_pieces = [b, swap(b, "row", 1)]
     y, gt, bias_rows = prepare(we, g, i_n, j_n)
 
     x, a_held, b_wide, (own, *messages) = outer(
@@ -613,26 +606,26 @@
     )
     share = channels // row_n
 
-    parts = [own] + send(messages, "row")
+    parts = [own] + swap_each(messages, "row")[::-1]
     left_kept, (message,) = gradient(
         b_wide, y, own, "col", in_pairs(col_n), col_n // 2, 1, i_n, j_n, sequences
     )
-    left_near = neighbour(message, "col")
+    left_near = swap(message, "col", 1)
 
     message = row_sum(parts, message, share)
-    near = neighbour(message, "col")
+    near = swap(message, "col", 1)
     left_own, left_messages = pair_sum(left_kept, left_near, message)
-    left = [left_own] + send_pairs(left_messages, "col")
-    y2 = product(w, gt, left_own)
+    left = [left_own] + swap_each(left_messages, "col", 2)
+    y2, a_wide = product(w, gt, a_held, left_own)
 
     message = column_pair_sum(message, near, y2, share)
-    parts = [message] + spread_pairs(message, "col")
+    parts = [message] + from_evens(message, "col")
     (right_own,), right_sent = gradient(
-        a_held, y2, message, "row", in_order(row_n), 1, row_n - 1, j_n, i_n, sequences
+        a_wide, y2, message, "row", alone(row_n), 1, row_n - 1, j_n, i_n, sequences
     )
 
     messages, piece, bias = column_sum(parts, right_sent, share)
-    pieces = [piece] + send(messages, "row")
+    pieces = [piece] + swap_each(messages, "row")[::-1]
     pair_map = pair(x, wt, output_bias, piece, sequences)
     projection, left_grad, right_grad, bias_grad = finish(
         pieces,

time: 42 us -> 41.8 us (level)
  starting transfers between devices: 18.8 us -> 17.4 us
  waiting for transfers between devices: 4.69 us -> 5.43 us
  Pallas kernels: 17.5 us -> 18.1 us
    ppermute x14, starting transfers between devices: 18.8 us -> 17.4 us  [swap(): lax.ppermute(x, axis, [(n, n ^ p) for n in range(lax.axis_size(axis))])]
    ppermute x14, waiting for transfers between devices: 4.69 us -> 5.43 us  [swap(): lax.ppermute(x, axis, [(n, n ^ p) for n in range(lax.axis_size(axis))])]
  transfers between devices with their start and end apart: 14 -> 14, of which waited for: 4 -> 6; matrix products, arithmetic and copies ran while one was open for 0% -> 0% of each run, Pallas kernels for 28% -> 29%
where the time goes in v12:
time: 41.8 us; the launch traced here: 41.6 us
  Pallas kernels  18.1 us (43%)
  starting transfers between devices  17.4 us (42%)
  waiting for transfers between devices  5.43 us (13%)
  between operations  0.72 us (2%)
    ppermute x14, starting transfers between devices, swap(): lax.ppermute(x, axis, [(n, n ^ p) for n in range(lax.axis_size(axis))])  17.4 us
    ppermute x14, waiting for transfers between devices, swap(): lax.ppermute(x, axis, [(n, n ^ p) for n in range(lax.axis_size(axis))])  5.43 us
    pallas_call x1, Pallas kernels, outer(): pl.pallas_call(functools.partial(outer_kernel, i_n, j_n), in_specs=[in_vm...  5.08 us
    pallas_call x2, Pallas kernels, gradient(): pl.pallas_call(functools.partial(gradient_kernel, axis, plan, kept, posit...  4.67 us
    pallas_call x1, Pallas kernels, pair(): pl.pallas_call(functools.partial(pair_kernel, sequences), grid=(count,),...  2.57 us
    pallas_call x1, Pallas kernels, prepare(): pl.pallas_call(functools.partial(prepare_kernel, i_n, j_n), in_specs=[in_...  1.76 us
    pallas_call x1, Pallas kernels, product(): pl.pallas_call(product_kernel, in_specs=[in_vmem()] * 3 + [pl.BlockSpec(m...  1.64 us
    pallas_call x1, Pallas kernels, load(): pl.pallas_call(load_kernel, in_specs=[pl.BlockSpec(memory_space=pltpu.HBM...  1.39 us
  transfers between devices with their start and end apart: 14, of which 6 were waited for; matrix products, arithmetic and copies ran while one was open for 0% of the time, Pallas kernels for 29%

profile of v12, /device:TPU:0, one launch (start us, length us, event | category | flops | bytes accessed | tf_op | source)
XLA Modules:
  0.0 41.6 jit_solution(10527441706692026530)
XLA Ops:
  0.6 4.1 %collective-permute-start = (bf16[8,1536]{1,0:T(8,128)(2,1)}, bf16[8,1536]{1,0:T(8,128)(2,1)S(1)}, u32[]{:S(2)}, u32[]{:S(2)}) collective-permute-start(bf16[8,1536]{1,0:T(8,128)(2,1)} %a_hbm.1), channel_id=1, source_target_pairs={{0,2},{1,3},{2,0},{3,1},{4,6},{5,7},{6,4},{7,5},{8,10},{9,11},{10,... | collective-permute-start | bytes 73736 | tf_op jit(solution)/shard_map/ppermute | solution.py:571
  4.7 1.5 %collective-permute-start.1 = (bf16[8,1536]{1,0:T(8,128)(2,1)}, bf16[8,1536]{1,0:T(8,128)(2,1)S(1)}, u32[]{:S(2)}, u32[]{:S(2)}) collective-permute-start(bf16[8,1536]{1,0:T(8,128)(2,1)} %b_hbm.1), channel_id=1, source_target_pairs={{0,8},{4,12},{8,0},{12,4},{1,9},{5,13},{9,1},{13,5},{2,10},{6,14},... | collective-permute-start | bytes 73736 | tf_op jit(solution)/shard_map/ppermute | solution.py:571
  6.2 1.4 %shard_map.92 = (bf16[1024,128]{1,0:T(8,128)(2,1)S(1)}, bf16[128,1024]{1,0:T(8,128)(2,1)S(1)}, bf16[8,1536]{1,0:T(8,128)(2,1)S(1)}, bf16[8,1536]{1,0:T(8,128)(2,...) custom-call(bf16[8,1536]{1,0:T(8,128)(2,1)} %a_hbm.1, bf16[8,1536]{1,0:T(8,128)(2,1)} %b_hbm.1, ...), custom_call_target="tpu_custom_call" | custom-call | flops 131072000 | bytes 2097152 | tf_op jit(solution)/shard_map/pallas_call | solution.py:67
  7.6 1.1 %collective-permute-done.1.refs_3_ = bf16[8,1536]{1,0:T(8,128)(2,1)S(1)} collective-permute-done((bf16[8,1536]{1,0:T(8,128)(2,1)}, bf16[8,1536]{1,0:T(8,128)(2,1)S(1)}, u32[]{:S(2)}, u32[]{:S(2)}) %collective-permute-start.1) | collective-permute-done | bytes 24608 | tf_op jit(solution)/shard_map/ppermute | solution.py:571
  8.8 1.6 %collective-permute-start.2 = (bf16[16,1536]{1,0:T(8,128)(2,1)S(1)}, bf16[16,1536]{1,0:T(8,128)(2,1)S(1)}, u32[]{:S(2)}, u32[]{:S(2)}) collective-permute-start(bf16[16,1536]{1,0:T(8,128)(2,1)S(1)} %get-tuple-element.45.refs_0_), channel_id=1, source_target_pairs={{0,1},{1,0},{2,3},{3,2},{4,5},{5,4},{6,7},{7,6},{8,9},{9,8},{10,11... | collective-permute-start | bytes 147464 | tf_op jit(solution)/shard_map/ppermute | solution.py:571
  10.4 0.0 collective-permute-start.3
  10.4 1.8 %shard_map.94 = (bf16[1024,2304]{1,0:T(8,128)(2,1)S(1)}, bf16[2304,128]{1,0:T(8,128)(2,1)S(1)}, bf16[16,128]{1,0:T(8,128)(2,1)S(1)}) custom-call(bf16[1024,128]{1,0:T(8,128)(2,1)S(1)} %get-tuple-element.48.we_ref, bf16[2304,128]{1,0:T(8,128)(2,1)S(1)} %get-tuple-element.47.g_ref.refs_4_), custom_call_target="tpu_custom_call" | custom-call | flops 603979776 | bytes 9437184 | tf_op jit(solution)/shard_map/pallas_call | solution.py:126
  12.2 0.7 %collective-permute-done.2.refs_1_ = bf16[16,1536]{1,0:T(8,128)(2,1)S(1)} collective-permute-done((bf16[16,1536]{1,0:T(8,128)(2,1)S(1)}, bf16[16,1536]{1,0:T(8,128)(2,1)S(1)}, u32[]{:S(2)}, u32[]{:S(2)}) %collective-permute-start.2) | collective-permute-done | bytes 49184 | tf_op jit(solution)/shard_map/ppermute | solution.py:571
  12.9 0.0 collective-permute-done.3.refs_3_
  12.9 5.1 %shard_map.95 = (bf16[1024,2304]{1,0:T(8,128)(2,1)S(1)}, f32[32,1536]{1,0:T(8,128)S(1)}, f32[2,1536,128]{2,1,0:T(8,128)S(1)}, f32[272,128]{1,0:T(8,128)S(1)}, bf...) custom-call(bf16[16,1536]{1,0:T(8,128)(2,1)S(1)} %get-tuple-element.45.refs_0_, ...), custom_call_target="tpu_custom_call" | custom-call | flops 1207959552 | bytes 4718592 | tf_op jit(solution)/shard_map/pallas_call | solution.py:283
  18.0 1.0 %collective-permute-start.4 = (bf16[272,128]{1,0:T(8,128)(2,1)S(1)}, bf16[272,128]{1,0:T(8,128)(2,1)S(1)}, u32[]{:S(2)}, u32[]{:S(2)}) collective-permute-start(bf16[272,128]{1,0:T(8,128)(2,1)S(1)} %get-tuple-element.53), channel_id=1, source_target_pairs={{0,12},{4,8},{8,4},{12,0},{1,13},{5,9},{9,5},{13,1},{2,14},{6,10},... | collective-permute-start | bytes 208904 | tf_op jit(solution)/shard_map/ppermute | solution.py:571
  19.0 0.7 %collective-permute-start.5 = (bf16[272,128]{1,0:T(8,128)(2,1)S(1)}, bf16[272,128]{1,0:T(8,128)(2,1)S(1)}, u32[]{:S(2)}, u32[]{:S(2)}) collective-permute-start(bf16[272,128]{1,0:T(8,128)(2,1)S(1)} %get-tuple-element.54), channel_id=1, source_target_pairs={{0,8},{4,12},{8,0},{12,4},{1,9},{5,13},{9,1},{13,5},{2,10},{6,14},... | collective-permute-start | bytes 208904 | tf_op jit(solution)/shard_map/ppermute | solution.py:571
  19.7 0.3 collective-permute-start.6
  20.0 2.4 %shard_map.96 = (f32[96,128]{1,0:T(8,128)S(1)}, f32[96,128]{1,0:T(8,128)S(1)}, bf16[192,128]{1,0:T(8,128)(2,1)S(1)}) custom-call(f32[2,1536,128]{2,1,0:T(8,128)S(1)} %get-tuple-element.56.refs_0_, bf16[1024,2304]{1,0:T(8,128)(2,1)S(1)} %get-tuple-element.57.refs_1_, f32[272,128]{1,0:T(8,128)S(1)} %get-tuple-element.52.refs_2_.refs_0_), custom_call_target="tpu_custom_call" | custom-call | flops 603979776 | bytes 4718592 | tf_op jit(solution)/shard_map/pallas_call | solution.py:371
  22.4 1.6 %collective-permute-start.8 = (bf16[192,128]{1,0:T(8,128)(2,1)S(1)}, bf16[192,128]{1,0:T(8,128)(2,1)S(1)}, u32[]{:S(2)}, u32[]{:S(2)}) collective-permute-start(bf16[192,128]{1,0:T(8,128)(2,1)S(1)} %get-tuple-element.58.refs_4_), channel_id=1, source_target_pairs={{0,1},{1,0},{2,3},{3,2},{4,5},{5,4},{6,7},{7,6},{8,9},{9,8},{10,11... | collective-permute-start | bytes 147464 | tf_op jit(solution)/shard_map/ppermute | solution.py:571
  24.0 0.0 collective-permute-done.5.refs_2_
  24.1 1.6 %collective-permute-start.7 = (bf16[272,128]{1,0:T(8,128)(2,1)S(1)}, bf16[272,128]{1,0:T(8,128)(2,1)S(1)}, u32[]{:S(2)}, u32[]{:S(2)}) collective-permute-start(bf16[272,128]{1,0:T(8,128)(2,1)S(1)} %shard_map.97.refs_3_.own), channel_id=1, source_target_pairs={{0,1},{1,0},{2,3},{3,2},{4,5},{5,4},{6,7},{7,6},{8,9},{9,8},{10,11... | collective-permute-start | bytes 208904 | tf_op jit(solution)/shard_map/ppermute | solution.py:571
  25.8 0.8 %collective-permute-done.8.refs_2_ = bf16[192,128]{1,0:T(8,128)(2,1)S(1)} collective-permute-done((bf16[192,128]{1,0:T(8,128)(2,1)S(1)}, bf16[192,128]{1,0:T(8,128)(2,1)S(1)}, u32[]{:S(2)}, u32[]{:S(2)}) %collective-permute-start.8) | collective-permute-done | bytes 49184 | tf_op jit(solution)/shard_map/ppermute | solution.py:571
  26.5 1.6 %shard_map.99 = (bf16[1024,2304]{1,0:T(8,128)(2,1)S(1)}, f32[2,1536,128]{2,1,0:T(8,128)S(1)}) custom-call(bf16[1024,128]{1,0:T(8,128)(2,1)S(1)} %get-tuple-element.59.left_ref, bf16[2304,128]{1,0:T(8,128)(2,1)S(1)} %get-tuple-element.60.right_ref, f32[32,1536]{1,0:T(8,128)S(1)} %get-tuple-element.61.held, f32[96,128]{1,0:T(8,128)S(1)} %get-tuple-element.64._.refs_4_), custom_call_target="tpu_custom_call" | custom-call | flops 603979776 | bytes 9437184 | tf_op jit(solution)/shard_map/pallas_call | solution.py:399
  28.2 0.3 collective-permute-done.7.near
  28.5 1.1 %collective-permute-start.9 = (bf16[272,128]{1,0:T(8,128)(2,1)S(1)}, bf16[272,128]{1,0:T(8,128)(2,1)S(1)}, u32[]{:S(2)}, u32[]{:S(2)}) collective-permute-start(bf16[272,128]{1,0:T(8,128)(2,1)S(1)} %shard_map.100.refs_2_.refs_0_), channel_id=1, source_target_pairs={{0,2},{1,3},{2,0},{3,1},{4,6},{5,7},{6,4},{7,5},{8,10},{9,11},{10,... | collective-permute-start | bytes 208904 | tf_op jit(solution)/shard_map/ppermute | solution.py:571
  29.6 1.9 %collective-permute-start.13 = (bf16[96,128]{1,0:T(8,128)(2,1)S(1)}, bf16[96,128]{1,0:T(8,128)(2,1)S(1)}, u32[]{:S(2)}, u32[]{:S(2)}) collective-permute-start(bf16[96,128]{1,0:T(8,128)(2,1)S(1)} %get-tuple-element.74), channel_id=1, source_target_pairs={{0,2},{1,3},{2,0},{3,1},{4,6},{5,7},{6,4},{7,5},{8,10},{9,11},{10,... | collective-permute-start | bytes 73736 | tf_op jit(solution)/shard_map/ppermute | solution.py:571
  31.5 2.3 %shard_map.101 = (f32[96,128]{1,0:T(8,128)S(1)}, bf16[96,128]{1,0:T(8,128)(2,1)S(1)}, bf16[96,128]{1,0:T(8,128)(2,1)S(1)}, bf16[96,128]{1,0:T(8,128)(2,1)S(1)}) custom-call(f32[2,1536,128]{2,1,0:T(8,128)S(1)} %get-tuple-element.66.refs_0_, bf16[1024,2304]{1,0:T(8,128)(2,1)S(1)} %get-tuple-element.65._.refs_1_, bf16[272,128]{1,0:T(8,128)(2,1)S(1)} %shard_map.100.refs_2_.refs_0_), custom_call_target="tpu_custom_call" | custom-call | flops 603979776 | bytes 4718592 | tf_op jit(solution)/shard_map/pallas_call | solution.py:371
  33.8 0.0 collective-permute-done.9.refs_1_
  33.8 0.1 shard_map.102
  33.9 0.1 collective-permute-start.10
  33.9 1.8 %collective-permute-start.11 = (bf16[352,128]{1,0:T(8,128)(2,1)S(1)}, bf16[352,128]{1,0:T(8,128)(2,1)S(1)}, u32[]{:S(2)}, u32[]{:S(2)}) collective-permute-start(bf16[352,128]{1,0:T(8,128)(2,1)S(1)} %get-tuple-element.72), channel_id=1, source_target_pairs={{0,8},{4,12},{8,0},{12,4},{1,9},{5,13},{9,1},{13,5},{2,10},{6,14},... | collective-permute-start | bytes 270344 | tf_op jit(solution)/shard_map/ppermute | solution.py:571
  35.7 0.1 collective-permute-start.12
  35.8 2.6 %shard_map.103 = bf16[2304,128]{1,0:T(8,128)(2,1)} custom-call(bf16[1024,2304]{1,0:T(8,128)(2,1)S(1)} %get-tuple-element.50.x_ref, bf16[128,1024]{1,0:T(8,128)(2,1)S(1)} %get-tuple-element.51.wt_ref, f32[1,128]{1,0:T(1,128)S(1)} %bitcast.4, bf16[256,128]{1,0:T(8,128)(2,1)S(1)} %get-tuple-element.70._.refs_0_), custom_call_target="tpu_custom_call" | custom-call | flops 1207959552 | bytes 4718592 | tf_op jit(solution)/shard_map/pallas_call | solution.py:422
  38.4 0.2 collective-permute-done.10.refs_1_
  38.6 2.2 %collective-permute-done.11.refs_2_ = bf16[352,128]{1,0:T(8,128)(2,1)S(1)} collective-permute-done((bf16[352,128]{1,0:T(8,128)(2,1)S(1)}, bf16[352,128]{1,0:T(8,128)(2,1)S(1)}, u32[]{:S(2)}, u32[]{:S(2)}) %collective-permute-start.11) | collective-permute-done | bytes 90144 | tf_op jit(solution)/shard_map/ppermute | solution.py:571
  40.8 0.9 %shard_map.104 = (f32[1024,128]{1,0:T(8,128)}, f32[8,1536]{1,0:T(8,128)}, f32[8,1536]{1,0:T(8,128)}, f32[1,128]{1,0:T(1,128)}) custom-call(bf16[256,128]{1,0:T(8,128)(2,1)S(1)} %get-tuple-element.70._.refs_0_, bf16[352,128]{1,0:T(8,128)(2,1)S(1)} %collective-permute-done.10.refs_1_, bf16[352,128]{1,0:T(8,128)(2,1)S(1)} %collective-permute-done.11.refs_2_, ...), custom_call_target="tpu_custom_call" | custom-call | tf_op jit(solution)/shard_map/pallas_call | solution.py:449
  (11 shorter events, 0.1 us)
Async XLA Ops:
  0.6 7.0 %collective-permute-start = (bf16[8,1536]{1,0:T(8,128)(2,1)}, bf16[8,1536]{1,0:T(8,128)(2,1)S(1)}, u32[]{:S(2)}, u32[]{:S(2)}) collective-permute-start(bf16[8,1536]{1,0:T(8,128)(2,1)} %a_hbm.1), channel_id=1, source_target_pairs={{0,2},{1,3},{2,0},{3,1},{4,6},{5,7},{6,4},{7,5},{8,10},{9,11},{10,... | collective-permute-start | bytes 73736 | tf_op jit(solution)/shard_map/ppermute | solution.py:571
  4.7 4.0 %collective-permute-start.1 = (bf16[8,1536]{1,0:T(8,128)(2,1)}, bf16[8,1536]{1,0:T(8,128)(2,1)S(1)}, u32[]{:S(2)}, u32[]{:S(2)}) collective-permute-start(bf16[8,1536]{1,0:T(8,128)(2,1)} %b_hbm.1), channel_id=1, source_target_pairs={{0,8},{4,12},{8,0},{12,4},{1,9},{5,13},{9,1},{13,5},{2,10},{6,14},... | collective-permute-start | bytes 73736 | tf_op jit(solution)/shard_map/ppermute | solution.py:571
  8.8 4.2 %collective-permute-start.2 = (bf16[16,1536]{1,0:T(8,128)(2,1)S(1)}, bf16[16,1536]{1,0:T(8,128)(2,1)S(1)}, u32[]{:S(2)}, u32[]{:S(2)}) collective-permute-start(bf16[16,1536]{1,0:T(8,128)(2,1)S(1)} %get-tuple-element.45.refs_0_), channel_id=1, source_target_pairs={{0,1},{1,0},{2,3},{3,2},{4,5},{5,4},{6,7},{7,6},{8,9},{9,8},{10,11... | collective-permute-start | bytes 147464 | tf_op jit(solution)/shard_map/ppermute | solution.py:571
  10.4 2.5 %collective-permute-start.3 = (bf16[16,1536]{1,0:T(8,128)(2,1)S(1)}, bf16[16,1536]{1,0:T(8,128)(2,1)S(1)}, u32[]{:S(2)}, u32[]{:S(2)}) collective-permute-start(bf16[16,1536]{1,0:T(8,128)(2,1)S(1)} %get-tuple-element.46.refs_2_), channel_id=1, source_target_pairs={{0,4},{4,0},{8,12},{12,8},{1,5},{5,1},{9,13},{13,9},{2,6},{6,2},{1... | collective-permute-start | bytes 147464 | tf_op jit(solution)/shard_map/ppermute | solution.py:571
  18.0 6.0 %collective-permute-start.4 = (bf16[272,128]{1,0:T(8,128)(2,1)S(1)}, bf16[272,128]{1,0:T(8,128)(2,1)S(1)}, u32[]{:S(2)}, u32[]{:S(2)}) collective-permute-start(bf16[272,128]{1,0:T(8,128)(2,1)S(1)} %get-tuple-element.53), channel_id=1, source_target_pairs={{0,12},{4,8},{8,4},{12,0},{1,13},{5,9},{9,5},{13,1},{2,14},{6,10},... | collective-permute-start | bytes 208904 | tf_op jit(solution)/shard_map/ppermute | solution.py:571
  19.0 5.1 %collective-permute-start.5 = (bf16[272,128]{1,0:T(8,128)(2,1)S(1)}, bf16[272,128]{1,0:T(8,128)(2,1)S(1)}, u32[]{:S(2)}, u32[]{:S(2)}) collective-permute-start(bf16[272,128]{1,0:T(8,128)(2,1)S(1)} %get-tuple-element.54), channel_id=1, source_target_pairs={{0,8},{4,12},{8,0},{12,4},{1,9},{5,13},{9,1},{13,5},{2,10},{6,14},... | collective-permute-start | bytes 208904 | tf_op jit(solution)/shard_map/ppermute | solution.py:571
  19.7 4.4 %collective-permute-start.6 = (bf16[272,128]{1,0:T(8,128)(2,1)S(1)}, bf16[272,128]{1,0:T(8,128)(2,1)S(1)}, u32[]{:S(2)}, u32[]{:S(2)}) collective-permute-start(bf16[272,128]{1,0:T(8,128)(2,1)S(1)} %get-tuple-element.55), channel_id=1, source_target_pairs={{0,4},{4,0},{8,12},{12,8},{1,5},{5,1},{9,13},{13,9},{2,6},{6,2},{1... | collective-permute-start | bytes 208904 | tf_op jit(solution)/shard_map/ppermute | solution.py:571
  22.4 4.2 %collective-permute-start.8 = (bf16[192,128]{1,0:T(8,128)(2,1)S(1)}, bf16[192,128]{1,0:T(8,128)(2,1)S(1)}, u32[]{:S(2)}, u32[]{:S(2)}) collective-permute-start(bf16[192,128]{1,0:T(8,128)(2,1)S(1)} %get-tuple-element.58.refs_4_), channel_id=1, source_target_pairs={{0,1},{1,0},{2,3},{3,2},{4,5},{5,4},{6,7},{7,6},{8,9},{9,8},{10,11... | collective-permute-start | bytes 147464 | tf_op jit(solution)/shard_map/ppermute | solution.py:571
  24.1 4.4 %collective-permute-start.7 = (bf16[272,128]{1,0:T(8,128)(2,1)S(1)}, bf16[272,128]{1,0:T(8,128)(2,1)S(1)}, u32[]{:S(2)}, u32[]{:S(2)}) collective-permute-start(bf16[272,128]{1,0:T(8,128)(2,1)S(1)} %shard_map.97.refs_3_.own), channel_id=1, source_target_pairs={{0,1},{1,0},{2,3},{3,2},{4,5},{5,4},{6,7},{7,6},{8,9},{9,8},{10,11... | collective-permute-start | bytes 208904 | tf_op jit(solution)/shard_map/ppermute | solution.py:571
  28.5 7.3 %copy-start = (f32[128]{0:T(128)S(1)}, f32[128]{0:T(128)}, u32[]{:S(2)}) copy-start(f32[128]{0:T(128)} %param.8) | copy-start | bytes 1540
  28.5 5.3 %collective-permute-start.9 = (bf16[272,128]{1,0:T(8,128)(2,1)S(1)}, bf16[272,128]{1,0:T(8,128)(2,1)S(1)}, u32[]{:S(2)}, u32[]{:S(2)}) collective-permute-start(bf16[272,128]{1,0:T(8,128)(2,1)S(1)} %shard_map.100.refs_2_.refs_0_), channel_id=1, source_target_pairs={{0,2},{1,3},{2,0},{3,1},{4,6},{5,7},{6,4},{7,5},{8,10},{9,11},{10,... | collective-permute-start | bytes 208904 | tf_op jit(solution)/shard_map/ppermute | solution.py:571
  29.6 8.8 %collective-permute-start.13 = (bf16[96,128]{1,0:T(8,128)(2,1)S(1)}, bf16[96,128]{1,0:T(8,128)(2,1)S(1)}, u32[]{:S(2)}, u32[]{:S(2)}) collective-permute-start(bf16[96,128]{1,0:T(8,128)(2,1)S(1)} %get-tuple-element.74), channel_id=1, source_target_pairs={{0,2},{1,3},{2,0},{3,1},{4,6},{5,7},{6,4},{7,5},{8,10},{9,11},{10,... | collective-permute-start | bytes 73736 | tf_op jit(solution)/shard_map/ppermute | solution.py:571
  33.9 4.7 %collective-permute-start.10 = (bf16[352,128]{1,0:T(8,128)(2,1)S(1)}, bf16[352,128]{1,0:T(8,128)(2,1)S(1)}, u32[]{:S(2)}, u32[]{:S(2)}) collective-permute-start(bf16[352,128]{1,0:T(8,128)(2,1)S(1)} %get-tuple-element.71), channel_id=1, source_target_pairs={{0,12},{4,8},{8,4},{12,0},{1,13},{5,9},{9,5},{13,1},{2,14},{6,10},... | collective-permute-start | bytes 270344 | tf_op jit(solution)/shard_map/ppermute | solution.py:571
  33.9 6.8 %collective-permute-start.11 = (bf16[352,128]{1,0:T(8,128)(2,1)S(1)}, bf16[352,128]{1,0:T(8,128)(2,1)S(1)}, u32[]{:S(2)}, u32[]{:S(2)}) collective-permute-start(bf16[352,128]{1,0:T(8,128)(2,1)S(1)} %get-tuple-element.72), channel_id=1, source_target_pairs={{0,8},{4,12},{8,0},{12,4},{1,9},{5,13},{9,1},{13,5},{2,10},{6,14},... | collective-permute-start | bytes 270344 | tf_op jit(solution)/shard_map/ppermute | solution.py:571
  35.7 5.1 %collective-permute-start.12 = (bf16[352,128]{1,0:T(8,128)(2,1)S(1)}, bf16[352,128]{1,0:T(8,128)(2,1)S(1)}, u32[]{:S(2)}, u32[]{:S(2)}) collective-permute-start(bf16[352,128]{1,0:T(8,128)(2,1)S(1)} %get-tuple-element.73), channel_id=1, source_target_pairs={{0,4},{4,0},{8,12},{12,8},{1,5},{5,1},{9,13},{13,9},{2,6},{6,2},{1... | collective-permute-start | bytes 270344 | tf_op jit(solution)/shard_map/ppermute | solution.py:571

commit v13 on v12

--- a/solution.py
+++ b/solution.py
@@ -11,7 +11,7 @@
 PAIR_FEATURES = 128
 GROUP = 8
 MULTIPLY_ROWS = 384
-CHUNKS = 1
+CHUNKS = 2
 BIAS_ROWS = 16
 LANES = 128
 F32 = jnp.float32
@@ -34,7 +34,31 @@
     return lax.dot_general(x, y, dims, preferred_element_type=F32)
 
 
-def load_kernel(a_hbm, b_hbm, w_hbm, g_hbm, we_ref, wt_ref, a_ref, b_ref, w_ref, g_ref, w32, sems):
+def in_vmem():
+    return pl.BlockSpec(memory_space=pltpu.VMEM)
+
+
+def split(total):
+    high = total.astype(BF16).astype(F32)
+    row = lax.broadcasted_iota(jnp.int32, (BIAS_ROWS, PAIR_FEATURES), 0)
+    return jnp.where(row == 0, high, jnp.where(row == 1, total - high, 0.0)).astype(BF16)
+
+
+def joined(block):
+    block = block.astype(F32)
+    return block[0:1] + block[1:2]
+
+
+def multiply(left_ref, right_ref, out_ref):
+    for n in range(0, right_ref.shape[0], MULTIPLY_ROWS):
+        rows = slice(n, n + MULTIPLY_ROWS)
+        out_ref[:, rows] = dot(left_ref[...], right_ref[rows, :], ROWS_BY_ROWS).astype(BF16)
+
+
+def prepare_kernel(
+    i_n, j_n, a_hbm, b_hbm, w_hbm, g_hbm, y_ref, gt_ref, wt_ref, bias_ref, a_ref, b_ref, w_ref, g_ref,
+    w32, we, g32, sems,
+):
     depth = PROJECTED_DEPTH
     copies = [
         pltpu.make_async_copy(source, target, sems.at[n])
@@ -48,106 +72,53 @@
     w32[...] = w_ref[...].astype(F32)
     for e in range(depth):
         block = w32[pl.ds(e, depth, stride=depth), :]
-        we_ref[e * depth : (e + 1) * depth, :] = block.astype(BF16)
-    wt_ref[...] = we_ref[...].astype(F32).T.astype(BF16)
-    for copy in copies[1:]:
+        we[e * depth : (e + 1) * depth, :] = block.astype(BF16)
+    wt_ref[...] = we[...].astype(F32).T.astype(BF16)
+    copies[1].wait()
+    g32[...] = g_ref[...].astype(F32)
+    bias_ref[...] = split(jnp.sum(g32[...], axis=0, keepdims=True))
+    multiply(we, g_ref, y_ref)
+    for j in range(j_n):
+        gt_ref[j * i_n : (j + 1) * i_n, :] = g32[pl.ds(j, i_n, stride=j_n), :].astype(BF16)
+    for copy in copies[2:]:
         copy.wait()
 
 
-def in_vmem():
-    return pl.BlockSpec(memory_space=pltpu.VMEM)
-
-
-def load(a, b, w, g):
+def prepare(a, b, w, g, i_n, j_n):
+    channels, pairs = w.shape[0], g.shape[0]
     shapes = [
-        jax.ShapeDtypeStruct(w.shape, BF16),
+        jax.ShapeDtypeStruct((channels, pairs), BF16),
+        jax.ShapeDtypeStruct(g.shape, BF16),
         jax.ShapeDtypeStruct(w.shape[::-1], BF16),
+        jax.ShapeDtypeStruct((BIAS_ROWS, PAIR_FEATURES), BF16),
         *[jax.ShapeDtypeStruct(x.shape, BF16) for x in (a, b, w, g)],
     ]
     return pl.pallas_call(
-        load_kernel,
+        functools.partial(prepare_kernel, i_n, j_n),
         in_specs=[pl.BlockSpec(memory_space=pltpu.HBM)] * 4,
         out_specs=[in_vmem()] * len(shapes),
         out_shape=shapes,
-        scratch_shapes=[pltpu.VMEM(w.shape, F32), pltpu.SemaphoreType.DMA((4,))],
-        compiler_params=params(),
-        cost_estimate=pl.CostEstimate(
-            flops=1000 * w.size, bytes_accessed=16 * w.size, transcendentals=0
-        ),
-    )(*[pltpu.with_memory_space_constraint(x, pltpu.HBM) for x in (a, b, w, g)])
-
-
-def stack(*groups):
-    def kernel(*refs):
-        refs, outs = refs[: -len(groups)], refs[-len(groups) :]
-        for group, out in zip(groups, outs, strict=True):
-            blocks = [ref[...].astype(F32) for ref in refs[: len(group)]]
-            refs = refs[len(group) :]
-            out[...] = jnp.concatenate(blocks, axis=0).astype(BF16)
-
-    shapes = [((len(group) * group[0].shape[0], group[0].shape[1]), BF16) for group in groups]
-    return call(kernel, [x for group in groups for x in group], shapes)
-
-
-def split(total):
-    high = total.astype(BF16).astype(F32)
-    row = lax.broadcasted_iota(jnp.int32, (BIAS_ROWS, PAIR_FEATURES), 0)
-    return jnp.where(row == 0, high, jnp.where(row == 1, total - high, 0.0)).astype(BF16)
-
-
-def joined(block):
-    block = block.astype(F32)
-    return block[0:1] + block[1:2]
-
-
-def multiply(left_ref, right_ref, out_ref):
-    for n in range(0, right_ref.shape[0], MULTIPLY_ROWS):
-        rows = slice(n, n + MULTIPLY_ROWS)
-        out_ref[:, rows] = dot(left_ref[...], right_ref[rows, :], ROWS_BY_ROWS).astype(BF16)
-
-
-def prepare_kernel(i_n, j_n, we_ref, g_ref, y_ref, gt_ref, bias_ref, g32):
-    g32[...] = g_ref[...].astype(F32)
-    bias_ref[...] = split(jnp.sum(g32[...], axis=0, keepdims=True))
-    multiply(we_ref, g_ref, y_ref)
-
-    for j in range(j_n):
-        gt_ref[j * i_n : (j + 1) * i_n, :] = g32[pl.ds(j, i_n, stride=j_n), :].astype(BF16)
-
-
-def prepare(we, g, i_n, j_n):
-    pairs = i_n * j_n
-    channels = we.shape[0]
-    shapes = [
-        jax.ShapeDtypeStruct((channels, pairs), BF16),
-        jax.ShapeDtypeStruct(g.shape, BF16),
-        jax.ShapeDtypeStruct((BIAS_ROWS, PAIR_FEATURES), BF16),
-    ]
-    return pl.pallas_call(
-        functools.partial(prepare_kernel, i_n, j_n),
-        in_specs=[in_vmem()] * 2,
-        out_specs=[in_vmem()] * len(shapes),
-        out_shape=shapes,
-        scratch_shapes=[pltpu.VMEM(g.shape, F32)],
+        scratch_shapes=[
+            pltpu.VMEM(w.shape, F32),
+            pltpu.VMEM(w.shape, BF16),
+            pltpu.VMEM(g.shape, F32),
+            pltpu.SemaphoreType.DMA((4,)),
+        ],
         compiler_params=params(16),
         cost_estimate=pl.CostEstimate(
             flops=2 * pairs * channels * PAIR_FEATURES,
             bytes_accessed=4 * pairs * channels,
             transcendentals=0,
         ),
-    )(we, g)
+    )(*[pltpu.with_memory_space_constraint(x, pltpu.HBM) for x in (a, b, w, g)])
 
 
 def join(pieces, axis, held):
-    half = lax.axis_size(axis) // 2
-    depth = pieces[0].shape[0] // half
+    depth = pieces[0].shape[0]
     me = lax.axis_index(axis)
-    odd, home = lax.rem(me, 2), lax.div(me, 2)
-    for piece, parity in zip(pieces, (odd, 1 - odd), strict=True):
-        block = piece[...].astype(F32)
-        for p in range(half):
-            place = (2 * lax.bitwise_xor(home, p) + parity) * depth
-            held[pl.ds(pl.multiple_of(place, depth), depth), :] = block[p * depth : (p + 1) * depth]
+    for p, piece in enumerate(pieces):
+        place = lax.bitwise_xor(me, p) * depth
+        held[pl.ds(pl.multiple_of(place, depth), depth), :] = piece[...].astype(F32)
 
 
 def repeat_matrix(sequences):
@@ -214,8 +185,8 @@
 
 def outer_kernel(i_n, j_n, *refs):
     depth = PROJECTED_DEPTH
-    row_n = lax.axis_size("row")
-    a_pieces, b_pieces, refs = refs[:2], refs[2:4], refs[4:]
+    row_n, col_n = lax.axis_size("row"), lax.axis_size("col")
+    a_pieces, b_pieces, refs = refs[:col_n], refs[col_n : col_n + row_n], refs[col_n + row_n :]
     g_ref, bias_ref, x_ref, a_held, b_wide = refs[:5]
     messages, (b_held, left, total) = refs[5 : 5 + row_n], refs[5 + row_n :]
     sequences = a_held.shape[0]
@@ -482,43 +453,41 @@
     return message
 
 
-def pair_sum(kept, near, after):
-    def kernel(*refs):
-        kept, near, (own, *messages) = refs[:count], refs[count], refs[count + 2 :]
-        size = own.shape[0]
-        for p, part in enumerate(kept):
-            both = part[...] + near[p * size : (p + 1) * size, :].astype(F32)
-            if p == 0:
-                own[...] = both
-            else:
-                messages[p - 1][...] = both.astype(BF16)
-
+def column_pair_sum(own, near, kept, grad_near, after, share):
+    rows = share + BIAS_ROWS
     count = len(kept)
-    shapes = [(kept[0].shape, F32)] + [(kept[0].shape, BF16)] * (count - 1)
-    own, *messages = call(kernel, [*kept, near], shapes, [after])
-    return own, messages
-
-
-def column_pair_sum(own, near, after, share):
-    def kernel(own, near, _, message):
+    size = kept[0].shape[0]
+
+    def kernel(own, near, grad_near, *refs):
+        kept, (_, grad_own), messages = refs[:count], refs[count : count + 2], refs[count + 2 :]
         total = own[0:share, :].astype(F32) + near[0:share, :].astype(F32)
-        message[0:share, :] = total.astype(BF16)
-        message[share:, :] = split(joined(own[share:, :]) + joined(near[share:, :]))
-
-    (message,) = call(kernel, [own, near], [(own.shape, BF16)], [after])
-    return message
-
-
-def column_sum(parts, grads, share):
+        bias = split(joined(own[share:, :]) + joined(near[share:, :]))
+        grad_own[...] = kept[0][...] + grad_near[0:size, :].astype(F32)
+        for p, message in enumerate(messages, 1):
+            message[0:share, :] = total.astype(BF16)
+            message[share:rows, :] = bias
+            part = kept[p][...] + grad_near[p * size : (p + 1) * size, :].astype(F32)
+            message[rows:, :] = part.astype(BF16)
+
+    shapes = [((size, LANES), F32)] + [((rows + size, LANES), BF16)] * (count - 1)
+    grad_own, *messages = call(kernel, [own, near, grad_near, *kept], shapes, [after])
+    return grad_own, messages
+
+
+def column_sum(own, parts, left_own, grads, share):
     rows = share + BIAS_ROWS
-    count, sent = len(parts), len(grads)
-
-    def kernel(*refs):
-        parts, grads, refs = refs[:count], refs[count : count + sent], refs[count + sent :]
-        messages, (piece_out, bias_out, held) = refs[:sent], refs[sent:]
+    count, sent = len(parts) + 1, len(grads)
+
+    def kernel(own, left_own, *refs):
+        parts, grads, refs = refs[: count - 1], refs[count - 1 : count - 1 + sent], refs[count - 1 + sent :]
+        messages, (piece_out, left_out, bias_out, held) = refs[:sent], refs[sent:]
         home = lax.div(lax.axis_index("col"), 2)
-        for p, part in enumerate(parts):
-            held[lax.bitwise_xor(home, p)] = part[...]
+        left = left_own[...]
+        for p, part in enumerate((own, *parts)):
+            held[lax.bitwise_xor(home, p)] = part[0:rows, :]
+            if p > 0:
+                left += part[rows:, :].astype(F32)
+        left_out[...] = left
         total, bias = held[0, 0:share, :].astype(F32), joined(held[0, share:, :])
         for n in range(1, count):
             total += held[n, 0:share, :].astype(F32)
@@ -531,19 +500,21 @@
         bias_out[...] = jnp.broadcast_to(bias, bias_out.shape)
 
     shapes = [((share + grad.shape[0], LANES), BF16) for grad in grads]
-    shapes += [((share, LANES), BF16), ((8, LANES), F32)]
+    shapes += [((share, LANES), BF16), (left_own.shape, F32), ((8, LANES), F32)]
     scratch = [pltpu.VMEM((count, rows, LANES), BF16)]
-    *messages, piece, bias = call(kernel, [*parts, *grads], shapes, scratch=scratch)
-    return messages, piece, bias
+    *messages, piece, left, bias = call(
+        kernel, [own, left_own, *parts, *grads], shapes, scratch=scratch
+    )
+    return messages, piece, left, bias
 
 
 def finish(pieces, left, right_own, bias, left_shape, right_shape, scale, bias_scale):
-    count, left_n = len(pieces), len(left)
+    count = len(pieces)
     share = pieces[0].shape[0]
 
     def kernel(*refs):
-        pieces, left, refs = refs[:count], refs[count : count + left_n], refs[count + left_n :]
-        right_own, bias, projection, left_out, right_out, bias_out = refs
+        pieces, refs = refs[:count], refs[count:]
+        left, right_own, bias, projection, left_out, right_out, bias_out = refs
         me = lax.axis_index("row")
         right_total = right_own[...]
         for p, piece in zip(partners(count), pieces, strict=True):
@@ -551,10 +522,7 @@
             projection[rows, :] = piece[0:share, :].astype(F32) * scale
             if p > 0:
                 right_total += piece[share:, :].astype(F32)
-        left_total = left[0][...]
-        for term in left[1:]:
-            left_total += term[...].astype(F32)
-        unfold(left_total, left_out.shape[0], left_out)
+        unfold(left[...], left_out.shape[0], left_out)
         unfold(right_total, right_out.shape[0], right_out)
         bias_out[...] = bias[0:1, :] * bias_scale
 
@@ -564,7 +532,7 @@
         (right_shape, F32),
         ((1, PAIR_FEATURES), F32),
     ]
-    return call(kernel, [*pieces, *left, right_own, bias], shapes)
+    return call(kernel, [*pieces, left, right_own, bias], shapes)
 
 
 def swap(x, axis, p):
@@ -574,10 +542,6 @@
 def swap_each(parts, axis, step=1):
     count = len(parts)
     return [swap(parts[n - 1], axis, n * step) for n in range(count, 0, -1)][::-1]
-
-
-def from_evens(x, axis):
-    return swap_each([x] * (lax.axis_size(axis) // 2 - 1), axis, 2)
 
 
 def local(
@@ -588,18 +552,20 @@
     sequences = second_homolog_features.shape[0] * row_n
     channels = final_projection_matrix.shape[0]
     res_total = i_n * row_n
-    a_far = from_evens(first_homolog_features, "col")
-    b_far = from_evens(second_homolog_features, "row")
-    we, wt, a, b, w, g = load(
+    gathered = {}
+    for axis, x in (("col", first_homolog_features), ("row", second_homolog_features)):
+        count = lax.axis_size(axis)
+        gathered[axis] = swap_each([x] * (count - 1), axis)
+    y, gt, wt, bias_rows, a, b, w, g = prepare(
         first_homolog_features,
         second_homolog_features,
         final_projection_matrix,
         cotangent.reshape(i_n * j_n, PAIR_FEATURES),
-    )
-    a, b = stack([a, *a_far], [b, *b_far])
-    a_pieces = [a, swap(a, "col", 1)]
-    b_pieces = [b, swap(b, "row", 1)]
-    y, gt, bias_rows = prepare(we, g, i_n, j_n)
+        i_n,
+        j_n,
+    )
+    a_pieces = [a] + gathered["col"]
+    b_pieces = [b] + gathered["row"]
 
     x, a_held, b_wide, (own, *messages) = outer(
         a_pieces, b_pieces, g, bias_rows, i_n, j_n, sequences
@@ -614,22 +580,19 @@
 
     message = row_sum(parts, message, share)
     near = swap(message, "col", 1)
-    left_own, left_messages = pair_sum(left_kept, left_near, message)
-    left = [left_own] + swap_each(left_messages, "col", 2)
-    y2, a_wide = product(w, gt, a_held, left_own)
-
-    message = column_pair_sum(message, near, y2, share)
-    parts = [message] + from_evens(message, "col")
+    y2, a_wide = product(w, gt, a_held, message)
+    left_own, messages = column_pair_sum(message, near, left_kept, left_near, y2, share)
+    parts = swap_each(messages, "col", 2)
     (right_own,), right_sent = gradient(
-        a_wide, y2, message, "row", alone(row_n), 1, row_n - 1, j_n, i_n, sequences
-    )
-
-    messages, piece, bias = column_sum(parts, right_sent, share)
+        a_wide, y2, left_own, "row", alone(row_n), 1, row_n - 1, j_n, i_n, sequences
+    )
+
+    messages, piece, left_own, bias = column_sum(messages[0], parts, left_own, right_sent, share)
     pieces = [piece] + swap_each(messages, "row")[::-1]
     pair_map = pair(x, wt, output_bias, piece, sequences)
     projection, left_grad, right_grad, bias_grad = finish(
         pieces,
-        left,
+        left_own,
         right_own,
         bias,
         first_homolog_features.shape,

time: 41.8 us -> 43 us (1.029)
  waiting for transfers between devices: 5.43 us -> 8.57 us
  starting transfers between devices: 17.4 us -> 16 us
  Pallas kernels: 18.1 us -> 17.5 us
    ppermute x14 -> x15, waiting for transfers between devices: 5.43 us -> 8.57 us  [swap(): lax.ppermute(x, axis, [(n, n ^ p) for n in range(lax.axis_size(axis))])]
    ppermute x14 -> x15, starting transfers between devices: 17.4 us -> 16 us  [swap(): lax.ppermute(x, axis, [(n, n ^ p) for n in range(lax.axis_size(axis))])]
    pallas_call x2 -> x1, Pallas kernels: 3.15 us -> 3.29 us  [prepare(): pl.pallas_call(functools.partial(prepare_kernel, i_n, j_n), in_specs=[pl....]
    pallas_call x6 -> x4, Pallas kernels: 1.01 us -> 1 us  [call(): pl.pallas_call(kernel, in_specs=specs, out_specs=[in_vmem()] * len(shapes...]
  transfers between devices with their start and end apart: 14 -> 15, of which waited for: 6 -> 7; matrix products, arithmetic and copies ran while one was open for 0% -> 0% of each run, Pallas kernels for 29% -> 27%
where the time goes in v13:
time: 43 us; the launch traced here: 42.8 us
  Pallas kernels  17.5 us (41%)
  starting transfers between devices  16 us (37%)
  waiting for transfers between devices  8.57 us (20%)
  between operations  0.73 us (2%)
    ppermute x15, starting transfers between devices, swap(): lax.ppermute(x, axis, [(n, n ^ p) for n in range(lax.axis_size(axis))])  16 us
    ppermute x15, waiting for transfers between devices, swap(): lax.ppermute(x, axis, [(n, n ^ p) for n in range(lax.axis_size(axis))])  8.57 us
    pallas_call x1, Pallas kernels, outer(): pl.pallas_call(functools.partial(outer_kernel, i_n, j_n), in_specs=[in_vm...  4.78 us
    pallas_call x2, Pallas kernels, gradient(): pl.pallas_call(functools.partial(gradient_kernel, axis, plan, kept, posit...  4.3 us
    pallas_call x1, Pallas kernels, prepare(): pl.pallas_call(functools.partial(prepare_kernel, i_n, j_n), in_specs=[pl....  3.29 us
    pallas_call x1, Pallas kernels, pair(): pl.pallas_call(functools.partial(pair_kernel, sequences), grid=(count,),...  2.54 us
    pallas_call x1, Pallas kernels, product(): pl.pallas_call(product_kernel, in_specs=[in_vmem()] * 3 + [pl.BlockSpec(m...  1.64 us
    pallas_call x4, Pallas kernels, call(): pl.pallas_call(kernel, in_specs=specs, out_specs=[in_vmem()] * len(shapes...  1 us
  transfers between devices with their start and end apart: 15, of which 7 were waited for; matrix products, arithmetic and copies ran while one was open for 0% of the time, Pallas kernels for 27%

profile of v13, /device:TPU:0, one launch (start us, length us, event | category | flops | bytes accessed | tf_op | source)
XLA Modules:
  0.0 42.8 jit_solution(8680417973346039474)
XLA Ops:
  0.6 3.1 %collective-permute-start = (bf16[8,1536]{1,0:T(8,128)(2,1)}, bf16[8,1536]{1,0:T(8,128)(2,1)S(1)}, u32[]{:S(2)}, u32[]{:S(2)}) collective-permute-start(bf16[8,1536]{1,0:T(8,128)(2,1)} %a_hbm.1), channel_id=1, source_target_pairs={{0,1},{1,0},{2,3},{3,2},{4,5},{5,4},{6,7},{7,6},{8,9},{9,8},{10,11... | collective-permute-start | bytes 73736 | tf_op jit(solution)/shard_map/ppermute | solution.py:539
  3.7 2.5 %collective-permute-start.2 = (bf16[8,1536]{1,0:T(8,128)(2,1)}, bf16[8,1536]{1,0:T(8,128)(2,1)S(1)}, u32[]{:S(2)}, u32[]{:S(2)}) collective-permute-start(bf16[8,1536]{1,0:T(8,128)(2,1)} %a_hbm.1), channel_id=1, source_target_pairs={{0,3},{1,2},{2,1},{3,0},{4,7},{5,6},{6,5},{7,4},{8,11},{9,10},{10,... | collective-permute-start | bytes 73736 | tf_op jit(solution)/shard_map/ppermute | solution.py:539
  6.2 0.1 collective-permute-start.1
  6.3 1.6 %collective-permute-start.5 = (bf16[8,1536]{1,0:T(8,128)(2,1)}, bf16[8,1536]{1,0:T(8,128)(2,1)S(1)}, u32[]{:S(2)}, u32[]{:S(2)}) collective-permute-start(bf16[8,1536]{1,0:T(8,128)(2,1)} %b_hbm.1), channel_id=1, source_target_pairs={{0,12},{4,8},{8,4},{12,0},{1,13},{5,9},{9,5},{13,1},{2,14},{6,10},... | collective-permute-start | bytes 73736 | tf_op jit(solution)/shard_map/ppermute | solution.py:539
  7.9 0.5 %collective-permute-start.4 = (bf16[8,1536]{1,0:T(8,128)(2,1)}, bf16[8,1536]{1,0:T(8,128)(2,1)S(1)}, u32[]{:S(2)}, u32[]{:S(2)}) collective-permute-start(bf16[8,1536]{1,0:T(8,128)(2,1)} %b_hbm.1), channel_id=1, source_target_pairs={{0,8},{4,12},{8,0},{12,4},{1,9},{5,13},{9,1},{13,5},{2,10},{6,14},... | collective-permute-start | bytes 73736 | tf_op jit(solution)/shard_map/ppermute | solution.py:539
  8.5 3.3 %shard_map.92 = (bf16[1024,2304]{1,0:T(8,128)(2,1)S(1)}, bf16[2304,128]{1,0:T(8,128)(2,1)S(1)}, bf16[128,1024]{1,0:T(8,128)(2,1)S(1)}, bf16[16,128]{1,0:T(8,128)...) custom-call(bf16[8,1536]{1,0:T(8,128)(2,1)} %a_hbm.1, ...), custom_call_target="tpu_custom_call" | custom-call | flops 603979776 | bytes 9437184 | tf_op jit(solution)/shard_map/pallas_call | solution.py:96
  11.8 0.0 collective-permute-done.2.refs_3_
  11.8 0.0 collective-permute-done.1.refs_2_
  11.8 0.0 collective-permute-done.5.refs_7_
  11.8 0.2 collective-permute-done.4.refs_6_
  12.0 4.8 %shard_map.93 = (bf16[1024,2304]{1,0:T(8,128)(2,1)S(1)}, f32[32,1536]{1,0:T(8,128)S(1)}, f32[2,1536,128]{2,1,0:T(8,128)S(1)}, f32[272,128]{1,0:T(8,128)S(1)}, bf...) custom-call(bf16[8,1536]{1,0:T(8,128)(2,1)S(1)} %get-tuple-element.41.refs_0_, ...), custom_call_target="tpu_custom_call" | custom-call | flops 1207959552 | bytes 4718592 | tf_op jit(solution)/shard_map/pallas_call | solution.py:254
  16.7 0.7 %collective-permute-start.6 = (bf16[272,128]{1,0:T(8,128)(2,1)S(1)}, bf16[272,128]{1,0:T(8,128)(2,1)S(1)}, u32[]{:S(2)}, u32[]{:S(2)}) collective-permute-start(bf16[272,128]{1,0:T(8,128)(2,1)S(1)} %get-tuple-element.48), channel_id=1, source_target_pairs={{0,12},{4,8},{8,4},{12,0},{1,13},{5,9},{9,5},{13,1},{2,14},{6,10},... | collective-permute-start | bytes 208904 | tf_op jit(solution)/shard_map/ppermute | solution.py:539
  17.5 0.8 %collective-permute-start.7 = (bf16[272,128]{1,0:T(8,128)(2,1)S(1)}, bf16[272,128]{1,0:T(8,128)(2,1)S(1)}, u32[]{:S(2)}, u32[]{:S(2)}) collective-permute-start(bf16[272,128]{1,0:T(8,128)(2,1)S(1)} %get-tuple-element.49), channel_id=1, source_target_pairs={{0,8},{4,12},{8,0},{12,4},{1,9},{5,13},{9,1},{13,5},{2,10},{6,14},... | collective-permute-start | bytes 208904 | tf_op jit(solution)/shard_map/ppermute | solution.py:539
  18.2 0.4 %collective-permute-start.8 = (bf16[272,128]{1,0:T(8,128)(2,1)S(1)}, bf16[272,128]{1,0:T(8,128)(2,1)S(1)}, u32[]{:S(2)}, u32[]{:S(2)}) collective-permute-start(bf16[272,128]{1,0:T(8,128)(2,1)S(1)} %get-tuple-element.50), channel_id=1, source_target_pairs={{0,4},{4,0},{8,12},{12,8},{1,5},{5,1},{9,13},{13,9},{2,6},{6,2},{1... | collective-permute-start | bytes 208904 | tf_op jit(solution)/shard_map/ppermute | solution.py:539
  18.7 2.1 %shard_map.94 = (f32[96,128]{1,0:T(8,128)S(1)}, f32[96,128]{1,0:T(8,128)S(1)}, bf16[192,128]{1,0:T(8,128)(2,1)S(1)}) custom-call(f32[2,1536,128]{2,1,0:T(8,128)S(1)} %get-tuple-element.51.refs_0_, bf16[1024,2304]{1,0:T(8,128)(2,1)S(1)} %get-tuple-element.52.refs_1_, f32[272,128]{1,0:T(8,128)S(1)} %get-tuple-element.47.refs_2_.refs_0_), custom_call_target="tpu_custom_call" | custom-call | flops 603979776 | bytes 4718592 | tf_op jit(solution)/shard_map/pallas_call | solution.py:342
  20.8 0.5 %collective-permute-done.6.refs_1_ = bf16[272,128]{1,0:T(8,128)(2,1)S(1)} collective-permute-done((bf16[272,128]{1,0:T(8,128)(2,1)S(1)}, bf16[272,128]{1,0:T(8,128)(2,1)S(1)}, u32[]{:S(2)}, u32[]{:S(2)}) %collective-permute-start.6) | collective-permute-done | bytes 69664 | tf_op jit(solution)/shard_map/ppermute | solution.py:539
  21.3 1.3 %collective-permute-done.7.refs_2_ = bf16[272,128]{1,0:T(8,128)(2,1)S(1)} collective-permute-done((bf16[272,128]{1,0:T(8,128)(2,1)S(1)}, bf16[272,128]{1,0:T(8,128)(2,1)S(1)}, u32[]{:S(2)}, u32[]{:S(2)}) %collective-permute-start.7) | collective-permute-done | bytes 69664 | tf_op jit(solution)/shard_map/ppermute | solution.py:539
  22.6 1.8 %collective-permute-start.9 = (bf16[272,128]{1,0:T(8,128)(2,1)S(1)}, bf16[272,128]{1,0:T(8,128)(2,1)S(1)}, u32[]{:S(2)}, u32[]{:S(2)}) collective-permute-start(bf16[272,128]{1,0:T(8,128)(2,1)S(1)} %shard_map.95._.own), channel_id=1, source_target_pairs={{0,1},{1,0},{2,3},{3,2},{4,5},{5,4},{6,7},{7,6},{8,9},{9,8},{10,11... | collective-permute-start | bytes 208904 | tf_op jit(solution)/shard_map/ppermute | solution.py:539
  24.5 0.2 collective-permute-start.10
  24.7 1.6 %shard_map.96 = (bf16[1024,2304]{1,0:T(8,128)(2,1)S(1)}, f32[2,1536,128]{2,1,0:T(8,128)S(1)}) custom-call(bf16[1024,128]{1,0:T(8,128)(2,1)S(1)} %get-tuple-element.56.left_ref, bf16[2304,128]{1,0:T(8,128)(2,1)S(1)} %get-tuple-element.57.right_ref, f32[32,1536]{1,0:T(8,128)S(1)} %get-tuple-element.58.held, bf16[272,128]{1,0:T(8,128)(2,1)S(1)} %shard_map.95._.own), custom_call_target="tpu_custom_call" | custom-call | flops 603979776 | bytes 9437184 | tf_op jit(solution)/shard_map/pallas_call | solution.py:370
  26.4 2.2 %collective-permute-done.10.grad_near = bf16[192,128]{1,0:T(8,128)(2,1)S(1)} collective-permute-done((bf16[192,128]{1,0:T(8,128)(2,1)S(1)}, bf16[192,128]{1,0:T(8,128)(2,1)S(1)}, u32[]{:S(2)}, u32[]{:S(2)}) %collective-permute-start.10) | collective-permute-done | bytes 49184 | tf_op jit(solution)/shard_map/ppermute | solution.py:539
  28.6 2.2 %collective-permute-start.11 = (bf16[368,128]{1,0:T(8,128)(2,1)S(1)}, bf16[368,128]{1,0:T(8,128)(2,1)S(1)}, u32[]{:S(2)}, u32[]{:S(2)}) collective-permute-start(bf16[368,128]{1,0:T(8,128)(2,1)S(1)} %get-tuple-element.60.own), channel_id=1, source_target_pairs={{0,2},{1,3},{2,0},{3,1},{4,6},{5,7},{6,4},{7,5},{8,10},{9,11},{10,... | collective-permute-start | bytes 282632 | tf_op jit(solution)/shard_map/ppermute | solution.py:539
  30.9 2.2 %shard_map.98 = (f32[96,128]{1,0:T(8,128)S(1)}, bf16[96,128]{1,0:T(8,128)(2,1)S(1)}, bf16[96,128]{1,0:T(8,128)(2,1)S(1)}, bf16[96,128]{1,0:T(8,128)(2,1)S(1)}) custom-call(f32[2,1536,128]{2,1,0:T(8,128)S(1)} %get-tuple-element.62.refs_0_, bf16[1024,2304]{1,0:T(8,128)(2,1)S(1)} %get-tuple-element.59.refs_2_.refs_1_, ...), custom_call_target="tpu_custom_call" | custom-call | flops 603979776 | bytes 4718592 | tf_op jit(solution)/shard_map/pallas_call | solution.py:342
  33.0 2.2 %collective-permute-done.11.refs_0_ = bf16[368,128]{1,0:T(8,128)(2,1)S(1)} collective-permute-done((bf16[368,128]{1,0:T(8,128)(2,1)S(1)}, bf16[368,128]{1,0:T(8,128)(2,1)S(1)}, u32[]{:S(2)}, u32[]{:S(2)}) %collective-permute-start.11) | collective-permute-done | bytes 94240 | tf_op jit(solution)/shard_map/ppermute | solution.py:539
  35.2 0.1 shard_map.99
  35.2 0.1 collective-permute-start.12
  35.3 1.4 %collective-permute-start.13 = (bf16[352,128]{1,0:T(8,128)(2,1)S(1)}, bf16[352,128]{1,0:T(8,128)(2,1)S(1)}, u32[]{:S(2)}, u32[]{:S(2)}) collective-permute-start(bf16[352,128]{1,0:T(8,128)(2,1)S(1)} %get-tuple-element.68), channel_id=1, source_target_pairs={{0,8},{4,12},{8,0},{12,4},{1,9},{5,13},{9,1},{13,5},{2,10},{6,14},... | collective-permute-start | bytes 270344 | tf_op jit(solution)/shard_map/ppermute | solution.py:539
  36.7 0.4 collective-permute-start.14
  37.2 2.5 %shard_map.100 = bf16[2304,128]{1,0:T(8,128)(2,1)} custom-call(bf16[1024,2304]{1,0:T(8,128)(2,1)S(1)} %get-tuple-element.45.x_ref, bf16[128,1024]{1,0:T(8,128)(2,1)S(1)} %get-tuple-element.46.wt_ref, f32[1,128]{1,0:T(1,128)S(1)} %bitcast.4, bf16[256,128]{1,0:T(8,128)(2,1)S(1)} %get-tuple-element.66._.refs_0_), custom_call_target="tpu_custom_call" | custom-call | flops 1207959552 | bytes 4718592 | tf_op jit(solution)/shard_map/pallas_call | solution.py:393
  39.7 0.5 %collective-permute-done.12.refs_1_ = bf16[352,128]{1,0:T(8,128)(2,1)S(1)} collective-permute-done((bf16[352,128]{1,0:T(8,128)(2,1)S(1)}, bf16[352,128]{1,0:T(8,128)(2,1)S(1)}, u32[]{:S(2)}, u32[]{:S(2)}) %collective-permute-start.12) | collective-permute-done | bytes 90144 | tf_op jit(solution)/shard_map/ppermute | solution.py:539
  40.2 1.7 %collective-permute-done.13.refs_2_ = bf16[352,128]{1,0:T(8,128)(2,1)S(1)} collective-permute-done((bf16[352,128]{1,0:T(8,128)(2,1)S(1)}, bf16[352,128]{1,0:T(8,128)(2,1)S(1)}, u32[]{:S(2)}, u32[]{:S(2)}) %collective-permute-start.13) | collective-permute-done | bytes 90144 | tf_op jit(solution)/shard_map/ppermute | solution.py:539
  42.0 0.9 %shard_map.101 = (f32[1024,128]{1,0:T(8,128)}, f32[8,1536]{1,0:T(8,128)}, f32[8,1536]{1,0:T(8,128)}, f32[1,128]{1,0:T(1,128)}) custom-call(bf16[256,128]{1,0:T(8,128)(2,1)S(1)} %get-tuple-element.66._.refs_0_, bf16[352,128]{1,0:T(8,128)(2,1)S(1)} %collective-permute-done.12.refs_1_, bf16[352,128]{1,0:T(8,128)(2,1)S(1)} %collective-permute-done.13.refs_2_, ...), custom_call_target="tpu_custom_call" | custom-call | tf_op jit(solution)/shard_map/pallas_call | solution.py:420
  (10 shorter events, 0.1 us)
Async XLA Ops:
  0.6 7.3 %collective-permute-start = (bf16[8,1536]{1,0:T(8,128)(2,1)}, bf16[8,1536]{1,0:T(8,128)(2,1)S(1)}, u32[]{:S(2)}, u32[]{:S(2)}) collective-permute-start(bf16[8,1536]{1,0:T(8,128)(2,1)} %a_hbm.1), channel_id=1, source_target_pairs={{0,1},{1,0},{2,3},{3,2},{4,5},{5,4},{6,7},{7,6},{8,9},{9,8},{10,11... | collective-permute-start | bytes 73736 | tf_op jit(solution)/shard_map/ppermute | solution.py:539
  3.7 8.0 %collective-permute-start.2 = (bf16[8,1536]{1,0:T(8,128)(2,1)}, bf16[8,1536]{1,0:T(8,128)(2,1)S(1)}, u32[]{:S(2)}, u32[]{:S(2)}) collective-permute-start(bf16[8,1536]{1,0:T(8,128)(2,1)} %a_hbm.1), channel_id=1, source_target_pairs={{0,3},{1,2},{2,1},{3,0},{4,7},{5,6},{6,5},{7,4},{8,11},{9,10},{10,... | collective-permute-start | bytes 73736 | tf_op jit(solution)/shard_map/ppermute | solution.py:539
  6.2 5.6 %collective-permute-start.1 = (bf16[8,1536]{1,0:T(8,128)(2,1)}, bf16[8,1536]{1,0:T(8,128)(2,1)S(1)}, u32[]{:S(2)}, u32[]{:S(2)}) collective-permute-start(bf16[8,1536]{1,0:T(8,128)(2,1)} %a_hbm.1), channel_id=1, source_target_pairs={{0,2},{1,3},{2,0},{3,1},{4,6},{5,7},{6,4},{7,5},{8,10},{9,11},{10,... | collective-permute-start | bytes 73736 | tf_op jit(solution)/shard_map/ppermute | solution.py:539
  6.3 5.5 %collective-permute-start.3 = (bf16[8,1536]{1,0:T(8,128)(2,1)}, bf16[8,1536]{1,0:T(8,128)(2,1)S(1)}, u32[]{:S(2)}, u32[]{:S(2)}) collective-permute-start(bf16[8,1536]{1,0:T(8,128)(2,1)} %b_hbm.1), channel_id=1, source_target_pairs={{0,4},{4,0},{8,12},{12,8},{1,5},{5,1},{9,13},{13,9},{2,6},{6,2},{1... | collective-permute-start | bytes 73736 | tf_op jit(solution)/shard_map/ppermute | solution.py:539
  6.3 5.5 %collective-permute-start.5 = (bf16[8,1536]{1,0:T(8,128)(2,1)}, bf16[8,1536]{1,0:T(8,128)(2,1)S(1)}, u32[]{:S(2)}, u32[]{:S(2)}) collective-permute-start(bf16[8,1536]{1,0:T(8,128)(2,1)} %b_hbm.1), channel_id=1, source_target_pairs={{0,12},{4,8},{8,4},{12,0},{1,13},{5,9},{9,5},{13,1},{2,14},{6,10},... | collective-permute-start | bytes 73736 | tf_op jit(solution)/shard_map/ppermute | solution.py:539
  7.9 4.0 %collective-permute-start.4 = (bf16[8,1536]{1,0:T(8,128)(2,1)}, bf16[8,1536]{1,0:T(8,128)(2,1)S(1)}, u32[]{:S(2)}, u32[]{:S(2)}) collective-permute-start(bf16[8,1536]{1,0:T(8,128)(2,1)} %b_hbm.1), channel_id=1, source_target_pairs={{0,8},{4,12},{8,0},{12,4},{1,9},{5,13},{9,1},{13,5},{2,10},{6,14},... | collective-permute-start | bytes 73736 | tf_op jit(solution)/shard_map/ppermute | solution.py:539
  16.7 4.5 %collective-permute-start.6 = (bf16[272,128]{1,0:T(8,128)(2,1)S(1)}, bf16[272,128]{1,0:T(8,128)(2,1)S(1)}, u32[]{:S(2)}, u32[]{:S(2)}) collective-permute-start(bf16[272,128]{1,0:T(8,128)(2,1)S(1)} %get-tuple-element.48), channel_id=1, source_target_pairs={{0,12},{4,8},{8,4},{12,0},{1,13},{5,9},{9,5},{13,1},{2,14},{6,10},... | collective-permute-start | bytes 208904 | tf_op jit(solution)/shard_map/ppermute | solution.py:539
  17.5 5.1 %collective-permute-start.7 = (bf16[272,128]{1,0:T(8,128)(2,1)S(1)}, bf16[272,128]{1,0:T(8,128)(2,1)S(1)}, u32[]{:S(2)}, u32[]{:S(2)}) collective-permute-start(bf16[272,128]{1,0:T(8,128)(2,1)S(1)} %get-tuple-element.49), channel_id=1, source_target_pairs={{0,8},{4,12},{8,0},{12,4},{1,9},{5,13},{9,1},{13,5},{2,10},{6,14},... | collective-permute-start | bytes 208904 | tf_op jit(solution)/shard_map/ppermute | solution.py:539
  18.2 4.4 %collective-permute-start.8 = (bf16[272,128]{1,0:T(8,128)(2,1)S(1)}, bf16[272,128]{1,0:T(8,128)(2,1)S(1)}, u32[]{:S(2)}, u32[]{:S(2)}) collective-permute-start(bf16[272,128]{1,0:T(8,128)(2,1)S(1)} %get-tuple-element.50), channel_id=1, source_target_pairs={{0,4},{4,0},{8,12},{12,8},{1,5},{5,1},{9,13},{13,9},{2,6},{6,2},{1... | collective-permute-start | bytes 208904 | tf_op jit(solution)/shard_map/ppermute | solution.py:539
  22.6 5.9 %collective-permute-start.9 = (bf16[272,128]{1,0:T(8,128)(2,1)S(1)}, bf16[272,128]{1,0:T(8,128)(2,1)S(1)}, u32[]{:S(2)}, u32[]{:S(2)}) collective-permute-start(bf16[272,128]{1,0:T(8,128)(2,1)S(1)} %shard_map.95._.own), channel_id=1, source_target_pairs={{0,1},{1,0},{2,3},{3,2},{4,5},{5,4},{6,7},{7,6},{8,9},{9,8},{10,11... | collective-permute-start | bytes 208904 | tf_op jit(solution)/shard_map/ppermute | solution.py:539
  24.5 4.1 %collective-permute-start.10 = (bf16[192,128]{1,0:T(8,128)(2,1)S(1)}, bf16[192,128]{1,0:T(8,128)(2,1)S(1)}, u32[]{:S(2)}, u32[]{:S(2)}) collective-permute-start(bf16[192,128]{1,0:T(8,128)(2,1)S(1)} %get-tuple-element.53.refs_4_), channel_id=1, source_target_pairs={{0,1},{1,0},{2,3},{3,2},{4,5},{5,4},{6,7},{7,6},{8,9},{9,8},{10,11... | collective-permute-start | bytes 147464 | tf_op jit(solution)/shard_map/ppermute | solution.py:539
  28.6 8.6 %copy-start = (f32[128]{0:T(128)S(1)}, f32[128]{0:T(128)}, u32[]{:S(2)}) copy-start(f32[128]{0:T(128)} %param.8) | copy-start | bytes 1540
  28.6 6.5 %collective-permute-start.11 = (bf16[368,128]{1,0:T(8,128)(2,1)S(1)}, bf16[368,128]{1,0:T(8,128)(2,1)S(1)}, u32[]{:S(2)}, u32[]{:S(2)}) collective-permute-start(bf16[368,128]{1,0:T(8,128)(2,1)S(1)} %get-tuple-element.60.own), channel_id=1, source_target_pairs={{0,2},{1,3},{2,0},{3,1},{4,6},{5,7},{6,4},{7,5},{8,10},{9,11},{10,... | collective-permute-start | bytes 282632 | tf_op jit(solution)/shard_map/ppermute | solution.py:539
  35.2 5.0 %collective-permute-start.12 = (bf16[352,128]{1,0:T(8,128)(2,1)S(1)}, bf16[352,128]{1,0:T(8,128)(2,1)S(1)}, u32[]{:S(2)}, u32[]{:S(2)}) collective-permute-start(bf16[352,128]{1,0:T(8,128)(2,1)S(1)} %get-tuple-element.67), channel_id=1, source_target_pairs={{0,12},{4,8},{8,4},{12,0},{1,13},{5,9},{9,5},{13,1},{2,14},{6,10},... | collective-permute-start | bytes 270344 | tf_op jit(solution)/shard_map/ppermute | solution.py:539
  35.3 6.7 %collective-permute-start.13 = (bf16[352,128]{1,0:T(8,128)(2,1)S(1)}, bf16[352,128]{1,0:T(8,128)(2,1)S(1)}, u32[]{:S(2)}, u32[]{:S(2)}) collective-permute-start(bf16[352,128]{1,0:T(8,128)(2,1)S(1)} %get-tuple-element.68), channel_id=1, source_target_pairs={{0,8},{4,12},{8,0},{12,4},{1,9},{5,13},{9,1},{13,5},{2,10},{6,14},... | collective-permute-start | bytes 270344 | tf_op jit(solution)/shard_map/ppermute | solution.py:539
  36.7 5.2 %collective-permute-start.14 = (bf16[352,128]{1,0:T(8,128)(2,1)S(1)}, bf16[352,128]{1,0:T(8,128)(2,1)S(1)}, u32[]{:S(2)}, u32[]{:S(2)}) collective-permute-start(bf16[352,128]{1,0:T(8,128)(2,1)S(1)} %get-tuple-element.69), channel_id=1, source_target_pairs={{0,4},{4,0},{8,12},{12,8},{1,5},{5,1},{9,13},{13,9},{2,6},{6,2},{1... | collective-permute-start | bytes 270344 | tf_op jit(solution)/shard_map/ppermute | solution.py:539

commit v14 on v12

--- a/solution.py
+++ b/solution.py
@@ -11,7 +11,7 @@
 PAIR_FEATURES = 128
 GROUP = 8
 MULTIPLY_ROWS = 384
-CHUNKS = 1
+CHUNKS = 2
 BIAS_ROWS = 16
 LANES = 128
 F32 = jnp.float32
@@ -157,8 +157,13 @@
     return (lax.rem(lane, sequences) == row).astype(BF16)
 
 
+def tile_count(sequences):
+    return GROUP * sequences // LANES, max(1, sequences // LANES)
+
+
 def spread(held, wide):
-    both = dot(held[...].T.astype(BF16), repeat_matrix(held.shape[0]))
+    repeated = repeat_matrix(held.shape[0])[:, : wide.shape[0] * LANES]
+    both = dot(held[...].T.astype(BF16), repeated)
     for l in range(wide.shape[0]):
         wide[l] = both[:, l * LANES : (l + 1) * LANES]
 
@@ -181,8 +186,12 @@
 
 def diagonal_of(wide, channel, positions, sequences):
     columns = []
-    for l in range(wide.shape[0]):
-        block = wide[l, pl.ds(channel, positions, stride=PROJECTED_DEPTH), :].astype(BF16)
+    blocks = [
+        wide[l, pl.ds(channel, positions, stride=PROJECTED_DEPTH), :].astype(BF16)
+        for l in range(wide.shape[0])
+    ]
+    for l in range(tile_count(sequences)[0]):
+        block = blocks[l % len(blocks)]
         members = dict(tiles_of(sequences, l))
         columns.append(
             jnp.concatenate(
@@ -269,7 +278,7 @@
     depth = PROJECTED_DEPTH
     channels = depth * depth
     pairs = i_n * j_n
-    tiles = GROUP * sequences // LANES
+    tiles = tile_count(sequences)[1]
     operands = [*a_pieces, *b_pieces, g, bias_rows]
     shapes = [jax.ShapeDtypeStruct((channels, pairs), BF16)]
     shapes += [
@@ -395,7 +404,7 @@
 
 def product(left, right, held, after):
     shape = (left.shape[0], right.shape[0])
-    spread_shape = (GROUP * held.shape[0] // LANES, held.shape[1], LANES)
+    spread_shape = (tile_count(held.shape[0])[1], held.shape[1], LANES)
     return pl.pallas_call(
         product_kernel,
         in_specs=[in_vmem()] * 3 + [pl.BlockSpec(memory_space=pl.ANY)],

time: 41.8 us -> 41.4 us (level)
  Pallas kernels: 18.1 us -> 17 us
    pallas_call x2, Pallas kernels: 4.67 us -> 4.12 us  [gradient(): pl.pallas_call(functools.partial(gradient_kernel, axis, plan, kept, posit...]
    pallas_call x1, Pallas kernels: 5.08 us -> 4.66 us  [outer(): pl.pallas_call(functools.partial(outer_kernel, i_n, j_n), in_specs=[in_vm...]
  transfers between devices with their start and end apart: 14 -> 14, of which waited for: 6 -> 7; matrix products, arithmetic and copies ran while one was open for 0% -> 0% of each run, Pallas kernels for 29% -> 28%
where the time goes in v14:
time: 41.4 us; the launch traced here: 41.2 us
  starting transfers between devices  17.8 us (43%)
  Pallas kernels  17 us (41%)
  waiting for transfers between devices  5.68 us (14%)
  between operations  0.72 us (2%)
    ppermute x14, starting transfers between devices, swap(): lax.ppermute(x, axis, [(n, n ^ p) for n in range(lax.axis_size(axis))])  17.8 us
    ppermute x14, waiting for transfers between devices, swap(): lax.ppermute(x, axis, [(n, n ^ p) for n in range(lax.axis_size(axis))])  5.68 us
    pallas_call x1, Pallas kernels, outer(): pl.pallas_call(functools.partial(outer_kernel, i_n, j_n), in_specs=[in_vm...  4.66 us
    pallas_call x2, Pallas kernels, gradient(): pl.pallas_call(functools.partial(gradient_kernel, axis, plan, kept, posit...  4.12 us
    pallas_call x1, Pallas kernels, pair(): pl.pallas_call(functools.partial(pair_kernel, sequences), grid=(count,),...  2.55 us
    pallas_call x1, Pallas kernels, prepare(): pl.pallas_call(functools.partial(prepare_kernel, i_n, j_n), in_specs=[in_...  1.75 us
    pallas_call x1, Pallas kernels, product(): pl.pallas_call(product_kernel, in_specs=[in_vmem()] * 3 + [pl.BlockSpec(m...  1.55 us
    pallas_call x1, Pallas kernels, load(): pl.pallas_call(load_kernel, in_specs=[pl.BlockSpec(memory_space=pltpu.HBM...  1.39 us
  transfers between devices with their start and end apart: 14, of which 7 were waited for; matrix products, arithmetic and copies ran while one was open for 0% of the time, Pallas kernels for 28%

profile of v14, /device:TPU:0, one launch (start us, length us, event | category | flops | bytes accessed | tf_op | source)
XLA Modules:
  0.0 41.2 jit_solution(9212048160391300686)
XLA Ops:
  0.6 4.1 %collective-permute-start = (bf16[8,1536]{1,0:T(8,128)(2,1)}, bf16[8,1536]{1,0:T(8,128)(2,1)S(1)}, u32[]{:S(2)}, u32[]{:S(2)}) collective-permute-start(bf16[8,1536]{1,0:T(8,128)(2,1)} %a_hbm.1), channel_id=1, source_target_pairs={{0,2},{1,3},{2,0},{3,1},{4,6},{5,7},{6,4},{7,5},{8,10},{9,11},{10,... | collective-permute-start | bytes 73736 | tf_op jit(solution)/shard_map/ppermute | solution.py:580
  4.7 1.5 %collective-permute-start.1 = (bf16[8,1536]{1,0:T(8,128)(2,1)}, bf16[8,1536]{1,0:T(8,128)(2,1)S(1)}, u32[]{:S(2)}, u32[]{:S(2)}) collective-permute-start(bf16[8,1536]{1,0:T(8,128)(2,1)} %b_hbm.1), channel_id=1, source_target_pairs={{0,8},{4,12},{8,0},{12,4},{1,9},{5,13},{9,1},{13,5},{2,10},{6,14},... | collective-permute-start | bytes 73736 | tf_op jit(solution)/shard_map/ppermute | solution.py:580
  6.2 1.4 %shard_map.92 = (bf16[1024,128]{1,0:T(8,128)(2,1)S(1)}, bf16[128,1024]{1,0:T(8,128)(2,1)S(1)}, bf16[8,1536]{1,0:T(8,128)(2,1)S(1)}, bf16[8,1536]{1,0:T(8,128)(2,...) custom-call(bf16[8,1536]{1,0:T(8,128)(2,1)} %a_hbm.1, bf16[8,1536]{1,0:T(8,128)(2,1)} %b_hbm.1, ...), custom_call_target="tpu_custom_call" | custom-call | flops 131072000 | bytes 2097152 | tf_op jit(solution)/shard_map/pallas_call | solution.py:67
  7.6 1.1 %collective-permute-done.1.refs_3_ = bf16[8,1536]{1,0:T(8,128)(2,1)S(1)} collective-permute-done((bf16[8,1536]{1,0:T(8,128)(2,1)}, bf16[8,1536]{1,0:T(8,128)(2,1)S(1)}, u32[]{:S(2)}, u32[]{:S(2)}) %collective-permute-start.1) | collective-permute-done | bytes 24608 | tf_op jit(solution)/shard_map/ppermute | solution.py:580
  8.8 1.6 %collective-permute-start.2 = (bf16[16,1536]{1,0:T(8,128)(2,1)S(1)}, bf16[16,1536]{1,0:T(8,128)(2,1)S(1)}, u32[]{:S(2)}, u32[]{:S(2)}) collective-permute-start(bf16[16,1536]{1,0:T(8,128)(2,1)S(1)} %get-tuple-element.45.refs_0_), channel_id=1, source_target_pairs={{0,1},{1,0},{2,3},{3,2},{4,5},{5,4},{6,7},{7,6},{8,9},{9,8},{10,11... | collective-permute-start | bytes 147464 | tf_op jit(solution)/shard_map/ppermute | solution.py:580
  10.4 1.8 %shard_map.94 = (bf16[1024,2304]{1,0:T(8,128)(2,1)S(1)}, bf16[2304,128]{1,0:T(8,128)(2,1)S(1)}, bf16[16,128]{1,0:T(8,128)(2,1)S(1)}) custom-call(bf16[1024,128]{1,0:T(8,128)(2,1)S(1)} %get-tuple-element.48.we_ref, bf16[2304,128]{1,0:T(8,128)(2,1)S(1)} %get-tuple-element.47.g_ref.refs_4_), custom_call_target="tpu_custom_call" | custom-call | flops 603979776 | bytes 9437184 | tf_op jit(solution)/shard_map/pallas_call | solution.py:126
  12.2 0.8 %collective-permute-done.2.refs_1_ = bf16[16,1536]{1,0:T(8,128)(2,1)S(1)} collective-permute-done((bf16[16,1536]{1,0:T(8,128)(2,1)S(1)}, bf16[16,1536]{1,0:T(8,128)(2,1)S(1)}, u32[]{:S(2)}, u32[]{:S(2)}) %collective-permute-start.2) | collective-permute-done | bytes 49184 | tf_op jit(solution)/shard_map/ppermute | solution.py:580
  12.9 4.7 %shard_map.95 = (bf16[1024,2304]{1,0:T(8,128)(2,1)S(1)}, f32[32,1536]{1,0:T(8,128)S(1)}, f32[1,1536,128]{2,1,0:T(8,128)S(1)}, f32[272,128]{1,0:T(8,128)S(1)}, bf...) custom-call(bf16[16,1536]{1,0:T(8,128)(2,1)S(1)} %get-tuple-element.45.refs_0_, ...), custom_call_target="tpu_custom_call" | custom-call | flops 1207959552 | bytes 4718592 | tf_op jit(solution)/shard_map/pallas_call | solution.py:292
  17.6 0.9 %collective-permute-start.4 = (bf16[272,128]{1,0:T(8,128)(2,1)S(1)}, bf16[272,128]{1,0:T(8,128)(2,1)S(1)}, u32[]{:S(2)}, u32[]{:S(2)}) collective-permute-start(bf16[272,128]{1,0:T(8,128)(2,1)S(1)} %get-tuple-element.53), channel_id=1, source_target_pairs={{0,12},{4,8},{8,4},{12,0},{1,13},{5,9},{9,5},{13,1},{2,14},{6,10},... | collective-permute-start | bytes 208904 | tf_op jit(solution)/shard_map/ppermute | solution.py:580
  18.6 0.7 %collective-permute-start.5 = (bf16[272,128]{1,0:T(8,128)(2,1)S(1)}, bf16[272,128]{1,0:T(8,128)(2,1)S(1)}, u32[]{:S(2)}, u32[]{:S(2)}) collective-permute-start(bf16[272,128]{1,0:T(8,128)(2,1)S(1)} %get-tuple-element.54), channel_id=1, source_target_pairs={{0,8},{4,12},{8,0},{12,4},{1,9},{5,13},{9,1},{13,5},{2,10},{6,14},... | collective-permute-start | bytes 208904 | tf_op jit(solution)/shard_map/ppermute | solution.py:580
  19.2 0.3 collective-permute-start.6
  19.5 2.1 %shard_map.96 = (f32[96,128]{1,0:T(8,128)S(1)}, f32[96,128]{1,0:T(8,128)S(1)}, bf16[192,128]{1,0:T(8,128)(2,1)S(1)}) custom-call(f32[1,1536,128]{2,1,0:T(8,128)S(1)} %get-tuple-element.56.refs_0_, bf16[1024,2304]{1,0:T(8,128)(2,1)S(1)} %get-tuple-element.57.refs_1_, f32[272,128]{1,0:T(8,128)S(1)} %get-tuple-element.52.refs_2_.refs_0_), custom_call_target="tpu_custom_call" | custom-call | flops 603979776 | bytes 4718592 | tf_op jit(solution)/shard_map/pallas_call | solution.py:380
  21.6 1.6 %collective-permute-start.8 = (bf16[192,128]{1,0:T(8,128)(2,1)S(1)}, bf16[192,128]{1,0:T(8,128)(2,1)S(1)}, u32[]{:S(2)}, u32[]{:S(2)}) collective-permute-start(bf16[192,128]{1,0:T(8,128)(2,1)S(1)} %get-tuple-element.58.refs_4_), channel_id=1, source_target_pairs={{0,1},{1,0},{2,3},{3,2},{4,5},{5,4},{6,7},{7,6},{8,9},{9,8},{10,11... | collective-permute-start | bytes 147464 | tf_op jit(solution)/shard_map/ppermute | solution.py:580
  23.2 0.0 collective-permute-done.4.refs_1_
  23.3 0.4 collective-permute-done.5.refs_2_
  23.6 0.0 collective-permute-done.6.refs_3_
  23.7 1.6 %collective-permute-start.7 = (bf16[272,128]{1,0:T(8,128)(2,1)S(1)}, bf16[272,128]{1,0:T(8,128)(2,1)S(1)}, u32[]{:S(2)}, u32[]{:S(2)}) collective-permute-start(bf16[272,128]{1,0:T(8,128)(2,1)S(1)} %shard_map.97.refs_3_.own), channel_id=1, source_target_pairs={{0,1},{1,0},{2,3},{3,2},{4,5},{5,4},{6,7},{7,6},{8,9},{9,8},{10,11... | collective-permute-start | bytes 208904 | tf_op jit(solution)/shard_map/ppermute | solution.py:580
  25.3 0.4 %collective-permute-done.8.refs_2_ = bf16[192,128]{1,0:T(8,128)(2,1)S(1)} collective-permute-done((bf16[192,128]{1,0:T(8,128)(2,1)S(1)}, bf16[192,128]{1,0:T(8,128)(2,1)S(1)}, u32[]{:S(2)}, u32[]{:S(2)}) %collective-permute-start.8) | collective-permute-done | bytes 49184 | tf_op jit(solution)/shard_map/ppermute | solution.py:580
  25.8 1.5 %shard_map.99 = (bf16[1024,2304]{1,0:T(8,128)(2,1)S(1)}, f32[1,1536,128]{2,1,0:T(8,128)S(1)}) custom-call(bf16[1024,128]{1,0:T(8,128)(2,1)S(1)} %get-tuple-element.59.left_ref, bf16[2304,128]{1,0:T(8,128)(2,1)S(1)} %get-tuple-element.60.right_ref, f32[32,1536]{1,0:T(8,128)S(1)} %get-tuple-element.61.held, f32[96,128]{1,0:T(8,128)S(1)} %get-tuple-element.64._.refs_4_), custom_call_target="tpu_custom_call" | custom-call | flops 603979776 | bytes 9437184 | tf_op jit(solution)/shard_map/pallas_call | solution.py:408
  27.3 0.7 %collective-permute-done.7.near = bf16[272,128]{1,0:T(8,128)(2,1)S(1)} collective-permute-done((bf16[272,128]{1,0:T(8,128)(2,1)S(1)}, bf16[272,128]{1,0:T(8,128)(2,1)S(1)}, u32[]{:S(2)}, u32[]{:S(2)}) %collective-permute-start.7) | collective-permute-done | bytes 69664 | tf_op jit(solution)/shard_map/ppermute | solution.py:580
  28.1 1.0 %collective-permute-start.9 = (bf16[272,128]{1,0:T(8,128)(2,1)S(1)}, bf16[272,128]{1,0:T(8,128)(2,1)S(1)}, u32[]{:S(2)}, u32[]{:S(2)}) collective-permute-start(bf16[272,128]{1,0:T(8,128)(2,1)S(1)} %shard_map.100.refs_2_.refs_0_), channel_id=1, source_target_pairs={{0,2},{1,3},{2,0},{3,1},{4,6},{5,7},{6,4},{7,5},{8,10},{9,11},{10,... | collective-permute-start | bytes 208904 | tf_op jit(solution)/shard_map/ppermute | solution.py:580
  29.1 2.0 %collective-permute-start.13 = (bf16[96,128]{1,0:T(8,128)(2,1)S(1)}, bf16[96,128]{1,0:T(8,128)(2,1)S(1)}, u32[]{:S(2)}, u32[]{:S(2)}) collective-permute-start(bf16[96,128]{1,0:T(8,128)(2,1)S(1)} %get-tuple-element.74), channel_id=1, source_target_pairs={{0,2},{1,3},{2,0},{3,1},{4,6},{5,7},{6,4},{7,5},{8,10},{9,11},{10,... | collective-permute-start | bytes 73736 | tf_op jit(solution)/shard_map/ppermute | solution.py:580
  31.1 2.1 %shard_map.101 = (f32[96,128]{1,0:T(8,128)S(1)}, bf16[96,128]{1,0:T(8,128)(2,1)S(1)}, bf16[96,128]{1,0:T(8,128)(2,1)S(1)}, bf16[96,128]{1,0:T(8,128)(2,1)S(1)}) custom-call(f32[1,1536,128]{2,1,0:T(8,128)S(1)} %get-tuple-element.66.refs_0_, bf16[1024,2304]{1,0:T(8,128)(2,1)S(1)} %get-tuple-element.65._.refs_1_, bf16[272,128]{1,0:T(8,128)(2,1)S(1)} %shard_map.100.refs_2_.refs_0_), custom_call_target="tpu_custom_call" | custom-call | flops 603979776 | bytes 4718592 | tf_op jit(solution)/shard_map/pallas_call | solution.py:380
  33.2 0.2 collective-permute-done.9.refs_1_
  33.4 0.1 shard_map.102
  33.4 0.1 collective-permute-start.10
  33.5 2.2 %collective-permute-start.11 = (bf16[352,128]{1,0:T(8,128)(2,1)S(1)}, bf16[352,128]{1,0:T(8,128)(2,1)S(1)}, u32[]{:S(2)}, u32[]{:S(2)}) collective-permute-start(bf16[352,128]{1,0:T(8,128)(2,1)S(1)} %get-tuple-element.72), channel_id=1, source_target_pairs={{0,8},{4,12},{8,0},{12,4},{1,9},{5,13},{9,1},{13,5},{2,10},{6,14},... | collective-permute-start | bytes 270344 | tf_op jit(solution)/shard_map/ppermute | solution.py:580
  35.8 0.0 collective-permute-start.12
  35.8 2.5 %shard_map.103 = bf16[2304,128]{1,0:T(8,128)(2,1)} custom-call(bf16[1024,2304]{1,0:T(8,128)(2,1)S(1)} %get-tuple-element.50.x_ref, bf16[128,1024]{1,0:T(8,128)(2,1)S(1)} %get-tuple-element.51.wt_ref, f32[1,128]{1,0:T(1,128)S(1)} %bitcast.4, bf16[256,128]{1,0:T(8,128)(2,1)S(1)} %get-tuple-element.70._.refs_0_), custom_call_target="tpu_custom_call" | custom-call | flops 1207959552 | bytes 4718592 | tf_op jit(solution)/shard_map/pallas_call | solution.py:431
  38.3 0.0 collective-permute-done.13.refs_5_
  38.4 2.0 %collective-permute-done.11.refs_2_ = bf16[352,128]{1,0:T(8,128)(2,1)S(1)} collective-permute-done((bf16[352,128]{1,0:T(8,128)(2,1)S(1)}, bf16[352,128]{1,0:T(8,128)(2,1)S(1)}, u32[]{:S(2)}, u32[]{:S(2)}) %collective-permute-start.11) | collective-permute-done | bytes 90144 | tf_op jit(solution)/shard_map/ppermute | solution.py:580
  40.4 0.9 %shard_map.104 = (f32[1024,128]{1,0:T(8,128)}, f32[8,1536]{1,0:T(8,128)}, f32[8,1536]{1,0:T(8,128)}, f32[1,128]{1,0:T(1,128)}) custom-call(bf16[256,128]{1,0:T(8,128)(2,1)S(1)} %get-tuple-element.70._.refs_0_, bf16[352,128]{1,0:T(8,128)(2,1)S(1)} %collective-permute-done.10.refs_1_, bf16[352,128]{1,0:T(8,128)(2,1)S(1)} %collective-permute-done.11.refs_2_, ...), custom_call_target="tpu_custom_call" | custom-call | tf_op jit(solution)/shard_map/pallas_call | solution.py:458
  (11 shorter events, 0.1 us)
Async XLA Ops:
  0.6 7.0 %collective-permute-start = (bf16[8,1536]{1,0:T(8,128)(2,1)}, bf16[8,1536]{1,0:T(8,128)(2,1)S(1)}, u32[]{:S(2)}, u32[]{:S(2)}) collective-permute-start(bf16[8,1536]{1,0:T(8,128)(2,1)} %a_hbm.1), channel_id=1, source_target_pairs={{0,2},{1,3},{2,0},{3,1},{4,6},{5,7},{6,4},{7,5},{8,10},{9,11},{10,... | collective-permute-start | bytes 73736 | tf_op jit(solution)/shard_map/ppermute | solution.py:580
  4.7 4.0 %collective-permute-start.1 = (bf16[8,1536]{1,0:T(8,128)(2,1)}, bf16[8,1536]{1,0:T(8,128)(2,1)S(1)}, u32[]{:S(2)}, u32[]{:S(2)}) collective-permute-start(bf16[8,1536]{1,0:T(8,128)(2,1)} %b_hbm.1), channel_id=1, source_target_pairs={{0,8},{4,12},{8,0},{12,4},{1,9},{5,13},{9,1},{13,5},{2,10},{6,14},... | collective-permute-start | bytes 73736 | tf_op jit(solution)/shard_map/ppermute | solution.py:580
  8.8 4.2 %collective-permute-start.2 = (bf16[16,1536]{1,0:T(8,128)(2,1)S(1)}, bf16[16,1536]{1,0:T(8,128)(2,1)S(1)}, u32[]{:S(2)}, u32[]{:S(2)}) collective-permute-start(bf16[16,1536]{1,0:T(8,128)(2,1)S(1)} %get-tuple-element.45.refs_0_), channel_id=1, source_target_pairs={{0,1},{1,0},{2,3},{3,2},{4,5},{5,4},{6,7},{7,6},{8,9},{9,8},{10,11... | collective-permute-start | bytes 147464 | tf_op jit(solution)/shard_map/ppermute | solution.py:580
  10.4 2.5 %collective-permute-start.3 = (bf16[16,1536]{1,0:T(8,128)(2,1)S(1)}, bf16[16,1536]{1,0:T(8,128)(2,1)S(1)}, u32[]{:S(2)}, u32[]{:S(2)}) collective-permute-start(bf16[16,1536]{1,0:T(8,128)(2,1)S(1)} %get-tuple-element.46.refs_2_), channel_id=1, source_target_pairs={{0,4},{4,0},{8,12},{12,8},{1,5},{5,1},{9,13},{13,9},{2,6},{6,2},{1... | collective-permute-start | bytes 147464 | tf_op jit(solution)/shard_map/ppermute | solution.py:580
  17.6 5.6 %collective-permute-start.4 = (bf16[272,128]{1,0:T(8,128)(2,1)S(1)}, bf16[272,128]{1,0:T(8,128)(2,1)S(1)}, u32[]{:S(2)}, u32[]{:S(2)}) collective-permute-start(bf16[272,128]{1,0:T(8,128)(2,1)S(1)} %get-tuple-element.53), channel_id=1, source_target_pairs={{0,12},{4,8},{8,4},{12,0},{1,13},{5,9},{9,5},{13,1},{2,14},{6,10},... | collective-permute-start | bytes 208904 | tf_op jit(solution)/shard_map/ppermute | solution.py:580
  18.6 5.1 %collective-permute-start.5 = (bf16[272,128]{1,0:T(8,128)(2,1)S(1)}, bf16[272,128]{1,0:T(8,128)(2,1)S(1)}, u32[]{:S(2)}, u32[]{:S(2)}) collective-permute-start(bf16[272,128]{1,0:T(8,128)(2,1)S(1)} %get-tuple-element.54), channel_id=1, source_target_pairs={{0,8},{4,12},{8,0},{12,4},{1,9},{5,13},{9,1},{13,5},{2,10},{6,14},... | collective-permute-start | bytes 208904 | tf_op jit(solution)/shard_map/ppermute | solution.py:580
  19.2 4.4 %collective-permute-start.6 = (bf16[272,128]{1,0:T(8,128)(2,1)S(1)}, bf16[272,128]{1,0:T(8,128)(2,1)S(1)}, u32[]{:S(2)}, u32[]{:S(2)}) collective-permute-start(bf16[272,128]{1,0:T(8,128)(2,1)S(1)} %get-tuple-element.55), channel_id=1, source_target_pairs={{0,4},{4,0},{8,12},{12,8},{1,5},{5,1},{9,13},{13,9},{2,6},{6,2},{1... | collective-permute-start | bytes 208904 | tf_op jit(solution)/shard_map/ppermute | solution.py:580
  21.6 4.2 %collective-permute-start.8 = (bf16[192,128]{1,0:T(8,128)(2,1)S(1)}, bf16[192,128]{1,0:T(8,128)(2,1)S(1)}, u32[]{:S(2)}, u32[]{:S(2)}) collective-permute-start(bf16[192,128]{1,0:T(8,128)(2,1)S(1)} %get-tuple-element.58.refs_4_), channel_id=1, source_target_pairs={{0,1},{1,0},{2,3},{3,2},{4,5},{5,4},{6,7},{7,6},{8,9},{9,8},{10,11... | collective-permute-start | bytes 147464 | tf_op jit(solution)/shard_map/ppermute | solution.py:580
  23.7 4.4 %collective-permute-start.7 = (bf16[272,128]{1,0:T(8,128)(2,1)S(1)}, bf16[272,128]{1,0:T(8,128)(2,1)S(1)}, u32[]{:S(2)}, u32[]{:S(2)}) collective-permute-start(bf16[272,128]{1,0:T(8,128)(2,1)S(1)} %shard_map.97.refs_3_.own), channel_id=1, source_target_pairs={{0,1},{1,0},{2,3},{3,2},{4,5},{5,4},{6,7},{7,6},{8,9},{9,8},{10,11... | collective-permute-start | bytes 208904 | tf_op jit(solution)/shard_map/ppermute | solution.py:580
  28.1 7.7 %copy-start = (f32[128]{0:T(128)S(1)}, f32[128]{0:T(128)}, u32[]{:S(2)}) copy-start(f32[128]{0:T(128)} %param.8) | copy-start | bytes 1540
  28.1 5.3 %collective-permute-start.9 = (bf16[272,128]{1,0:T(8,128)(2,1)S(1)}, bf16[272,128]{1,0:T(8,128)(2,1)S(1)}, u32[]{:S(2)}, u32[]{:S(2)}) collective-permute-start(bf16[272,128]{1,0:T(8,128)(2,1)S(1)} %shard_map.100.refs_2_.refs_0_), channel_id=1, source_target_pairs={{0,2},{1,3},{2,0},{3,1},{4,6},{5,7},{6,4},{7,5},{8,10},{9,11},{10,... | collective-permute-start | bytes 208904 | tf_op jit(solution)/shard_map/ppermute | solution.py:580
  29.1 9.3 %collective-permute-start.13 = (bf16[96,128]{1,0:T(8,128)(2,1)S(1)}, bf16[96,128]{1,0:T(8,128)(2,1)S(1)}, u32[]{:S(2)}, u32[]{:S(2)}) collective-permute-start(bf16[96,128]{1,0:T(8,128)(2,1)S(1)} %get-tuple-element.74), channel_id=1, source_target_pairs={{0,2},{1,3},{2,0},{3,1},{4,6},{5,7},{6,4},{7,5},{8,10},{9,11},{10,... | collective-permute-start | bytes 73736 | tf_op jit(solution)/shard_map/ppermute | solution.py:580
  33.4 4.9 %collective-permute-start.10 = (bf16[352,128]{1,0:T(8,128)(2,1)S(1)}, bf16[352,128]{1,0:T(8,128)(2,1)S(1)}, u32[]{:S(2)}, u32[]{:S(2)}) collective-permute-start(bf16[352,128]{1,0:T(8,128)(2,1)S(1)} %get-tuple-element.71), channel_id=1, source_target_pairs={{0,12},{4,8},{8,4},{12,0},{1,13},{5,9},{9,5},{13,1},{2,14},{6,10},... | collective-permute-start | bytes 270344 | tf_op jit(solution)/shard_map/ppermute | solution.py:580
  33.5 6.8 %collective-permute-start.11 = (bf16[352,128]{1,0:T(8,128)(2,1)S(1)}, bf16[352,128]{1,0:T(8,128)(2,1)S(1)}, u32[]{:S(2)}, u32[]{:S(2)}) collective-permute-start(bf16[352,128]{1,0:T(8,128)(2,1)S(1)} %get-tuple-element.72), channel_id=1, source_target_pairs={{0,8},{4,12},{8,0},{12,4},{1,9},{5,13},{9,1},{13,5},{2,10},{6,14},... | collective-permute-start | bytes 270344 | tf_op jit(solution)/shard_map/ppermute | solution.py:580
  35.8 4.6 %collective-permute-start.12 = (bf16[352,128]{1,0:T(8,128)(2,1)S(1)}, bf16[352,128]{1,0:T(8,128)(2,1)S(1)}, u32[]{:S(2)}, u32[]{:S(2)}) collective-permute-start(bf16[352,128]{1,0:T(8,128)(2,1)S(1)} %get-tuple-element.73), channel_id=1, source_target_pairs={{0,4},{4,0},{8,12},{12,8},{1,5},{5,1},{9,13},{13,9},{2,6},{6,2},{1... | collective-permute-start | bytes 270344 | tf_op jit(solution)/shard_map/ppermute | solution.py:580

commit v15 on v14

--- a/solution.py
+++ b/solution.py
@@ -11,6 +11,7 @@
 PAIR_FEATURES = 128
 GROUP = 8
 MULTIPLY_ROWS = 384
+PAIR_BLOCKS = 3
 CHUNKS = 2
 BIAS_ROWS = 16
 LANES = 128
@@ -419,33 +420,41 @@
     )(left, right, held, after)
 
 
-def pair_kernel(sequences, x_ref, wt_ref, bias_ref, _, out_ref):
+def pair_kernel(sequences, x_ref, wt_ref, bias_ref, _after, *refs):
+    out_ref, done_ref = refs[-2:]
+    done_ref[...] = jnp.zeros(done_ref.shape, F32)
     product = dot(wt_ref[...], x_ref[...])
     out_ref[...] = (product.T * (1.0 / sequences) + bias_ref[...]).astype(BF16)
 
 
-def pair(x, wt, output_bias, after, sequences):
+def pair(x, wt, output_bias, after, sequences, first, last, before=None):
     channels, pairs = x.shape
-    count = 3
-    size = pairs // count
+    size = pairs // PAIR_BLOCKS
+    anywhere = pl.BlockSpec(memory_space=pl.ANY)
+    done = jax.ShapeDtypeStruct((8, LANES), F32)
     return pl.pallas_call(
         functools.partial(pair_kernel, sequences),
-        grid=(count,),
+        grid=(last - first,),
         in_specs=[
-            pl.BlockSpec((channels, size), lambda t: (0, t)),
+            pl.BlockSpec((channels, size), lambda t: (0, t + first)),
             whole(wt.shape),
             whole((1, PAIR_FEATURES)),
-            pl.BlockSpec(memory_space=pl.ANY),
+            anywhere,
+        ]
+        + [anywhere] * (before is not None),
+        out_specs=[
+            pl.BlockSpec((size, PAIR_FEATURES), lambda t: (t + first, 0)),
+            whole(done.shape),
         ],
-        out_specs=pl.BlockSpec((size, PAIR_FEATURES), lambda t: (t, 0)),
-        out_shape=jax.ShapeDtypeStruct((pairs, PAIR_FEATURES), BF16),
+        out_shape=[jax.ShapeDtypeStruct((pairs, PAIR_FEATURES), BF16), done],
+        input_output_aliases={} if before is None else {4: 0},
         compiler_params=params(),
         cost_estimate=pl.CostEstimate(
-            flops=4 * pairs * channels * PAIR_FEATURES,
-            bytes_accessed=2 * pairs * channels,
+            flops=(last - first) * size * channels * PAIR_FEATURES,
+            bytes_accessed=2 * (last - first) * size * channels,
             transcendentals=0,
         ),
-    )(x, wt, output_bias.reshape(1, PAIR_FEATURES), after)
+    )(x, wt, output_bias.reshape(1, PAIR_FEATURES), after, *([] if before is None else [before]))
 
 
 def unfold(total, share, out):
@@ -491,23 +500,6 @@
     return message
 
 
-def pair_sum(kept, near, after):
-    def kernel(*refs):
-        kept, near, (own, *messages) = refs[:count], refs[count], refs[count + 2 :]
-        size = own.shape[0]
-        for p, part in enumerate(kept):
-            both = part[...] + near[p * size : (p + 1) * size, :].astype(F32)
-            if p == 0:
-                own[...] = both
-            else:
-                messages[p - 1][...] = both.astype(BF16)
-
-    count = len(kept)
-    shapes = [(kept[0].shape, F32)] + [(kept[0].shape, BF16)] * (count - 1)
-    own, *messages = call(kernel, [*kept, near], shapes, [after])
-    return own, messages
-
-
 def column_pair_sum(own, near, after, share):
     def kernel(own, near, _, message):
         total = own[0:share, :].astype(F32) + near[0:share, :].astype(F32)
@@ -518,13 +510,14 @@
     return message
 
 
-def column_sum(parts, grads, share):
+def column_sum(parts, grads, kept, near, share):
     rows = share + BIAS_ROWS
-    count, sent = len(parts), len(grads)
-
-    def kernel(*refs):
+    count, sent, kept_n = len(parts), len(grads), len(kept)
+
+    def kernel(near, *refs):
         parts, grads, refs = refs[:count], refs[count : count + sent], refs[count + sent :]
-        messages, (piece_out, bias_out, held) = refs[:sent], refs[sent:]
+        kept, refs = refs[:kept_n], refs[kept_n:]
+        messages, (piece_out, bias_out, left_own, *left_messages, held) = refs[:sent], refs[sent:]
         home = lax.div(lax.axis_index("col"), 2)
         for p, part in enumerate(parts):
             held[lax.bitwise_xor(home, p)] = part[...]
@@ -538,12 +531,28 @@
             message[0:share, :] = piece
             message[share:, :] = grad[...]
         bias_out[...] = jnp.broadcast_to(bias, bias_out.shape)
+        size = left_own.shape[0]
+        for p, part in enumerate(kept):
+            both = part[...] + near[p * size : (p + 1) * size, :].astype(F32)
+            if p == 0:
+                left_own[...] = both
+            else:
+                left_messages[p - 1][...] = both.astype(BF16)
 
     shapes = [((share + grad.shape[0], LANES), BF16) for grad in grads]
-    shapes += [((share, LANES), BF16), ((8, LANES), F32)]
+    shapes += [((share, LANES), BF16), ((8, LANES), F32), (kept[0].shape, F32)]
+    shapes += [(kept[0].shape, BF16)] * (kept_n - 1)
     scratch = [pltpu.VMEM((count, rows, LANES), BF16)]
-    *messages, piece, bias = call(kernel, [*parts, *grads], shapes, scratch=scratch)
-    return messages, piece, bias
+    results = call(kernel, [near, *parts, *grads, *kept], shapes, scratch=scratch)
+    return results[:sent], *results[sent : sent + 3], results[sent + 3 :]
+
+
+def hand_on(arrays, after):
+    def kernel(*refs):
+        for ref, out in zip(refs[: len(arrays)], refs[len(arrays) + 1 :], strict=True):
+            out[...] = ref[...]
+
+    return call(kernel, arrays, [(x.shape, x.dtype) for x in arrays], [after])
 
 
 def finish(pieces, left, right_own, bias, left_shape, right_shape, scale, bias_scale):
@@ -623,9 +632,7 @@
 
     message = row_sum(parts, message, share)
     near = swap(message, "col", 1)
-    left_own, left_messages = pair_sum(left_kept, left_near, message)
-    left = [left_own] + swap_each(left_messages, "col", 2)
-    y2, a_wide = product(w, gt, a_held, left_own)
+    y2, a_wide = product(w, gt, a_held, left_near)
 
     message = column_pair_sum(message, near, y2, share)
     parts = [message] + from_evens(message, "col")
@@ -633,9 +640,13 @@
         a_wide, y2, message, "row", alone(row_n), 1, row_n - 1, j_n, i_n, sequences
     )
 
-    messages, piece, bias = column_sum(parts, right_sent, share)
+    messages, piece, bias, left_own, left_messages = column_sum(
+        parts, right_sent, left_kept, left_near, share
+    )
     pieces = [piece] + swap_each(messages, "row")[::-1]
-    pair_map = pair(x, wt, output_bias, piece, sequences)
+    pair_map, pair_done = pair(x, wt, output_bias, piece, sequences, 0, 1)
+    left = [left_own] + swap_each(hand_on(left_messages, pair_done), "col", 2)
+    pair_map, _ = pair(x, wt, output_bias, pair_done, sequences, 1, PAIR_BLOCKS, pair_map)
     projection, left_grad, right_grad, bias_grad = finish(
         pieces,
         left,

time: 41.4 us -> 42.7 us (1.031)
  waiting for transfers between devices: 5.68 us -> 8.02 us
  starting transfers between devices: 17.8 us -> 16.3 us
  Pallas kernels: 17 us -> 17.5 us
    ppermute x14, waiting for transfers between devices: 5.68 us -> 8.02 us  [swap(): lax.ppermute(x, axis, [(n, n ^ p) for n in range(lax.axis_size(axis))])]
    ppermute x14, starting transfers between devices: 17.8 us -> 16.3 us  [swap(): lax.ppermute(x, axis, [(n, n ^ p) for n in range(lax.axis_size(axis))])]
    pallas_call x1 -> x2, Pallas kernels: 2.55 us -> 3.04 us  [pair(): pl.pallas_call(functools.partial(pair_kernel, sequences), grid=(last - fi...]
where the time goes in v15:
time: 42.7 us; the launch traced here: 42.6 us
  Pallas kernels  17.5 us (41%)
  starting transfers between devices  16.3 us (38%)
  waiting for transfers between devices  8.02 us (19%)
  between operations  0.72 us (2%)
    ppermute x14, starting transfers between devices, swap(): lax.ppermute(x, axis, [(n, n ^ p) for n in range(lax.axis_size(axis))])  16.3 us
    ppermute x14, waiting for transfers between devices, swap(): lax.ppermute(x, axis, [(n, n ^ p) for n in range(lax.axis_size(axis))])  8.02 us
    pallas_call x1, Pallas kernels, outer(): pl.pallas_call(functools.partial(outer_kernel, i_n, j_n), in_specs=[in_vm...  4.66 us
    pallas_call x2, Pallas kernels, gradient(): pl.pallas_call(functools.partial(gradient_kernel, axis, plan, kept, posit...  4.13 us
    pallas_call x2, Pallas kernels, pair(): pl.pallas_call(functools.partial(pair_kernel, sequences), grid=(last - fi...  3.04 us
    pallas_call x1, Pallas kernels, prepare(): pl.pallas_call(functools.partial(prepare_kernel, i_n, j_n), in_specs=[in_...  1.75 us
    pallas_call x1, Pallas kernels, product(): pl.pallas_call(product_kernel, in_specs=[in_vmem()] * 3 + [pl.BlockSpec(m...  1.55 us
    pallas_call x1, Pallas kernels, load(): pl.pallas_call(load_kernel, in_specs=[pl.BlockSpec(memory_space=pltpu.HBM...  1.39 us
  transfers between devices with their start and end apart: 14, of which 7 were waited for; matrix products, arithmetic and copies ran while one was open for 0% of the time, Pallas kernels for 28%

profile of v15, /device:TPU:0, one launch (start us, length us, event | category | flops | bytes accessed | tf_op | source)
XLA Modules:
  0.0 42.6 jit_solution(515268564978645620)
XLA Ops:
  0.6 4.1 %collective-permute-start = (bf16[8,1536]{1,0:T(8,128)(2,1)}, bf16[8,1536]{1,0:T(8,128)(2,1)S(1)}, u32[]{:S(2)}, u32[]{:S(2)}) collective-permute-start(bf16[8,1536]{1,0:T(8,128)(2,1)} %a_hbm.1), channel_id=1, source_target_pairs={{0,2},{1,3},{2,0},{3,1},{4,6},{5,7},{6,4},{7,5},{8,10},{9,11},{10,... | collective-permute-start | bytes 73736 | tf_op jit(solution)/shard_map/ppermute | solution.py:589
  4.7 1.5 %collective-permute-start.1 = (bf16[8,1536]{1,0:T(8,128)(2,1)}, bf16[8,1536]{1,0:T(8,128)(2,1)S(1)}, u32[]{:S(2)}, u32[]{:S(2)}) collective-permute-start(bf16[8,1536]{1,0:T(8,128)(2,1)} %b_hbm.1), channel_id=1, source_target_pairs={{0,8},{4,12},{8,0},{12,4},{1,9},{5,13},{9,1},{13,5},{2,10},{6,14},... | collective-permute-start | bytes 73736 | tf_op jit(solution)/shard_map/ppermute | solution.py:589
  6.2 1.4 %shard_map.92 = (bf16[1024,128]{1,0:T(8,128)(2,1)S(1)}, bf16[128,1024]{1,0:T(8,128)(2,1)S(1)}, bf16[8,1536]{1,0:T(8,128)(2,1)S(1)}, bf16[8,1536]{1,0:T(8,128)(2,...) custom-call(bf16[8,1536]{1,0:T(8,128)(2,1)} %a_hbm.1, bf16[8,1536]{1,0:T(8,128)(2,1)} %b_hbm.1, ...), custom_call_target="tpu_custom_call" | custom-call | flops 131072000 | bytes 2097152 | tf_op jit(solution)/shard_map/pallas_call | solution.py:68
  7.6 0.0 collective-permute-done.refs_1_
  7.6 1.1 %collective-permute-done.1.refs_3_ = bf16[8,1536]{1,0:T(8,128)(2,1)S(1)} collective-permute-done((bf16[8,1536]{1,0:T(8,128)(2,1)}, bf16[8,1536]{1,0:T(8,128)(2,1)S(1)}, u32[]{:S(2)}, u32[]{:S(2)}) %collective-permute-start.1) | collective-permute-done | bytes 24608 | tf_op jit(solution)/shard_map/ppermute | solution.py:589
  8.8 1.6 %collective-permute-start.2 = (bf16[16,1536]{1,0:T(8,128)(2,1)S(1)}, bf16[16,1536]{1,0:T(8,128)(2,1)S(1)}, u32[]{:S(2)}, u32[]{:S(2)}) collective-permute-start(bf16[16,1536]{1,0:T(8,128)(2,1)S(1)} %get-tuple-element.48.refs_0_), channel_id=1, source_target_pairs={{0,1},{1,0},{2,3},{3,2},{4,5},{5,4},{6,7},{7,6},{8,9},{9,8},{10,11... | collective-permute-start | bytes 147464 | tf_op jit(solution)/shard_map/ppermute | solution.py:589
  10.4 1.7 %shard_map.94 = (bf16[1024,2304]{1,0:T(8,128)(2,1)S(1)}, bf16[2304,128]{1,0:T(8,128)(2,1)S(1)}, bf16[16,128]{1,0:T(8,128)(2,1)S(1)}) custom-call(bf16[1024,128]{1,0:T(8,128)(2,1)S(1)} %get-tuple-element.51.we_ref, bf16[2304,128]{1,0:T(8,128)(2,1)S(1)} %get-tuple-element.50.g_ref.refs_4_), custom_call_target="tpu_custom_call" | custom-call | flops 603979776 | bytes 9437184 | tf_op jit(solution)/shard_map/pallas_call | solution.py:127
  12.2 0.8 %collective-permute-done.2.refs_1_ = bf16[16,1536]{1,0:T(8,128)(2,1)S(1)} collective-permute-done((bf16[16,1536]{1,0:T(8,128)(2,1)S(1)}, bf16[16,1536]{1,0:T(8,128)(2,1)S(1)}, u32[]{:S(2)}, u32[]{:S(2)}) %collective-permute-start.2) | collective-permute-done | bytes 49184 | tf_op jit(solution)/shard_map/ppermute | solution.py:589
  12.9 0.0 collective-permute-done.3.refs_3_
  12.9 4.7 %shard_map.95 = (bf16[1024,2304]{1,0:T(8,128)(2,1)S(1)}, f32[32,1536]{1,0:T(8,128)S(1)}, f32[1,1536,128]{2,1,0:T(8,128)S(1)}, f32[272,128]{1,0:T(8,128)S(1)}, bf...) custom-call(bf16[16,1536]{1,0:T(8,128)(2,1)S(1)} %get-tuple-element.48.refs_0_, ...), custom_call_target="tpu_custom_call" | custom-call | flops 1207959552 | bytes 4718592 | tf_op jit(solution)/shard_map/pallas_call | solution.py:293
  17.6 0.9 %collective-permute-start.5 = (bf16[272,128]{1,0:T(8,128)(2,1)S(1)}, bf16[272,128]{1,0:T(8,128)(2,1)S(1)}, u32[]{:S(2)}, u32[]{:S(2)}) collective-permute-start(bf16[272,128]{1,0:T(8,128)(2,1)S(1)} %get-tuple-element.59), channel_id=1, source_target_pairs={{0,12},{4,8},{8,4},{12,0},{1,13},{5,9},{9,5},{13,1},{2,14},{6,10},... | collective-permute-start | bytes 208904 | tf_op jit(solution)/shard_map/ppermute | solution.py:589
  18.5 0.7 %collective-permute-start.6 = (bf16[272,128]{1,0:T(8,128)(2,1)S(1)}, bf16[272,128]{1,0:T(8,128)(2,1)S(1)}, u32[]{:S(2)}, u32[]{:S(2)}) collective-permute-start(bf16[272,128]{1,0:T(8,128)(2,1)S(1)} %get-tuple-element.60), channel_id=1, source_target_pairs={{0,8},{4,12},{8,0},{12,4},{1,9},{5,13},{9,1},{13,5},{2,10},{6,14},... | collective-permute-start | bytes 208904 | tf_op jit(solution)/shard_map/ppermute | solution.py:589
  19.2 0.3 collective-permute-start.7
  19.5 2.1 %shard_map.96 = (f32[96,128]{1,0:T(8,128)S(1)}, f32[96,128]{1,0:T(8,128)S(1)}, bf16[192,128]{1,0:T(8,128)(2,1)S(1)}) custom-call(f32[1,1536,128]{2,1,0:T(8,128)S(1)} %get-tuple-element.55.refs_0_, bf16[1024,2304]{1,0:T(8,128)(2,1)S(1)} %get-tuple-element.56.refs_1_, f32[272,128]{1,0:T(8,128)S(1)} %get-tuple-element.57.refs_2_.refs_0_), custom_call_target="tpu_custom_call" | custom-call | flops 603979776 | bytes 4718592 | tf_op jit(solution)/shard_map/pallas_call | solution.py:381
  21.6 1.6 %collective-permute-start.4 = (bf16[192,128]{1,0:T(8,128)(2,1)S(1)}, bf16[192,128]{1,0:T(8,128)(2,1)S(1)}, u32[]{:S(2)}, u32[]{:S(2)}) collective-permute-start(bf16[192,128]{1,0:T(8,128)(2,1)S(1)} %get-tuple-element.58.refs_4_), channel_id=1, source_target_pairs={{0,1},{1,0},{2,3},{3,2},{4,5},{5,4},{6,7},{7,6},{8,9},{9,8},{10,11... | collective-permute-start | bytes 147464 | tf_op jit(solution)/shard_map/ppermute | solution.py:589
  23.3 0.4 collective-permute-done.6.refs_2_
  23.7 1.6 %collective-permute-start.8 = (bf16[272,128]{1,0:T(8,128)(2,1)S(1)}, bf16[272,128]{1,0:T(8,128)(2,1)S(1)}, u32[]{:S(2)}, u32[]{:S(2)}) collective-permute-start(bf16[272,128]{1,0:T(8,128)(2,1)S(1)} %shard_map.97.own), channel_id=1, source_target_pairs={{0,1},{1,0},{2,3},{3,2},{4,5},{5,4},{6,7},{7,6},{8,9},{9,8},{10,11... | collective-permute-start | bytes 208904 | tf_op jit(solution)/shard_map/ppermute | solution.py:589
  25.3 0.4 collective-permute-done.4._.near
  25.8 1.5 %shard_map.98 = (bf16[1024,2304]{1,0:T(8,128)(2,1)S(1)}, f32[1,1536,128]{2,1,0:T(8,128)S(1)}) custom-call(bf16[1024,128]{1,0:T(8,128)(2,1)S(1)} %get-tuple-element.62.left_ref, bf16[2304,128]{1,0:T(8,128)(2,1)S(1)} %get-tuple-element.63.right_ref, f32[32,1536]{1,0:T(8,128)S(1)} %get-tuple-element.64.held, bf16[192,128]{1,0:T(8,128)(2,1)S(1)} %collective-permute-done.4._.near), custom_call_target="tpu_custom_call" | custom-call | flops 603979776 | bytes 9437184 | tf_op jit(solution)/shard_map/pallas_call | solution.py:409
  27.3 0.8 %collective-permute-done.8.near = bf16[272,128]{1,0:T(8,128)(2,1)S(1)} collective-permute-done((bf16[272,128]{1,0:T(8,128)(2,1)S(1)}, bf16[272,128]{1,0:T(8,128)(2,1)S(1)}, u32[]{:S(2)}, u32[]{:S(2)}) %collective-permute-start.8) | collective-permute-done | bytes 69664 | tf_op jit(solution)/shard_map/ppermute | solution.py:589
  28.1 1.0 %collective-permute-start.9 = (bf16[272,128]{1,0:T(8,128)(2,1)S(1)}, bf16[272,128]{1,0:T(8,128)(2,1)S(1)}, u32[]{:S(2)}, u32[]{:S(2)}) collective-permute-start(bf16[272,128]{1,0:T(8,128)(2,1)S(1)} %shard_map.99.refs_2_.refs_0_), channel_id=1, source_target_pairs={{0,2},{1,3},{2,0},{3,1},{4,6},{5,7},{6,4},{7,5},{8,10},{9,11},{10,... | collective-permute-start | bytes 208904 | tf_op jit(solution)/shard_map/ppermute | solution.py:589
  29.1 2.1 %shard_map.100 = (f32[96,128]{1,0:T(8,128)S(1)}, bf16[96,128]{1,0:T(8,128)(2,1)S(1)}, bf16[96,128]{1,0:T(8,128)(2,1)S(1)}, bf16[96,128]{1,0:T(8,128)(2,1)S(1)}) custom-call(f32[1,1536,128]{2,1,0:T(8,128)S(1)} %get-tuple-element.66.refs_0_, bf16[1024,2304]{1,0:T(8,128)(2,1)S(1)} %get-tuple-element.65._.refs_1_, bf16[272,128]{1,0:T(8,128)(2,1)S(1)} %shard_map.99.refs_2_.refs_0_), custom_call_target="tpu_custom_call" | custom-call | flops 603979776 | bytes 4718592 | tf_op jit(solution)/shard_map/pallas_call | solution.py:381
  31.2 2.2 %collective-permute-done.9.refs_1_ = bf16[272,128]{1,0:T(8,128)(2,1)S(1)} collective-permute-done((bf16[272,128]{1,0:T(8,128)(2,1)S(1)}, bf16[272,128]{1,0:T(8,128)(2,1)S(1)}, u32[]{:S(2)}, u32[]{:S(2)}) %collective-permute-start.9) | collective-permute-done | bytes 69664 | tf_op jit(solution)/shard_map/ppermute | solution.py:589
  33.4 0.1 shard_map.101
  33.4 0.1 collective-permute-start.10
  33.5 2.2 %collective-permute-start.11 = (bf16[352,128]{1,0:T(8,128)(2,1)S(1)}, bf16[352,128]{1,0:T(8,128)(2,1)S(1)}, u32[]{:S(2)}, u32[]{:S(2)}) collective-permute-start(bf16[352,128]{1,0:T(8,128)(2,1)S(1)} %get-tuple-element.77), channel_id=1, source_target_pairs={{0,8},{4,12},{8,0},{12,4},{1,9},{5,13},{9,1},{13,5},{2,10},{6,14},... | collective-permute-start | bytes 270344 | tf_op jit(solution)/shard_map/ppermute | solution.py:589
  35.7 0.0 collective-permute-start.12
  35.8 1.2 %shard_map.102 = (bf16[2304,128]{1,0:T(8,128)(2,1)}, f32[8,128]{1,0:T(8,128)S(1)}) custom-call(bf16[1024,2304]{1,0:T(8,128)(2,1)S(1)} %get-tuple-element.53.x_ref, bf16[128,1024]{1,0:T(8,128)(2,1)S(1)} %get-tuple-element.54.wt_ref, f32[1,128]{1,0:T(1,128)S(1)} %bitcast.4, bf16[256,128]{1,0:T(8,128)(2,1)S(1)} %get-tuple-element.72._after.refs_0_), custom_call_target="tpu_custom_call" | custom-call | flops 100663296 | bytes 1572864 | tf_op jit(solution)/shard_map/pallas_call | solution.py:435
  36.9 0.6 %collective-permute-start.13 = (bf16[96,128]{1,0:T(8,128)(2,1)S(1)}, bf16[96,128]{1,0:T(8,128)(2,1)S(1)}, u32[]{:S(2)}, u32[]{:S(2)}) collective-permute-start(bf16[96,128]{1,0:T(8,128)(2,1)S(1)} %shard_map.104), channel_id=1, source_target_pairs={{0,2},{1,3},{2,0},{3,1},{4,6},{5,7},{6,4},{7,5},{8,10},{9,11},{10,... | collective-permute-start | bytes 73736 | tf_op jit(solution)/shard_map/ppermute | solution.py:589
  37.5 1.9 %shard_map.103 = (bf16[2304,128]{1,0:T(8,128)(2,1)}, f32[8,128]{1,0:T(8,128)}) custom-call(bf16[1024,2304]{1,0:T(8,128)(2,1)S(1)} %get-tuple-element.53.x_ref, bf16[128,1024]{1,0:T(8,128)(2,1)S(1)} %get-tuple-element.54.wt_ref, f32[1,128]{1,0:T(1,128)S(1)} %bitcast.5, ...), custom_call_target="tpu_custom_call", output_to_operand_aliasing={{0}: (4, {})} | custom-call | flops 201326592 | bytes 3145728 | tf_op jit(solution)/shard_map/pallas_call | solution.py:435
  39.4 2.3 %collective-permute-done.13.refs_5_ = bf16[96,128]{1,0:T(8,128)(2,1)S(1)} collective-permute-done((bf16[96,128]{1,0:T(8,128)(2,1)S(1)}, bf16[96,128]{1,0:T(8,128)(2,1)S(1)}, u32[]{:S(2)}, u32[]{:S(2)}) %collective-permute-start.13) | collective-permute-done | bytes 24608 | tf_op jit(solution)/shard_map/ppermute | solution.py:589
  41.7 0.9 %shard_map.105 = (f32[1024,128]{1,0:T(8,128)}, f32[8,1536]{1,0:T(8,128)}, f32[8,1536]{1,0:T(8,128)}, f32[1,128]{1,0:T(1,128)}) custom-call(bf16[256,128]{1,0:T(8,128)(2,1)S(1)} %get-tuple-element.72._after.refs_0_, bf16[352,128]{1,0:T(8,128)(2,1)S(1)} %collective-permute-done.10.refs_1_, bf16[352,128]{1,0:T(8,128)(2,1)S(1)} %collective-permute-done.11.refs_2_, ...), custom_call_target="tpu_custom_call" | custom-call | tf_op jit(solution)/shard_map/pallas_call | solution.py:467
  (12 shorter events, 0.1 us)
Async XLA Ops:
  0.6 7.0 %collective-permute-start = (bf16[8,1536]{1,0:T(8,128)(2,1)}, bf16[8,1536]{1,0:T(8,128)(2,1)S(1)}, u32[]{:S(2)}, u32[]{:S(2)}) collective-permute-start(bf16[8,1536]{1,0:T(8,128)(2,1)} %a_hbm.1), channel_id=1, source_target_pairs={{0,2},{1,3},{2,0},{3,1},{4,6},{5,7},{6,4},{7,5},{8,10},{9,11},{10,... | collective-permute-start | bytes 73736 | tf_op jit(solution)/shard_map/ppermute | solution.py:589
  4.7 4.0 %collective-permute-start.1 = (bf16[8,1536]{1,0:T(8,128)(2,1)}, bf16[8,1536]{1,0:T(8,128)(2,1)S(1)}, u32[]{:S(2)}, u32[]{:S(2)}) collective-permute-start(bf16[8,1536]{1,0:T(8,128)(2,1)} %b_hbm.1), channel_id=1, source_target_pairs={{0,8},{4,12},{8,0},{12,4},{1,9},{5,13},{9,1},{13,5},{2,10},{6,14},... | collective-permute-start | bytes 73736 | tf_op jit(solution)/shard_map/ppermute | solution.py:589
  8.8 4.2 %collective-permute-start.2 = (bf16[16,1536]{1,0:T(8,128)(2,1)S(1)}, bf16[16,1536]{1,0:T(8,128)(2,1)S(1)}, u32[]{:S(2)}, u32[]{:S(2)}) collective-permute-start(bf16[16,1536]{1,0:T(8,128)(2,1)S(1)} %get-tuple-element.48.refs_0_), channel_id=1, source_target_pairs={{0,1},{1,0},{2,3},{3,2},{4,5},{5,4},{6,7},{7,6},{8,9},{9,8},{10,11... | collective-permute-start | bytes 147464 | tf_op jit(solution)/shard_map/ppermute | solution.py:589
  10.4 2.5 %collective-permute-start.3 = (bf16[16,1536]{1,0:T(8,128)(2,1)S(1)}, bf16[16,1536]{1,0:T(8,128)(2,1)S(1)}, u32[]{:S(2)}, u32[]{:S(2)}) collective-permute-start(bf16[16,1536]{1,0:T(8,128)(2,1)S(1)} %get-tuple-element.49.refs_2_), channel_id=1, source_target_pairs={{0,4},{4,0},{8,12},{12,8},{1,5},{5,1},{9,13},{13,9},{2,6},{6,2},{1... | collective-permute-start | bytes 147464 | tf_op jit(solution)/shard_map/ppermute | solution.py:589
  17.6 5.6 %collective-permute-start.5 = (bf16[272,128]{1,0:T(8,128)(2,1)S(1)}, bf16[272,128]{1,0:T(8,128)(2,1)S(1)}, u32[]{:S(2)}, u32[]{:S(2)}) collective-permute-start(bf16[272,128]{1,0:T(8,128)(2,1)S(1)} %get-tuple-element.59), channel_id=1, source_target_pairs={{0,12},{4,8},{8,4},{12,0},{1,13},{5,9},{9,5},{13,1},{2,14},{6,10},... | collective-permute-start | bytes 208904 | tf_op jit(solution)/shard_map/ppermute | solution.py:589
  18.5 5.1 %collective-permute-start.6 = (bf16[272,128]{1,0:T(8,128)(2,1)S(1)}, bf16[272,128]{1,0:T(8,128)(2,1)S(1)}, u32[]{:S(2)}, u32[]{:S(2)}) collective-permute-start(bf16[272,128]{1,0:T(8,128)(2,1)S(1)} %get-tuple-element.60), channel_id=1, source_target_pairs={{0,8},{4,12},{8,0},{12,4},{1,9},{5,13},{9,1},{13,5},{2,10},{6,14},... | collective-permute-start | bytes 208904 | tf_op jit(solution)/shard_map/ppermute | solution.py:589
  19.2 4.4 %collective-permute-start.7 = (bf16[272,128]{1,0:T(8,128)(2,1)S(1)}, bf16[272,128]{1,0:T(8,128)(2,1)S(1)}, u32[]{:S(2)}, u32[]{:S(2)}) collective-permute-start(bf16[272,128]{1,0:T(8,128)(2,1)S(1)} %get-tuple-element.61), channel_id=1, source_target_pairs={{0,4},{4,0},{8,12},{12,8},{1,5},{5,1},{9,13},{13,9},{2,6},{6,2},{1... | collective-permute-start | bytes 208904 | tf_op jit(solution)/shard_map/ppermute | solution.py:589
  21.6 4.2 %collective-permute-start.4 = (bf16[192,128]{1,0:T(8,128)(2,1)S(1)}, bf16[192,128]{1,0:T(8,128)(2,1)S(1)}, u32[]{:S(2)}, u32[]{:S(2)}) collective-permute-start(bf16[192,128]{1,0:T(8,128)(2,1)S(1)} %get-tuple-element.58.refs_4_), channel_id=1, source_target_pairs={{0,1},{1,0},{2,3},{3,2},{4,5},{5,4},{6,7},{7,6},{8,9},{9,8},{10,11... | collective-permute-start | bytes 147464 | tf_op jit(solution)/shard_map/ppermute | solution.py:589
  23.7 4.4 %collective-permute-start.8 = (bf16[272,128]{1,0:T(8,128)(2,1)S(1)}, bf16[272,128]{1,0:T(8,128)(2,1)S(1)}, u32[]{:S(2)}, u32[]{:S(2)}) collective-permute-start(bf16[272,128]{1,0:T(8,128)(2,1)S(1)} %shard_map.97.own), channel_id=1, source_target_pairs={{0,1},{1,0},{2,3},{3,2},{4,5},{5,4},{6,7},{7,6},{8,9},{9,8},{10,11... | collective-permute-start | bytes 208904 | tf_op jit(solution)/shard_map/ppermute | solution.py:589
  28.1 7.7 %copy-start = (f32[128]{0:T(128)S(1)}, f32[128]{0:T(128)}, u32[]{:S(2)}) copy-start(f32[128]{0:T(128)} %param.8) | copy-start | bytes 1540
  28.1 5.3 %collective-permute-start.9 = (bf16[272,128]{1,0:T(8,128)(2,1)S(1)}, bf16[272,128]{1,0:T(8,128)(2,1)S(1)}, u32[]{:S(2)}, u32[]{:S(2)}) collective-permute-start(bf16[272,128]{1,0:T(8,128)(2,1)S(1)} %shard_map.99.refs_2_.refs_0_), channel_id=1, source_target_pairs={{0,2},{1,3},{2,0},{3,1},{4,6},{5,7},{6,4},{7,5},{8,10},{9,11},{10,... | collective-permute-start | bytes 208904 | tf_op jit(solution)/shard_map/ppermute | solution.py:589
  33.4 8.3 %collective-permute-start.10 = (bf16[352,128]{1,0:T(8,128)(2,1)S(1)}, bf16[352,128]{1,0:T(8,128)(2,1)S(1)}, u32[]{:S(2)}, u32[]{:S(2)}) collective-permute-start(bf16[352,128]{1,0:T(8,128)(2,1)S(1)} %get-tuple-element.76), channel_id=1, source_target_pairs={{0,12},{4,8},{8,4},{12,0},{1,13},{5,9},{9,5},{13,1},{2,14},{6,10},... | collective-permute-start | bytes 270344 | tf_op jit(solution)/shard_map/ppermute | solution.py:589
  33.5 8.2 %collective-permute-start.11 = (bf16[352,128]{1,0:T(8,128)(2,1)S(1)}, bf16[352,128]{1,0:T(8,128)(2,1)S(1)}, u32[]{:S(2)}, u32[]{:S(2)}) collective-permute-start(bf16[352,128]{1,0:T(8,128)(2,1)S(1)} %get-tuple-element.77), channel_id=1, source_target_pairs={{0,8},{4,12},{8,0},{12,4},{1,9},{5,13},{9,1},{13,5},{2,10},{6,14},... | collective-permute-start | bytes 270344 | tf_op jit(solution)/shard_map/ppermute | solution.py:589
  35.7 6.0 %collective-permute-start.12 = (bf16[352,128]{1,0:T(8,128)(2,1)S(1)}, bf16[352,128]{1,0:T(8,128)(2,1)S(1)}, u32[]{:S(2)}, u32[]{:S(2)}) collective-permute-start(bf16[352,128]{1,0:T(8,128)(2,1)S(1)} %get-tuple-element.78), channel_id=1, source_target_pairs={{0,4},{4,0},{8,12},{12,8},{1,5},{5,1},{9,13},{13,9},{2,6},{6,2},{1... | collective-permute-start | bytes 270344 | tf_op jit(solution)/shard_map/ppermute | solution.py:589
  36.9 4.8 %collective-permute-start.13 = (bf16[96,128]{1,0:T(8,128)(2,1)S(1)}, bf16[96,128]{1,0:T(8,128)(2,1)S(1)}, u32[]{:S(2)}, u32[]{:S(2)}) collective-permute-start(bf16[96,128]{1,0:T(8,128)(2,1)S(1)} %shard_map.104), channel_id=1, source_target_pairs={{0,2},{1,3},{2,0},{3,1},{4,6},{5,7},{6,4},{7,5},{8,10},{9,11},{10,... | collective-permute-start | bytes 73736 | tf_op jit(solution)/shard_map/ppermute | solution.py:589

commit v16 on v14

--- a/solution.py
+++ b/solution.py
@@ -49,7 +49,9 @@
     for e in range(depth):
         block = w32[pl.ds(e, depth, stride=depth), :]
         we_ref[e * depth : (e + 1) * depth, :] = block.astype(BF16)
-    wt_ref[...] = we_ref[...].astype(F32).T.astype(BF16)
+    turned = we_ref[...].astype(F32).T.astype(BF16)
+    for n in range(wt_ref.shape[0]):
+        wt_ref[n] = turned[:, n * wt_ref.shape[2] : (n + 1) * wt_ref.shape[2]]
     for copy in copies[1:]:
         copy.wait()
 
@@ -58,10 +60,10 @@
     return pl.BlockSpec(memory_space=pltpu.VMEM)
 
 
-def load(a, b, w, g):
+def load(a, b, w, g, shares):
     shapes = [
         jax.ShapeDtypeStruct(w.shape, BF16),
-        jax.ShapeDtypeStruct(w.shape[::-1], BF16),
+        jax.ShapeDtypeStruct((shares, w.shape[1], w.shape[0] // shares), BF16),
         *[jax.ShapeDtypeStruct(x.shape, BF16) for x in (a, b, w, g)],
     ]
     return pl.pallas_call(
@@ -221,17 +223,38 @@
     return plan
 
 
-def outer_kernel(i_n, j_n, *refs):
+def outer_share(left, wide, g_ref, x_part, share, i_n, j_n, sequences):
     depth = PROJECTED_DEPTH
-    row_n = lax.axis_size("row")
-    a_pieces, b_pieces, refs = refs[:2], refs[2:4], refs[4:]
-    g_ref, bias_ref, x_ref, a_held, b_wide = refs[:5]
-    messages, (b_held, left, total) = refs[5 : 5 + row_n], refs[5 + row_n :]
+    span = GROUP * j_n
+    per_share = x_part.shape[0] // depth
+    for e in range(0, per_share, 2):
+        right = [diagonal_of(wide, share * per_share + e + n, j_n, sequences) for n in range(2)]
+        product = dot(left[...], jnp.concatenate(right, axis=0), ROWS_BY_ROWS).astype(BF16)
+        for n in range(2):
+            for k in range(i_n // GROUP):
+                x_part[(e + n) * depth : (e + n + 1) * depth, k * span : (k + 1) * span] = product[
+                    k * depth : (k + 1) * depth, n * span : (n + 1) * span
+                ]
+    return dot(x_part[...], g_ref[...])
+
+
+def outer_shares(partner_list, left, wide, g_ref, bias_ref, x_ref, messages, i_n, j_n, sequences):
+    rows = x_ref.shape[0] // len(partner_list)
+    me = lax.axis_index("row")
+    for n, (p, message) in enumerate(zip(partner_list, messages, strict=True)):
+        part = x_ref.at[n * rows : (n + 1) * rows]
+        share = lax.bitwise_xor(me, p)
+        total = outer_share(left, wide, g_ref, part, share, i_n, j_n, sequences)
+        message[0:rows, :] = total.astype(message.dtype)
+        message[rows:, :] = bias_ref[...].astype(message.dtype)
+
+
+def outer_start_kernel(i_n, j_n, *refs):
+    depth = PROJECTED_DEPTH
+    far = partners(lax.axis_size("row"))[1:-1]
+    a_pieces, b_pieces, (g_ref, bias_ref), refs = refs[:2], refs[2:4], refs[4:6], refs[6:]
+    (x_ref, a_held, b_wide, left), messages, b_held = refs[:4], refs[4:-1], refs[-1]
     sequences = a_held.shape[0]
-    groups = i_n // GROUP
-    per_step = depth // CHUNKS
-    span = GROUP * j_n
-
     join(a_pieces, "col", a_held)
     join(b_pieces, "row", b_held)
     spread(b_held, b_wide)
@@ -241,72 +264,71 @@
     value = jnp.zeros(left.shape, F32)
     for m in range(GROUP):
         rows = [
-            turned[(k * GROUP + m) * depth : (k * GROUP + m + 1) * depth, :] for k in range(groups)
+            turned[(k * GROUP + m) * depth : (k * GROUP + m + 1) * depth, :]
+            for k in range(i_n // GROUP)
         ]
         value += dot(jnp.concatenate(rows, axis=0), (shifted == m * sequences).astype(BF16))
     left[...] = value.astype(BF16)
-
-    @chunks
-    def _(t):
-        size = per_step * depth
-        rows = pl.ds(t * size if CHUNKS == 1 else pl.multiple_of(t * size, size), size)
-        x_part = x_ref.at[rows]
-        for e in range(0, per_step, 2):
-            right = [diagonal_of(b_wide, t * per_step + e + n, j_n, sequences) for n in range(2)]
-            product = dot(
-                left[...], jnp.concatenate(right, axis=0), ROWS_BY_ROWS
-            ).astype(BF16)
-            for n in range(2):
-                for k in range(groups):
-                    x_part[(e + n) * depth : (e + n + 1) * depth, k * span : (k + 1) * span] = product[
-                        k * depth : (k + 1) * depth, n * span : (n + 1) * span
-                    ]
-        total[rows, :] = dot(x_part[...], g_ref[...])
-
-    share = total.shape[0] // row_n
-    me = lax.axis_index("row")
-    for p, message in enumerate(messages):
-        part = lax.bitwise_xor(me, p)
-        for n in range(share // depth):
-            block = total[pl.ds(part * (share // depth) + n, depth, stride=depth), :]
-            message[n * depth : (n + 1) * depth, :] = block.astype(message.dtype)
-        message[share:, :] = bias_ref[...].astype(message.dtype)
-
-
-def outer(a_pieces, b_pieces, g, bias_rows, i_n, j_n, sequences):
-    row_n = lax.axis_size("row")
-    depth = PROJECTED_DEPTH
-    channels = depth * depth
-    pairs = i_n * j_n
-    tiles = tile_count(sequences)[1]
-    operands = [*a_pieces, *b_pieces, g, bias_rows]
-    shapes = [jax.ShapeDtypeStruct((channels, pairs), BF16)]
-    shapes += [
-        jax.ShapeDtypeStruct((sequences, i_n * depth), F32),
-        jax.ShapeDtypeStruct((tiles, j_n * depth, LANES), F32),
-    ]
-    shapes += [
-        jax.ShapeDtypeStruct((channels // row_n + BIAS_ROWS, LANES), BF16 if p else F32)
-        for p in range(row_n)
-    ]
-    results = pl.pallas_call(
-        functools.partial(outer_kernel, i_n, j_n),
+    outer_shares(far, left, b_wide, g_ref, bias_ref, x_ref, messages, i_n, j_n, sequences)
+
+
+def outer_end_kernel(i_n, j_n, sequences, left, b_wide, g_ref, bias_ref, x_ref, *messages):
+    outer_shares((1, 0), left, b_wide, g_ref, bias_ref, x_ref, messages, i_n, j_n, sequences)
+
+
+def outer_call(kernel, operands, shapes, scratch, rows, pairs, sequences):
+    return pl.pallas_call(
+        kernel,
         in_specs=[in_vmem()] * len(operands),
         out_specs=[in_vmem()] * len(shapes),
-        out_shape=shapes,
-        scratch_shapes=[
-            pltpu.VMEM((sequences, j_n * depth), F32),
-            pltpu.VMEM((i_n // GROUP * depth, GROUP * sequences), BF16),
-            pltpu.VMEM((channels, PAIR_FEATURES), F32),
-        ],
+        out_shape=[jax.ShapeDtypeStruct(shape, kind) for shape, kind in shapes],
+        scratch_shapes=scratch,
         compiler_params=params(sequences),
         cost_estimate=pl.CostEstimate(
-            flops=4 * pairs * channels * PAIR_FEATURES,
-            bytes_accessed=2 * pairs * channels,
+            flops=4 * pairs * rows * PAIR_FEATURES,
+            bytes_accessed=2 * pairs * rows,
             transcendentals=0,
         ),
     )(*operands)
-    return *results[:3], results[3:]
+
+
+def outer_start(a_pieces, b_pieces, g, bias_rows, i_n, j_n, sequences):
+    row_n = lax.axis_size("row")
+    depth = PROJECTED_DEPTH
+    share = depth * depth // row_n
+    rows = share * (row_n - 2)
+    shapes = [
+        ((rows, i_n * j_n), BF16),
+        ((sequences, i_n * depth), F32),
+        ((tile_count(sequences)[1], j_n * depth, LANES), F32),
+        ((i_n // GROUP * depth, GROUP * sequences), BF16),
+    ]
+    shapes += [((share + BIAS_ROWS, LANES), BF16)] * (row_n - 2)
+    results = outer_call(
+        functools.partial(outer_start_kernel, i_n, j_n),
+        [*a_pieces, *b_pieces, g, bias_rows],
+        shapes,
+        [pltpu.VMEM((sequences, j_n * depth), F32)],
+        rows,
+        i_n * j_n,
+        sequences,
+    )
+    return *results[:4], results[4:]
+
+
+def outer_end(left, b_wide, g, bias_rows, i_n, j_n, sequences):
+    share = PROJECTED_DEPTH * PROJECTED_DEPTH // lax.axis_size("row")
+    shapes = [((2 * share, i_n * j_n), BF16)]
+    shapes += [((share + BIAS_ROWS, LANES), kind) for kind in (BF16, F32)]
+    return outer_call(
+        functools.partial(outer_end_kernel, i_n, j_n, sequences),
+        [left, b_wide, g, bias_rows],
+        shapes,
+        [],
+        2 * share,
+        i_n * j_n,
+        sequences,
+    )
 
 
 def gradient_kernel(axis, plan, kept, positions, others, sequences, *refs):
@@ -397,7 +419,8 @@
     return results[:kept], results[kept:]
 
 
-def product_kernel(left_ref, right_ref, held, _, out_ref, wide):
+def product_kernel(left_ref, right_ref, held, *refs):
+    out_ref, wide = refs[-2:]
     spread(held, wide)
     multiply(left_ref, right_ref, out_ref)
 
@@ -407,7 +430,7 @@
     spread_shape = (tile_count(held.shape[0])[1], held.shape[1], LANES)
     return pl.pallas_call(
         product_kernel,
-        in_specs=[in_vmem()] * 3 + [pl.BlockSpec(memory_space=pl.ANY)],
+        in_specs=[in_vmem()] * 3 + [pl.BlockSpec(memory_space=pl.ANY)] * len(after),
         out_specs=[in_vmem()] * 2,
         out_shape=[jax.ShapeDtypeStruct(shape, BF16), jax.ShapeDtypeStruct(spread_shape, F32)],
         compiler_params=params(32),
@@ -416,23 +439,30 @@
             bytes_accessed=4 * shape[0] * shape[1],
             transcendentals=0,
         ),
-    )(left, right, held, after)
-
-
-def pair_kernel(sequences, x_ref, wt_ref, bias_ref, _, out_ref):
-    product = dot(wt_ref[...], x_ref[...])
+    )(left, right, held, *after)
+
+
+def pair_kernel(sequences, far_ref, near_ref, wt_ref, bias_ref, _, out_ref):
+    me = lax.axis_index("row")
+    count = wt_ref.shape[0]
+    product = None
+    for x_ref, ps in ((far_ref, partners(count)[1:-1]), (near_ref, (1, 0))):
+        weights = [wt_ref[lax.bitwise_xor(me, p)] for p in ps]
+        term = dot(jnp.concatenate(weights, axis=1), x_ref[...])
+        product = term if product is None else product + term
     out_ref[...] = (product.T * (1.0 / sequences) + bias_ref[...]).astype(BF16)
 
 
-def pair(x, wt, output_bias, after, sequences):
-    channels, pairs = x.shape
+def pair(x_far, x_near, wt, output_bias, after, sequences):
+    pairs = x_far.shape[1]
     count = 3
     size = pairs // count
     return pl.pallas_call(
         functools.partial(pair_kernel, sequences),
         grid=(count,),
         in_specs=[
-            pl.BlockSpec((channels, size), lambda t: (0, t)),
+            pl.BlockSpec((x_far.shape[0], size), lambda t: (0, t)),
+            pl.BlockSpec((x_near.shape[0], size), lambda t: (0, t)),
             whole(wt.shape),
             whole((1, PAIR_FEATURES)),
             pl.BlockSpec(memory_space=pl.ANY),
@@ -441,11 +471,9 @@
         out_shape=jax.ShapeDtypeStruct((pairs, PAIR_FEATURES), BF16),
         compiler_params=params(),
         cost_estimate=pl.CostEstimate(
-            flops=4 * pairs * channels * PAIR_FEATURES,
-            bytes_accessed=2 * pairs * channels,
-            transcendentals=0,
+            flops=4 * pairs * wt.size, bytes_accessed=16 * pairs * wt.shape[2], transcendentals=0
         ),
-    )(x, wt, output_bias.reshape(1, PAIR_FEATURES), after)
+    )(x_far, x_near, wt, output_bias.reshape(1, PAIR_FEATURES), after)
 
 
 def unfold(total, share, out):
@@ -518,12 +546,12 @@
     return message
 
 
-def column_sum(parts, grads, share):
+def column_sum(parts, grads, after, share):
     rows = share + BIAS_ROWS
     count, sent = len(parts), len(grads)
 
     def kernel(*refs):
-        parts, grads, refs = refs[:count], refs[count : count + sent], refs[count + sent :]
+        parts, grads, refs = refs[:count], refs[count : count + sent], refs[count + sent + 1 :]
         messages, (piece_out, bias_out, held) = refs[:sent], refs[sent:]
         home = lax.div(lax.axis_index("col"), 2)
         for p, part in enumerate(parts):
@@ -542,7 +570,7 @@
     shapes = [((share + grad.shape[0], LANES), BF16) for grad in grads]
     shapes += [((share, LANES), BF16), ((8, LANES), F32)]
     scratch = [pltpu.VMEM((count, rows, LANES), BF16)]
-    *messages, piece, bias = call(kernel, [*parts, *grads], shapes, scratch=scratch)
+    *messages, piece, bias = call(kernel, [*parts, *grads], shapes, [after], scratch)
     return messages, piece, bias
 
 
@@ -552,14 +580,18 @@
 
     def kernel(*refs):
         pieces, left, refs = refs[:count], refs[count : count + left_n], refs[count + left_n :]
-        right_own, bias, projection, left_out, right_out, bias_out = refs
+        right_own, bias, projection, left_out, right_out, bias_out, ordered = refs
         me = lax.axis_index("row")
         right_total = right_own[...]
         for p, piece in zip(partners(count), pieces, strict=True):
             rows = pl.ds(pl.multiple_of(lax.bitwise_xor(me, p) * share, share), share)
-            projection[rows, :] = piece[0:share, :].astype(F32) * scale
+            ordered[rows, :] = piece[0:share, :].astype(F32) * scale
             if p > 0:
                 right_total += piece[share:, :].astype(F32)
+        depth = PROJECTED_DEPTH
+        for c in range(depth):
+            block = ordered[pl.ds(c, depth, stride=depth), :]
+            projection[c * depth : (c + 1) * depth, :] = block
         left_total = left[0][...]
         for term in left[1:]:
             left_total += term[...].astype(F32)
@@ -573,7 +605,8 @@
         (right_shape, F32),
         ((1, PAIR_FEATURES), F32),
     ]
-    return call(kernel, [*pieces, *left, right_own, bias], shapes)
+    scratch = [pltpu.VMEM(shapes[0][0], F32)]
+    return call(kernel, [*pieces, *left, right_own, bias], shapes, scratch=scratch)
 
 
 def swap(x, axis, p):
@@ -604,38 +637,43 @@
         second_homolog_features,
         final_projection_matrix,
         cotangent.reshape(i_n * j_n, PAIR_FEATURES),
+        row_n,
     )
     a, b = stack([a, *a_far], [b, *b_far])
     a_pieces = [a, swap(a, "col", 1)]
     b_pieces = [b, swap(b, "row", 1)]
     y, gt, bias_rows = prepare(we, g, i_n, j_n)
 
-    x, a_held, b_wide, (own, *messages) = outer(
+    x_far, a_held, b_wide, left_operand, messages = outer_start(
         a_pieces, b_pieces, g, bias_rows, i_n, j_n, sequences
     )
     share = channels // row_n
-
-    parts = [own] + swap_each(messages, "row")[::-1]
-    left_kept, (message,) = gradient(
-        b_wide, y, own, "col", in_pairs(col_n), col_n // 2, 1, i_n, j_n, sequences
-    )
-    left_near = swap(message, "col", 1)
-
-    message = row_sum(parts, message, share)
+    parts = [
+        swap(message, "row", p)
+        for message, p in zip(messages, partners(row_n)[1:-1], strict=True)
+    ]
+    x_near, message, own = outer_end(left_operand, b_wide, g, bias_rows, i_n, j_n, sequences)
+    parts = [own, *parts, swap(message, "row", 1)]
+    y2, a_wide = product(w, gt, a_held, parts[1:-1])
+
+    message = row_sum(parts, y2, share)
     near = swap(message, "col", 1)
-    left_own, left_messages = pair_sum(left_kept, left_near, message)
-    left = [left_own] + swap_each(left_messages, "col", 2)
-    y2, a_wide = product(w, gt, a_held, left_own)
-
-    message = column_pair_sum(message, near, y2, share)
+    left_kept, (left_sent,) = gradient(
+        b_wide, y, message, "col", in_pairs(col_n), col_n // 2, 1, i_n, j_n, sequences
+    )
+    left_near = swap(left_sent, "col", 1)
+
+    message = column_pair_sum(message, near, left_sent, share)
     parts = [message] + from_evens(message, "col")
     (right_own,), right_sent = gradient(
         a_wide, y2, message, "row", alone(row_n), 1, row_n - 1, j_n, i_n, sequences
     )
-
-    messages, piece, bias = column_sum(parts, right_sent, share)
+    left_own, left_messages = pair_sum(left_kept, left_near, right_own)
+    left = [left_own] + swap_each(left_messages, "col", 2)
+
+    messages, piece, bias = column_sum(parts, right_sent, left_own, share)
     pieces = [piece] + swap_each(messages, "row")[::-1]
-    pair_map = pair(x, wt, output_bias, piece, sequences)
+    pair_map = pair(x_far, x_near, wt, output_bias, piece, sequences)
     projection, left_grad, right_grad, bias_grad = finish(
         pieces,
         left,

time: 41.4 us -> 42.4 us (1.024)
  waiting for transfers between devices: 5.68 us -> 7.5 us
  starting transfers between devices: 17.8 us -> 17.1 us
    ppermute x14, waiting for transfers between devices: 5.68 us -> 7.5 us  [swap(): lax.ppermute(x, axis, [(n, n ^ p) for n in range(lax.axis_size(axis))])]
    ppermute x14, starting transfers between devices: 17.8 us -> 17.1 us  [swap(): lax.ppermute(x, axis, [(n, n ^ p) for n in range(lax.axis_size(axis))])]
    pallas_call x1 -> x2, Pallas kernels: 4.66 us -> 4.22 us  [outer_call(): pl.pallas_call(kernel, in_specs=[in_vmem()] * len(operands), out_specs=[i...]
  transfers between devices with their start and end apart: 14 -> 14, of which waited for: 7 -> 8; matrix products, arithmetic and copies ran while one was open for 0% -> 0% of each run, Pallas kernels for 28% -> 32%
where the time goes in v16:
time: 42.4 us; the launch traced here: 42.3 us
  starting transfers between devices  17.1 us (40%)
  Pallas kernels  16.9 us (40%)
  waiting for transfers between devices  7.5 us (18%)
  between operations  0.73 us (2%)
    ppermute x14, starting transfers between devices, swap(): lax.ppermute(x, axis, [(n, n ^ p) for n in range(lax.axis_size(axis))])  17.1 us
    ppermute x14, waiting for transfers between devices, swap(): lax.ppermute(x, axis, [(n, n ^ p) for n in range(lax.axis_size(axis))])  7.5 us
    pallas_call x2, Pallas kernels, outer_call(): pl.pallas_call(kernel, in_specs=[in_vmem()] * len(operands), out_specs=[i...  4.22 us
    pallas_call x2, Pallas kernels, gradient(): pl.pallas_call(functools.partial(gradient_kernel, axis, plan, kept, posit...  4.13 us
    pallas_call x1, Pallas kernels, pair(): pl.pallas_call(functools.partial(pair_kernel, sequences), grid=(count,),...  2.56 us
    pallas_call x1, Pallas kernels, prepare(): pl.pallas_call(functools.partial(prepare_kernel, i_n, j_n), in_specs=[in_...  1.76 us
    pallas_call x1, Pallas kernels, product(): pl.pallas_call(product_kernel, in_specs=[in_vmem()] * 3 + [pl.BlockSpec(m...  1.55 us
    pallas_call x1, Pallas kernels, load(): pl.pallas_call(load_kernel, in_specs=[pl.BlockSpec(memory_space=pltpu.HBM...  1.39 us
  transfers between devices with their start and end apart: 14, of which 8 were waited for; matrix products, arithmetic and copies ran while one was open for 0% of the time, Pallas kernels for 32%

profile of v16, /device:TPU:0, one launch (start us, length us, event | category | flops | bytes accessed | tf_op | source)
XLA Modules:
  0.0 42.3 jit_solution(18060901113405588471)
XLA Ops:
  0.6 4.1 %collective-permute-start = (bf16[8,1536]{1,0:T(8,128)(2,1)}, bf16[8,1536]{1,0:T(8,128)(2,1)S(1)}, u32[]{:S(2)}, u32[]{:S(2)}) collective-permute-start(bf16[8,1536]{1,0:T(8,128)(2,1)} %a_hbm.1), channel_id=1, source_target_pairs={{0,2},{1,3},{2,0},{3,1},{4,6},{5,7},{6,4},{7,5},{8,10},{9,11},{10,... | collective-permute-start | bytes 73736 | tf_op jit(solution)/shard_map/ppermute | solution.py:613
  4.7 1.5 %collective-permute-start.1 = (bf16[8,1536]{1,0:T(8,128)(2,1)}, bf16[8,1536]{1,0:T(8,128)(2,1)S(1)}, u32[]{:S(2)}, u32[]{:S(2)}) collective-permute-start(bf16[8,1536]{1,0:T(8,128)(2,1)} %b_hbm.1), channel_id=1, source_target_pairs={{0,8},{4,12},{8,0},{12,4},{1,9},{5,13},{9,1},{13,5},{2,10},{6,14},... | collective-permute-start | bytes 73736 | tf_op jit(solution)/shard_map/ppermute | solution.py:613
  6.2 1.4 %shard_map.92 = (bf16[1024,128]{1,0:T(8,128)(2,1)S(1)}, bf16[4,128,256]{2,1,0:T(8,128)(2,1)S(1)}, bf16[8,1536]{1,0:T(8,128)(2,1)S(1)}, bf16[8,1536]{1,0:T(8,128)...) custom-call(bf16[8,1536]{1,0:T(8,128)(2,1)} %a_hbm.1, bf16[8,1536]{1,0:T(8,128)(2,1)} %b_hbm.1, ...), custom_call_target="tpu_custom_call" | custom-call | flops 131072000 | bytes 2097152 | tf_op jit(solution)/shard_map/pallas_call | solution.py:69
  7.6 0.0 collective-permute-done.refs_1_
  7.6 1.1 %collective-permute-done.1.refs_3_ = bf16[8,1536]{1,0:T(8,128)(2,1)S(1)} collective-permute-done((bf16[8,1536]{1,0:T(8,128)(2,1)}, bf16[8,1536]{1,0:T(8,128)(2,1)S(1)}, u32[]{:S(2)}, u32[]{:S(2)}) %collective-permute-start.1) | collective-permute-done | bytes 24608 | tf_op jit(solution)/shard_map/ppermute | solution.py:613
  8.8 1.6 %collective-permute-start.2 = (bf16[16,1536]{1,0:T(8,128)(2,1)S(1)}, bf16[16,1536]{1,0:T(8,128)(2,1)S(1)}, u32[]{:S(2)}, u32[]{:S(2)}) collective-permute-start(bf16[16,1536]{1,0:T(8,128)(2,1)S(1)} %get-tuple-element.47.refs_0_), channel_id=1, source_target_pairs={{0,1},{1,0},{2,3},{3,2},{4,5},{5,4},{6,7},{7,6},{8,9},{9,8},{10,11... | collective-permute-start | bytes 147464 | tf_op jit(solution)/shard_map/ppermute | solution.py:613
  10.4 1.8 %shard_map.94 = (bf16[1024,2304]{1,0:T(8,128)(2,1)S(1)}, bf16[2304,128]{1,0:T(8,128)(2,1)S(1)}, bf16[16,128]{1,0:T(8,128)(2,1)S(1)}) custom-call(bf16[1024,128]{1,0:T(8,128)(2,1)S(1)} %get-tuple-element.50.we_ref, bf16[2304,128]{1,0:T(8,128)(2,1)S(1)} %get-tuple-element.49.g_ref.refs_4_), custom_call_target="tpu_custom_call" | custom-call | flops 603979776 | bytes 9437184 | tf_op jit(solution)/shard_map/pallas_call | solution.py:128
  12.2 0.7 %collective-permute-done.2.refs_1_ = bf16[16,1536]{1,0:T(8,128)(2,1)S(1)} collective-permute-done((bf16[16,1536]{1,0:T(8,128)(2,1)S(1)}, bf16[16,1536]{1,0:T(8,128)(2,1)S(1)}, u32[]{:S(2)}, u32[]{:S(2)}) %collective-permute-start.2) | collective-permute-done | bytes 49184 | tf_op jit(solution)/shard_map/ppermute | solution.py:613
  12.9 2.3 %shard_map.95 = (bf16[512,2304]{1,0:T(8,128)(2,1)S(1)}, f32[32,1536]{1,0:T(8,128)S(1)}, f32[1,1536,128]{2,1,0:T(8,128)S(1)}, bf16[192,256]{1,0:T(8,128)(2,1)S(1)...) custom-call(bf16[16,1536]{1,0:T(8,128)(2,1)S(1)} %get-tuple-element.47.refs_0_, ...), custom_call_target="tpu_custom_call" | custom-call | flops 603979776 | bytes 2359296 | tf_op jit(solution)/shard_map/pallas_call | solution.py:280
  15.3 0.9 %collective-permute-start.4 = (bf16[272,128]{1,0:T(8,128)(2,1)S(1)}, bf16[272,128]{1,0:T(8,128)(2,1)S(1)}, u32[]{:S(2)}, u32[]{:S(2)}) collective-permute-start(bf16[272,128]{1,0:T(8,128)(2,1)S(1)} %get-tuple-element.58), channel_id=1, source_target_pairs={{0,12},{4,8},{8,4},{12,0},{1,13},{5,9},{9,5},{13,1},{2,14},{6,10},... | collective-permute-start | bytes 208904 | tf_op jit(solution)/shard_map/ppermute | solution.py:613
  16.2 0.7 %collective-permute-start.5 = (bf16[272,128]{1,0:T(8,128)(2,1)S(1)}, bf16[272,128]{1,0:T(8,128)(2,1)S(1)}, u32[]{:S(2)}, u32[]{:S(2)}) collective-permute-start(bf16[272,128]{1,0:T(8,128)(2,1)S(1)} %get-tuple-element.59), channel_id=1, source_target_pairs={{0,8},{4,12},{8,0},{12,4},{1,9},{5,13},{9,1},{13,5},{2,10},{6,14},... | collective-permute-start | bytes 208904 | tf_op jit(solution)/shard_map/ppermute | solution.py:613
  16.9 1.9 %shard_map.96 = (bf16[512,2304]{1,0:T(8,128)(2,1)S(1)}, bf16[272,128]{1,0:T(8,128)(2,1)S(1)}, f32[272,128]{1,0:T(8,128)S(1)}) custom-call(bf16[192,256]{1,0:T(8,128)(2,1)S(1)} %get-tuple-element.53.left, f32[1,1536,128]{2,1,0:T(8,128)S(1)} %get-tuple-element.54.b_wide.refs_0_, bf16[2304,128]{1,0:T(8,128)(2,1)S(1)} %get-tuple-element.49.g_ref.refs_4_, ...), custom_call_target="tpu_custom_call" | custom-call | flops 603979776 | bytes 2359296 | tf_op jit(solution)/shard_map/pallas_call | solution.py:280
  18.8 0.4 collective-permute-start.6
  19.2 0.6 %collective-permute-done.4.refs_0_.refs_1_ = bf16[272,128]{1,0:T(8,128)(2,1)S(1)} collective-permute-done((bf16[272,128]{1,0:T(8,128)(2,1)S(1)}, bf16[272,128]{1,0:T(8,128)(2,1)S(1)}, u32[]{:S(2)}, u32[]{:S(2)}) %collective-permute-start.4) | collective-permute-done | bytes 69664 | tf_op jit(solution)/shard_map/ppermute | solution.py:613
  19.8 1.5 %collective-permute-done.5.refs_1_.refs_2_ = bf16[272,128]{1,0:T(8,128)(2,1)S(1)} collective-permute-done((bf16[272,128]{1,0:T(8,128)(2,1)S(1)}, bf16[272,128]{1,0:T(8,128)(2,1)S(1)}, u32[]{:S(2)}, u32[]{:S(2)}) %collective-permute-start.5) | collective-permute-done | bytes 69664 | tf_op jit(solution)/shard_map/ppermute | solution.py:613
  21.3 1.6 %shard_map.97 = (bf16[1024,2304]{1,0:T(8,128)(2,1)S(1)}, f32[1,1536,128]{2,1,0:T(8,128)S(1)}) custom-call(bf16[1024,128]{1,0:T(8,128)(2,1)S(1)} %get-tuple-element.61.left_ref, bf16[2304,128]{1,0:T(8,128)(2,1)S(1)} %get-tuple-element.62.right_ref, f32[32,1536]{1,0:T(8,128)S(1)} %get-tuple-element.63.held, ...), custom_call_target="tpu_custom_call" | custom-call | flops 603979776 | bytes 9437184 | tf_op jit(solution)/shard_map/pallas_call | solution.py:431
  22.9 1.6 %collective-permute-start.7 = (bf16[272,128]{1,0:T(8,128)(2,1)S(1)}, bf16[272,128]{1,0:T(8,128)(2,1)S(1)}, u32[]{:S(2)}, u32[]{:S(2)}) collective-permute-start(bf16[272,128]{1,0:T(8,128)(2,1)S(1)} %shard_map.98.refs_2_.own), channel_id=1, source_target_pairs={{0,1},{1,0},{2,3},{3,2},{4,5},{5,4},{6,7},{7,6},{8,9},{9,8},{10,11... | collective-permute-start | bytes 208904 | tf_op jit(solution)/shard_map/ppermute | solution.py:613
  24.6 2.1 %shard_map.99 = (f32[96,128]{1,0:T(8,128)S(1)}, f32[96,128]{1,0:T(8,128)S(1)}, bf16[192,128]{1,0:T(8,128)(2,1)S(1)}) custom-call(f32[1,1536,128]{2,1,0:T(8,128)S(1)} %get-tuple-element.54.b_wide.refs_0_, bf16[1024,2304]{1,0:T(8,128)(2,1)S(1)} %get-tuple-element.65.refs_1_, bf16[272,128]{1,0:T(8,128)(2,1)S(1)} %shard_map.98.refs_2_.own), custom_call_target="tpu_custom_call" | custom-call | flops 603979776 | bytes 4718592 | tf_op jit(solution)/shard_map/pallas_call | solution.py:402
  26.7 0.7 %collective-permute-done.7.near = bf16[272,128]{1,0:T(8,128)(2,1)S(1)} collective-permute-done((bf16[272,128]{1,0:T(8,128)(2,1)S(1)}, bf16[272,128]{1,0:T(8,128)(2,1)S(1)}, u32[]{:S(2)}, u32[]{:S(2)}) %collective-permute-start.7) | collective-permute-done | bytes 69664 | tf_op jit(solution)/shard_map/ppermute | solution.py:613
  27.3 1.0 %collective-permute-start.8 = (bf16[272,128]{1,0:T(8,128)(2,1)S(1)}, bf16[272,128]{1,0:T(8,128)(2,1)S(1)}, u32[]{:S(2)}, u32[]{:S(2)}) collective-permute-start(bf16[272,128]{1,0:T(8,128)(2,1)S(1)} %shard_map.100.refs_2_.refs_0_), channel_id=1, source_target_pairs={{0,2},{1,3},{2,0},{3,1},{4,6},{5,7},{6,4},{7,5},{8,10},{9,11},{10,... | collective-permute-start | bytes 208904 | tf_op jit(solution)/shard_map/ppermute | solution.py:613
  28.3 1.7 %collective-permute-start.9 = (bf16[192,128]{1,0:T(8,128)(2,1)S(1)}, bf16[192,128]{1,0:T(8,128)(2,1)S(1)}, u32[]{:S(2)}, u32[]{:S(2)}) collective-permute-start(bf16[192,128]{1,0:T(8,128)(2,1)S(1)} %get-tuple-element.66._), channel_id=1, source_target_pairs={{0,1},{1,0},{2,3},{3,2},{4,5},{5,4},{6,7},{7,6},{8,9},{9,8},{10,11... | collective-permute-start | bytes 147464 | tf_op jit(solution)/shard_map/ppermute | solution.py:613
  30.0 2.1 %shard_map.101 = (f32[96,128]{1,0:T(8,128)S(1)}, bf16[96,128]{1,0:T(8,128)(2,1)S(1)}, bf16[96,128]{1,0:T(8,128)(2,1)S(1)}, bf16[96,128]{1,0:T(8,128)(2,1)S(1)}) custom-call(f32[1,1536,128]{2,1,0:T(8,128)S(1)} %get-tuple-element.67.refs_0_, bf16[1024,2304]{1,0:T(8,128)(2,1)S(1)} %get-tuple-element.64.refs_4_.refs_1_, ...), custom_call_target="tpu_custom_call" | custom-call | flops 603979776 | bytes 4718592 | tf_op jit(solution)/shard_map/pallas_call | solution.py:402
  32.1 1.0 %collective-permute-done.9.refs_2_ = bf16[192,128]{1,0:T(8,128)(2,1)S(1)} collective-permute-done((bf16[192,128]{1,0:T(8,128)(2,1)S(1)}, bf16[192,128]{1,0:T(8,128)(2,1)S(1)}, u32[]{:S(2)}, u32[]{:S(2)}) %collective-permute-start.9) | collective-permute-done | bytes 49184 | tf_op jit(solution)/shard_map/ppermute | solution.py:613
  33.2 1.6 %collective-permute-start.13 = (bf16[96,128]{1,0:T(8,128)(2,1)S(1)}, bf16[96,128]{1,0:T(8,128)(2,1)S(1)}, u32[]{:S(2)}, u32[]{:S(2)}) collective-permute-start(bf16[96,128]{1,0:T(8,128)(2,1)S(1)} %get-tuple-element.79), channel_id=1, source_target_pairs={{0,2},{1,3},{2,0},{3,1},{4,6},{5,7},{6,4},{7,5},{8,10},{9,11},{10,... | collective-permute-start | bytes 73736 | tf_op jit(solution)/shard_map/ppermute | solution.py:613
  34.8 0.1 shard_map.103
  34.9 0.1 collective-permute-start.10
  34.9 1.2 %collective-permute-start.11 = (bf16[352,128]{1,0:T(8,128)(2,1)S(1)}, bf16[352,128]{1,0:T(8,128)(2,1)S(1)}, u32[]{:S(2)}, u32[]{:S(2)}) collective-permute-start(bf16[352,128]{1,0:T(8,128)(2,1)S(1)} %get-tuple-element.77), channel_id=1, source_target_pairs={{0,8},{4,12},{8,0},{12,4},{1,9},{5,13},{9,1},{13,5},{2,10},{6,14},... | collective-permute-start | bytes 270344 | tf_op jit(solution)/shard_map/ppermute | solution.py:613
  36.1 0.7 %collective-permute-start.12 = (bf16[352,128]{1,0:T(8,128)(2,1)S(1)}, bf16[352,128]{1,0:T(8,128)(2,1)S(1)}, u32[]{:S(2)}, u32[]{:S(2)}) collective-permute-start(bf16[352,128]{1,0:T(8,128)(2,1)S(1)} %get-tuple-element.78), channel_id=1, source_target_pairs={{0,4},{4,0},{8,12},{12,8},{1,5},{5,1},{9,13},{13,9},{2,6},{6,2},{1... | collective-permute-start | bytes 270344 | tf_op jit(solution)/shard_map/ppermute | solution.py:613
  36.8 2.6 %shard_map.104 = bf16[2304,128]{1,0:T(8,128)(2,1)} custom-call(bf16[512,2304]{1,0:T(8,128)(2,1)S(1)} %get-tuple-element.52.far_ref, bf16[512,2304]{1,0:T(8,128)(2,1)S(1)} %get-tuple-element.55.near_ref, bf16[4,128,256]{2,1,0:T(8,128)(2,1)S(1)} %get-tuple-element.56.wt_ref, f32[1,128]{1,0:T(1,128)S(1)} %bitcast.4, ...), custom_call_target="tpu_custom_call" | custom-call | flops 1207959552 | bytes 9437184 | tf_op jit(solution)/shard_map/pallas_call | solution.py:460
  39.4 0.5 %collective-permute-done.10.refs_1_ = bf16[352,128]{1,0:T(8,128)(2,1)S(1)} collective-permute-done((bf16[352,128]{1,0:T(8,128)(2,1)S(1)}, bf16[352,128]{1,0:T(8,128)(2,1)S(1)}, u32[]{:S(2)}, u32[]{:S(2)}) %collective-permute-start.10) | collective-permute-done | bytes 90144 | tf_op jit(solution)/shard_map/ppermute | solution.py:613
  39.8 1.3 %collective-permute-done.11.refs_2_ = bf16[352,128]{1,0:T(8,128)(2,1)S(1)} collective-permute-done((bf16[352,128]{1,0:T(8,128)(2,1)S(1)}, bf16[352,128]{1,0:T(8,128)(2,1)S(1)}, u32[]{:S(2)}, u32[]{:S(2)}) %collective-permute-start.11) | collective-permute-done | bytes 90144 | tf_op jit(solution)/shard_map/ppermute | solution.py:613
  41.1 1.2 %shard_map.105 = (f32[1024,128]{1,0:T(8,128)}, f32[8,1536]{1,0:T(8,128)}, f32[8,1536]{1,0:T(8,128)}, f32[1,128]{1,0:T(1,128)}) custom-call(bf16[256,128]{1,0:T(8,128)(2,1)S(1)} %get-tuple-element.75._.refs_0_, bf16[352,128]{1,0:T(8,128)(2,1)S(1)} %collective-permute-done.10.refs_1_, bf16[352,128]{1,0:T(8,128)(2,1)S(1)} %collective-permute-done.11.refs_2_, ...), custom_call_target="tpu_custom_call" | custom-call | tf_op jit(solution)/shard_map/pallas_call | solution.py:486
  (12 shorter events, 0.1 us)
Async XLA Ops:
  0.6 7.0 %collective-permute-start = (bf16[8,1536]{1,0:T(8,128)(2,1)}, bf16[8,1536]{1,0:T(8,128)(2,1)S(1)}, u32[]{:S(2)}, u32[]{:S(2)}) collective-permute-start(bf16[8,1536]{1,0:T(8,128)(2,1)} %a_hbm.1), channel_id=1, source_target_pairs={{0,2},{1,3},{2,0},{3,1},{4,6},{5,7},{6,4},{7,5},{8,10},{9,11},{10,... | collective-permute-start | bytes 73736 | tf_op jit(solution)/shard_map/ppermute | solution.py:613
  4.7 4.0 %collective-permute-start.1 = (bf16[8,1536]{1,0:T(8,128)(2,1)}, bf16[8,1536]{1,0:T(8,128)(2,1)S(1)}, u32[]{:S(2)}, u32[]{:S(2)}) collective-permute-start(bf16[8,1536]{1,0:T(8,128)(2,1)} %b_hbm.1), channel_id=1, source_target_pairs={{0,8},{4,12},{8,0},{12,4},{1,9},{5,13},{9,1},{13,5},{2,10},{6,14},... | collective-permute-start | bytes 73736 | tf_op jit(solution)/shard_map/ppermute | solution.py:613
  8.8 4.2 %collective-permute-start.2 = (bf16[16,1536]{1,0:T(8,128)(2,1)S(1)}, bf16[16,1536]{1,0:T(8,128)(2,1)S(1)}, u32[]{:S(2)}, u32[]{:S(2)}) collective-permute-start(bf16[16,1536]{1,0:T(8,128)(2,1)S(1)} %get-tuple-element.47.refs_0_), channel_id=1, source_target_pairs={{0,1},{1,0},{2,3},{3,2},{4,5},{5,4},{6,7},{7,6},{8,9},{9,8},{10,11... | collective-permute-start | bytes 147464 | tf_op jit(solution)/shard_map/ppermute | solution.py:613
  10.4 2.5 %collective-permute-start.3 = (bf16[16,1536]{1,0:T(8,128)(2,1)S(1)}, bf16[16,1536]{1,0:T(8,128)(2,1)S(1)}, u32[]{:S(2)}, u32[]{:S(2)}) collective-permute-start(bf16[16,1536]{1,0:T(8,128)(2,1)S(1)} %get-tuple-element.48.refs_2_), channel_id=1, source_target_pairs={{0,4},{4,0},{8,12},{12,8},{1,5},{5,1},{9,13},{13,9},{2,6},{6,2},{1... | collective-permute-start | bytes 147464 | tf_op jit(solution)/shard_map/ppermute | solution.py:613
  15.3 4.5 %collective-permute-start.4 = (bf16[272,128]{1,0:T(8,128)(2,1)S(1)}, bf16[272,128]{1,0:T(8,128)(2,1)S(1)}, u32[]{:S(2)}, u32[]{:S(2)}) collective-permute-start(bf16[272,128]{1,0:T(8,128)(2,1)S(1)} %get-tuple-element.58), channel_id=1, source_target_pairs={{0,12},{4,8},{8,4},{12,0},{1,13},{5,9},{9,5},{13,1},{2,14},{6,10},... | collective-permute-start | bytes 208904 | tf_op jit(solution)/shard_map/ppermute | solution.py:613
  16.2 5.1 %collective-permute-start.5 = (bf16[272,128]{1,0:T(8,128)(2,1)S(1)}, bf16[272,128]{1,0:T(8,128)(2,1)S(1)}, u32[]{:S(2)}, u32[]{:S(2)}) collective-permute-start(bf16[272,128]{1,0:T(8,128)(2,1)S(1)} %get-tuple-element.59), channel_id=1, source_target_pairs={{0,8},{4,12},{8,0},{12,4},{1,9},{5,13},{9,1},{13,5},{2,10},{6,14},... | collective-permute-start | bytes 208904 | tf_op jit(solution)/shard_map/ppermute | solution.py:613
  18.8 4.1 %collective-permute-start.6 = (bf16[272,128]{1,0:T(8,128)(2,1)S(1)}, bf16[272,128]{1,0:T(8,128)(2,1)S(1)}, u32[]{:S(2)}, u32[]{:S(2)}) collective-permute-start(bf16[272,128]{1,0:T(8,128)(2,1)S(1)} %get-tuple-element.60), channel_id=1, source_target_pairs={{0,4},{4,0},{8,12},{12,8},{1,5},{5,1},{9,13},{13,9},{2,6},{6,2},{1... | collective-permute-start | bytes 208904 | tf_op jit(solution)/shard_map/ppermute | solution.py:613
  22.9 4.4 %collective-permute-start.7 = (bf16[272,128]{1,0:T(8,128)(2,1)S(1)}, bf16[272,128]{1,0:T(8,128)(2,1)S(1)}, u32[]{:S(2)}, u32[]{:S(2)}) collective-permute-start(bf16[272,128]{1,0:T(8,128)(2,1)S(1)} %shard_map.98.refs_2_.own), channel_id=1, source_target_pairs={{0,1},{1,0},{2,3},{3,2},{4,5},{5,4},{6,7},{7,6},{8,9},{9,8},{10,11... | collective-permute-start | bytes 208904 | tf_op jit(solution)/shard_map/ppermute | solution.py:613
  24.6 12.2 %copy-start = (f32[128]{0:T(128)S(1)}, f32[128]{0:T(128)}, u32[]{:S(2)}) copy-start(f32[128]{0:T(128)} %param.8) | copy-start | bytes 1540
  27.3 7.5 %collective-permute-start.8 = (bf16[272,128]{1,0:T(8,128)(2,1)S(1)}, bf16[272,128]{1,0:T(8,128)(2,1)S(1)}, u32[]{:S(2)}, u32[]{:S(2)}) collective-permute-start(bf16[272,128]{1,0:T(8,128)(2,1)S(1)} %shard_map.100.refs_2_.refs_0_), channel_id=1, source_target_pairs={{0,2},{1,3},{2,0},{3,1},{4,6},{5,7},{6,4},{7,5},{8,10},{9,11},{10,... | collective-permute-start | bytes 208904 | tf_op jit(solution)/shard_map/ppermute | solution.py:613
  28.3 4.8 %collective-permute-start.9 = (bf16[192,128]{1,0:T(8,128)(2,1)S(1)}, bf16[192,128]{1,0:T(8,128)(2,1)S(1)}, u32[]{:S(2)}, u32[]{:S(2)}) collective-permute-start(bf16[192,128]{1,0:T(8,128)(2,1)S(1)} %get-tuple-element.66._), channel_id=1, source_target_pairs={{0,1},{1,0},{2,3},{3,2},{4,5},{5,4},{6,7},{7,6},{8,9},{9,8},{10,11... | collective-permute-start | bytes 147464 | tf_op jit(solution)/shard_map/ppermute | solution.py:613
  33.2 6.2 %collective-permute-start.13 = (bf16[96,128]{1,0:T(8,128)(2,1)S(1)}, bf16[96,128]{1,0:T(8,128)(2,1)S(1)}, u32[]{:S(2)}, u32[]{:S(2)}) collective-permute-start(bf16[96,128]{1,0:T(8,128)(2,1)S(1)} %get-tuple-element.79), channel_id=1, source_target_pairs={{0,2},{1,3},{2,0},{3,1},{4,6},{5,7},{6,4},{7,5},{8,10},{9,11},{10,... | collective-permute-start | bytes 73736 | tf_op jit(solution)/shard_map/ppermute | solution.py:613
  34.9 5.0 %collective-permute-start.10 = (bf16[352,128]{1,0:T(8,128)(2,1)S(1)}, bf16[352,128]{1,0:T(8,128)(2,1)S(1)}, u32[]{:S(2)}, u32[]{:S(2)}) collective-permute-start(bf16[352,128]{1,0:T(8,128)(2,1)S(1)} %get-tuple-element.76), channel_id=1, source_target_pairs={{0,12},{4,8},{8,4},{12,0},{1,13},{5,9},{9,5},{13,1},{2,14},{6,10},... | collective-permute-start | bytes 270344 | tf_op jit(solution)/shard_map/ppermute | solution.py:613
  34.9 6.2 %collective-permute-start.11 = (bf16[352,128]{1,0:T(8,128)(2,1)S(1)}, bf16[352,128]{1,0:T(8,128)(2,1)S(1)}, u32[]{:S(2)}, u32[]{:S(2)}) collective-permute-start(bf16[352,128]{1,0:T(8,128)(2,1)S(1)} %get-tuple-element.77), channel_id=1, source_target_pairs={{0,8},{4,12},{8,0},{12,4},{1,9},{5,13},{9,1},{13,5},{2,10},{6,14},... | collective-permute-start | bytes 270344 | tf_op jit(solution)/shard_map/ppermute | solution.py:613
  36.1 5.0 %collective-permute-start.12 = (bf16[352,128]{1,0:T(8,128)(2,1)S(1)}, bf16[352,128]{1,0:T(8,128)(2,1)S(1)}, u32[]{:S(2)}, u32[]{:S(2)}) collective-permute-start(bf16[352,128]{1,0:T(8,128)(2,1)S(1)} %get-tuple-element.78), channel_id=1, source_target_pairs={{0,4},{4,0},{8,12},{12,8},{1,5},{5,1},{9,13},{13,9},{2,6},{6,2},{1... | collective-permute-start | bytes 270344 | tf_op jit(solution)/shard_map/ppermute | solution.py:613

commit v17 on v14

--- a/solution.py
+++ b/solution.py
@@ -266,10 +266,8 @@
     share = total.shape[0] // row_n
     me = lax.axis_index("row")
     for p, message in enumerate(messages):
-        part = lax.bitwise_xor(me, p)
-        for n in range(share // depth):
-            block = total[pl.ds(part * (share // depth) + n, depth, stride=depth), :]
-            message[n * depth : (n + 1) * depth, :] = block.astype(message.dtype)
+        part = pl.ds(pl.multiple_of(lax.bitwise_xor(me, p) * share, share), share)
+        message[0:share, :] = total[part, :].astype(message.dtype)
         message[share:, :] = bias_ref[...].astype(message.dtype)
 
 
@@ -524,7 +522,7 @@
 
     def kernel(*refs):
         parts, grads, refs = refs[:count], refs[count : count + sent], refs[count + sent :]
-        messages, (piece_out, bias_out, held) = refs[:sent], refs[sent:]
+        messages, (piece_out, bias_out, held, by_e, by_c) = refs[:sent], refs[sent:]
         home = lax.div(lax.axis_index("col"), 2)
         for p, part in enumerate(parts):
             held[lax.bitwise_xor(home, p)] = part[...]
@@ -532,7 +530,12 @@
         for n in range(1, count):
             total += held[n, 0:share, :].astype(F32)
             bias += joined(held[n, share:, :])
-        piece = total.astype(BF16)
+        by_e[...] = total
+        depth = PROJECTED_DEPTH
+        width = share // depth
+        for c in range(depth):
+            by_c[c * width : (c + 1) * width, :] = by_e[pl.ds(c, width, stride=depth), :]
+        piece = by_c[...].astype(BF16)
         piece_out[...] = piece
         for message, grad in zip(messages, grads, strict=True):
             message[0:share, :] = piece
@@ -541,7 +544,7 @@
 
     shapes = [((share + grad.shape[0], LANES), BF16) for grad in grads]
     shapes += [((share, LANES), BF16), ((8, LANES), F32)]
-    scratch = [pltpu.VMEM((count, rows, LANES), BF16)]
+    scratch = [pltpu.VMEM((count, rows, LANES), BF16)] + [pltpu.VMEM((share, LANES), F32)] * 2
     *messages, piece, bias = call(kernel, [*parts, *grads], shapes, scratch=scratch)
     return messages, piece, bias
 
@@ -555,9 +558,13 @@
         right_own, bias, projection, left_out, right_out, bias_out = refs
         me = lax.axis_index("row")
         right_total = right_own[...]
+        depth = PROJECTED_DEPTH
+        width = share // depth
         for p, piece in zip(partners(count), pieces, strict=True):
-            rows = pl.ds(pl.multiple_of(lax.bitwise_xor(me, p) * share, share), share)
-            projection[rows, :] = piece[0:share, :].astype(F32) * scale
+            block = piece[0:share, :].astype(F32) * scale
+            for c in range(depth):
+                start = c * depth + pl.multiple_of(lax.bitwise_xor(me, p) * width, width)
+                projection[pl.ds(start, width), :] = block[c * width : (c + 1) * width]
             if p > 0:
                 right_total += piece[share:, :].astype(F32)
         left_total = left[0][...]

time: 41.4 us -> 41.2 us (level)
  no operation moved by 1% of the time
where the time goes in v17:
time: 41.2 us; the launch traced here: 41 us
  starting transfers between devices  17.8 us (43%)
  Pallas kernels  16.9 us (41%)
  waiting for transfers between devices  5.69 us (14%)
  between operations  0.72 us (2%)
    ppermute x14, starting transfers between devices, swap(): lax.ppermute(x, axis, [(n, n ^ p) for n in range(lax.axis_size(axis))])  17.8 us
    ppermute x14, waiting for transfers between devices, swap(): lax.ppermute(x, axis, [(n, n ^ p) for n in range(lax.axis_size(axis))])  5.69 us
    pallas_call x1, Pallas kernels, outer(): pl.pallas_call(functools.partial(outer_kernel, i_n, j_n), in_specs=[in_vm...  4.39 us
    pallas_call x2, Pallas kernels, gradient(): pl.pallas_call(functools.partial(gradient_kernel, axis, plan, kept, posit...  4.12 us
    pallas_call x1, Pallas kernels, pair(): pl.pallas_call(functools.partial(pair_kernel, sequences), grid=(count,),...  2.55 us
    pallas_call x1, Pallas kernels, prepare(): pl.pallas_call(functools.partial(prepare_kernel, i_n, j_n), in_specs=[in_...  1.75 us
    pallas_call x1, Pallas kernels, product(): pl.pallas_call(product_kernel, in_specs=[in_vmem()] * 3 + [pl.BlockSpec(m...  1.55 us
    pallas_call x1, Pallas kernels, load(): pl.pallas_call(load_kernel, in_specs=[pl.BlockSpec(memory_space=pltpu.HBM...  1.39 us
  transfers between devices with their start and end apart: 14, of which 7 were waited for; matrix products, arithmetic and copies ran while one was open for 0% of the time, Pallas kernels for 28%

profile of v17, /device:TPU:0, one launch (start us, length us, event | category | flops | bytes accessed | tf_op | source)
XLA Modules:
  0.0 41.0 jit_solution(335115928601525471)
XLA Ops:
  0.6 4.1 %collective-permute-start = (bf16[8,1536]{1,0:T(8,128)(2,1)}, bf16[8,1536]{1,0:T(8,128)(2,1)S(1)}, u32[]{:S(2)}, u32[]{:S(2)}) collective-permute-start(bf16[8,1536]{1,0:T(8,128)(2,1)} %a_hbm.1), channel_id=1, source_target_pairs={{0,2},{1,3},{2,0},{3,1},{4,6},{5,7},{6,4},{7,5},{8,10},{9,11},{10,... | collective-permute-start | bytes 73736 | tf_op jit(solution)/shard_map/ppermute | solution.py:587
  4.7 1.5 %collective-permute-start.1 = (bf16[8,1536]{1,0:T(8,128)(2,1)}, bf16[8,1536]{1,0:T(8,128)(2,1)S(1)}, u32[]{:S(2)}, u32[]{:S(2)}) collective-permute-start(bf16[8,1536]{1,0:T(8,128)(2,1)} %b_hbm.1), channel_id=1, source_target_pairs={{0,8},{4,12},{8,0},{12,4},{1,9},{5,13},{9,1},{13,5},{2,10},{6,14},... | collective-permute-start | bytes 73736 | tf_op jit(solution)/shard_map/ppermute | solution.py:587
  6.2 1.4 %shard_map.92 = (bf16[1024,128]{1,0:T(8,128)(2,1)S(1)}, bf16[128,1024]{1,0:T(8,128)(2,1)S(1)}, bf16[8,1536]{1,0:T(8,128)(2,1)S(1)}, bf16[8,1536]{1,0:T(8,128)(2,...) custom-call(bf16[8,1536]{1,0:T(8,128)(2,1)} %a_hbm.1, bf16[8,1536]{1,0:T(8,128)(2,1)} %b_hbm.1, ...), custom_call_target="tpu_custom_call" | custom-call | flops 131072000 | bytes 2097152 | tf_op jit(solution)/shard_map/pallas_call | solution.py:67
  7.6 0.0 collective-permute-done.refs_1_
  7.6 1.1 %collective-permute-done.1.refs_3_ = bf16[8,1536]{1,0:T(8,128)(2,1)S(1)} collective-permute-done((bf16[8,1536]{1,0:T(8,128)(2,1)}, bf16[8,1536]{1,0:T(8,128)(2,1)S(1)}, u32[]{:S(2)}, u32[]{:S(2)}) %collective-permute-start.1) | collective-permute-done | bytes 24608 | tf_op jit(solution)/shard_map/ppermute | solution.py:587
  8.8 1.6 %collective-permute-start.2 = (bf16[16,1536]{1,0:T(8,128)(2,1)S(1)}, bf16[16,1536]{1,0:T(8,128)(2,1)S(1)}, u32[]{:S(2)}, u32[]{:S(2)}) collective-permute-start(bf16[16,1536]{1,0:T(8,128)(2,1)S(1)} %get-tuple-element.45.refs_0_), channel_id=1, source_target_pairs={{0,1},{1,0},{2,3},{3,2},{4,5},{5,4},{6,7},{7,6},{8,9},{9,8},{10,11... | collective-permute-start | bytes 147464 | tf_op jit(solution)/shard_map/ppermute | solution.py:587
  10.4 0.0 collective-permute-start.3
  10.4 1.8 %shard_map.94 = (bf16[1024,2304]{1,0:T(8,128)(2,1)S(1)}, bf16[2304,128]{1,0:T(8,128)(2,1)S(1)}, bf16[16,128]{1,0:T(8,128)(2,1)S(1)}) custom-call(bf16[1024,128]{1,0:T(8,128)(2,1)S(1)} %get-tuple-element.48.we_ref, bf16[2304,128]{1,0:T(8,128)(2,1)S(1)} %get-tuple-element.47.g_ref.refs_4_), custom_call_target="tpu_custom_call" | custom-call | flops 603979776 | bytes 9437184 | tf_op jit(solution)/shard_map/pallas_call | solution.py:126
  12.2 0.8 %collective-permute-done.2.refs_1_ = bf16[16,1536]{1,0:T(8,128)(2,1)S(1)} collective-permute-done((bf16[16,1536]{1,0:T(8,128)(2,1)S(1)}, bf16[16,1536]{1,0:T(8,128)(2,1)S(1)}, u32[]{:S(2)}, u32[]{:S(2)}) %collective-permute-start.2) | collective-permute-done | bytes 49184 | tf_op jit(solution)/shard_map/ppermute | solution.py:587
  12.9 0.0 collective-permute-done.3.refs_3_
  12.9 4.4 %shard_map.95 = (bf16[1024,2304]{1,0:T(8,128)(2,1)S(1)}, f32[32,1536]{1,0:T(8,128)S(1)}, f32[1,1536,128]{2,1,0:T(8,128)S(1)}, f32[272,128]{1,0:T(8,128)S(1)}, bf...) custom-call(bf16[16,1536]{1,0:T(8,128)(2,1)S(1)} %get-tuple-element.45.refs_0_, ...), custom_call_target="tpu_custom_call" | custom-call | flops 1207959552 | bytes 4718592 | tf_op jit(solution)/shard_map/pallas_call | solution.py:290
  17.3 0.9 %collective-permute-start.4 = (bf16[272,128]{1,0:T(8,128)(2,1)S(1)}, bf16[272,128]{1,0:T(8,128)(2,1)S(1)}, u32[]{:S(2)}, u32[]{:S(2)}) collective-permute-start(bf16[272,128]{1,0:T(8,128)(2,1)S(1)} %get-tuple-element.53), channel_id=1, source_target_pairs={{0,12},{4,8},{8,4},{12,0},{1,13},{5,9},{9,5},{13,1},{2,14},{6,10},... | collective-permute-start | bytes 208904 | tf_op jit(solution)/shard_map/ppermute | solution.py:587
  18.3 0.7 %collective-permute-start.5 = (bf16[272,128]{1,0:T(8,128)(2,1)S(1)}, bf16[272,128]{1,0:T(8,128)(2,1)S(1)}, u32[]{:S(2)}, u32[]{:S(2)}) collective-permute-start(bf16[272,128]{1,0:T(8,128)(2,1)S(1)} %get-tuple-element.54), channel_id=1, source_target_pairs={{0,8},{4,12},{8,0},{12,4},{1,9},{5,13},{9,1},{13,5},{2,10},{6,14},... | collective-permute-start | bytes 208904 | tf_op jit(solution)/shard_map/ppermute | solution.py:587
  19.0 0.3 collective-permute-start.6
  19.3 2.1 %shard_map.96 = (f32[96,128]{1,0:T(8,128)S(1)}, f32[96,128]{1,0:T(8,128)S(1)}, bf16[192,128]{1,0:T(8,128)(2,1)S(1)}) custom-call(f32[1,1536,128]{2,1,0:T(8,128)S(1)} %get-tuple-element.56.refs_0_, bf16[1024,2304]{1,0:T(8,128)(2,1)S(1)} %get-tuple-element.57.refs_1_, f32[272,128]{1,0:T(8,128)S(1)} %get-tuple-element.52.refs_2_.refs_0_), custom_call_target="tpu_custom_call" | custom-call | flops 603979776 | bytes 4718592 | tf_op jit(solution)/shard_map/pallas_call | solution.py:378
  21.3 1.6 %collective-permute-start.8 = (bf16[192,128]{1,0:T(8,128)(2,1)S(1)}, bf16[192,128]{1,0:T(8,128)(2,1)S(1)}, u32[]{:S(2)}, u32[]{:S(2)}) collective-permute-start(bf16[192,128]{1,0:T(8,128)(2,1)S(1)} %get-tuple-element.58.refs_4_), channel_id=1, source_target_pairs={{0,1},{1,0},{2,3},{3,2},{4,5},{5,4},{6,7},{7,6},{8,9},{9,8},{10,11... | collective-permute-start | bytes 147464 | tf_op jit(solution)/shard_map/ppermute | solution.py:587
  23.0 0.4 collective-permute-done.5.refs_2_
  23.4 1.6 %collective-permute-start.7 = (bf16[272,128]{1,0:T(8,128)(2,1)S(1)}, bf16[272,128]{1,0:T(8,128)(2,1)S(1)}, u32[]{:S(2)}, u32[]{:S(2)}) collective-permute-start(bf16[272,128]{1,0:T(8,128)(2,1)S(1)} %shard_map.97.refs_3_.own), channel_id=1, source_target_pairs={{0,1},{1,0},{2,3},{3,2},{4,5},{5,4},{6,7},{7,6},{8,9},{9,8},{10,11... | collective-permute-start | bytes 208904 | tf_op jit(solution)/shard_map/ppermute | solution.py:587
  25.1 0.4 %collective-permute-done.8.refs_2_ = bf16[192,128]{1,0:T(8,128)(2,1)S(1)} collective-permute-done((bf16[192,128]{1,0:T(8,128)(2,1)S(1)}, bf16[192,128]{1,0:T(8,128)(2,1)S(1)}, u32[]{:S(2)}, u32[]{:S(2)}) %collective-permute-start.8) | collective-permute-done | bytes 49184 | tf_op jit(solution)/shard_map/ppermute | solution.py:587
  25.5 1.5 %shard_map.99 = (bf16[1024,2304]{1,0:T(8,128)(2,1)S(1)}, f32[1,1536,128]{2,1,0:T(8,128)S(1)}) custom-call(bf16[1024,128]{1,0:T(8,128)(2,1)S(1)} %get-tuple-element.59.left_ref, bf16[2304,128]{1,0:T(8,128)(2,1)S(1)} %get-tuple-element.60.right_ref, f32[32,1536]{1,0:T(8,128)S(1)} %get-tuple-element.61.held, f32[96,128]{1,0:T(8,128)S(1)} %get-tuple-element.64._.refs_4_), custom_call_target="tpu_custom_call" | custom-call | flops 603979776 | bytes 9437184 | tf_op jit(solution)/shard_map/pallas_call | solution.py:406
  27.1 0.7 %collective-permute-done.7.near = bf16[272,128]{1,0:T(8,128)(2,1)S(1)} collective-permute-done((bf16[272,128]{1,0:T(8,128)(2,1)S(1)}, bf16[272,128]{1,0:T(8,128)(2,1)S(1)}, u32[]{:S(2)}, u32[]{:S(2)}) %collective-permute-start.7) | collective-permute-done | bytes 69664 | tf_op jit(solution)/shard_map/ppermute | solution.py:587
  27.8 1.0 %collective-permute-start.9 = (bf16[272,128]{1,0:T(8,128)(2,1)S(1)}, bf16[272,128]{1,0:T(8,128)(2,1)S(1)}, u32[]{:S(2)}, u32[]{:S(2)}) collective-permute-start(bf16[272,128]{1,0:T(8,128)(2,1)S(1)} %shard_map.100.refs_2_.refs_0_), channel_id=1, source_target_pairs={{0,2},{1,3},{2,0},{3,1},{4,6},{5,7},{6,4},{7,5},{8,10},{9,11},{10,... | collective-permute-start | bytes 208904 | tf_op jit(solution)/shard_map/ppermute | solution.py:587
  28.8 2.0 %collective-permute-start.13 = (bf16[96,128]{1,0:T(8,128)(2,1)S(1)}, bf16[96,128]{1,0:T(8,128)(2,1)S(1)}, u32[]{:S(2)}, u32[]{:S(2)}) collective-permute-start(bf16[96,128]{1,0:T(8,128)(2,1)S(1)} %get-tuple-element.74), channel_id=1, source_target_pairs={{0,2},{1,3},{2,0},{3,1},{4,6},{5,7},{6,4},{7,5},{8,10},{9,11},{10,... | collective-permute-start | bytes 73736 | tf_op jit(solution)/shard_map/ppermute | solution.py:587
  30.8 2.1 %shard_map.101 = (f32[96,128]{1,0:T(8,128)S(1)}, bf16[96,128]{1,0:T(8,128)(2,1)S(1)}, bf16[96,128]{1,0:T(8,128)(2,1)S(1)}, bf16[96,128]{1,0:T(8,128)(2,1)S(1)}) custom-call(f32[1,1536,128]{2,1,0:T(8,128)S(1)} %get-tuple-element.66.refs_0_, bf16[1024,2304]{1,0:T(8,128)(2,1)S(1)} %get-tuple-element.65._.refs_1_, bf16[272,128]{1,0:T(8,128)(2,1)S(1)} %shard_map.100.refs_2_.refs_0_), custom_call_target="tpu_custom_call" | custom-call | flops 603979776 | bytes 4718592 | tf_op jit(solution)/shard_map/pallas_call | solution.py:378
  32.9 0.2 collective-permute-done.9.refs_1_
  33.1 0.1 shard_map.102
  33.2 0.1 collective-permute-start.10
  33.3 2.2 %collective-permute-start.11 = (bf16[352,128]{1,0:T(8,128)(2,1)S(1)}, bf16[352,128]{1,0:T(8,128)(2,1)S(1)}, u32[]{:S(2)}, u32[]{:S(2)}) collective-permute-start(bf16[352,128]{1,0:T(8,128)(2,1)S(1)} %get-tuple-element.72), channel_id=1, source_target_pairs={{0,8},{4,12},{8,0},{12,4},{1,9},{5,13},{9,1},{13,5},{2,10},{6,14},... | collective-permute-start | bytes 270344 | tf_op jit(solution)/shard_map/ppermute | solution.py:587
  35.5 0.0 collective-permute-start.12
  35.6 2.5 %shard_map.103 = bf16[2304,128]{1,0:T(8,128)(2,1)} custom-call(bf16[1024,2304]{1,0:T(8,128)(2,1)S(1)} %get-tuple-element.50.x_ref, bf16[128,1024]{1,0:T(8,128)(2,1)S(1)} %get-tuple-element.51.wt_ref, f32[1,128]{1,0:T(1,128)S(1)} %bitcast.4, bf16[256,128]{1,0:T(8,128)(2,1)S(1)} %get-tuple-element.70._.refs_0_), custom_call_target="tpu_custom_call" | custom-call | flops 1207959552 | bytes 4718592 | tf_op jit(solution)/shard_map/pallas_call | solution.py:429
  38.1 2.0 %collective-permute-done.11.refs_2_ = bf16[352,128]{1,0:T(8,128)(2,1)S(1)} collective-permute-done((bf16[352,128]{1,0:T(8,128)(2,1)S(1)}, bf16[352,128]{1,0:T(8,128)(2,1)S(1)}, u32[]{:S(2)}, u32[]{:S(2)}) %collective-permute-start.11) | collective-permute-done | bytes 90144 | tf_op jit(solution)/shard_map/ppermute | solution.py:587
  40.2 0.9 %shard_map.104 = (f32[1024,128]{1,0:T(8,128)}, f32[8,1536]{1,0:T(8,128)}, f32[8,1536]{1,0:T(8,128)}, f32[1,128]{1,0:T(1,128)}) custom-call(bf16[256,128]{1,0:T(8,128)(2,1)S(1)} %get-tuple-element.70._.refs_0_, bf16[352,128]{1,0:T(8,128)(2,1)S(1)} %collective-permute-done.10.refs_1_, bf16[352,128]{1,0:T(8,128)(2,1)S(1)} %collective-permute-done.11.refs_2_, ...), custom_call_target="tpu_custom_call" | custom-call | tf_op jit(solution)/shard_map/pallas_call | solution.py:456
  (11 shorter events, 0.1 us)
Async XLA Ops:
  0.6 7.0 %collective-permute-start = (bf16[8,1536]{1,0:T(8,128)(2,1)}, bf16[8,1536]{1,0:T(8,128)(2,1)S(1)}, u32[]{:S(2)}, u32[]{:S(2)}) collective-permute-start(bf16[8,1536]{1,0:T(8,128)(2,1)} %a_hbm.1), channel_id=1, source_target_pairs={{0,2},{1,3},{2,0},{3,1},{4,6},{5,7},{6,4},{7,5},{8,10},{9,11},{10,... | collective-permute-start | bytes 73736 | tf_op jit(solution)/shard_map/ppermute | solution.py:587
  4.7 4.0 %collective-permute-start.1 = (bf16[8,1536]{1,0:T(8,128)(2,1)}, bf16[8,1536]{1,0:T(8,128)(2,1)S(1)}, u32[]{:S(2)}, u32[]{:S(2)}) collective-permute-start(bf16[8,1536]{1,0:T(8,128)(2,1)} %b_hbm.1), channel_id=1, source_target_pairs={{0,8},{4,12},{8,0},{12,4},{1,9},{5,13},{9,1},{13,5},{2,10},{6,14},... | collective-permute-start | bytes 73736 | tf_op jit(solution)/shard_map/ppermute | solution.py:587
  8.8 4.2 %collective-permute-start.2 = (bf16[16,1536]{1,0:T(8,128)(2,1)S(1)}, bf16[16,1536]{1,0:T(8,128)(2,1)S(1)}, u32[]{:S(2)}, u32[]{:S(2)}) collective-permute-start(bf16[16,1536]{1,0:T(8,128)(2,1)S(1)} %get-tuple-element.45.refs_0_), channel_id=1, source_target_pairs={{0,1},{1,0},{2,3},{3,2},{4,5},{5,4},{6,7},{7,6},{8,9},{9,8},{10,11... | collective-permute-start | bytes 147464 | tf_op jit(solution)/shard_map/ppermute | solution.py:587
  10.4 2.5 %collective-permute-start.3 = (bf16[16,1536]{1,0:T(8,128)(2,1)S(1)}, bf16[16,1536]{1,0:T(8,128)(2,1)S(1)}, u32[]{:S(2)}, u32[]{:S(2)}) collective-permute-start(bf16[16,1536]{1,0:T(8,128)(2,1)S(1)} %get-tuple-element.46.refs_2_), channel_id=1, source_target_pairs={{0,4},{4,0},{8,12},{12,8},{1,5},{5,1},{9,13},{13,9},{2,6},{6,2},{1... | collective-permute-start | bytes 147464 | tf_op jit(solution)/shard_map/ppermute | solution.py:587
  17.3 5.6 %collective-permute-start.4 = (bf16[272,128]{1,0:T(8,128)(2,1)S(1)}, bf16[272,128]{1,0:T(8,128)(2,1)S(1)}, u32[]{:S(2)}, u32[]{:S(2)}) collective-permute-start(bf16[272,128]{1,0:T(8,128)(2,1)S(1)} %get-tuple-element.53), channel_id=1, source_target_pairs={{0,12},{4,8},{8,4},{12,0},{1,13},{5,9},{9,5},{13,1},{2,14},{6,10},... | collective-permute-start | bytes 208904 | tf_op jit(solution)/shard_map/ppermute | solution.py:587
  18.3 5.1 %collective-permute-start.5 = (bf16[272,128]{1,0:T(8,128)(2,1)S(1)}, bf16[272,128]{1,0:T(8,128)(2,1)S(1)}, u32[]{:S(2)}, u32[]{:S(2)}) collective-permute-start(bf16[272,128]{1,0:T(8,128)(2,1)S(1)} %get-tuple-element.54), channel_id=1, source_target_pairs={{0,8},{4,12},{8,0},{12,4},{1,9},{5,13},{9,1},{13,5},{2,10},{6,14},... | collective-permute-start | bytes 208904 | tf_op jit(solution)/shard_map/ppermute | solution.py:587
  19.0 4.4 %collective-permute-start.6 = (bf16[272,128]{1,0:T(8,128)(2,1)S(1)}, bf16[272,128]{1,0:T(8,128)(2,1)S(1)}, u32[]{:S(2)}, u32[]{:S(2)}) collective-permute-start(bf16[272,128]{1,0:T(8,128)(2,1)S(1)} %get-tuple-element.55), channel_id=1, source_target_pairs={{0,4},{4,0},{8,12},{12,8},{1,5},{5,1},{9,13},{13,9},{2,6},{6,2},{1... | collective-permute-start | bytes 208904 | tf_op jit(solution)/shard_map/ppermute | solution.py:587
  21.3 4.2 %collective-permute-start.8 = (bf16[192,128]{1,0:T(8,128)(2,1)S(1)}, bf16[192,128]{1,0:T(8,128)(2,1)S(1)}, u32[]{:S(2)}, u32[]{:S(2)}) collective-permute-start(bf16[192,128]{1,0:T(8,128)(2,1)S(1)} %get-tuple-element.58.refs_4_), channel_id=1, source_target_pairs={{0,1},{1,0},{2,3},{3,2},{4,5},{5,4},{6,7},{7,6},{8,9},{9,8},{10,11... | collective-permute-start | bytes 147464 | tf_op jit(solution)/shard_map/ppermute | solution.py:587
  23.4 4.4 %collective-permute-start.7 = (bf16[272,128]{1,0:T(8,128)(2,1)S(1)}, bf16[272,128]{1,0:T(8,128)(2,1)S(1)}, u32[]{:S(2)}, u32[]{:S(2)}) collective-permute-start(bf16[272,128]{1,0:T(8,128)(2,1)S(1)} %shard_map.97.refs_3_.own), channel_id=1, source_target_pairs={{0,1},{1,0},{2,3},{3,2},{4,5},{5,4},{6,7},{7,6},{8,9},{9,8},{10,11... | collective-permute-start | bytes 208904 | tf_op jit(solution)/shard_map/ppermute | solution.py:587
  27.8 7.8 %copy-start = (f32[128]{0:T(128)S(1)}, f32[128]{0:T(128)}, u32[]{:S(2)}) copy-start(f32[128]{0:T(128)} %param.8) | copy-start | bytes 1540
  27.8 5.3 %collective-permute-start.9 = (bf16[272,128]{1,0:T(8,128)(2,1)S(1)}, bf16[272,128]{1,0:T(8,128)(2,1)S(1)}, u32[]{:S(2)}, u32[]{:S(2)}) collective-permute-start(bf16[272,128]{1,0:T(8,128)(2,1)S(1)} %shard_map.100.refs_2_.refs_0_), channel_id=1, source_target_pairs={{0,2},{1,3},{2,0},{3,1},{4,6},{5,7},{6,4},{7,5},{8,10},{9,11},{10,... | collective-permute-start | bytes 208904 | tf_op jit(solution)/shard_map/ppermute | solution.py:587
  28.8 9.3 %collective-permute-start.13 = (bf16[96,128]{1,0:T(8,128)(2,1)S(1)}, bf16[96,128]{1,0:T(8,128)(2,1)S(1)}, u32[]{:S(2)}, u32[]{:S(2)}) collective-permute-start(bf16[96,128]{1,0:T(8,128)(2,1)S(1)} %get-tuple-element.74), channel_id=1, source_target_pairs={{0,2},{1,3},{2,0},{3,1},{4,6},{5,7},{6,4},{7,5},{8,10},{9,11},{10,... | collective-permute-start | bytes 73736 | tf_op jit(solution)/shard_map/ppermute | solution.py:587
  33.2 4.9 %collective-permute-start.10 = (bf16[352,128]{1,0:T(8,128)(2,1)S(1)}, bf16[352,128]{1,0:T(8,128)(2,1)S(1)}, u32[]{:S(2)}, u32[]{:S(2)}) collective-permute-start(bf16[352,128]{1,0:T(8,128)(2,1)S(1)} %get-tuple-element.71), channel_id=1, source_target_pairs={{0,12},{4,8},{8,4},{12,0},{1,13},{5,9},{9,5},{13,1},{2,14},{6,10},... | collective-permute-start | bytes 270344 | tf_op jit(solution)/shard_map/ppermute | solution.py:587
  33.3 6.8 %collective-permute-start.11 = (bf16[352,128]{1,0:T(8,128)(2,1)S(1)}, bf16[352,128]{1,0:T(8,128)(2,1)S(1)}, u32[]{:S(2)}, u32[]{:S(2)}) collective-permute-start(bf16[352,128]{1,0:T(8,128)(2,1)S(1)} %get-tuple-element.72), channel_id=1, source_target_pairs={{0,8},{4,12},{8,0},{12,4},{1,9},{5,13},{9,1},{13,5},{2,10},{6,14},... | collective-permute-start | bytes 270344 | tf_op jit(solution)/shard_map/ppermute | solution.py:587
  35.5 4.6 %collective-permute-start.12 = (bf16[352,128]{1,0:T(8,128)(2,1)S(1)}, bf16[352,128]{1,0:T(8,128)(2,1)S(1)}, u32[]{:S(2)}, u32[]{:S(2)}) collective-permute-start(bf16[352,128]{1,0:T(8,128)(2,1)S(1)} %get-tuple-element.73), channel_id=1, source_target_pairs={{0,4},{4,0},{8,12},{12,8},{1,5},{5,1},{9,13},{13,9},{2,6},{6,2},{1... | collective-permute-start | bytes 270344 | tf_op jit(solution)/shard_map/ppermute | solution.py:587

commit v18 on v17

--- a/solution.py
+++ b/solution.py
@@ -10,8 +10,8 @@
 PROJECTED_DEPTH = 32
 PAIR_FEATURES = 128
 GROUP = 8
-MULTIPLY_ROWS = 384
-CHUNKS = 2
+MULTIPLY_ROWS = 768
+CHUNKS = 4
 BIAS_ROWS = 16
 LANES = 128
 F32 = jnp.float32

time: 41.2 us -> 41.7 us (1.012)
  Pallas kernels: 16.9 us -> 18 us
    pallas_call x2, Pallas kernels: 4.12 us -> 4.91 us  [gradient(): pl.pallas_call(functools.partial(gradient_kernel, axis, plan, kept, posit...]
  transfers between devices with their start and end apart: 14 -> 14, of which waited for: 7 -> 6; matrix products, arithmetic and copies ran while one was open for 0% -> 0% of each run, Pallas kernels for 28% -> 30%
where the time goes in v18:
time: 41.7 us; the launch traced here: 41.6 us
  Pallas kernels  18 us (43%)
  starting transfers between devices  17.4 us (42%)
  waiting for transfers between devices  5.51 us (13%)
  between operations  0.73 us (2%)
    ppermute x14, starting transfers between devices, swap(): lax.ppermute(x, axis, [(n, n ^ p) for n in range(lax.axis_size(axis))])  17.4 us
    ppermute x14, waiting for transfers between devices, swap(): lax.ppermute(x, axis, [(n, n ^ p) for n in range(lax.axis_size(axis))])  5.51 us
    pallas_call x2, Pallas kernels, gradient(): pl.pallas_call(functools.partial(gradient_kernel, axis, plan, kept, posit...  4.91 us
    pallas_call x1, Pallas kernels, outer(): pl.pallas_call(functools.partial(outer_kernel, i_n, j_n), in_specs=[in_vm...  4.72 us
    pallas_call x1, Pallas kernels, pair(): pl.pallas_call(functools.partial(pair_kernel, sequences), grid=(count,),...  2.55 us
    pallas_call x1, Pallas kernels, prepare(): pl.pallas_call(functools.partial(prepare_kernel, i_n, j_n), in_specs=[in_...  1.75 us
    pallas_call x1, Pallas kernels, product(): pl.pallas_call(product_kernel, in_specs=[in_vmem()] * 3 + [pl.BlockSpec(m...  1.55 us
    pallas_call x1, Pallas kernels, load(): pl.pallas_call(load_kernel, in_specs=[pl.BlockSpec(memory_space=pltpu.HBM...  1.39 us
  transfers between devices with their start and end apart: 14, of which 6 were waited for; matrix products, arithmetic and copies ran while one was open for 0% of the time, Pallas kernels for 30%

profile of v18, /device:TPU:0, one launch (start us, length us, event | category | flops | bytes accessed | tf_op | source)
XLA Modules:
  0.0 41.6 jit_solution(15379886365214978506)
XLA Ops:
  0.6 4.1 %collective-permute-start = (bf16[8,1536]{1,0:T(8,128)(2,1)}, bf16[8,1536]{1,0:T(8,128)(2,1)S(1)}, u32[]{:S(2)}, u32[]{:S(2)}) collective-permute-start(bf16[8,1536]{1,0:T(8,128)(2,1)} %a_hbm.1), channel_id=1, source_target_pairs={{0,2},{1,3},{2,0},{3,1},{4,6},{5,7},{6,4},{7,5},{8,10},{9,11},{10,... | collective-permute-start | bytes 73736 | tf_op jit(solution)/shard_map/ppermute | solution.py:587
  4.7 1.5 %collective-permute-start.1 = (bf16[8,1536]{1,0:T(8,128)(2,1)}, bf16[8,1536]{1,0:T(8,128)(2,1)S(1)}, u32[]{:S(2)}, u32[]{:S(2)}) collective-permute-start(bf16[8,1536]{1,0:T(8,128)(2,1)} %b_hbm.1), channel_id=1, source_target_pairs={{0,8},{4,12},{8,0},{12,4},{1,9},{5,13},{9,1},{13,5},{2,10},{6,14},... | collective-permute-start | bytes 73736 | tf_op jit(solution)/shard_map/ppermute | solution.py:587
  6.2 1.4 %shard_map.92 = (bf16[1024,128]{1,0:T(8,128)(2,1)S(1)}, bf16[128,1024]{1,0:T(8,128)(2,1)S(1)}, bf16[8,1536]{1,0:T(8,128)(2,1)S(1)}, bf16[8,1536]{1,0:T(8,128)(2,...) custom-call(bf16[8,1536]{1,0:T(8,128)(2,1)} %a_hbm.1, bf16[8,1536]{1,0:T(8,128)(2,1)} %b_hbm.1, ...), custom_call_target="tpu_custom_call" | custom-call | flops 131072000 | bytes 2097152 | tf_op jit(solution)/shard_map/pallas_call | solution.py:67
  7.6 0.0 collective-permute-done.refs_1_
  7.6 1.1 %collective-permute-done.1.refs_3_ = bf16[8,1536]{1,0:T(8,128)(2,1)S(1)} collective-permute-done((bf16[8,1536]{1,0:T(8,128)(2,1)}, bf16[8,1536]{1,0:T(8,128)(2,1)S(1)}, u32[]{:S(2)}, u32[]{:S(2)}) %collective-permute-start.1) | collective-permute-done | bytes 24608 | tf_op jit(solution)/shard_map/ppermute | solution.py:587
  8.8 1.6 %collective-permute-start.2 = (bf16[16,1536]{1,0:T(8,128)(2,1)S(1)}, bf16[16,1536]{1,0:T(8,128)(2,1)S(1)}, u32[]{:S(2)}, u32[]{:S(2)}) collective-permute-start(bf16[16,1536]{1,0:T(8,128)(2,1)S(1)} %get-tuple-element.45.refs_0_), channel_id=1, source_target_pairs={{0,1},{1,0},{2,3},{3,2},{4,5},{5,4},{6,7},{7,6},{8,9},{9,8},{10,11... | collective-permute-start | bytes 147464 | tf_op jit(solution)/shard_map/ppermute | solution.py:587
  10.4 1.7 %shard_map.94 = (bf16[1024,2304]{1,0:T(8,128)(2,1)S(1)}, bf16[2304,128]{1,0:T(8,128)(2,1)S(1)}, bf16[16,128]{1,0:T(8,128)(2,1)S(1)}) custom-call(bf16[1024,128]{1,0:T(8,128)(2,1)S(1)} %get-tuple-element.48.we_ref, bf16[2304,128]{1,0:T(8,128)(2,1)S(1)} %get-tuple-element.47.g_ref.refs_4_), custom_call_target="tpu_custom_call" | custom-call | flops 603979776 | bytes 9437184 | tf_op jit(solution)/shard_map/pallas_call | solution.py:126
  12.2 0.8 %collective-permute-done.2.refs_1_ = bf16[16,1536]{1,0:T(8,128)(2,1)S(1)} collective-permute-done((bf16[16,1536]{1,0:T(8,128)(2,1)S(1)}, bf16[16,1536]{1,0:T(8,128)(2,1)S(1)}, u32[]{:S(2)}, u32[]{:S(2)}) %collective-permute-start.2) | collective-permute-done | bytes 49184 | tf_op jit(solution)/shard_map/ppermute | solution.py:587
  12.9 0.0 collective-permute-done.3.refs_3_
  12.9 4.7 %shard_map.95 = (bf16[1024,2304]{1,0:T(8,128)(2,1)S(1)}, f32[32,1536]{1,0:T(8,128)S(1)}, f32[1,1536,128]{2,1,0:T(8,128)S(1)}, f32[272,128]{1,0:T(8,128)S(1)}, bf...) custom-call(bf16[16,1536]{1,0:T(8,128)(2,1)S(1)} %get-tuple-element.45.refs_0_, ...), custom_call_target="tpu_custom_call" | custom-call | flops 1207959552 | bytes 4718592 | tf_op jit(solution)/shard_map/pallas_call | solution.py:290
  17.7 1.0 %collective-permute-start.4 = (bf16[272,128]{1,0:T(8,128)(2,1)S(1)}, bf16[272,128]{1,0:T(8,128)(2,1)S(1)}, u32[]{:S(2)}, u32[]{:S(2)}) collective-permute-start(bf16[272,128]{1,0:T(8,128)(2,1)S(1)} %get-tuple-element.53), channel_id=1, source_target_pairs={{0,12},{4,8},{8,4},{12,0},{1,13},{5,9},{9,5},{13,1},{2,14},{6,10},... | collective-permute-start | bytes 208904 | tf_op jit(solution)/shard_map/ppermute | solution.py:587
  18.6 0.7 %collective-permute-start.5 = (bf16[272,128]{1,0:T(8,128)(2,1)S(1)}, bf16[272,128]{1,0:T(8,128)(2,1)S(1)}, u32[]{:S(2)}, u32[]{:S(2)}) collective-permute-start(bf16[272,128]{1,0:T(8,128)(2,1)S(1)} %get-tuple-element.54), channel_id=1, source_target_pairs={{0,8},{4,12},{8,0},{12,4},{1,9},{5,13},{9,1},{13,5},{2,10},{6,14},... | collective-permute-start | bytes 208904 | tf_op jit(solution)/shard_map/ppermute | solution.py:587
  19.3 0.3 collective-permute-start.6
  19.6 2.4 %shard_map.96 = (f32[96,128]{1,0:T(8,128)S(1)}, f32[96,128]{1,0:T(8,128)S(1)}, bf16[192,128]{1,0:T(8,128)(2,1)S(1)}) custom-call(f32[1,1536,128]{2,1,0:T(8,128)S(1)} %get-tuple-element.56.refs_0_, bf16[1024,2304]{1,0:T(8,128)(2,1)S(1)} %get-tuple-element.57.refs_1_, f32[272,128]{1,0:T(8,128)S(1)} %get-tuple-element.52.refs_2_.refs_0_), custom_call_target="tpu_custom_call" | custom-call | flops 603979776 | bytes 4718592 | tf_op jit(solution)/shard_map/pallas_call | solution.py:378
  22.1 1.7 %collective-permute-start.8 = (bf16[192,128]{1,0:T(8,128)(2,1)S(1)}, bf16[192,128]{1,0:T(8,128)(2,1)S(1)}, u32[]{:S(2)}, u32[]{:S(2)}) collective-permute-start(bf16[192,128]{1,0:T(8,128)(2,1)S(1)} %get-tuple-element.58.refs_4_), channel_id=1, source_target_pairs={{0,1},{1,0},{2,3},{3,2},{4,5},{5,4},{6,7},{7,6},{8,9},{9,8},{10,11... | collective-permute-start | bytes 147464 | tf_op jit(solution)/shard_map/ppermute | solution.py:587
  23.8 1.6 %collective-permute-start.7 = (bf16[272,128]{1,0:T(8,128)(2,1)S(1)}, bf16[272,128]{1,0:T(8,128)(2,1)S(1)}, u32[]{:S(2)}, u32[]{:S(2)}) collective-permute-start(bf16[272,128]{1,0:T(8,128)(2,1)S(1)} %shard_map.97.refs_3_.own), channel_id=1, source_target_pairs={{0,1},{1,0},{2,3},{3,2},{4,5},{5,4},{6,7},{7,6},{8,9},{9,8},{10,11... | collective-permute-start | bytes 208904 | tf_op jit(solution)/shard_map/ppermute | solution.py:587
  25.4 0.8 %collective-permute-done.8.refs_2_ = bf16[192,128]{1,0:T(8,128)(2,1)S(1)} collective-permute-done((bf16[192,128]{1,0:T(8,128)(2,1)S(1)}, bf16[192,128]{1,0:T(8,128)(2,1)S(1)}, u32[]{:S(2)}, u32[]{:S(2)}) %collective-permute-start.8) | collective-permute-done | bytes 49184 | tf_op jit(solution)/shard_map/ppermute | solution.py:587
  26.2 1.5 %shard_map.99 = (bf16[1024,2304]{1,0:T(8,128)(2,1)S(1)}, f32[1,1536,128]{2,1,0:T(8,128)S(1)}) custom-call(bf16[1024,128]{1,0:T(8,128)(2,1)S(1)} %get-tuple-element.59.left_ref, bf16[2304,128]{1,0:T(8,128)(2,1)S(1)} %get-tuple-element.60.right_ref, f32[32,1536]{1,0:T(8,128)S(1)} %get-tuple-element.61.held, f32[96,128]{1,0:T(8,128)S(1)} %get-tuple-element.64._.refs_4_), custom_call_target="tpu_custom_call" | custom-call | flops 603979776 | bytes 9437184 | tf_op jit(solution)/shard_map/pallas_call | solution.py:406
  27.8 0.4 collective-permute-done.7.near
  28.2 1.1 %collective-permute-start.9 = (bf16[272,128]{1,0:T(8,128)(2,1)S(1)}, bf16[272,128]{1,0:T(8,128)(2,1)S(1)}, u32[]{:S(2)}, u32[]{:S(2)}) collective-permute-start(bf16[272,128]{1,0:T(8,128)(2,1)S(1)} %shard_map.100.refs_2_.refs_0_), channel_id=1, source_target_pairs={{0,2},{1,3},{2,0},{3,1},{4,6},{5,7},{6,4},{7,5},{8,10},{9,11},{10,... | collective-permute-start | bytes 208904 | tf_op jit(solution)/shard_map/ppermute | solution.py:587
  29.3 1.9 %collective-permute-start.13 = (bf16[96,128]{1,0:T(8,128)(2,1)S(1)}, bf16[96,128]{1,0:T(8,128)(2,1)S(1)}, u32[]{:S(2)}, u32[]{:S(2)}) collective-permute-start(bf16[96,128]{1,0:T(8,128)(2,1)S(1)} %get-tuple-element.74), channel_id=1, source_target_pairs={{0,2},{1,3},{2,0},{3,1},{4,6},{5,7},{6,4},{7,5},{8,10},{9,11},{10,... | collective-permute-start | bytes 73736 | tf_op jit(solution)/shard_map/ppermute | solution.py:587
  31.2 2.5 %shard_map.101 = (f32[96,128]{1,0:T(8,128)S(1)}, bf16[96,128]{1,0:T(8,128)(2,1)S(1)}, bf16[96,128]{1,0:T(8,128)(2,1)S(1)}, bf16[96,128]{1,0:T(8,128)(2,1)S(1)}) custom-call(f32[1,1536,128]{2,1,0:T(8,128)S(1)} %get-tuple-element.66.refs_0_, bf16[1024,2304]{1,0:T(8,128)(2,1)S(1)} %get-tuple-element.65._.refs_1_, bf16[272,128]{1,0:T(8,128)(2,1)S(1)} %shard_map.100.refs_2_.refs_0_), custom_call_target="tpu_custom_call" | custom-call | flops 603979776 | bytes 4718592 | tf_op jit(solution)/shard_map/pallas_call | solution.py:378
  33.6 0.0 collective-permute-done.9.refs_1_
  33.6 0.1 shard_map.102
  33.8 0.1 collective-permute-start.10
  33.9 1.6 %collective-permute-start.11 = (bf16[352,128]{1,0:T(8,128)(2,1)S(1)}, bf16[352,128]{1,0:T(8,128)(2,1)S(1)}, u32[]{:S(2)}, u32[]{:S(2)}) collective-permute-start(bf16[352,128]{1,0:T(8,128)(2,1)S(1)} %get-tuple-element.72), channel_id=1, source_target_pairs={{0,8},{4,12},{8,0},{12,4},{1,9},{5,13},{9,1},{13,5},{2,10},{6,14},... | collective-permute-start | bytes 270344 | tf_op jit(solution)/shard_map/ppermute | solution.py:587
  35.4 0.3 collective-permute-start.12
  35.7 2.5 %shard_map.103 = bf16[2304,128]{1,0:T(8,128)(2,1)} custom-call(bf16[1024,2304]{1,0:T(8,128)(2,1)S(1)} %get-tuple-element.50.x_ref, bf16[128,1024]{1,0:T(8,128)(2,1)S(1)} %get-tuple-element.51.wt_ref, f32[1,128]{1,0:T(1,128)S(1)} %bitcast.4, bf16[256,128]{1,0:T(8,128)(2,1)S(1)} %get-tuple-element.70._.refs_0_), custom_call_target="tpu_custom_call" | custom-call | flops 1207959552 | bytes 4718592 | tf_op jit(solution)/shard_map/pallas_call | solution.py:429
  38.3 0.0 collective-permute-done.13.refs_5_
  38.3 0.4 %collective-permute-done.10.refs_1_ = bf16[352,128]{1,0:T(8,128)(2,1)S(1)} collective-permute-done((bf16[352,128]{1,0:T(8,128)(2,1)S(1)}, bf16[352,128]{1,0:T(8,128)(2,1)S(1)}, u32[]{:S(2)}, u32[]{:S(2)}) %collective-permute-start.10) | collective-permute-done | bytes 90144 | tf_op jit(solution)/shard_map/ppermute | solution.py:587
  38.7 2.0 %collective-permute-done.11.refs_2_ = bf16[352,128]{1,0:T(8,128)(2,1)S(1)} collective-permute-done((bf16[352,128]{1,0:T(8,128)(2,1)S(1)}, bf16[352,128]{1,0:T(8,128)(2,1)S(1)}, u32[]{:S(2)}, u32[]{:S(2)}) %collective-permute-start.11) | collective-permute-done | bytes 90144 | tf_op jit(solution)/shard_map/ppermute | solution.py:587
  40.7 0.9 %shard_map.104 = (f32[1024,128]{1,0:T(8,128)}, f32[8,1536]{1,0:T(8,128)}, f32[8,1536]{1,0:T(8,128)}, f32[1,128]{1,0:T(1,128)}) custom-call(bf16[256,128]{1,0:T(8,128)(2,1)S(1)} %get-tuple-element.70._.refs_0_, bf16[352,128]{1,0:T(8,128)(2,1)S(1)} %collective-permute-done.10.refs_1_, bf16[352,128]{1,0:T(8,128)(2,1)S(1)} %collective-permute-done.11.refs_2_, ...), custom_call_target="tpu_custom_call" | custom-call | tf_op jit(solution)/shard_map/pallas_call | solution.py:456
  (11 shorter events, 0.1 us)
Async XLA Ops:
  0.6 7.0 %collective-permute-start = (bf16[8,1536]{1,0:T(8,128)(2,1)}, bf16[8,1536]{1,0:T(8,128)(2,1)S(1)}, u32[]{:S(2)}, u32[]{:S(2)}) collective-permute-start(bf16[8,1536]{1,0:T(8,128)(2,1)} %a_hbm.1), channel_id=1, source_target_pairs={{0,2},{1,3},{2,0},{3,1},{4,6},{5,7},{6,4},{7,5},{8,10},{9,11},{10,... | collective-permute-start | bytes 73736 | tf_op jit(solution)/shard_map/ppermute | solution.py:587
  4.7 4.0 %collective-permute-start.1 = (bf16[8,1536]{1,0:T(8,128)(2,1)}, bf16[8,1536]{1,0:T(8,128)(2,1)S(1)}, u32[]{:S(2)}, u32[]{:S(2)}) collective-permute-start(bf16[8,1536]{1,0:T(8,128)(2,1)} %b_hbm.1), channel_id=1, source_target_pairs={{0,8},{4,12},{8,0},{12,4},{1,9},{5,13},{9,1},{13,5},{2,10},{6,14},... | collective-permute-start | bytes 73736 | tf_op jit(solution)/shard_map/ppermute | solution.py:587
  8.8 4.2 %collective-permute-start.2 = (bf16[16,1536]{1,0:T(8,128)(2,1)S(1)}, bf16[16,1536]{1,0:T(8,128)(2,1)S(1)}, u32[]{:S(2)}, u32[]{:S(2)}) collective-permute-start(bf16[16,1536]{1,0:T(8,128)(2,1)S(1)} %get-tuple-element.45.refs_0_), channel_id=1, source_target_pairs={{0,1},{1,0},{2,3},{3,2},{4,5},{5,4},{6,7},{7,6},{8,9},{9,8},{10,11... | collective-permute-start | bytes 147464 | tf_op jit(solution)/shard_map/ppermute | solution.py:587
  10.4 2.5 %collective-permute-start.3 = (bf16[16,1536]{1,0:T(8,128)(2,1)S(1)}, bf16[16,1536]{1,0:T(8,128)(2,1)S(1)}, u32[]{:S(2)}, u32[]{:S(2)}) collective-permute-start(bf16[16,1536]{1,0:T(8,128)(2,1)S(1)} %get-tuple-element.46.refs_2_), channel_id=1, source_target_pairs={{0,4},{4,0},{8,12},{12,8},{1,5},{5,1},{9,13},{13,9},{2,6},{6,2},{1... | collective-permute-start | bytes 147464 | tf_op jit(solution)/shard_map/ppermute | solution.py:587
  17.7 6.0 %collective-permute-start.4 = (bf16[272,128]{1,0:T(8,128)(2,1)S(1)}, bf16[272,128]{1,0:T(8,128)(2,1)S(1)}, u32[]{:S(2)}, u32[]{:S(2)}) collective-permute-start(bf16[272,128]{1,0:T(8,128)(2,1)S(1)} %get-tuple-element.53), channel_id=1, source_target_pairs={{0,12},{4,8},{8,4},{12,0},{1,13},{5,9},{9,5},{13,1},{2,14},{6,10},... | collective-permute-start | bytes 208904 | tf_op jit(solution)/shard_map/ppermute | solution.py:587
  18.6 5.1 %collective-permute-start.5 = (bf16[272,128]{1,0:T(8,128)(2,1)S(1)}, bf16[272,128]{1,0:T(8,128)(2,1)S(1)}, u32[]{:S(2)}, u32[]{:S(2)}) collective-permute-start(bf16[272,128]{1,0:T(8,128)(2,1)S(1)} %get-tuple-element.54), channel_id=1, source_target_pairs={{0,8},{4,12},{8,0},{12,4},{1,9},{5,13},{9,1},{13,5},{2,10},{6,14},... | collective-permute-start | bytes 208904 | tf_op jit(solution)/shard_map/ppermute | solution.py:587
  19.3 4.4 %collective-permute-start.6 = (bf16[272,128]{1,0:T(8,128)(2,1)S(1)}, bf16[272,128]{1,0:T(8,128)(2,1)S(1)}, u32[]{:S(2)}, u32[]{:S(2)}) collective-permute-start(bf16[272,128]{1,0:T(8,128)(2,1)S(1)} %get-tuple-element.55), channel_id=1, source_target_pairs={{0,4},{4,0},{8,12},{12,8},{1,5},{5,1},{9,13},{13,9},{2,6},{6,2},{1... | collective-permute-start | bytes 208904 | tf_op jit(solution)/shard_map/ppermute | solution.py:587
  22.1 4.2 %collective-permute-start.8 = (bf16[192,128]{1,0:T(8,128)(2,1)S(1)}, bf16[192,128]{1,0:T(8,128)(2,1)S(1)}, u32[]{:S(2)}, u32[]{:S(2)}) collective-permute-start(bf16[192,128]{1,0:T(8,128)(2,1)S(1)} %get-tuple-element.58.refs_4_), channel_id=1, source_target_pairs={{0,1},{1,0},{2,3},{3,2},{4,5},{5,4},{6,7},{7,6},{8,9},{9,8},{10,11... | collective-permute-start | bytes 147464 | tf_op jit(solution)/shard_map/ppermute | solution.py:587
  23.8 4.4 %collective-permute-start.7 = (bf16[272,128]{1,0:T(8,128)(2,1)S(1)}, bf16[272,128]{1,0:T(8,128)(2,1)S(1)}, u32[]{:S(2)}, u32[]{:S(2)}) collective-permute-start(bf16[272,128]{1,0:T(8,128)(2,1)S(1)} %shard_map.97.refs_3_.own), channel_id=1, source_target_pairs={{0,1},{1,0},{2,3},{3,2},{4,5},{5,4},{6,7},{7,6},{8,9},{9,8},{10,11... | collective-permute-start | bytes 208904 | tf_op jit(solution)/shard_map/ppermute | solution.py:587
  28.2 7.6 %copy-start = (f32[128]{0:T(128)S(1)}, f32[128]{0:T(128)}, u32[]{:S(2)}) copy-start(f32[128]{0:T(128)} %param.8) | copy-start | bytes 1540
  28.2 5.5 %collective-permute-start.9 = (bf16[272,128]{1,0:T(8,128)(2,1)S(1)}, bf16[272,128]{1,0:T(8,128)(2,1)S(1)}, u32[]{:S(2)}, u32[]{:S(2)}) collective-permute-start(bf16[272,128]{1,0:T(8,128)(2,1)S(1)} %shard_map.100.refs_2_.refs_0_), channel_id=1, source_target_pairs={{0,2},{1,3},{2,0},{3,1},{4,6},{5,7},{6,4},{7,5},{8,10},{9,11},{10,... | collective-permute-start | bytes 208904 | tf_op jit(solution)/shard_map/ppermute | solution.py:587
  29.3 8.9 %collective-permute-start.13 = (bf16[96,128]{1,0:T(8,128)(2,1)S(1)}, bf16[96,128]{1,0:T(8,128)(2,1)S(1)}, u32[]{:S(2)}, u32[]{:S(2)}) collective-permute-start(bf16[96,128]{1,0:T(8,128)(2,1)S(1)} %get-tuple-element.74), channel_id=1, source_target_pairs={{0,2},{1,3},{2,0},{3,1},{4,6},{5,7},{6,4},{7,5},{8,10},{9,11},{10,... | collective-permute-start | bytes 73736 | tf_op jit(solution)/shard_map/ppermute | solution.py:587
  33.8 4.9 %collective-permute-start.10 = (bf16[352,128]{1,0:T(8,128)(2,1)S(1)}, bf16[352,128]{1,0:T(8,128)(2,1)S(1)}, u32[]{:S(2)}, u32[]{:S(2)}) collective-permute-start(bf16[352,128]{1,0:T(8,128)(2,1)S(1)} %get-tuple-element.71), channel_id=1, source_target_pairs={{0,12},{4,8},{8,4},{12,0},{1,13},{5,9},{9,5},{13,1},{2,14},{6,10},... | collective-permute-start | bytes 270344 | tf_op jit(solution)/shard_map/ppermute | solution.py:587
  33.9 6.8 %collective-permute-start.11 = (bf16[352,128]{1,0:T(8,128)(2,1)S(1)}, bf16[352,128]{1,0:T(8,128)(2,1)S(1)}, u32[]{:S(2)}, u32[]{:S(2)}) collective-permute-start(bf16[352,128]{1,0:T(8,128)(2,1)S(1)} %get-tuple-element.72), channel_id=1, source_target_pairs={{0,8},{4,12},{8,0},{12,4},{1,9},{5,13},{9,1},{13,5},{2,10},{6,14},... | collective-permute-start | bytes 270344 | tf_op jit(solution)/shard_map/ppermute | solution.py:587
  35.4 5.3 %collective-permute-start.12 = (bf16[352,128]{1,0:T(8,128)(2,1)S(1)}, bf16[352,128]{1,0:T(8,128)(2,1)S(1)}, u32[]{:S(2)}, u32[]{:S(2)}) collective-permute-start(bf16[352,128]{1,0:T(8,128)(2,1)S(1)} %get-tuple-element.73), channel_id=1, source_target_pairs={{0,4},{4,0},{8,12},{12,8},{1,5},{5,1},{9,13},{13,9},{2,6},{6,2},{1... | collective-permute-start | bytes 270344 | tf_op jit(solution)/shard_map/ppermute | solution.py:587

commit v19 on v17

--- a/solution.py
+++ b/solution.py
@@ -250,7 +250,8 @@
     def _(t):
         size = per_step * depth
         rows = pl.ds(t * size if CHUNKS == 1 else pl.multiple_of(t * size, size), size)
-        x_part = x_ref.at[rows]
+        x_part, total_part = x_ref.at[rows], total.at[rows]
+        half = per_step // 2
         for e in range(0, per_step, 2):
             right = [diagonal_of(b_wide, t * per_step + e + n, j_n, sequences) for n in range(2)]
             product = dot(
@@ -261,7 +262,9 @@
                     x_part[(e + n) * depth : (e + n + 1) * depth, k * span : (k + 1) * span] = product[
                         k * depth : (k + 1) * depth, n * span : (n + 1) * span
                     ]
-        total[rows, :] = dot(x_part[...], g_ref[...])
+            if (e + 2) % half == 0:
+                done = slice((e + 2 - half) * depth, (e + 2) * depth)
+                total_part[done, :] = dot(x_part[done, :], g_ref[...])
 
     share = total.shape[0] // row_n
     me = lax.axis_index("row")

time: 41.2 us -> 41.1 us (level)
  no operation moved by 1% of the time
where the time goes in v19:
time: 41.1 us; the launch traced here: 41 us
  starting transfers between devices  17.8 us (43%)
  Pallas kernels  16.8 us (41%)
  waiting for transfers between devices  5.67 us (14%)
  between operations  0.72 us (2%)
    ppermute x14, starting transfers between devices, swap(): lax.ppermute(x, axis, [(n, n ^ p) for n in range(lax.axis_size(axis))])  17.8 us
    ppermute x14, waiting for transfers between devices, swap(): lax.ppermute(x, axis, [(n, n ^ p) for n in range(lax.axis_size(axis))])  5.67 us
    pallas_call x1, Pallas kernels, outer(): pl.pallas_call(functools.partial(outer_kernel, i_n, j_n), in_specs=[in_vm...  4.33 us
    pallas_call x2, Pallas kernels, gradient(): pl.pallas_call(functools.partial(gradient_kernel, axis, plan, kept, posit...  4.12 us
    pallas_call x1, Pallas kernels, pair(): pl.pallas_call(functools.partial(pair_kernel, sequences), grid=(count,),...  2.55 us
    pallas_call x1, Pallas kernels, prepare(): pl.pallas_call(functools.partial(prepare_kernel, i_n, j_n), in_specs=[in_...  1.75 us
    pallas_call x1, Pallas kernels, product(): pl.pallas_call(product_kernel, in_specs=[in_vmem()] * 3 + [pl.BlockSpec(m...  1.55 us
    pallas_call x1, Pallas kernels, load(): pl.pallas_call(load_kernel, in_specs=[pl.BlockSpec(memory_space=pltpu.HBM...  1.39 us
  transfers between devices with their start and end apart: 14, of which 7 were waited for; matrix products, arithmetic and copies ran while one was open for 0% of the time, Pallas kernels for 28%

profile of v19, /device:TPU:0, one launch (start us, length us, event | category | flops | bytes accessed | tf_op | source)
XLA Modules:
  0.0 41.0 jit_solution(16193112334876087858)
XLA Ops:
  0.6 4.1 %collective-permute-start = (bf16[8,1536]{1,0:T(8,128)(2,1)}, bf16[8,1536]{1,0:T(8,128)(2,1)S(1)}, u32[]{:S(2)}, u32[]{:S(2)}) collective-permute-start(bf16[8,1536]{1,0:T(8,128)(2,1)} %a_hbm.1), channel_id=1, source_target_pairs={{0,2},{1,3},{2,0},{3,1},{4,6},{5,7},{6,4},{7,5},{8,10},{9,11},{10,... | collective-permute-start | bytes 73736 | tf_op jit(solution)/shard_map/ppermute | solution.py:590
  4.7 1.5 %collective-permute-start.1 = (bf16[8,1536]{1,0:T(8,128)(2,1)}, bf16[8,1536]{1,0:T(8,128)(2,1)S(1)}, u32[]{:S(2)}, u32[]{:S(2)}) collective-permute-start(bf16[8,1536]{1,0:T(8,128)(2,1)} %b_hbm.1), channel_id=1, source_target_pairs={{0,8},{4,12},{8,0},{12,4},{1,9},{5,13},{9,1},{13,5},{2,10},{6,14},... | collective-permute-start | bytes 73736 | tf_op jit(solution)/shard_map/ppermute | solution.py:590
  6.2 1.4 %shard_map.92 = (bf16[1024,128]{1,0:T(8,128)(2,1)S(1)}, bf16[128,1024]{1,0:T(8,128)(2,1)S(1)}, bf16[8,1536]{1,0:T(8,128)(2,1)S(1)}, bf16[8,1536]{1,0:T(8,128)(2,...) custom-call(bf16[8,1536]{1,0:T(8,128)(2,1)} %a_hbm.1, bf16[8,1536]{1,0:T(8,128)(2,1)} %b_hbm.1, ...), custom_call_target="tpu_custom_call" | custom-call | flops 131072000 | bytes 2097152 | tf_op jit(solution)/shard_map/pallas_call | solution.py:67
  7.6 0.0 collective-permute-done.refs_1_
  7.6 1.1 %collective-permute-done.1.refs_3_ = bf16[8,1536]{1,0:T(8,128)(2,1)S(1)} collective-permute-done((bf16[8,1536]{1,0:T(8,128)(2,1)}, bf16[8,1536]{1,0:T(8,128)(2,1)S(1)}, u32[]{:S(2)}, u32[]{:S(2)}) %collective-permute-start.1) | collective-permute-done | bytes 24608 | tf_op jit(solution)/shard_map/ppermute | solution.py:590
  8.8 1.6 %collective-permute-start.2 = (bf16[16,1536]{1,0:T(8,128)(2,1)S(1)}, bf16[16,1536]{1,0:T(8,128)(2,1)S(1)}, u32[]{:S(2)}, u32[]{:S(2)}) collective-permute-start(bf16[16,1536]{1,0:T(8,128)(2,1)S(1)} %get-tuple-element.45.refs_0_), channel_id=1, source_target_pairs={{0,1},{1,0},{2,3},{3,2},{4,5},{5,4},{6,7},{7,6},{8,9},{9,8},{10,11... | collective-permute-start | bytes 147464 | tf_op jit(solution)/shard_map/ppermute | solution.py:590
  10.4 0.0 collective-permute-start.3
  10.4 1.8 %shard_map.94 = (bf16[1024,2304]{1,0:T(8,128)(2,1)S(1)}, bf16[2304,128]{1,0:T(8,128)(2,1)S(1)}, bf16[16,128]{1,0:T(8,128)(2,1)S(1)}) custom-call(bf16[1024,128]{1,0:T(8,128)(2,1)S(1)} %get-tuple-element.48.we_ref, bf16[2304,128]{1,0:T(8,128)(2,1)S(1)} %get-tuple-element.47.g_ref.refs_4_), custom_call_target="tpu_custom_call" | custom-call | flops 603979776 | bytes 9437184 | tf_op jit(solution)/shard_map/pallas_call | solution.py:126
  12.2 0.8 %collective-permute-done.2.refs_1_ = bf16[16,1536]{1,0:T(8,128)(2,1)S(1)} collective-permute-done((bf16[16,1536]{1,0:T(8,128)(2,1)S(1)}, bf16[16,1536]{1,0:T(8,128)(2,1)S(1)}, u32[]{:S(2)}, u32[]{:S(2)}) %collective-permute-start.2) | collective-permute-done | bytes 49184 | tf_op jit(solution)/shard_map/ppermute | solution.py:590
  12.9 4.3 %shard_map.95 = (bf16[1024,2304]{1,0:T(8,128)(2,1)S(1)}, f32[32,1536]{1,0:T(8,128)S(1)}, f32[1,1536,128]{2,1,0:T(8,128)S(1)}, f32[272,128]{1,0:T(8,128)S(1)}, bf...) custom-call(bf16[16,1536]{1,0:T(8,128)(2,1)S(1)} %get-tuple-element.45.refs_0_, ...), custom_call_target="tpu_custom_call" | custom-call | flops 1207959552 | bytes 4718592 | tf_op jit(solution)/shard_map/pallas_call | solution.py:293
  17.3 0.9 %collective-permute-start.4 = (bf16[272,128]{1,0:T(8,128)(2,1)S(1)}, bf16[272,128]{1,0:T(8,128)(2,1)S(1)}, u32[]{:S(2)}, u32[]{:S(2)}) collective-permute-start(bf16[272,128]{1,0:T(8,128)(2,1)S(1)} %get-tuple-element.53), channel_id=1, source_target_pairs={{0,12},{4,8},{8,4},{12,0},{1,13},{5,9},{9,5},{13,1},{2,14},{6,10},... | collective-permute-start | bytes 208904 | tf_op jit(solution)/shard_map/ppermute | solution.py:590
  18.2 0.7 %collective-permute-start.5 = (bf16[272,128]{1,0:T(8,128)(2,1)S(1)}, bf16[272,128]{1,0:T(8,128)(2,1)S(1)}, u32[]{:S(2)}, u32[]{:S(2)}) collective-permute-start(bf16[272,128]{1,0:T(8,128)(2,1)S(1)} %get-tuple-element.54), channel_id=1, source_target_pairs={{0,8},{4,12},{8,0},{12,4},{1,9},{5,13},{9,1},{13,5},{2,10},{6,14},... | collective-permute-start | bytes 208904 | tf_op jit(solution)/shard_map/ppermute | solution.py:590
  18.9 0.3 collective-permute-start.6
  19.2 2.1 %shard_map.96 = (f32[96,128]{1,0:T(8,128)S(1)}, f32[96,128]{1,0:T(8,128)S(1)}, bf16[192,128]{1,0:T(8,128)(2,1)S(1)}) custom-call(f32[1,1536,128]{2,1,0:T(8,128)S(1)} %get-tuple-element.56.refs_0_, bf16[1024,2304]{1,0:T(8,128)(2,1)S(1)} %get-tuple-element.57.refs_1_, f32[272,128]{1,0:T(8,128)S(1)} %get-tuple-element.52.refs_2_.refs_0_), custom_call_target="tpu_custom_call" | custom-call | flops 603979776 | bytes 4718592 | tf_op jit(solution)/shard_map/pallas_call | solution.py:381
  21.3 1.6 %collective-permute-start.8 = (bf16[192,128]{1,0:T(8,128)(2,1)S(1)}, bf16[192,128]{1,0:T(8,128)(2,1)S(1)}, u32[]{:S(2)}, u32[]{:S(2)}) collective-permute-start(bf16[192,128]{1,0:T(8,128)(2,1)S(1)} %get-tuple-element.58.refs_4_), channel_id=1, source_target_pairs={{0,1},{1,0},{2,3},{3,2},{4,5},{5,4},{6,7},{7,6},{8,9},{9,8},{10,11... | collective-permute-start | bytes 147464 | tf_op jit(solution)/shard_map/ppermute | solution.py:590
  22.9 0.4 collective-permute-done.5.refs_2_
  23.3 0.0 collective-permute-done.6.refs_3_
  23.4 1.6 %collective-permute-start.7 = (bf16[272,128]{1,0:T(8,128)(2,1)S(1)}, bf16[272,128]{1,0:T(8,128)(2,1)S(1)}, u32[]{:S(2)}, u32[]{:S(2)}) collective-permute-start(bf16[272,128]{1,0:T(8,128)(2,1)S(1)} %shard_map.97.refs_3_.own), channel_id=1, source_target_pairs={{0,1},{1,0},{2,3},{3,2},{4,5},{5,4},{6,7},{7,6},{8,9},{9,8},{10,11... | collective-permute-start | bytes 208904 | tf_op jit(solution)/shard_map/ppermute | solution.py:590
  25.0 0.4 %collective-permute-done.8.refs_2_ = bf16[192,128]{1,0:T(8,128)(2,1)S(1)} collective-permute-done((bf16[192,128]{1,0:T(8,128)(2,1)S(1)}, bf16[192,128]{1,0:T(8,128)(2,1)S(1)}, u32[]{:S(2)}, u32[]{:S(2)}) %collective-permute-start.8) | collective-permute-done | bytes 49184 | tf_op jit(solution)/shard_map/ppermute | solution.py:590
  25.4 1.5 %shard_map.99 = (bf16[1024,2304]{1,0:T(8,128)(2,1)S(1)}, f32[1,1536,128]{2,1,0:T(8,128)S(1)}) custom-call(bf16[1024,128]{1,0:T(8,128)(2,1)S(1)} %get-tuple-element.59.left_ref, bf16[2304,128]{1,0:T(8,128)(2,1)S(1)} %get-tuple-element.60.right_ref, f32[32,1536]{1,0:T(8,128)S(1)} %get-tuple-element.61.held, f32[96,128]{1,0:T(8,128)S(1)} %get-tuple-element.64._.refs_4_), custom_call_target="tpu_custom_call" | custom-call | flops 603979776 | bytes 9437184 | tf_op jit(solution)/shard_map/pallas_call | solution.py:409
  27.0 0.7 %collective-permute-done.7.near = bf16[272,128]{1,0:T(8,128)(2,1)S(1)} collective-permute-done((bf16[272,128]{1,0:T(8,128)(2,1)S(1)}, bf16[272,128]{1,0:T(8,128)(2,1)S(1)}, u32[]{:S(2)}, u32[]{:S(2)}) %collective-permute-start.7) | collective-permute-done | bytes 69664 | tf_op jit(solution)/shard_map/ppermute | solution.py:590
  27.8 1.0 %collective-permute-start.9 = (bf16[272,128]{1,0:T(8,128)(2,1)S(1)}, bf16[272,128]{1,0:T(8,128)(2,1)S(1)}, u32[]{:S(2)}, u32[]{:S(2)}) collective-permute-start(bf16[272,128]{1,0:T(8,128)(2,1)S(1)} %shard_map.100.refs_2_.refs_0_), channel_id=1, source_target_pairs={{0,2},{1,3},{2,0},{3,1},{4,6},{5,7},{6,4},{7,5},{8,10},{9,11},{10,... | collective-permute-start | bytes 208904 | tf_op jit(solution)/shard_map/ppermute | solution.py:590
  28.8 2.0 %collective-permute-start.13 = (bf16[96,128]{1,0:T(8,128)(2,1)S(1)}, bf16[96,128]{1,0:T(8,128)(2,1)S(1)}, u32[]{:S(2)}, u32[]{:S(2)}) collective-permute-start(bf16[96,128]{1,0:T(8,128)(2,1)S(1)} %get-tuple-element.74), channel_id=1, source_target_pairs={{0,2},{1,3},{2,0},{3,1},{4,6},{5,7},{6,4},{7,5},{8,10},{9,11},{10,... | collective-permute-start | bytes 73736 | tf_op jit(solution)/shard_map/ppermute | solution.py:590
  30.8 2.1 %shard_map.101 = (f32[96,128]{1,0:T(8,128)S(1)}, bf16[96,128]{1,0:T(8,128)(2,1)S(1)}, bf16[96,128]{1,0:T(8,128)(2,1)S(1)}, bf16[96,128]{1,0:T(8,128)(2,1)S(1)}) custom-call(f32[1,1536,128]{2,1,0:T(8,128)S(1)} %get-tuple-element.66.refs_0_, bf16[1024,2304]{1,0:T(8,128)(2,1)S(1)} %get-tuple-element.65._.refs_1_, bf16[272,128]{1,0:T(8,128)(2,1)S(1)} %shard_map.100.refs_2_.refs_0_), custom_call_target="tpu_custom_call" | custom-call | flops 603979776 | bytes 4718592 | tf_op jit(solution)/shard_map/pallas_call | solution.py:381
  32.8 0.2 collective-permute-done.9.refs_1_
  33.0 0.1 shard_map.102
  33.2 0.1 collective-permute-start.10
  33.2 2.2 %collective-permute-start.11 = (bf16[352,128]{1,0:T(8,128)(2,1)S(1)}, bf16[352,128]{1,0:T(8,128)(2,1)S(1)}, u32[]{:S(2)}, u32[]{:S(2)}) collective-permute-start(bf16[352,128]{1,0:T(8,128)(2,1)S(1)} %get-tuple-element.72), channel_id=1, source_target_pairs={{0,8},{4,12},{8,0},{12,4},{1,9},{5,13},{9,1},{13,5},{2,10},{6,14},... | collective-permute-start | bytes 270344 | tf_op jit(solution)/shard_map/ppermute | solution.py:590
  35.5 0.0 collective-permute-start.12
  35.5 2.5 %shard_map.103 = bf16[2304,128]{1,0:T(8,128)(2,1)} custom-call(bf16[1024,2304]{1,0:T(8,128)(2,1)S(1)} %get-tuple-element.50.x_ref, bf16[128,1024]{1,0:T(8,128)(2,1)S(1)} %get-tuple-element.51.wt_ref, f32[1,128]{1,0:T(1,128)S(1)} %bitcast.4, bf16[256,128]{1,0:T(8,128)(2,1)S(1)} %get-tuple-element.70._.refs_0_), custom_call_target="tpu_custom_call" | custom-call | flops 1207959552 | bytes 4718592 | tf_op jit(solution)/shard_map/pallas_call | solution.py:432
  38.1 2.0 %collective-permute-done.11.refs_2_ = bf16[352,128]{1,0:T(8,128)(2,1)S(1)} collective-permute-done((bf16[352,128]{1,0:T(8,128)(2,1)S(1)}, bf16[352,128]{1,0:T(8,128)(2,1)S(1)}, u32[]{:S(2)}, u32[]{:S(2)}) %collective-permute-start.11) | collective-permute-done | bytes 90144 | tf_op jit(solution)/shard_map/ppermute | solution.py:590
  40.1 0.9 %shard_map.104 = (f32[1024,128]{1,0:T(8,128)}, f32[8,1536]{1,0:T(8,128)}, f32[8,1536]{1,0:T(8,128)}, f32[1,128]{1,0:T(1,128)}) custom-call(bf16[256,128]{1,0:T(8,128)(2,1)S(1)} %get-tuple-element.70._.refs_0_, bf16[352,128]{1,0:T(8,128)(2,1)S(1)} %collective-permute-done.10.refs_1_, bf16[352,128]{1,0:T(8,128)(2,1)S(1)} %collective-permute-done.11.refs_2_, ...), custom_call_target="tpu_custom_call" | custom-call | tf_op jit(solution)/shard_map/pallas_call | solution.py:459
  (11 shorter events, 0.1 us)
Async XLA Ops:
  0.6 7.0 %collective-permute-start = (bf16[8,1536]{1,0:T(8,128)(2,1)}, bf16[8,1536]{1,0:T(8,128)(2,1)S(1)}, u32[]{:S(2)}, u32[]{:S(2)}) collective-permute-start(bf16[8,1536]{1,0:T(8,128)(2,1)} %a_hbm.1), channel_id=1, source_target_pairs={{0,2},{1,3},{2,0},{3,1},{4,6},{5,7},{6,4},{7,5},{8,10},{9,11},{10,... | collective-permute-start | bytes 73736 | tf_op jit(solution)/shard_map/ppermute | solution.py:590
  4.7 4.0 %collective-permute-start.1 = (bf16[8,1536]{1,0:T(8,128)(2,1)}, bf16[8,1536]{1,0:T(8,128)(2,1)S(1)}, u32[]{:S(2)}, u32[]{:S(2)}) collective-permute-start(bf16[8,1536]{1,0:T(8,128)(2,1)} %b_hbm.1), channel_id=1, source_target_pairs={{0,8},{4,12},{8,0},{12,4},{1,9},{5,13},{9,1},{13,5},{2,10},{6,14},... | collective-permute-start | bytes 73736 | tf_op jit(solution)/shard_map/ppermute | solution.py:590
  8.8 4.2 %collective-permute-start.2 = (bf16[16,1536]{1,0:T(8,128)(2,1)S(1)}, bf16[16,1536]{1,0:T(8,128)(2,1)S(1)}, u32[]{:S(2)}, u32[]{:S(2)}) collective-permute-start(bf16[16,1536]{1,0:T(8,128)(2,1)S(1)} %get-tuple-element.45.refs_0_), channel_id=1, source_target_pairs={{0,1},{1,0},{2,3},{3,2},{4,5},{5,4},{6,7},{7,6},{8,9},{9,8},{10,11... | collective-permute-start | bytes 147464 | tf_op jit(solution)/shard_map/ppermute | solution.py:590
  10.4 2.5 %collective-permute-start.3 = (bf16[16,1536]{1,0:T(8,128)(2,1)S(1)}, bf16[16,1536]{1,0:T(8,128)(2,1)S(1)}, u32[]{:S(2)}, u32[]{:S(2)}) collective-permute-start(bf16[16,1536]{1,0:T(8,128)(2,1)S(1)} %get-tuple-element.46.refs_2_), channel_id=1, source_target_pairs={{0,4},{4,0},{8,12},{12,8},{1,5},{5,1},{9,13},{13,9},{2,6},{6,2},{1... | collective-permute-start | bytes 147464 | tf_op jit(solution)/shard_map/ppermute | solution.py:590
  17.3 5.6 %collective-permute-start.4 = (bf16[272,128]{1,0:T(8,128)(2,1)S(1)}, bf16[272,128]{1,0:T(8,128)(2,1)S(1)}, u32[]{:S(2)}, u32[]{:S(2)}) collective-permute-start(bf16[272,128]{1,0:T(8,128)(2,1)S(1)} %get-tuple-element.53), channel_id=1, source_target_pairs={{0,12},{4,8},{8,4},{12,0},{1,13},{5,9},{9,5},{13,1},{2,14},{6,10},... | collective-permute-start | bytes 208904 | tf_op jit(solution)/shard_map/ppermute | solution.py:590
  18.2 5.1 %collective-permute-start.5 = (bf16[272,128]{1,0:T(8,128)(2,1)S(1)}, bf16[272,128]{1,0:T(8,128)(2,1)S(1)}, u32[]{:S(2)}, u32[]{:S(2)}) collective-permute-start(bf16[272,128]{1,0:T(8,128)(2,1)S(1)} %get-tuple-element.54), channel_id=1, source_target_pairs={{0,8},{4,12},{8,0},{12,4},{1,9},{5,13},{9,1},{13,5},{2,10},{6,14},... | collective-permute-start | bytes 208904 | tf_op jit(solution)/shard_map/ppermute | solution.py:590
  18.9 4.4 %collective-permute-start.6 = (bf16[272,128]{1,0:T(8,128)(2,1)S(1)}, bf16[272,128]{1,0:T(8,128)(2,1)S(1)}, u32[]{:S(2)}, u32[]{:S(2)}) collective-permute-start(bf16[272,128]{1,0:T(8,128)(2,1)S(1)} %get-tuple-element.55), channel_id=1, source_target_pairs={{0,4},{4,0},{8,12},{12,8},{1,5},{5,1},{9,13},{13,9},{2,6},{6,2},{1... | collective-permute-start | bytes 208904 | tf_op jit(solution)/shard_map/ppermute | solution.py:590
  21.3 4.2 %collective-permute-start.8 = (bf16[192,128]{1,0:T(8,128)(2,1)S(1)}, bf16[192,128]{1,0:T(8,128)(2,1)S(1)}, u32[]{:S(2)}, u32[]{:S(2)}) collective-permute-start(bf16[192,128]{1,0:T(8,128)(2,1)S(1)} %get-tuple-element.58.refs_4_), channel_id=1, source_target_pairs={{0,1},{1,0},{2,3},{3,2},{4,5},{5,4},{6,7},{7,6},{8,9},{9,8},{10,11... | collective-permute-start | bytes 147464 | tf_op jit(solution)/shard_map/ppermute | solution.py:590
  23.4 4.4 %collective-permute-start.7 = (bf16[272,128]{1,0:T(8,128)(2,1)S(1)}, bf16[272,128]{1,0:T(8,128)(2,1)S(1)}, u32[]{:S(2)}, u32[]{:S(2)}) collective-permute-start(bf16[272,128]{1,0:T(8,128)(2,1)S(1)} %shard_map.97.refs_3_.own), channel_id=1, source_target_pairs={{0,1},{1,0},{2,3},{3,2},{4,5},{5,4},{6,7},{7,6},{8,9},{9,8},{10,11... | collective-permute-start | bytes 208904 | tf_op jit(solution)/shard_map/ppermute | solution.py:590
  27.7 7.8 %copy-start = (f32[128]{0:T(128)S(1)}, f32[128]{0:T(128)}, u32[]{:S(2)}) copy-start(f32[128]{0:T(128)} %param.8) | copy-start | bytes 1540
  27.8 5.3 %collective-permute-start.9 = (bf16[272,128]{1,0:T(8,128)(2,1)S(1)}, bf16[272,128]{1,0:T(8,128)(2,1)S(1)}, u32[]{:S(2)}, u32[]{:S(2)}) collective-permute-start(bf16[272,128]{1,0:T(8,128)(2,1)S(1)} %shard_map.100.refs_2_.refs_0_), channel_id=1, source_target_pairs={{0,2},{1,3},{2,0},{3,1},{4,6},{5,7},{6,4},{7,5},{8,10},{9,11},{10,... | collective-permute-start | bytes 208904 | tf_op jit(solution)/shard_map/ppermute | solution.py:590
  28.8 9.3 %collective-permute-start.13 = (bf16[96,128]{1,0:T(8,128)(2,1)S(1)}, bf16[96,128]{1,0:T(8,128)(2,1)S(1)}, u32[]{:S(2)}, u32[]{:S(2)}) collective-permute-start(bf16[96,128]{1,0:T(8,128)(2,1)S(1)} %get-tuple-element.74), channel_id=1, source_target_pairs={{0,2},{1,3},{2,0},{3,1},{4,6},{5,7},{6,4},{7,5},{8,10},{9,11},{10,... | collective-permute-start | bytes 73736 | tf_op jit(solution)/shard_map/ppermute | solution.py:590
  33.2 4.9 %collective-permute-start.10 = (bf16[352,128]{1,0:T(8,128)(2,1)S(1)}, bf16[352,128]{1,0:T(8,128)(2,1)S(1)}, u32[]{:S(2)}, u32[]{:S(2)}) collective-permute-start(bf16[352,128]{1,0:T(8,128)(2,1)S(1)} %get-tuple-element.71), channel_id=1, source_target_pairs={{0,12},{4,8},{8,4},{12,0},{1,13},{5,9},{9,5},{13,1},{2,14},{6,10},... | collective-permute-start | bytes 270344 | tf_op jit(solution)/shard_map/ppermute | solution.py:590
  33.2 6.8 %collective-permute-start.11 = (bf16[352,128]{1,0:T(8,128)(2,1)S(1)}, bf16[352,128]{1,0:T(8,128)(2,1)S(1)}, u32[]{:S(2)}, u32[]{:S(2)}) collective-permute-start(bf16[352,128]{1,0:T(8,128)(2,1)S(1)} %get-tuple-element.72), channel_id=1, source_target_pairs={{0,8},{4,12},{8,0},{12,4},{1,9},{5,13},{9,1},{13,5},{2,10},{6,14},... | collective-permute-start | bytes 270344 | tf_op jit(solution)/shard_map/ppermute | solution.py:590
  35.5 4.6 %collective-permute-start.12 = (bf16[352,128]{1,0:T(8,128)(2,1)S(1)}, bf16[352,128]{1,0:T(8,128)(2,1)S(1)}, u32[]{:S(2)}, u32[]{:S(2)}) collective-permute-start(bf16[352,128]{1,0:T(8,128)(2,1)S(1)} %get-tuple-element.73), channel_id=1, source_target_pairs={{0,4},{4,0},{8,12},{12,8},{1,5},{5,1},{9,13},{13,9},{2,6},{6,2},{1... | collective-permute-start | bytes 270344 | tf_op jit(solution)/shard_map/ppermute | solution.py:590

commit v20 on v17

--- a/solution.py
+++ b/solution.py
@@ -139,15 +139,13 @@
 
 
 def join(pieces, axis, held):
-    half = lax.axis_size(axis) // 2
-    depth = pieces[0].shape[0] // half
+    depth = pieces[0].shape[0] // 2
     me = lax.axis_index(axis)
-    odd, home = lax.rem(me, 2), lax.div(me, 2)
-    for piece, parity in zip(pieces, (odd, 1 - odd), strict=True):
+    for p, piece in enumerate(pieces):
         block = piece[...].astype(F32)
-        for p in range(half):
-            place = (2 * lax.bitwise_xor(home, p) + parity) * depth
-            held[pl.ds(pl.multiple_of(place, depth), depth), :] = block[p * depth : (p + 1) * depth]
+        for n in range(2):
+            place = lax.bitwise_xor(me, 2 * p + n) * depth
+            held[pl.ds(pl.multiple_of(place, depth), depth), :] = block[n * depth : (n + 1) * depth]
 
 
 def repeat_matrix(sequences):
@@ -224,7 +222,9 @@
 def outer_kernel(i_n, j_n, *refs):
     depth = PROJECTED_DEPTH
     row_n = lax.axis_size("row")
-    a_pieces, b_pieces, refs = refs[:2], refs[2:4], refs[4:]
+    halves = [lax.axis_size("col") // 2, row_n // 2]
+    a_pieces, refs = refs[: halves[0]], refs[halves[0] :]
+    b_pieces, refs = refs[: halves[1]], refs[halves[1] :]
     g_ref, bias_ref, x_ref, a_held, b_wide = refs[:5]
     messages, (b_held, left, total) = refs[5 : 5 + row_n], refs[5 + row_n :]
     sequences = a_held.shape[0]
@@ -604,17 +604,17 @@
     sequences = second_homolog_features.shape[0] * row_n
     channels = final_projection_matrix.shape[0]
     res_total = i_n * row_n
-    a_far = from_evens(first_homolog_features, "col")
-    b_far = from_evens(second_homolog_features, "row")
+    a_near = swap(first_homolog_features, "col", 1)
+    b_near = swap(second_homolog_features, "row", 1)
     we, wt, a, b, w, g = load(
         first_homolog_features,
         second_homolog_features,
         final_projection_matrix,
         cotangent.reshape(i_n * j_n, PAIR_FEATURES),
     )
-    a, b = stack([a, *a_far], [b, *b_far])
-    a_pieces = [a, swap(a, "col", 1)]
-    b_pieces = [b, swap(b, "row", 1)]
+    a, b = stack([a, a_near], [b, b_near])
+    a_pieces = [a] + from_evens(a, "col")
+    b_pieces = [b] + from_evens(b, "row")
     y, gt, bias_rows = prepare(we, g, i_n, j_n)
 
     x, a_held, b_wide, (own, *messages) = outer(

time: 41.2 us -> 40.8 us (level)
  waiting for transfers between devices: 5.69 us -> 5.25 us
    ppermute x14, waiting for transfers between devices: 5.69 us -> 5.25 us  [swap(): lax.ppermute(x, axis, [(n, n ^ p) for n in range(lax.axis_size(axis))])]
  transfers between devices with their start and end apart: 14 -> 14, of which waited for: 7 -> 8; matrix products, arithmetic and copies ran while one was open for 0% -> 0% of each run, Pallas kernels for 28% -> 28%
where the time goes in v20:
time: 40.8 us; the launch traced here: 40.6 us
  starting transfers between devices  17.8 us (44%)
  Pallas kernels  16.9 us (41%)
  waiting for transfers between devices  5.25 us (13%)
  between operations  0.73 us (2%)
    ppermute x14, starting transfers between devices, swap(): lax.ppermute(x, axis, [(n, n ^ p) for n in range(lax.axis_size(axis))])  17.8 us
    ppermute x14, waiting for transfers between devices, swap(): lax.ppermute(x, axis, [(n, n ^ p) for n in range(lax.axis_size(axis))])  5.25 us
    pallas_call x1, Pallas kernels, outer(): pl.pallas_call(functools.partial(outer_kernel, i_n, j_n), in_specs=[in_vm...  4.4 us
    pallas_call x2, Pallas kernels, gradient(): pl.pallas_call(functools.partial(gradient_kernel, axis, plan, kept, posit...  4.12 us
    pallas_call x1, Pallas kernels, pair(): pl.pallas_call(functools.partial(pair_kernel, sequences), grid=(count,),...  2.55 us
    pallas_call x1, Pallas kernels, prepare(): pl.pallas_call(functools.partial(prepare_kernel, i_n, j_n), in_specs=[in_...  1.75 us
    pallas_call x1, Pallas kernels, product(): pl.pallas_call(product_kernel, in_specs=[in_vmem()] * 3 + [pl.BlockSpec(m...  1.55 us
    pallas_call x1, Pallas kernels, load(): pl.pallas_call(load_kernel, in_specs=[pl.BlockSpec(memory_space=pltpu.HBM...  1.39 us
  transfers between devices with their start and end apart: 14, of which 8 were waited for; matrix products, arithmetic and copies ran while one was open for 0% of the time, Pallas kernels for 28%

profile of v20, /device:TPU:0, one launch (start us, length us, event | category | flops | bytes accessed | tf_op | source)
XLA Modules:
  0.0 40.6 jit_solution(14124790380612432686)
XLA Ops:
  0.6 3.1 %collective-permute-start = (bf16[8,1536]{1,0:T(8,128)(2,1)}, bf16[8,1536]{1,0:T(8,128)(2,1)S(1)}, u32[]{:S(2)}, u32[]{:S(2)}) collective-permute-start(bf16[8,1536]{1,0:T(8,128)(2,1)} %a_hbm.1), channel_id=1, source_target_pairs={{0,1},{1,0},{2,3},{3,2},{4,5},{5,4},{6,7},{7,6},{8,9},{9,8},{10,11... | collective-permute-start | bytes 73736 | tf_op jit(solution)/shard_map/ppermute | solution.py:587
  3.7 0.0 collective-permute-start.1
  3.7 1.4 %shard_map.92 = (bf16[1024,128]{1,0:T(8,128)(2,1)S(1)}, bf16[128,1024]{1,0:T(8,128)(2,1)S(1)}, bf16[8,1536]{1,0:T(8,128)(2,1)S(1)}, bf16[8,1536]{1,0:T(8,128)(2,...) custom-call(bf16[8,1536]{1,0:T(8,128)(2,1)} %a_hbm.1, bf16[8,1536]{1,0:T(8,128)(2,1)} %b_hbm.1, ...), custom_call_target="tpu_custom_call" | custom-call | flops 131072000 | bytes 2097152 | tf_op jit(solution)/shard_map/pallas_call | solution.py:67
  5.1 0.6 %collective-permute-done.refs_1_ = bf16[8,1536]{1,0:T(8,128)(2,1)S(1)} collective-permute-done((bf16[8,1536]{1,0:T(8,128)(2,1)}, bf16[8,1536]{1,0:T(8,128)(2,1)S(1)}, u32[]{:S(2)}, u32[]{:S(2)}) %collective-permute-start) | collective-permute-done | bytes 24608 | tf_op jit(solution)/shard_map/ppermute | solution.py:587
  5.8 3.1 %collective-permute-start.2 = (bf16[16,1536]{1,0:T(8,128)(2,1)S(1)}, bf16[16,1536]{1,0:T(8,128)(2,1)S(1)}, u32[]{:S(2)}, u32[]{:S(2)}) collective-permute-start(bf16[16,1536]{1,0:T(8,128)(2,1)S(1)} %get-tuple-element.45.refs_0_), channel_id=1, source_target_pairs={{0,2},{1,3},{2,0},{3,1},{4,6},{5,7},{6,4},{7,5},{8,10},{9,11},{10,... | collective-permute-start | bytes 147464 | tf_op jit(solution)/shard_map/ppermute | solution.py:587
  8.9 1.5 %collective-permute-start.3 = (bf16[16,1536]{1,0:T(8,128)(2,1)S(1)}, bf16[16,1536]{1,0:T(8,128)(2,1)S(1)}, u32[]{:S(2)}, u32[]{:S(2)}) collective-permute-start(bf16[16,1536]{1,0:T(8,128)(2,1)S(1)} %get-tuple-element.46.refs_2_), channel_id=1, source_target_pairs={{0,8},{4,12},{8,0},{12,4},{1,9},{5,13},{9,1},{13,5},{2,10},{6,14},... | collective-permute-start | bytes 147464 | tf_op jit(solution)/shard_map/ppermute | solution.py:587
  10.3 1.8 %shard_map.94 = (bf16[1024,2304]{1,0:T(8,128)(2,1)S(1)}, bf16[2304,128]{1,0:T(8,128)(2,1)S(1)}, bf16[16,128]{1,0:T(8,128)(2,1)S(1)}) custom-call(bf16[1024,128]{1,0:T(8,128)(2,1)S(1)} %get-tuple-element.48.we_ref, bf16[2304,128]{1,0:T(8,128)(2,1)S(1)} %get-tuple-element.47.g_ref.refs_4_), custom_call_target="tpu_custom_call" | custom-call | flops 603979776 | bytes 9437184 | tf_op jit(solution)/shard_map/pallas_call | solution.py:126
  12.1 0.0 collective-permute-done.2.refs_1_
  12.1 0.8 %collective-permute-done.3.refs_3_ = bf16[16,1536]{1,0:T(8,128)(2,1)S(1)} collective-permute-done((bf16[16,1536]{1,0:T(8,128)(2,1)S(1)}, bf16[16,1536]{1,0:T(8,128)(2,1)S(1)}, u32[]{:S(2)}, u32[]{:S(2)}) %collective-permute-start.3) | collective-permute-done | bytes 49184 | tf_op jit(solution)/shard_map/ppermute | solution.py:587
  12.9 4.4 %shard_map.95 = (bf16[1024,2304]{1,0:T(8,128)(2,1)S(1)}, f32[32,1536]{1,0:T(8,128)S(1)}, f32[1,1536,128]{2,1,0:T(8,128)S(1)}, f32[272,128]{1,0:T(8,128)S(1)}, bf...) custom-call(bf16[16,1536]{1,0:T(8,128)(2,1)S(1)} %get-tuple-element.45.refs_0_, ...), custom_call_target="tpu_custom_call" | custom-call | flops 1207959552 | bytes 4718592 | tf_op jit(solution)/shard_map/pallas_call | solution.py:290
  17.4 0.1 collective-permute-start.4
  17.4 1.5 %collective-permute-start.5 = (bf16[272,128]{1,0:T(8,128)(2,1)S(1)}, bf16[272,128]{1,0:T(8,128)(2,1)S(1)}, u32[]{:S(2)}, u32[]{:S(2)}) collective-permute-start(bf16[272,128]{1,0:T(8,128)(2,1)S(1)} %get-tuple-element.54), channel_id=1, source_target_pairs={{0,8},{4,12},{8,0},{12,4},{1,9},{5,13},{9,1},{13,5},{2,10},{6,14},... | collective-permute-start | bytes 208904 | tf_op jit(solution)/shard_map/ppermute | solution.py:587
  19.0 0.3 collective-permute-start.6
  19.3 2.1 %shard_map.96 = (f32[96,128]{1,0:T(8,128)S(1)}, f32[96,128]{1,0:T(8,128)S(1)}, bf16[192,128]{1,0:T(8,128)(2,1)S(1)}) custom-call(f32[1,1536,128]{2,1,0:T(8,128)S(1)} %get-tuple-element.56.refs_0_, bf16[1024,2304]{1,0:T(8,128)(2,1)S(1)} %get-tuple-element.57.refs_1_, f32[272,128]{1,0:T(8,128)S(1)} %get-tuple-element.52.refs_2_.refs_0_), custom_call_target="tpu_custom_call" | custom-call | flops 603979776 | bytes 4718592 | tf_op jit(solution)/shard_map/pallas_call | solution.py:378
  21.4 1.6 %collective-permute-start.8 = (bf16[192,128]{1,0:T(8,128)(2,1)S(1)}, bf16[192,128]{1,0:T(8,128)(2,1)S(1)}, u32[]{:S(2)}, u32[]{:S(2)}) collective-permute-start(bf16[192,128]{1,0:T(8,128)(2,1)S(1)} %get-tuple-element.58.refs_4_), channel_id=1, source_target_pairs={{0,1},{1,0},{2,3},{3,2},{4,5},{5,4},{6,7},{7,6},{8,9},{9,8},{10,11... | collective-permute-start | bytes 147464 | tf_op jit(solution)/shard_map/ppermute | solution.py:587
  23.0 0.4 collective-permute-done.5.refs_2_
  23.4 1.6 %collective-permute-start.7 = (bf16[272,128]{1,0:T(8,128)(2,1)S(1)}, bf16[272,128]{1,0:T(8,128)(2,1)S(1)}, u32[]{:S(2)}, u32[]{:S(2)}) collective-permute-start(bf16[272,128]{1,0:T(8,128)(2,1)S(1)} %shard_map.97.refs_3_.own), channel_id=1, source_target_pairs={{0,1},{1,0},{2,3},{3,2},{4,5},{5,4},{6,7},{7,6},{8,9},{9,8},{10,11... | collective-permute-start | bytes 208904 | tf_op jit(solution)/shard_map/ppermute | solution.py:587
  25.1 0.4 %collective-permute-done.8.refs_2_ = bf16[192,128]{1,0:T(8,128)(2,1)S(1)} collective-permute-done((bf16[192,128]{1,0:T(8,128)(2,1)S(1)}, bf16[192,128]{1,0:T(8,128)(2,1)S(1)}, u32[]{:S(2)}, u32[]{:S(2)}) %collective-permute-start.8) | collective-permute-done | bytes 49184 | tf_op jit(solution)/shard_map/ppermute | solution.py:587
  25.5 1.5 %shard_map.99 = (bf16[1024,2304]{1,0:T(8,128)(2,1)S(1)}, f32[1,1536,128]{2,1,0:T(8,128)S(1)}) custom-call(bf16[1024,128]{1,0:T(8,128)(2,1)S(1)} %get-tuple-element.59.left_ref, bf16[2304,128]{1,0:T(8,128)(2,1)S(1)} %get-tuple-element.60.right_ref, f32[32,1536]{1,0:T(8,128)S(1)} %get-tuple-element.61.held, f32[96,128]{1,0:T(8,128)S(1)} %get-tuple-element.64._.refs_4_), custom_call_target="tpu_custom_call" | custom-call | flops 603979776 | bytes 9437184 | tf_op jit(solution)/shard_map/pallas_call | solution.py:406
  27.1 0.7 %collective-permute-done.7.near = bf16[272,128]{1,0:T(8,128)(2,1)S(1)} collective-permute-done((bf16[272,128]{1,0:T(8,128)(2,1)S(1)}, bf16[272,128]{1,0:T(8,128)(2,1)S(1)}, u32[]{:S(2)}, u32[]{:S(2)}) %collective-permute-start.7) | collective-permute-done | bytes 69664 | tf_op jit(solution)/shard_map/ppermute | solution.py:587
  27.8 1.1 %collective-permute-start.9 = (bf16[272,128]{1,0:T(8,128)(2,1)S(1)}, bf16[272,128]{1,0:T(8,128)(2,1)S(1)}, u32[]{:S(2)}, u32[]{:S(2)}) collective-permute-start(bf16[272,128]{1,0:T(8,128)(2,1)S(1)} %shard_map.100.refs_2_.refs_0_), channel_id=1, source_target_pairs={{0,2},{1,3},{2,0},{3,1},{4,6},{5,7},{6,4},{7,5},{8,10},{9,11},{10,... | collective-permute-start | bytes 208904 | tf_op jit(solution)/shard_map/ppermute | solution.py:587
  28.9 1.9 %collective-permute-start.13 = (bf16[96,128]{1,0:T(8,128)(2,1)S(1)}, bf16[96,128]{1,0:T(8,128)(2,1)S(1)}, u32[]{:S(2)}, u32[]{:S(2)}) collective-permute-start(bf16[96,128]{1,0:T(8,128)(2,1)S(1)} %get-tuple-element.74), channel_id=1, source_target_pairs={{0,2},{1,3},{2,0},{3,1},{4,6},{5,7},{6,4},{7,5},{8,10},{9,11},{10,... | collective-permute-start | bytes 73736 | tf_op jit(solution)/shard_map/ppermute | solution.py:587
  30.8 2.1 %shard_map.101 = (f32[96,128]{1,0:T(8,128)S(1)}, bf16[96,128]{1,0:T(8,128)(2,1)S(1)}, bf16[96,128]{1,0:T(8,128)(2,1)S(1)}, bf16[96,128]{1,0:T(8,128)(2,1)S(1)}) custom-call(f32[1,1536,128]{2,1,0:T(8,128)S(1)} %get-tuple-element.66.refs_0_, bf16[1024,2304]{1,0:T(8,128)(2,1)S(1)} %get-tuple-element.65._.refs_1_, bf16[272,128]{1,0:T(8,128)(2,1)S(1)} %shard_map.100.refs_2_.refs_0_), custom_call_target="tpu_custom_call" | custom-call | flops 603979776 | bytes 4718592 | tf_op jit(solution)/shard_map/pallas_call | solution.py:378
  32.9 0.5 %collective-permute-done.9.refs_1_ = bf16[272,128]{1,0:T(8,128)(2,1)S(1)} collective-permute-done((bf16[272,128]{1,0:T(8,128)(2,1)S(1)}, bf16[272,128]{1,0:T(8,128)(2,1)S(1)}, u32[]{:S(2)}, u32[]{:S(2)}) %collective-permute-start.9) | collective-permute-done | bytes 69664 | tf_op jit(solution)/shard_map/ppermute | solution.py:587
  33.4 0.1 shard_map.102
  33.5 0.1 collective-permute-start.10
  33.6 1.2 %collective-permute-start.11 = (bf16[352,128]{1,0:T(8,128)(2,1)S(1)}, bf16[352,128]{1,0:T(8,128)(2,1)S(1)}, u32[]{:S(2)}, u32[]{:S(2)}) collective-permute-start(bf16[352,128]{1,0:T(8,128)(2,1)S(1)} %get-tuple-element.72), channel_id=1, source_target_pairs={{0,8},{4,12},{8,0},{12,4},{1,9},{5,13},{9,1},{13,5},{2,10},{6,14},... | collective-permute-start | bytes 270344 | tf_op jit(solution)/shard_map/ppermute | solution.py:587
  34.8 0.7 %collective-permute-start.12 = (bf16[352,128]{1,0:T(8,128)(2,1)S(1)}, bf16[352,128]{1,0:T(8,128)(2,1)S(1)}, u32[]{:S(2)}, u32[]{:S(2)}) collective-permute-start(bf16[352,128]{1,0:T(8,128)(2,1)S(1)} %get-tuple-element.73), channel_id=1, source_target_pairs={{0,4},{4,0},{8,12},{12,8},{1,5},{5,1},{9,13},{13,9},{2,6},{6,2},{1... | collective-permute-start | bytes 270344 | tf_op jit(solution)/shard_map/ppermute | solution.py:587
  35.4 2.5 %shard_map.103 = bf16[2304,128]{1,0:T(8,128)(2,1)} custom-call(bf16[1024,2304]{1,0:T(8,128)(2,1)S(1)} %get-tuple-element.50.x_ref, bf16[128,1024]{1,0:T(8,128)(2,1)S(1)} %get-tuple-element.51.wt_ref, f32[1,128]{1,0:T(1,128)S(1)} %bitcast.4, bf16[256,128]{1,0:T(8,128)(2,1)S(1)} %get-tuple-element.70._.refs_0_), custom_call_target="tpu_custom_call" | custom-call | flops 1207959552 | bytes 4718592 | tf_op jit(solution)/shard_map/pallas_call | solution.py:429
  38.0 0.5 %collective-permute-done.10.refs_1_ = bf16[352,128]{1,0:T(8,128)(2,1)S(1)} collective-permute-done((bf16[352,128]{1,0:T(8,128)(2,1)S(1)}, bf16[352,128]{1,0:T(8,128)(2,1)S(1)}, u32[]{:S(2)}, u32[]{:S(2)}) %collective-permute-start.10) | collective-permute-done | bytes 90144 | tf_op jit(solution)/shard_map/ppermute | solution.py:587
  38.5 1.3 %collective-permute-done.11.refs_2_ = bf16[352,128]{1,0:T(8,128)(2,1)S(1)} collective-permute-done((bf16[352,128]{1,0:T(8,128)(2,1)S(1)}, bf16[352,128]{1,0:T(8,128)(2,1)S(1)}, u32[]{:S(2)}, u32[]{:S(2)}) %collective-permute-start.11) | collective-permute-done | bytes 90144 | tf_op jit(solution)/shard_map/ppermute | solution.py:587
  39.7 0.9 %shard_map.104 = (f32[1024,128]{1,0:T(8,128)}, f32[8,1536]{1,0:T(8,128)}, f32[8,1536]{1,0:T(8,128)}, f32[1,128]{1,0:T(1,128)}) custom-call(bf16[256,128]{1,0:T(8,128)(2,1)S(1)} %get-tuple-element.70._.refs_0_, bf16[352,128]{1,0:T(8,128)(2,1)S(1)} %collective-permute-done.10.refs_1_, bf16[352,128]{1,0:T(8,128)(2,1)S(1)} %collective-permute-done.11.refs_2_, ...), custom_call_target="tpu_custom_call" | custom-call | tf_op jit(solution)/shard_map/pallas_call | solution.py:456
  (11 shorter events, 0.1 us)
Async XLA Ops:
  0.6 5.1 %collective-permute-start = (bf16[8,1536]{1,0:T(8,128)(2,1)}, bf16[8,1536]{1,0:T(8,128)(2,1)S(1)}, u32[]{:S(2)}, u32[]{:S(2)}) collective-permute-start(bf16[8,1536]{1,0:T(8,128)(2,1)} %a_hbm.1), channel_id=1, source_target_pairs={{0,1},{1,0},{2,3},{3,2},{4,5},{5,4},{6,7},{7,6},{8,9},{9,8},{10,11... | collective-permute-start | bytes 73736 | tf_op jit(solution)/shard_map/ppermute | solution.py:587
  3.7 2.0 %collective-permute-start.1 = (bf16[8,1536]{1,0:T(8,128)(2,1)}, bf16[8,1536]{1,0:T(8,128)(2,1)S(1)}, u32[]{:S(2)}, u32[]{:S(2)}) collective-permute-start(bf16[8,1536]{1,0:T(8,128)(2,1)} %b_hbm.1), channel_id=1, source_target_pairs={{0,4},{4,0},{8,12},{12,8},{1,5},{5,1},{9,13},{13,9},{2,6},{6,2},{1... | collective-permute-start | bytes 73736 | tf_op jit(solution)/shard_map/ppermute | solution.py:587
  5.8 6.4 %collective-permute-start.2 = (bf16[16,1536]{1,0:T(8,128)(2,1)S(1)}, bf16[16,1536]{1,0:T(8,128)(2,1)S(1)}, u32[]{:S(2)}, u32[]{:S(2)}) collective-permute-start(bf16[16,1536]{1,0:T(8,128)(2,1)S(1)} %get-tuple-element.45.refs_0_), channel_id=1, source_target_pairs={{0,2},{1,3},{2,0},{3,1},{4,6},{5,7},{6,4},{7,5},{8,10},{9,11},{10,... | collective-permute-start | bytes 147464 | tf_op jit(solution)/shard_map/ppermute | solution.py:587
  8.9 4.1 %collective-permute-start.3 = (bf16[16,1536]{1,0:T(8,128)(2,1)S(1)}, bf16[16,1536]{1,0:T(8,128)(2,1)S(1)}, u32[]{:S(2)}, u32[]{:S(2)}) collective-permute-start(bf16[16,1536]{1,0:T(8,128)(2,1)S(1)} %get-tuple-element.46.refs_2_), channel_id=1, source_target_pairs={{0,8},{4,12},{8,0},{12,4},{1,9},{5,13},{9,1},{13,5},{2,10},{6,14},... | collective-permute-start | bytes 147464 | tf_op jit(solution)/shard_map/ppermute | solution.py:587
  17.4 5.6 %collective-permute-start.4 = (bf16[272,128]{1,0:T(8,128)(2,1)S(1)}, bf16[272,128]{1,0:T(8,128)(2,1)S(1)}, u32[]{:S(2)}, u32[]{:S(2)}) collective-permute-start(bf16[272,128]{1,0:T(8,128)(2,1)S(1)} %get-tuple-element.53), channel_id=1, source_target_pairs={{0,12},{4,8},{8,4},{12,0},{1,13},{5,9},{9,5},{13,1},{2,14},{6,10},... | collective-permute-start | bytes 208904 | tf_op jit(solution)/shard_map/ppermute | solution.py:587
  17.4 6.0 %collective-permute-start.5 = (bf16[272,128]{1,0:T(8,128)(2,1)S(1)}, bf16[272,128]{1,0:T(8,128)(2,1)S(1)}, u32[]{:S(2)}, u32[]{:S(2)}) collective-permute-start(bf16[272,128]{1,0:T(8,128)(2,1)S(1)} %get-tuple-element.54), channel_id=1, source_target_pairs={{0,8},{4,12},{8,0},{12,4},{1,9},{5,13},{9,1},{13,5},{2,10},{6,14},... | collective-permute-start | bytes 208904 | tf_op jit(solution)/shard_map/ppermute | solution.py:587
  19.0 4.4 %collective-permute-start.6 = (bf16[272,128]{1,0:T(8,128)(2,1)S(1)}, bf16[272,128]{1,0:T(8,128)(2,1)S(1)}, u32[]{:S(2)}, u32[]{:S(2)}) collective-permute-start(bf16[272,128]{1,0:T(8,128)(2,1)S(1)} %get-tuple-element.55), channel_id=1, source_target_pairs={{0,4},{4,0},{8,12},{12,8},{1,5},{5,1},{9,13},{13,9},{2,6},{6,2},{1... | collective-permute-start | bytes 208904 | tf_op jit(solution)/shard_map/ppermute | solution.py:587
  21.4 4.2 %collective-permute-start.8 = (bf16[192,128]{1,0:T(8,128)(2,1)S(1)}, bf16[192,128]{1,0:T(8,128)(2,1)S(1)}, u32[]{:S(2)}, u32[]{:S(2)}) collective-permute-start(bf16[192,128]{1,0:T(8,128)(2,1)S(1)} %get-tuple-element.58.refs_4_), channel_id=1, source_target_pairs={{0,1},{1,0},{2,3},{3,2},{4,5},{5,4},{6,7},{7,6},{8,9},{9,8},{10,11... | collective-permute-start | bytes 147464 | tf_op jit(solution)/shard_map/ppermute | solution.py:587
  23.4 4.4 %collective-permute-start.7 = (bf16[272,128]{1,0:T(8,128)(2,1)S(1)}, bf16[272,128]{1,0:T(8,128)(2,1)S(1)}, u32[]{:S(2)}, u32[]{:S(2)}) collective-permute-start(bf16[272,128]{1,0:T(8,128)(2,1)S(1)} %shard_map.97.refs_3_.own), channel_id=1, source_target_pairs={{0,1},{1,0},{2,3},{3,2},{4,5},{5,4},{6,7},{7,6},{8,9},{9,8},{10,11... | collective-permute-start | bytes 208904 | tf_op jit(solution)/shard_map/ppermute | solution.py:587
  27.8 7.6 %copy-start = (f32[128]{0:T(128)S(1)}, f32[128]{0:T(128)}, u32[]{:S(2)}) copy-start(f32[128]{0:T(128)} %param.8) | copy-start | bytes 1540
  27.8 5.5 %collective-permute-start.9 = (bf16[272,128]{1,0:T(8,128)(2,1)S(1)}, bf16[272,128]{1,0:T(8,128)(2,1)S(1)}, u32[]{:S(2)}, u32[]{:S(2)}) collective-permute-start(bf16[272,128]{1,0:T(8,128)(2,1)S(1)} %shard_map.100.refs_2_.refs_0_), channel_id=1, source_target_pairs={{0,2},{1,3},{2,0},{3,1},{4,6},{5,7},{6,4},{7,5},{8,10},{9,11},{10,... | collective-permute-start | bytes 208904 | tf_op jit(solution)/shard_map/ppermute | solution.py:587
  28.9 9.1 %collective-permute-start.13 = (bf16[96,128]{1,0:T(8,128)(2,1)S(1)}, bf16[96,128]{1,0:T(8,128)(2,1)S(1)}, u32[]{:S(2)}, u32[]{:S(2)}) collective-permute-start(bf16[96,128]{1,0:T(8,128)(2,1)S(1)} %get-tuple-element.74), channel_id=1, source_target_pairs={{0,2},{1,3},{2,0},{3,1},{4,6},{5,7},{6,4},{7,5},{8,10},{9,11},{10,... | collective-permute-start | bytes 73736 | tf_op jit(solution)/shard_map/ppermute | solution.py:587
  33.5 5.0 %collective-permute-start.10 = (bf16[352,128]{1,0:T(8,128)(2,1)S(1)}, bf16[352,128]{1,0:T(8,128)(2,1)S(1)}, u32[]{:S(2)}, u32[]{:S(2)}) collective-permute-start(bf16[352,128]{1,0:T(8,128)(2,1)S(1)} %get-tuple-element.71), channel_id=1, source_target_pairs={{0,12},{4,8},{8,4},{12,0},{1,13},{5,9},{9,5},{13,1},{2,14},{6,10},... | collective-permute-start | bytes 270344 | tf_op jit(solution)/shard_map/ppermute | solution.py:587
  33.6 6.2 %collective-permute-start.11 = (bf16[352,128]{1,0:T(8,128)(2,1)S(1)}, bf16[352,128]{1,0:T(8,128)(2,1)S(1)}, u32[]{:S(2)}, u32[]{:S(2)}) collective-permute-start(bf16[352,128]{1,0:T(8,128)(2,1)S(1)} %get-tuple-element.72), channel_id=1, source_target_pairs={{0,8},{4,12},{8,0},{12,4},{1,9},{5,13},{9,1},{13,5},{2,10},{6,14},... | collective-permute-start | bytes 270344 | tf_op jit(solution)/shard_map/ppermute | solution.py:587
  34.8 5.0 %collective-permute-start.12 = (bf16[352,128]{1,0:T(8,128)(2,1)S(1)}, bf16[352,128]{1,0:T(8,128)(2,1)S(1)}, u32[]{:S(2)}, u32[]{:S(2)}) collective-permute-start(bf16[352,128]{1,0:T(8,128)(2,1)S(1)} %get-tuple-element.73), channel_id=1, source_target_pairs={{0,4},{4,0},{8,12},{12,8},{1,5},{5,1},{9,13},{13,9},{2,6},{6,2},{1... | collective-permute-start | bytes 270344 | tf_op jit(solution)/shard_map/ppermute | solution.py:587

commit v21 on v20

--- a/solution.py
+++ b/solution.py
@@ -307,21 +307,14 @@
     return *results[:3], results[3:]
 
 
-def gradient_kernel(axis, plan, kept, positions, others, sequences, *refs):
+def add_channels(wide, source, result, steps, positions, others, sequences):
     depth = PROJECTED_DEPTH
-    wide, source = refs[:2]
-    outs, (result, grown, grad) = refs[3:-3], refs[-3:]
-    parts = lax.axis_size(axis)
     per_step = depth // CHUNKS
     span = GROUP * others
 
-    result[...] = jnp.zeros(result.shape, F32)
-
-    @chunks
-    def _(t):
+    def step(t):
         size = per_step * depth
-        rows = pl.ds(t * size if CHUNKS == 1 else pl.multiple_of(t * size, size), size)
-        part = source.at[rows]
+        part = source.at[pl.ds(t * size if len(steps) == 1 else pl.multiple_of(t * size, size), size)]
         for n in range(0, per_step, 2):
             blocks = [
                 jnp.concatenate(
@@ -338,6 +331,41 @@
             ]
             result[...] += dot(jnp.concatenate(blocks, axis=0), jnp.concatenate(right, axis=0))
 
+    if len(steps) == 1:
+        step(steps[0])
+    else:
+        pl.loop(steps[0], steps[-1] + 1)(step)
+
+
+def gradient_start_kernel(positions, others, sequences, wide, source, result):
+    result[...] = jnp.zeros(result.shape, F32)
+    steps = range(CHUNKS // 2)
+    add_channels(wide, source, result, steps, positions, others, sequences)
+
+
+def gradient_start(wide, source, positions, others, sequences):
+    shape = (positions // GROUP * PROJECTED_DEPTH, GROUP * sequences)
+    return pl.pallas_call(
+        functools.partial(gradient_start_kernel, positions, others, sequences),
+        in_specs=[in_vmem()] * 2,
+        out_specs=in_vmem(),
+        out_shape=jax.ShapeDtypeStruct(shape, F32),
+        compiler_params=params(sequences),
+        cost_estimate=pl.CostEstimate(
+            flops=source.size * PAIR_FEATURES, bytes_accessed=source.size, transcendentals=0
+        ),
+    )(wide, source)
+
+
+def gradient_kernel(axis, plan, kept, positions, others, sequences, started, *refs):
+    depth = PROJECTED_DEPTH
+    wide, source = refs[:2]
+    outs, (result, grown, grad) = refs[3 + started : -3], refs[-3:]
+    parts = lax.axis_size(axis)
+    result[...] = refs[3][...] if started else jnp.zeros(result.shape, F32)
+    steps = range(CHUNKS // 2 if started else 0, CHUNKS)
+    add_channels(wide, source, result, steps, positions, others, sequences)
+
     scaled = (result[...] * (1.0 / sequences)).astype(BF16)
     for l in range(scaled.shape[1] // LANES):
         members = dict(tiles_of(sequences, l))
@@ -368,7 +396,9 @@
             out[n * size : (n + 1) * size, :] = rows_of(p).astype(BF16)
 
 
-def gradient(wide, source, after, axis, plan, kept, groups, positions, others, sequences):
+def gradient(
+    wide, source, after, axis, plan, kept, groups, positions, others, sequences, before=()
+):
     depth = PROJECTED_DEPTH
     parts = lax.axis_size(axis)
     rows = sequences // parts * positions * depth // LANES
@@ -376,8 +406,11 @@
     group = (parts - kept) // groups
     shapes += [jax.ShapeDtypeStruct((group * rows, LANES), BF16)] * groups
     results = pl.pallas_call(
-        functools.partial(gradient_kernel, axis, plan, kept, positions, others, sequences),
-        in_specs=[in_vmem(), in_vmem(), pl.BlockSpec(memory_space=pl.ANY)],
+        functools.partial(
+            gradient_kernel, axis, plan, kept, positions, others, sequences, len(before)
+        ),
+        in_specs=[in_vmem(), in_vmem(), pl.BlockSpec(memory_space=pl.ANY)]
+        + [in_vmem()] * len(before),
         out_specs=[in_vmem()] * len(shapes),
         out_shape=shapes,
         scratch_shapes=[
@@ -391,7 +424,7 @@
             bytes_accessed=2 * source.size,
             transcendentals=0,
         ),
-    )(wide, source, after)
+    )(wide, source, after, *before)
     return results[:kept], results[kept:]
 
 
@@ -634,10 +667,11 @@
     left = [left_own] + swap_each(left_messages, "col", 2)
     y2, a_wide = product(w, gt, a_held, left_own)
 
-    message = column_pair_sum(message, near, y2, share)
+    before = gradient_start(a_wide, y2, j_n, i_n, sequences)
+    message = column_pair_sum(message, near, before, share)
     parts = [message] + from_evens(message, "col")
     (right_own,), right_sent = gradient(
-        a_wide, y2, message, "row", alone(row_n), 1, row_n - 1, j_n, i_n, sequences
+        a_wide, y2, message, "row", alone(row_n), 1, row_n - 1, j_n, i_n, sequences, [before]
     )
 
     messages, piece, bias = column_sum(parts, right_sent, share)

time: 40.8 us -> 41.2 us (level)
    pallas_call x0 -> x1, Pallas kernels: none -> 0.8 us  [gradient_start(): pl.pallas_call(functools.partial(gradient_start_kernel, positions, others...]
    pallas_call x2, Pallas kernels: 4.12 us -> 3.61 us  [gradient(): pl.pallas_call(functools.partial(gradient_kernel, axis, plan, kept, posit...]
  transfers between devices with their start and end apart: 14 -> 14, of which waited for: 8 -> 6; matrix products, arithmetic and copies ran while one was open for 0% -> 0% of each run, Pallas kernels for 28% -> 29%
where the time goes in v21:
time: 41.2 us; the launch traced here: 41 us
  starting transfers between devices  17.8 us (43%)
  Pallas kernels  17.2 us (42%)
  waiting for transfers between devices  5.26 us (13%)
  between operations  0.75 us (2%)
    ppermute x14, starting transfers between devices, swap(): lax.ppermute(x, axis, [(n, n ^ p) for n in range(lax.axis_size(axis))])  17.8 us
    ppermute x14, waiting for transfers between devices, swap(): lax.ppermute(x, axis, [(n, n ^ p) for n in range(lax.axis_size(axis))])  5.26 us
    pallas_call x1, Pallas kernels, outer(): pl.pallas_call(functools.partial(outer_kernel, i_n, j_n), in_specs=[in_vm...  4.4 us
    pallas_call x2, Pallas kernels, gradient(): pl.pallas_call(functools.partial(gradient_kernel, axis, plan, kept, posit...  3.61 us
    pallas_call x1, Pallas kernels, pair(): pl.pallas_call(functools.partial(pair_kernel, sequences), grid=(count,),...  2.55 us
    pallas_call x1, Pallas kernels, prepare(): pl.pallas_call(functools.partial(prepare_kernel, i_n, j_n), in_specs=[in_...  1.76 us
    pallas_call x1, Pallas kernels, product(): pl.pallas_call(product_kernel, in_specs=[in_vmem()] * 3 + [pl.BlockSpec(m...  1.55 us
    pallas_call x1, Pallas kernels, load(): pl.pallas_call(load_kernel, in_specs=[pl.BlockSpec(memory_space=pltpu.HBM...  1.39 us
  transfers between devices with their start and end apart: 14, of which 6 were waited for; matrix products, arithmetic and copies ran while one was open for 0% of the time, Pallas kernels for 29%

profile of v21, /device:TPU:0, one launch (start us, length us, event | category | flops | bytes accessed | tf_op | source)
XLA Modules:
  0.0 41.0 jit_solution(3004958047748894130)
XLA Ops:
  0.6 3.1 %collective-permute-start = (bf16[8,1536]{1,0:T(8,128)(2,1)}, bf16[8,1536]{1,0:T(8,128)(2,1)S(1)}, u32[]{:S(2)}, u32[]{:S(2)}) collective-permute-start(bf16[8,1536]{1,0:T(8,128)(2,1)} %a_hbm.1), channel_id=1, source_target_pairs={{0,1},{1,0},{2,3},{3,2},{4,5},{5,4},{6,7},{7,6},{8,9},{9,8},{10,11... | collective-permute-start | bytes 73736 | tf_op jit(solution)/shard_map/ppermute | solution.py:620
  3.7 0.0 collective-permute-start.1
  3.7 1.4 %shard_map.92 = (bf16[1024,128]{1,0:T(8,128)(2,1)S(1)}, bf16[128,1024]{1,0:T(8,128)(2,1)S(1)}, bf16[8,1536]{1,0:T(8,128)(2,1)S(1)}, bf16[8,1536]{1,0:T(8,128)(2,...) custom-call(bf16[8,1536]{1,0:T(8,128)(2,1)} %a_hbm.1, bf16[8,1536]{1,0:T(8,128)(2,1)} %b_hbm.1, ...), custom_call_target="tpu_custom_call" | custom-call | flops 131072000 | bytes 2097152 | tf_op jit(solution)/shard_map/pallas_call | solution.py:67
  5.1 0.6 %collective-permute-done.refs_1_ = bf16[8,1536]{1,0:T(8,128)(2,1)S(1)} collective-permute-done((bf16[8,1536]{1,0:T(8,128)(2,1)}, bf16[8,1536]{1,0:T(8,128)(2,1)S(1)}, u32[]{:S(2)}, u32[]{:S(2)}) %collective-permute-start) | collective-permute-done | bytes 24608 | tf_op jit(solution)/shard_map/ppermute | solution.py:620
  5.7 0.0 collective-permute-done.1.refs_3_
  5.8 3.1 %collective-permute-start.2 = (bf16[16,1536]{1,0:T(8,128)(2,1)S(1)}, bf16[16,1536]{1,0:T(8,128)(2,1)S(1)}, u32[]{:S(2)}, u32[]{:S(2)}) collective-permute-start(bf16[16,1536]{1,0:T(8,128)(2,1)S(1)} %get-tuple-element.45.refs_0_), channel_id=1, source_target_pairs={{0,2},{1,3},{2,0},{3,1},{4,6},{5,7},{6,4},{7,5},{8,10},{9,11},{10,... | collective-permute-start | bytes 147464 | tf_op jit(solution)/shard_map/ppermute | solution.py:620
  8.9 1.5 %collective-permute-start.3 = (bf16[16,1536]{1,0:T(8,128)(2,1)S(1)}, bf16[16,1536]{1,0:T(8,128)(2,1)S(1)}, u32[]{:S(2)}, u32[]{:S(2)}) collective-permute-start(bf16[16,1536]{1,0:T(8,128)(2,1)S(1)} %get-tuple-element.46.refs_2_), channel_id=1, source_target_pairs={{0,8},{4,12},{8,0},{12,4},{1,9},{5,13},{9,1},{13,5},{2,10},{6,14},... | collective-permute-start | bytes 147464 | tf_op jit(solution)/shard_map/ppermute | solution.py:620
  10.3 1.8 %shard_map.94 = (bf16[1024,2304]{1,0:T(8,128)(2,1)S(1)}, bf16[2304,128]{1,0:T(8,128)(2,1)S(1)}, bf16[16,128]{1,0:T(8,128)(2,1)S(1)}) custom-call(bf16[1024,128]{1,0:T(8,128)(2,1)S(1)} %get-tuple-element.48.we_ref, bf16[2304,128]{1,0:T(8,128)(2,1)S(1)} %get-tuple-element.47.g_ref.refs_4_), custom_call_target="tpu_custom_call" | custom-call | flops 603979776 | bytes 9437184 | tf_op jit(solution)/shard_map/pallas_call | solution.py:126
  12.1 0.8 %collective-permute-done.3.refs_3_ = bf16[16,1536]{1,0:T(8,128)(2,1)S(1)} collective-permute-done((bf16[16,1536]{1,0:T(8,128)(2,1)S(1)}, bf16[16,1536]{1,0:T(8,128)(2,1)S(1)}, u32[]{:S(2)}, u32[]{:S(2)}) %collective-permute-start.3) | collective-permute-done | bytes 49184 | tf_op jit(solution)/shard_map/ppermute | solution.py:620
  12.9 4.4 %shard_map.95 = (bf16[1024,2304]{1,0:T(8,128)(2,1)S(1)}, f32[32,1536]{1,0:T(8,128)S(1)}, f32[1,1536,128]{2,1,0:T(8,128)S(1)}, f32[272,128]{1,0:T(8,128)S(1)}, bf...) custom-call(bf16[16,1536]{1,0:T(8,128)(2,1)S(1)} %get-tuple-element.45.refs_0_, ...), custom_call_target="tpu_custom_call" | custom-call | flops 1207959552 | bytes 4718592 | tf_op jit(solution)/shard_map/pallas_call | solution.py:290
  17.3 0.1 collective-permute-start.4
  17.4 1.6 %collective-permute-start.5 = (bf16[272,128]{1,0:T(8,128)(2,1)S(1)}, bf16[272,128]{1,0:T(8,128)(2,1)S(1)}, u32[]{:S(2)}, u32[]{:S(2)}) collective-permute-start(bf16[272,128]{1,0:T(8,128)(2,1)S(1)} %get-tuple-element.54), channel_id=1, source_target_pairs={{0,8},{4,12},{8,0},{12,4},{1,9},{5,13},{9,1},{13,5},{2,10},{6,14},... | collective-permute-start | bytes 208904 | tf_op jit(solution)/shard_map/ppermute | solution.py:620
  19.0 0.3 collective-permute-start.6
  19.3 2.1 %shard_map.96 = (f32[96,128]{1,0:T(8,128)S(1)}, f32[96,128]{1,0:T(8,128)S(1)}, bf16[192,128]{1,0:T(8,128)(2,1)S(1)}) custom-call(f32[1,1536,128]{2,1,0:T(8,128)S(1)} %get-tuple-element.56.refs_0_, bf16[1024,2304]{1,0:T(8,128)(2,1)S(1)} %get-tuple-element.57.refs_1_, f32[272,128]{1,0:T(8,128)S(1)} %get-tuple-element.52.refs_2_.refs_0_), custom_call_target="tpu_custom_call" | custom-call | flops 603979776 | bytes 4718592 | tf_op jit(solution)/shard_map/pallas_call | solution.py:408
  21.4 1.7 %collective-permute-start.8 = (bf16[192,128]{1,0:T(8,128)(2,1)S(1)}, bf16[192,128]{1,0:T(8,128)(2,1)S(1)}, u32[]{:S(2)}, u32[]{:S(2)}) collective-permute-start(bf16[192,128]{1,0:T(8,128)(2,1)S(1)} %get-tuple-element.58.refs_4_), channel_id=1, source_target_pairs={{0,1},{1,0},{2,3},{3,2},{4,5},{5,4},{6,7},{7,6},{8,9},{9,8},{10,11... | collective-permute-start | bytes 147464 | tf_op jit(solution)/shard_map/ppermute | solution.py:620
  23.0 0.4 collective-permute-done.5.refs_2_
  23.4 1.7 %collective-permute-start.7 = (bf16[272,128]{1,0:T(8,128)(2,1)S(1)}, bf16[272,128]{1,0:T(8,128)(2,1)S(1)}, u32[]{:S(2)}, u32[]{:S(2)}) collective-permute-start(bf16[272,128]{1,0:T(8,128)(2,1)S(1)} %shard_map.97.refs_3_.own), channel_id=1, source_target_pairs={{0,1},{1,0},{2,3},{3,2},{4,5},{5,4},{6,7},{7,6},{8,9},{9,8},{10,11... | collective-permute-start | bytes 208904 | tf_op jit(solution)/shard_map/ppermute | solution.py:620
  25.1 0.4 %collective-permute-done.8.refs_2_ = bf16[192,128]{1,0:T(8,128)(2,1)S(1)} collective-permute-done((bf16[192,128]{1,0:T(8,128)(2,1)S(1)}, bf16[192,128]{1,0:T(8,128)(2,1)S(1)}, u32[]{:S(2)}, u32[]{:S(2)}) %collective-permute-start.8) | collective-permute-done | bytes 49184 | tf_op jit(solution)/shard_map/ppermute | solution.py:620
  25.5 1.6 %shard_map.99 = (bf16[1024,2304]{1,0:T(8,128)(2,1)S(1)}, f32[1,1536,128]{2,1,0:T(8,128)S(1)}) custom-call(bf16[1024,128]{1,0:T(8,128)(2,1)S(1)} %get-tuple-element.59.left_ref, bf16[2304,128]{1,0:T(8,128)(2,1)S(1)} %get-tuple-element.60.right_ref, f32[32,1536]{1,0:T(8,128)S(1)} %get-tuple-element.61.held, f32[96,128]{1,0:T(8,128)S(1)} %get-tuple-element.64._.refs_4_), custom_call_target="tpu_custom_call" | custom-call | flops 603979776 | bytes 9437184 | tf_op jit(solution)/shard_map/pallas_call | solution.py:439
  27.1 0.0 copy-start
  27.1 0.8 %shard_map.100._.refs_3_ = f32[192,256]{1,0:T(8,128)S(1)} custom-call(f32[1,1536,128]{2,1,0:T(8,128)S(1)} %get-tuple-element.65.wide.refs_0_, bf16[1024,2304]{1,0:T(8,128)(2,1)S(1)} %get-tuple-element.66.source.refs_1_), custom_call_target="tpu_custom_call" | custom-call | flops 301989888 | bytes 2359296 | tf_op jit(solution)/shard_map/pallas_call | solution.py:348
  27.9 1.0 %collective-permute-start.9 = (bf16[272,128]{1,0:T(8,128)(2,1)S(1)}, bf16[272,128]{1,0:T(8,128)(2,1)S(1)}, u32[]{:S(2)}, u32[]{:S(2)}) collective-permute-start(bf16[272,128]{1,0:T(8,128)(2,1)S(1)} %shard_map.101.refs_2_.refs_0_), channel_id=1, source_target_pairs={{0,2},{1,3},{2,0},{3,1},{4,6},{5,7},{6,4},{7,5},{8,10},{9,11},{10,... | collective-permute-start | bytes 208904 | tf_op jit(solution)/shard_map/ppermute | solution.py:620
  29.0 2.0 %collective-permute-start.13 = (bf16[96,128]{1,0:T(8,128)(2,1)S(1)}, bf16[96,128]{1,0:T(8,128)(2,1)S(1)}, u32[]{:S(2)}, u32[]{:S(2)}) collective-permute-start(bf16[96,128]{1,0:T(8,128)(2,1)S(1)} %get-tuple-element.74), channel_id=1, source_target_pairs={{0,2},{1,3},{2,0},{3,1},{4,6},{5,7},{6,4},{7,5},{8,10},{9,11},{10,... | collective-permute-start | bytes 73736 | tf_op jit(solution)/shard_map/ppermute | solution.py:620
  30.9 1.5 %shard_map.102 = (f32[96,128]{1,0:T(8,128)S(1)}, bf16[96,128]{1,0:T(8,128)(2,1)S(1)}, bf16[96,128]{1,0:T(8,128)(2,1)S(1)}, bf16[96,128]{1,0:T(8,128)(2,1)S(1)}) custom-call(f32[1,1536,128]{2,1,0:T(8,128)S(1)} %get-tuple-element.65.wide.refs_0_, bf16[1024,2304]{1,0:T(8,128)(2,1)S(1)} %get-tuple-element.66.source.refs_1_, ...), custom_call_target="tpu_custom_call" | custom-call | flops 603979776 | bytes 4718592 | tf_op jit(solution)/shard_map/pallas_call | solution.py:408
  32.5 1.9 %collective-permute-done.9.refs_1_ = bf16[272,128]{1,0:T(8,128)(2,1)S(1)} collective-permute-done((bf16[272,128]{1,0:T(8,128)(2,1)S(1)}, bf16[272,128]{1,0:T(8,128)(2,1)S(1)}, u32[]{:S(2)}, u32[]{:S(2)}) %collective-permute-start.9) | collective-permute-done | bytes 69664 | tf_op jit(solution)/shard_map/ppermute | solution.py:620
  34.4 0.1 shard_map.103
  34.5 0.1 collective-permute-start.10
  34.6 0.6 %collective-permute-start.11 = (bf16[352,128]{1,0:T(8,128)(2,1)S(1)}, bf16[352,128]{1,0:T(8,128)(2,1)S(1)}, u32[]{:S(2)}, u32[]{:S(2)}) collective-permute-start(bf16[352,128]{1,0:T(8,128)(2,1)S(1)} %get-tuple-element.72), channel_id=1, source_target_pairs={{0,8},{4,12},{8,0},{12,4},{1,9},{5,13},{9,1},{13,5},{2,10},{6,14},... | collective-permute-start | bytes 270344 | tf_op jit(solution)/shard_map/ppermute | solution.py:620
  35.2 1.3 %collective-permute-start.12 = (bf16[352,128]{1,0:T(8,128)(2,1)S(1)}, bf16[352,128]{1,0:T(8,128)(2,1)S(1)}, u32[]{:S(2)}, u32[]{:S(2)}) collective-permute-start(bf16[352,128]{1,0:T(8,128)(2,1)S(1)} %get-tuple-element.73), channel_id=1, source_target_pairs={{0,4},{4,0},{8,12},{12,8},{1,5},{5,1},{9,13},{13,9},{2,6},{6,2},{1... | collective-permute-start | bytes 270344 | tf_op jit(solution)/shard_map/ppermute | solution.py:620
  36.5 2.5 %shard_map.104 = bf16[2304,128]{1,0:T(8,128)(2,1)} custom-call(bf16[1024,2304]{1,0:T(8,128)(2,1)S(1)} %get-tuple-element.50.x_ref, bf16[128,1024]{1,0:T(8,128)(2,1)S(1)} %get-tuple-element.51.wt_ref, f32[1,128]{1,0:T(1,128)S(1)} %bitcast.4, bf16[256,128]{1,0:T(8,128)(2,1)S(1)} %get-tuple-element.70._.refs_0_), custom_call_target="tpu_custom_call" | custom-call | flops 1207959552 | bytes 4718592 | tf_op jit(solution)/shard_map/pallas_call | solution.py:462
  39.0 1.1 %collective-permute-done.11.refs_2_ = bf16[352,128]{1,0:T(8,128)(2,1)S(1)} collective-permute-done((bf16[352,128]{1,0:T(8,128)(2,1)S(1)}, bf16[352,128]{1,0:T(8,128)(2,1)S(1)}, u32[]{:S(2)}, u32[]{:S(2)}) %collective-permute-start.11) | collective-permute-done | bytes 90144 | tf_op jit(solution)/shard_map/ppermute | solution.py:620
  40.1 0.9 %shard_map.105 = (f32[1024,128]{1,0:T(8,128)}, f32[8,1536]{1,0:T(8,128)}, f32[8,1536]{1,0:T(8,128)}, f32[1,128]{1,0:T(1,128)}) custom-call(bf16[256,128]{1,0:T(8,128)(2,1)S(1)} %get-tuple-element.70._.refs_0_, bf16[352,128]{1,0:T(8,128)(2,1)S(1)} %collective-permute-done.10.refs_1_, bf16[352,128]{1,0:T(8,128)(2,1)S(1)} %collective-permute-done.11.refs_2_, ...), custom_call_target="tpu_custom_call" | custom-call | tf_op jit(solution)/shard_map/pallas_call | solution.py:489
  (12 shorter events, 0.1 us)
Async XLA Ops:
  0.6 5.1 %collective-permute-start = (bf16[8,1536]{1,0:T(8,128)(2,1)}, bf16[8,1536]{1,0:T(8,128)(2,1)S(1)}, u32[]{:S(2)}, u32[]{:S(2)}) collective-permute-start(bf16[8,1536]{1,0:T(8,128)(2,1)} %a_hbm.1), channel_id=1, source_target_pairs={{0,1},{1,0},{2,3},{3,2},{4,5},{5,4},{6,7},{7,6},{8,9},{9,8},{10,11... | collective-permute-start | bytes 73736 | tf_op jit(solution)/shard_map/ppermute | solution.py:620
  3.7 2.0 %collective-permute-start.1 = (bf16[8,1536]{1,0:T(8,128)(2,1)}, bf16[8,1536]{1,0:T(8,128)(2,1)S(1)}, u32[]{:S(2)}, u32[]{:S(2)}) collective-permute-start(bf16[8,1536]{1,0:T(8,128)(2,1)} %b_hbm.1), channel_id=1, source_target_pairs={{0,4},{4,0},{8,12},{12,8},{1,5},{5,1},{9,13},{13,9},{2,6},{6,2},{1... | collective-permute-start | bytes 73736 | tf_op jit(solution)/shard_map/ppermute | solution.py:620
  5.8 6.4 %collective-permute-start.2 = (bf16[16,1536]{1,0:T(8,128)(2,1)S(1)}, bf16[16,1536]{1,0:T(8,128)(2,1)S(1)}, u32[]{:S(2)}, u32[]{:S(2)}) collective-permute-start(bf16[16,1536]{1,0:T(8,128)(2,1)S(1)} %get-tuple-element.45.refs_0_), channel_id=1, source_target_pairs={{0,2},{1,3},{2,0},{3,1},{4,6},{5,7},{6,4},{7,5},{8,10},{9,11},{10,... | collective-permute-start | bytes 147464 | tf_op jit(solution)/shard_map/ppermute | solution.py:620
  8.9 4.1 %collective-permute-start.3 = (bf16[16,1536]{1,0:T(8,128)(2,1)S(1)}, bf16[16,1536]{1,0:T(8,128)(2,1)S(1)}, u32[]{:S(2)}, u32[]{:S(2)}) collective-permute-start(bf16[16,1536]{1,0:T(8,128)(2,1)S(1)} %get-tuple-element.46.refs_2_), channel_id=1, source_target_pairs={{0,8},{4,12},{8,0},{12,4},{1,9},{5,13},{9,1},{13,5},{2,10},{6,14},... | collective-permute-start | bytes 147464 | tf_op jit(solution)/shard_map/ppermute | solution.py:620
  17.3 5.7 %collective-permute-start.4 = (bf16[272,128]{1,0:T(8,128)(2,1)S(1)}, bf16[272,128]{1,0:T(8,128)(2,1)S(1)}, u32[]{:S(2)}, u32[]{:S(2)}) collective-permute-start(bf16[272,128]{1,0:T(8,128)(2,1)S(1)} %get-tuple-element.53), channel_id=1, source_target_pairs={{0,12},{4,8},{8,4},{12,0},{1,13},{5,9},{9,5},{13,1},{2,14},{6,10},... | collective-permute-start | bytes 208904 | tf_op jit(solution)/shard_map/ppermute | solution.py:620
  17.4 6.0 %collective-permute-start.5 = (bf16[272,128]{1,0:T(8,128)(2,1)S(1)}, bf16[272,128]{1,0:T(8,128)(2,1)S(1)}, u32[]{:S(2)}, u32[]{:S(2)}) collective-permute-start(bf16[272,128]{1,0:T(8,128)(2,1)S(1)} %get-tuple-element.54), channel_id=1, source_target_pairs={{0,8},{4,12},{8,0},{12,4},{1,9},{5,13},{9,1},{13,5},{2,10},{6,14},... | collective-permute-start | bytes 208904 | tf_op jit(solution)/shard_map/ppermute | solution.py:620
  19.0 4.4 %collective-permute-start.6 = (bf16[272,128]{1,0:T(8,128)(2,1)S(1)}, bf16[272,128]{1,0:T(8,128)(2,1)S(1)}, u32[]{:S(2)}, u32[]{:S(2)}) collective-permute-start(bf16[272,128]{1,0:T(8,128)(2,1)S(1)} %get-tuple-element.55), channel_id=1, source_target_pairs={{0,4},{4,0},{8,12},{12,8},{1,5},{5,1},{9,13},{13,9},{2,6},{6,2},{1... | collective-permute-start | bytes 208904 | tf_op jit(solution)/shard_map/ppermute | solution.py:620
  21.4 4.2 %collective-permute-start.8 = (bf16[192,128]{1,0:T(8,128)(2,1)S(1)}, bf16[192,128]{1,0:T(8,128)(2,1)S(1)}, u32[]{:S(2)}, u32[]{:S(2)}) collective-permute-start(bf16[192,128]{1,0:T(8,128)(2,1)S(1)} %get-tuple-element.58.refs_4_), channel_id=1, source_target_pairs={{0,1},{1,0},{2,3},{3,2},{4,5},{5,4},{6,7},{7,6},{8,9},{9,8},{10,11... | collective-permute-start | bytes 147464 | tf_op jit(solution)/shard_map/ppermute | solution.py:620
  23.4 4.5 %collective-permute-start.7 = (bf16[272,128]{1,0:T(8,128)(2,1)S(1)}, bf16[272,128]{1,0:T(8,128)(2,1)S(1)}, u32[]{:S(2)}, u32[]{:S(2)}) collective-permute-start(bf16[272,128]{1,0:T(8,128)(2,1)S(1)} %shard_map.97.refs_3_.own), channel_id=1, source_target_pairs={{0,1},{1,0},{2,3},{3,2},{4,5},{5,4},{6,7},{7,6},{8,9},{9,8},{10,11... | collective-permute-start | bytes 208904 | tf_op jit(solution)/shard_map/ppermute | solution.py:620
  27.1 9.4 %copy-start = (f32[128]{0:T(128)S(1)}, f32[128]{0:T(128)}, u32[]{:S(2)}) copy-start(f32[128]{0:T(128)} %param.8) | copy-start | bytes 1540
  27.9 6.5 %collective-permute-start.9 = (bf16[272,128]{1,0:T(8,128)(2,1)S(1)}, bf16[272,128]{1,0:T(8,128)(2,1)S(1)}, u32[]{:S(2)}, u32[]{:S(2)}) collective-permute-start(bf16[272,128]{1,0:T(8,128)(2,1)S(1)} %shard_map.101.refs_2_.refs_0_), channel_id=1, source_target_pairs={{0,2},{1,3},{2,0},{3,1},{4,6},{5,7},{6,4},{7,5},{8,10},{9,11},{10,... | collective-permute-start | bytes 208904 | tf_op jit(solution)/shard_map/ppermute | solution.py:620
  29.0 10.0 %collective-permute-start.13 = (bf16[96,128]{1,0:T(8,128)(2,1)S(1)}, bf16[96,128]{1,0:T(8,128)(2,1)S(1)}, u32[]{:S(2)}, u32[]{:S(2)}) collective-permute-start(bf16[96,128]{1,0:T(8,128)(2,1)S(1)} %get-tuple-element.74), channel_id=1, source_target_pairs={{0,2},{1,3},{2,0},{3,1},{4,6},{5,7},{6,4},{7,5},{8,10},{9,11},{10,... | collective-permute-start | bytes 73736 | tf_op jit(solution)/shard_map/ppermute | solution.py:620
  34.5 4.5 %collective-permute-start.10 = (bf16[352,128]{1,0:T(8,128)(2,1)S(1)}, bf16[352,128]{1,0:T(8,128)(2,1)S(1)}, u32[]{:S(2)}, u32[]{:S(2)}) collective-permute-start(bf16[352,128]{1,0:T(8,128)(2,1)S(1)} %get-tuple-element.71), channel_id=1, source_target_pairs={{0,12},{4,8},{8,4},{12,0},{1,13},{5,9},{9,5},{13,1},{2,14},{6,10},... | collective-permute-start | bytes 270344 | tf_op jit(solution)/shard_map/ppermute | solution.py:620
  34.6 5.5 %collective-permute-start.11 = (bf16[352,128]{1,0:T(8,128)(2,1)S(1)}, bf16[352,128]{1,0:T(8,128)(2,1)S(1)}, u32[]{:S(2)}, u32[]{:S(2)}) collective-permute-start(bf16[352,128]{1,0:T(8,128)(2,1)S(1)} %get-tuple-element.72), channel_id=1, source_target_pairs={{0,8},{4,12},{8,0},{12,4},{1,9},{5,13},{9,1},{13,5},{2,10},{6,14},... | collective-permute-start | bytes 270344 | tf_op jit(solution)/shard_map/ppermute | solution.py:620
  35.2 4.9 %collective-permute-start.12 = (bf16[352,128]{1,0:T(8,128)(2,1)S(1)}, bf16[352,128]{1,0:T(8,128)(2,1)S(1)}, u32[]{:S(2)}, u32[]{:S(2)}) collective-permute-start(bf16[352,128]{1,0:T(8,128)(2,1)S(1)} %get-tuple-element.73), channel_id=1, source_target_pairs={{0,4},{4,0},{8,12},{12,8},{1,5},{5,1},{9,13},{13,9},{2,6},{6,2},{1... | collective-permute-start | bytes 270344 | tf_op jit(solution)/shard_map/ppermute | solution.py:620

commit v22 on v20

--- a/solution.py
+++ b/solution.py
@@ -146,6 +146,17 @@
         for n in range(2):
             place = lax.bitwise_xor(me, 2 * p + n) * depth
             held[pl.ds(pl.multiple_of(place, depth), depth), :] = block[n * depth : (n + 1) * depth]
+
+
+def join_far(pieces, axis, held):
+    half = lax.axis_size(axis) // 2
+    depth = pieces[0].shape[0] // half
+    me = lax.axis_index(axis)
+    for n, piece in enumerate(pieces):
+        block = piece[...].astype(F32)
+        for p in range(half):
+            place = lax.bitwise_xor(me, 2 * p + n) * depth
+            held[pl.ds(pl.multiple_of(place, depth), depth), :] = block[p * depth : (p + 1) * depth]
 
 
 def repeat_matrix(sequences):
@@ -222,9 +233,8 @@
 def outer_kernel(i_n, j_n, *refs):
     depth = PROJECTED_DEPTH
     row_n = lax.axis_size("row")
-    halves = [lax.axis_size("col") // 2, row_n // 2]
-    a_pieces, refs = refs[: halves[0]], refs[halves[0] :]
-    b_pieces, refs = refs[: halves[1]], refs[halves[1] :]
+    half = lax.axis_size("col") // 2
+    a_pieces, b_pieces, refs = refs[:half], refs[half : half + 2], refs[half + 2 :]
     g_ref, bias_ref, x_ref, a_held, b_wide = refs[:5]
     messages, (b_held, left, total) = refs[5 : 5 + row_n], refs[5 + row_n :]
     sequences = a_held.shape[0]
@@ -233,7 +243,7 @@
     span = GROUP * j_n
 
     join(a_pieces, "col", a_held)
-    join(b_pieces, "row", b_held)
+    join_far(b_pieces, "row", b_held)
     spread(b_held, b_wide)
     turned = a_held[...].T.astype(BF16)
     shape = (sequences, GROUP * sequences)
@@ -605,16 +615,16 @@
     channels = final_projection_matrix.shape[0]
     res_total = i_n * row_n
     a_near = swap(first_homolog_features, "col", 1)
-    b_near = swap(second_homolog_features, "row", 1)
+    b_far = from_evens(second_homolog_features, "row")
     we, wt, a, b, w, g = load(
         first_homolog_features,
         second_homolog_features,
         final_projection_matrix,
         cotangent.reshape(i_n * j_n, PAIR_FEATURES),
     )
-    a, b = stack([a, a_near], [b, b_near])
+    a, b = stack([a, a_near], [b, *b_far])
     a_pieces = [a] + from_evens(a, "col")
-    b_pieces = [b] + from_evens(b, "row")
+    b_pieces = [b, swap(b, "row", 1)]
     y, gt, bias_rows = prepare(we, g, i_n, j_n)
 
     x, a_held, b_wide, (own, *messages) = outer(

time: 40.8 us -> 41.8 us (1.025)
  waiting for transfers between devices: 5.25 us -> 9.45 us
  starting transfers between devices: 17.8 us -> 14.6 us
    ppermute x14, waiting for transfers between devices: 5.25 us -> 9.45 us  [swap(): lax.ppermute(x, axis, [(n, n ^ p) for n in range(lax.axis_size(axis))])]
    ppermute x14, starting transfers between devices: 17.8 us -> 14.6 us  [swap(): lax.ppermute(x, axis, [(n, n ^ p) for n in range(lax.axis_size(axis))])]
where the time goes in v22:
time: 41.8 us; the launch traced here: 41.6 us
  Pallas kernels  16.9 us (40%)
  starting transfers between devices  14.6 us (35%)
  waiting for transfers between devices  9.45 us (23%)
  between operations  0.72 us (2%)
    ppermute x14, starting transfers between devices, swap(): lax.ppermute(x, axis, [(n, n ^ p) for n in range(lax.axis_size(axis))])  14.6 us
    ppermute x14, waiting for transfers between devices, swap(): lax.ppermute(x, axis, [(n, n ^ p) for n in range(lax.axis_size(axis))])  9.45 us
    pallas_call x1, Pallas kernels, outer(): pl.pallas_call(functools.partial(outer_kernel, i_n, j_n), in_specs=[in_vm...  4.39 us
    pallas_call x2, Pallas kernels, gradient(): pl.pallas_call(functools.partial(gradient_kernel, axis, plan, kept, posit...  4.12 us
    pallas_call x1, Pallas kernels, pair(): pl.pallas_call(functools.partial(pair_kernel, sequences), grid=(count,),...  2.55 us
    pallas_call x1, Pallas kernels, prepare(): pl.pallas_call(functools.partial(prepare_kernel, i_n, j_n), in_specs=[in_...  1.75 us
    pallas_call x1, Pallas kernels, product(): pl.pallas_call(product_kernel, in_specs=[in_vmem()] * 3 + [pl.BlockSpec(m...  1.55 us
    pallas_call x1, Pallas kernels, load(): pl.pallas_call(load_kernel, in_specs=[pl.BlockSpec(memory_space=pltpu.HBM...  1.39 us
  transfers between devices with their start and end apart: 14, of which 8 were waited for; matrix products, arithmetic and copies ran while one was open for 0% of the time, Pallas kernels for 28%

profile of v22, /device:TPU:0, one launch (start us, length us, event | category | flops | bytes accessed | tf_op | source)
XLA Modules:
  0.0 41.6 jit_solution(3706857797757232381)
XLA Ops:
  0.6 3.1 %collective-permute-start = (bf16[8,1536]{1,0:T(8,128)(2,1)}, bf16[8,1536]{1,0:T(8,128)(2,1)S(1)}, u32[]{:S(2)}, u32[]{:S(2)}) collective-permute-start(bf16[8,1536]{1,0:T(8,128)(2,1)} %a_hbm.1), channel_id=1, source_target_pairs={{0,1},{1,0},{2,3},{3,2},{4,5},{5,4},{6,7},{7,6},{8,9},{9,8},{10,11... | collective-permute-start | bytes 73736 | tf_op jit(solution)/shard_map/ppermute | solution.py:597
  3.7 1.5 %collective-permute-start.1 = (bf16[8,1536]{1,0:T(8,128)(2,1)}, bf16[8,1536]{1,0:T(8,128)(2,1)S(1)}, u32[]{:S(2)}, u32[]{:S(2)}) collective-permute-start(bf16[8,1536]{1,0:T(8,128)(2,1)} %b_hbm.1), channel_id=1, source_target_pairs={{0,8},{4,12},{8,0},{12,4},{1,9},{5,13},{9,1},{13,5},{2,10},{6,14},... | collective-permute-start | bytes 73736 | tf_op jit(solution)/shard_map/ppermute | solution.py:597
  5.2 1.4 %shard_map.92 = (bf16[1024,128]{1,0:T(8,128)(2,1)S(1)}, bf16[128,1024]{1,0:T(8,128)(2,1)S(1)}, bf16[8,1536]{1,0:T(8,128)(2,1)S(1)}, bf16[8,1536]{1,0:T(8,128)(2,...) custom-call(bf16[8,1536]{1,0:T(8,128)(2,1)} %a_hbm.1, bf16[8,1536]{1,0:T(8,128)(2,1)} %b_hbm.1, ...), custom_call_target="tpu_custom_call" | custom-call | flops 131072000 | bytes 2097152 | tf_op jit(solution)/shard_map/pallas_call | solution.py:67
  6.6 1.1 %collective-permute-done.1.refs_3_ = bf16[8,1536]{1,0:T(8,128)(2,1)S(1)} collective-permute-done((bf16[8,1536]{1,0:T(8,128)(2,1)}, bf16[8,1536]{1,0:T(8,128)(2,1)S(1)}, u32[]{:S(2)}, u32[]{:S(2)}) %collective-permute-start.1) | collective-permute-done | bytes 24608 | tf_op jit(solution)/shard_map/ppermute | solution.py:597
  7.8 2.7 %collective-permute-start.2 = (bf16[16,1536]{1,0:T(8,128)(2,1)S(1)}, bf16[16,1536]{1,0:T(8,128)(2,1)S(1)}, u32[]{:S(2)}, u32[]{:S(2)}) collective-permute-start(bf16[16,1536]{1,0:T(8,128)(2,1)S(1)} %get-tuple-element.45.refs_0_), channel_id=1, source_target_pairs={{0,2},{1,3},{2,0},{3,1},{4,6},{5,7},{6,4},{7,5},{8,10},{9,11},{10,... | collective-permute-start | bytes 147464 | tf_op jit(solution)/shard_map/ppermute | solution.py:597
  10.4 0.0 collective-permute-start.3
  10.4 1.8 %shard_map.94 = (bf16[1024,2304]{1,0:T(8,128)(2,1)S(1)}, bf16[2304,128]{1,0:T(8,128)(2,1)S(1)}, bf16[16,128]{1,0:T(8,128)(2,1)S(1)}) custom-call(bf16[1024,128]{1,0:T(8,128)(2,1)S(1)} %get-tuple-element.48.we_ref, bf16[2304,128]{1,0:T(8,128)(2,1)S(1)} %get-tuple-element.47.g_ref.refs_4_), custom_call_target="tpu_custom_call" | custom-call | flops 603979776 | bytes 9437184 | tf_op jit(solution)/shard_map/pallas_call | solution.py:126
  12.2 0.7 %collective-permute-done.2.refs_1_ = bf16[16,1536]{1,0:T(8,128)(2,1)S(1)} collective-permute-done((bf16[16,1536]{1,0:T(8,128)(2,1)S(1)}, bf16[16,1536]{1,0:T(8,128)(2,1)S(1)}, u32[]{:S(2)}, u32[]{:S(2)}) %collective-permute-start.2) | collective-permute-done | bytes 49184 | tf_op jit(solution)/shard_map/ppermute | solution.py:597
  12.9 4.4 %shard_map.95 = (bf16[1024,2304]{1,0:T(8,128)(2,1)S(1)}, f32[32,1536]{1,0:T(8,128)S(1)}, f32[1,1536,128]{2,1,0:T(8,128)S(1)}, f32[272,128]{1,0:T(8,128)S(1)}, bf...) custom-call(bf16[16,1536]{1,0:T(8,128)(2,1)S(1)} %get-tuple-element.45.refs_0_, ...), custom_call_target="tpu_custom_call" | custom-call | flops 1207959552 | bytes 4718592 | tf_op jit(solution)/shard_map/pallas_call | solution.py:300
  17.3 1.0 %collective-permute-start.4 = (bf16[272,128]{1,0:T(8,128)(2,1)S(1)}, bf16[272,128]{1,0:T(8,128)(2,1)S(1)}, u32[]{:S(2)}, u32[]{:S(2)}) collective-permute-start(bf16[272,128]{1,0:T(8,128)(2,1)S(1)} %get-tuple-element.53), channel_id=1, source_target_pairs={{0,12},{4,8},{8,4},{12,0},{1,13},{5,9},{9,5},{13,1},{2,14},{6,10},... | collective-permute-start | bytes 208904 | tf_op jit(solution)/shard_map/ppermute | solution.py:597
  18.3 1.0 %collective-permute-start.5 = (bf16[272,128]{1,0:T(8,128)(2,1)S(1)}, bf16[272,128]{1,0:T(8,128)(2,1)S(1)}, u32[]{:S(2)}, u32[]{:S(2)}) collective-permute-start(bf16[272,128]{1,0:T(8,128)(2,1)S(1)} %get-tuple-element.54), channel_id=1, source_target_pairs={{0,8},{4,12},{8,0},{12,4},{1,9},{5,13},{9,1},{13,5},{2,10},{6,14},... | collective-permute-start | bytes 208904 | tf_op jit(solution)/shard_map/ppermute | solution.py:597
  19.3 0.0 collective-permute-start.6
  19.3 2.1 %shard_map.96 = (f32[96,128]{1,0:T(8,128)S(1)}, f32[96,128]{1,0:T(8,128)S(1)}, bf16[192,128]{1,0:T(8,128)(2,1)S(1)}) custom-call(f32[1,1536,128]{2,1,0:T(8,128)S(1)} %get-tuple-element.56.refs_0_, bf16[1024,2304]{1,0:T(8,128)(2,1)S(1)} %get-tuple-element.57.refs_1_, f32[272,128]{1,0:T(8,128)S(1)} %get-tuple-element.52.refs_2_.refs_0_), custom_call_target="tpu_custom_call" | custom-call | flops 603979776 | bytes 4718592 | tf_op jit(solution)/shard_map/pallas_call | solution.py:388
  21.4 0.1 collective-permute-start.8
  21.5 0.0 collective-permute-done.4.refs_1_
  21.6 1.7 %collective-permute-done.5.refs_2_ = bf16[272,128]{1,0:T(8,128)(2,1)S(1)} collective-permute-done((bf16[272,128]{1,0:T(8,128)(2,1)S(1)}, bf16[272,128]{1,0:T(8,128)(2,1)S(1)}, u32[]{:S(2)}, u32[]{:S(2)}) %collective-permute-start.5) | collective-permute-done | bytes 69664 | tf_op jit(solution)/shard_map/ppermute | solution.py:597
  23.3 0.3 collective-permute-start.7
  23.6 2.0 %collective-permute-done.8.refs_2_ = bf16[192,128]{1,0:T(8,128)(2,1)S(1)} collective-permute-done((bf16[192,128]{1,0:T(8,128)(2,1)S(1)}, bf16[192,128]{1,0:T(8,128)(2,1)S(1)}, u32[]{:S(2)}, u32[]{:S(2)}) %collective-permute-start.8) | collective-permute-done | bytes 49184 | tf_op jit(solution)/shard_map/ppermute | solution.py:597
  25.6 1.5 %shard_map.99 = (bf16[1024,2304]{1,0:T(8,128)(2,1)S(1)}, f32[1,1536,128]{2,1,0:T(8,128)S(1)}) custom-call(bf16[1024,128]{1,0:T(8,128)(2,1)S(1)} %get-tuple-element.59.left_ref, bf16[2304,128]{1,0:T(8,128)(2,1)S(1)} %get-tuple-element.60.right_ref, f32[32,1536]{1,0:T(8,128)S(1)} %get-tuple-element.61.held, f32[96,128]{1,0:T(8,128)S(1)} %get-tuple-element.64._.refs_4_), custom_call_target="tpu_custom_call" | custom-call | flops 603979776 | bytes 9437184 | tf_op jit(solution)/shard_map/pallas_call | solution.py:416
  27.1 0.6 %collective-permute-done.7.near = bf16[272,128]{1,0:T(8,128)(2,1)S(1)} collective-permute-done((bf16[272,128]{1,0:T(8,128)(2,1)S(1)}, bf16[272,128]{1,0:T(8,128)(2,1)S(1)}, u32[]{:S(2)}, u32[]{:S(2)}) %collective-permute-start.7) | collective-permute-done | bytes 69664 | tf_op jit(solution)/shard_map/ppermute | solution.py:597
  27.7 2.6 %collective-permute-start.9 = (bf16[272,128]{1,0:T(8,128)(2,1)S(1)}, bf16[272,128]{1,0:T(8,128)(2,1)S(1)}, u32[]{:S(2)}, u32[]{:S(2)}) collective-permute-start(bf16[272,128]{1,0:T(8,128)(2,1)S(1)} %shard_map.100.refs_2_.refs_0_), channel_id=1, source_target_pairs={{0,2},{1,3},{2,0},{3,1},{4,6},{5,7},{6,4},{7,5},{8,10},{9,11},{10,... | collective-permute-start | bytes 208904 | tf_op jit(solution)/shard_map/ppermute | solution.py:597
  30.4 0.3 collective-permute-start.13
  30.7 2.1 %shard_map.101 = (f32[96,128]{1,0:T(8,128)S(1)}, bf16[96,128]{1,0:T(8,128)(2,1)S(1)}, bf16[96,128]{1,0:T(8,128)(2,1)S(1)}, bf16[96,128]{1,0:T(8,128)(2,1)S(1)}) custom-call(f32[1,1536,128]{2,1,0:T(8,128)S(1)} %get-tuple-element.66.refs_0_, bf16[1024,2304]{1,0:T(8,128)(2,1)S(1)} %get-tuple-element.65._.refs_1_, bf16[272,128]{1,0:T(8,128)(2,1)S(1)} %shard_map.100.refs_2_.refs_0_), custom_call_target="tpu_custom_call" | custom-call | flops 603979776 | bytes 4718592 | tf_op jit(solution)/shard_map/pallas_call | solution.py:388
  32.8 1.2 %collective-permute-done.9.refs_1_ = bf16[272,128]{1,0:T(8,128)(2,1)S(1)} collective-permute-done((bf16[272,128]{1,0:T(8,128)(2,1)S(1)}, bf16[272,128]{1,0:T(8,128)(2,1)S(1)}, u32[]{:S(2)}, u32[]{:S(2)}) %collective-permute-start.9) | collective-permute-done | bytes 69664 | tf_op jit(solution)/shard_map/ppermute | solution.py:597
  33.9 0.1 shard_map.102
  34.1 0.1 collective-permute-start.10
  34.1 1.4 %collective-permute-start.11 = (bf16[352,128]{1,0:T(8,128)(2,1)S(1)}, bf16[352,128]{1,0:T(8,128)(2,1)S(1)}, u32[]{:S(2)}, u32[]{:S(2)}) collective-permute-start(bf16[352,128]{1,0:T(8,128)(2,1)S(1)} %get-tuple-element.72), channel_id=1, source_target_pairs={{0,8},{4,12},{8,0},{12,4},{1,9},{5,13},{9,1},{13,5},{2,10},{6,14},... | collective-permute-start | bytes 270344 | tf_op jit(solution)/shard_map/ppermute | solution.py:597
  35.5 0.5 %collective-permute-start.12 = (bf16[352,128]{1,0:T(8,128)(2,1)S(1)}, bf16[352,128]{1,0:T(8,128)(2,1)S(1)}, u32[]{:S(2)}, u32[]{:S(2)}) collective-permute-start(bf16[352,128]{1,0:T(8,128)(2,1)S(1)} %get-tuple-element.73), channel_id=1, source_target_pairs={{0,4},{4,0},{8,12},{12,8},{1,5},{5,1},{9,13},{13,9},{2,6},{6,2},{1... | collective-permute-start | bytes 270344 | tf_op jit(solution)/shard_map/ppermute | solution.py:597
  36.0 2.5 %shard_map.103 = bf16[2304,128]{1,0:T(8,128)(2,1)} custom-call(bf16[1024,2304]{1,0:T(8,128)(2,1)S(1)} %get-tuple-element.50.x_ref, bf16[128,1024]{1,0:T(8,128)(2,1)S(1)} %get-tuple-element.51.wt_ref, f32[1,128]{1,0:T(1,128)S(1)} %bitcast.4, bf16[256,128]{1,0:T(8,128)(2,1)S(1)} %get-tuple-element.70._.refs_0_), custom_call_target="tpu_custom_call" | custom-call | flops 1207959552 | bytes 4718592 | tf_op jit(solution)/shard_map/pallas_call | solution.py:439
  38.5 0.5 %collective-permute-done.10.refs_1_ = bf16[352,128]{1,0:T(8,128)(2,1)S(1)} collective-permute-done((bf16[352,128]{1,0:T(8,128)(2,1)S(1)}, bf16[352,128]{1,0:T(8,128)(2,1)S(1)}, u32[]{:S(2)}, u32[]{:S(2)}) %collective-permute-start.10) | collective-permute-done | bytes 90144 | tf_op jit(solution)/shard_map/ppermute | solution.py:597
  39.0 1.7 %collective-permute-done.11.refs_2_ = bf16[352,128]{1,0:T(8,128)(2,1)S(1)} collective-permute-done((bf16[352,128]{1,0:T(8,128)(2,1)S(1)}, bf16[352,128]{1,0:T(8,128)(2,1)S(1)}, u32[]{:S(2)}, u32[]{:S(2)}) %collective-permute-start.11) | collective-permute-done | bytes 90144 | tf_op jit(solution)/shard_map/ppermute | solution.py:597
  40.7 0.9 %shard_map.104 = (f32[1024,128]{1,0:T(8,128)}, f32[8,1536]{1,0:T(8,128)}, f32[8,1536]{1,0:T(8,128)}, f32[1,128]{1,0:T(1,128)}) custom-call(bf16[256,128]{1,0:T(8,128)(2,1)S(1)} %get-tuple-element.70._.refs_0_, bf16[352,128]{1,0:T(8,128)(2,1)S(1)} %collective-permute-done.10.refs_1_, bf16[352,128]{1,0:T(8,128)(2,1)S(1)} %collective-permute-done.11.refs_2_, ...), custom_call_target="tpu_custom_call" | custom-call | tf_op jit(solution)/shard_map/pallas_call | solution.py:466
  (11 shorter events, 0.1 us)
Async XLA Ops:
  0.6 6.0 %collective-permute-start = (bf16[8,1536]{1,0:T(8,128)(2,1)}, bf16[8,1536]{1,0:T(8,128)(2,1)S(1)}, u32[]{:S(2)}, u32[]{:S(2)}) collective-permute-start(bf16[8,1536]{1,0:T(8,128)(2,1)} %a_hbm.1), channel_id=1, source_target_pairs={{0,1},{1,0},{2,3},{3,2},{4,5},{5,4},{6,7},{7,6},{8,9},{9,8},{10,11... | collective-permute-start | bytes 73736 | tf_op jit(solution)/shard_map/ppermute | solution.py:597
  3.7 4.0 %collective-permute-start.1 = (bf16[8,1536]{1,0:T(8,128)(2,1)}, bf16[8,1536]{1,0:T(8,128)(2,1)S(1)}, u32[]{:S(2)}, u32[]{:S(2)}) collective-permute-start(bf16[8,1536]{1,0:T(8,128)(2,1)} %b_hbm.1), channel_id=1, source_target_pairs={{0,8},{4,12},{8,0},{12,4},{1,9},{5,13},{9,1},{13,5},{2,10},{6,14},... | collective-permute-start | bytes 73736 | tf_op jit(solution)/shard_map/ppermute | solution.py:597
  7.8 5.1 %collective-permute-start.2 = (bf16[16,1536]{1,0:T(8,128)(2,1)S(1)}, bf16[16,1536]{1,0:T(8,128)(2,1)S(1)}, u32[]{:S(2)}, u32[]{:S(2)}) collective-permute-start(bf16[16,1536]{1,0:T(8,128)(2,1)S(1)} %get-tuple-element.45.refs_0_), channel_id=1, source_target_pairs={{0,2},{1,3},{2,0},{3,1},{4,6},{5,7},{6,4},{7,5},{8,10},{9,11},{10,... | collective-permute-start | bytes 147464 | tf_op jit(solution)/shard_map/ppermute | solution.py:597
  10.4 2.5 %collective-permute-start.3 = (bf16[16,1536]{1,0:T(8,128)(2,1)S(1)}, bf16[16,1536]{1,0:T(8,128)(2,1)S(1)}, u32[]{:S(2)}, u32[]{:S(2)}) collective-permute-start(bf16[16,1536]{1,0:T(8,128)(2,1)S(1)} %get-tuple-element.46.refs_2_), channel_id=1, source_target_pairs={{0,4},{4,0},{8,12},{12,8},{1,5},{5,1},{9,13},{13,9},{2,6},{6,2},{1... | collective-permute-start | bytes 147464 | tf_op jit(solution)/shard_map/ppermute | solution.py:597
  17.3 4.2 %collective-permute-start.4 = (bf16[272,128]{1,0:T(8,128)(2,1)S(1)}, bf16[272,128]{1,0:T(8,128)(2,1)S(1)}, u32[]{:S(2)}, u32[]{:S(2)}) collective-permute-start(bf16[272,128]{1,0:T(8,128)(2,1)S(1)} %get-tuple-element.53), channel_id=1, source_target_pairs={{0,12},{4,8},{8,4},{12,0},{1,13},{5,9},{9,5},{13,1},{2,14},{6,10},... | collective-permute-start | bytes 208904 | tf_op jit(solution)/shard_map/ppermute | solution.py:597
  18.3 5.0 %collective-permute-start.5 = (bf16[272,128]{1,0:T(8,128)(2,1)S(1)}, bf16[272,128]{1,0:T(8,128)(2,1)S(1)}, u32[]{:S(2)}, u32[]{:S(2)}) collective-permute-start(bf16[272,128]{1,0:T(8,128)(2,1)S(1)} %get-tuple-element.54), channel_id=1, source_target_pairs={{0,8},{4,12},{8,0},{12,4},{1,9},{5,13},{9,1},{13,5},{2,10},{6,14},... | collective-permute-start | bytes 208904 | tf_op jit(solution)/shard_map/ppermute | solution.py:597
  19.3 4.0 %collective-permute-start.6 = (bf16[272,128]{1,0:T(8,128)(2,1)S(1)}, bf16[272,128]{1,0:T(8,128)(2,1)S(1)}, u32[]{:S(2)}, u32[]{:S(2)}) collective-permute-start(bf16[272,128]{1,0:T(8,128)(2,1)S(1)} %get-tuple-element.55), channel_id=1, source_target_pairs={{0,4},{4,0},{8,12},{12,8},{1,5},{5,1},{9,13},{13,9},{2,6},{6,2},{1... | collective-permute-start | bytes 208904 | tf_op jit(solution)/shard_map/ppermute | solution.py:597
  21.4 4.2 %collective-permute-start.8 = (bf16[192,128]{1,0:T(8,128)(2,1)S(1)}, bf16[192,128]{1,0:T(8,128)(2,1)S(1)}, u32[]{:S(2)}, u32[]{:S(2)}) collective-permute-start(bf16[192,128]{1,0:T(8,128)(2,1)S(1)} %get-tuple-element.58.refs_4_), channel_id=1, source_target_pairs={{0,1},{1,0},{2,3},{3,2},{4,5},{5,4},{6,7},{7,6},{8,9},{9,8},{10,11... | collective-permute-start | bytes 147464 | tf_op jit(solution)/shard_map/ppermute | solution.py:597
  23.3 4.4 %collective-permute-start.7 = (bf16[272,128]{1,0:T(8,128)(2,1)S(1)}, bf16[272,128]{1,0:T(8,128)(2,1)S(1)}, u32[]{:S(2)}, u32[]{:S(2)}) collective-permute-start(bf16[272,128]{1,0:T(8,128)(2,1)S(1)} %shard_map.97.refs_3_.own), channel_id=1, source_target_pairs={{0,1},{1,0},{2,3},{3,2},{4,5},{5,4},{6,7},{7,6},{8,9},{9,8},{10,11... | collective-permute-start | bytes 208904 | tf_op jit(solution)/shard_map/ppermute | solution.py:597
  27.7 8.3 %copy-start = (f32[128]{0:T(128)S(1)}, f32[128]{0:T(128)}, u32[]{:S(2)}) copy-start(f32[128]{0:T(128)} %param.8) | copy-start | bytes 1540
  27.7 6.2 %collective-permute-start.9 = (bf16[272,128]{1,0:T(8,128)(2,1)S(1)}, bf16[272,128]{1,0:T(8,128)(2,1)S(1)}, u32[]{:S(2)}, u32[]{:S(2)}) collective-permute-start(bf16[272,128]{1,0:T(8,128)(2,1)S(1)} %shard_map.100.refs_2_.refs_0_), channel_id=1, source_target_pairs={{0,2},{1,3},{2,0},{3,1},{4,6},{5,7},{6,4},{7,5},{8,10},{9,11},{10,... | collective-permute-start | bytes 208904 | tf_op jit(solution)/shard_map/ppermute | solution.py:597
  30.4 8.2 %collective-permute-start.13 = (bf16[96,128]{1,0:T(8,128)(2,1)S(1)}, bf16[96,128]{1,0:T(8,128)(2,1)S(1)}, u32[]{:S(2)}, u32[]{:S(2)}) collective-permute-start(bf16[96,128]{1,0:T(8,128)(2,1)S(1)} %get-tuple-element.74), channel_id=1, source_target_pairs={{0,2},{1,3},{2,0},{3,1},{4,6},{5,7},{6,4},{7,5},{8,10},{9,11},{10,... | collective-permute-start | bytes 73736 | tf_op jit(solution)/shard_map/ppermute | solution.py:597
  34.1 5.0 %collective-permute-start.10 = (bf16[352,128]{1,0:T(8,128)(2,1)S(1)}, bf16[352,128]{1,0:T(8,128)(2,1)S(1)}, u32[]{:S(2)}, u32[]{:S(2)}) collective-permute-start(bf16[352,128]{1,0:T(8,128)(2,1)S(1)} %get-tuple-element.71), channel_id=1, source_target_pairs={{0,12},{4,8},{8,4},{12,0},{1,13},{5,9},{9,5},{13,1},{2,14},{6,10},... | collective-permute-start | bytes 270344 | tf_op jit(solution)/shard_map/ppermute | solution.py:597
  34.1 6.6 %collective-permute-start.11 = (bf16[352,128]{1,0:T(8,128)(2,1)S(1)}, bf16[352,128]{1,0:T(8,128)(2,1)S(1)}, u32[]{:S(2)}, u32[]{:S(2)}) collective-permute-start(bf16[352,128]{1,0:T(8,128)(2,1)S(1)} %get-tuple-element.72), channel_id=1, source_target_pairs={{0,8},{4,12},{8,0},{12,4},{1,9},{5,13},{9,1},{13,5},{2,10},{6,14},... | collective-permute-start | bytes 270344 | tf_op jit(solution)/shard_map/ppermute | solution.py:597
  35.5 5.2 %collective-permute-start.12 = (bf16[352,128]{1,0:T(8,128)(2,1)S(1)}, bf16[352,128]{1,0:T(8,128)(2,1)S(1)}, u32[]{:S(2)}, u32[]{:S(2)}) collective-permute-start(bf16[352,128]{1,0:T(8,128)(2,1)S(1)} %get-tuple-element.73), channel_id=1, source_target_pairs={{0,4},{4,0},{8,12},{12,8},{1,5},{5,1},{9,13},{13,9},{2,6},{6,2},{1... | collective-permute-start | bytes 270344 | tf_op jit(solution)/shard_map/ppermute | solution.py:597

commit v23 on v20

--- a/solution.py
+++ b/solution.py
@@ -464,7 +464,7 @@
 
 
 def partners(count):
-    return [0, *range(count - 1, 0, -1)]
+    return [0, *[p ^ 1 for p in range(count - 1, 1, -1)], 1]
 
 
 def row_sum(parts, after, share):
@@ -587,6 +587,10 @@
     return lax.ppermute(x, axis, [(n, n ^ p) for n in range(lax.axis_size(axis))])
 
 
+def in_turn(parts):
+    return [parts[p - 1] for p in partners(len(parts) + 1)[1:]]
+
+
 def swap_each(parts, axis, step=1):
     count = len(parts)
     return [swap(parts[n - 1], axis, n * step) for n in range(count, 0, -1)][::-1]
@@ -622,7 +626,7 @@
     )
     share = channels // row_n
 
-    parts = [own] + swap_each(messages, "row")[::-1]
+    parts = [own] + in_turn(swap_each(messages, "row"))
     left_kept, (message,) = gradient(
         b_wide, y, own, "col", in_pairs(col_n), col_n // 2, 1, i_n, j_n, sequences
     )
@@ -641,7 +645,7 @@
     )
 
     messages, piece, bias = column_sum(parts, right_sent, share)
-    pieces = [piece] + swap_each(messages, "row")[::-1]
+    pieces = [piece] + in_turn(swap_each(messages, "row"))
     pair_map = pair(x, wt, output_bias, piece, sequences)
     projection, left_grad, right_grad, bias_grad = finish(
         pieces,

time: 40.8 us -> 41.3 us (1.012)
  starting transfers between devices: 17.8 us -> 18.9 us
  waiting for transfers between devices: 5.25 us -> 4.68 us
    ppermute x14, starting transfers between devices: 17.8 us -> 18.9 us  [swap(): lax.ppermute(x, axis, [(n, n ^ p) for n in range(lax.axis_size(axis))])]
    ppermute x14, waiting for transfers between devices: 5.25 us -> 4.68 us  [swap(): lax.ppermute(x, axis, [(n, n ^ p) for n in range(lax.axis_size(axis))])]
  transfers between devices with their start and end apart: 14 -> 14, of which waited for: 8 -> 6; matrix products, arithmetic and copies ran while one was open for 0% -> 0% of each run, Pallas kernels for 28% -> 28%
where the time goes in v23:
time: 41.3 us; the launch traced here: 41.2 us
  starting transfers between devices  18.9 us (46%)
  Pallas kernels  16.9 us (41%)
  waiting for transfers between devices  4.68 us (11%)
  between operations  0.71 us (2%)
    ppermute x14, starting transfers between devices, swap(): lax.ppermute(x, axis, [(n, n ^ p) for n in range(lax.axis_size(axis))])  18.9 us
    ppermute x14, waiting for transfers between devices, swap(): lax.ppermute(x, axis, [(n, n ^ p) for n in range(lax.axis_size(axis))])  4.68 us
    pallas_call x1, Pallas kernels, outer(): pl.pallas_call(functools.partial(outer_kernel, i_n, j_n), in_specs=[in_vm...  4.4 us
    pallas_call x2, Pallas kernels, gradient(): pl.pallas_call(functools.partial(gradient_kernel, axis, plan, kept, posit...  4.13 us
    pallas_call x1, Pallas kernels, pair(): pl.pallas_call(functools.partial(pair_kernel, sequences), grid=(count,),...  2.55 us
    pallas_call x1, Pallas kernels, prepare(): pl.pallas_call(functools.partial(prepare_kernel, i_n, j_n), in_specs=[in_...  1.75 us
    pallas_call x1, Pallas kernels, product(): pl.pallas_call(product_kernel, in_specs=[in_vmem()] * 3 + [pl.BlockSpec(m...  1.55 us
    pallas_call x1, Pallas kernels, load(): pl.pallas_call(load_kernel, in_specs=[pl.BlockSpec(memory_space=pltpu.HBM...  1.39 us
  transfers between devices with their start and end apart: 14, of which 6 were waited for; matrix products, arithmetic and copies ran while one was open for 0% of the time, Pallas kernels for 28%

profile of v23, /device:TPU:0, one launch (start us, length us, event | category | flops | bytes accessed | tf_op | source)
XLA Modules:
  0.0 41.2 jit_solution(10798708293879286856)
XLA Ops:
  0.6 3.1 %collective-permute-start = (bf16[8,1536]{1,0:T(8,128)(2,1)}, bf16[8,1536]{1,0:T(8,128)(2,1)S(1)}, u32[]{:S(2)}, u32[]{:S(2)}) collective-permute-start(bf16[8,1536]{1,0:T(8,128)(2,1)} %a_hbm.1), channel_id=1, source_target_pairs={{0,1},{1,0},{2,3},{3,2},{4,5},{5,4},{6,7},{7,6},{8,9},{9,8},{10,11... | collective-permute-start | bytes 73736 | tf_op jit(solution)/shard_map/ppermute | solution.py:587
  3.7 0.0 collective-permute-start.1
  3.7 1.4 %shard_map.92 = (bf16[1024,128]{1,0:T(8,128)(2,1)S(1)}, bf16[128,1024]{1,0:T(8,128)(2,1)S(1)}, bf16[8,1536]{1,0:T(8,128)(2,1)S(1)}, bf16[8,1536]{1,0:T(8,128)(2,...) custom-call(bf16[8,1536]{1,0:T(8,128)(2,1)} %a_hbm.1, bf16[8,1536]{1,0:T(8,128)(2,1)} %b_hbm.1, ...), custom_call_target="tpu_custom_call" | custom-call | flops 131072000 | bytes 2097152 | tf_op jit(solution)/shard_map/pallas_call | solution.py:67
  5.1 0.6 %collective-permute-done.refs_1_ = bf16[8,1536]{1,0:T(8,128)(2,1)S(1)} collective-permute-done((bf16[8,1536]{1,0:T(8,128)(2,1)}, bf16[8,1536]{1,0:T(8,128)(2,1)S(1)}, u32[]{:S(2)}, u32[]{:S(2)}) %collective-permute-start) | collective-permute-done | bytes 24608 | tf_op jit(solution)/shard_map/ppermute | solution.py:587
  5.7 0.0 collective-permute-done.1.refs_3_
  5.8 3.1 %collective-permute-start.2 = (bf16[16,1536]{1,0:T(8,128)(2,1)S(1)}, bf16[16,1536]{1,0:T(8,128)(2,1)S(1)}, u32[]{:S(2)}, u32[]{:S(2)}) collective-permute-start(bf16[16,1536]{1,0:T(8,128)(2,1)S(1)} %get-tuple-element.45.refs_0_), channel_id=1, source_target_pairs={{0,2},{1,3},{2,0},{3,1},{4,6},{5,7},{6,4},{7,5},{8,10},{9,11},{10,... | collective-permute-start | bytes 147464 | tf_op jit(solution)/shard_map/ppermute | solution.py:587
  8.9 1.5 %collective-permute-start.3 = (bf16[16,1536]{1,0:T(8,128)(2,1)S(1)}, bf16[16,1536]{1,0:T(8,128)(2,1)S(1)}, u32[]{:S(2)}, u32[]{:S(2)}) collective-permute-start(bf16[16,1536]{1,0:T(8,128)(2,1)S(1)} %get-tuple-element.46.refs_2_), channel_id=1, source_target_pairs={{0,8},{4,12},{8,0},{12,4},{1,9},{5,13},{9,1},{13,5},{2,10},{6,14},... | collective-permute-start | bytes 147464 | tf_op jit(solution)/shard_map/ppermute | solution.py:587
  10.3 1.8 %shard_map.94 = (bf16[1024,2304]{1,0:T(8,128)(2,1)S(1)}, bf16[2304,128]{1,0:T(8,128)(2,1)S(1)}, bf16[16,128]{1,0:T(8,128)(2,1)S(1)}) custom-call(bf16[1024,128]{1,0:T(8,128)(2,1)S(1)} %get-tuple-element.48.we_ref, bf16[2304,128]{1,0:T(8,128)(2,1)S(1)} %get-tuple-element.47.g_ref.refs_4_), custom_call_target="tpu_custom_call" | custom-call | flops 603979776 | bytes 9437184 | tf_op jit(solution)/shard_map/pallas_call | solution.py:126
  12.1 0.8 %collective-permute-done.3.refs_3_ = bf16[16,1536]{1,0:T(8,128)(2,1)S(1)} collective-permute-done((bf16[16,1536]{1,0:T(8,128)(2,1)S(1)}, bf16[16,1536]{1,0:T(8,128)(2,1)S(1)}, u32[]{:S(2)}, u32[]{:S(2)}) %collective-permute-start.3) | collective-permute-done | bytes 49184 | tf_op jit(solution)/shard_map/ppermute | solution.py:587
  12.9 4.4 %shard_map.95 = (bf16[1024,2304]{1,0:T(8,128)(2,1)S(1)}, f32[32,1536]{1,0:T(8,128)S(1)}, f32[1,1536,128]{2,1,0:T(8,128)S(1)}, f32[272,128]{1,0:T(8,128)S(1)}, bf...) custom-call(bf16[16,1536]{1,0:T(8,128)(2,1)S(1)} %get-tuple-element.45.refs_0_, ...), custom_call_target="tpu_custom_call" | custom-call | flops 1207959552 | bytes 4718592 | tf_op jit(solution)/shard_map/pallas_call | solution.py:290
  17.4 1.5 %collective-permute-start.4 = (bf16[272,128]{1,0:T(8,128)(2,1)S(1)}, bf16[272,128]{1,0:T(8,128)(2,1)S(1)}, u32[]{:S(2)}, u32[]{:S(2)}) collective-permute-start(bf16[272,128]{1,0:T(8,128)(2,1)S(1)} %get-tuple-element.53), channel_id=1, source_target_pairs={{0,8},{4,12},{8,0},{12,4},{1,9},{5,13},{9,1},{13,5},{2,10},{6,14},... | collective-permute-start | bytes 208904 | tf_op jit(solution)/shard_map/ppermute | solution.py:587
  18.9 0.0 collective-permute-start.5
  18.9 0.7 %collective-permute-start.6 = (bf16[272,128]{1,0:T(8,128)(2,1)S(1)}, bf16[272,128]{1,0:T(8,128)(2,1)S(1)}, u32[]{:S(2)}, u32[]{:S(2)}) collective-permute-start(bf16[272,128]{1,0:T(8,128)(2,1)S(1)} %get-tuple-element.55), channel_id=1, source_target_pairs={{0,4},{4,0},{8,12},{12,8},{1,5},{5,1},{9,13},{13,9},{2,6},{6,2},{1... | collective-permute-start | bytes 208904 | tf_op jit(solution)/shard_map/ppermute | solution.py:587
  19.6 2.1 %shard_map.96 = (f32[96,128]{1,0:T(8,128)S(1)}, f32[96,128]{1,0:T(8,128)S(1)}, bf16[192,128]{1,0:T(8,128)(2,1)S(1)}) custom-call(f32[1,1536,128]{2,1,0:T(8,128)S(1)} %get-tuple-element.56.refs_0_, bf16[1024,2304]{1,0:T(8,128)(2,1)S(1)} %get-tuple-element.57.refs_1_, f32[272,128]{1,0:T(8,128)S(1)} %get-tuple-element.52.refs_2_.refs_0_), custom_call_target="tpu_custom_call" | custom-call | flops 603979776 | bytes 4718592 | tf_op jit(solution)/shard_map/pallas_call | solution.py:378
  21.6 1.6 %collective-permute-start.8 = (bf16[192,128]{1,0:T(8,128)(2,1)S(1)}, bf16[192,128]{1,0:T(8,128)(2,1)S(1)}, u32[]{:S(2)}, u32[]{:S(2)}) collective-permute-start(bf16[192,128]{1,0:T(8,128)(2,1)S(1)} %get-tuple-element.58.refs_4_), channel_id=1, source_target_pairs={{0,1},{1,0},{2,3},{3,2},{4,5},{5,4},{6,7},{7,6},{8,9},{9,8},{10,11... | collective-permute-start | bytes 147464 | tf_op jit(solution)/shard_map/ppermute | solution.py:587
  23.3 0.0 collective-permute-done.4.refs_1_
  23.3 0.0 collective-permute-done.5.refs_2_
  23.3 0.0 collective-permute-done.6.refs_3_
  23.3 1.6 %collective-permute-start.7 = (bf16[272,128]{1,0:T(8,128)(2,1)S(1)}, bf16[272,128]{1,0:T(8,128)(2,1)S(1)}, u32[]{:S(2)}, u32[]{:S(2)}) collective-permute-start(bf16[272,128]{1,0:T(8,128)(2,1)S(1)} %shard_map.97.refs_3_.own), channel_id=1, source_target_pairs={{0,1},{1,0},{2,3},{3,2},{4,5},{5,4},{6,7},{7,6},{8,9},{9,8},{10,11... | collective-permute-start | bytes 208904 | tf_op jit(solution)/shard_map/ppermute | solution.py:587
  24.9 0.9 %collective-permute-done.8.refs_2_ = bf16[192,128]{1,0:T(8,128)(2,1)S(1)} collective-permute-done((bf16[192,128]{1,0:T(8,128)(2,1)S(1)}, bf16[192,128]{1,0:T(8,128)(2,1)S(1)}, u32[]{:S(2)}, u32[]{:S(2)}) %collective-permute-start.8) | collective-permute-done | bytes 49184 | tf_op jit(solution)/shard_map/ppermute | solution.py:587
  25.8 1.5 %shard_map.99 = (bf16[1024,2304]{1,0:T(8,128)(2,1)S(1)}, f32[1,1536,128]{2,1,0:T(8,128)S(1)}) custom-call(bf16[1024,128]{1,0:T(8,128)(2,1)S(1)} %get-tuple-element.59.left_ref, bf16[2304,128]{1,0:T(8,128)(2,1)S(1)} %get-tuple-element.60.right_ref, f32[32,1536]{1,0:T(8,128)S(1)} %get-tuple-element.61.held, f32[96,128]{1,0:T(8,128)S(1)} %get-tuple-element.64._.refs_4_), custom_call_target="tpu_custom_call" | custom-call | flops 603979776 | bytes 9437184 | tf_op jit(solution)/shard_map/pallas_call | solution.py:406
  27.4 0.4 collective-permute-done.7.near
  27.7 1.4 %collective-permute-start.9 = (bf16[272,128]{1,0:T(8,128)(2,1)S(1)}, bf16[272,128]{1,0:T(8,128)(2,1)S(1)}, u32[]{:S(2)}, u32[]{:S(2)}) collective-permute-start(bf16[272,128]{1,0:T(8,128)(2,1)S(1)} %shard_map.100.refs_2_.refs_0_), channel_id=1, source_target_pairs={{0,2},{1,3},{2,0},{3,1},{4,6},{5,7},{6,4},{7,5},{8,10},{9,11},{10,... | collective-permute-start | bytes 208904 | tf_op jit(solution)/shard_map/ppermute | solution.py:587
  29.1 1.6 %collective-permute-start.13 = (bf16[96,128]{1,0:T(8,128)(2,1)S(1)}, bf16[96,128]{1,0:T(8,128)(2,1)S(1)}, u32[]{:S(2)}, u32[]{:S(2)}) collective-permute-start(bf16[96,128]{1,0:T(8,128)(2,1)S(1)} %get-tuple-element.74), channel_id=1, source_target_pairs={{0,2},{1,3},{2,0},{3,1},{4,6},{5,7},{6,4},{7,5},{8,10},{9,11},{10,... | collective-permute-start | bytes 73736 | tf_op jit(solution)/shard_map/ppermute | solution.py:587
  30.7 2.1 %shard_map.101 = (f32[96,128]{1,0:T(8,128)S(1)}, bf16[96,128]{1,0:T(8,128)(2,1)S(1)}, bf16[96,128]{1,0:T(8,128)(2,1)S(1)}, bf16[96,128]{1,0:T(8,128)(2,1)S(1)}) custom-call(f32[1,1536,128]{2,1,0:T(8,128)S(1)} %get-tuple-element.66.refs_0_, bf16[1024,2304]{1,0:T(8,128)(2,1)S(1)} %get-tuple-element.65._.refs_1_, bf16[272,128]{1,0:T(8,128)(2,1)S(1)} %shard_map.100.refs_2_.refs_0_), custom_call_target="tpu_custom_call" | custom-call | flops 603979776 | bytes 4718592 | tf_op jit(solution)/shard_map/pallas_call | solution.py:378
  32.8 0.3 collective-permute-done.9.refs_1_
  33.1 0.1 shard_map.102
  33.2 2.6 %collective-permute-start.10 = (bf16[352,128]{1,0:T(8,128)(2,1)S(1)}, bf16[352,128]{1,0:T(8,128)(2,1)S(1)}, u32[]{:S(2)}, u32[]{:S(2)}) collective-permute-start(bf16[352,128]{1,0:T(8,128)(2,1)S(1)} %get-tuple-element.71), channel_id=1, source_target_pairs={{0,8},{4,12},{8,0},{12,4},{1,9},{5,13},{9,1},{13,5},{2,10},{6,14},... | collective-permute-start | bytes 270344 | tf_op jit(solution)/shard_map/ppermute | solution.py:587
  35.8 0.2 collective-permute-start.12
  36.0 2.5 %shard_map.103 = bf16[2304,128]{1,0:T(8,128)(2,1)} custom-call(bf16[1024,2304]{1,0:T(8,128)(2,1)S(1)} %get-tuple-element.50.x_ref, bf16[128,1024]{1,0:T(8,128)(2,1)S(1)} %get-tuple-element.51.wt_ref, f32[1,128]{1,0:T(1,128)S(1)} %bitcast.4, bf16[256,128]{1,0:T(8,128)(2,1)S(1)} %get-tuple-element.70._.refs_0_), custom_call_target="tpu_custom_call" | custom-call | flops 1207959552 | bytes 4718592 | tf_op jit(solution)/shard_map/pallas_call | solution.py:429
  38.6 1.7 %collective-permute-done.11.refs_2_ = bf16[352,128]{1,0:T(8,128)(2,1)S(1)} collective-permute-done((bf16[352,128]{1,0:T(8,128)(2,1)S(1)}, bf16[352,128]{1,0:T(8,128)(2,1)S(1)}, u32[]{:S(2)}, u32[]{:S(2)}) %collective-permute-start.11) | collective-permute-done | bytes 90144 | tf_op jit(solution)/shard_map/ppermute | solution.py:587
  40.3 0.9 %shard_map.104 = (f32[1024,128]{1,0:T(8,128)}, f32[8,1536]{1,0:T(8,128)}, f32[8,1536]{1,0:T(8,128)}, f32[1,128]{1,0:T(1,128)}) custom-call(bf16[256,128]{1,0:T(8,128)(2,1)S(1)} %get-tuple-element.70._.refs_0_, bf16[352,128]{1,0:T(8,128)(2,1)S(1)} %collective-permute-done.10.refs_1_, bf16[352,128]{1,0:T(8,128)(2,1)S(1)} %collective-permute-done.11.refs_2_, ...), custom_call_target="tpu_custom_call" | custom-call | tf_op jit(solution)/shard_map/pallas_call | solution.py:456
  (11 shorter events, 0.1 us)
Async XLA Ops:
  0.6 5.1 %collective-permute-start = (bf16[8,1536]{1,0:T(8,128)(2,1)}, bf16[8,1536]{1,0:T(8,128)(2,1)S(1)}, u32[]{:S(2)}, u32[]{:S(2)}) collective-permute-start(bf16[8,1536]{1,0:T(8,128)(2,1)} %a_hbm.1), channel_id=1, source_target_pairs={{0,1},{1,0},{2,3},{3,2},{4,5},{5,4},{6,7},{7,6},{8,9},{9,8},{10,11... | collective-permute-start | bytes 73736 | tf_op jit(solution)/shard_map/ppermute | solution.py:587
  3.7 2.0 %collective-permute-start.1 = (bf16[8,1536]{1,0:T(8,128)(2,1)}, bf16[8,1536]{1,0:T(8,128)(2,1)S(1)}, u32[]{:S(2)}, u32[]{:S(2)}) collective-permute-start(bf16[8,1536]{1,0:T(8,128)(2,1)} %b_hbm.1), channel_id=1, source_target_pairs={{0,4},{4,0},{8,12},{12,8},{1,5},{5,1},{9,13},{13,9},{2,6},{6,2},{1... | collective-permute-start | bytes 73736 | tf_op jit(solution)/shard_map/ppermute | solution.py:587
  5.8 6.4 %collective-permute-start.2 = (bf16[16,1536]{1,0:T(8,128)(2,1)S(1)}, bf16[16,1536]{1,0:T(8,128)(2,1)S(1)}, u32[]{:S(2)}, u32[]{:S(2)}) collective-permute-start(bf16[16,1536]{1,0:T(8,128)(2,1)S(1)} %get-tuple-element.45.refs_0_), channel_id=1, source_target_pairs={{0,2},{1,3},{2,0},{3,1},{4,6},{5,7},{6,4},{7,5},{8,10},{9,11},{10,... | collective-permute-start | bytes 147464 | tf_op jit(solution)/shard_map/ppermute | solution.py:587
  8.9 4.1 %collective-permute-start.3 = (bf16[16,1536]{1,0:T(8,128)(2,1)S(1)}, bf16[16,1536]{1,0:T(8,128)(2,1)S(1)}, u32[]{:S(2)}, u32[]{:S(2)}) collective-permute-start(bf16[16,1536]{1,0:T(8,128)(2,1)S(1)} %get-tuple-element.46.refs_2_), channel_id=1, source_target_pairs={{0,8},{4,12},{8,0},{12,4},{1,9},{5,13},{9,1},{13,5},{2,10},{6,14},... | collective-permute-start | bytes 147464 | tf_op jit(solution)/shard_map/ppermute | solution.py:587
  17.4 5.9 %collective-permute-start.4 = (bf16[272,128]{1,0:T(8,128)(2,1)S(1)}, bf16[272,128]{1,0:T(8,128)(2,1)S(1)}, u32[]{:S(2)}, u32[]{:S(2)}) collective-permute-start(bf16[272,128]{1,0:T(8,128)(2,1)S(1)} %get-tuple-element.53), channel_id=1, source_target_pairs={{0,8},{4,12},{8,0},{12,4},{1,9},{5,13},{9,1},{13,5},{2,10},{6,14},... | collective-permute-start | bytes 208904 | tf_op jit(solution)/shard_map/ppermute | solution.py:587
  18.9 4.4 %collective-permute-start.5 = (bf16[272,128]{1,0:T(8,128)(2,1)S(1)}, bf16[272,128]{1,0:T(8,128)(2,1)S(1)}, u32[]{:S(2)}, u32[]{:S(2)}) collective-permute-start(bf16[272,128]{1,0:T(8,128)(2,1)S(1)} %get-tuple-element.54), channel_id=1, source_target_pairs={{0,12},{4,8},{8,4},{12,0},{1,13},{5,9},{9,5},{13,1},{2,14},{6,10},... | collective-permute-start | bytes 208904 | tf_op jit(solution)/shard_map/ppermute | solution.py:587
  18.9 4.4 %collective-permute-start.6 = (bf16[272,128]{1,0:T(8,128)(2,1)S(1)}, bf16[272,128]{1,0:T(8,128)(2,1)S(1)}, u32[]{:S(2)}, u32[]{:S(2)}) collective-permute-start(bf16[272,128]{1,0:T(8,128)(2,1)S(1)} %get-tuple-element.55), channel_id=1, source_target_pairs={{0,4},{4,0},{8,12},{12,8},{1,5},{5,1},{9,13},{13,9},{2,6},{6,2},{1... | collective-permute-start | bytes 208904 | tf_op jit(solution)/shard_map/ppermute | solution.py:587
  21.6 4.2 %collective-permute-start.8 = (bf16[192,128]{1,0:T(8,128)(2,1)S(1)}, bf16[192,128]{1,0:T(8,128)(2,1)S(1)}, u32[]{:S(2)}, u32[]{:S(2)}) collective-permute-start(bf16[192,128]{1,0:T(8,128)(2,1)S(1)} %get-tuple-element.58.refs_4_), channel_id=1, source_target_pairs={{0,1},{1,0},{2,3},{3,2},{4,5},{5,4},{6,7},{7,6},{8,9},{9,8},{10,11... | collective-permute-start | bytes 147464 | tf_op jit(solution)/shard_map/ppermute | solution.py:587
  23.3 4.4 %collective-permute-start.7 = (bf16[272,128]{1,0:T(8,128)(2,1)S(1)}, bf16[272,128]{1,0:T(8,128)(2,1)S(1)}, u32[]{:S(2)}, u32[]{:S(2)}) collective-permute-start(bf16[272,128]{1,0:T(8,128)(2,1)S(1)} %shard_map.97.refs_3_.own), channel_id=1, source_target_pairs={{0,1},{1,0},{2,3},{3,2},{4,5},{5,4},{6,7},{7,6},{8,9},{9,8},{10,11... | collective-permute-start | bytes 208904 | tf_op jit(solution)/shard_map/ppermute | solution.py:587
  27.7 8.3 %copy-start = (f32[128]{0:T(128)S(1)}, f32[128]{0:T(128)}, u32[]{:S(2)}) copy-start(f32[128]{0:T(128)} %param.8) | copy-start | bytes 1540
  27.7 5.4 %collective-permute-start.9 = (bf16[272,128]{1,0:T(8,128)(2,1)S(1)}, bf16[272,128]{1,0:T(8,128)(2,1)S(1)}, u32[]{:S(2)}, u32[]{:S(2)}) collective-permute-start(bf16[272,128]{1,0:T(8,128)(2,1)S(1)} %shard_map.100.refs_2_.refs_0_), channel_id=1, source_target_pairs={{0,2},{1,3},{2,0},{3,1},{4,6},{5,7},{6,4},{7,5},{8,10},{9,11},{10,... | collective-permute-start | bytes 208904 | tf_op jit(solution)/shard_map/ppermute | solution.py:587
  29.1 9.4 %collective-permute-start.13 = (bf16[96,128]{1,0:T(8,128)(2,1)S(1)}, bf16[96,128]{1,0:T(8,128)(2,1)S(1)}, u32[]{:S(2)}, u32[]{:S(2)}) collective-permute-start(bf16[96,128]{1,0:T(8,128)(2,1)S(1)} %get-tuple-element.74), channel_id=1, source_target_pairs={{0,2},{1,3},{2,0},{3,1},{4,6},{5,7},{6,4},{7,5},{8,10},{9,11},{10,... | collective-permute-start | bytes 73736 | tf_op jit(solution)/shard_map/ppermute | solution.py:587
  33.2 5.3 %collective-permute-start.10 = (bf16[352,128]{1,0:T(8,128)(2,1)S(1)}, bf16[352,128]{1,0:T(8,128)(2,1)S(1)}, u32[]{:S(2)}, u32[]{:S(2)}) collective-permute-start(bf16[352,128]{1,0:T(8,128)(2,1)S(1)} %get-tuple-element.71), channel_id=1, source_target_pairs={{0,8},{4,12},{8,0},{12,4},{1,9},{5,13},{9,1},{13,5},{2,10},{6,14},... | collective-permute-start | bytes 270344 | tf_op jit(solution)/shard_map/ppermute | solution.py:587
  35.8 4.4 %collective-permute-start.11 = (bf16[352,128]{1,0:T(8,128)(2,1)S(1)}, bf16[352,128]{1,0:T(8,128)(2,1)S(1)}, u32[]{:S(2)}, u32[]{:S(2)}) collective-permute-start(bf16[352,128]{1,0:T(8,128)(2,1)S(1)} %get-tuple-element.72), channel_id=1, source_target_pairs={{0,12},{4,8},{8,4},{12,0},{1,13},{5,9},{9,5},{13,1},{2,14},{6,10},... | collective-permute-start | bytes 270344 | tf_op jit(solution)/shard_map/ppermute | solution.py:587
  35.8 4.4 %collective-permute-start.12 = (bf16[352,128]{1,0:T(8,128)(2,1)S(1)}, bf16[352,128]{1,0:T(8,128)(2,1)S(1)}, u32[]{:S(2)}, u32[]{:S(2)}) collective-permute-start(bf16[352,128]{1,0:T(8,128)(2,1)S(1)} %get-tuple-element.73), channel_id=1, source_target_pairs={{0,4},{4,0},{8,12},{12,8},{1,5},{5,1},{9,13},{13,9},{2,6},{6,2},{1... | collective-permute-start | bytes 270344 | tf_op jit(solution)/shard_map/ppermute | solution.py:587
